TPU v7x, 32 devices: a whole 2x2x4 slice. The times are simulated.
32 devices in a mesh: dp: 4 (over y, x), ep: 8 (over z, core).
Axes of the slice: x: 2, y: 2, z: 4, core: 2. Of those that a mesh axis runs over, the one named last changes fastest.
Arguments:
- tokens: bfloat16 [4096, 2048], P(('dp', 'ep')), may hold values from -6 to 6
- cotangent: bfloat16 [4096, 2048], P(('dp', 'ep')), may hold values from -6 to 6
- expert_ids: int32 [4096, 8], P(('dp', 'ep')), may hold values from 0 to 31, all different within a row; in each aligned block of 128 rows (0 to 127, 128 to 255, ...) at most 34 rows name the same one
- gate_weights: bfloat16 [4096, 8], P(('dp', 'ep')), may hold values from 0.019897461 to 0.3984375
- w_up: bfloat16 [32, 2048, 384], P('ep'), may hold values from -0.125 to 0.125
- w_down: bfloat16 [32, 2048, 384], P('ep'), may hold values from -0.3125 to 0.3125
Outputs:
- token_grad: bfloat16 [4096, 2048], P(('dp', 'ep'))
- gate_grad: bfloat16 [4096, 8], P(('dp', 'ep'))
- down_grad: float32 [32, 2048, 384], P('ep', 'dp')
Inputs may be any that keep to these rules, and one draw needn't show every extreme that they name: `expert_ids`: each token names 8 different experts; among the 128 tokens of one device (aligned blocks of rows) no expert is named more than 34 times, and in some block one expert is named exactly 34 times.
All inputs are finite; a program needn't handle non-finite values.
Results may differ from a plain program's by a relative error of at most 0.008.
Values may be sent and summed in bfloat16 or wider, within the bound.
No kernel may reach another device: no remote copies, remote signals or barrier semaphores. Data moves between devices by JAX's collectives and lax.ppermute only.
A program may use at most 128 MiB of HBM per device.

v0:
```python
import jax
import jax.numpy as jnp
from jax import lax
from jax.sharding import PartitionSpec as P


def expert_forward(tokens_in, w_up):
    pre_act = jnp.einsum("sbcd,bdh->sbch", tokens_in, w_up, preferred_element_type=jnp.float32)
    hidden = jax.nn.silu(pre_act).astype(jnp.bfloat16)
    return (pre_act, hidden)


def shards(tokens, cotangent, expert_ids, gate_weights, w_up, w_down):
    tok_rows, width = tokens.shape
    top_count = expert_ids.shape[1]
    ep_count = lax.axis_size("ep")
    local_experts = w_up.shape[0]
    experts_total = local_experts * ep_count
    base_load = tok_rows * top_count // experts_total
    capacity = base_load + max(1, base_load // 16)
    route_count = tok_rows * top_count
    flat_ids = expert_ids.reshape(route_count)
    expert_hits = (
        expert_ids[:, :, None] == jnp.arange(experts_total, dtype=jnp.int32)[None, None, :]
    ).astype(jnp.bfloat16)
    token_counts = jnp.sum(expert_hits, axis=1)
    row_index = jnp.arange(tok_rows, dtype=jnp.int32)
    lower_ones = (row_index[:, None] > row_index[None, :]).astype(jnp.bfloat16)
    prior_counts = jnp.dot(lower_ones, token_counts, preferred_element_type=jnp.float32)
    earlier = (
        jnp.sum(expert_hits.astype(jnp.float32) * prior_counts[:, None, :], axis=2)
        .astype(jnp.int32)
        .reshape(route_count)
    )
    buffer_pos = flat_ids * capacity + earlier
    slot_total = experts_total * capacity
    inverse = jnp.full((slot_total,), route_count, jnp.int32)
    inverse = inverse.at[buffer_pos].set(jnp.arange(route_count, dtype=jnp.int32))
    occupied = inverse < route_count
    route_of = jnp.minimum(inverse, route_count - 1)
    token_of = route_of // top_count
    blank = jnp.zeros((), jnp.bfloat16)
    x_send = jnp.where(occupied[:, None], tokens[token_of], blank)
    dy_send = jnp.where(occupied[:, None], cotangent[token_of], blank)
    g_send = jnp.where(occupied, gate_weights.reshape(route_count)[route_of], blank)
    layout = (ep_count, local_experts, capacity, width)
    x_recv, dy_recv, g_recv = (
        lax.all_to_all(x_send, "ep", split_axis=0, concat_axis=0, tiled=True),
        lax.all_to_all(dy_send, "ep", split_axis=0, concat_axis=0, tiled=True),
        lax.all_to_all(g_send, "ep", split_axis=0, concat_axis=0, tiled=True),
    )
    pre_act, hidden = expert_forward(x_recv.reshape(layout), w_up)
    dy_in = dy_recv.reshape(layout)
    gate_f = g_recv.reshape(ep_count, local_experts, capacity).astype(jnp.float32)[..., None]
    back_hidden = jnp.einsum("sbcd,bdh->sbch", dy_in, w_down, preferred_element_type=jnp.float32)
    gate_slots = jnp.sum(back_hidden * hidden.astype(jnp.float32), axis=3).astype(jnp.bfloat16)
    sig = jax.nn.sigmoid(pre_act)
    slope = sig * (1.0 + pre_act * (1.0 - sig))
    grad_pre = (gate_f * back_hidden * slope).astype(jnp.bfloat16)
    route_grad = jnp.einsum(
        "sbch,bdh->sbcd", grad_pre, w_up, preferred_element_type=jnp.float32
    ).astype(jnp.bfloat16)
    scaled_cot = (gate_f * dy_in).astype(jnp.bfloat16)
    back_grad, back_gate = (
        lax.all_to_all(
            route_grad.reshape(slot_total, width), "ep", split_axis=0, concat_axis=0, tiled=True
        ),
        lax.all_to_all(
            gate_slots.reshape(slot_total), "ep", split_axis=0, concat_axis=0, tiled=True
        ),
    )
    token_grad = jnp.sum(
        back_grad[buffer_pos].reshape(tok_rows, top_count, width), axis=1, dtype=jnp.float32
    ).astype(jnp.bfloat16)
    gate_grad = back_gate[buffer_pos].reshape(tok_rows, top_count)
    partial_grad = jnp.einsum(
        "sbcd,sbch->bdh", scaled_cot, hidden, preferred_element_type=jnp.float32
    )
    down_grad = lax.psum_scatter(partial_grad, "dp", scatter_dimension=1, tiled=True)
    return (token_grad, gate_grad, down_grad)


def solution(mesh):
    return jax.shard_map(
        shards,
        mesh=mesh,
        in_specs=(
            P(("dp", "ep"), None),
            P(("dp", "ep"), None),
            P(("dp", "ep"), None),
            P(("dp", "ep"), None),
            P("ep", None, None),
            P("ep", None, None),
        ),
        out_specs=(P(("dp", "ep"), None), P(("dp", "ep"), None), P("ep", "dp", None)),
        check_vma=False,
    )
```

profile of v0, /device:TPU:0, one launch (start us, length us, event | category | flops | bytes accessed | tf_op | source)
XLA Modules:
  0.0 426.3 jit_solution(12386250375908561708)
XLA Ops:
  7.2 0.0 copy-start
  7.2 0.8 fusion.20
  7.9 0.1 fusion.21
  8.1 0.7 multiply_reduce_fusion
  8.8 0.7 convert_add_fusion
  9.5 0.8 copy.81
  10.3 0.1 reshape.110
  10.4 0.1 copy.80
  10.5 0.1 add.44
  10.7 4.3 %scatter_custom_fusion = s32[1088]{0:T(1024)S(1)} fusion(s32[1024]{0:T(1024)S(1)} %bitcast.74, s32[1024]{0:T(1024)S(1)} %iota.14, s32[]{:T(128)} %constant.11.clone.1), kind=kCustom, calls=%fused_computation.55 | custom fusion | bytes 4356 | tf_op jit(solution)/shard_map/scatter | solution.py:38
  15.0 6.9 %gather_fusion = bf16[1088]{0:T(1024)(128)(2,1)S(1)} fusion(bf16[1024]{0:T(1024)(128)(2,1)S(1)} %reshape.110, s32[2048]{0:T(1024)S(1)} %get-tuple-element.30), kind=kCustom, calls=%fused_computation | custom fusion | bytes 8704 | tf_op jit(solution)/shard_map/gather | solution.py:45
  22.0 0.7 all_to_all.37
  22.6 6.3 %all-to-all-start = ((bf16[8,136,1]{1,2,0:T(2,128)(2,1)}), bf16[8,136,1]{1,2,0:T(2,128)(2,1)S(1)}, u32[]{:S(2)}, u32[]{:S(2)}) async-start(bf16[8,136,1]{1,2,0:T(2,128)(2,1)} %all_to_all.37), calls=%async_computation | async-start | bytes 16384 | tf_op jit(solution)/shard_map/all_to_all | solution.py:50
  29.0 0.1 broadcast_in_dim.42
  29.1 0.0 copy-start.2
  29.1 5.9 %gather_fusion.2 = bf16[1088,2048]{1,0:T(8,128)(2,1)} fusion(bf16[128,2048]{1,0:T(8,128)(2,1)S(1)} %copy-done, s32[2048]{0:T(1024)S(1)} %get-tuple-element.29), kind=kCustom, calls=%fused_computation.2 | custom fusion | bytes 8917248 | tf_op jit(solution)/shard_map/gather | solution.py:43
  34.9 0.0 copy-done.2
  35.0 5.9 %gather_fusion.1 = bf16[1088,2048]{1,0:T(8,128)(2,1)} fusion(bf16[128,2048]{1,0:T(8,128)(2,1)S(1)} %copy-done.2, s32[2048]{0:T(1024)S(1)} %get-tuple-element.29), kind=kCustom, calls=%fused_computation.1 | custom fusion | bytes 8917248 | tf_op jit(solution)/shard_map/gather | solution.py:44
  40.8 6.1 %broadcast_select_fusion.1 = (bf16[8,136,2048]{2,1,0:T(8,128)(2,1)}, bf16[8,136,2048]{2,1,0:T(8,128)(2,1)}) fusion(bf16[8,136,2048]{2,1,0:T(8,128)(2,1)} %bitcast.71, pred[8,136]{1,0:T(8,128)(4,1)S(1)} %broadcast_in_dim.42, bf16[8,136,2048]{2,1,0:T(8,128)(2,1)} %bitcast.70), kind=kLoop, calls=%fused_computation.17 | loop fusion | flops 4456448 | bytes 17826880 | tf_op jit(solution)/shard_map/jit(_where)/select_n | solution.py:44
  46.9 0.0 all-to-all-done
  46.9 104.9 %all_to_all.43 = bf16[8,136,2048]{2,1,0:T(8,128)(2,1)} all-to-all(bf16[8,136,2048]{2,1,0:T(8,128)(2,1)} %get-tuple-element.28), channel_id=1, replica_groups=mesh['dp'=4,'ep'=8] {'ep'}, dimensions={0} | all-to-all | bytes 8912896 | tf_op jit(solution)/shard_map/all_to_all | solution.py:48
  151.8 4.6 %all-to-all-start.1 = ((bf16[8,136,2048]{2,1,0:T(8,128)(2,1)}), bf16[8,136,2048]{2,1,0:T(8,128)(2,1)}, u32[]{:S(2)}, u32[]{:S(2)}) async-start(bf16[8,136,2048]{2,1,0:T(8,128)(2,1)} %get-tuple-element.27), calls=%async_computation.1 | async-start | bytes 8912896 | tf_op jit(solution)/shard_map/all_to_all | solution.py:49
  156.4 0.2 reduce-scatter.2.cloned.1.call-start
  156.7 0.1 reshape.115
  156.8 0.1 copy.83
  156.9 4.7 %copy.85 = bf16[8,136,2048]{2,0,1:T(8,128)(2,1)S(1)} copy(bf16[8,136,2048]{2,1,0:T(8,128)(2,1)} %all_to_all.43) | data formatting | bytes 8912896 | tf_op jit(solution)/shard_map/all_to_all | solution.py:48
  161.6 5.3 %fusion.2 = f32[4,8,34,384]{3,1,2,0:T(8,128)S(1)} fusion(bf16[8,4,34,2048]{3,0,2,1:T(8,128)(2,1)S(1)} %bitcast.68, bf16[4,2048,384]{2,1,0:T(8,128)(2,1)} %param.10), kind=kOutput, calls=%fused_computation.9 | convolution fusion | flops 1711276032 | bytes 12419072 | tf_op jit(solution)/shard_map/sbcd,bdh->sbch/dot_general | solution.py:8
  166.9 89.1 %all-to-all-done.1 = bf16[8,136,2048]{2,1,0:T(8,128)(2,1)} async-done(((bf16[8,136,2048]{2,1,0:T(8,128)(2,1)}), bf16[8,136,2048]{2,1,0:T(8,128)(2,1)}, u32[]{:S(2)}, u32[]{:S(2)}) %all-to-all-start.1) | async-done | bytes 4456480 | tf_op jit(solution)/shard_map/all_to_all | solution.py:49
  256.0 4.7 %copy.84 = bf16[8,136,2048]{2,0,1:T(8,128)(2,1)S(1)} copy(bf16[8,136,2048]{2,1,0:T(8,128)(2,1)} %all-to-all-done.1) | data formatting | bytes 8912896 | tf_op jit(solution)/shard_map/all_to_all | solution.py:49
  260.8 2.0 copy-done.3
  262.8 7.3 %convolution_bitcast_fusion = f32[4,2048,384]{2,1,0:T(8,128)} fusion(bf16[8,4,34,2048]{3,0,2,1:T(8,128)(2,1)S(1)} %bitcast.72, f32[8,4,34]{0,2,1:T(8,128)S(1)} %copy.83, f32[4,8,34,384]{3,1,2,0:T(8,128)S(1)} %fusion.2), kind=kOutput, calls=%fused_computation.13 | convolution fusion | flops 1720049664 | bytes 18714880 | tf_op jit(solution)/shard_map/sbcd,sbch->bdh/dot_general | solution.py:76
  270.1 0.0 reduce-scatter.2.cloned.1.call-update
  270.1 7.0 %fusion.17 = (bf16[8,4,34]{0,2,1:T(8,128)(2,1)S(1)}, bf16[8,4,34,384]{3,0,2,1:T(8,128)(2,1)S(1)}) fusion(f32[4,8,34,384]{3,1,2,0:T(8,128)S(1)} %fusion.2, f32[8,4,34]{0,2,1:T(8,128)S(1)} %copy.83, bf16[8,4,34,2048]{3,0,2,1:T(8,128)(2,1)} %bitcast.73, bf16[4,2048,384]{2,1,0:T(8,128)(2,1)} %param.11), kind=kOutput, calls=%fused_computation.32 | convolution fusion | flops 1717541888 | bytes 13261184 | tf_op jit(solution)/shard_map/sbcd,bdh->sbch/dot_general | solution.py:55
  277.1 0.1 copy.89
  277.2 0.7 convert_element_type.83
  277.9 3.6 all-to-all-start.4
  281.5 8.8 %convert_bitcast_fusion = bf16[8,4,34,2048]{3,2,0,1:T(8,128)(2,1)S(1)} fusion(bf16[4,2048,384]{2,1,0:T(8,128)(2,1)} %param.10, bf16[8,4,34,384]{3,0,2,1:T(8,128)(2,1)S(1)} %get-tuple-element.24), kind=kOutput, calls=%fused_computation.14 | convolution fusion | flops 1713504256 | bytes 11583488 | tf_op jit(solution)/shard_map/sbch,bdh->sbcd/dot_general | solution.py:60
  290.3 2.4 copy.87
  292.8 4.5 %copy.88 = bf16[8,136,2048]{2,1,0:T(8,128)(2,1)} copy(bf16[8,136,2048]{2,0,1:T(8,128)(2,1)S(1)} %bitcast.69) | data formatting | bytes 8912896 | tf_op jit(solution)/shard_map/all_to_all | solution.py:65
  297.3 0.0 all-to-all-done.4
  297.3 4.9 %all-to-all-start.3 = ((bf16[8,136,2048]{2,1,0:T(8,128)(2,1)}), bf16[8,136,2048]{2,1,0:T(8,128)(2,1)}, u32[]{:S(2)}, u32[]{:S(2)}) async-start(bf16[8,136,2048]{2,1,0:T(8,128)(2,1)} %copy.88), calls=%async_computation.3 | async-start | bytes 8912896 | tf_op jit(solution)/shard_map/all_to_all | solution.py:65
  302.2 0.1 all_to_all.36
  302.3 6.8 %gather_fusion.4 = bf16[1024]{0:T(1024)(128)(2,1)S(1)} fusion(bf16[1088]{0:T(1024)(128)(2,1)S(1)} %all_to_all.36, s32[1024]{0:T(1024)S(1)} %broadcast_clamp_fusion), kind=kCustom, calls=%fused_computation.4 | custom fusion | bytes 8192 | tf_op jit(solution)/shard_map/gather | solution.py:75
  309.1 0.1 reshape.114
  309.2 0.7 copy.93
  309.9 91.9 %all-to-all-done.3 = bf16[8,136,2048]{2,1,0:T(8,128)(2,1)} async-done(((bf16[8,136,2048]{2,1,0:T(8,128)(2,1)}), bf16[8,136,2048]{2,1,0:T(8,128)(2,1)}, u32[]{:S(2)}, u32[]{:S(2)}) %all-to-all-start.3) | async-done | bytes 4456480 | tf_op jit(solution)/shard_map/all_to_all | solution.py:65
  401.8 11.7 %gather_fusion.3 = bf16[1024,2048]{1,0:T(8,128)(2,1)} fusion(bf16[1088,2048]{1,0:T(8,128)(2,1)} %bitcast.13, s32[1024]{0:T(1024)S(1)} %broadcast_clamp_fusion), kind=kCustom, calls=%fused_computation.3 | custom fusion | bytes 8392704 | tf_op jit(solution)/shard_map/gather | solution.py:73
  413.5 5.9 %bitcast_reduce_fusion = bf16[128,2048]{1,0:T(8,128)(2,1)} fusion(bf16[1024,2048]{1,0:T(8,128)(2,1)} %gather_fusion.3), kind=kLoop, calls=%fused_computation.18 | loop fusion | flops 1835008 | bytes 4718592 | tf_op jit(solution)/shard_map/reduce_sum | solution.py:72
  (14 shorter events, 0.1 us)
Async XLA Ops:
  7.2 21.9 %copy-start = (bf16[128,2048]{1,0:T(8,128)(2,1)S(1)}, bf16[128,2048]{1,0:T(8,128)(2,1)}, u32[]{:S(2)}) copy-start(bf16[128,2048]{1,0:T(8,128)(2,1)} %param.6) | copy-start | bytes 1572868
  22.6 24.3 %all-to-all-start = ((bf16[8,136,1]{1,2,0:T(2,128)(2,1)}), bf16[8,136,1]{1,2,0:T(2,128)(2,1)S(1)}, u32[]{:S(2)}, u32[]{:S(2)}) async-start(bf16[8,136,1]{1,2,0:T(2,128)(2,1)} %all_to_all.37), calls=%async_computation | async-start | bytes 16384 | tf_op jit(solution)/shard_map/all_to_all | solution.py:50
  29.1 5.9 %copy-start.2 = (bf16[128,2048]{1,0:T(8,128)(2,1)S(1)}, bf16[128,2048]{1,0:T(8,128)(2,1)}, u32[]{:S(2)}) copy-start(bf16[128,2048]{1,0:T(8,128)(2,1)} %param.7) | copy-start | bytes 1572868
  151.8 104.2 %all-to-all-start.1 = ((bf16[8,136,2048]{2,1,0:T(8,128)(2,1)}), bf16[8,136,2048]{2,1,0:T(8,128)(2,1)}, u32[]{:S(2)}, u32[]{:S(2)}) async-start(bf16[8,136,2048]{2,1,0:T(8,128)(2,1)} %get-tuple-element.27), calls=%async_computation.1 | async-start | bytes 8912896 | tf_op jit(solution)/shard_map/all_to_all | solution.py:49
  156.4 263.0 %reduce-scatter.2.cloned.1.call-start = ((), (), s32[]{:S(2)}) async-start(), calls=%async_computation.6 | async-start | bytes 15728640 | tf_op jit(solution)/shard_map/reduce_scatter | solution.py:79
  260.7 2.0 copy-start.3
  277.9 19.4 %all-to-all-start.4 = ((bf16[8,136,1]{1,2,0:T(2,128)(2,1)}), bf16[8,136,1]{1,2,0:T(2,128)(2,1)S(1)}, u32[]{:S(2)}, u32[]{:S(2)}) async-start(bf16[8,136,1]{1,2,0:T(2,128)(2,1)} %convert_element_type.83), calls=%async_computation.4 | async-start | bytes 16384 | tf_op jit(solution)/shard_map/all_to_all | solution.py:68
  297.3 104.5 %all-to-all-start.3 = ((bf16[8,136,2048]{2,1,0:T(8,128)(2,1)}), bf16[8,136,2048]{2,1,0:T(8,128)(2,1)}, u32[]{:S(2)}, u32[]{:S(2)}) async-start(bf16[8,136,2048]{2,1,0:T(8,128)(2,1)} %copy.88), calls=%async_computation.3 | async-start | bytes 8912896 | tf_op jit(solution)/shard_map/all_to_all | solution.py:65
  401.8 17.6 %copy-start.1 = (bf16[128,2048]{1,0:T(8,128)(2,1)S(1)}, bf16[128,2048]{1,0:T(8,128)(2,1)}, u32[]{:S(2)}) copy-start(bf16[128,2048]{1,0:T(8,128)(2,1)} %param.6) | copy-start | bytes 1572868
Sparse Core Ops, SparseCore 0:
  270.2 119.6 reduce-scatter.1
where the time goes:
time: 427 us; the launch traced here: 426 us
  waiting for transfers between devices  181 us (42%)
  blocking collectives  105 us (25%)
  local copies, waits for them, and re-layouts  63.6 us (15%)
  matrix products  28.6 us (7%)
  starting transfers between devices  19.6 us (5%)
  other arithmetic  14.3 us (3%)
  between operations  14.2 us (3%)
    all_to_all x1, blocking collectives, shards(): lax.all_to_all(x_send, 'ep', split_axis=0, concat_axis=0, tiled=True)  105 us
    all_to_all x1, waiting for transfers between devices, shards(): lax.all_to_all(route_grad.reshape(slot_total, width), 'ep', split_axis=0,...  91.9 us
    all_to_all x1, waiting for transfers between devices, shards(): lax.all_to_all(dy_send, 'ep', split_axis=0, concat_axis=0, tiled=True)  89.1 us
    gather x1, local copies, waits for them, and re-layouts, shards(): back_grad[buffer_pos].reshape(tok_rows, top_count, width)  11.7 us
    dot_general x1, matrix products, shards(): jnp.einsum('sbch,bdh->sbcd', grad_pre, w_up, preferred_element_type=jnp.f...  8.8 us
  transfers between devices with their start and end apart: 5, of which 2 were waited for; matrix products, arithmetic and copies ran while one was open for 18% of the time, Pallas kernels for 0%

commit v1 on v0

v1 whole, which is shorter than its diff:
```python
import jax
import jax.numpy as jnp
from jax import lax
from jax.sharding import PartitionSpec as P


def shards(tokens, cotangent, expert_ids, gate_weights, w_up, w_down):
    tok_rows, width = tokens.shape
    top_count = expert_ids.shape[1]
    ep_count = lax.axis_size("ep")
    local_experts = w_up.shape[0]
    experts_total = local_experts * ep_count
    base_load = tok_rows * top_count // experts_total
    capacity = base_load + max(1, base_load // 16)
    rows = ep_count * capacity
    bf16, f32 = jnp.bfloat16, jnp.float32

    ids_all = lax.all_gather(expert_ids, "ep", axis=0, tiled=True)
    gates_all = lax.all_gather(gate_weights, "ep", axis=0, tiled=True)
    x_all = lax.all_gather(tokens, "ep", axis=0, tiled=True)
    dy_all = lax.all_gather(cotangent, "ep", axis=0, tiled=True)

    first = lax.axis_index("ep") * local_experts
    mine = first + jnp.arange(local_experts, dtype=jnp.int32)
    hits = ids_all[:, :, None] == mine[None, None, :]
    member = jnp.any(hits, axis=1)
    gate_of = jnp.sum(jnp.where(hits, gates_all[:, :, None].astype(f32), 0.0), axis=1)
    place = jnp.cumsum(member.astype(jnp.int32), axis=0) - 1
    place = jnp.where(member, place, rows)
    pick = (place.T[:, None, :] == jnp.arange(rows, dtype=jnp.int32)[None, :, None]).astype(bf16)

    def pick_rows(values):
        return jnp.einsum("brt,td->brd", pick, values, preferred_element_type=f32).astype(bf16)

    x_rows = pick_rows(x_all)
    gate_rows = jnp.einsum("brt,tb->br", pick, gate_of.astype(bf16), preferred_element_type=f32)[..., None]
    pre_act = jnp.einsum("brd,bdh->brh", x_rows, w_up, preferred_element_type=f32)
    sig = jax.nn.sigmoid(pre_act)
    hidden = (pre_act * sig).astype(bf16)
    slope = sig * (1.0 + pre_act * (1.0 - sig))
    dy_rows = pick_rows(dy_all)
    back_hidden = jnp.einsum("brd,bdh->brh", dy_rows, w_down, preferred_element_type=f32)
    gate_slots = jnp.sum(back_hidden * hidden.astype(f32), axis=2).astype(bf16)
    grad_pre = (gate_rows * back_hidden * slope).astype(bf16)
    scaled_cot = (gate_rows * dy_rows.astype(f32)).astype(bf16)
    partial_grad = jnp.einsum("brd,brh->bdh", scaled_cot, hidden, preferred_element_type=f32).astype(bf16)
    down_grad = lax.psum_scatter(partial_grad, "dp", scatter_dimension=1, tiled=True).astype(f32)
    route_grad = jnp.einsum("brh,bdh->brd", grad_pre, w_up, preferred_element_type=f32).astype(bf16)
    token_part = jnp.einsum("brt,brd->td", pick, route_grad, preferred_element_type=f32).astype(bf16)
    token_grad = lax.psum_scatter(token_part, "ep", scatter_dimension=0, tiled=True)
    gate_part = jnp.einsum("brt,br->tb", pick, gate_slots, preferred_element_type=f32)
    gate_part = jnp.sum(jnp.where(hits, gate_part[:, None, :], 0.0), axis=2).astype(bf16)
    gate_grad = lax.psum_scatter(gate_part, "ep", scatter_dimension=0, tiled=True)
    return (token_grad, gate_grad, down_grad)


def solution(mesh):
    return jax.shard_map(
        shards,
        mesh=mesh,
        in_specs=(
            P(("dp", "ep"), None),
            P(("dp", "ep"), None),
            P(("dp", "ep"), None),
            P(("dp", "ep"), None),
            P("ep", None, None),
            P("ep", None, None),
        ),
        out_specs=(P(("dp", "ep"), None), P(("dp", "ep"), None), P("ep", "dp", None)),
        check_vma=False,
    )
```

time: 427 us -> 288 us (0.67)
  blocking collectives: 105 us -> 28.9 us
  local copies, waits for them, and re-layouts: 63.6 us -> 2.48 us
  matrix products: 28.6 us -> 49.3 us
  starting transfers between devices: 19.6 us -> 0.38 us
  other arithmetic: 14.3 us -> 4.95 us
  waiting for transfers between devices: 181 us -> 188 us
    all_to_all x4 -> x0, waiting for transfers between devices: 181 us -> none  [the longest x1 91.9 us: shards(): lax.all_to_all(route_grad.reshape(slot_total, width), 'ep', split_axis=0,...]
    all_to_all x1 -> x0, blocking collectives: 105 us -> none  [shards(): lax.all_to_all(x_send, 'ep', split_axis=0, concat_axis=0, tiled=True)]
    reduce_scatter x1, waiting for transfers between devices: 0.01 us -> 70.1 us  [shards(): lax.psum_scatter(partial_grad, 'dp', scatter_dimension=1, tiled=True)]
    all_gather x0 -> x2, waiting for transfers between devices: none -> 59.3 us  [the longest x1 39.1 us: shards(): x_all = lax.all_gather(tokens, 'ep', axis=0, tiled=True)]
    reduce_scatter x0 -> x1, waiting for transfers between devices: none -> 49.6 us  [shards(): lax.psum_scatter(token_part, 'ep', scatter_dimension=0, tiled=True)]
    gather x5 -> x0, local copies, waits for them, and re-layouts: 37.2 us -> none  [the longest x1 11.7 us: shards(): back_grad[buffer_pos].reshape(tok_rows, top_count, width)]
    all_gather x0 -> x2, blocking collectives: none -> 28.9 us  [the longest x1 15.8 us: shards(): ids_all = lax.all_gather(expert_ids, 'ep', axis=0, tiled=True)]
    dot_general x5 -> x7, matrix products: 28.6 us -> 49.3 us  [the longest x1 12 us: shards(): jnp.einsum('brt,brd->td', pick, route_grad, preferred_element_type=f32)]
  transfers between devices with their start and end apart: 5 -> 5, of which waited for: 2 -> 5; matrix products, arithmetic and copies ran while one was open for 18% -> 13% of each run, Pallas kernels for 0% -> 0%
where the time goes in v1:
time: 288 us
  waiting for transfers between devices  188 us (65%)
  matrix products  49.3 us (17%)
  blocking collectives  28.9 us (10%)
  between operations  13.8 us (5%)
  other arithmetic  4.95 us (2%)
    reduce_scatter x1, waiting for transfers between devices, shards(): lax.psum_scatter(partial_grad, 'dp', scatter_dimension=1, tiled=True)  70.1 us
    reduce_scatter x1, waiting for transfers between devices, shards(): lax.psum_scatter(token_part, 'ep', scatter_dimension=0, tiled=True)  49.6 us
    all_gather x1, waiting for transfers between devices, shards(): x_all = lax.all_gather(tokens, 'ep', axis=0, tiled=True)  39.1 us
    all_gather x1, waiting for transfers between devices, shards(): dy_all = lax.all_gather(cotangent, 'ep', axis=0, tiled=True)  20.2 us
    all_gather x1, blocking collectives, shards(): ids_all = lax.all_gather(expert_ids, 'ep', axis=0, tiled=True)  15.8 us
    all_gather x1, blocking collectives, shards(): gates_all = lax.all_gather(gate_weights, 'ep', axis=0, tiled=True)  13.1 us
    dot_general x1, matrix products, shards(): jnp.einsum('brt,brd->td', pick, route_grad, preferred_element_type=f32)  12 us
    dot_general x1, matrix products, shards(): jnp.einsum('brd,bdh->brh', x_rows, w_up, preferred_element_type=f32)  11.1 us
  transfers between devices with their start and end apart: 5, of which 5 were waited for; matrix products, arithmetic and copies ran while one was open for 13% of the time, Pallas kernels for 0%

profile of v1, /device:TPU:0, one launch (start us, length us, event | category | flops | bytes accessed | tf_op | source)
XLA Modules:
  0.0 287.8 jit_solution(15530063018952749945)
XLA Ops:
  7.2 0.0 all-gather.3.cloned.1.call-start
  7.2 0.7 all-gather.3.cloned.1.call-update
  7.9 0.0 all-gather.5.cloned.1.call-start
  7.9 0.7 all-gather.5.cloned.1.call-update
  8.6 0.0 reduce-scatter.10.cloned.1.call-start
  8.7 15.8 %all_gather.12 = s32[1024,8]{0,1:T(8,128)S(1)} all-gather(s32[128,8]{0,1:T(8,128)} %param.8), channel_id=1, replica_groups=mesh['dp'=4,'ep'=8] {'ep'}, dimensions={0}, use_global_device_ids=true | all-gather | bytes 36864 | tf_op jit(solution)/shard_map/all_gather | solution.py:18
  24.5 0.1 compare_reduce_fusion
  24.7 1.1 reduce-window.6
  25.8 0.2 slice_reduce_fusion
  26.0 0.2 reduce-window.9
  26.2 13.1 %all_gather.13 = bf16[1024,8]{0,1:T(8,128)(2,1)S(1)} all-gather(bf16[128,8]{0,1:T(8,128)(2,1)} %param.9), channel_id=1, replica_groups=mesh['dp'=4,'ep'=8] {'ep'}, dimensions={0}, use_global_device_ids=true | all-gather | bytes 18432 | tf_op jit(solution)/shard_map/all_gather | solution.py:19
  39.3 0.1 add_bitcast_fusion
  39.4 20.2 %all-gather.3.cloned.1.call-done = bf16[1024,2048]{1,0:T(8,128)(2,1)} async-done(((bf16[128,2048]{1,0:T(8,128)(2,1)}), bf16[1024,2048]{1,0:T(8,128)(2,1)}) %all-gather.3.cloned.1.call-update) | async-done | bytes 4194320 | tf_op jit(solution)/shard_map/all_gather | solution.py:21
  59.6 8.6 %fusion.11 = bf16[4,272,2048]{2,1,0:T(8,128)(2,1)} fusion(bf16[1024,2048]{1,0:T(8,128)(2,1)} %all-gather.3.cloned.1.call-done, s32[4,1024]{1,0:T(4,128)S(1)} %bitcast_select_fusion), kind=kOutput, calls=%fused_computation.15 | convolution fusion | flops 4566745088 | bytes 8667136 | tf_op jit(solution)/shard_map/brt,td->brd/dot_general | solution.py:33
  68.1 39.1 %all-gather.5.cloned.1.call-done = bf16[1024,2048]{1,0:T(8,128)(2,1)} async-done(((bf16[128,2048]{1,0:T(8,128)(2,1)}), bf16[1024,2048]{1,0:T(8,128)(2,1)}) %all-gather.5.cloned.1.call-update) | async-done | bytes 4194320 | tf_op jit(solution)/shard_map/all_gather | solution.py:20
  107.2 11.1 %fusion.3 = f32[4,272,384]{2,1,0:T(8,128)S(1)} fusion(bf16[4,2048,384]{2,1,0:T(8,128)(2,1)} %param.10, bf16[1024,2048]{1,0:T(8,128)(2,1)} %all-gather.5.cloned.1.call-done, s32[4,1024]{1,0:T(4,128)S(1)} %bitcast_select_fusion), kind=kOutput, calls=%fused_computation.6 | convolution fusion | flops 6278021120 | bytes 12173312 | tf_op jit(solution)/shard_map/brd,bdh->brh/dot_general | solution.py:37
  118.3 6.8 %multiply_reduce_fusion = (bf16[4,272]{1,0:T(4,128)(2,1)S(1)}, f32[4,272,384]{2,1,0:T(8,128)S(1)}) fusion(f32[4,272,384]{2,1,0:T(8,128)S(1)} %fusion.3, bf16[4,272,2048]{2,1,0:T(8,128)(2,1)} %fusion.11, bf16[4,2048,384]{2,1,0:T(8,128)(2,1)} %param.11), kind=kOutput, calls=%fused_computation.22 | convolution fusion | flops 1714617344 | bytes 14092416 | tf_op jit(solution)/shard_map/brd,bdh->brh/dot_general | solution.py:42
  125.1 0.8 fusion.5
  125.9 0.1 fusion.32
  126.0 0.8 fusion.8
  126.8 0.8 copy.19
  127.7 0.0 reduce-scatter.10.cloned.1.call-update
  127.7 0.2 reduce-scatter.8.cloned.1.call-start
  127.9 9.2 %convolution_convert_fusion = bf16[4,2048,384]{2,1,0:T(8,128)(2,1)} fusion(bf16[4,272,2048]{2,1,0:T(8,128)(2,1)} %fusion.11, f32[4,272]{1,0:T(4,128)S(1)} %bitcast.50, f32[4,272,384]{2,1,0:T(8,128)S(1)} %fusion.3), kind=kOutput, calls=%fused_computation.2 | convolution fusion | flops 1723195392 | bytes 12423424 | tf_op jit(solution)/shard_map/brd,brh->bdh/dot_general | solution.py:46
  137.2 0.0 reduce-scatter.8.cloned.1.call-update
  137.2 0.0 reduce-scatter.6.cloned.1.call-start
  137.2 12.0 %bitcast_convert_fusion = bf16[1024,2048]{1,0:T(8,128)(2,1)} fusion(bf16[4,2048,384]{2,1,0:T(8,128)(2,1)} %param.10, s32[4,1024]{1,0:T(4,128)S(1)} %bitcast_select_fusion, f32[4,272,384]{2,1,0:T(8,128)S(1)} %fusion.3, f32[4,272,384]{2,1,0:T(8,128)S(1)} %get-tuple-element.6, f32[4,272]{1,0:T(4,128)S(1)} %bitcast.51), kind=kOutput, calls=%fused_computation.1 | convolution fusion | flops 6284296192 | bytes 13848832 | tf_op jit(solution)/shard_map/brt,brd->td/dot_general | solution.py:49
  149.2 0.0 reduce-scatter.6.cloned.1.call-update
  149.3 7.7 %reduce-scatter.10.cloned.1.call-done = bf16[128,8]{1,0:T(8,128)(2,1)} async-done(((bf16[1024,8]{1,0:T(8,128)(2,1)}), bf16[128,8]{1,0:T(8,128)(2,1)}) %reduce-scatter.10.cloned.1.call-update) | async-done | bytes 2064
  157.0 1.4 copy.20
  158.4 70.1 %reduce-scatter.8.cloned.1.call-done = bf16[4,512,384]{2,1,0:T(8,128)(2,1)} async-done(((bf16[4,2048,384]{2,1,0:T(8,128)(2,1)}), bf16[4,512,384]{2,1,0:T(8,128)(2,1)}) %reduce-scatter.8.cloned.1.call-update) | async-done | bytes 1572880 | tf_op jit(solution)/shard_map/reduce_scatter | solution.py:47
  228.5 3.3 %convert_element_type.63 = f32[4,512,384]{2,1,0:T(8,128)} convert(bf16[4,512,384]{2,1,0:T(8,128)(2,1)} %reduce-scatter.8.cloned.1.call-done) | non-fusion elementwise | flops 786432 | bytes 4718592 | tf_op jit(solution)/shard_map/convert_element_type | solution.py:47
  231.8 49.6 %reduce-scatter.6.cloned.1.call-done = bf16[128,2048]{1,0:T(8,128)(2,1)} async-done(((bf16[1024,2048]{1,0:T(8,128)(2,1)}), bf16[128,2048]{1,0:T(8,128)(2,1)}) %reduce-scatter.6.cloned.1.call-update) | async-done | bytes 524304 | tf_op jit(solution)/shard_map/reduce_scatter | solution.py:50
  (7 shorter events, 0.0 us)
Async XLA Ops:
  7.2 52.4 %all-gather.3.cloned.1.call-start = ((), (), s32[]{:S(2)}) async-start(), calls=%async_computation.3 | async-start | bytes 4718592 | tf_op jit(solution)/shard_map/all_gather | solution.py:21
  7.9 99.3 %all-gather.5.cloned.1.call-start = ((), (), s32[]{:S(2)}) async-start(), calls=%async_computation.4 | async-start | bytes 4718592 | tf_op jit(solution)/shard_map/all_gather | solution.py:20
  8.6 148.3 %reduce-scatter.10.cloned.1.call-start = ((), (), s32[]{:S(2)}) async-start(), calls=%async_computation.7 | async-start | bytes 294912
  127.7 100.8 %reduce-scatter.8.cloned.1.call-start = ((), (), s32[]{:S(2)}) async-start(), calls=%async_computation.6 | async-start | bytes 7864320 | tf_op jit(solution)/shard_map/reduce_scatter | solution.py:47
  137.2 144.1 %reduce-scatter.6.cloned.1.call-start = ((), (), s32[]{:S(2)}) async-start(), calls=%async_computation.5 | async-start | bytes 4718592 | tf_op jit(solution)/shard_map/reduce_scatter | solution.py:50
Sparse Core Ops, SparseCore 0:
  9.6 49.9 all-gather.2
  61.2 45.9 all-gather.4
  127.8 29.0 reduce-scatter.9
  160.1 68.3 reduce-scatter.7
  231.3 49.9 reduce-scatter.5

commit v2 on v1

v2 whole, which is shorter than its diff:
```python
import functools

import jax
import jax.numpy as jnp
from jax import lax
from jax.experimental import pallas as pl
from jax.experimental.pallas import tpu as pltpu
from jax.sharding import PartitionSpec as P

LANES = 128
SLICES = 2
VMEM_LIMIT = 60 * 1024 * 1024
bf16, f32 = jnp.bfloat16, jnp.float32
ANY = pl.BlockSpec(memory_space=pl.ANY)
VMEM = pl.BlockSpec(memory_space=pltpu.VMEM)
SMEM = pl.BlockSpec(memory_space=pltpu.SMEM)


def pick_block(place, slot, chips, mine, other, act):
    left, even = place[0] >= slot, place[1] == 0
    for is_left in (True, False):
        for is_even in (True, False):
            step = slot if is_left else chips - slot
            ref = (mine if is_left == is_even else other)[step - 1]

            @pl.when((left == is_left) & (even == is_even))
            def _():
                act(ref)


def start_blocks(place, chips, own, mine, other, dst, sem):
    rows = own.shape[0]
    pltpu.make_async_copy(own, dst.at[pl.ds(0, rows), :], sem.at[0]).start()
    for slot in range(1, chips):
        target = dst.at[pl.ds(slot * rows, rows), :]
        pick_block(
            place, slot, chips, mine, other,
            lambda ref: pltpu.make_async_copy(ref, target, sem.at[slot]).start(),
        )


def wait_blocks(chips, own, dst, sem):
    rows = own.shape[0]
    for slot in range(chips):
        pltpu.make_async_copy(own, dst.at[pl.ds(slot * rows, rows), :], sem.at[slot]).wait()


def weight_copies(weights, dst, sem, pieces):
    experts, _, hidden = weights.shape
    copies = []
    for b in range(experts):
        for start, size, to in pieces:
            copies.append(
                pltpu.make_async_copy(
                    weights.at[b, pl.ds(start, size), :],
                    dst.at[pl.ds(to, size), pl.ds(b * hidden, hidden)],
                    sem,
                )
            )
    return copies


def run_all(copies):
    for copy in copies:
        copy.start()
    return copies


def wait_all(copies):
    for copy in copies:
        copy.wait()


def row_tile(total):
    return 512 if total % 512 == 0 else total


def up_kernel(chips, experts, hidden, width, top, place, own, *refs):
    mine, other = refs[: chips - 1], refs[chips - 1 : 2 * chips - 2]
    w_up, hid, scaled, slope_g, meta, rows_v, w_v, sem, w_sem = refs[2 * chips - 2 :]
    loads = run_all(weight_copies(w_up, w_v, w_sem, ((0, width, 0),)))
    start_blocks(place, chips, own, mine, other, rows_v, sem)
    wait_blocks(chips, own, rows_v, sem)
    wait_all(loads)
    total = rows_v.shape[0]
    tile = row_tile(total)
    lane = lax.broadcasted_iota(jnp.int32, (tile, LANES), 1)
    first = place[2] * experts

    def step(i, carry):
        at = pl.ds(pl.multiple_of(i * tile, tile), tile)
        info = rows_v[at, pl.ds(width, LANES)].astype(f32)
        meta[at, :] = info
        ids = jnp.where(lane < top, info, -1.0)
        gates = pltpu.roll(info, LANES - top, 1)
        pair = 2 if experts % 2 == 0 else 1
        for b0 in range(0, experts, pair):
            pre = jnp.dot(
                rows_v[at, pl.ds(0, width)],
                w_v[:, pl.ds(b0 * hidden, pair * hidden)],
                preferred_element_type=f32,
            )
            for b in range(b0, b0 + pair):
                hit = ids == (first + b).astype(f32)
                gate = jnp.sum(jnp.where(hit, gates, 0.0), axis=1, keepdims=True)
                part = pre[:, (b - b0) * hidden : (b - b0 + 1) * hidden]
                sig = 1.0 / (1.0 + jnp.exp(-part))
                act = part * sig
                cols = pl.ds(b * hidden, hidden)
                hid[at, cols] = act.astype(bf16)
                scaled[at, cols] = (gate * act).astype(bf16)
                slope_g[at, cols] = (gate * (sig * (1.0 + part * (1.0 - sig)))).astype(bf16)
        return carry

    lax.fori_loop(0, total // tile, step, 0)


def back_kernel(chips, experts, hidden, top, pieces, last, place, own, *refs):
    mine, other = refs[: chips - 1], refs[chips - 1 : 2 * chips - 2]
    refs = refs[2 * chips - 2 :]
    w_down, refs = refs[0], refs[1:]
    before = None
    if last:
        if last == 2:
            before, refs = refs[0], refs[1:]
        hid, slope_g, meta, grad_pre, gate_back, rows_v, w_v, sem, w_sem = refs
    else:
        if last is None:
            before, refs = refs[0], refs[1:]
        out, rows_v, w_v, sem, w_sem = refs
    loads = run_all(weight_copies(w_down, w_v, w_sem, pieces))
    start_blocks(place, chips, own, mine, other, rows_v, sem)
    wait_blocks(chips, own, rows_v, sem)
    wait_all(loads)
    total = rows_v.shape[0]
    tile = row_tile(total)
    lane = lax.broadcasted_iota(jnp.int32, (tile, LANES), 1)
    first = place[2] * experts

    def step(i, carry):
        at = pl.ds(pl.multiple_of(i * tile, tile), tile)
        if last:
            ids = jnp.where(lane < top, meta[at, :], -1.0)
            picked = jnp.zeros((tile, LANES), f32)
        pair = 2 if experts % 2 == 0 else 1
        for b0 in range(0, experts, pair):
            both = pl.ds(b0 * hidden, pair * hidden)
            back = jnp.dot(rows_v[at, :], w_v[:, both], preferred_element_type=f32)
            if before is not None:
                back = back + before[at, both]
            if not last:
                out[at, both] = back
                continue
            for b in range(b0, b0 + pair):
                cols = pl.ds(b * hidden, hidden)
                part = back[:, (b - b0) * hidden : (b - b0 + 1) * hidden]
                grad_pre[at, cols] = (part * slope_g[at, cols].astype(f32)).astype(bf16)
                gate = jnp.sum(part * hid[at, cols].astype(f32), axis=1, keepdims=True)
                picked = picked + jnp.where(ids == (first + b).astype(f32), gate, 0.0)
        if last:
            gate_back[at, :] = picked.astype(bf16)
        return carry

    lax.fori_loop(0, total // tile, step, 0)


def down_kernel(chips, experts, hidden, place, own, *refs):
    mine, other = refs[: chips - 1], refs[chips - 1 : 2 * chips - 2]
    scaled, out, rows_v, sem = refs[2 * chips - 2 :]
    start_blocks(place, chips, own, mine, other, rows_v, sem)
    wait_blocks(chips, own, rows_v, sem)
    width = rows_v.shape[1]
    tile = 256 if width % 256 == 0 else LANES
    for b in range(experts):

        def step(i, carry):
            at = pl.ds(pl.multiple_of(i * tile, tile), tile)
            out[b, at, :] = lax.dot_general(
                rows_v[:, at], scaled[:, pl.ds(b * hidden, hidden)],
                (((0,), (0,)), ((), ())), preferred_element_type=f32,
            ).astype(bf16)
            return carry

        lax.fori_loop(0, width // tile, step, 0)


def token_kernel(chips, pieces, extra, place, *refs):
    grad_pre, refs = refs[0], refs[1:]
    if extra:
        gate_back, refs = refs[0], refs[1:]
    w_up, own, refs = refs[0], refs[1], refs[2:]
    mine, other = refs[: chips - 1], refs[chips - 1 : 2 * chips - 2]
    w_v, rows_v, sem, w_sem = refs[2 * chips - 2 :]
    loads = run_all(weight_copies(w_up, w_v, w_sem, pieces))
    rows, width = own.shape[0], w_v.shape[0]
    if extra:
        rows_v[:, pl.ds(width, LANES)] = gate_back[...]
    wait_all(loads)
    for slot in reversed(range(chips)):
        at = pl.ds(slot * rows, rows)
        rows_v[at, pl.ds(0, width)] = lax.dot_general(
            grad_pre[at, :], w_v[...], (((1,), (1,)), ((), ())), preferred_element_type=f32
        ).astype(bf16)
        source = rows_v.at[at, :]
        if slot == 0:
            pltpu.make_async_copy(source, own, sem.at[0]).start()
        else:
            pick_block(
                place, slot, chips, mine, other,
                lambda ref: pltpu.make_async_copy(source, ref, sem.at[slot]).start(),
            )
    for slot in range(chips):
        pltpu.make_async_copy(rows_v.at[pl.ds(slot * rows, rows), :], own, sem.at[slot]).wait()


def cost(flops, nbytes):
    return pl.CostEstimate(flops=int(flops), bytes_accessed=int(nbytes), transcendentals=0)


def params():
    return pltpu.CompilerParams(vmem_limit_bytes=VMEM_LIMIT)


def shards(tokens, cotangent, expert_ids, gate_weights, w_up, w_down):
    tok_rows, width = tokens.shape
    top = expert_ids.shape[1]
    ep_count, dp_count = lax.axis_size("ep"), lax.axis_size("dp")
    experts, _, hidden = w_up.shape
    chips = ep_count // 2
    total = ep_count * tok_rows
    inner = experts * hidden
    here = lax.axis_index("ep")
    place = jnp.stack([here // 2, here % 2, here]).astype(jnp.int32)
    swap = [(p, p ^ 1) for p in range(ep_count)]

    def reach(p, step):
        return p + 2 * step if p % 2 == 0 else p - 2 * step

    def inside(p):
        return 0 <= p < ep_count

    def gather(own):
        block = jnp.concatenate([own, lax.ppermute(own, "ep", swap)], axis=0)
        mine, other, held = [], [], block
        for step in range(1, chips):
            pairs = [(p, reach(p, 1)) for p in range(ep_count) if inside(reach(p, 1)) and inside(reach(p, 1 - step))]
            held = lax.ppermute(held, "ep", pairs)
            mine.append(held)
            other.append(lax.ppermute(held, "ep", [(p, p ^ 1) for p in range(ep_count) if inside(reach(p, -step))]))
        return block, mine, other

    def scatter(own, mine, other):
        carry = None
        for step in range(chips - 1, 0, -1):
            swapped = lax.ppermute(other[step - 1], "ep", [(p, p ^ 1) for p in range(ep_count) if inside(reach(p ^ 1, -step))])
            held = mine[step - 1].astype(f32) + swapped.astype(f32)
            if carry is not None:
                held = held + carry.astype(f32)
            carry = lax.ppermute(
                held.astype(bf16), "ep", [(p, reach(p, -1)) for p in range(ep_count) if inside(reach(p, -step))]
            )
        block = own.astype(f32)
        if carry is not None:
            block = block + carry.astype(f32)
        given = lax.ppermute(block[tok_rows:].astype(bf16), "ep", swap)
        return (block[:tok_rows] + given.astype(f32)).astype(bf16)

    info = jnp.concatenate(
        [expert_ids.astype(bf16), gate_weights, jnp.zeros((tok_rows, LANES - 2 * top), bf16)], axis=1
    )
    x_blocks = gather(jnp.concatenate([tokens, info], axis=1))
    share = width // dp_count
    piece = share // SLICES
    cut = cotangent.reshape(tok_rows, dp_count, SLICES, piece)
    dy_blocks = [gather(cut[:, :, s].reshape(tok_rows, dp_count * piece)) for s in range(SLICES)]

    def flat(blocks):
        return (blocks[0], *blocks[1], *blocks[2])

    many = 2 * chips - 1
    full = width + LANES
    hid, scaled, slope_g, meta = pl.pallas_call(
        functools.partial(up_kernel, chips, experts, hidden, width, top),
        in_specs=[SMEM] + [ANY] * (many + 1),
        out_specs=[VMEM] * 4,
        out_shape=[jax.ShapeDtypeStruct((total, inner), bf16)] * 3 + [jax.ShapeDtypeStruct((total, LANES), f32)],
        scratch_shapes=[
            pltpu.VMEM((total, full), bf16),
            pltpu.VMEM((width, inner), bf16),
            pltpu.SemaphoreType.DMA((chips,)),
            pltpu.SemaphoreType.DMA,
        ],
        compiler_params=params(),
        cost_estimate=cost(2 * total * width * inner, 2 * (total * full + width * inner + 3 * total * inner)),
        name="up",
    )(place, *flat(x_blocks), w_up)

    down_parts, before = [], None
    for s in range(SLICES):
        cols = dp_count * piece
        pieces = tuple((i * share + s * piece, piece, i * piece) for i in range(dp_count))
        last = s == SLICES - 1
        mode = (2 if s else 1) if last else (None if s else 0)
        ins = [place, *flat(dy_blocks[s]), w_down]
        specs = [SMEM] + [ANY] * (many + 1)
        if s:
            ins.append(before)
            specs.append(VMEM)
        if last:
            ins += [hid, slope_g, meta]
            specs += [VMEM] * 3
            outs = [jax.ShapeDtypeStruct((total, inner), bf16), jax.ShapeDtypeStruct((total, LANES), bf16)]
        else:
            outs = [jax.ShapeDtypeStruct((total, inner), f32)]
        result = pl.pallas_call(
            functools.partial(back_kernel, chips, experts, hidden, top, pieces, mode),
            in_specs=specs,
            out_specs=[VMEM] * len(outs),
            out_shape=outs,
            scratch_shapes=[
                pltpu.VMEM((total, cols), bf16),
                pltpu.VMEM((cols, inner), bf16),
                pltpu.SemaphoreType.DMA((chips,)),
                pltpu.SemaphoreType.DMA,
            ],
            compiler_params=params(),
            cost_estimate=cost(2 * total * cols * inner, 2 * (total * cols + cols * inner + 4 * total * inner)),
            name="back",
        )(*ins)
        if last:
            grad_pre, gate_back = result
        else:
            (before,) = result
        down_parts.append(
            pl.pallas_call(
                functools.partial(down_kernel, chips, experts, hidden),
                in_specs=[SMEM] + [ANY] * many + [VMEM],
                out_specs=VMEM,
                out_shape=jax.ShapeDtypeStruct((experts, cols, hidden), bf16),
                scratch_shapes=[pltpu.VMEM((total, cols), bf16), pltpu.SemaphoreType.DMA((chips,))],
                compiler_params=params(),
                cost_estimate=cost(2 * total * cols * inner, 2 * (total * cols + total * inner + cols * inner)),
                name="down",
            )(place, *flat(dy_blocks[s]), scaled)
        )

    token_parts = []
    half = width // SLICES
    for s in range(SLICES):
        extra = s == 0
        cols = half + (LANES if extra else 0)
        outs = pl.pallas_call(
            functools.partial(token_kernel, chips, ((s * half, half, 0),), extra),
            in_specs=[SMEM] + [VMEM] * (2 if extra else 1) + [ANY],
            out_specs=[ANY] * many,
            out_shape=[jax.ShapeDtypeStruct((2 * tok_rows, cols), bf16)] * many,
            scratch_shapes=[
                pltpu.VMEM((half, inner), bf16),
                pltpu.VMEM((total, cols), bf16),
                pltpu.SemaphoreType.DMA((chips,)),
                pltpu.SemaphoreType.DMA,
            ],
            compiler_params=params(),
            cost_estimate=cost(2 * total * half * inner, 2 * (total * cols + total * inner + half * inner)),
            name="token",
        )(place, grad_pre, *((gate_back,) if extra else ()), w_up)
        token_parts.append(scatter(outs[0], outs[1:chips], outs[chips:]))

    gate_grad = token_parts[0][:, half : half + top]
    token_grad = jnp.concatenate([token_parts[0][:, :half]] + token_parts[1:], axis=1)
    down_grad = jnp.concatenate(
        [lax.psum_scatter(part, "dp", scatter_dimension=1, tiled=True) for part in down_parts], axis=1
    ).astype(f32)
    return (token_grad, gate_grad, down_grad)


def solution(mesh):
    return jax.shard_map(
        shards,
        mesh=mesh,
        in_specs=(
            P(("dp", "ep"), None),
            P(("dp", "ep"), None),
            P(("dp", "ep"), None),
            P(("dp", "ep"), None),
            P("ep", None, None),
            P("ep", None, None),
        ),
        out_specs=(P(("dp", "ep"), None), P(("dp", "ep"), None), P("ep", "dp", None)),
        check_vma=False,
    )
```

time: 288 us -> 279 us (0.969)
  waiting for transfers between devices: 188 us -> 78.1 us
  starting transfers between devices: 0.38 us -> 87.6 us
  Pallas kernels: 0 us -> 82.5 us
  matrix products: 49.3 us -> 0 us
  blocking collectives: 28.9 us -> 0 us
  local copies, waits for them, and re-layouts: 2.48 us -> 7.56 us
    reduce_scatter x2, waiting for transfers between devices: 120 us -> 0.01 us  [shards(): lax.psum_scatter(part, 'dp', scatter_dimension=1, tiled=True)]
    ppermute x0 -> x35, starting transfers between devices: none -> 87.5 us  [the longest x3 31.4 us: gather(): block = jnp.concatenate([own, lax.ppermute(own, 'ep', swap)], axis=0)]
    pallas_call x0 -> x7, Pallas kernels: none -> 82.5 us  [the longest x2 25.9 us: shards(): pl.pallas_call(functools.partial(down_kernel, chips, experts, hidden), in...]
    ppermute x0 -> x35, waiting for transfers between devices: none -> 78.1 us  [the longest x6 31.9 us: scatter(): lax.ppermute(held.astype(bf16), 'ep', [(p, reach(p, -1)) for p in range(e...]
    all_gather x2 -> x0, waiting for transfers between devices: 59.3 us -> none  [the longest x1 39.1 us: shards(): x_all = lax.all_gather(tokens, 'ep', axis=0, tiled=True)]
    dot_general x7 -> x0, matrix products: 49.3 us -> none  [the longest x1 12 us: shards(): jnp.einsum('brt,brd->td', pick, route_grad, preferred_element_type=f32)]
    all_gather x2 -> x0, blocking collectives: 28.9 us -> none  [the longest x1 15.8 us: shards(): ids_all = lax.all_gather(expert_ids, 'ep', axis=0, tiled=True)]
    unnamed x6 -> x2, waiting for transfers between devices: 9.12 us -> 0.03 us
  transfers between devices with their start and end apart: 5 -> 37, of which waited for: 5 -> 14; matrix products, arithmetic and copies ran while one was open for 13% -> 2% of each run, Pallas kernels for 0% -> 25%
where the time goes in v2:
time: 279 us; the launch traced here: 278 us
  starting transfers between devices  87.6 us (31%)
  Pallas kernels  82.5 us (30%)
  waiting for transfers between devices  78.1 us (28%)
  between operations  15 us (5%)
  local copies, waits for them, and re-layouts  7.56 us (3%)
  other arithmetic  7.11 us (3%)
    ppermute x6, waiting for transfers between devices, scatter(): lax.ppermute(held.astype(bf16), 'ep', [(p, reach(p, -1)) for p in range(e...  31.9 us
    ppermute x3, starting transfers between devices, gather(): block = jnp.concatenate([own, lax.ppermute(own, 'ep', swap)], axis=0)  31.4 us
    pallas_call x2, Pallas kernels, shards(): pl.pallas_call(functools.partial(down_kernel, chips, experts, hidden), in...  25.9 us
    pallas_call x2, Pallas kernels, shards(): pl.pallas_call(functools.partial(back_kernel, chips, experts, hidden, top...  22.8 us
    ppermute x9, waiting for transfers between devices, gather(): held = lax.ppermute(held, 'ep', pairs)  21.4 us
    ppermute x6, starting transfers between devices, scatter(): lax.ppermute(other[step - 1], 'ep', [(p, p ^ 1) for p in range(ep_count)...  19.8 us
    ppermute x9, waiting for transfers between devices, gather(): lax.ppermute(held, 'ep', [(p, p ^ 1) for p in range(ep_count) if inside(r...  19.4 us
    ppermute x9, starting transfers between devices, gather(): held = lax.ppermute(held, 'ep', pairs)  18.6 us
  transfers between devices with their start and end apart: 37, of which 14 were waited for; matrix products, arithmetic and copies ran while one was open for 2% of the time, Pallas kernels for 25%

profile of v2, /device:TPU:0, one launch (start us, length us, event | category | flops | bytes accessed | tf_op | source)
XLA Modules:
  0.0 277.8 jit_solution(1508383980195538655)
XLA Ops:
  8.8 1.2 concatenate.20
  10.5 1.6 collective-permute-done.14
  12.2 5.9 %collective-permute-start.15 = (bf16[256,2176]{1,0:T(8,128)(2,1)S(1)}, bf16[256,2176]{1,0:T(8,128)(2,1)}, u32[]{:S(2)}, u32[]{:S(2)}) collective-permute-start(bf16[256,2176]{1,0:T(8,128)(2,1)S(1)} %pad_maximum_fusion.own), channel_id=1, source_target_pairs={{0,2},{2,4},{3,1},{4,6},{5,3},{7,5},{8,10},{10,12},{11,9},{12,14},... | collective-permute-start | bytes 3342344 | tf_op jit(solution)/shard_map/ppermute | solution.py:247
  18.1 12.0 %collective-permute-done.15.refs_0_ = bf16[256,2176]{1,0:T(8,128)(2,1)} collective-permute-done((bf16[256,2176]{1,0:T(8,128)(2,1)S(1)}, bf16[256,2176]{1,0:T(8,128)(2,1)}, u32[]{:S(2)}, u32[]{:S(2)}) %collective-permute-start.15) | collective-permute-done | bytes 1114144 | tf_op jit(solution)/shard_map/ppermute | solution.py:247
  30.1 1.7 collective-permute-start.16
  32.1 1.7 collective-permute-start.17
  33.8 2.5 slice_reduce_fusion
  36.3 14.3 %collective-permute-start.7 = (bf16[128,1024]{1,0:T(8,128)(2,1)S(1)}, bf16[128,1024]{1,0:T(8,128)(2,1)S(1)}, u32[]{:S(2)}, u32[]{:S(2)}) collective-permute-start(bf16[128,1024]{1,0:T(8,128)(2,1)S(1)} %bitcast.7), channel_id=1, source_target_pairs={{0,1},{1,0},{2,3},{3,2},{4,5},{5,4},{6,7},{7,6},{8,9},{9,8},{10,11... | collective-permute-start | bytes 786440 | tf_op jit(solution)/shard_map/ppermute | solution.py:243
  50.6 1.1 collective-permute-done.7
  51.8 5.4 %collective-permute-start.8 = (bf16[256,1024]{1,0:T(8,128)(2,1)S(1)}, bf16[256,1024]{1,0:T(8,128)(2,1)S(1)}, u32[]{:S(2)}, u32[]{:S(2)}) collective-permute-start(bf16[256,1024]{1,0:T(8,128)(2,1)S(1)} %constant_dynamic-update-slice_fusion.2.own), channel_id=1, source_target_pairs={{0,2},{2,4},{3,1},{4,6},{5,3},{7,5},{8,10},{10,12},{11,9},{12,14},... | collective-permute-start | bytes 1572872 | tf_op jit(solution)/shard_map/ppermute | solution.py:247
  57.2 1.3 collective-permute-start.18
  58.5 1.3 collective-permute-start.19
  59.8 1.3 collective-permute-start.20
  61.1 2.7 collective-permute-done.8.refs_0_
  65.8 1.3 collective-permute-start.11
  67.1 1.3 collective-permute-start.12
  68.5 1.3 collective-permute-start.13
  69.8 17.4 %up.1 = (bf16[1024,1536]{1,0:T(8,128)(2,1)}, bf16[1024,1536]{1,0:T(8,128)(2,1)}, bf16[1024,1536]{1,0:T(8,128)(2,1)}, f32[1024,128]{1,0:T(8,128)}) custom-call(s32[3]{0:T(128)} %pad_add_fusion.place, bf16[256,2176]{1,0:T(8,128)(2,1)} %copy-done.2, bf16[256,2176]{1,0:T(8,128)(2,1)} %collective-permute-done.15.refs_0_, ...), custom_call_target="tpu_custom_call" | custom-call | flops 6442450944 | bytes 20185088 | tf_op jit(solution)/shard_map/up/pallas_call | solution.py:282
  87.2 4.1 %collective-permute-done.12.refs_4_ = bf16[256,1024]{1,0:T(8,128)(2,1)S(1)} collective-permute-done((bf16[256,1024]{1,0:T(8,128)(2,1)S(1)}, bf16[256,1024]{1,0:T(8,128)(2,1)S(1)}, u32[]{:S(2)}, u32[]{:S(2)}) %collective-permute-start.12) | collective-permute-done | bytes 524320 | tf_op jit(solution)/shard_map/ppermute | solution.py:249
  91.3 1.3 collective-permute-done.13.refs_5_
  93.5 12.9 %down.2 = bf16[4,1024,384]{2,1,0:T(8,128)(2,1)} custom-call(s32[3]{0:T(128)} %pad_add_fusion.place, bf16[256,1024]{1,0:T(8,128)(2,1)} %copy-done, bf16[256,1024]{1,0:T(8,128)(2,1)} %copy-done.7, bf16[256,1024]{1,0:T(8,128)(2,1)} %copy-done.8, bf16[256,1024]{1,0:T(8,128)(2,1)} %copy-done.9, bf16[256,1024]{1,0:T(8,128)(2,1)} %copy-done.10, ...), custom_call_target="tpu_custom_call" | custom-call | flops 3221225472 | bytes 8388608 | tf_op jit(solution)/shard_map/down/pallas_call | solution.py:335
  106.6 16.5 %collective-permute-start = (bf16[128,1024]{1,0:T(8,128)(2,1)S(1)}, bf16[128,1024]{1,0:T(8,128)(2,1)S(1)}, u32[]{:S(2)}, u32[]{:S(2)}) collective-permute-start(bf16[128,1024]{1,0:T(8,128)(2,1)S(1)} %bitcast.9), channel_id=1, source_target_pairs={{0,1},{1,0},{2,3},{3,2},{4,5},{5,4},{6,7},{7,6},{8,9},{9,8},{10,11... | collective-permute-start | bytes 786440 | tf_op jit(solution)/shard_map/ppermute | solution.py:243
  123.1 1.1 collective-permute-done
  124.3 1.3 collective-permute-start.1
  125.6 6.6 %collective-permute-done.1.refs_0_ = bf16[256,1024]{1,0:T(8,128)(2,1)S(1)} collective-permute-done((bf16[256,1024]{1,0:T(8,128)(2,1)S(1)}, bf16[256,1024]{1,0:T(8,128)(2,1)S(1)}, u32[]{:S(2)}, u32[]{:S(2)}) %collective-permute-start.1) | collective-permute-done | bytes 524320 | tf_op jit(solution)/shard_map/ppermute | solution.py:247
  133.7 1.3 collective-permute-start.4
  135.0 1.3 collective-permute-start.5
  136.3 1.5 collective-permute-start.6
  137.8 9.5 %back.2.refs_7_ = f32[1024,1536]{1,0:T(8,128)} custom-call(s32[3]{0:T(128)} %pad_add_fusion.place, bf16[256,1024]{1,0:T(8,128)(2,1)} %copy-done, bf16[256,1024]{1,0:T(8,128)(2,1)} %copy-done.7, bf16[256,1024]{1,0:T(8,128)(2,1)} %copy-done.8, bf16[256,1024]{1,0:T(8,128)(2,1)} %copy-done.9, bf16[256,1024]{1,0:T(8,128)(2,1)} %copy-done.10, ...), custom_call_target="tpu_custom_call" | custom-call | flops 3221225472 | bytes 17825792 | tf_op jit(solution)/shard_map/back/pallas_call | solution.py:315
  147.4 5.3 %collective-permute-done.4.refs_3_ = bf16[256,1024]{1,0:T(8,128)(2,1)S(1)} collective-permute-done((bf16[256,1024]{1,0:T(8,128)(2,1)S(1)}, bf16[256,1024]{1,0:T(8,128)(2,1)S(1)}, u32[]{:S(2)}, u32[]{:S(2)}) %collective-permute-start.4) | collective-permute-done | bytes 524320 | tf_op jit(solution)/shard_map/ppermute | solution.py:249
  152.7 1.3 collective-permute-done.5.refs_4_
  154.0 7.3 %collective-permute-done.6.refs_5_ = bf16[256,1024]{1,0:T(8,128)(2,1)S(1)} collective-permute-done((bf16[256,1024]{1,0:T(8,128)(2,1)S(1)}, bf16[256,1024]{1,0:T(8,128)(2,1)S(1)}, u32[]{:S(2)}, u32[]{:S(2)}) %collective-permute-start.6) | collective-permute-done | bytes 524320 | tf_op jit(solution)/shard_map/ppermute | solution.py:249
  162.1 13.0 %down.3 = bf16[4,1024,384]{2,1,0:T(8,128)(2,1)} custom-call(s32[3]{0:T(128)} %pad_add_fusion.place, bf16[256,1024]{1,0:T(8,128)(2,1)} %copy-done.1, bf16[256,1024]{1,0:T(8,128)(2,1)} %copy-done.13, bf16[256,1024]{1,0:T(8,128)(2,1)} %copy-done.14, bf16[256,1024]{1,0:T(8,128)(2,1)} %copy-done.15, bf16[256,1024]{1,0:T(8,128)(2,1)} %copy-done.16, ...), custom_call_target="tpu_custom_call" | custom-call | flops 3221225472 | bytes 8388608 | tf_op jit(solution)/shard_map/down/pallas_call | solution.py:335
  175.1 13.3 %back.3 = (bf16[1024,1536]{1,0:T(8,128)(2,1)}, bf16[1024,128]{1,0:T(8,128)(2,1)}) custom-call(s32[3]{0:T(128)} %pad_add_fusion.place, bf16[256,1024]{1,0:T(8,128)(2,1)} %copy-done.1, bf16[256,1024]{1,0:T(8,128)(2,1)} %copy-done.13, bf16[256,1024]{1,0:T(8,128)(2,1)} %copy-done.14, bf16[256,1024]{1,0:T(8,128)(2,1)} %copy-done.15, ...), custom_call_target="tpu_custom_call" | custom-call | flops 3221225472 | bytes 17825792 | tf_op jit(solution)/shard_map/back/pallas_call | solution.py:315
  188.4 8.0 %token_.3 = (bf16[256,1024]{1,0:T(8,128)(2,1)}, bf16[256,1024]{1,0:T(8,128)(2,1)}, bf16[256,1024]{1,0:T(8,128)(2,1)}, bf16[256,1024]{1,0:T(8,128)(2,1)}, bf16[25...) custom-call(s32[3]{0:T(128)} %pad_add_fusion.place, ...), custom_call_target="tpu_custom_call" | custom-call | flops 3221225472 | bytes 8388608 | tf_op jit(solution)/shard_map/token/pallas_call | solution.py:352
  196.4 11.9 %collective-permute-start.30 = (bf16[256,1024]{1,0:T(8,128)(2,1)}, bf16[256,1024]{1,0:T(8,128)(2,1)S(1)}, u32[]{:S(2)}, u32[]{:S(2)}) collective-permute-start(bf16[256,1024]{1,0:T(8,128)(2,1)} %get-tuple-element.41), channel_id=1, source_target_pairs={{0,1},{7,6},{8,9},{15,14},{16,17},{23,22},{24,25},{31,30}} | collective-permute-start | bytes 1572872 | tf_op jit(solution)/shard_map/ppermute | solution.py:255
  208.3 8.4 %token_.2 = (bf16[256,1152]{1,0:T(8,128)(2,1)}, bf16[256,1152]{1,0:T(8,128)(2,1)}, bf16[256,1152]{1,0:T(8,128)(2,1)}, bf16[256,1152]{1,0:T(8,128)(2,1)}, bf16[25...) custom-call(s32[3]{0:T(128)} %pad_add_fusion.place, ...), custom_call_target="tpu_custom_call" | custom-call | flops 3221225472 | bytes 8650752 | tf_op jit(solution)/shard_map/token/pallas_call | solution.py:352
  216.7 1.5 collective-permute-start.23
  218.2 1.3 collective-permute-start.22
  219.5 1.3 collective-permute-start.29
  223.0 2.5 collective-permute-start.21
  225.5 1.3 collective-permute-start.28
  229.2 1.3 collective-permute-start.33
  230.8 1.3 collective-permute-start.26
  232.1 24.5 %collective-permute-done.33 = bf16[256,1024]{1,0:T(8,128)(2,1)S(1)} collective-permute-done((bf16[256,1024]{1,0:T(8,128)(2,1)S(1)}, bf16[256,1024]{1,0:T(8,128)(2,1)S(1)}, u32[]{:S(2)}, u32[]{:S(2)}) %collective-permute-start.33) | collective-permute-done | bytes 524320 | tf_op jit(solution)/shard_map/ppermute | solution.py:259
  256.9 7.5 %collective-permute-done.26 = bf16[256,1152]{1,0:T(8,128)(2,1)S(1)} collective-permute-done((bf16[256,1152]{1,0:T(8,128)(2,1)S(1)}, bf16[256,1152]{1,0:T(8,128)(2,1)S(1)}, u32[]{:S(2)}, u32[]{:S(2)}) %collective-permute-start.26) | collective-permute-done | bytes 589856 | tf_op jit(solution)/shard_map/ppermute | solution.py:259
  264.6 1.5 collective-permute-done.27
  267.7 3.2 %maximum_convert_fusion = f32[4,512,384]{2,1,0:T(8,128)} fusion(bf16[4,256,384]{2,1,0:T(8,128)(2,1)} %reduce-scatter.5.cloned.1.call-done, bf16[4,256,384]{2,1,0:T(8,128)(2,1)} %reduce-scatter.3.cloned.1.call-done), kind=kLoop, calls=%fused_computation | loop fusion | flops 3145728 | bytes 4718592 | tf_op jit(solution)/shard_map/convert_element_type | solution.py:373
  (121 shorter events, 14.6 us)
Async XLA Ops:
  7.2 260.6 %reduce-scatter.3.cloned.1.call-start = ((), (), s32[]{:S(2)}) async-start(), calls=%async_computation.2 | async-start | bytes 3932160 | tf_op jit(solution)/shard_map/reduce_scatter | solution.py:372
  10.0 21.7 %copy-start.20 = (bf16[128,2048]{1,0:T(8,128)(2,1)S(1)}, bf16[128,2048]{1,0:T(8,128)(2,1)}, u32[]{:S(2)}) copy-start(bf16[128,2048]{1,0:T(8,128)(2,1)} %param.7) | copy-start | bytes 1572868
  10.0 2.1 collective-permute-start.14
  12.2 24.0 %copy-start.2 = (bf16[256,2176]{1,0:T(8,128)(2,1)}, bf16[256,2176]{1,0:T(8,128)(2,1)S(1)}, u32[]{:S(2)}) copy-start(bf16[256,2176]{1,0:T(8,128)(2,1)S(1)} %pad_maximum_fusion.own) | copy-start | bytes 3342340
  12.2 17.9 %collective-permute-start.15 = (bf16[256,2176]{1,0:T(8,128)(2,1)S(1)}, bf16[256,2176]{1,0:T(8,128)(2,1)}, u32[]{:S(2)}, u32[]{:S(2)}) collective-permute-start(bf16[256,2176]{1,0:T(8,128)(2,1)S(1)} %pad_maximum_fusion.own), channel_id=1, source_target_pairs={{0,2},{2,4},{3,1},{4,6},{5,3},{7,5},{8,10},{10,12},{11,9},{12,14},... | collective-permute-start | bytes 3342344 | tf_op jit(solution)/shard_map/ppermute | solution.py:247
  30.1 2.1 collective-permute-start.16
  32.1 27.7 %collective-permute-start.17 = (bf16[256,2176]{1,0:T(8,128)(2,1)}, bf16[256,2176]{1,0:T(8,128)(2,1)}, u32[]{:S(2)}, u32[]{:S(2)}) collective-permute-start(bf16[256,2176]{1,0:T(8,128)(2,1)} %collective-permute-done.16.refs_1_), channel_id=1, source_target_pairs={{3,1},{4,6},{11,9},{12,14},{19,17},{20,22},{27,25},{28,30}} | collective-permute-start | bytes 3342344 | tf_op jit(solution)/shard_map/ppermute | solution.py:247
  36.3 15.5 %collective-permute-start.7 = (bf16[128,1024]{1,0:T(8,128)(2,1)S(1)}, bf16[128,1024]{1,0:T(8,128)(2,1)S(1)}, u32[]{:S(2)}, u32[]{:S(2)}) collective-permute-start(bf16[128,1024]{1,0:T(8,128)(2,1)S(1)} %bitcast.7), channel_id=1, source_target_pairs={{0,1},{1,0},{2,3},{3,2},{4,5},{5,4},{6,7},{7,6},{8,9},{9,8},{10,11... | collective-permute-start | bytes 786440 | tf_op jit(solution)/shard_map/ppermute | solution.py:243
  51.8 35.3 %copy-start = (bf16[256,1024]{1,0:T(8,128)(2,1)}, bf16[256,1024]{1,0:T(8,128)(2,1)S(1)}, u32[]{:S(2)}) copy-start(bf16[256,1024]{1,0:T(8,128)(2,1)S(1)} %constant_dynamic-update-slice_fusion.2.own) | copy-start | bytes 1572868
  51.8 12.0 %collective-permute-start.8 = (bf16[256,1024]{1,0:T(8,128)(2,1)S(1)}, bf16[256,1024]{1,0:T(8,128)(2,1)S(1)}, u32[]{:S(2)}, u32[]{:S(2)}) collective-permute-start(bf16[256,1024]{1,0:T(8,128)(2,1)S(1)} %constant_dynamic-update-slice_fusion.2.own), channel_id=1, source_target_pairs={{0,2},{2,4},{3,1},{4,6},{5,3},{7,5},{8,10},{10,12},{11,9},{12,14},... | collective-permute-start | bytes 1572872 | tf_op jit(solution)/shard_map/ppermute | solution.py:247
  57.2 11.3 %collective-permute-start.18 = (bf16[256,2176]{1,0:T(8,128)(2,1)}, bf16[256,2176]{1,0:T(8,128)(2,1)}, u32[]{:S(2)}, u32[]{:S(2)}) collective-permute-start(bf16[256,2176]{1,0:T(8,128)(2,1)} %collective-permute-done.15.refs_0_), channel_id=1, source_target_pairs={{1,0},{2,3},{3,2},{4,5},{5,4},{6,7},{9,8},{10,11},{11,10},{12,13},... | collective-permute-start | bytes 3342344 | tf_op jit(solution)/shard_map/ppermute | solution.py:249
  58.5 11.3 %collective-permute-start.19 = (bf16[256,2176]{1,0:T(8,128)(2,1)}, bf16[256,2176]{1,0:T(8,128)(2,1)}, u32[]{:S(2)}, u32[]{:S(2)}) collective-permute-start(bf16[256,2176]{1,0:T(8,128)(2,1)} %collective-permute-done.16.refs_1_), channel_id=1, source_target_pairs={{1,0},{3,2},{4,5},{6,7},{9,8},{11,10},{12,13},{14,15},{17,16},{19,... | collective-permute-start | bytes 3342344 | tf_op jit(solution)/shard_map/ppermute | solution.py:249
  59.8 10.0 %collective-permute-start.20 = (bf16[256,2176]{1,0:T(8,128)(2,1)}, bf16[256,2176]{1,0:T(8,128)(2,1)}, u32[]{:S(2)}, u32[]{:S(2)}) collective-permute-start(bf16[256,2176]{1,0:T(8,128)(2,1)} %collective-permute-done.17.refs_2_), channel_id=1, source_target_pairs={{1,0},{6,7},{9,8},{14,15},{17,16},{22,23},{25,24},{30,31}} | collective-permute-start | bytes 3342344 | tf_op jit(solution)/shard_map/ppermute | solution.py:249
  63.8 23.3 %copy-start.7 = (bf16[256,1024]{1,0:T(8,128)(2,1)}, bf16[256,1024]{1,0:T(8,128)(2,1)S(1)}, u32[]{:S(2)}) copy-start(bf16[256,1024]{1,0:T(8,128)(2,1)S(1)} %collective-permute-done.8.refs_0_) | copy-start | bytes 1572868
  63.8 0.7 collective-permute-start.9
  64.5 22.6 %copy-start.8 = (bf16[256,1024]{1,0:T(8,128)(2,1)}, bf16[256,1024]{1,0:T(8,128)(2,1)S(1)}, u32[]{:S(2)}) copy-start(bf16[256,1024]{1,0:T(8,128)(2,1)S(1)} %collective-permute-done.9.refs_1_) | copy-start | bytes 1572868
  64.6 2.6 collective-permute-start.10
  65.8 21.4 %collective-permute-start.11 = (bf16[256,1024]{1,0:T(8,128)(2,1)S(1)}, bf16[256,1024]{1,0:T(8,128)(2,1)S(1)}, u32[]{:S(2)}, u32[]{:S(2)}) collective-permute-start(bf16[256,1024]{1,0:T(8,128)(2,1)S(1)} %collective-permute-done.8.refs_0_), channel_id=1, source_target_pairs={{1,0},{2,3},{3,2},{4,5},{5,4},{6,7},{9,8},{10,11},{11,10},{12,13},... | collective-permute-start | bytes 1572872 | tf_op jit(solution)/shard_map/ppermute | solution.py:249
  67.1 20.0 %copy-start.9 = (bf16[256,1024]{1,0:T(8,128)(2,1)}, bf16[256,1024]{1,0:T(8,128)(2,1)S(1)}, u32[]{:S(2)}) copy-start(bf16[256,1024]{1,0:T(8,128)(2,1)S(1)} %collective-permute-done.10.refs_2_) | copy-start | bytes 1572868
  67.1 24.2 %collective-permute-start.12 = (bf16[256,1024]{1,0:T(8,128)(2,1)S(1)}, bf16[256,1024]{1,0:T(8,128)(2,1)S(1)}, u32[]{:S(2)}, u32[]{:S(2)}) collective-permute-start(bf16[256,1024]{1,0:T(8,128)(2,1)S(1)} %collective-permute-done.9.refs_1_), channel_id=1, source_target_pairs={{1,0},{3,2},{4,5},{6,7},{9,8},{11,10},{12,13},{14,15},{17,16},{19,... | collective-permute-start | bytes 1572872 | tf_op jit(solution)/shard_map/ppermute | solution.py:249
  68.5 24.2 %collective-permute-start.13 = (bf16[256,1024]{1,0:T(8,128)(2,1)S(1)}, bf16[256,1024]{1,0:T(8,128)(2,1)S(1)}, u32[]{:S(2)}, u32[]{:S(2)}) collective-permute-start(bf16[256,1024]{1,0:T(8,128)(2,1)S(1)} %collective-permute-done.10.refs_2_), channel_id=1, source_target_pairs={{1,0},{6,7},{9,8},{14,15},{17,16},{22,23},{25,24},{30,31}} | collective-permute-start | bytes 1572872 | tf_op jit(solution)/shard_map/ppermute | solution.py:249
  106.5 161.2 %reduce-scatter.5.cloned.1.call-start = ((), (), s32[]{:S(2)}) async-start(), calls=%async_computation.3 | async-start | bytes 3932160 | tf_op jit(solution)/shard_map/reduce_scatter | solution.py:372
  106.6 17.7 %collective-permute-start = (bf16[128,1024]{1,0:T(8,128)(2,1)S(1)}, bf16[128,1024]{1,0:T(8,128)(2,1)S(1)}, u32[]{:S(2)}, u32[]{:S(2)}) collective-permute-start(bf16[128,1024]{1,0:T(8,128)(2,1)S(1)} %bitcast.9), channel_id=1, source_target_pairs={{0,1},{1,0},{2,3},{3,2},{4,5},{5,4},{6,7},{7,6},{8,9},{9,8},{10,11... | collective-permute-start | bytes 786440 | tf_op jit(solution)/shard_map/ppermute | solution.py:243
  124.3 23.0 %copy-start.1 = (bf16[256,1024]{1,0:T(8,128)(2,1)}, bf16[256,1024]{1,0:T(8,128)(2,1)S(1)}, u32[]{:S(2)}) copy-start(bf16[256,1024]{1,0:T(8,128)(2,1)S(1)} %constant_dynamic-update-slice_fusion.own) | copy-start | bytes 1572868
  124.3 8.0 %collective-permute-start.1 = (bf16[256,1024]{1,0:T(8,128)(2,1)S(1)}, bf16[256,1024]{1,0:T(8,128)(2,1)S(1)}, u32[]{:S(2)}, u32[]{:S(2)}) collective-permute-start(bf16[256,1024]{1,0:T(8,128)(2,1)S(1)} %constant_dynamic-update-slice_fusion.own), channel_id=1, source_target_pairs={{0,2},{2,4},{3,1},{4,6},{5,3},{7,5},{8,10},{10,12},{11,9},{12,14},... | collective-permute-start | bytes 1572872 | tf_op jit(solution)/shard_map/ppermute | solution.py:247
  132.3 15.1 %copy-start.13 = (bf16[256,1024]{1,0:T(8,128)(2,1)}, bf16[256,1024]{1,0:T(8,128)(2,1)S(1)}, u32[]{:S(2)}) copy-start(bf16[256,1024]{1,0:T(8,128)(2,1)S(1)} %collective-permute-done.1.refs_0_) | copy-start | bytes 1572868
  132.3 0.7 collective-permute-start.2
  133.0 14.4 %copy-start.14 = (bf16[256,1024]{1,0:T(8,128)(2,1)}, bf16[256,1024]{1,0:T(8,128)(2,1)S(1)}, u32[]{:S(2)}) copy-start(bf16[256,1024]{1,0:T(8,128)(2,1)S(1)} %collective-permute-done.2.refs_1_) | copy-start | bytes 1572868
  133.0 3.3 %collective-permute-start.3 = (bf16[256,1024]{1,0:T(8,128)(2,1)S(1)}, bf16[256,1024]{1,0:T(8,128)(2,1)S(1)}, u32[]{:S(2)}, u32[]{:S(2)}) collective-permute-start(bf16[256,1024]{1,0:T(8,128)(2,1)S(1)} %collective-permute-done.2.refs_1_), channel_id=1, source_target_pairs={{3,1},{4,6},{11,9},{12,14},{19,17},{20,22},{27,25},{28,30}} | collective-permute-start | bytes 1572872 | tf_op jit(solution)/shard_map/ppermute | solution.py:247
  133.7 19.0 %collective-permute-start.4 = (bf16[256,1024]{1,0:T(8,128)(2,1)S(1)}, bf16[256,1024]{1,0:T(8,128)(2,1)S(1)}, u32[]{:S(2)}, u32[]{:S(2)}) collective-permute-start(bf16[256,1024]{1,0:T(8,128)(2,1)S(1)} %collective-permute-done.1.refs_0_), channel_id=1, source_target_pairs={{1,0},{2,3},{3,2},{4,5},{5,4},{6,7},{9,8},{10,11},{11,10},{12,13},... | collective-permute-start | bytes 1572872 | tf_op jit(solution)/shard_map/ppermute | solution.py:249
  135.0 19.0 %collective-permute-start.5 = (bf16[256,1024]{1,0:T(8,128)(2,1)S(1)}, bf16[256,1024]{1,0:T(8,128)(2,1)S(1)}, u32[]{:S(2)}, u32[]{:S(2)}) collective-permute-start(bf16[256,1024]{1,0:T(8,128)(2,1)S(1)} %collective-permute-done.2.refs_1_), channel_id=1, source_target_pairs={{1,0},{3,2},{4,5},{6,7},{9,8},{11,10},{12,13},{14,15},{17,16},{19,... | collective-permute-start | bytes 1572872 | tf_op jit(solution)/shard_map/ppermute | solution.py:249
  136.3 25.0 %collective-permute-start.6 = (bf16[256,1024]{1,0:T(8,128)(2,1)S(1)}, bf16[256,1024]{1,0:T(8,128)(2,1)S(1)}, u32[]{:S(2)}, u32[]{:S(2)}) collective-permute-start(bf16[256,1024]{1,0:T(8,128)(2,1)S(1)} %collective-permute-done.3.refs_2_), channel_id=1, source_target_pairs={{1,0},{6,7},{9,8},{14,15},{17,16},{22,23},{25,24},{30,31}} | collective-permute-start | bytes 1572872 | tf_op jit(solution)/shard_map/ppermute | solution.py:249
  196.4 24.5 %collective-permute-start.30 = (bf16[256,1024]{1,0:T(8,128)(2,1)}, bf16[256,1024]{1,0:T(8,128)(2,1)S(1)}, u32[]{:S(2)}, u32[]{:S(2)}) collective-permute-start(bf16[256,1024]{1,0:T(8,128)(2,1)} %get-tuple-element.41), channel_id=1, source_target_pairs={{0,1},{7,6},{8,9},{15,14},{16,17},{23,22},{24,25},{31,30}} | collective-permute-start | bytes 1572872 | tf_op jit(solution)/shard_map/ppermute | solution.py:255
  208.3 12.6 %copy-start.19 = (bf16[256,1024]{1,0:T(8,128)(2,1)S(1)}, bf16[256,1024]{1,0:T(8,128)(2,1)}, u32[]{:S(2)}) copy-start(bf16[256,1024]{1,0:T(8,128)(2,1)} %get-tuple-element.40) | copy-start | bytes 1572868
  216.7 5.2 %collective-permute-start.23 = (bf16[256,1152]{1,0:T(8,128)(2,1)}, bf16[256,1152]{1,0:T(8,128)(2,1)S(1)}, u32[]{:S(2)}, u32[]{:S(2)}) collective-permute-start(bf16[256,1152]{1,0:T(8,128)(2,1)} %get-tuple-element.34), channel_id=1, source_target_pairs={{0,1},{7,6},{8,9},{15,14},{16,17},{23,22},{24,25},{31,30}} | collective-permute-start | bytes 1769480 | tf_op jit(solution)/shard_map/ppermute | solution.py:255
  218.2 9.6 %collective-permute-start.22 = (bf16[256,1152]{1,0:T(8,128)(2,1)}, bf16[256,1152]{1,0:T(8,128)(2,1)S(1)}, u32[]{:S(2)}, u32[]{:S(2)}) collective-permute-start(bf16[256,1152]{1,0:T(8,128)(2,1)} %get-tuple-element.32), channel_id=1, source_target_pairs={{0,1},{2,3},{5,4},{7,6},{8,9},{10,11},{13,12},{15,14},{16,17},{18,... | collective-permute-start | bytes 1769480 | tf_op jit(solution)/shard_map/ppermute | solution.py:255
  219.5 5.9 %collective-permute-start.29 = (bf16[256,1024]{1,0:T(8,128)(2,1)S(1)}, bf16[256,1024]{1,0:T(8,128)(2,1)S(1)}, u32[]{:S(2)}, u32[]{:S(2)}) collective-permute-start(bf16[256,1024]{1,0:T(8,128)(2,1)S(1)} %copy-done.26), channel_id=1, source_target_pairs={{0,1},{2,3},{5,4},{7,6},{8,9},{10,11},{13,12},{15,14},{16,17},{18,... | collective-permute-start | bytes 1572872 | tf_op jit(solution)/shard_map/ppermute | solution.py:255
  221.1 5.7 %collective-permute-start.31 = (bf16[256,1024]{1,0:T(8,128)(2,1)S(1)}, bf16[256,1024]{1,0:T(8,128)(2,1)S(1)}, u32[]{:S(2)}, u32[]{:S(2)}) collective-permute-start(bf16[256,1024]{1,0:T(8,128)(2,1)S(1)} %add_convert_fusion.5), channel_id=1, source_target_pairs={{1,3},{6,4},{9,11},{14,12},{17,19},{22,20},{25,27},{30,28}} | collective-permute-start | bytes 1572872 | tf_op jit(solution)/shard_map/ppermute | solution.py:259
  222.1 5.7 %collective-permute-start.24 = (bf16[256,1152]{1,0:T(8,128)(2,1)S(1)}, bf16[256,1152]{1,0:T(8,128)(2,1)S(1)}, u32[]{:S(2)}, u32[]{:S(2)}) collective-permute-start(bf16[256,1152]{1,0:T(8,128)(2,1)S(1)} %add_convert_fusion.2), channel_id=1, source_target_pairs={{1,3},{6,4},{9,11},{14,12},{17,19},{22,20},{25,27},{30,28}} | collective-permute-start | bytes 1769480 | tf_op jit(solution)/shard_map/ppermute | solution.py:259
  223.0 7.6 %collective-permute-start.21 = (bf16[256,1152]{1,0:T(8,128)(2,1)S(1)}, bf16[256,1152]{1,0:T(8,128)(2,1)S(1)}, u32[]{:S(2)}, u32[]{:S(2)}) collective-permute-start(bf16[256,1152]{1,0:T(8,128)(2,1)S(1)} %copy-done.24), channel_id=1, source_target_pairs={{0,1},{2,3},{3,2},{4,5},{5,4},{7,6},{8,9},{10,11},{11,10},{12,13},... | collective-permute-start | bytes 1769480 | tf_op jit(solution)/shard_map/ppermute | solution.py:255
  225.5 3.4 %collective-permute-start.28 = (bf16[256,1024]{1,0:T(8,128)(2,1)S(1)}, bf16[256,1024]{1,0:T(8,128)(2,1)S(1)}, u32[]{:S(2)}, u32[]{:S(2)}) collective-permute-start(bf16[256,1024]{1,0:T(8,128)(2,1)S(1)} %copy-done.25), channel_id=1, source_target_pairs={{0,1},{2,3},{3,2},{4,5},{5,4},{7,6},{8,9},{10,11},{11,10},{12,13},... | collective-permute-start | bytes 1572872 | tf_op jit(solution)/shard_map/ppermute | solution.py:255
  227.1 1.8 collective-permute-start.32
  228.1 2.5 collective-permute-start.25
  229.2 27.3 %collective-permute-start.33 = (bf16[256,1024]{1,0:T(8,128)(2,1)S(1)}, bf16[256,1024]{1,0:T(8,128)(2,1)S(1)}, u32[]{:S(2)}, u32[]{:S(2)}) collective-permute-start(bf16[256,1024]{1,0:T(8,128)(2,1)S(1)} %add_convert_fusion.3), channel_id=1, source_target_pairs={{1,3},{2,0},{3,5},{4,2},{5,7},{6,4},{9,11},{10,8},{11,13},{12,10},... | collective-permute-start | bytes 1572872 | tf_op jit(solution)/shard_map/ppermute | solution.py:259
  230.6 26.0 %copy-start.21 = (bf16[256,1024]{1,0:T(8,128)(2,1)S(1)}, bf16[256,1024]{1,0:T(8,128)(2,1)}, u32[]{:S(2)}) copy-start(bf16[256,1024]{1,0:T(8,128)(2,1)} %get-tuple-element.35) | copy-start | bytes 1572868
  230.8 33.5 %collective-permute-start.26 = (bf16[256,1152]{1,0:T(8,128)(2,1)S(1)}, bf16[256,1152]{1,0:T(8,128)(2,1)S(1)}, u32[]{:S(2)}, u32[]{:S(2)}) collective-permute-start(bf16[256,1152]{1,0:T(8,128)(2,1)S(1)} %add_convert_fusion), channel_id=1, source_target_pairs={{1,3},{2,0},{3,5},{4,2},{5,7},{6,4},{9,11},{10,8},{11,13},{12,10},... | collective-permute-start | bytes 1769480 | tf_op jit(solution)/shard_map/ppermute | solution.py:259
  256.8 7.8 %collective-permute-start.34 = (bf16[128,1024]{1,0:T(8,128)(2,1)S(1)}, bf16[128,1024]{1,0:T(8,128)(2,1)S(1)}, u32[]{:S(2)}, u32[]{:S(2)}) collective-permute-start(bf16[128,1024]{1,0:T(8,128)(2,1)S(1)} %slice.53), channel_id=1, source_target_pairs={{0,1},{1,0},{2,3},{3,2},{4,5},{5,4},{6,7},{7,6},{8,9},{9,8},{10,11... | collective-permute-start | bytes 786440 | tf_op jit(solution)/shard_map/ppermute | solution.py:265
  264.5 1.6 collective-permute-start.27
  (16 other events, 80.9 us)
Sparse Core Ops, SparseCore 0:
  106.6 67.1 reduce-scatter.2
  176.8 57.7 reduce-scatter.4

commit v3 on v1

v3 whole, which is shorter than its diff:
```python
import functools

import jax
import jax.numpy as jnp
from jax import lax
from jax.experimental import pallas as pl
from jax.experimental.pallas import tpu as pltpu
from jax.sharding import PartitionSpec as P

LANES = 128
SLICES = 2
VMEM_LIMIT = 60 * 1024 * 1024
bf16, f32 = jnp.bfloat16, jnp.float32
ANY = pl.BlockSpec(memory_space=pl.ANY)
VMEM = pl.BlockSpec(memory_space=pltpu.VMEM)
SMEM = pl.BlockSpec(memory_space=pltpu.SMEM)


def weight_copies(weights, dst, sem, pieces):
    experts, _, hidden = weights.shape
    return [
        pltpu.make_async_copy(
            weights.at[b, pl.ds(start, size), :],
            dst.at[pl.ds(to, size), pl.ds(b * hidden, hidden)],
            sem.at[b],
        )
        for b in range(experts)
        for start, size, to in pieces
    ]


def load_weights(weights, dst, sem, pieces):
    @pl.when(pl.program_id(0) == 0)
    def _():
        for copy in weight_copies(weights, dst, sem, pieces):
            copy.start()


def wait_weights(weights, dst, sem, pieces, b0, b1):
    @pl.when(pl.program_id(0) == 0)
    def _():
        copies = weight_copies(weights, dst, sem, pieces)
        for copy in copies[b0 * len(pieces) : b1 * len(pieces)]:
            copy.wait()


def pair_of(experts):
    return 2 if experts % 2 == 0 else 1


def up_kernel(width, top, place, rows, w_up, hid, scaled, slope_g, w_v, sem):
    experts, _, hidden = w_up.shape
    pieces = ((0, width, 0),)
    load_weights(w_up, w_v, sem, pieces)
    info = rows[:, pl.ds(width, LANES)].astype(f32)
    lane = lax.broadcasted_iota(jnp.int32, info.shape, 1)
    ids = jnp.where(lane < top, info, -1.0)
    gates = pltpu.roll(info, LANES - top, 1)
    pair = pair_of(experts)
    for b0 in range(0, experts, pair):
        wait_weights(w_up, w_v, sem, pieces, b0, b0 + pair)
        pre = jnp.dot(
            rows[:, pl.ds(0, width)], w_v[:, pl.ds(b0 * hidden, pair * hidden)], preferred_element_type=f32
        )
        for b in range(b0, b0 + pair):
            hit = ids == (place[0] * experts + b).astype(f32)
            gate = jnp.sum(jnp.where(hit, gates, 0.0), axis=1, keepdims=True)
            part = pre[:, (b - b0) * hidden : (b - b0 + 1) * hidden]
            sig = 1.0 / (1.0 + jnp.exp(-part))
            act = part * sig
            cols = pl.ds(b * hidden, hidden)
            hid[:, cols] = act.astype(bf16)
            scaled[:, cols] = (gate * act).astype(bf16)
            slope_g[:, cols] = (gate * (sig * (1.0 + part * (1.0 - sig)))).astype(bf16)


def back_kernel(width, top, pieces, first, last, after, place, rows, w_down, *refs):
    refs = list(refs)[after:]
    before = None if first else refs.pop(0)
    if last:
        hid, slope_g, meta, grad_pre, gate_back, w_v, sem = refs
    else:
        out, w_v, sem = refs
    experts, _, hidden = w_down.shape
    load_weights(w_down, w_v, sem, pieces)
    if last:
        info = meta[...].astype(f32)
        lane = lax.broadcasted_iota(jnp.int32, info.shape, 1)
        ids = jnp.where(lane < top, info, -1.0)
        picked = jnp.zeros(info.shape, f32)
    pair = pair_of(experts)
    for b0 in range(0, experts, pair):
        wait_weights(w_down, w_v, sem, pieces, b0, b0 + pair)
        both = pl.ds(b0 * hidden, pair * hidden)
        back = jnp.dot(rows[...], w_v[:, both], preferred_element_type=f32)
        if before is not None:
            back = back + before[:, both]
        if not last:
            out[:, both] = back
            continue
        for b in range(b0, b0 + pair):
            cols = pl.ds(b * hidden, hidden)
            part = back[:, (b - b0) * hidden : (b - b0 + 1) * hidden]
            grad_pre[:, cols] = (part * slope_g[:, cols].astype(f32)).astype(bf16)
            gate = jnp.sum(part * hid[:, cols].astype(f32), axis=1, keepdims=True)
            picked = picked + jnp.where(ids == (place[0] * experts + b).astype(f32), gate, 0.0)
    if last:
        gate_back[...] = picked.astype(bf16)


def down_kernel(experts, orders, place, rows, scaled, *refs):
    outs, (held, sem) = refs[:-2], refs[-2:]
    groups, parts = len(orders), len(orders[0])
    hidden = scaled.shape[1] // experts
    piece = rows.shape[1] // parts
    cut = piece // groups
    copies = []
    for q in reversed(range(parts)):
        at = pl.multiple_of((place[1] ^ q) * piece, piece)
        full = lax.dot_general(
            rows[:, pl.ds(at, piece)], scaled[...], (((0,), (0,)), ((), ())), preferred_element_type=f32
        ).astype(bf16)
        for g, order in enumerate(orders):
            for b in range(experts):
                held[g, q, b] = full[g * cut : (g + 1) * cut, b * hidden : (b + 1) * hidden]
            p = order.index(q)
            half = parts // 2
            out = outs[2 * g + p // half]
            copy = pltpu.make_async_copy(held.at[g, q], out.at[p % half], sem.at[g, q])
            copy.start()
            copies.append(copy)
    for copy in copies:
        copy.wait()


def token_kernel(pieces, extra, after, *refs):
    grad_pre, refs = refs[after], refs[after + 1 :]
    if extra:
        gate_back, refs = refs[0], refs[1:]
    w_up, out, w_v, sem = refs
    load_weights(w_up, w_v, sem, pieces)
    wait_weights(w_up, w_v, sem, pieces, 0, w_up.shape[0])
    width = w_v.shape[0]
    out[:, pl.ds(0, width)] = lax.dot_general(
        grad_pre[...], w_v[...], (((1,), (1,)), ((), ())), preferred_element_type=f32
    ).astype(bf16)
    if extra:
        out[:, pl.ds(width, LANES)] = gate_back[...]


def cost(flops, nbytes):
    return pl.CostEstimate(flops=int(flops), bytes_accessed=int(nbytes), transcendentals=0)


def params(name=None):
    return pltpu.CompilerParams(vmem_limit_bytes=VMEM_LIMIT)


def shards(tokens, cotangent, expert_ids, gate_weights, w_up, w_down):
    tok_rows, width = tokens.shape
    top = expert_ids.shape[1]
    ep_count, dp_count = lax.axis_size("ep"), lax.axis_size("dp")
    experts, _, hidden = w_up.shape
    total = ep_count * tok_rows
    inner = experts * hidden
    place = jnp.stack([lax.axis_index("ep"), lax.axis_index("dp")]).astype(jnp.int32)
    bits = dp_count.bit_length() - 1
    groups = 2

    info = jnp.concatenate(
        [expert_ids.astype(bf16), gate_weights, jnp.zeros((tok_rows, LANES - 2 * top), bf16)], axis=1
    )
    x_all = lax.all_gather(jnp.concatenate([tokens, info], axis=1), "ep", axis=0, tiled=True)
    share = width // dp_count
    slices = SLICES if share % (SLICES * LANES) == 0 else 1
    piece = share // slices
    cols = dp_count * piece
    cut = cotangent.reshape(tok_rows, dp_count, slices, piece)
    cut = [cut[:, :, s].reshape(tok_rows, cols) for s in range(slices)]
    dy_all = []
    for part in cut:
        x_all, part = lax.optimization_barrier((x_all, part))
        dy_all.append(lax.all_gather(part, "ep", axis=0, tiled=True))

    full = width + LANES
    tile = 512 if total % 512 == 0 else total
    grid = (total // tile,)

    def by_rows(n):
        return pl.BlockSpec((tile, n), lambda i: (i, 0))

    def weights_scratch(rows):
        return [pltpu.VMEM((rows, inner), bf16), pltpu.SemaphoreType.DMA((experts,))]

    def shape(rows, n, dtype=bf16):
        return jax.ShapeDtypeStruct((rows, n), dtype)

    hid, scaled, slope_g = pl.pallas_call(
        functools.partial(up_kernel, width, top),
        grid=grid,
        in_specs=[SMEM, by_rows(full), ANY],
        out_specs=[by_rows(inner)] * 3,
        out_shape=[shape(total, inner)] * 3,
        scratch_shapes=weights_scratch(width),
        compiler_params=params(),
        cost_estimate=cost(2 * total * width * inner, 2 * (total * full + width * inner + 3 * total * inner)),
        name="up",
    )(place, x_all, w_up)

    orders = []
    for g in range(groups):
        turn = [(g + t) % bits for t in range(bits)]
        orders.append(
            tuple(sum(((p >> (bits - 1 - t)) & 1) << turn[t] for t in range(bits)) for p in range(dp_count))
        )

    def down(s):
        half = dp_count // 2
        cut_rows = piece // groups
        return pl.pallas_call(
            functools.partial(down_kernel, experts, tuple(orders)),
            in_specs=[SMEM, VMEM, VMEM],
            out_specs=[ANY] * (2 * groups),
            out_shape=[jax.ShapeDtypeStruct((half, experts, cut_rows, hidden), bf16)] * (2 * groups),
            scratch_shapes=[
                pltpu.VMEM((groups, dp_count, experts, cut_rows, hidden), bf16),
                pltpu.SemaphoreType.DMA((groups, dp_count)),
            ],
            compiler_params=params(),
            cost_estimate=cost(2 * total * cols * inner, 2 * (total * cols + total * inner + cols * inner)),
            name="down",
        )(place, dy_all[s], scaled)

    def exchange(state, t):
        new = []
        for g, (keep, send) in enumerate(state):
            bit = 1 << ((g + t) % bits)
            got = lax.ppermute(send, "dp", [(i, i ^ bit) for i in range(dp_count)])
            both = keep.astype(f32) + got.astype(f32)
            if t < bits - 1:
                both = both.astype(bf16)
            half = both.shape[0] // 2
            new.append((both[:half], both[half:]) if half else both[0])
        return new

    def back(s, before, after):
        first, last = s == 0, s == slices - 1
        pieces = tuple((i * share + s * piece, piece, i * piece) for i in range(dp_count))
        ins, specs = [place, dy_all[s], w_down, *after], [SMEM, by_rows(cols), ANY] + [ANY] * len(after)
        if not first:
            ins.append(before)
            specs.append(by_rows(inner))
        if last:
            ins += [hid, slope_g, x_all]
            specs += [by_rows(inner), by_rows(inner), pl.BlockSpec((tile, LANES), lambda i: (i, width // LANES))]
            outs, out_specs = [shape(total, inner), shape(total, LANES)], [by_rows(inner), by_rows(LANES)]
        else:
            outs, out_specs = shape(total, inner, f32), by_rows(inner)
        return pl.pallas_call(
            functools.partial(back_kernel, cols, top, pieces, first, last, len(after)),
            grid=grid,
            in_specs=specs,
            out_specs=out_specs,
            out_shape=outs,
            scratch_shapes=weights_scratch(cols),
            compiler_params=params(),
            cost_estimate=cost(2 * total * cols * inner, 2 * (total * cols + cols * inner + 4 * total * inner)),
            name="back",
        )(*ins)

    def token(s, grad_pre, gate_back, after):
        half = width // slices
        extra = s == 0
        n = half + (LANES if extra else 0)
        return pl.pallas_call(
            functools.partial(token_kernel, ((s * half, half, 0),), extra, len(after)),
            grid=grid,
            in_specs=[ANY] * len(after) + [by_rows(inner)] + ([by_rows(LANES)] if extra else []) + [ANY],
            out_specs=by_rows(n),
            out_shape=shape(total, n),
            scratch_shapes=weights_scratch(half),
            compiler_params=params(),
            cost_estimate=cost(2 * total * half * inner, 2 * (total * n + total * inner + half * inner)),
            name="token",
        )(*after, grad_pre, *((gate_back,) if extra else ()), w_up)

    states, before = [], None
    for s in range(slices):
        outs = down(s)
        before = back(s, before, outs[:1] if s < slices - 1 else [])
        states.append([(outs[2 * g], outs[2 * g + 1]) for g in range(groups)])
    grad_pre, gate_back = before
    down_parts = []
    for t in range(bits):
        states = [exchange(state, t) for state in states]
        if t == 0:
            first_sums = [pair[0] for pair in states[0]] if slices > 1 and bits > 1 else []
    down_parts = [part for state in states for part in state]
    token_parts = [
        lax.psum_scatter(
            token(s, grad_pre, gate_back, first_sums if s else []), "ep", scatter_dimension=0, tiled=True
        )
        for s in range(slices)
    ]
    half = width // slices
    gate_grad = token_parts[0][:, half : half + top]
    token_grad = jnp.concatenate([token_parts[0][:, :half]] + token_parts[1:], axis=1)
    down_grad = jnp.concatenate(down_parts, axis=1)
    return (token_grad, gate_grad, down_grad)


def solution(mesh):
    return jax.shard_map(
        shards,
        mesh=mesh,
        in_specs=(
            P(("dp", "ep"), None),
            P(("dp", "ep"), None),
            P(("dp", "ep"), None),
            P(("dp", "ep"), None),
            P("ep", None, None),
            P("ep", None, None),
        ),
        out_specs=(P(("dp", "ep"), None), P(("dp", "ep"), None), P("ep", "dp", None)),
        check_vma=False,
    )
```

time: 288 us -> 232 us (0.81)
  Pallas kernels: 0 us -> 69.2 us
  waiting for transfers between devices: 188 us -> 119 us
  matrix products: 49.3 us -> 0 us
  blocking collectives: 28.9 us -> 0 us
  starting transfers between devices: 0.38 us -> 10.6 us
  local copies, waits for them, and re-layouts: 2.48 us -> 12.2 us
    reduce_scatter x2, waiting for transfers between devices: 120 us -> 0.02 us  [shards(): lax.psum_scatter(token(s, grad_pre, gate_back, first_sums if s else []),...]
    pallas_call x0 -> x7, Pallas kernels: none -> 69.2 us  [the longest x2 22.1 us: back(): pl.pallas_call(functools.partial(back_kernel, cols, top, pieces, first, l...]
    dot_general x7 -> x0, matrix products: 49.3 us -> none  [the longest x1 12 us: shards(): jnp.einsum('brt,brd->td', pick, route_grad, preferred_element_type=f32)]
    ppermute x0 -> x8, waiting for transfers between devices: none -> 45.2 us  [exchange(): got = lax.ppermute(send, 'dp', [(i, i ^ bit) for i in range(dp_count)])]
    all_gather x2 -> x0, blocking collectives: 28.9 us -> none  [the longest x1 15.8 us: shards(): ids_all = lax.all_gather(expert_ids, 'ep', axis=0, tiled=True)]
    all_gather x2 -> x3, waiting for transfers between devices: 59.3 us -> 73.4 us  [the longest x1 47.8 us: shards(): lax.all_gather(jnp.concatenate([tokens, info], axis=1), 'ep', axis=0, til...]
    ppermute x0 -> x8, starting transfers between devices: none -> 10 us  [exchange(): got = lax.ppermute(send, 'dp', [(i, i ^ bit) for i in range(dp_count)])]
    unnamed x6 -> x5, waiting for transfers between devices: 9.12 us -> 0.08 us
  transfers between devices with their start and end apart: 5 -> 13, of which waited for: 5 -> 8; matrix products, arithmetic and copies ran while one was open for 13% -> 6% of each run, Pallas kernels for 0% -> 21%
where the time goes in v3:
time: 232 us
  waiting for transfers between devices  119 us (51%)
  Pallas kernels  69.2 us (30%)
  between operations  14 us (6%)
  local copies, waits for them, and re-layouts  12.2 us (5%)
  starting transfers between devices  10.6 us (5%)
  other arithmetic  7.17 us (3%)
    all_gather x1, waiting for transfers between devices, shards(): lax.all_gather(jnp.concatenate([tokens, info], axis=1), 'ep', axis=0, til...  47.8 us
    ppermute x8, waiting for transfers between devices, exchange(): got = lax.ppermute(send, 'dp', [(i, i ^ bit) for i in range(dp_count)])  45.2 us
    all_gather x2, waiting for transfers between devices, shards(): dy_all.append(lax.all_gather(part, 'ep', axis=0, tiled=True))  25.6 us
    pallas_call x2, Pallas kernels, back(): pl.pallas_call(functools.partial(back_kernel, cols, top, pieces, first, l...  22.1 us
    pallas_call x2, Pallas kernels, token(): pl.pallas_call(functools.partial(token_kernel, ((s * half, half, 0),), ex...  16.5 us
    pallas_call x1, Pallas kernels, shards(): pl.pallas_call(functools.partial(up_kernel, width, top), grid=grid, in_sp...  16.4 us
    pallas_call x2, Pallas kernels, down(): pl.pallas_call(functools.partial(down_kernel, experts, tuple(orders)), in...  14.2 us
    ppermute x8, starting transfers between devices, exchange(): got = lax.ppermute(send, 'dp', [(i, i ^ bit) for i in range(dp_count)])  10 us
  transfers between devices with their start and end apart: 13, of which 8 were waited for; matrix products, arithmetic and copies ran while one was open for 6% of the time, Pallas kernels for 21%

profile of v3, /device:TPU:0, one launch (start us, length us, event | category | flops | bytes accessed | tf_op | source)
XLA Modules:
  0.0 231.9 jit_solution(12889468005242557770)
XLA Ops:
  7.2 0.7 convert_element_type.63
  7.9 0.1 copy.9
  8.0 0.8 copy.10
  8.8 1.9 concatenate.9
  10.8 1.4 reshape.9
  12.2 2.4 %slice_reduce_fusion = (bf16[128,4,256]{2,1,0:T(4,128)(2,1)S(1)}, bf16[128,4,256]{2,1,0:T(4,128)(2,1)S(1)}) fusion(bf16[128,4,2,256]{3,2,1,0:T(2,128)(2,1)S(1)} %reshape.9), kind=kLoop, calls=%fused_computation.9 | loop fusion | bytes 1048576 | tf_op jit(solution)/shard_map/slice | solution.py:179
  14.6 0.7 copy.16
  15.3 47.8 %all-gather.4.cloned.1.call-done.rows.refs_3_ = bf16[1024,2176]{1,0:T(8,128)(2,1)} async-done(((bf16[128,2176]{1,0:T(8,128)(2,1)}), bf16[1024,2176]{1,0:T(8,128)(2,1)}) %all-gather.4.cloned.1.call-update) | async-done | bytes 4456464 | tf_op jit(solution)/shard_map/all_gather | solution.py:173
  63.2 0.7 copy.17
  63.9 0.2 reduce-scatter.3.cloned.1.call-start
  64.2 0.6 pad_add_fusion.place
  64.8 16.4 %up.1 = (bf16[1024,1536]{1,0:T(8,128)(2,1)}, bf16[1024,1536]{1,0:T(8,128)(2,1)}, bf16[1024,1536]{1,0:T(8,128)(2,1)}) custom-call(s32[2]{0:T(128)} %pad_add_fusion.place, bf16[1024,2176]{1,0:T(8,128)(2,1)} %all-gather.4.cloned.1.call-done.rows.refs_3_, bf16[4,2048,384]{2,1,0:T(8,128)(2,1)} %refs_3_.1), custom_call_target="tpu_custom_call" | custom-call | flops 6442450944 | bytes 20185088 | tf_op jit(solution)/shard_map/up/pallas_call | solution.py:198
  81.2 12.0 %all-gather.8.cloned.1.call-done.rows = bf16[1024,1024]{1,0:T(8,128)(2,1)} async-done(((bf16[128,1024]{1,0:T(8,128)(2,1)}), bf16[1024,1024]{1,0:T(8,128)(2,1)}) %all-gather.8.cloned.1.call-update) | async-done | bytes 2097168 | tf_op jit(solution)/shard_map/all_gather | solution.py:183
  93.2 7.1 %down.2 = (bf16[2,4,128,384]{3,2,1,0:T(8,128)(2,1)}, bf16[2,4,128,384]{3,2,1,0:T(8,128)(2,1)}, bf16[2,4,128,384]{3,2,1,0:T(8,128)(2,1)}, bf16[2,4,128,384]{3,2,1,0:T(8,128)(2,1)}) custom-call(s32[2]{0:T(128)} %pad_add_fusion.place, bf16[1024,1024]{1,0:T(8,128)(2,1)} %all-gather.8.cloned.1.call-done.rows, bf16[1024,1536]{1,0:T(8,128)(2,1)} %get-tuple-element.24.scaled), custom_call_target="tpu_custom_call" | custom-call | flops 3221225472 | bytes 8388608 | tf_op jit(solution)/shard_map/down/pallas_call | solution.py:220
  100.3 9.6 %back.2.refs_0_ = f32[1024,1536]{1,0:T(8,128)} custom-call(s32[2]{0:T(128)} %pad_add_fusion.place, bf16[1024,1024]{1,0:T(8,128)(2,1)} %all-gather.8.cloned.1.call-done.rows, bf16[4,2048,384]{2,1,0:T(8,128)(2,1)} %w_down.3, bf16[2,4,128,384]{3,2,1,0:T(8,128)(2,1)} %get-tuple-element.25.refs_0_), custom_call_target="tpu_custom_call" | custom-call | flops 3221225472 | bytes 17825792 | tf_op jit(solution)/shard_map/back/pallas_call | solution.py:259
  109.9 13.6 %all-gather.6.cloned.1.call-done.rows = bf16[1024,1024]{1,0:T(8,128)(2,1)} async-done(((bf16[128,1024]{1,0:T(8,128)(2,1)}), bf16[1024,1024]{1,0:T(8,128)(2,1)}) %all-gather.6.cloned.1.call-update) | async-done | bytes 2097168 | tf_op jit(solution)/shard_map/all_gather | solution.py:183
  123.5 12.5 %back.3 = (bf16[1024,1536]{1,0:T(8,128)(2,1)}, bf16[1024,128]{1,0:T(8,128)(2,1)}) custom-call(s32[2]{0:T(128)} %pad_add_fusion.place, bf16[1024,1024]{1,0:T(8,128)(2,1)} %all-gather.6.cloned.1.call-done.rows, bf16[4,2048,384]{2,1,0:T(8,128)(2,1)} %w_down.3, f32[1024,1536]{1,0:T(8,128)} %back.2.refs_0_, bf16[1024,1536]{1,0:T(8,128)(2,1)} %get-tuple-element.26.refs_1_, ...), custom_call_target="tpu_custom_call" | custom-call | flops 3221225472 | bytes 17825792 | tf_op jit(solution)/shard_map/back/pallas_call | solution.py:259
  136.0 8.4 %token_.2 = bf16[1024,1152]{1,0:T(8,128)(2,1)} custom-call(bf16[1024,1536]{1,0:T(8,128)(2,1)} %get-tuple-element.28.refs_0_.refs_2_, bf16[1024,128]{1,0:T(8,128)(2,1)} %get-tuple-element.29.refs_1_, bf16[4,2048,384]{2,1,0:T(8,128)(2,1)} %refs_3_.1), custom_call_target="tpu_custom_call" | custom-call | flops 3221225472 | bytes 8650752 | tf_op jit(solution)/shard_map/token/pallas_call | solution.py:275
  144.5 0.3 reduce-scatter.5.cloned.1.call-start
  144.8 1.5 collective-permute-start
  146.3 1.5 collective-permute-start.1
  147.8 16.7 %collective-permute-done = bf16[2,4,128,384]{3,2,1,0:T(8,128)(2,1)S(1)} collective-permute-done((bf16[2,4,128,384]{3,2,1,0:T(8,128)(2,1)S(1)}, bf16[2,4,128,384]{3,2,1,0:T(8,128)(2,1)S(1)}, u32[]{:S(2)}, u32[]{:S(2)}) %collective-permute-start) | collective-permute-done | bytes 786464 | tf_op jit(solution)/shard_map/ppermute | solution.py:238
  164.5 0.2 add_convert_fusion.3
  164.7 0.8 fusion
  165.6 0.1 collective-permute-done.1
  165.7 0.2 add_convert_fusion.2
  165.9 0.8 fusion.1
  166.7 8.1 %token_.3 = bf16[1024,1024]{1,0:T(8,128)(2,1)} custom-call(bf16[1,4,128,384]{3,2,1,0:T(8,128)(2,1)} %get-tuple-element.43.refs_0_, bf16[1,4,128,384]{3,2,1,0:T(8,128)(2,1)} %get-tuple-element.45.refs_1_, bf16[1024,1536]{1,0:T(8,128)(2,1)} %get-tuple-element.28.refs_0_.refs_2_, bf16[4,2048,384]{2,1,0:T(8,128)(2,1)} %refs_3_.1), custom_call_target="tpu_custom_call" | custom-call | flops 3221225472 | bytes 8388608 | tf_op jit(solution)/shard_map/token/pallas_call | solution.py:275
  174.9 7.1 %down.3 = (bf16[2,4,128,384]{3,2,1,0:T(8,128)(2,1)}, bf16[2,4,128,384]{3,2,1,0:T(8,128)(2,1)}, bf16[2,4,128,384]{3,2,1,0:T(8,128)(2,1)}, bf16[2,4,128,384]{3,2,1,0:T(8,128)(2,1)}) custom-call(s32[2]{0:T(128)} %pad_add_fusion.place, bf16[1024,1024]{1,0:T(8,128)(2,1)} %all-gather.6.cloned.1.call-done.rows, bf16[1024,1536]{1,0:T(8,128)(2,1)} %get-tuple-element.24.scaled), custom_call_target="tpu_custom_call" | custom-call | flops 3221225472 | bytes 8388608 | tf_op jit(solution)/shard_map/down/pallas_call | solution.py:220
  182.0 1.4 collective-permute-start.4
  183.3 1.5 collective-permute-start.6
  184.8 0.5 collective-permute-start.2
  185.4 0.7 collective-permute-start.3
  186.1 16.6 %collective-permute-done.4 = bf16[2,4,128,384]{3,2,1,0:T(8,128)(2,1)S(1)} collective-permute-done((bf16[2,4,128,384]{3,2,1,0:T(8,128)(2,1)}, bf16[2,4,128,384]{3,2,1,0:T(8,128)(2,1)S(1)}, u32[]{:S(2)}, u32[]{:S(2)}) %collective-permute-start.4) | collective-permute-done | bytes 786464 | tf_op jit(solution)/shard_map/ppermute | solution.py:238
  202.7 1.3 add_convert_fusion.1
  204.1 1.5 collective-permute-start.5
  205.7 0.2 add_convert_fusion
  205.9 1.4 collective-permute-start.7
  207.3 5.2 %collective-permute-done.2 = bf16[1,4,128,384]{3,2,1,0:T(8,128)(2,1)S(1)} collective-permute-done((bf16[1,4,128,384]{3,2,1,0:T(8,128)(2,1)S(1)}, bf16[1,4,128,384]{3,2,1,0:T(8,128)(2,1)S(1)}, u32[]{:S(2)}, u32[]{:S(2)}) %collective-permute-start.2) | collective-permute-done | bytes 393248 | tf_op jit(solution)/shard_map/ppermute | solution.py:238
  212.5 0.1 add_bitcast_fusion.2
  212.6 6.5 %collective-permute-done.5 = bf16[1,4,128,384]{3,2,1,0:T(8,128)(2,1)S(1)} collective-permute-done((bf16[1,4,128,384]{3,2,1,0:T(8,128)(2,1)S(1)}, bf16[1,4,128,384]{3,2,1,0:T(8,128)(2,1)S(1)}, u32[]{:S(2)}, u32[]{:S(2)}) %collective-permute-start.5) | collective-permute-done | bytes 393248 | tf_op jit(solution)/shard_map/ppermute | solution.py:238
  219.1 0.1 add_bitcast_fusion.1
  219.2 0.1 add_bitcast_fusion
  219.3 1.9 pad_maximum_fusion
  221.2 0.8 slice.53
  221.9 0.7 copy.13
  222.6 1.0 slice.50
  223.6 1.8 pad_maximum_fusion.1
  (27 shorter events, 0.4 us)
Async XLA Ops:
  7.2 55.9 %all-gather.4.cloned.1.call-start = ((), (), s32[]{:S(2)}) async-start(), calls=%async_computation.2 | async-start | bytes 5013504 | tf_op jit(solution)/shard_map/all_gather | solution.py:173
  10.7 82.5 %all-gather.8.cloned.1.call-start = ((), (), s32[]{:S(2)}) async-start(), calls=%async_computation.4 | async-start | bytes 2359296 | tf_op jit(solution)/shard_map/all_gather | solution.py:183
  63.1 60.3 %all-gather.6.cloned.1.call-start = ((), (), s32[]{:S(2)}) async-start(), calls=%async_computation.3 | async-start | bytes 2359296 | tf_op jit(solution)/shard_map/all_gather | solution.py:183
  63.9 157.2 %reduce-scatter.3.cloned.1.call-start = ((), (), s32[]{:S(2)}) async-start(), calls=%async_computation.5 | async-start | bytes 2654208 | tf_op jit(solution)/shard_map/reduce_scatter | solution.py:300
  136.0 8.8 %copy-start.4 = (bf16[2,4,128,384]{3,2,1,0:T(8,128)(2,1)S(1)}, bf16[2,4,128,384]{3,2,1,0:T(8,128)(2,1)}, u32[]{:S(2)}) copy-start(bf16[2,4,128,384]{3,2,1,0:T(8,128)(2,1)} %get-tuple-element.30) | copy-start | bytes 2359300
  136.0 10.3 %copy-start.3 = (bf16[2,4,128,384]{3,2,1,0:T(8,128)(2,1)S(1)}, bf16[2,4,128,384]{3,2,1,0:T(8,128)(2,1)}, u32[]{:S(2)}) copy-start(bf16[2,4,128,384]{3,2,1,0:T(8,128)(2,1)} %get-tuple-element.32) | copy-start | bytes 2359300
  136.0 28.5 %copy-start = (bf16[2,4,128,384]{3,2,1,0:T(8,128)(2,1)S(1)}, bf16[2,4,128,384]{3,2,1,0:T(8,128)(2,1)}, u32[]{:S(2)}) copy-start(bf16[2,4,128,384]{3,2,1,0:T(8,128)(2,1)} %get-tuple-element.25.refs_0_) | copy-start | bytes 2359300
  144.5 21.2 %copy-start.1 = (bf16[2,4,128,384]{3,2,1,0:T(8,128)(2,1)S(1)}, bf16[2,4,128,384]{3,2,1,0:T(8,128)(2,1)}, u32[]{:S(2)}) copy-start(bf16[2,4,128,384]{3,2,1,0:T(8,128)(2,1)} %get-tuple-element.31) | copy-start | bytes 2359300
  144.5 79.1 %reduce-scatter.5.cloned.1.call-start = ((), (), s32[]{:S(2)}) async-start(), calls=%async_computation.6 | async-start | bytes 2359296 | tf_op jit(solution)/shard_map/reduce_scatter | solution.py:300
  144.8 19.7 %collective-permute-start = (bf16[2,4,128,384]{3,2,1,0:T(8,128)(2,1)S(1)}, bf16[2,4,128,384]{3,2,1,0:T(8,128)(2,1)S(1)}, u32[]{:S(2)}, u32[]{:S(2)}) collective-permute-start(bf16[2,4,128,384]{3,2,1,0:T(8,128)(2,1)S(1)} %copy-done.4), channel_id=1, source_target_pairs={{0,8},{8,0},{16,24},{24,16},{1,9},{9,1},{17,25},{25,17},{2,10},{10... | collective-permute-start | bytes 2359304 | tf_op jit(solution)/shard_map/ppermute | solution.py:238
  146.3 19.4 %collective-permute-start.1 = (bf16[2,4,128,384]{3,2,1,0:T(8,128)(2,1)S(1)}, bf16[2,4,128,384]{3,2,1,0:T(8,128)(2,1)S(1)}, u32[]{:S(2)}, u32[]{:S(2)}) collective-permute-start(bf16[2,4,128,384]{3,2,1,0:T(8,128)(2,1)S(1)} %copy-done.3), channel_id=1, source_target_pairs={{0,16},{8,24},{16,0},{24,8},{1,17},{9,25},{17,1},{25,9},{2,18},{10... | collective-permute-start | bytes 2359304 | tf_op jit(solution)/shard_map/ppermute | solution.py:238
  182.0 23.7 %copy-start.2 = (bf16[2,4,128,384]{3,2,1,0:T(8,128)(2,1)S(1)}, bf16[2,4,128,384]{3,2,1,0:T(8,128)(2,1)}, u32[]{:S(2)}) copy-start(bf16[2,4,128,384]{3,2,1,0:T(8,128)(2,1)} %get-tuple-element.35) | copy-start | bytes 2359300
  182.0 20.8 %collective-permute-start.4 = (bf16[2,4,128,384]{3,2,1,0:T(8,128)(2,1)}, bf16[2,4,128,384]{3,2,1,0:T(8,128)(2,1)S(1)}, u32[]{:S(2)}, u32[]{:S(2)}) collective-permute-start(bf16[2,4,128,384]{3,2,1,0:T(8,128)(2,1)} %get-tuple-element.34), channel_id=1, source_target_pairs={{0,8},{8,0},{16,24},{24,16},{1,9},{9,1},{17,25},{25,17},{2,10},{10... | collective-permute-start | bytes 2359304 | tf_op jit(solution)/shard_map/ppermute | solution.py:238
  183.3 22.3 %collective-permute-start.6 = (bf16[2,4,128,384]{3,2,1,0:T(8,128)(2,1)}, bf16[2,4,128,384]{3,2,1,0:T(8,128)(2,1)S(1)}, u32[]{:S(2)}, u32[]{:S(2)}) collective-permute-start(bf16[2,4,128,384]{3,2,1,0:T(8,128)(2,1)} %get-tuple-element.36), channel_id=1, source_target_pairs={{0,16},{8,24},{16,0},{24,8},{1,17},{9,25},{17,1},{25,9},{2,18},{10... | collective-permute-start | bytes 2359304 | tf_op jit(solution)/shard_map/ppermute | solution.py:238
  184.8 27.6 %collective-permute-start.2 = (bf16[1,4,128,384]{3,2,1,0:T(8,128)(2,1)S(1)}, bf16[1,4,128,384]{3,2,1,0:T(8,128)(2,1)S(1)}, u32[]{:S(2)}, u32[]{:S(2)}) collective-permute-start(bf16[1,4,128,384]{3,2,1,0:T(8,128)(2,1)S(1)} %get-tuple-element.42), channel_id=1, source_target_pairs={{0,16},{8,24},{16,0},{24,8},{1,17},{9,25},{17,1},{25,9},{2,18},{10... | collective-permute-start | bytes 1179656 | tf_op jit(solution)/shard_map/ppermute | solution.py:238
  185.4 27.2 %collective-permute-start.3 = (bf16[1,4,128,384]{3,2,1,0:T(8,128)(2,1)S(1)}, bf16[1,4,128,384]{3,2,1,0:T(8,128)(2,1)S(1)}, u32[]{:S(2)}, u32[]{:S(2)}) collective-permute-start(bf16[1,4,128,384]{3,2,1,0:T(8,128)(2,1)S(1)} %get-tuple-element.44), channel_id=1, source_target_pairs={{0,8},{8,0},{16,24},{24,16},{1,9},{9,1},{17,25},{25,17},{2,10},{10... | collective-permute-start | bytes 1179656 | tf_op jit(solution)/shard_map/ppermute | solution.py:238
  204.1 15.0 %collective-permute-start.5 = (bf16[1,4,128,384]{3,2,1,0:T(8,128)(2,1)S(1)}, bf16[1,4,128,384]{3,2,1,0:T(8,128)(2,1)S(1)}, u32[]{:S(2)}, u32[]{:S(2)}) collective-permute-start(bf16[1,4,128,384]{3,2,1,0:T(8,128)(2,1)S(1)} %slice.57), channel_id=1, source_target_pairs={{0,16},{8,24},{16,0},{24,8},{1,17},{9,25},{17,1},{25,9},{2,18},{10... | collective-permute-start | bytes 1179656 | tf_op jit(solution)/shard_map/ppermute | solution.py:238
  205.9 13.3 %collective-permute-start.7 = (bf16[1,4,128,384]{3,2,1,0:T(8,128)(2,1)S(1)}, bf16[1,4,128,384]{3,2,1,0:T(8,128)(2,1)S(1)}, u32[]{:S(2)}, u32[]{:S(2)}) collective-permute-start(bf16[1,4,128,384]{3,2,1,0:T(8,128)(2,1)S(1)} %slice.59), channel_id=1, source_target_pairs={{0,8},{8,0},{16,24},{24,16},{1,9},{9,1},{17,25},{25,17},{2,10},{10... | collective-permute-start | bytes 1179656 | tf_op jit(solution)/shard_map/ppermute | solution.py:238
Sparse Core Ops, SparseCore 0:
  10.8 52.2 all-gather.3
  65.3 27.9 all-gather.7
  94.8 28.5 all-gather.5
  144.6 35.7 reduce-scatter.2
  182.5 34.9 reduce-scatter.4

commit v4 on v1

v4 whole, which is shorter than its diff:
```python
import functools

import jax
import jax.numpy as jnp
from jax import lax
from jax.experimental import pallas as pl
from jax.experimental.pallas import tpu as pltpu
from jax.sharding import PartitionSpec as P

LANES = 128
PACK = 16
SLICES = 2
GROUP = 2
VMEM_LIMIT = 60 * 1024 * 1024
bf16, f32 = jnp.bfloat16, jnp.float32
ANY = pl.BlockSpec(memory_space=pl.ANY)
SMEM = pl.BlockSpec(memory_space=pltpu.SMEM)
FIRST = (((0,), (0,)), ((), ()))
LAST = (((1,), (1,)), ((), ()))


def dot(a, b, dims=(((1,), (0,)), ((), ()))):
    return lax.dot_general(a, b, dims, preferred_element_type=f32)


def up_kernel(groups, width, top, cap, place, rows, w_up, pick, meta, hid, scaled, slope_g, held, gates):
    experts = held.shape[0]
    i = pl.program_id(0)

    @pl.when(i < groups)
    def _():
        info = rows[:, pl.ds(width, LANES)]
        meta[...] = info
        across = info.astype(f32).T
        count = across.shape[1]
        ids, weights = across[:top], across[top : 2 * top]
        before = lax.broadcasted_iota(jnp.int32, (count, count), 0) < lax.broadcasted_iota(
            jnp.int32, (count, count), 1
        )
        chosen = [ids == (place[0] * experts + b).astype(f32) for b in range(experts)]
        member = [jnp.sum(jnp.where(hit, 1.0, 0.0), axis=0, keepdims=True) for hit in chosen]
        table = jnp.concatenate(member + [jnp.zeros((PACK - experts, count), f32)], axis=0)
        prior = dot(table.astype(bf16), before.astype(bf16))
        spot = lax.broadcasted_iota(jnp.int32, (cap, count), 0).astype(f32)
        for b in range(experts):
            rank = jnp.where(member[b] > 0.0, prior[b : b + 1], -1.0)
            hot = spot == rank
            gate = jnp.sum(jnp.where(chosen[b], weights, 0.0), axis=0, keepdims=True)
            one = jnp.where(hot, 1.0, 0.0)
            pick[0, pl.ds(b * cap, cap), :] = one.astype(bf16)
            at = pl.ds(pl.multiple_of(i * cap, PACK), cap)
            gates[b, at, :] = jnp.broadcast_to(jnp.sum(one * gate, axis=1, keepdims=True), (cap, LANES))
        got = dot(pick[0], rows[:, pl.ds(0, width)]).astype(bf16)
        for b in range(experts):
            held[b, pl.ds(pl.multiple_of(i * cap, PACK), cap), :] = got[b * cap : (b + 1) * cap]

    @pl.when(i >= groups)
    def _():
        b = i - groups
        pre = dot(held[b], w_up[0])
        gate = gates[b][:, :1]
        sig = 0.5 + 0.5 * jnp.tanh(0.5 * pre)
        act = pre * sig
        hid[0] = act.astype(bf16)
        scaled[0] = (gate * act).astype(bf16)
        slope_g[0] = (gate * (sig + act * (1.0 - sig))).astype(bf16)


def gather_rows(i, cap, pick, rows, held):
    experts = held.shape[0]
    got = dot(pick[0], rows[...]).astype(bf16)
    for b in range(experts):
        held[b, pl.ds(pl.multiple_of(i * cap, PACK), cap), :] = got[b * cap : (b + 1) * cap]


def down_copies(orders, b, sent, outs, sem):
    parts = len(orders[0])
    half = parts // 2
    copies = []
    for q in range(parts):
        for g, order in enumerate(orders):
            p = order.index(q)
            copies.append(
                pltpu.make_async_copy(sent.at[g, q, b], outs[2 * g + p // half].at[p % half, b], sem.at[g, q, b])
            )
    return copies


def down_rows(orders, place, b, held, scaled, sent, outs, sem):
    parts = len(orders[0])
    piece = held.shape[1] // parts
    cut = piece // len(orders)
    for q in range(parts):
        at = pl.multiple_of((place[1] ^ q) * piece, LANES)
        full = dot(held[:, pl.ds(at, piece)], scaled, FIRST).astype(bf16)
        for g in range(len(orders)):
            sent[g, q, b] = full[g * cut : (g + 1) * cut]
    for copy in down_copies(orders, b, sent, outs, sem):
        copy.start()


def mid_kernel(groups, cap, orders, place, pick, rows, w_down, scaled, back, *refs):
    outs, (held, sent, sem) = refs[:-3], refs[-3:]
    experts = held.shape[0]
    i = pl.program_id(0)

    @pl.when(i < groups)
    def _():
        gather_rows(i, cap, pick, rows, held)

    @pl.when(i >= groups)
    def _():
        b = i - groups
        down_rows(orders, place, b, held.at[b], scaled[0], sent, outs, sem)
        back[0] = dot(held[b], w_down[...].reshape(held.shape[2], back.shape[2]))

    @pl.when(i == groups + experts - 1)
    def _():
        for b in range(experts):
            for copy in down_copies(orders, b, sent, outs, sem):
                copy.wait()


def down_kernel(orders, place, rows, scaled, *refs):
    outs, (sent, sem) = refs[:-2], refs[-2:]
    experts = sent.shape[2]
    b = pl.program_id(0)
    down_rows(orders, place, b, rows.at[0], scaled[0], sent, outs, sem)

    @pl.when(b == experts - 1)
    def _():
        for e in range(experts):
            for copy in down_copies(orders, e, sent, outs, sem):
                copy.wait()


def tail_kernel(groups, cap, width, top, has_before, after, place, pick, rows, w_down, w_up, hid, slope_g, meta, *refs):
    before = refs[0] if has_before else None
    out, kept, held, grads, sem = refs[has_before + after :]
    experts = held.shape[0]
    i = pl.program_id(0)

    @pl.when(i < groups)
    def _():
        gather_rows(i, cap, pick, rows, held)

    @pl.when((i >= groups) & (i < groups + experts))
    def _():
        b = i - groups
        pltpu.make_async_copy(held.at[b], kept.at[b], sem.at[b]).start()
        back = dot(held[b], w_down[...].reshape(held.shape[2], hid.shape[2]))
        if before is not None:
            back = back + before[0]
        gate = jnp.sum(back * hid[0].astype(f32), axis=1, keepdims=True)
        lane = lax.broadcasted_iota(jnp.int32, (back.shape[0], LANES), 1)
        gate = jnp.where(lane == b, gate, 0.0).astype(bf16)
        grad = (back * slope_g[0].astype(f32)).astype(bf16)
        route = dot(grad, w_up[0], LAST).astype(bf16)
        at = pl.ds(pl.multiple_of(b * cap, PACK), cap)
        for g in range(groups):
            grads[g, at, pl.ds(0, width)] = route[g * cap : (g + 1) * cap]
            grads[g, at, pl.ds(width, LANES)] = gate[g * cap : (g + 1) * cap]

    @pl.when(i >= groups + experts)
    def _():
        g = i - groups - experts
        total = dot(pick[0], grads[g], FIRST)
        out[:, pl.ds(0, width)] = total[:, :width].astype(bf16)
        by_expert = total[:, width:]
        info = meta[...].astype(f32)
        lane = lax.broadcasted_iota(jnp.int32, info.shape, 1)
        ids = jnp.where(lane < top, info, -1.0)
        picked = jnp.zeros(info.shape, f32)
        for b in range(experts):
            hit = ids == (place[0] * experts + b).astype(f32)
            picked = picked + jnp.where(hit, by_expert[:, b : b + 1], 0.0)
        out[:, pl.ds(width, LANES)] = picked.astype(bf16)

    @pl.when(i == 2 * groups + experts - 1)
    def _():
        for b in range(experts):
            pltpu.make_async_copy(held.at[b], kept.at[b], sem.at[b]).wait()


def cost(flops, nbytes):
    return pl.CostEstimate(flops=int(flops), bytes_accessed=int(nbytes), transcendentals=0)


def shards(tokens, cotangent, expert_ids, gate_weights, w_up, w_down):
    tok_rows, width = tokens.shape
    top = expert_ids.shape[1]
    ep_count, dp_count = lax.axis_size("ep"), lax.axis_size("dp")
    experts, _, hidden = w_up.shape
    base_load = tok_rows * top // (experts * ep_count)
    capacity = base_load + max(1, base_load // 16)
    total = ep_count * tok_rows
    groups = ep_count // GROUP
    members = GROUP * tok_rows
    cap = -(-GROUP * capacity // PACK) * PACK
    routes = groups * cap
    full = width + LANES
    place = jnp.stack([lax.axis_index("ep"), lax.axis_index("dp")]).astype(jnp.int32)
    bits = dp_count.bit_length() - 1
    turns = 2
    share = width // dp_count
    slices = SLICES if share % (SLICES * LANES) == 0 else 1
    piece = share // slices
    cols = dp_count * piece

    info = jnp.concatenate(
        [expert_ids.astype(bf16), gate_weights, jnp.zeros((tok_rows, LANES - 2 * top), bf16)], axis=1
    )
    x_all = lax.all_gather(jnp.concatenate([tokens, info], axis=1), "ep", axis=0, tiled=True)
    cut = cotangent.reshape(tok_rows, dp_count, slices, piece)
    cut = [cut[:, :, s].reshape(tok_rows, cols) for s in range(slices)]
    dy_all = []
    for part in cut:
        x_all, part = lax.optimization_barrier((x_all, part))
        dy_all.append(lax.all_gather(part, "ep", axis=0, tiled=True))

    def at_group(i):
        return jnp.minimum(i, groups - 1)

    def at_expert(i):
        return jnp.clip(i - groups, 0, experts - 1)

    def by_group(n):
        return pl.BlockSpec((members, n), lambda i: (at_group(i), 0))

    def by_expert(rows, n):
        return pl.BlockSpec((1, rows, n), lambda i: (at_expert(i), 0, 0))

    def shape(*dims, dtype=bf16):
        return jax.ShapeDtypeStruct(dims, dtype)

    def call(kernel, name, grid, flops, nbytes, **kw):
        return pl.pallas_call(
            kernel,
            grid=(grid,),
            compiler_params=pltpu.CompilerParams(vmem_limit_bytes=VMEM_LIMIT),
            cost_estimate=cost(flops, nbytes),
            name=name,
            **kw,
        )

    act = shape(experts, routes, hidden)
    act_spec = by_expert(routes, hidden)
    pick_spec = pl.BlockSpec((1, experts * cap, members), lambda i: (at_group(i), 0, 0))
    pick_flops = 2 * total * experts * cap * width
    main_flops = 2 * experts * routes * width * hidden
    row_bytes = 2 * experts * hidden * width
    pick, meta, hid, scaled, slope_g = call(
        functools.partial(up_kernel, groups, width, top, cap),
        "up",
        groups + experts,
        pick_flops + main_flops,
        2 * total * full + row_bytes,
        in_specs=[SMEM, by_group(full), by_expert(width, hidden)],
        out_specs=[pick_spec, by_group(LANES), act_spec, act_spec, act_spec],
        out_shape=[shape(groups, experts * cap, members), shape(total, LANES), act, act, act],
        scratch_shapes=[pltpu.VMEM((experts, routes, width), bf16), pltpu.VMEM((experts, routes, LANES), f32)],
    )(place, x_all, w_up)

    orders = []
    for g in range(turns):
        turn = [(g + t) % bits for t in range(bits)]
        orders.append(
            tuple(sum(((p >> (bits - 1 - t)) & 1) << turn[t] for t in range(bits)) for p in range(dp_count))
        )
    orders = tuple(orders)
    cut_rows = piece // turns
    down_outs = [shape(dp_count // 2, experts, cut_rows, hidden)] * (2 * turns)
    down_scratch = [
        pltpu.VMEM((turns, dp_count, experts, cut_rows, hidden), bf16),
        pltpu.SemaphoreType.DMA((turns, dp_count, experts)),
    ]
    w_cut = w_down.reshape(experts, dp_count, slices, piece, hidden)

    def cut_spec(s):
        return pl.BlockSpec((1, dp_count, 1, piece, hidden), lambda i: (at_expert(i), 0, s, 0, 0))

    def exchange(state, t):
        new = []
        for g, (keep, send) in enumerate(state):
            bit = 1 << ((g + t) % bits)
            got = lax.ppermute(send, "dp", [(i, i ^ bit) for i in range(dp_count)])
            both = keep.astype(f32) + got.astype(f32)
            if t < bits - 1:
                both = both.astype(bf16)
            half = both.shape[0] // 2
            new.append((both[:half], both[half:]) if half else both[0])
        return new

    states, before = [], None
    for s in range(slices - 1):
        before, *outs = call(
            functools.partial(mid_kernel, groups, cap, orders),
            "mid",
            groups + experts,
            (pick_flops + 2 * main_flops) // slices,
            2 * total * cols + 2 * row_bytes // slices,
            in_specs=[SMEM, pick_spec, by_group(cols), cut_spec(s), act_spec],
            out_specs=[act_spec] + [ANY] * len(down_outs),
            out_shape=[shape(experts, routes, hidden, dtype=f32)] + down_outs,
            scratch_shapes=[pltpu.VMEM((experts, routes, cols), bf16)] + down_scratch,
        )(place, pick, dy_all[s], w_cut, scaled)
        states.append([(outs[2 * g], outs[2 * g + 1]) for g in range(turns)])

    done, after = 0, []
    if states and bits > 1:
        states = [exchange(state, 0) for state in states]
        done, after = 1, [pair[0] for state in states for pair in state]

    def at_end(i):
        return jnp.clip(i - groups - experts, 0, groups - 1)

    last = slices - 1
    token_part, kept = call(
        functools.partial(tail_kernel, groups, cap, width, top, before is not None, len(after)),
        "tail",
        2 * groups + experts,
        pick_flops * (1 + 1 / slices) + main_flops * (1 + 1 / slices),
        2 * total * (full + cols) + 2 * row_bytes,
        in_specs=[
            SMEM,
            pl.BlockSpec(
                (1, experts * cap, members),
                lambda i: (jnp.where(i < groups, i, at_end(i)), 0, 0),
            ),
            by_group(cols),
            cut_spec(last),
            by_expert(width, hidden),
            act_spec,
            act_spec,
            pl.BlockSpec((members, LANES), lambda i: (at_end(i), 0)),
        ]
        + ([act_spec] if before is not None else [])
        + [ANY] * len(after),
        out_specs=[pl.BlockSpec((members, full), lambda i: (at_end(i), 0)), ANY],
        out_shape=[shape(total, full), shape(experts, routes, cols)],
        scratch_shapes=[
            pltpu.VMEM((experts, routes, cols), bf16),
            pltpu.VMEM((groups, experts * cap, full), bf16),
            pltpu.SemaphoreType.DMA((experts,)),
        ],
    )(place, pick, dy_all[last], w_cut, w_up, hid, slope_g, meta, *([] if before is None else [before]), *after)
    summed = lax.psum_scatter(token_part, "ep", scatter_dimension=0, tiled=True)

    outs = call(
        functools.partial(down_kernel, orders),
        "down",
        experts,
        main_flops // slices,
        2 * experts * routes * cols + row_bytes // slices,
        in_specs=[SMEM]
        + [pl.BlockSpec((1, routes, n), lambda b: (b, 0, 0)) for n in (cols, hidden)],
        out_specs=[ANY] * len(down_outs),
        out_shape=down_outs,
        scratch_shapes=down_scratch,
    )(place, kept, scaled)
    states = [(done, state) for state in states]
    states.append((0, [(outs[2 * g], outs[2 * g + 1]) for g in range(turns)]))
    for t in range(bits):
        states = [(done, state) if t < done else (done, exchange(state, t)) for done, state in states]
    states = [state for _, state in states]
    down_grad = jnp.concatenate([part for state in states for part in state], axis=1)
    return (summed[:, :width], summed[:, width : width + top], down_grad)


def solution(mesh):
    return jax.shard_map(
        shards,
        mesh=mesh,
        in_specs=(
            P(("dp", "ep"), None),
            P(("dp", "ep"), None),
            P(("dp", "ep"), None),
            P(("dp", "ep"), None),
            P("ep", None, None),
            P("ep", None, None),
        ),
        out_specs=(P(("dp", "ep"), None), P(("dp", "ep"), None), P("ep", "dp", None)),
        check_vma=False,
    )
```

time: 288 us -> 207 us (0.72)
  waiting for transfers between devices: 188 us -> 120 us
  matrix products: 49.3 us -> 0 us
  Pallas kernels: 0 us -> 45 us
  blocking collectives: 28.9 us -> 0 us
  local copies, waits for them, and re-layouts: 2.48 us -> 12.1 us
  starting transfers between devices: 0.38 us -> 9.54 us
    reduce_scatter x2 -> x1, waiting for transfers between devices: 120 us -> 5.5 us  [shards(): summed = lax.psum_scatter(token_part, 'ep', scatter_dimension=0, tiled=True)]
    dot_general x7 -> x0, matrix products: 49.3 us -> none  [the longest x1 12 us: shards(): jnp.einsum('brt,brd->td', pick, route_grad, preferred_element_type=f32)]
    ppermute x0 -> x8, waiting for transfers between devices: none -> 48.5 us  [exchange(): got = lax.ppermute(send, 'dp', [(i, i ^ bit) for i in range(dp_count)])]
    pallas_call x0 -> x4, Pallas kernels: none -> 45 us  [the longest x1 16.8 us: shards(): call(functools.partial(tail_kernel, groups, cap, width, top, before is no...]
    all_gather x2 -> x0, blocking collectives: 28.9 us -> none  [the longest x1 15.8 us: shards(): ids_all = lax.all_gather(expert_ids, 'ep', axis=0, tiled=True)]
    ppermute x0 -> x8, starting transfers between devices: none -> 9.38 us  [exchange(): got = lax.ppermute(send, 'dp', [(i, i ^ bit) for i in range(dp_count)])]
    unnamed x6 -> x4, waiting for transfers between devices: 9.12 us -> 0.07 us
    all_gather x2 -> x3, waiting for transfers between devices: 59.3 us -> 65.9 us  [the longest x1 48.8 us: shards(): lax.all_gather(jnp.concatenate([tokens, info], axis=1), 'ep', axis=0, til...]
  transfers between devices with their start and end apart: 5 -> 12, of which waited for: 5 -> 9; matrix products, arithmetic and copies ran while one was open for 13% -> 5% of each run, Pallas kernels for 0% -> 14%
where the time goes in v4:
time: 207 us; the launch traced here: 206 us
  waiting for transfers between devices  120 us (58%)
  Pallas kernels  45 us (22%)
  between operations  13.9 us (7%)
  local copies, waits for them, and re-layouts  12.1 us (6%)
  starting transfers between devices  9.54 us (5%)
  other arithmetic  5.45 us (3%)
    all_gather x1, waiting for transfers between devices, shards(): lax.all_gather(jnp.concatenate([tokens, info], axis=1), 'ep', axis=0, til...  48.8 us
    ppermute x8, waiting for transfers between devices, exchange(): got = lax.ppermute(send, 'dp', [(i, i ^ bit) for i in range(dp_count)])  48.5 us
    all_gather x2, waiting for transfers between devices, shards(): dy_all.append(lax.all_gather(part, 'ep', axis=0, tiled=True))  17 us
    pallas_call x1, Pallas kernels, shards(): call(functools.partial(tail_kernel, groups, cap, width, top, before is no...  16.8 us
    pallas_call x1, Pallas kernels, shards(): call(functools.partial(up_kernel, groups, width, top, cap), 'up', groups...  11.7 us
    pallas_call x1, Pallas kernels, shards(): call(functools.partial(mid_kernel, groups, cap, orders), 'mid', groups +...  10.5 us
    ppermute x8, starting transfers between devices, exchange(): got = lax.ppermute(send, 'dp', [(i, i ^ bit) for i in range(dp_count)])  9.38 us
    pallas_call x1, Pallas kernels, shards(): call(functools.partial(down_kernel, orders), 'down', experts, main_flops...  6 us
  transfers between devices with their start and end apart: 12, of which 9 were waited for; matrix products, arithmetic and copies ran while one was open for 5% of the time, Pallas kernels for 14%

profile of v4, /device:TPU:0, one launch (start us, length us, event | category | flops | bytes accessed | tf_op | source)
XLA Modules:
  0.0 205.9 jit_solution(15770701847095006675)
XLA Ops:
  7.2 0.0 all-gather.4.cloned.1.call-start
  7.2 0.7 convert_element_type.63
  8.0 0.1 copy.9
  8.1 0.8 copy.10
  8.9 1.9 concatenate.6
  10.8 0.0 all-gather.8.cloned.1.call-start
  10.8 0.4 reshape.12
  11.2 2.4 %slice_reduce_fusion = (bf16[128,4,256]{2,1,0:T(4,128)(2,1)S(1)}, bf16[128,4,256]{2,1,0:T(4,128)(2,1)S(1)}) fusion(bf16[128,4,2,256]{3,2,1,0:T(2,128)(2,1)S(1)} %reshape.12), kind=kLoop, calls=%fused_computation.9 | loop fusion | bytes 1048576 | tf_op jit(solution)/shard_map/slice | solution.py:215
  13.6 0.7 copy.16
  14.3 48.8 %all-gather.4.cloned.1.call-done.rows = bf16[1024,2176]{1,0:T(8,128)(2,1)} async-done(((bf16[128,2176]{1,0:T(8,128)(2,1)}), bf16[1024,2176]{1,0:T(8,128)(2,1)}) %all-gather.4.cloned.1.call-update) | async-done | bytes 4456464 | tf_op jit(solution)/shard_map/all_gather | solution.py:213
  63.2 0.0 all-gather.6.cloned.1.call-start
  63.2 0.8 copy.17
  64.0 0.0 reduce-scatter.2.cloned.1.call-start
  64.1 0.6 pad_add_fusion.place
  64.7 11.7 %up.1 = (bf16[4,320,256]{2,1,0:T(8,128)(2,1)}, bf16[1024,128]{1,0:T(8,128)(2,1)}, bf16[4,320,384]{2,1,0:T(8,128)(2,1)}, bf16[4,320,384]{2,1,0:T(8,128)(2,1)}, bf16[4,320,384]{2,1,0:T(8,128)(2,1)}) custom-call(s32[2]{0:T(128)} %pad_add_fusion.place, bf16[1024,2176]{1,0:T(8,128)(2,1)} %all-gather.4.cloned.1.call-done.rows, bf16[4,2048,384]{2,1,0:T(8,128)(2,1)} %w_up.3), custom_call_target="tpu_custom_call" | custom-call | flops 3355443200 | bytes 10747904 | tf_op jit(solution)/shard_map/up/pallas_call | solution.py:252
  76.4 17.0 %all-gather.8.cloned.1.call-done.rows = bf16[1024,1024]{1,0:T(8,128)(2,1)} async-done(((bf16[128,1024]{1,0:T(8,128)(2,1)}), bf16[1024,1024]{1,0:T(8,128)(2,1)}) %all-gather.8.cloned.1.call-update) | async-done | bytes 2097168 | tf_op jit(solution)/shard_map/all_gather | solution.py:219
  93.4 10.5 %mid.1 = (f32[4,320,384]{2,1,0:T(8,128)}, bf16[2,4,128,384]{3,2,1,0:T(8,128)(2,1)}, bf16[2,4,128,384]{3,2,1,0:T(8,128)(2,1)}, bf16[2,4,128,384]{3,2,1,0:T(8,128)(2,1)}, bf16[2,4,128,384]{3,2,1,0:T(8,128)(2,1)}) custom-call(s32[2]{0:T(128)} %pad_add_fusion.place, bf16[4,320,256]{2,1,0:T(8,128)(2,1)} %get-tuple-element.25.pick, ...), custom_call_target="tpu_custom_call" | custom-call | flops 2684354560 | bytes 8388608 | tf_op jit(solution)/shard_map/mid/pallas_call | solution.py:296
  103.9 1.6 collective-permute-start
  105.6 1.5 collective-permute-start.1
  107.0 16.8 %collective-permute-done = bf16[2,4,128,384]{3,2,1,0:T(8,128)(2,1)S(1)} collective-permute-done((bf16[2,4,128,384]{3,2,1,0:T(8,128)(2,1)}, bf16[2,4,128,384]{3,2,1,0:T(8,128)(2,1)S(1)}, u32[]{:S(2)}, u32[]{:S(2)}) %collective-permute-start) | collective-permute-done | bytes 786464 | tf_op jit(solution)/shard_map/ppermute | solution.py:286
  123.9 1.3 add_convert_fusion.3
  125.2 0.8 fusion
  126.1 0.2 add_convert_fusion.2
  126.3 0.8 fusion.1
  127.1 16.8 %tail.1 = (bf16[1024,2176]{1,0:T(8,128)(2,1)}, bf16[4,320,1024]{2,1,0:T(8,128)(2,1)}) custom-call(s32[2]{0:T(128)} %pad_add_fusion.place, bf16[4,320,256]{2,1,0:T(8,128)(2,1)} %get-tuple-element.25.pick, bf16[1024,1024]{1,0:T(8,128)(2,1)} %all-gather.6.cloned.1.call-done.rows, bf16[4,4,2,256,384]{4,3,2,1,0:T(8,128)(2,1)} %bitcast.16, ...), custom_call_target="tpu_custom_call" | custom-call | flops 5033164800 | bytes 19136512 | tf_op jit(solution)/shard_map/tail/pallas_call | solution.py:318
  143.9 6.0 %down.1 = (bf16[2,4,128,384]{3,2,1,0:T(8,128)(2,1)}, bf16[2,4,128,384]{3,2,1,0:T(8,128)(2,1)}, bf16[2,4,128,384]{3,2,1,0:T(8,128)(2,1)}, bf16[2,4,128,384]{3,2,1,0:T(8,128)(2,1)}) custom-call(s32[2]{0:T(128)} %pad_add_fusion.place, bf16[4,320,1024]{2,1,0:T(8,128)(2,1)} %get-tuple-element.38.rows, bf16[4,320,384]{2,1,0:T(8,128)(2,1)} %get-tuple-element.31.scaled), custom_call_target="tpu_custom_call" | custom-call | flops 1006632960 | bytes 5767168 | tf_op jit(solution)/shard_map/down/pallas_call | solution.py:349
  149.9 1.7 collective-permute-start.4
  151.6 1.5 collective-permute-start.2
  153.1 0.5 collective-permute-start.6
  153.6 0.4 collective-permute-start.3
  154.1 9.6 %collective-permute-done.2 = bf16[1,4,128,384]{3,2,1,0:T(8,128)(2,1)S(1)} collective-permute-done((bf16[1,4,128,384]{3,2,1,0:T(8,128)(2,1)S(1)}, bf16[1,4,128,384]{3,2,1,0:T(8,128)(2,1)S(1)}, u32[]{:S(2)}, u32[]{:S(2)}) %collective-permute-start.2) | collective-permute-done | bytes 393248 | tf_op jit(solution)/shard_map/ppermute | solution.py:286
  163.6 0.1 add_bitcast_fusion.3
  163.7 7.0 %collective-permute-done.4 = bf16[2,4,128,384]{3,2,1,0:T(8,128)(2,1)S(1)} collective-permute-done((bf16[2,4,128,384]{3,2,1,0:T(8,128)(2,1)}, bf16[2,4,128,384]{3,2,1,0:T(8,128)(2,1)S(1)}, u32[]{:S(2)}, u32[]{:S(2)}) %collective-permute-start.4) | collective-permute-done | bytes 786464 | tf_op jit(solution)/shard_map/ppermute | solution.py:286
  170.7 0.2 add_convert_fusion.1
  170.9 1.7 collective-permute-start.5
  172.6 7.9 %collective-permute-done.6 = bf16[2,4,128,384]{3,2,1,0:T(8,128)(2,1)S(1)} collective-permute-done((bf16[2,4,128,384]{3,2,1,0:T(8,128)(2,1)}, bf16[2,4,128,384]{3,2,1,0:T(8,128)(2,1)S(1)}, u32[]{:S(2)}, u32[]{:S(2)}) %collective-permute-start.6) | collective-permute-done | bytes 786464 | tf_op jit(solution)/shard_map/ppermute | solution.py:286
  180.5 0.2 add_convert_fusion
  180.7 0.5 collective-permute-start.7
  181.3 0.1 add_bitcast_fusion.2
  181.3 5.7 %collective-permute-done.5 = bf16[1,4,128,384]{3,2,1,0:T(8,128)(2,1)S(1)} collective-permute-done((bf16[1,4,128,384]{3,2,1,0:T(8,128)(2,1)S(1)}, bf16[1,4,128,384]{3,2,1,0:T(8,128)(2,1)S(1)}, u32[]{:S(2)}, u32[]{:S(2)}) %collective-permute-start.5) | collective-permute-done | bytes 393248 | tf_op jit(solution)/shard_map/ppermute | solution.py:286
  187.0 0.1 add_bitcast_fusion.1
  187.1 1.5 collective-permute-done.7
  188.6 0.1 add_bitcast_fusion
  188.7 1.9 pad_maximum_fusion
  190.5 5.5 %reduce-scatter.2.cloned.1.call-done = bf16[128,2176]{1,0:T(8,128)(2,1)} async-done(((bf16[1024,2176]{1,0:T(8,128)(2,1)}), bf16[128,2176]{1,0:T(8,128)(2,1)}) %reduce-scatter.2.cloned.1.call-update) | async-done | bytes 557072 | tf_op jit(solution)/shard_map/reduce_scatter | solution.py:347
  196.0 0.8 slice.53
  196.8 0.7 copy.13
  197.5 1.9 slice.52
  (18 shorter events, 0.2 us)
Async XLA Ops:
  7.2 3.7 %copy-start.3 = (bf16[128,2048]{1,0:T(8,128)(2,1)S(1)}, bf16[128,2048]{1,0:T(8,128)(2,1)}, u32[]{:S(2)}) copy-start(bf16[128,2048]{1,0:T(8,128)(2,1)} %param.7) | copy-start | bytes 1572868
  7.2 56.0 %all-gather.4.cloned.1.call-start = ((), (), s32[]{:S(2)}) async-start(), calls=%async_computation.1 | async-start | bytes 5013504 | tf_op jit(solution)/shard_map/all_gather | solution.py:213
  10.8 82.7 %all-gather.8.cloned.1.call-start = ((), (), s32[]{:S(2)}) async-start(), calls=%async_computation.3 | async-start | bytes 2359296 | tf_op jit(solution)/shard_map/all_gather | solution.py:219
  63.2 63.9 %all-gather.6.cloned.1.call-start = ((), (), s32[]{:S(2)}) async-start(), calls=%async_computation.2 | async-start | bytes 2359296 | tf_op jit(solution)/shard_map/all_gather | solution.py:219
  64.0 132.0 %reduce-scatter.2.cloned.1.call-start = ((), (), s32[]{:S(2)}) async-start(), calls=%async_computation.4 | async-start | bytes 5013504 | tf_op jit(solution)/shard_map/reduce_scatter | solution.py:347
  103.9 22.1 %copy-start.2 = (bf16[2,4,128,384]{3,2,1,0:T(8,128)(2,1)S(1)}, bf16[2,4,128,384]{3,2,1,0:T(8,128)(2,1)}, u32[]{:S(2)}) copy-start(bf16[2,4,128,384]{3,2,1,0:T(8,128)(2,1)} %get-tuple-element.35) | copy-start | bytes 2359300
  103.9 19.9 %collective-permute-start = (bf16[2,4,128,384]{3,2,1,0:T(8,128)(2,1)}, bf16[2,4,128,384]{3,2,1,0:T(8,128)(2,1)S(1)}, u32[]{:S(2)}, u32[]{:S(2)}) collective-permute-start(bf16[2,4,128,384]{3,2,1,0:T(8,128)(2,1)} %get-tuple-element.34), channel_id=1, source_target_pairs={{0,8},{8,0},{16,24},{24,16},{1,9},{9,1},{17,25},{25,17},{2,10},{10... | collective-permute-start | bytes 2359304 | tf_op jit(solution)/shard_map/ppermute | solution.py:286
  105.6 20.5 %collective-permute-start.1 = (bf16[2,4,128,384]{3,2,1,0:T(8,128)(2,1)}, bf16[2,4,128,384]{3,2,1,0:T(8,128)(2,1)S(1)}, u32[]{:S(2)}, u32[]{:S(2)}) collective-permute-start(bf16[2,4,128,384]{3,2,1,0:T(8,128)(2,1)} %get-tuple-element.36), channel_id=1, source_target_pairs={{0,16},{8,24},{16,0},{24,8},{1,17},{9,25},{17,1},{25,9},{2,18},{10... | collective-permute-start | bytes 2359304 | tf_op jit(solution)/shard_map/ppermute | solution.py:286
  149.9 20.8 %copy-start.1 = (bf16[2,4,128,384]{3,2,1,0:T(8,128)(2,1)S(1)}, bf16[2,4,128,384]{3,2,1,0:T(8,128)(2,1)}, u32[]{:S(2)}) copy-start(bf16[2,4,128,384]{3,2,1,0:T(8,128)(2,1)} %get-tuple-element.39) | copy-start | bytes 2359300
  149.9 20.8 %collective-permute-start.4 = (bf16[2,4,128,384]{3,2,1,0:T(8,128)(2,1)}, bf16[2,4,128,384]{3,2,1,0:T(8,128)(2,1)S(1)}, u32[]{:S(2)}, u32[]{:S(2)}) collective-permute-start(bf16[2,4,128,384]{3,2,1,0:T(8,128)(2,1)} %get-tuple-element.40), channel_id=1, source_target_pairs={{0,8},{8,0},{16,24},{24,16},{1,9},{9,1},{17,25},{25,17},{2,10},{10... | collective-permute-start | bytes 2359304 | tf_op jit(solution)/shard_map/ppermute | solution.py:286
  151.6 12.1 %collective-permute-start.2 = (bf16[1,4,128,384]{3,2,1,0:T(8,128)(2,1)S(1)}, bf16[1,4,128,384]{3,2,1,0:T(8,128)(2,1)S(1)}, u32[]{:S(2)}, u32[]{:S(2)}) collective-permute-start(bf16[1,4,128,384]{3,2,1,0:T(8,128)(2,1)S(1)} %get-tuple-element.48), channel_id=1, source_target_pairs={{0,16},{8,24},{16,0},{24,8},{1,17},{9,25},{17,1},{25,9},{2,18},{10... | collective-permute-start | bytes 1179656 | tf_op jit(solution)/shard_map/ppermute | solution.py:286
  153.1 27.4 %collective-permute-start.6 = (bf16[2,4,128,384]{3,2,1,0:T(8,128)(2,1)}, bf16[2,4,128,384]{3,2,1,0:T(8,128)(2,1)S(1)}, u32[]{:S(2)}, u32[]{:S(2)}) collective-permute-start(bf16[2,4,128,384]{3,2,1,0:T(8,128)(2,1)} %get-tuple-element.42), channel_id=1, source_target_pairs={{0,16},{8,24},{16,0},{24,8},{1,17},{9,25},{17,1},{25,9},{2,18},{10... | collective-permute-start | bytes 2359304 | tf_op jit(solution)/shard_map/ppermute | solution.py:286
  153.6 26.9 %copy-start = (bf16[2,4,128,384]{3,2,1,0:T(8,128)(2,1)S(1)}, bf16[2,4,128,384]{3,2,1,0:T(8,128)(2,1)}, u32[]{:S(2)}) copy-start(bf16[2,4,128,384]{3,2,1,0:T(8,128)(2,1)} %get-tuple-element.41) | copy-start | bytes 2359300
  153.6 27.6 %collective-permute-start.3 = (bf16[1,4,128,384]{3,2,1,0:T(8,128)(2,1)S(1)}, bf16[1,4,128,384]{3,2,1,0:T(8,128)(2,1)S(1)}, u32[]{:S(2)}, u32[]{:S(2)}) collective-permute-start(bf16[1,4,128,384]{3,2,1,0:T(8,128)(2,1)S(1)} %get-tuple-element.50), channel_id=1, source_target_pairs={{0,8},{8,0},{16,24},{24,16},{1,9},{9,1},{17,25},{25,17},{2,10},{10... | collective-permute-start | bytes 1179656 | tf_op jit(solution)/shard_map/ppermute | solution.py:286
  170.9 16.1 %collective-permute-start.5 = (bf16[1,4,128,384]{3,2,1,0:T(8,128)(2,1)S(1)}, bf16[1,4,128,384]{3,2,1,0:T(8,128)(2,1)S(1)}, u32[]{:S(2)}, u32[]{:S(2)}) collective-permute-start(bf16[1,4,128,384]{3,2,1,0:T(8,128)(2,1)S(1)} %slice.57), channel_id=1, source_target_pairs={{0,16},{8,24},{16,0},{24,8},{1,17},{9,25},{17,1},{25,9},{2,18},{10... | collective-permute-start | bytes 1179656 | tf_op jit(solution)/shard_map/ppermute | solution.py:286
  180.7 7.8 %collective-permute-start.7 = (bf16[1,4,128,384]{3,2,1,0:T(8,128)(2,1)S(1)}, bf16[1,4,128,384]{3,2,1,0:T(8,128)(2,1)S(1)}, u32[]{:S(2)}, u32[]{:S(2)}) collective-permute-start(bf16[1,4,128,384]{3,2,1,0:T(8,128)(2,1)S(1)} %slice.59), channel_id=1, source_target_pairs={{0,8},{8,0},{16,24},{24,16},{1,9},{9,1},{17,25},{25,17},{2,10},{10... | collective-permute-start | bytes 1179656 | tf_op jit(solution)/shard_map/ppermute | solution.py:286
Sparse Core Ops, SparseCore 0:
  10.9 52.2 all-gather.3
  65.3 28.0 all-gather.7
  95.0 28.5 all-gather.5
  144.0 51.9 reduce-scatter.1

commit v5 on v4

--- a/solution.py
+++ b/solution.py
@@ -23,12 +23,66 @@
     return lax.dot_general(a, b, dims, preferred_element_type=f32)
 
 
-def up_kernel(groups, width, top, cap, place, rows, w_up, pick, meta, hid, scaled, slope_g, held, gates):
+def pack_kernel(top, parts, tokens, cotangent, ids, gates, x_out, *dy_out):
+    count, width = tokens.shape
+    x_out[:, pl.ds(0, width)] = tokens[...]
+    info = jnp.concatenate(
+        [ids[...].astype(f32), gates[...].astype(f32), jnp.zeros((LANES - 2 * top, count), f32)], axis=0
+    )
+    x_out[:, pl.ds(width, LANES)] = info.T.astype(bf16)
+    piece = width // parts // len(dy_out)
+    for s, out in enumerate(dy_out):
+        for i in range(parts):
+            out[:, pl.ds(i * piece, piece)] = cotangent[:, pl.ds((i * len(dy_out) + s) * piece, piece)]
+
+
+def start_blocks(place, chips, own, mine, other, dst, sem):
+    half = own.shape[0] // 2
+    left_core = place[2] == 0
+
+    def start(ref, slot, flip):
+        for part in range(2):
+            to = (part ^ flip) * half
+            if not isinstance(flip, int):
+                to = pl.multiple_of(to, half)
+            pltpu.make_async_copy(
+                ref.at[pl.ds(part * half, half), :], dst.at[slot, pl.ds(to, half), :], sem.at[slot, part]
+            ).start()
+
+    start(own, 0, place[2])
+    for slot in range(1, chips):
+        left = place[3] >= slot
+        for is_left in (True, False):
+            for is_core in (True, False):
+                step = slot if is_left else chips - slot
+                ref = (mine if is_left == is_core else other)[step - 1]
+
+                @pl.when((left == is_left) & (left_core == is_core))
+                def _():
+                    start(ref, slot, 0 if is_left else 1)
+
+
+def up_kernel(groups, width, top, cap, place, *refs):
+    own, refs = refs[0], refs[1:]
+    mine, other = refs[: groups - 1], refs[groups - 1 : 2 * groups - 2]
+    w_up, pick, meta, hid, scaled, slope_g, held, gates, all_rows, sem = refs[2 * groups - 2 :]
     experts = held.shape[0]
     i = pl.program_id(0)
 
+    @pl.when(i == 0)
+    def _():
+        start_blocks(place, groups, own, mine, other, all_rows, sem)
+
     @pl.when(i < groups)
     def _():
+        half = own.shape[0] // 2
+        for part in range(2):
+            pltpu.make_async_copy(
+                own.at[pl.ds(part * half, half), :], all_rows.at[i, pl.ds(part * half, half), :], sem.at[i, part]
+            ).wait()
+        rows = all_rows.at[i]
+        group = lax.rem(place[3] - i + groups, groups)
+        first = pl.multiple_of(group * cap, PACK)
         info = rows[:, pl.ds(width, LANES)]
         meta[...] = info
         across = info.astype(f32).T
@@ -44,15 +98,15 @@
         spot = lax.broadcasted_iota(jnp.int32, (cap, count), 0).astype(f32)
         for b in range(experts):
             rank = jnp.where(member[b] > 0.0, prior[b : b + 1], -1.0)
-            hot = spot == rank
+            one = jnp.where(spot == rank, 1.0, 0.0)
             gate = jnp.sum(jnp.where(chosen[b], weights, 0.0), axis=0, keepdims=True)
-            one = jnp.where(hot, 1.0, 0.0)
             pick[0, pl.ds(b * cap, cap), :] = one.astype(bf16)
-            at = pl.ds(pl.multiple_of(i * cap, PACK), cap)
-            gates[b, at, :] = jnp.broadcast_to(jnp.sum(one * gate, axis=1, keepdims=True), (cap, LANES))
+            gates[b, pl.ds(first, cap), :] = jnp.broadcast_to(
+                jnp.sum(one * gate, axis=1, keepdims=True), (cap, LANES)
+            )
         got = dot(pick[0], rows[:, pl.ds(0, width)]).astype(bf16)
         for b in range(experts):
-            held[b, pl.ds(pl.multiple_of(i * cap, PACK), cap), :] = got[b * cap : (b + 1) * cap]
+            held[b, pl.ds(first, cap), :] = got[b * cap : (b + 1) * cap]
 
     @pl.when(i >= groups)
     def _():
@@ -121,8 +175,8 @@
                 copy.wait()
 
 
-def down_kernel(orders, place, rows, scaled, *refs):
-    outs, (sent, sem) = refs[:-2], refs[-2:]
+def down_kernel(orders, after, place, rows, scaled, *refs):
+    outs, (sent, sem) = refs[after:-2], refs[-2:]
     experts = sent.shape[2]
     b = pl.program_id(0)
     down_rows(orders, place, b, rows.at[0], scaled[0], sent, outs, sem)
@@ -134,9 +188,9 @@
                 copy.wait()
 
 
-def tail_kernel(groups, cap, width, top, has_before, after, place, pick, rows, w_down, w_up, hid, slope_g, meta, *refs):
+def tail_kernel(groups, cap, width, top, has_before, place, pick, rows, w_down, w_up, hid, slope_g, meta, *refs):
     before = refs[0] if has_before else None
-    out, kept, held, grads, sem = refs[has_before + after :]
+    out, kept, held, grads, sem = refs[has_before:]
     experts = held.shape[0]
     i = pl.program_id(0)
 
@@ -199,7 +253,8 @@
     cap = -(-GROUP * capacity // PACK) * PACK
     routes = groups * cap
     full = width + LANES
-    place = jnp.stack([lax.axis_index("ep"), lax.axis_index("dp")]).astype(jnp.int32)
+    here = lax.axis_index("ep")
+    place = jnp.stack([here, lax.axis_index("dp"), here % GROUP, here // GROUP]).astype(jnp.int32)
     bits = dp_count.bit_length() - 1
     turns = 2
     share = width // dp_count
@@ -207,16 +262,34 @@
     piece = share // slices
     cols = dp_count * piece
 
-    info = jnp.concatenate(
-        [expert_ids.astype(bf16), gate_weights, jnp.zeros((tok_rows, LANES - 2 * top), bf16)], axis=1
-    )
-    x_all = lax.all_gather(jnp.concatenate([tokens, info], axis=1), "ep", axis=0, tiled=True)
-    cut = cotangent.reshape(tok_rows, dp_count, slices, piece)
-    cut = [cut[:, :, s].reshape(tok_rows, cols) for s in range(slices)]
-    dy_all = []
-    for part in cut:
-        x_all, part = lax.optimization_barrier((x_all, part))
-        dy_all.append(lax.all_gather(part, "ep", axis=0, tiled=True))
+    def shape(*dims, dtype=bf16):
+        return jax.ShapeDtypeStruct(dims, dtype)
+
+    x_own, *dy_own = pl.pallas_call(
+        functools.partial(pack_kernel, top, dp_count),
+        out_shape=[shape(tok_rows, full)] + [shape(tok_rows, cols)] * slices,
+        compiler_params=pltpu.CompilerParams(vmem_limit_bytes=VMEM_LIMIT),
+        cost_estimate=cost(0, 8 * tok_rows * width),
+        name="pack",
+    )(tokens, cotangent, expert_ids.T, gate_weights.T)
+    dy_all = [lax.all_gather(part, "ep", axis=0, tiled=True) for part in dy_own]
+
+    def reach(p, step):
+        q = p + GROUP * step if p % GROUP == 0 else p - GROUP * step
+        return q if 0 <= q < ep_count else None
+
+    def hop(value, pairs):
+        return lax.ppermute(value, "ep", pairs)
+
+    x_own = jnp.concatenate([x_own, hop(x_own, [(p, p ^ 1) for p in range(ep_count)])], axis=0)
+    x_mine, x_other, moving = [], [], x_own
+    for step in range(1, groups):
+        moving = hop(
+            moving,
+            [(p, reach(p, 1)) for p in range(ep_count) if None not in (reach(p, 1), reach(p, 1 - step))],
+        )
+        x_mine.append(moving)
+        x_other.append(hop(moving, [(p, p ^ 1) for p in range(ep_count) if reach(p, -step) is not None]))
 
     def at_group(i):
         return jnp.minimum(i, groups - 1)
@@ -224,28 +297,34 @@
     def at_expert(i):
         return jnp.clip(i - groups, 0, experts - 1)
 
+    def at_slot(i, place):
+        return lax.rem(place[3] - at_group(i) + groups, groups)
+
     def by_group(n):
-        return pl.BlockSpec((members, n), lambda i: (at_group(i), 0))
+        return pl.BlockSpec((members, n), lambda i, *_: (at_group(i), 0))
 
     def by_expert(rows, n):
-        return pl.BlockSpec((1, rows, n), lambda i: (at_expert(i), 0, 0))
-
-    def shape(*dims, dtype=bf16):
-        return jax.ShapeDtypeStruct(dims, dtype)
-
-    def call(kernel, name, grid, flops, nbytes, **kw):
+        return pl.BlockSpec((1, rows, n), lambda i, *_: (at_expert(i), 0, 0))
+
+    def call(kernel, name, grid, flops, nbytes, in_specs, out_specs, out_shape, scratch_shapes, prefetch=0):
         return pl.pallas_call(
             kernel,
-            grid=(grid,),
+            grid_spec=pltpu.PrefetchScalarGridSpec(
+                num_scalar_prefetch=prefetch,
+                grid=(grid,),
+                in_specs=in_specs,
+                out_specs=out_specs,
+                scratch_shapes=scratch_shapes,
+            ),
+            out_shape=out_shape,
             compiler_params=pltpu.CompilerParams(vmem_limit_bytes=VMEM_LIMIT),
             cost_estimate=cost(flops, nbytes),
             name=name,
-            **kw,
         )
 
     act = shape(experts, routes, hidden)
     act_spec = by_expert(routes, hidden)
-    pick_spec = pl.BlockSpec((1, experts * cap, members), lambda i: (at_group(i), 0, 0))
+    pick_spec = pl.BlockSpec((1, experts * cap, members), lambda i, *_: (at_group(i), 0, 0))
     pick_flops = 2 * total * experts * cap * width
     main_flops = 2 * experts * routes * width * hidden
     row_bytes = 2 * experts * hidden * width
@@ -255,11 +334,23 @@
         groups + experts,
         pick_flops + main_flops,
         2 * total * full + row_bytes,
-        in_specs=[SMEM, by_group(full), by_expert(width, hidden)],
-        out_specs=[pick_spec, by_group(LANES), act_spec, act_spec, act_spec],
+        prefetch=1,
+        in_specs=[ANY] * (2 * groups - 1) + [by_expert(width, hidden)],
+        out_specs=[
+            pl.BlockSpec((1, experts * cap, members), lambda i, place: (at_slot(i, place), 0, 0)),
+            pl.BlockSpec((members, LANES), lambda i, place: (at_slot(i, place), 0)),
+            act_spec,
+            act_spec,
+            act_spec,
+        ],
         out_shape=[shape(groups, experts * cap, members), shape(total, LANES), act, act, act],
-        scratch_shapes=[pltpu.VMEM((experts, routes, width), bf16), pltpu.VMEM((experts, routes, LANES), f32)],
-    )(place, x_all, w_up)
+        scratch_shapes=[
+            pltpu.VMEM((experts, routes, width), bf16),
+            pltpu.VMEM((experts, routes, LANES), f32),
+            pltpu.VMEM((groups, members, full), bf16),
+            pltpu.SemaphoreType.DMA((groups, 2)),
+        ],
+    )(place, x_own, *x_mine, *x_other, w_up)
 
     orders = []
     for g in range(turns):
@@ -316,11 +407,11 @@
 
     last = slices - 1
     token_part, kept = call(
-        functools.partial(tail_kernel, groups, cap, width, top, before is not None, len(after)),
+        functools.partial(tail_kernel, groups, cap, width, top, before is not None),
         "tail",
         2 * groups + experts,
-        pick_flops * (1 + 1 / slices) + main_flops * (1 + 1 / slices),
-        2 * total * (full + cols) + 2 * row_bytes,
+        8 * main_flops,
+        4 * row_bytes,
         in_specs=[
             SMEM,
             pl.BlockSpec(
@@ -334,8 +425,7 @@
             act_spec,
             pl.BlockSpec((members, LANES), lambda i: (at_end(i), 0)),
         ]
-        + ([act_spec] if before is not None else [])
-        + [ANY] * len(after),
+        + ([act_spec] if before is not None else []),
         out_specs=[pl.BlockSpec((members, full), lambda i: (at_end(i), 0)), ANY],
         out_shape=[shape(total, full), shape(experts, routes, cols)],
         scratch_shapes=[
@@ -343,21 +433,22 @@
             pltpu.VMEM((groups, experts * cap, full), bf16),
             pltpu.SemaphoreType.DMA((experts,)),
         ],
-    )(place, pick, dy_all[last], w_cut, w_up, hid, slope_g, meta, *([] if before is None else [before]), *after)
+    )(place, pick, dy_all[last], w_cut, w_up, hid, slope_g, meta, *([] if before is None else [before]))
     summed = lax.psum_scatter(token_part, "ep", scatter_dimension=0, tiled=True)
 
     outs = call(
-        functools.partial(down_kernel, orders),
+        functools.partial(down_kernel, orders, len(after)),
         "down",
         experts,
-        main_flops // slices,
-        2 * experts * routes * cols + row_bytes // slices,
+        16 * main_flops,
+        8 * row_bytes,
         in_specs=[SMEM]
-        + [pl.BlockSpec((1, routes, n), lambda b: (b, 0, 0)) for n in (cols, hidden)],
+        + [pl.BlockSpec((1, routes, n), lambda b: (b, 0, 0)) for n in (cols, hidden)]
+        + [ANY] * len(after),
         out_specs=[ANY] * len(down_outs),
         out_shape=down_outs,
         scratch_shapes=down_scratch,
-    )(place, kept, scaled)
+    )(place, kept, scaled, *after)
     states = [(done, state) for state in states]
     states.append((0, [(outs[2 * g], outs[2 * g + 1]) for g in range(turns)]))
     for t in range(bits):

time: 207 us -> 222 us (1.072)
  the two profiles are of different devices: /device:TPU:0 before, /device:TPU:24 now
where the time goes in v5:
time: 222 us; the launch traced here: 221 us
  waiting for transfers between devices  128 us (58%)
  Pallas kernels  48.1 us (22%)
  starting transfers between devices  20.4 us (9%)
  between operations  13.9 us (6%)
  local copies, waits for them, and re-layouts  7.3 us (3%)
  other arithmetic  3.62 us (2%)
    ppermute x7, waiting for transfers between devices, hop(): return lax.ppermute(value, 'ep', pairs)  79.5 us
    ppermute x8, waiting for transfers between devices, exchange(): got = lax.ppermute(send, 'dp', [(i, i ^ bit) for i in range(dp_count)])  48.5 us
    pallas_call x1, Pallas kernels, shards(): call(functools.partial(tail_kernel, groups, cap, width, top, before is no...  16.8 us
    pallas_call x1, Pallas kernels, shards(): call(functools.partial(up_kernel, groups, width, top, cap), 'up', groups...  12.6 us
    ppermute x7, starting transfers between devices, hop(): return lax.ppermute(value, 'ep', pairs)  10.9 us
    pallas_call x1, Pallas kernels, shards(): call(functools.partial(mid_kernel, groups, cap, orders), 'mid', groups +...  10.5 us
    ppermute x8, starting transfers between devices, exchange(): got = lax.ppermute(send, 'dp', [(i, i ^ bit) for i in range(dp_count)])  9.37 us
    pallas_call x1, Pallas kernels, shards(): call(functools.partial(down_kernel, orders, len(after)), 'down', experts,...  5.97 us
  transfers between devices with their start and end apart: 18, of which 12 were waited for; matrix products, arithmetic and copies ran while one was open for 3% of the time, Pallas kernels for 13%

profile of v5, /device:TPU:24, one launch (start us, length us, event | category | flops | bytes accessed | tf_op | source)
XLA Modules:
  0.0 221.4 jit_solution(4302952657683571022)
XLA Ops:
  7.2 2.2 pack.1
  9.6 1.1 constant_dynamic-update-slice_fusion.1
  10.7 1.1 collective-permute-done
  11.8 1.3 collective-permute-start.1
  13.1 32.9 %collective-permute-done.1.refs_1_ = bf16[256,2176]{1,0:T(8,128)(2,1)S(1)} collective-permute-done((bf16[256,2176]{1,0:T(8,128)(2,1)S(1)}, bf16[256,2176]{1,0:T(8,128)(2,1)S(1)}, u32[]{:S(2)}, u32[]{:S(2)}) %collective-permute-start.1) | collective-permute-done | bytes 1114144 | tf_op jit(solution)/shard_map/ppermute | solution.py:282
  46.0 1.3 collective-permute-start.2
  47.4 32.9 %collective-permute-done.2.refs_2_ = bf16[256,2176]{1,0:T(8,128)(2,1)S(1)} collective-permute-done((bf16[256,2176]{1,0:T(8,128)(2,1)S(1)}, bf16[256,2176]{1,0:T(8,128)(2,1)S(1)}, u32[]{:S(2)}, u32[]{:S(2)}) %collective-permute-start.2) | collective-permute-done | bytes 1114144 | tf_op jit(solution)/shard_map/ppermute | solution.py:282
  80.3 1.3 collective-permute-start.3
  81.6 2.4 %collective-permute-start.4 = (bf16[256,2176]{1,0:T(8,128)(2,1)S(1)}, bf16[256,2176]{1,0:T(8,128)(2,1)}, u32[]{:S(2)}, u32[]{:S(2)}) collective-permute-start(bf16[256,2176]{1,0:T(8,128)(2,1)S(1)} %collective-permute-done.1.refs_1_), channel_id=1, source_target_pairs={{1,0},{2,3},{3,2},{4,5},{5,4},{6,7},{9,8},{10,11},{11,10},{12,13},... | collective-permute-start | bytes 3342344 | tf_op jit(solution)/shard_map/ppermute | solution.py:282
  83.9 2.3 %collective-permute-start.5 = (bf16[256,2176]{1,0:T(8,128)(2,1)S(1)}, bf16[256,2176]{1,0:T(8,128)(2,1)}, u32[]{:S(2)}, u32[]{:S(2)}) collective-permute-start(bf16[256,2176]{1,0:T(8,128)(2,1)S(1)} %collective-permute-done.2.refs_2_), channel_id=1, source_target_pairs={{1,0},{3,2},{4,5},{6,7},{9,8},{11,10},{12,13},{14,15},{17,16},{19,... | collective-permute-start | bytes 3342344 | tf_op jit(solution)/shard_map/ppermute | solution.py:282
  86.2 11.6 %collective-permute-done.3.refs_3_ = bf16[256,2176]{1,0:T(8,128)(2,1)} collective-permute-done((bf16[256,2176]{1,0:T(8,128)(2,1)S(1)}, bf16[256,2176]{1,0:T(8,128)(2,1)}, u32[]{:S(2)}, u32[]{:S(2)}) %collective-permute-start.3) | collective-permute-done | bytes 1114144 | tf_op jit(solution)/shard_map/ppermute | solution.py:282
  97.8 2.3 %collective-permute-start.6 = (bf16[256,2176]{1,0:T(8,128)(2,1)}, bf16[256,2176]{1,0:T(8,128)(2,1)}, u32[]{:S(2)}, u32[]{:S(2)}) collective-permute-start(bf16[256,2176]{1,0:T(8,128)(2,1)} %collective-permute-done.3.refs_3_), channel_id=1, source_target_pairs={{1,0},{6,7},{9,8},{14,15},{17,16},{22,23},{25,24},{30,31}} | collective-permute-start | bytes 3342344 | tf_op jit(solution)/shard_map/ppermute | solution.py:282
  100.1 0.7 pad_add_fusion.place
  100.7 1.0 collective-permute-done.6.refs_6_
  101.8 12.6 %up.1 = (bf16[4,320,256]{2,1,0:T(8,128)(2,1)}, bf16[1024,128]{1,0:T(8,128)(2,1)}, bf16[4,320,384]{2,1,0:T(8,128)(2,1)}, bf16[4,320,384]{2,1,0:T(8,128)(2,1)}, bf16[4,320,384]{2,1,0:T(8,128)(2,1)}) custom-call(s32[4]{0:T(128)} %pad_add_fusion.place, bf16[256,2176]{1,0:T(8,128)(2,1)} %copy-done, bf16[256,2176]{1,0:T(8,128)(2,1)} %copy-done.1, ...), custom_call_target="tpu_custom_call" | custom-call | flops 3355443200 | bytes 10747904 | tf_op jit(solution)/shard_map/up/pallas_call | solution.py:331
  114.4 10.5 %mid.1 = (f32[4,320,384]{2,1,0:T(8,128)}, bf16[2,4,128,384]{3,2,1,0:T(8,128)(2,1)}, bf16[2,4,128,384]{3,2,1,0:T(8,128)(2,1)}, bf16[2,4,128,384]{3,2,1,0:T(8,128)(2,1)}, bf16[2,4,128,384]{3,2,1,0:T(8,128)(2,1)}) custom-call(s32[4]{0:T(128)} %pad_add_fusion.place, bf16[4,320,256]{2,1,0:T(8,128)(2,1)} %get-tuple-element.23.pick, ...), custom_call_target="tpu_custom_call" | custom-call | flops 2684354560 | bytes 8388608 | tf_op jit(solution)/shard_map/mid/pallas_call | solution.py:387
  125.0 16.8 %tail.1 = (bf16[1024,2176]{1,0:T(8,128)(2,1)}, bf16[4,320,1024]{2,1,0:T(8,128)(2,1)}) custom-call(s32[4]{0:T(128)} %pad_add_fusion.place, bf16[4,320,256]{2,1,0:T(8,128)(2,1)} %get-tuple-element.23.pick, bf16[1024,1024]{1,0:T(8,128)(2,1)} %all-gather.3.cloned.1.call-done.rows, bf16[4,4,2,256,384]{4,3,2,1,0:T(8,128)(2,1)} %bitcast.16, ...), custom_call_target="tpu_custom_call" | custom-call | flops 16106127360 | bytes 25165824 | tf_op jit(solution)/shard_map/tail/pallas_call | solution.py:409
  141.9 1.1 copy-done.8
  143.0 1.5 collective-permute-start.7
  144.5 1.5 collective-permute-start.9
  146.0 16.8 %collective-permute-done.7 = bf16[2,4,128,384]{3,2,1,0:T(8,128)(2,1)S(1)} collective-permute-done((bf16[2,4,128,384]{3,2,1,0:T(8,128)(2,1)S(1)}, bf16[2,4,128,384]{3,2,1,0:T(8,128)(2,1)S(1)}, u32[]{:S(2)}, u32[]{:S(2)}) %collective-permute-start.7) | collective-permute-done | bytes 786464 | tf_op jit(solution)/shard_map/ppermute | solution.py:377
  162.8 0.2 add_convert_fusion.3
  163.0 0.8 fusion
  163.8 0.2 collective-permute-done.9
  164.0 0.2 add_convert_fusion.2
  164.2 0.8 fusion.1
  165.0 6.0 %down.1 = (bf16[2,4,128,384]{3,2,1,0:T(8,128)(2,1)}, bf16[2,4,128,384]{3,2,1,0:T(8,128)(2,1)}, bf16[2,4,128,384]{3,2,1,0:T(8,128)(2,1)}, bf16[2,4,128,384]{3,2,1,0:T(8,128)(2,1)}) custom-call(s32[4]{0:T(128)} %pad_add_fusion.place, bf16[4,320,1024]{2,1,0:T(8,128)(2,1)} %get-tuple-element.36.rows, bf16[4,320,384]{2,1,0:T(8,128)(2,1)} %get-tuple-element.29.scaled, ...), custom_call_target="tpu_custom_call" | custom-call | flops 32212254720 | bytes 50331648 | tf_op jit(solution)/shard_map/down/pallas_call | solution.py:439
  171.0 1.5 collective-permute-start.11
  172.5 1.5 collective-permute-start.8
  174.0 0.5 collective-permute-start.13
  174.6 0.6 collective-permute-start.10
  175.1 9.4 %collective-permute-done.8 = bf16[1,4,128,384]{3,2,1,0:T(8,128)(2,1)S(1)} collective-permute-done((bf16[1,4,128,384]{3,2,1,0:T(8,128)(2,1)S(1)}, bf16[1,4,128,384]{3,2,1,0:T(8,128)(2,1)S(1)}, u32[]{:S(2)}, u32[]{:S(2)}) %collective-permute-start.8) | collective-permute-done | bytes 393248 | tf_op jit(solution)/shard_map/ppermute | solution.py:377
  184.6 0.1 add_bitcast_fusion.3
  184.7 7.1 %collective-permute-done.11 = bf16[2,4,128,384]{3,2,1,0:T(8,128)(2,1)S(1)} collective-permute-done((bf16[2,4,128,384]{3,2,1,0:T(8,128)(2,1)}, bf16[2,4,128,384]{3,2,1,0:T(8,128)(2,1)S(1)}, u32[]{:S(2)}, u32[]{:S(2)}) %collective-permute-start.11) | collective-permute-done | bytes 786464 | tf_op jit(solution)/shard_map/ppermute | solution.py:377
  191.8 0.2 add_convert_fusion.1
  192.0 1.6 collective-permute-start.12
  193.6 7.8 %collective-permute-done.13 = bf16[2,4,128,384]{3,2,1,0:T(8,128)(2,1)S(1)} collective-permute-done((bf16[2,4,128,384]{3,2,1,0:T(8,128)(2,1)}, bf16[2,4,128,384]{3,2,1,0:T(8,128)(2,1)S(1)}, u32[]{:S(2)}, u32[]{:S(2)}) %collective-permute-start.13) | collective-permute-done | bytes 786464 | tf_op jit(solution)/shard_map/ppermute | solution.py:377
  201.4 0.2 add_convert_fusion
  201.7 0.6 collective-permute-start.14
  202.3 0.1 add_bitcast_fusion.2
  202.4 5.8 %collective-permute-done.12 = bf16[1,4,128,384]{3,2,1,0:T(8,128)(2,1)S(1)} collective-permute-done((bf16[1,4,128,384]{3,2,1,0:T(8,128)(2,1)S(1)}, bf16[1,4,128,384]{3,2,1,0:T(8,128)(2,1)S(1)}, u32[]{:S(2)}, u32[]{:S(2)}) %collective-permute-start.12) | collective-permute-done | bytes 393248 | tf_op jit(solution)/shard_map/ppermute | solution.py:377
  208.2 0.1 add_bitcast_fusion.1
  208.3 1.3 collective-permute-done.14
  209.6 0.1 add_bitcast_fusion
  209.7 1.9 pad_maximum_fusion
  211.6 0.8 slice.41
  212.3 0.7 copy.9
  213.0 1.9 slice.40
  (33 shorter events, 0.5 us)
Async XLA Ops:
  7.2 107.3 %all-gather.5.cloned.1.call-start = ((), (), s32[]{:S(2)}) async-start(), calls=%async_computation.2 | async-start | bytes 2359296 | tf_op jit(solution)/shard_map/all_gather | solution.py:275
  9.4 115.6 %all-gather.3.cloned.1.call-start = ((), (), s32[]{:S(2)}) async-start(), calls=%async_computation.1 | async-start | bytes 2359296 | tf_op jit(solution)/shard_map/all_gather | solution.py:275
  9.5 2.2 %collective-permute-start = (bf16[128,2176]{1,0:T(8,128)(2,1)}, bf16[128,2176]{1,0:T(8,128)(2,1)S(1)}, u32[]{:S(2)}, u32[]{:S(2)}) collective-permute-start(bf16[128,2176]{1,0:T(8,128)(2,1)} %get-tuple-element.22), channel_id=1, source_target_pairs={{0,1},{1,0},{2,3},{3,2},{4,5},{5,4},{6,7},{7,6},{8,9},{9,8},{10,11... | collective-permute-start | bytes 1671176 | tf_op jit(solution)/shard_map/ppermute | solution.py:282
  11.8 90.0 %copy-start = (bf16[256,2176]{1,0:T(8,128)(2,1)}, bf16[256,2176]{1,0:T(8,128)(2,1)S(1)}, u32[]{:S(2)}) copy-start(bf16[256,2176]{1,0:T(8,128)(2,1)S(1)} %constant_dynamic-update-slice_fusion.refs_0_) | copy-start | bytes 3342340
  11.8 34.2 %collective-permute-start.1 = (bf16[256,2176]{1,0:T(8,128)(2,1)S(1)}, bf16[256,2176]{1,0:T(8,128)(2,1)S(1)}, u32[]{:S(2)}, u32[]{:S(2)}) collective-permute-start(bf16[256,2176]{1,0:T(8,128)(2,1)S(1)} %constant_dynamic-update-slice_fusion.refs_0_), channel_id=1, source_target_pairs={{0,2},{2,4},{3,1},{4,6},{5,3},{7,5},{8,10},{10,12},{11,9},{12,14},... | collective-permute-start | bytes 3342344 | tf_op jit(solution)/shard_map/ppermute | solution.py:282
  46.0 55.7 %copy-start.1 = (bf16[256,2176]{1,0:T(8,128)(2,1)}, bf16[256,2176]{1,0:T(8,128)(2,1)S(1)}, u32[]{:S(2)}) copy-start(bf16[256,2176]{1,0:T(8,128)(2,1)S(1)} %collective-permute-done.1.refs_1_) | copy-start | bytes 3342340
  46.0 34.2 %collective-permute-start.2 = (bf16[256,2176]{1,0:T(8,128)(2,1)S(1)}, bf16[256,2176]{1,0:T(8,128)(2,1)S(1)}, u32[]{:S(2)}, u32[]{:S(2)}) collective-permute-start(bf16[256,2176]{1,0:T(8,128)(2,1)S(1)} %collective-permute-done.1.refs_1_), channel_id=1, source_target_pairs={{2,4},{3,1},{4,6},{5,3},{10,12},{11,9},{12,14},{13,11},{18,20},{19... | collective-permute-start | bytes 3342344 | tf_op jit(solution)/shard_map/ppermute | solution.py:282
  47.4 164.2 %reduce-scatter.2.cloned.1.call-start = ((), (), s32[]{:S(2)}) async-start(), calls=%async_computation.3 | async-start | bytes 5013504 | tf_op jit(solution)/shard_map/reduce_scatter | solution.py:437
  80.3 21.5 %copy-start.2 = (bf16[256,2176]{1,0:T(8,128)(2,1)}, bf16[256,2176]{1,0:T(8,128)(2,1)S(1)}, u32[]{:S(2)}) copy-start(bf16[256,2176]{1,0:T(8,128)(2,1)S(1)} %collective-permute-done.2.refs_2_) | copy-start | bytes 3342340
  80.3 17.5 %collective-permute-start.3 = (bf16[256,2176]{1,0:T(8,128)(2,1)S(1)}, bf16[256,2176]{1,0:T(8,128)(2,1)}, u32[]{:S(2)}, u32[]{:S(2)}) collective-permute-start(bf16[256,2176]{1,0:T(8,128)(2,1)S(1)} %collective-permute-done.2.refs_2_), channel_id=1, source_target_pairs={{3,1},{4,6},{11,9},{12,14},{19,17},{20,22},{27,25},{28,30}} | collective-permute-start | bytes 3342344 | tf_op jit(solution)/shard_map/ppermute | solution.py:282
  81.6 19.2 %collective-permute-start.4 = (bf16[256,2176]{1,0:T(8,128)(2,1)S(1)}, bf16[256,2176]{1,0:T(8,128)(2,1)}, u32[]{:S(2)}, u32[]{:S(2)}) collective-permute-start(bf16[256,2176]{1,0:T(8,128)(2,1)S(1)} %collective-permute-done.1.refs_1_), channel_id=1, source_target_pairs={{1,0},{2,3},{3,2},{4,5},{5,4},{6,7},{9,8},{10,11},{11,10},{12,13},... | collective-permute-start | bytes 3342344 | tf_op jit(solution)/shard_map/ppermute | solution.py:282
  83.9 16.8 %collective-permute-start.5 = (bf16[256,2176]{1,0:T(8,128)(2,1)S(1)}, bf16[256,2176]{1,0:T(8,128)(2,1)}, u32[]{:S(2)}, u32[]{:S(2)}) collective-permute-start(bf16[256,2176]{1,0:T(8,128)(2,1)S(1)} %collective-permute-done.2.refs_2_), channel_id=1, source_target_pairs={{1,0},{3,2},{4,5},{6,7},{9,8},{11,10},{12,13},{14,15},{17,16},{19,... | collective-permute-start | bytes 3342344 | tf_op jit(solution)/shard_map/ppermute | solution.py:282
  97.8 4.0 %collective-permute-start.6 = (bf16[256,2176]{1,0:T(8,128)(2,1)}, bf16[256,2176]{1,0:T(8,128)(2,1)}, u32[]{:S(2)}, u32[]{:S(2)}) collective-permute-start(bf16[256,2176]{1,0:T(8,128)(2,1)} %collective-permute-done.3.refs_3_), channel_id=1, source_target_pairs={{1,0},{6,7},{9,8},{14,15},{17,16},{22,23},{25,24},{30,31}} | collective-permute-start | bytes 3342344 | tf_op jit(solution)/shard_map/ppermute | solution.py:282
  141.8 1.1 copy-start.8
  141.8 2.6 %copy-start.7 = (bf16[2,4,128,384]{3,2,1,0:T(8,128)(2,1)S(1)}, bf16[2,4,128,384]{3,2,1,0:T(8,128)(2,1)}, u32[]{:S(2)}) copy-start(bf16[2,4,128,384]{3,2,1,0:T(8,128)(2,1)} %get-tuple-element.35) | copy-start | bytes 2359300
  141.8 21.0 %copy-start.5 = (bf16[2,4,128,384]{3,2,1,0:T(8,128)(2,1)S(1)}, bf16[2,4,128,384]{3,2,1,0:T(8,128)(2,1)}, u32[]{:S(2)}) copy-start(bf16[2,4,128,384]{3,2,1,0:T(8,128)(2,1)} %get-tuple-element.32) | copy-start | bytes 2359300
  143.0 19.8 %collective-permute-start.7 = (bf16[2,4,128,384]{3,2,1,0:T(8,128)(2,1)S(1)}, bf16[2,4,128,384]{3,2,1,0:T(8,128)(2,1)S(1)}, u32[]{:S(2)}, u32[]{:S(2)}) collective-permute-start(bf16[2,4,128,384]{3,2,1,0:T(8,128)(2,1)S(1)} %copy-done.8), channel_id=1, source_target_pairs={{0,8},{8,0},{16,24},{24,16},{1,9},{9,1},{17,25},{25,17},{2,10},{10... | collective-permute-start | bytes 2359304 | tf_op jit(solution)/shard_map/ppermute | solution.py:377
  144.5 19.5 %collective-permute-start.9 = (bf16[2,4,128,384]{3,2,1,0:T(8,128)(2,1)S(1)}, bf16[2,4,128,384]{3,2,1,0:T(8,128)(2,1)S(1)}, u32[]{:S(2)}, u32[]{:S(2)}) collective-permute-start(bf16[2,4,128,384]{3,2,1,0:T(8,128)(2,1)S(1)} %copy-done.7), channel_id=1, source_target_pairs={{0,16},{8,24},{16,0},{24,8},{1,17},{9,25},{17,1},{25,9},{2,18},{10... | collective-permute-start | bytes 2359304 | tf_op jit(solution)/shard_map/ppermute | solution.py:377
  162.8 1.2 copy-start.4
  171.0 20.8 %copy-start.6 = (bf16[2,4,128,384]{3,2,1,0:T(8,128)(2,1)S(1)}, bf16[2,4,128,384]{3,2,1,0:T(8,128)(2,1)}, u32[]{:S(2)}) copy-start(bf16[2,4,128,384]{3,2,1,0:T(8,128)(2,1)} %get-tuple-element.37) | copy-start | bytes 2359300
  171.0 20.7 %collective-permute-start.11 = (bf16[2,4,128,384]{3,2,1,0:T(8,128)(2,1)}, bf16[2,4,128,384]{3,2,1,0:T(8,128)(2,1)S(1)}, u32[]{:S(2)}, u32[]{:S(2)}) collective-permute-start(bf16[2,4,128,384]{3,2,1,0:T(8,128)(2,1)} %get-tuple-element.38), channel_id=1, source_target_pairs={{0,8},{8,0},{16,24},{24,16},{1,9},{9,1},{17,25},{25,17},{2,10},{10... | collective-permute-start | bytes 2359304 | tf_op jit(solution)/shard_map/ppermute | solution.py:377
  172.5 12.1 %collective-permute-start.8 = (bf16[1,4,128,384]{3,2,1,0:T(8,128)(2,1)S(1)}, bf16[1,4,128,384]{3,2,1,0:T(8,128)(2,1)S(1)}, u32[]{:S(2)}, u32[]{:S(2)}) collective-permute-start(bf16[1,4,128,384]{3,2,1,0:T(8,128)(2,1)S(1)} %get-tuple-element.44), channel_id=1, source_target_pairs={{0,16},{8,24},{16,0},{24,8},{1,17},{9,25},{17,1},{25,9},{2,18},{10... | collective-permute-start | bytes 1179656 | tf_op jit(solution)/shard_map/ppermute | solution.py:377
  174.0 27.4 %collective-permute-start.13 = (bf16[2,4,128,384]{3,2,1,0:T(8,128)(2,1)}, bf16[2,4,128,384]{3,2,1,0:T(8,128)(2,1)S(1)}, u32[]{:S(2)}, u32[]{:S(2)}) collective-permute-start(bf16[2,4,128,384]{3,2,1,0:T(8,128)(2,1)} %get-tuple-element.40), channel_id=1, source_target_pairs={{0,16},{8,24},{16,0},{24,8},{1,17},{9,25},{17,1},{25,9},{2,18},{10... | collective-permute-start | bytes 2359304 | tf_op jit(solution)/shard_map/ppermute | solution.py:377
  174.6 27.8 %collective-permute-start.10 = (bf16[1,4,128,384]{3,2,1,0:T(8,128)(2,1)S(1)}, bf16[1,4,128,384]{3,2,1,0:T(8,128)(2,1)S(1)}, u32[]{:S(2)}, u32[]{:S(2)}) collective-permute-start(bf16[1,4,128,384]{3,2,1,0:T(8,128)(2,1)S(1)} %get-tuple-element.46), channel_id=1, source_target_pairs={{0,8},{8,0},{16,24},{24,16},{1,9},{9,1},{17,25},{25,17},{2,10},{10... | collective-permute-start | bytes 1179656 | tf_op jit(solution)/shard_map/ppermute | solution.py:377
  191.8 9.7 %copy-start.3 = (bf16[2,4,128,384]{3,2,1,0:T(8,128)(2,1)S(1)}, bf16[2,4,128,384]{3,2,1,0:T(8,128)(2,1)}, u32[]{:S(2)}) copy-start(bf16[2,4,128,384]{3,2,1,0:T(8,128)(2,1)} %get-tuple-element.39) | copy-start | bytes 2359300
  192.0 16.2 %collective-permute-start.12 = (bf16[1,4,128,384]{3,2,1,0:T(8,128)(2,1)S(1)}, bf16[1,4,128,384]{3,2,1,0:T(8,128)(2,1)S(1)}, u32[]{:S(2)}, u32[]{:S(2)}) collective-permute-start(bf16[1,4,128,384]{3,2,1,0:T(8,128)(2,1)S(1)} %slice.47), channel_id=1, source_target_pairs={{0,16},{8,24},{16,0},{24,8},{1,17},{9,25},{17,1},{25,9},{2,18},{10... | collective-permute-start | bytes 1179656 | tf_op jit(solution)/shard_map/ppermute | solution.py:377
  201.7 7.9 %collective-permute-start.14 = (bf16[1,4,128,384]{3,2,1,0:T(8,128)(2,1)S(1)}, bf16[1,4,128,384]{3,2,1,0:T(8,128)(2,1)S(1)}, u32[]{:S(2)}, u32[]{:S(2)}) collective-permute-start(bf16[1,4,128,384]{3,2,1,0:T(8,128)(2,1)S(1)} %slice.49), channel_id=1, source_target_pairs={{0,8},{8,0},{16,24},{24,16},{1,9},{9,1},{17,25},{25,17},{2,10},{10... | collective-permute-start | bytes 1179656 | tf_op jit(solution)/shard_map/ppermute | solution.py:377
Sparse Core Ops, SparseCore 0:
  10.2 33.0 all-gather.4
  47.5 34.1 all-gather.2
  142.0 50.9 reduce-scatter.1

commit v6 on v5

--- a/solution.py
+++ b/solution.py
@@ -62,27 +62,13 @@
                     start(ref, slot, 0 if is_left else 1)
 
 
-def up_kernel(groups, width, top, cap, place, *refs):
-    own, refs = refs[0], refs[1:]
-    mine, other = refs[: groups - 1], refs[groups - 1 : 2 * groups - 2]
-    w_up, pick, meta, hid, scaled, slope_g, held, gates, all_rows, sem = refs[2 * groups - 2 :]
+def up_kernel(groups, width, top, cap, after, place, rows, w_up, *refs):
+    pick, meta, hid, scaled, slope_g, held, gates = refs[after:]
     experts = held.shape[0]
     i = pl.program_id(0)
 
-    @pl.when(i == 0)
-    def _():
-        start_blocks(place, groups, own, mine, other, all_rows, sem)
-
     @pl.when(i < groups)
     def _():
-        half = own.shape[0] // 2
-        for part in range(2):
-            pltpu.make_async_copy(
-                own.at[pl.ds(part * half, half), :], all_rows.at[i, pl.ds(part * half, half), :], sem.at[i, part]
-            ).wait()
-        rows = all_rows.at[i]
-        group = lax.rem(place[3] - i + groups, groups)
-        first = pl.multiple_of(group * cap, PACK)
         info = rows[:, pl.ds(width, LANES)]
         meta[...] = info
         across = info.astype(f32).T
@@ -98,15 +84,15 @@
         spot = lax.broadcasted_iota(jnp.int32, (cap, count), 0).astype(f32)
         for b in range(experts):
             rank = jnp.where(member[b] > 0.0, prior[b : b + 1], -1.0)
-            one = jnp.where(spot == rank, 1.0, 0.0)
+            hot = spot == rank
             gate = jnp.sum(jnp.where(chosen[b], weights, 0.0), axis=0, keepdims=True)
+            one = jnp.where(hot, 1.0, 0.0)
             pick[0, pl.ds(b * cap, cap), :] = one.astype(bf16)
-            gates[b, pl.ds(first, cap), :] = jnp.broadcast_to(
-                jnp.sum(one * gate, axis=1, keepdims=True), (cap, LANES)
-            )
+            at = pl.ds(pl.multiple_of(i * cap, PACK), cap)
+            gates[b, at, :] = jnp.broadcast_to(jnp.sum(one * gate, axis=1, keepdims=True), (cap, LANES))
         got = dot(pick[0], rows[:, pl.ds(0, width)]).astype(bf16)
         for b in range(experts):
-            held[b, pl.ds(first, cap), :] = got[b * cap : (b + 1) * cap]
+            held[b, pl.ds(pl.multiple_of(i * cap, PACK), cap), :] = got[b * cap : (b + 1) * cap]
 
     @pl.when(i >= groups)
     def _():
@@ -120,11 +106,22 @@
         slope_g[0] = (gate * (sig + act * (1.0 - sig))).astype(bf16)
 
 
-def gather_rows(i, cap, pick, rows, held):
-    experts = held.shape[0]
-    got = dot(pick[0], rows[...]).astype(bf16)
+def gather_rows(place, i, cap, pick, blocks, moved, held, sem):
+    experts, groups = held.shape[0], moved.shape[0]
+    own, mine, other = blocks[0], blocks[1:groups], blocks[groups:]
+
+    @pl.when(i == 0)
+    def _():
+        start_blocks(place, groups, own, mine, other, moved, sem)
+
+    half = own.shape[0] // 2
+    for part in range(2):
+        at = pl.ds(part * half, half)
+        pltpu.make_async_copy(own.at[at, :], moved.at[i, at, :], sem.at[i, part]).wait()
+    first = pl.multiple_of(lax.rem(place[3] - i + groups, groups) * cap, PACK)
+    got = dot(pick[0], moved[i]).astype(bf16)
     for b in range(experts):
-        held[b, pl.ds(pl.multiple_of(i * cap, PACK), cap), :] = got[b * cap : (b + 1) * cap]
+        held[b, pl.ds(first, cap), :] = got[b * cap : (b + 1) * cap]
 
 
 def down_copies(orders, b, sent, outs, sem):
@@ -153,14 +150,16 @@
         copy.start()
 
 
-def mid_kernel(groups, cap, orders, place, pick, rows, w_down, scaled, back, *refs):
-    outs, (held, sent, sem) = refs[:-3], refs[-3:]
+def mid_kernel(groups, cap, orders, after, place, pick, *refs):
+    blocks, refs = refs[: 2 * groups - 1], refs[2 * groups - 1 :]
+    w_down, scaled, refs = refs[0], refs[1], refs[2 + after :]
+    back, outs, (held, moved, block_sem, sent, sem) = refs[0], refs[1:-5], refs[-5:]
     experts = held.shape[0]
     i = pl.program_id(0)
 
     @pl.when(i < groups)
     def _():
-        gather_rows(i, cap, pick, rows, held)
+        gather_rows(place, i, cap, pick, blocks, moved, held, block_sem)
 
     @pl.when(i >= groups)
     def _():
@@ -188,15 +187,17 @@
                 copy.wait()
 
 
-def tail_kernel(groups, cap, width, top, has_before, place, pick, rows, w_down, w_up, hid, slope_g, meta, *refs):
-    before = refs[0] if has_before else None
-    out, kept, held, grads, sem = refs[has_before:]
+def tail_kernel(groups, cap, width, top, has_before, place, pick, *refs):
+    blocks, refs = refs[: 2 * groups - 1], refs[2 * groups - 1 :]
+    w_down, w_up, hid, slope_g, meta = refs[:5]
+    before = refs[5] if has_before else None
+    out, kept, held, moved, block_sem, grads, sem = refs[5 + has_before :]
     experts = held.shape[0]
     i = pl.program_id(0)
 
     @pl.when(i < groups)
     def _():
-        gather_rows(i, cap, pick, rows, held)
+        gather_rows(place, i, cap, pick, blocks, moved, held, block_sem)
 
     @pl.when((i >= groups) & (i < groups + experts))
     def _():
@@ -272,7 +273,7 @@
         cost_estimate=cost(0, 8 * tok_rows * width),
         name="pack",
     )(tokens, cotangent, expert_ids.T, gate_weights.T)
-    dy_all = [lax.all_gather(part, "ep", axis=0, tiled=True) for part in dy_own]
+    x_all = lax.all_gather(x_own, "ep", axis=0, tiled=True)
 
     def reach(p, step):
         q = p + GROUP * step if p % GROUP == 0 else p - GROUP * step
@@ -281,15 +282,19 @@
     def hop(value, pairs):
         return lax.ppermute(value, "ep", pairs)
 
-    x_own = jnp.concatenate([x_own, hop(x_own, [(p, p ^ 1) for p in range(ep_count)])], axis=0)
-    x_mine, x_other, moving = [], [], x_own
+    dy_own = [jnp.concatenate([part, hop(part, [(p, p ^ 1) for p in range(ep_count)])], axis=0) for part in dy_own]
+    moving, dy_mine, dy_other = dy_own, [], []
     for step in range(1, groups):
-        moving = hop(
-            moving,
-            [(p, reach(p, 1)) for p in range(ep_count) if None not in (reach(p, 1), reach(p, 1 - step))],
-        )
-        x_mine.append(moving)
-        x_other.append(hop(moving, [(p, p ^ 1) for p in range(ep_count) if reach(p, -step) is not None]))
+        line = [(p, reach(p, 1)) for p in range(ep_count) if None not in (reach(p, 1), reach(p, 1 - step))]
+        swap = [(p, p ^ 1) for p in range(ep_count) if reach(p, -step) is not None]
+        moving = [hop(part, line) for part in moving]
+        dy_mine.append(moving)
+        dy_other.append([hop(part, swap) for part in moving])
+    dy_blocks = [
+        [dy_own[s]] + [part[s] for part in dy_mine] + [part[s] for part in dy_other] for s in range(slices)
+    ]
+    up_after = dy_mine[-2][-1:] if groups > 2 else []
+    mid_after = dy_mine[-1][-1:]
 
     def at_group(i):
         return jnp.minimum(i, groups - 1)
@@ -329,28 +334,16 @@
     main_flops = 2 * experts * routes * width * hidden
     row_bytes = 2 * experts * hidden * width
     pick, meta, hid, scaled, slope_g = call(
-        functools.partial(up_kernel, groups, width, top, cap),
+        functools.partial(up_kernel, groups, width, top, cap, len(up_after)),
         "up",
         groups + experts,
         pick_flops + main_flops,
         2 * total * full + row_bytes,
-        prefetch=1,
-        in_specs=[ANY] * (2 * groups - 1) + [by_expert(width, hidden)],
-        out_specs=[
-            pl.BlockSpec((1, experts * cap, members), lambda i, place: (at_slot(i, place), 0, 0)),
-            pl.BlockSpec((members, LANES), lambda i, place: (at_slot(i, place), 0)),
-            act_spec,
-            act_spec,
-            act_spec,
-        ],
+        in_specs=[SMEM, by_group(full), by_expert(width, hidden)] + [ANY] * len(up_after),
+        out_specs=[pick_spec, by_group(LANES), act_spec, act_spec, act_spec],
         out_shape=[shape(groups, experts * cap, members), shape(total, LANES), act, act, act],
-        scratch_shapes=[
-            pltpu.VMEM((experts, routes, width), bf16),
-            pltpu.VMEM((experts, routes, LANES), f32),
-            pltpu.VMEM((groups, members, full), bf16),
-            pltpu.SemaphoreType.DMA((groups, 2)),
-        ],
-    )(place, x_own, *x_mine, *x_other, w_up)
+        scratch_shapes=[pltpu.VMEM((experts, routes, width), bf16), pltpu.VMEM((experts, routes, LANES), f32)],
+    )(place, x_all, w_up, *up_after)
 
     orders = []
     for g in range(turns):
@@ -368,7 +361,7 @@
     w_cut = w_down.reshape(experts, dp_count, slices, piece, hidden)
 
     def cut_spec(s):
-        return pl.BlockSpec((1, dp_count, 1, piece, hidden), lambda i: (at_expert(i), 0, s, 0, 0))
+        return pl.BlockSpec((1, dp_count, 1, piece, hidden), lambda i, *_: (at_expert(i), 0, s, 0, 0))
 
     def exchange(state, t):
         new = []
@@ -382,19 +375,22 @@
             new.append((both[:half], both[half:]) if half else both[0])
         return new
 
+    slot_spec = pl.BlockSpec((1, experts * cap, members), lambda i, place: (at_slot(i, place), 0, 0))
+    block_scratch = [pltpu.VMEM((groups, members, cols), bf16), pltpu.SemaphoreType.DMA((groups, 2))]
     states, before = [], None
     for s in range(slices - 1):
         before, *outs = call(
-            functools.partial(mid_kernel, groups, cap, orders),
+            functools.partial(mid_kernel, groups, cap, orders, len(mid_after)),
             "mid",
             groups + experts,
             (pick_flops + 2 * main_flops) // slices,
             2 * total * cols + 2 * row_bytes // slices,
-            in_specs=[SMEM, pick_spec, by_group(cols), cut_spec(s), act_spec],
+            prefetch=1,
+            in_specs=[slot_spec] + [ANY] * (2 * groups - 1) + [cut_spec(s), act_spec] + [ANY] * len(mid_after),
             out_specs=[act_spec] + [ANY] * len(down_outs),
             out_shape=[shape(experts, routes, hidden, dtype=f32)] + down_outs,
-            scratch_shapes=[pltpu.VMEM((experts, routes, cols), bf16)] + down_scratch,
-        )(place, pick, dy_all[s], w_cut, scaled)
+            scratch_shapes=[pltpu.VMEM((experts, routes, cols), bf16)] + block_scratch + down_scratch,
+        )(place, pick, *dy_blocks[s], w_cut, scaled, *mid_after)
         states.append([(outs[2 * g], outs[2 * g + 1]) for g in range(turns)])
 
     done, after = 0, []
@@ -412,28 +408,31 @@
         2 * groups + experts,
         8 * main_flops,
         4 * row_bytes,
+        prefetch=1,
         in_specs=[
-            SMEM,
             pl.BlockSpec(
                 (1, experts * cap, members),
-                lambda i: (jnp.where(i < groups, i, at_end(i)), 0, 0),
+                lambda i, place: (jnp.where(i < groups, at_slot(i, place), at_end(i)), 0, 0),
             ),
-            by_group(cols),
+        ]
+        + [ANY] * (2 * groups - 1)
+        + [
             cut_spec(last),
             by_expert(width, hidden),
             act_spec,
             act_spec,
-            pl.BlockSpec((members, LANES), lambda i: (at_end(i), 0)),
+            pl.BlockSpec((members, LANES), lambda i, *_: (at_end(i), 0)),
         ]
         + ([act_spec] if before is not None else []),
-        out_specs=[pl.BlockSpec((members, full), lambda i: (at_end(i), 0)), ANY],
+        out_specs=[pl.BlockSpec((members, full), lambda i, *_: (at_end(i), 0)), ANY],
         out_shape=[shape(total, full), shape(experts, routes, cols)],
         scratch_shapes=[
             pltpu.VMEM((experts, routes, cols), bf16),
+            *block_scratch,
             pltpu.VMEM((groups, experts * cap, full), bf16),
             pltpu.SemaphoreType.DMA((experts,)),
         ],
-    )(place, pick, dy_all[last], w_cut, w_up, hid, slope_g, meta, *([] if before is None else [before]))
+    )(place, pick, *dy_blocks[last], w_cut, w_up, hid, slope_g, meta, *([] if before is None else [before]))
     summed = lax.psum_scatter(token_part, "ep", scatter_dimension=0, tiled=True)
 
     outs = call(

time: 222 us -> 210 us (0.946)
  the two profiles are of different devices: /device:TPU:24 before, /device:TPU:8 now
where the time goes in v6:
time: 210 us; the launch traced here: 209 us
  waiting for transfers between devices  90.6 us (43%)
  Pallas kernels  49.6 us (24%)
  starting transfers between devices  41.7 us (20%)
  between operations  14.4 us (7%)
  local copies, waits for them, and re-layouts  8.12 us (4%)
  other arithmetic  4.75 us (2%)
    ppermute x8, waiting for transfers between devices, exchange(): got = lax.ppermute(send, 'dp', [(i, i ^ bit) for i in range(dp_count)])  49.2 us
    ppermute x14, waiting for transfers between devices, hop(): return lax.ppermute(value, 'ep', pairs)  41.4 us
    ppermute x14, starting transfers between devices, hop(): return lax.ppermute(value, 'ep', pairs)  31.4 us
    pallas_call x1, Pallas kernels, shards(): call(functools.partial(tail_kernel, groups, cap, width, top, before is no...  18.1 us
    pallas_call x1, Pallas kernels, shards(): call(functools.partial(mid_kernel, groups, cap, orders, len(mid_after)),...  11.8 us
    pallas_call x1, Pallas kernels, shards(): call(functools.partial(up_kernel, groups, width, top, cap, len(up_after))...  11.6 us
    ppermute x8, starting transfers between devices, exchange(): got = lax.ppermute(send, 'dp', [(i, i ^ bit) for i in range(dp_count)])  10.2 us
    pallas_call x1, Pallas kernels, shards(): call(functools.partial(down_kernel, orders, len(after)), 'down', experts,...  5.98 us
  transfers between devices with their start and end apart: 24, of which 12 were waited for; matrix products, arithmetic and copies ran while one was open for 4% of the time, Pallas kernels for 14%

profile of v6, /device:TPU:8, one launch (start us, length us, event | category | flops | bytes accessed | tf_op | source)
XLA Modules:
  0.0 209.3 jit_solution(7968370469410434750)
XLA Ops:
  7.2 2.2 %pack.1 = (bf16[128,2176]{1,0:T(8,128)(2,1)}, bf16[128,1024]{1,0:T(8,128)(2,1)}, bf16[128,1024]{1,0:T(8,128)(2,1)}) custom-call(bf16[128,2048]{1,0:T(8,128)(2,1)} %tokens.1, bf16[128,2048]{1,0:T(8,128)(2,1)} %cotangent.1, s32[8,128]{1,0:T(8,128)} %bitcast.17, bf16[8,128]{1,0:T(8,128)(2,1)} %bitcast.18), custom_call_target="tpu_custom_call" | custom-call | bytes 2097152 | tf_op jit(solution)/shard_map/pack/pallas_call | solution.py:269
  9.6 0.5 collective-permute-start
  10.1 1.0 constant_dynamic-update-slice_fusion.3
  11.3 3.5 %collective-permute-start.8 = (bf16[256,1024]{1,0:T(8,128)(2,1)S(1)}, bf16[256,1024]{1,0:T(8,128)(2,1)S(1)}, u32[]{:S(2)}, u32[]{:S(2)}) collective-permute-start(bf16[256,1024]{1,0:T(8,128)(2,1)S(1)} %constant_dynamic-update-slice_fusion.2.refs_0_), channel_id=1, source_target_pairs={{0,2},{2,4},{3,1},{4,6},{5,3},{7,5},{8,10},{10,12},{11,9},{12,14},... | collective-permute-start | bytes 1572872 | tf_op jit(solution)/shard_map/ppermute | solution.py:283
  14.8 1.0 constant_dynamic-update-slice_fusion.1
  15.8 3.5 %collective-permute-start.1 = (bf16[256,1024]{1,0:T(8,128)(2,1)S(1)}, bf16[256,1024]{1,0:T(8,128)(2,1)S(1)}, u32[]{:S(2)}, u32[]{:S(2)}) collective-permute-start(bf16[256,1024]{1,0:T(8,128)(2,1)S(1)} %constant_dynamic-update-slice_fusion.refs_0_), channel_id=1, source_target_pairs={{0,2},{2,4},{3,1},{4,6},{5,3},{7,5},{8,10},{10,12},{11,9},{12,14},... | collective-permute-start | bytes 1572872 | tf_op jit(solution)/shard_map/ppermute | solution.py:283
  19.3 8.2 %collective-permute-done.8.refs_1_ = bf16[256,1024]{1,0:T(8,128)(2,1)S(1)} collective-permute-done((bf16[256,1024]{1,0:T(8,128)(2,1)S(1)}, bf16[256,1024]{1,0:T(8,128)(2,1)S(1)}, u32[]{:S(2)}, u32[]{:S(2)}) %collective-permute-start.8) | collective-permute-done | bytes 524320 | tf_op jit(solution)/shard_map/ppermute | solution.py:283
  27.5 4.4 %collective-permute-start.9 = (bf16[256,1024]{1,0:T(8,128)(2,1)S(1)}, bf16[256,1024]{1,0:T(8,128)(2,1)S(1)}, u32[]{:S(2)}, u32[]{:S(2)}) collective-permute-start(bf16[256,1024]{1,0:T(8,128)(2,1)S(1)} %collective-permute-done.8.refs_1_), channel_id=1, source_target_pairs={{2,4},{3,1},{4,6},{5,3},{10,12},{11,9},{12,14},{13,11},{18,20},{19... | collective-permute-start | bytes 1572872 | tf_op jit(solution)/shard_map/ppermute | solution.py:283
  31.9 24.1 %collective-permute-done.1.refs_1_ = bf16[256,1024]{1,0:T(8,128)(2,1)S(1)} collective-permute-done((bf16[256,1024]{1,0:T(8,128)(2,1)S(1)}, bf16[256,1024]{1,0:T(8,128)(2,1)S(1)}, u32[]{:S(2)}, u32[]{:S(2)}) %collective-permute-start.1) | collective-permute-done | bytes 524320 | tf_op jit(solution)/shard_map/ppermute | solution.py:283
  56.0 5.5 %collective-permute-start.2 = (bf16[256,1024]{1,0:T(8,128)(2,1)S(1)}, bf16[256,1024]{1,0:T(8,128)(2,1)}, u32[]{:S(2)}, u32[]{:S(2)}) collective-permute-start(bf16[256,1024]{1,0:T(8,128)(2,1)S(1)} %collective-permute-done.1.refs_1_), channel_id=1, source_target_pairs={{2,4},{3,1},{4,6},{5,3},{10,12},{11,9},{12,14},{13,11},{18,20},{19... | collective-permute-start | bytes 1572872 | tf_op jit(solution)/shard_map/ppermute | solution.py:283
  61.5 7.1 %collective-permute-done.9.refs_2_ = bf16[256,1024]{1,0:T(8,128)(2,1)S(1)} collective-permute-done((bf16[256,1024]{1,0:T(8,128)(2,1)S(1)}, bf16[256,1024]{1,0:T(8,128)(2,1)S(1)}, u32[]{:S(2)}, u32[]{:S(2)}) %collective-permute-start.9) | collective-permute-done | bytes 524320 | tf_op jit(solution)/shard_map/ppermute | solution.py:283
  68.6 0.7 collective-permute-start.10
  69.2 3.1 %collective-permute-start.11 = (bf16[256,1024]{1,0:T(8,128)(2,1)S(1)}, bf16[256,1024]{1,0:T(8,128)(2,1)S(1)}, u32[]{:S(2)}, u32[]{:S(2)}) collective-permute-start(bf16[256,1024]{1,0:T(8,128)(2,1)S(1)} %collective-permute-done.8.refs_1_), channel_id=1, source_target_pairs={{1,0},{2,3},{3,2},{4,5},{5,4},{6,7},{9,8},{10,11},{11,10},{12,13},... | collective-permute-start | bytes 1572872 | tf_op jit(solution)/shard_map/ppermute | solution.py:283
  72.4 1.8 collective-permute-done.2.refs_0_.refs_2_
  74.2 0.7 collective-permute-start.3
  74.9 1.3 collective-permute-start.12
  76.2 1.5 collective-permute-start.13
  77.7 0.7 pad_add_fusion.place
  78.3 3.9 %collective-permute-start.4 = (bf16[256,1024]{1,0:T(8,128)(2,1)}, bf16[256,1024]{1,0:T(8,128)(2,1)}, u32[]{:S(2)}, u32[]{:S(2)}) collective-permute-start(bf16[256,1024]{1,0:T(8,128)(2,1)} %copy-done.12), channel_id=1, source_target_pairs={{1,0},{2,3},{3,2},{4,5},{5,4},{6,7},{9,8},{10,11},{11,10},{12,13},... | collective-permute-start | bytes 1572872 | tf_op jit(solution)/shard_map/ppermute | solution.py:283
  82.3 1.3 collective-permute-start.5
  83.6 1.5 collective-permute-start.6
  85.1 11.6 %up.1 = (bf16[4,320,256]{2,1,0:T(8,128)(2,1)}, bf16[1024,128]{1,0:T(8,128)(2,1)}, bf16[4,320,384]{2,1,0:T(8,128)(2,1)}, bf16[4,320,384]{2,1,0:T(8,128)(2,1)}, bf16[4,320,384]{2,1,0:T(8,128)(2,1)}) custom-call(s32[4]{0:T(128)} %pad_add_fusion.place, bf16[1024,2176]{1,0:T(8,128)(2,1)} %all-gather.2.cloned.1.call-done.rows, bf16[4,2048,384]{2,1,0:T(8,128)(2,1)} %refs_8_.1, ...), custom_call_target="tpu_custom_call" | custom-call | flops 3355443200 | bytes 10747904 | tf_op jit(solution)/shard_map/up/pallas_call | solution.py:336
  96.7 11.8 %mid.1 = (f32[4,320,384]{2,1,0:T(8,128)}, bf16[2,4,128,384]{3,2,1,0:T(8,128)(2,1)}, bf16[2,4,128,384]{3,2,1,0:T(8,128)(2,1)}, bf16[2,4,128,384]{3,2,1,0:T(8,128)(2,1)}, bf16[2,4,128,384]{3,2,1,0:T(8,128)(2,1)}) custom-call(s32[4]{0:T(128)} %pad_add_fusion.place, bf16[4,320,256]{2,1,0:T(8,128)(2,1)} %get-tuple-element.24.pick, bf16[256,1024]{1,0:T(8,128)(2,1)} %copy-done, ...), custom_call_target="tpu_custom_call" | custom-call | flops 2684354560 | bytes 8388608 | tf_op jit(solution)/shard_map/mid/pallas_call | solution.py:382
  108.5 18.1 %tail.1 = (bf16[1024,2176]{1,0:T(8,128)(2,1)}, bf16[4,320,1024]{2,1,0:T(8,128)(2,1)}) custom-call(s32[4]{0:T(128)} %pad_add_fusion.place, bf16[4,320,256]{2,1,0:T(8,128)(2,1)} %get-tuple-element.24.pick, bf16[256,1024]{1,0:T(8,128)(2,1)} %copy-done.9, bf16[256,1024]{1,0:T(8,128)(2,1)} %copy-done.12, ...), custom_call_target="tpu_custom_call" | custom-call | flops 16106127360 | bytes 25165824 | tf_op jit(solution)/shard_map/tail/pallas_call | solution.py:405
  126.7 1.1 copy-done.11
  127.8 1.7 collective-permute-start.14
  129.4 1.5 collective-permute-start.16
  131.0 16.3 %collective-permute-done.14 = bf16[2,4,128,384]{3,2,1,0:T(8,128)(2,1)S(1)} collective-permute-done((bf16[2,4,128,384]{3,2,1,0:T(8,128)(2,1)S(1)}, bf16[2,4,128,384]{3,2,1,0:T(8,128)(2,1)S(1)}, u32[]{:S(2)}, u32[]{:S(2)}) %collective-permute-start.14) | collective-permute-done | bytes 786464 | tf_op jit(solution)/shard_map/ppermute | solution.py:370
  147.5 0.8 fusion
  148.3 1.0 collective-permute-done.16
  149.5 0.8 fusion.1
  150.3 6.0 %down.1 = (bf16[2,4,128,384]{3,2,1,0:T(8,128)(2,1)}, bf16[2,4,128,384]{3,2,1,0:T(8,128)(2,1)}, bf16[2,4,128,384]{3,2,1,0:T(8,128)(2,1)}, bf16[2,4,128,384]{3,2,1,0:T(8,128)(2,1)}) custom-call(s32[4]{0:T(128)} %pad_add_fusion.place, bf16[4,320,1024]{2,1,0:T(8,128)(2,1)} %get-tuple-element.36.rows, bf16[4,320,384]{2,1,0:T(8,128)(2,1)} %get-tuple-element.29.refs_8_.scaled, ...), custom_call_target="tpu_custom_call" | custom-call | flops 32212254720 | bytes 50331648 | tf_op jit(solution)/shard_map/down/pallas_call | solution.py:438
  156.3 0.8 collective-permute-start.18
  157.1 1.5 collective-permute-start.15
  158.6 0.5 collective-permute-start.20
  159.1 1.3 collective-permute-start.17
  160.4 8.6 %collective-permute-done.15 = bf16[1,4,128,384]{3,2,1,0:T(8,128)(2,1)S(1)} collective-permute-done((bf16[1,4,128,384]{3,2,1,0:T(8,128)(2,1)S(1)}, bf16[1,4,128,384]{3,2,1,0:T(8,128)(2,1)S(1)}, u32[]{:S(2)}, u32[]{:S(2)}) %collective-permute-start.15) | collective-permute-done | bytes 393248 | tf_op jit(solution)/shard_map/ppermute | solution.py:370
  169.1 7.9 %collective-permute-done.18 = bf16[2,4,128,384]{3,2,1,0:T(8,128)(2,1)S(1)} collective-permute-done((bf16[2,4,128,384]{3,2,1,0:T(8,128)(2,1)}, bf16[2,4,128,384]{3,2,1,0:T(8,128)(2,1)S(1)}, u32[]{:S(2)}, u32[]{:S(2)}) %collective-permute-start.18) | collective-permute-done | bytes 786464 | tf_op jit(solution)/shard_map/ppermute | solution.py:370
  177.0 1.3 add_convert_fusion.1
  178.4 1.6 collective-permute-start.19
  180.0 5.9 %collective-permute-done.20 = bf16[2,4,128,384]{3,2,1,0:T(8,128)(2,1)S(1)} collective-permute-done((bf16[2,4,128,384]{3,2,1,0:T(8,128)(2,1)}, bf16[2,4,128,384]{3,2,1,0:T(8,128)(2,1)S(1)}, u32[]{:S(2)}, u32[]{:S(2)}) %collective-permute-start.20) | collective-permute-done | bytes 786464 | tf_op jit(solution)/shard_map/ppermute | solution.py:370
  186.1 1.3 collective-permute-start.21
  187.6 6.7 %collective-permute-done.19 = bf16[1,4,128,384]{3,2,1,0:T(8,128)(2,1)S(1)} collective-permute-done((bf16[1,4,128,384]{3,2,1,0:T(8,128)(2,1)S(1)}, bf16[1,4,128,384]{3,2,1,0:T(8,128)(2,1)S(1)}, u32[]{:S(2)}, u32[]{:S(2)}) %collective-permute-start.19) | collective-permute-done | bytes 393248 | tf_op jit(solution)/shard_map/ppermute | solution.py:370
  194.3 2.9 %collective-permute-done.21 = bf16[1,4,128,384]{3,2,1,0:T(8,128)(2,1)S(1)} collective-permute-done((bf16[1,4,128,384]{3,2,1,0:T(8,128)(2,1)S(1)}, bf16[1,4,128,384]{3,2,1,0:T(8,128)(2,1)S(1)}, u32[]{:S(2)}, u32[]{:S(2)}) %collective-permute-start.21) | collective-permute-done | bytes 393248 | tf_op jit(solution)/shard_map/ppermute | solution.py:370
  197.3 1.9 pad_maximum_fusion
  199.1 0.8 slice.41
  199.9 0.7 copy.9
  200.5 1.9 slice.40
  (54 shorter events, 1.6 us)
Async XLA Ops:
  7.2 77.9 %all-gather.2.cloned.1.call-start = ((), (), s32[]{:S(2)}) async-start(), calls=%async_computation.1 | async-start | bytes 5013504 | tf_op jit(solution)/shard_map/all_gather | solution.py:276
  9.4 189.7 %reduce-scatter.2.cloned.1.call-start = ((), (), s32[]{:S(2)}) async-start(), calls=%async_computation.2 | async-start | bytes 5013504 | tf_op jit(solution)/shard_map/reduce_scatter | solution.py:436
  9.5 1.8 collective-permute-start.7
  9.6 6.2 %collective-permute-start = (bf16[128,1024]{1,0:T(8,128)(2,1)}, bf16[128,1024]{1,0:T(8,128)(2,1)S(1)}, u32[]{:S(2)}, u32[]{:S(2)}) collective-permute-start(bf16[128,1024]{1,0:T(8,128)(2,1)} %get-tuple-element.23), channel_id=1, source_target_pairs={{0,1},{1,0},{2,3},{3,2},{4,5},{5,4},{6,7},{7,6},{8,9},{9,8},{10,11... | collective-permute-start | bytes 786440 | tf_op jit(solution)/shard_map/ppermute | solution.py:283
  11.3 85.3 %copy-start = (bf16[256,1024]{1,0:T(8,128)(2,1)}, bf16[256,1024]{1,0:T(8,128)(2,1)S(1)}, u32[]{:S(2)}) copy-start(bf16[256,1024]{1,0:T(8,128)(2,1)S(1)} %constant_dynamic-update-slice_fusion.2.refs_0_) | copy-start | bytes 1572868
  11.3 16.2 %collective-permute-start.8 = (bf16[256,1024]{1,0:T(8,128)(2,1)S(1)}, bf16[256,1024]{1,0:T(8,128)(2,1)S(1)}, u32[]{:S(2)}, u32[]{:S(2)}) collective-permute-start(bf16[256,1024]{1,0:T(8,128)(2,1)S(1)} %constant_dynamic-update-slice_fusion.2.refs_0_), channel_id=1, source_target_pairs={{0,2},{2,4},{3,1},{4,6},{5,3},{7,5},{8,10},{10,12},{11,9},{12,14},... | collective-permute-start | bytes 1572872 | tf_op jit(solution)/shard_map/ppermute | solution.py:283
  15.8 60.3 %copy-start.9 = (bf16[256,1024]{1,0:T(8,128)(2,1)}, bf16[256,1024]{1,0:T(8,128)(2,1)S(1)}, u32[]{:S(2)}) copy-start(bf16[256,1024]{1,0:T(8,128)(2,1)S(1)} %constant_dynamic-update-slice_fusion.refs_0_) | copy-start | bytes 1572868
  15.8 40.1 %collective-permute-start.1 = (bf16[256,1024]{1,0:T(8,128)(2,1)S(1)}, bf16[256,1024]{1,0:T(8,128)(2,1)S(1)}, u32[]{:S(2)}, u32[]{:S(2)}) collective-permute-start(bf16[256,1024]{1,0:T(8,128)(2,1)S(1)} %constant_dynamic-update-slice_fusion.refs_0_), channel_id=1, source_target_pairs={{0,2},{2,4},{3,1},{4,6},{5,3},{7,5},{8,10},{10,12},{11,9},{12,14},... | collective-permute-start | bytes 1572872 | tf_op jit(solution)/shard_map/ppermute | solution.py:283
  27.5 69.2 %copy-start.4 = (bf16[256,1024]{1,0:T(8,128)(2,1)}, bf16[256,1024]{1,0:T(8,128)(2,1)S(1)}, u32[]{:S(2)}) copy-start(bf16[256,1024]{1,0:T(8,128)(2,1)S(1)} %collective-permute-done.8.refs_1_) | copy-start | bytes 1572868
  27.5 41.0 %collective-permute-start.9 = (bf16[256,1024]{1,0:T(8,128)(2,1)S(1)}, bf16[256,1024]{1,0:T(8,128)(2,1)S(1)}, u32[]{:S(2)}, u32[]{:S(2)}) collective-permute-start(bf16[256,1024]{1,0:T(8,128)(2,1)S(1)} %collective-permute-done.8.refs_1_), channel_id=1, source_target_pairs={{2,4},{3,1},{4,6},{5,3},{10,12},{11,9},{12,14},{13,11},{18,20},{19... | collective-permute-start | bytes 1572872 | tf_op jit(solution)/shard_map/ppermute | solution.py:283
  56.0 16.4 %copy-start.12 = (bf16[256,1024]{1,0:T(8,128)(2,1)}, bf16[256,1024]{1,0:T(8,128)(2,1)S(1)}, u32[]{:S(2)}) copy-start(bf16[256,1024]{1,0:T(8,128)(2,1)S(1)} %collective-permute-done.1.refs_1_) | copy-start | bytes 1572868
  56.0 18.2 %collective-permute-start.2 = (bf16[256,1024]{1,0:T(8,128)(2,1)S(1)}, bf16[256,1024]{1,0:T(8,128)(2,1)}, u32[]{:S(2)}, u32[]{:S(2)}) collective-permute-start(bf16[256,1024]{1,0:T(8,128)(2,1)S(1)} %collective-permute-done.1.refs_1_), channel_id=1, source_target_pairs={{2,4},{3,1},{4,6},{5,3},{10,12},{11,9},{12,14},{13,11},{18,20},{19... | collective-permute-start | bytes 1572872 | tf_op jit(solution)/shard_map/ppermute | solution.py:283
  68.6 28.1 %copy-start.5 = (bf16[256,1024]{1,0:T(8,128)(2,1)}, bf16[256,1024]{1,0:T(8,128)(2,1)S(1)}, u32[]{:S(2)}) copy-start(bf16[256,1024]{1,0:T(8,128)(2,1)S(1)} %collective-permute-done.9.refs_2_) | copy-start | bytes 1572868
  68.6 7.6 %collective-permute-start.10 = (bf16[256,1024]{1,0:T(8,128)(2,1)S(1)}, bf16[256,1024]{1,0:T(8,128)(2,1)S(1)}, u32[]{:S(2)}, u32[]{:S(2)}) collective-permute-start(bf16[256,1024]{1,0:T(8,128)(2,1)S(1)} %collective-permute-done.9.refs_2_), channel_id=1, source_target_pairs={{3,1},{4,6},{11,9},{12,14},{19,17},{20,22},{27,25},{28,30}} | collective-permute-start | bytes 1572872 | tf_op jit(solution)/shard_map/ppermute | solution.py:283
  69.2 13.0 %collective-permute-start.11 = (bf16[256,1024]{1,0:T(8,128)(2,1)S(1)}, bf16[256,1024]{1,0:T(8,128)(2,1)S(1)}, u32[]{:S(2)}, u32[]{:S(2)}) collective-permute-start(bf16[256,1024]{1,0:T(8,128)(2,1)S(1)} %collective-permute-done.8.refs_1_), channel_id=1, source_target_pairs={{1,0},{2,3},{3,2},{4,5},{5,4},{6,7},{9,8},{10,11},{11,10},{12,13},... | collective-permute-start | bytes 1572872 | tf_op jit(solution)/shard_map/ppermute | solution.py:283
  74.2 9.4 %collective-permute-start.3 = (bf16[256,1024]{1,0:T(8,128)(2,1)}, bf16[256,1024]{1,0:T(8,128)(2,1)S(1)}, u32[]{:S(2)}, u32[]{:S(2)}) collective-permute-start(bf16[256,1024]{1,0:T(8,128)(2,1)} %collective-permute-done.2.refs_0_.refs_2_), channel_id=1, source_target_pairs={{3,1},{4,6},{11,9},{12,14},{19,17},{20,22},{27,25},{28,30}} | collective-permute-start | bytes 1572872 | tf_op jit(solution)/shard_map/ppermute | solution.py:283
  74.9 21.9 %collective-permute-start.12 = (bf16[256,1024]{1,0:T(8,128)(2,1)S(1)}, bf16[256,1024]{1,0:T(8,128)(2,1)}, u32[]{:S(2)}, u32[]{:S(2)}) collective-permute-start(bf16[256,1024]{1,0:T(8,128)(2,1)S(1)} %collective-permute-done.9.refs_2_), channel_id=1, source_target_pairs={{1,0},{3,2},{4,5},{6,7},{9,8},{11,10},{12,13},{14,15},{17,16},{19,... | collective-permute-start | bytes 1572872 | tf_op jit(solution)/shard_map/ppermute | solution.py:283
  76.2 20.5 %copy-start.7 = (bf16[256,1024]{1,0:T(8,128)(2,1)}, bf16[256,1024]{1,0:T(8,128)(2,1)S(1)}, u32[]{:S(2)}) copy-start(bf16[256,1024]{1,0:T(8,128)(2,1)S(1)} %collective-permute-done.10.refs_3_) | copy-start | bytes 1572868
  76.2 20.5 %collective-permute-start.13 = (bf16[256,1024]{1,0:T(8,128)(2,1)S(1)}, bf16[256,1024]{1,0:T(8,128)(2,1)}, u32[]{:S(2)}, u32[]{:S(2)}) collective-permute-start(bf16[256,1024]{1,0:T(8,128)(2,1)S(1)} %collective-permute-done.10.refs_3_), channel_id=1, source_target_pairs={{1,0},{6,7},{9,8},{14,15},{17,16},{22,23},{25,24},{30,31}} | collective-permute-start | bytes 1572872 | tf_op jit(solution)/shard_map/ppermute | solution.py:283
  78.3 30.2 %collective-permute-start.4 = (bf16[256,1024]{1,0:T(8,128)(2,1)}, bf16[256,1024]{1,0:T(8,128)(2,1)}, u32[]{:S(2)}, u32[]{:S(2)}) collective-permute-start(bf16[256,1024]{1,0:T(8,128)(2,1)} %copy-done.12), channel_id=1, source_target_pairs={{1,0},{2,3},{3,2},{4,5},{5,4},{6,7},{9,8},{10,11},{11,10},{12,13},... | collective-permute-start | bytes 1572872 | tf_op jit(solution)/shard_map/ppermute | solution.py:283
  82.3 14.4 %copy-start.8 = (bf16[256,1024]{1,0:T(8,128)(2,1)}, bf16[256,1024]{1,0:T(8,128)(2,1)S(1)}, u32[]{:S(2)}) copy-start(bf16[256,1024]{1,0:T(8,128)(2,1)S(1)} %collective-permute-done.11.refs_4_) | copy-start | bytes 1572868
  82.3 26.2 %collective-permute-start.5 = (bf16[256,1024]{1,0:T(8,128)(2,1)}, bf16[256,1024]{1,0:T(8,128)(2,1)}, u32[]{:S(2)}, u32[]{:S(2)}) collective-permute-start(bf16[256,1024]{1,0:T(8,128)(2,1)} %collective-permute-done.2.refs_0_.refs_2_), channel_id=1, source_target_pairs={{1,0},{3,2},{4,5},{6,7},{9,8},{11,10},{12,13},{14,15},{17,16},{19,... | collective-permute-start | bytes 1572872 | tf_op jit(solution)/shard_map/ppermute | solution.py:283
  83.6 13.1 %copy-start.6 = (bf16[256,1024]{1,0:T(8,128)(2,1)}, bf16[256,1024]{1,0:T(8,128)(2,1)S(1)}, u32[]{:S(2)}) copy-start(bf16[256,1024]{1,0:T(8,128)(2,1)S(1)} %collective-permute-done.3.refs_9_.refs_3_) | copy-start | bytes 1572868
  83.6 24.9 %collective-permute-start.6 = (bf16[256,1024]{1,0:T(8,128)(2,1)S(1)}, bf16[256,1024]{1,0:T(8,128)(2,1)}, u32[]{:S(2)}, u32[]{:S(2)}) collective-permute-start(bf16[256,1024]{1,0:T(8,128)(2,1)S(1)} %collective-permute-done.3.refs_9_.refs_3_), channel_id=1, source_target_pairs={{1,0},{6,7},{9,8},{14,15},{17,16},{22,23},{25,24},{30,31}} | collective-permute-start | bytes 1572872 | tf_op jit(solution)/shard_map/ppermute | solution.py:283
  126.6 1.1 copy-start.11
  126.7 2.8 %copy-start.10 = (bf16[2,4,128,384]{3,2,1,0:T(8,128)(2,1)S(1)}, bf16[2,4,128,384]{3,2,1,0:T(8,128)(2,1)}, u32[]{:S(2)}) copy-start(bf16[2,4,128,384]{3,2,1,0:T(8,128)(2,1)} %get-tuple-element.35) | copy-start | bytes 2359300
  126.7 20.6 %copy-start.2 = (bf16[2,4,128,384]{3,2,1,0:T(8,128)(2,1)S(1)}, bf16[2,4,128,384]{3,2,1,0:T(8,128)(2,1)}, u32[]{:S(2)}) copy-start(bf16[2,4,128,384]{3,2,1,0:T(8,128)(2,1)} %get-tuple-element.32) | copy-start | bytes 2359300
  126.7 22.6 %copy-start.1 = (bf16[2,4,128,384]{3,2,1,0:T(8,128)(2,1)S(1)}, bf16[2,4,128,384]{3,2,1,0:T(8,128)(2,1)}, u32[]{:S(2)}) copy-start(bf16[2,4,128,384]{3,2,1,0:T(8,128)(2,1)} %get-tuple-element.34) | copy-start | bytes 2359300
  127.8 19.5 %collective-permute-start.14 = (bf16[2,4,128,384]{3,2,1,0:T(8,128)(2,1)S(1)}, bf16[2,4,128,384]{3,2,1,0:T(8,128)(2,1)S(1)}, u32[]{:S(2)}, u32[]{:S(2)}) collective-permute-start(bf16[2,4,128,384]{3,2,1,0:T(8,128)(2,1)S(1)} %copy-done.11), channel_id=1, source_target_pairs={{0,8},{8,0},{16,24},{24,16},{1,9},{9,1},{17,25},{25,17},{2,10},{10... | collective-permute-start | bytes 2359304 | tf_op jit(solution)/shard_map/ppermute | solution.py:370
  129.4 19.8 %collective-permute-start.16 = (bf16[2,4,128,384]{3,2,1,0:T(8,128)(2,1)S(1)}, bf16[2,4,128,384]{3,2,1,0:T(8,128)(2,1)S(1)}, u32[]{:S(2)}, u32[]{:S(2)}) collective-permute-start(bf16[2,4,128,384]{3,2,1,0:T(8,128)(2,1)S(1)} %copy-done.10), channel_id=1, source_target_pairs={{0,16},{8,24},{16,0},{24,8},{1,17},{9,25},{17,1},{25,9},{2,18},{10... | collective-permute-start | bytes 2359304 | tf_op jit(solution)/shard_map/ppermute | solution.py:370
  156.3 29.6 %copy-start.3 = (bf16[2,4,128,384]{3,2,1,0:T(8,128)(2,1)S(1)}, bf16[2,4,128,384]{3,2,1,0:T(8,128)(2,1)}, u32[]{:S(2)}) copy-start(bf16[2,4,128,384]{3,2,1,0:T(8,128)(2,1)} %get-tuple-element.39) | copy-start | bytes 2359300
  156.3 20.7 %collective-permute-start.18 = (bf16[2,4,128,384]{3,2,1,0:T(8,128)(2,1)}, bf16[2,4,128,384]{3,2,1,0:T(8,128)(2,1)S(1)}, u32[]{:S(2)}, u32[]{:S(2)}) collective-permute-start(bf16[2,4,128,384]{3,2,1,0:T(8,128)(2,1)} %get-tuple-element.38), channel_id=1, source_target_pairs={{0,8},{8,0},{16,24},{24,16},{1,9},{9,1},{17,25},{25,17},{2,10},{10... | collective-permute-start | bytes 2359304 | tf_op jit(solution)/shard_map/ppermute | solution.py:370
  157.1 12.0 %collective-permute-start.15 = (bf16[1,4,128,384]{3,2,1,0:T(8,128)(2,1)S(1)}, bf16[1,4,128,384]{3,2,1,0:T(8,128)(2,1)S(1)}, u32[]{:S(2)}, u32[]{:S(2)}) collective-permute-start(bf16[1,4,128,384]{3,2,1,0:T(8,128)(2,1)S(1)} %get-tuple-element.44), channel_id=1, source_target_pairs={{0,16},{8,24},{16,0},{24,8},{1,17},{9,25},{17,1},{25,9},{2,18},{10... | collective-permute-start | bytes 1179656 | tf_op jit(solution)/shard_map/ppermute | solution.py:370
  158.6 27.3 %collective-permute-start.20 = (bf16[2,4,128,384]{3,2,1,0:T(8,128)(2,1)}, bf16[2,4,128,384]{3,2,1,0:T(8,128)(2,1)S(1)}, u32[]{:S(2)}, u32[]{:S(2)}) collective-permute-start(bf16[2,4,128,384]{3,2,1,0:T(8,128)(2,1)} %get-tuple-element.40), channel_id=1, source_target_pairs={{0,16},{8,24},{16,0},{24,8},{1,17},{9,25},{17,1},{25,9},{2,18},{10... | collective-permute-start | bytes 2359304 | tf_op jit(solution)/shard_map/ppermute | solution.py:370
  159.1 28.4 %collective-permute-start.17 = (bf16[1,4,128,384]{3,2,1,0:T(8,128)(2,1)S(1)}, bf16[1,4,128,384]{3,2,1,0:T(8,128)(2,1)S(1)}, u32[]{:S(2)}, u32[]{:S(2)}) collective-permute-start(bf16[1,4,128,384]{3,2,1,0:T(8,128)(2,1)S(1)} %get-tuple-element.46), channel_id=1, source_target_pairs={{0,8},{8,0},{16,24},{24,16},{1,9},{9,1},{17,25},{25,17},{2,10},{10... | collective-permute-start | bytes 1179656 | tf_op jit(solution)/shard_map/ppermute | solution.py:370
  178.4 15.9 %collective-permute-start.19 = (bf16[1,4,128,384]{3,2,1,0:T(8,128)(2,1)S(1)}, bf16[1,4,128,384]{3,2,1,0:T(8,128)(2,1)S(1)}, u32[]{:S(2)}, u32[]{:S(2)}) collective-permute-start(bf16[1,4,128,384]{3,2,1,0:T(8,128)(2,1)S(1)} %slice.47), channel_id=1, source_target_pairs={{0,16},{8,24},{16,0},{24,8},{1,17},{9,25},{17,1},{25,9},{2,18},{10... | collective-permute-start | bytes 1179656 | tf_op jit(solution)/shard_map/ppermute | solution.py:370
  186.1 11.0 %collective-permute-start.21 = (bf16[1,4,128,384]{3,2,1,0:T(8,128)(2,1)S(1)}, bf16[1,4,128,384]{3,2,1,0:T(8,128)(2,1)S(1)}, u32[]{:S(2)}, u32[]{:S(2)}) collective-permute-start(bf16[1,4,128,384]{3,2,1,0:T(8,128)(2,1)S(1)} %slice.49), channel_id=1, source_target_pairs={{0,8},{8,0},{16,24},{24,16},{1,9},{9,1},{17,25},{25,17},{2,10},{10... | collective-permute-start | bytes 1179656 | tf_op jit(solution)/shard_map/ppermute | solution.py:370
Sparse Core Ops, SparseCore 0:
  10.2 55.4 all-gather.1
  126.8 54.6 reduce-scatter.1

commit v7 on v6

--- a/solution.py
+++ b/solution.py
@@ -23,17 +23,17 @@
     return lax.dot_general(a, b, dims, preferred_element_type=f32)
 
 
-def pack_kernel(top, parts, tokens, cotangent, ids, gates, x_out, *dy_out):
+def pack_kernel(top, tokens, ids, gates, x_out):
     count, width = tokens.shape
     x_out[:, pl.ds(0, width)] = tokens[...]
     info = jnp.concatenate(
         [ids[...].astype(f32), gates[...].astype(f32), jnp.zeros((LANES - 2 * top, count), f32)], axis=0
     )
     x_out[:, pl.ds(width, LANES)] = info.T.astype(bf16)
-    piece = width // parts // len(dy_out)
-    for s, out in enumerate(dy_out):
-        for i in range(parts):
-            out[:, pl.ds(i * piece, piece)] = cotangent[:, pl.ds((i * len(dy_out) + s) * piece, piece)]
+
+
+def flip_kernel(w, out):
+    out[0] = w[0].T
 
 
 def start_blocks(place, chips, own, mine, other, dst, sem):
@@ -137,12 +137,13 @@
     return copies
 
 
-def down_rows(orders, place, b, held, scaled, sent, outs, sem):
+def down_rows(orders, place, b, s, slices, held, scaled, sent, outs, sem):
     parts = len(orders[0])
-    piece = held.shape[1] // parts
+    share = held.shape[1] // parts
+    piece = share // slices
     cut = piece // len(orders)
     for q in range(parts):
-        at = pl.multiple_of((place[1] ^ q) * piece, LANES)
+        at = pl.multiple_of((place[1] ^ q) * share + s * piece, LANES)
         full = dot(held[:, pl.ds(at, piece)], scaled, FIRST).astype(bf16)
         for g in range(len(orders)):
             sent[g, q, b] = full[g * cut : (g + 1) * cut]
@@ -150,35 +151,11 @@
         copy.start()
 
 
-def mid_kernel(groups, cap, orders, after, place, pick, *refs):
-    blocks, refs = refs[: 2 * groups - 1], refs[2 * groups - 1 :]
-    w_down, scaled, refs = refs[0], refs[1], refs[2 + after :]
-    back, outs, (held, moved, block_sem, sent, sem) = refs[0], refs[1:-5], refs[-5:]
-    experts = held.shape[0]
-    i = pl.program_id(0)
-
-    @pl.when(i < groups)
-    def _():
-        gather_rows(place, i, cap, pick, blocks, moved, held, block_sem)
-
-    @pl.when(i >= groups)
-    def _():
-        b = i - groups
-        down_rows(orders, place, b, held.at[b], scaled[0], sent, outs, sem)
-        back[0] = dot(held[b], w_down[...].reshape(held.shape[2], back.shape[2]))
-
-    @pl.when(i == groups + experts - 1)
-    def _():
-        for b in range(experts):
-            for copy in down_copies(orders, b, sent, outs, sem):
-                copy.wait()
-
-
-def down_kernel(orders, after, place, rows, scaled, *refs):
+def down_kernel(orders, s, slices, after, place, rows, scaled, *refs):
     outs, (sent, sem) = refs[after:-2], refs[-2:]
     experts = sent.shape[2]
     b = pl.program_id(0)
-    down_rows(orders, place, b, rows.at[0], scaled[0], sent, outs, sem)
+    down_rows(orders, place, b, s, slices, rows.at[0], scaled[0], sent, outs, sem)
 
     @pl.when(b == experts - 1)
     def _():
@@ -187,11 +164,9 @@
                 copy.wait()
 
 
-def tail_kernel(groups, cap, width, top, has_before, place, pick, *refs):
+def tail_kernel(groups, cap, width, top, place, pick, *refs):
     blocks, refs = refs[: 2 * groups - 1], refs[2 * groups - 1 :]
-    w_down, w_up, hid, slope_g, meta = refs[:5]
-    before = refs[5] if has_before else None
-    out, kept, held, moved, block_sem, grads, sem = refs[5 + has_before :]
+    w_down, w_flip, hid, slope_g, meta, out, kept, held, moved, block_sem, grads, sem = refs
     experts = held.shape[0]
     i = pl.program_id(0)
 
@@ -203,14 +178,12 @@
     def _():
         b = i - groups
         pltpu.make_async_copy(held.at[b], kept.at[b], sem.at[b]).start()
-        back = dot(held[b], w_down[...].reshape(held.shape[2], hid.shape[2]))
-        if before is not None:
-            back = back + before[0]
+        back = dot(held[b], w_down[0])
         gate = jnp.sum(back * hid[0].astype(f32), axis=1, keepdims=True)
         lane = lax.broadcasted_iota(jnp.int32, (back.shape[0], LANES), 1)
         gate = jnp.where(lane == b, gate, 0.0).astype(bf16)
         grad = (back * slope_g[0].astype(f32)).astype(bf16)
-        route = dot(grad, w_up[0], LAST).astype(bf16)
+        route = dot(grad, w_flip[0]).astype(bf16)
         at = pl.ds(pl.multiple_of(b * cap, PACK), cap)
         for g in range(groups):
             grads[g, at, pl.ds(0, width)] = route[g * cap : (g + 1) * cap]
@@ -261,18 +234,17 @@
     share = width // dp_count
     slices = SLICES if share % (SLICES * LANES) == 0 else 1
     piece = share // slices
-    cols = dp_count * piece
 
     def shape(*dims, dtype=bf16):
         return jax.ShapeDtypeStruct(dims, dtype)
 
-    x_own, *dy_own = pl.pallas_call(
-        functools.partial(pack_kernel, top, dp_count),
-        out_shape=[shape(tok_rows, full)] + [shape(tok_rows, cols)] * slices,
+    x_own = pl.pallas_call(
+        functools.partial(pack_kernel, top),
+        out_shape=shape(tok_rows, full),
         compiler_params=pltpu.CompilerParams(vmem_limit_bytes=VMEM_LIMIT),
-        cost_estimate=cost(0, 8 * tok_rows * width),
+        cost_estimate=cost(0, 4 * tok_rows * width),
         name="pack",
-    )(tokens, cotangent, expert_ids.T, gate_weights.T)
+    )(tokens, expert_ids.T, gate_weights.T)
     x_all = lax.all_gather(x_own, "ep", axis=0, tiled=True)
 
     def reach(p, step):
@@ -281,20 +253,6 @@
 
     def hop(value, pairs):
         return lax.ppermute(value, "ep", pairs)
-
-    dy_own = [jnp.concatenate([part, hop(part, [(p, p ^ 1) for p in range(ep_count)])], axis=0) for part in dy_own]
-    moving, dy_mine, dy_other = dy_own, [], []
-    for step in range(1, groups):
-        line = [(p, reach(p, 1)) for p in range(ep_count) if None not in (reach(p, 1), reach(p, 1 - step))]
-        swap = [(p, p ^ 1) for p in range(ep_count) if reach(p, -step) is not None]
-        moving = [hop(part, line) for part in moving]
-        dy_mine.append(moving)
-        dy_other.append([hop(part, swap) for part in moving])
-    dy_blocks = [
-        [dy_own[s]] + [part[s] for part in dy_mine] + [part[s] for part in dy_other] for s in range(slices)
-    ]
-    up_after = dy_mine[-2][-1:] if groups > 2 else []
-    mid_after = dy_mine[-1][-1:]
 
     def at_group(i):
         return jnp.minimum(i, groups - 1)
@@ -327,12 +285,36 @@
             name=name,
         )
 
+    row_bytes = 2 * experts * hidden * width
+    w_flip = call(
+        flip_kernel,
+        "flip",
+        experts,
+        0,
+        2 * row_bytes,
+        in_specs=[pl.BlockSpec((1, width, hidden), lambda b: (b, 0, 0))],
+        out_specs=pl.BlockSpec((1, hidden, width), lambda b: (b, 0, 0)),
+        out_shape=shape(experts, hidden, width),
+        scratch_shapes=[],
+    )(w_up)
+    dy_own = jnp.concatenate([cotangent, hop(cotangent, [(p, p ^ 1) for p in range(ep_count)])], axis=0)
+    moving, dy_mine, dy_other = dy_own, [], []
+    for step in range(1, groups):
+        line = [(p, reach(p, 1)) for p in range(ep_count) if None not in (reach(p, 1), reach(p, 1 - step))]
+        swap = [(p, p ^ 1) for p in range(ep_count) if reach(p, -step) is not None]
+        moving = hop(moving, line)
+        dy_mine.append(moving)
+        dy_other.append(swap)
+        if step == 1:
+            moving, w_flip = lax.optimization_barrier((moving, w_flip))
+    dy_other = [hop(part, swap) for part, swap in zip(dy_mine[:-1], dy_other[:-1])] + dy_other[-1:]
+
     act = shape(experts, routes, hidden)
     act_spec = by_expert(routes, hidden)
     pick_spec = pl.BlockSpec((1, experts * cap, members), lambda i, *_: (at_group(i), 0, 0))
     pick_flops = 2 * total * experts * cap * width
     main_flops = 2 * experts * routes * width * hidden
-    row_bytes = 2 * experts * hidden * width
+    up_after = dy_mine[-2:-1]
     pick, meta, hid, scaled, slope_g = call(
         functools.partial(up_kernel, groups, width, top, cap, len(up_after)),
         "up",
@@ -344,6 +326,9 @@
         out_shape=[shape(groups, experts * cap, members), shape(total, LANES), act, act, act],
         scratch_shapes=[pltpu.VMEM((experts, routes, width), bf16), pltpu.VMEM((experts, routes, LANES), f32)],
     )(place, x_all, w_up, *up_after)
+
+    last_block, hid = lax.optimization_barrier((dy_mine[-1], hid))
+    dy_other[-1] = hop(last_block, dy_other[-1])
 
     orders = []
     for g in range(turns):
@@ -358,11 +343,6 @@
         pltpu.VMEM((turns, dp_count, experts, cut_rows, hidden), bf16),
         pltpu.SemaphoreType.DMA((turns, dp_count, experts)),
     ]
-    w_cut = w_down.reshape(experts, dp_count, slices, piece, hidden)
-
-    def cut_spec(s):
-        return pl.BlockSpec((1, dp_count, 1, piece, hidden), lambda i, *_: (at_expert(i), 0, s, 0, 0))
-
     def exchange(state, t):
         new = []
         for g, (keep, send) in enumerate(state):
@@ -375,35 +355,11 @@
             new.append((both[:half], both[half:]) if half else both[0])
         return new
 
-    slot_spec = pl.BlockSpec((1, experts * cap, members), lambda i, place: (at_slot(i, place), 0, 0))
-    block_scratch = [pltpu.VMEM((groups, members, cols), bf16), pltpu.SemaphoreType.DMA((groups, 2))]
-    states, before = [], None
-    for s in range(slices - 1):
-        before, *outs = call(
-            functools.partial(mid_kernel, groups, cap, orders, len(mid_after)),
-            "mid",
-            groups + experts,
-            (pick_flops + 2 * main_flops) // slices,
-            2 * total * cols + 2 * row_bytes // slices,
-            prefetch=1,
-            in_specs=[slot_spec] + [ANY] * (2 * groups - 1) + [cut_spec(s), act_spec] + [ANY] * len(mid_after),
-            out_specs=[act_spec] + [ANY] * len(down_outs),
-            out_shape=[shape(experts, routes, hidden, dtype=f32)] + down_outs,
-            scratch_shapes=[pltpu.VMEM((experts, routes, cols), bf16)] + block_scratch + down_scratch,
-        )(place, pick, *dy_blocks[s], w_cut, scaled, *mid_after)
-        states.append([(outs[2 * g], outs[2 * g + 1]) for g in range(turns)])
-
-    done, after = 0, []
-    if states and bits > 1:
-        states = [exchange(state, 0) for state in states]
-        done, after = 1, [pair[0] for state in states for pair in state]
-
     def at_end(i):
         return jnp.clip(i - groups - experts, 0, groups - 1)
 
-    last = slices - 1
     token_part, kept = call(
-        functools.partial(tail_kernel, groups, cap, width, top, before is not None),
+        functools.partial(tail_kernel, groups, cap, width, top),
         "tail",
         2 * groups + experts,
         8 * main_flops,
@@ -417,42 +373,40 @@
         ]
         + [ANY] * (2 * groups - 1)
         + [
-            cut_spec(last),
             by_expert(width, hidden),
+            by_expert(hidden, width),
             act_spec,
             act_spec,
             pl.BlockSpec((members, LANES), lambda i, *_: (at_end(i), 0)),
-        ]
-        + ([act_spec] if before is not None else []),
+        ],
         out_specs=[pl.BlockSpec((members, full), lambda i, *_: (at_end(i), 0)), ANY],
-        out_shape=[shape(total, full), shape(experts, routes, cols)],
+        out_shape=[shape(total, full), shape(experts, routes, width)],
         scratch_shapes=[
-            pltpu.VMEM((experts, routes, cols), bf16),
-            *block_scratch,
+            pltpu.VMEM((experts, routes, width), bf16),
+            pltpu.VMEM((groups, members, width), bf16),
+            pltpu.SemaphoreType.DMA((groups, 2)),
             pltpu.VMEM((groups, experts * cap, full), bf16),
             pltpu.SemaphoreType.DMA((experts,)),
         ],
-    )(place, pick, *dy_blocks[last], w_cut, w_up, hid, slope_g, meta, *([] if before is None else [before]))
+    )(place, pick, dy_own, *dy_mine, *dy_other, w_down, w_flip, hid, slope_g, meta)
     summed = lax.psum_scatter(token_part, "ep", scatter_dimension=0, tiled=True)
 
-    outs = call(
-        functools.partial(down_kernel, orders, len(after)),
-        "down",
-        experts,
-        16 * main_flops,
-        8 * row_bytes,
-        in_specs=[SMEM]
-        + [pl.BlockSpec((1, routes, n), lambda b: (b, 0, 0)) for n in (cols, hidden)]
-        + [ANY] * len(after),
-        out_specs=[ANY] * len(down_outs),
-        out_shape=down_outs,
-        scratch_shapes=down_scratch,
-    )(place, kept, scaled, *after)
-    states = [(done, state) for state in states]
-    states.append((0, [(outs[2 * g], outs[2 * g + 1]) for g in range(turns)]))
+    states = []
+    for s in range(slices):
+        outs = call(
+            functools.partial(down_kernel, orders, s, slices, 0),
+            "down",
+            experts,
+            16 * main_flops,
+            8 * row_bytes,
+            in_specs=[SMEM] + [pl.BlockSpec((1, routes, n), lambda b: (b, 0, 0)) for n in (width, hidden)],
+            out_specs=[ANY] * len(down_outs),
+            out_shape=down_outs,
+            scratch_shapes=down_scratch,
+        )(place, kept, scaled)
+        states.append([(outs[2 * g], outs[2 * g + 1]) for g in range(turns)])
     for t in range(bits):
-        states = [(done, state) if t < done else (done, exchange(state, t)) for done, state in states]
-    states = [state for _, state in states]
+        states = [exchange(state, t) for state in states]
     down_grad = jnp.concatenate([part for state in states for part in state], axis=1)
     return (summed[:, :width], summed[:, width : width + top], down_grad)
 

time: 210 us -> 193 us (0.919)
  the two profiles are of different devices: /device:TPU:8 before, /device:TPU:0 now
where the time goes in v7:
time: 193 us; the launch traced here: 191 us
  waiting for transfers between devices  93.1 us (48%)
  Pallas kernels  53 us (27%)
  starting transfers between devices  21.6 us (11%)
  between operations  14.3 us (7%)
  local copies, waits for them, and re-layouts  5.61 us (3%)
  other arithmetic  3.58 us (2%)
    ppermute x8, waiting for transfers between devices, exchange(): got = lax.ppermute(send, 'dp', [(i, i ^ bit) for i in range(dp_count)])  36.5 us
    ppermute x7, waiting for transfers between devices, hop(): return lax.ppermute(value, 'ep', pairs)  36.4 us
    all_gather x1, waiting for transfers between devices, shards(): x_all = lax.all_gather(x_own, 'ep', axis=0, tiled=True)  20.2 us
    pallas_call x1, Pallas kernels, shards(): call(functools.partial(tail_kernel, groups, cap, width, top), 'tail', 2 *...  19.7 us
    pallas_call x2, Pallas kernels, shards(): call(functools.partial(down_kernel, orders, s, slices, 0), 'down', expert...  12.8 us
    pallas_call x1, Pallas kernels, shards(): call(functools.partial(up_kernel, groups, width, top, cap, len(up_after))...  11.6 us
    ppermute x8, starting transfers between devices, exchange(): got = lax.ppermute(send, 'dp', [(i, i ^ bit) for i in range(dp_count)])  10.8 us
    ppermute x7, starting transfers between devices, hop(): return lax.ppermute(value, 'ep', pairs)  10.7 us
  transfers between devices with their start and end apart: 17, of which 9 were waited for; matrix products, arithmetic and copies ran while one was open for 3% of the time, Pallas kernels for 16%

profile of v7, /device:TPU:0, one launch (start us, length us, event | category | flops | bytes accessed | tf_op | source)
XLA Modules:
  0.0 191.2 jit_solution(16228896296412564919)
XLA Ops:
  7.2 0.0 all-gather.2.cloned.1.call-start
  7.2 2.0 %pack.1 = bf16[128,2176]{1,0:T(8,128)(2,1)} custom-call(bf16[128,2048]{1,0:T(8,128)(2,1)} %tokens.1, s32[8,128]{1,0:T(8,128)} %bitcast.14, bf16[8,128]{1,0:T(8,128)(2,1)} %bitcast.15), custom_call_target="tpu_custom_call" | custom-call | bytes 1048576 | tf_op jit(solution)/shard_map/pack/pallas_call | solution.py:241
  9.2 0.0 reduce-scatter.2.cloned.1.call-start
  9.3 0.5 collective-permute-start
  9.8 1.1 constant_dynamic-update-slice_fusion.1
  10.9 0.7 collective-permute-done
  11.6 4.9 %collective-permute-start.1 = (bf16[256,2048]{1,0:T(8,128)(2,1)S(1)}, bf16[256,2048]{1,0:T(8,128)(2,1)S(1)}, u32[]{:S(2)}, u32[]{:S(2)}) collective-permute-start(bf16[256,2048]{1,0:T(8,128)(2,1)S(1)} %constant_dynamic-update-slice_fusion.refs_0_), channel_id=1, source_target_pairs={{0,2},{2,4},{3,1},{4,6},{5,3},{7,5},{8,10},{10,12},{11,9},{12,14},... | collective-permute-start | bytes 3145736 | tf_op jit(solution)/shard_map/ppermute | solution.py:255
  16.5 7.0 %flip.1.refs_8_ = bf16[4,384,2048]{2,1,0:T(8,128)(2,1)} custom-call(bf16[4,2048,384]{2,1,0:T(8,128)(2,1)} %w_up.1), custom_call_target="tpu_custom_call" | custom-call | bytes 12582912 | tf_op jit(solution)/shard_map/flip/pallas_call | solution.py:289
  23.5 21.3 %collective-permute-done.1.refs_1_ = bf16[256,2048]{1,0:T(8,128)(2,1)S(1)} collective-permute-done((bf16[256,2048]{1,0:T(8,128)(2,1)S(1)}, bf16[256,2048]{1,0:T(8,128)(2,1)S(1)}, u32[]{:S(2)}, u32[]{:S(2)}) %collective-permute-start.1) | collective-permute-done | bytes 1048608 | tf_op jit(solution)/shard_map/ppermute | solution.py:255
  44.8 0.7 collective-permute-start.2
  45.6 0.7 collective-permute-start.3
  46.3 0.6 pad_add_fusion.place
  46.9 1.3 collective-permute-start.4
  48.2 1.3 collective-permute-start.5
  49.5 20.2 %all-gather.2.cloned.1.call-done.rows = bf16[1024,2176]{1,0:T(8,128)(2,1)} async-done(((bf16[128,2176]{1,0:T(8,128)(2,1)}), bf16[1024,2176]{1,0:T(8,128)(2,1)}) %all-gather.2.cloned.1.call-update) | async-done | bytes 4456464 | tf_op jit(solution)/shard_map/all_gather | solution.py:248
  69.7 11.6 %up.1 = (bf16[4,320,256]{2,1,0:T(8,128)(2,1)}, bf16[1024,128]{1,0:T(8,128)(2,1)}, bf16[4,320,384]{2,1,0:T(8,128)(2,1)}, bf16[4,320,384]{2,1,0:T(8,128)(2,1)}, bf16[4,320,384]{2,1,0:T(8,128)(2,1)}) custom-call(s32[4]{0:T(128)} %pad_add_fusion.place, bf16[1024,2176]{1,0:T(8,128)(2,1)} %all-gather.2.cloned.1.call-done.rows, bf16[4,2048,384]{2,1,0:T(8,128)(2,1)} %w_up.1, ...), custom_call_target="tpu_custom_call" | custom-call | flops 3355443200 | bytes 10747904 | tf_op jit(solution)/shard_map/up/pallas_call | solution.py:318
  81.2 1.3 collective-permute-start.6
  82.6 0.7 collective-permute-done.5.refs_5_
  83.3 13.7 %collective-permute-done.6.refs_6_ = bf16[256,2048]{1,0:T(8,128)(2,1)S(1)} collective-permute-done((bf16[256,2048]{1,0:T(8,128)(2,1)S(1)}, bf16[256,2048]{1,0:T(8,128)(2,1)S(1)}, u32[]{:S(2)}, u32[]{:S(2)}) %collective-permute-start.6) | collective-permute-done | bytes 1048608 | tf_op jit(solution)/shard_map/ppermute | solution.py:255
  97.0 1.0 copy-done.8
  98.0 19.7 %tail.1 = (bf16[1024,2176]{1,0:T(8,128)(2,1)}, bf16[4,320,2048]{2,1,0:T(8,128)(2,1)}) custom-call(s32[4]{0:T(128)} %pad_add_fusion.place, bf16[4,320,256]{2,1,0:T(8,128)(2,1)} %get-tuple-element.23.pick, bf16[256,2048]{1,0:T(8,128)(2,1)} %copy-done.4, bf16[256,2048]{1,0:T(8,128)(2,1)} %copy-done.5, bf16[256,2048]{1,0:T(8,128)(2,1)} %copy-done.6, ...), custom_call_target="tpu_custom_call" | custom-call | flops 16106127360 | bytes 25165824 | tf_op jit(solution)/shard_map/tail/pallas_call | solution.py:361
  117.7 0.0 reduce-scatter.2.cloned.1.call-update
  117.7 6.4 %down.3 = (bf16[2,4,128,384]{3,2,1,0:T(8,128)(2,1)}, bf16[2,4,128,384]{3,2,1,0:T(8,128)(2,1)}, bf16[2,4,128,384]{3,2,1,0:T(8,128)(2,1)}, bf16[2,4,128,384]{3,2,1,0:T(8,128)(2,1)}) custom-call(s32[4]{0:T(128)} %pad_add_fusion.place, bf16[4,320,2048]{2,1,0:T(8,128)(2,1)} %get-tuple-element.31.rows, bf16[4,320,384]{2,1,0:T(8,128)(2,1)} %get-tuple-element.32.scaled), custom_call_target="tpu_custom_call" | custom-call | flops 32212254720 | bytes 50331648 | tf_op jit(solution)/shard_map/down/pallas_call | solution.py:396
  124.1 1.7 collective-permute-start.11
  125.8 1.5 collective-permute-start.13
  127.4 6.4 %down.2 = (bf16[2,4,128,384]{3,2,1,0:T(8,128)(2,1)}, bf16[2,4,128,384]{3,2,1,0:T(8,128)(2,1)}, bf16[2,4,128,384]{3,2,1,0:T(8,128)(2,1)}, bf16[2,4,128,384]{3,2,1,0:T(8,128)(2,1)}) custom-call(s32[4]{0:T(128)} %pad_add_fusion.place, bf16[4,320,2048]{2,1,0:T(8,128)(2,1)} %get-tuple-element.31.rows, bf16[4,320,384]{2,1,0:T(8,128)(2,1)} %get-tuple-element.32.scaled), custom_call_target="tpu_custom_call" | custom-call | flops 32212254720 | bytes 50331648 | tf_op jit(solution)/shard_map/down/pallas_call | solution.py:396
  133.8 0.7 collective-permute-start.7
  134.5 0.2 collective-permute-start.9
  134.8 10.0 %collective-permute-done.11 = bf16[2,4,128,384]{3,2,1,0:T(8,128)(2,1)S(1)} collective-permute-done((bf16[2,4,128,384]{3,2,1,0:T(8,128)(2,1)}, bf16[2,4,128,384]{3,2,1,0:T(8,128)(2,1)S(1)}, u32[]{:S(2)}, u32[]{:S(2)}) %collective-permute-start.11) | collective-permute-done | bytes 786464 | tf_op jit(solution)/shard_map/ppermute | solution.py:350
  144.8 0.2 add_convert_fusion.1
  145.0 1.7 collective-permute-start.12
  146.8 0.2 add_convert_fusion
  147.0 1.6 collective-permute-start.14
  148.6 13.0 %collective-permute-done.7 = bf16[2,4,128,384]{3,2,1,0:T(8,128)(2,1)S(1)} collective-permute-done((bf16[2,4,128,384]{3,2,1,0:T(8,128)(2,1)}, bf16[2,4,128,384]{3,2,1,0:T(8,128)(2,1)S(1)}, u32[]{:S(2)}, u32[]{:S(2)}) %collective-permute-start.7) | collective-permute-done | bytes 786464 | tf_op jit(solution)/shard_map/ppermute | solution.py:350
  161.6 0.2 add_convert_fusion.3
  161.9 1.7 collective-permute-start.8
  163.6 0.2 add_convert_fusion.2
  163.9 1.6 collective-permute-start.10
  165.4 6.3 %collective-permute-done.12 = bf16[1,4,128,384]{3,2,1,0:T(8,128)(2,1)S(1)} collective-permute-done((bf16[1,4,128,384]{3,2,1,0:T(8,128)(2,1)S(1)}, bf16[1,4,128,384]{3,2,1,0:T(8,128)(2,1)S(1)}, u32[]{:S(2)}, u32[]{:S(2)}) %collective-permute-start.12) | collective-permute-done | bytes 393248 | tf_op jit(solution)/shard_map/ppermute | solution.py:350
  171.7 0.1 add_bitcast_fusion.1
  171.8 0.1 add_bitcast_fusion
  171.9 7.1 %collective-permute-done.8 = bf16[1,4,128,384]{3,2,1,0:T(8,128)(2,1)S(1)} collective-permute-done((bf16[1,4,128,384]{3,2,1,0:T(8,128)(2,1)S(1)}, bf16[1,4,128,384]{3,2,1,0:T(8,128)(2,1)S(1)}, u32[]{:S(2)}, u32[]{:S(2)}) %collective-permute-start.8) | collective-permute-done | bytes 393248 | tf_op jit(solution)/shard_map/ppermute | solution.py:350
  179.0 0.1 add_bitcast_fusion.3
  179.1 0.1 add_bitcast_fusion.2
  179.2 1.9 pad_maximum_fusion
  181.1 0.8 slice.41
  181.9 0.7 copy.9
  182.5 1.9 slice.40
  (31 shorter events, 0.3 us)
Async XLA Ops:
  7.2 62.5 %all-gather.2.cloned.1.call-start = ((), (), s32[]{:S(2)}) async-start(), calls=%async_computation.1 | async-start | bytes 5013504 | tf_op jit(solution)/shard_map/all_gather | solution.py:248
  9.2 171.9 %reduce-scatter.2.cloned.1.call-start = ((), (), s32[]{:S(2)}) async-start(), calls=%async_computation.2 | async-start | bytes 5013504 | tf_op jit(solution)/shard_map/reduce_scatter | solution.py:392
  9.3 2.3 %collective-permute-start = (bf16[128,2048]{1,0:T(8,128)(2,1)}, bf16[128,2048]{1,0:T(8,128)(2,1)S(1)}, u32[]{:S(2)}, u32[]{:S(2)}) collective-permute-start(bf16[128,2048]{1,0:T(8,128)(2,1)} %param.7), channel_id=1, source_target_pairs={{0,1},{1,0},{2,3},{3,2},{4,5},{5,4},{6,7},{7,6},{8,9},{9,8},{10,11... | collective-permute-start | bytes 1572872 | tf_op jit(solution)/shard_map/ppermute | solution.py:255
  11.6 11.9 %copy-start.4 = (bf16[256,2048]{1,0:T(8,128)(2,1)}, bf16[256,2048]{1,0:T(8,128)(2,1)S(1)}, u32[]{:S(2)}) copy-start(bf16[256,2048]{1,0:T(8,128)(2,1)S(1)} %constant_dynamic-update-slice_fusion.refs_0_) | copy-start | bytes 3145732
  11.6 33.2 %collective-permute-start.1 = (bf16[256,2048]{1,0:T(8,128)(2,1)S(1)}, bf16[256,2048]{1,0:T(8,128)(2,1)S(1)}, u32[]{:S(2)}, u32[]{:S(2)}) collective-permute-start(bf16[256,2048]{1,0:T(8,128)(2,1)S(1)} %constant_dynamic-update-slice_fusion.refs_0_), channel_id=1, source_target_pairs={{0,2},{2,4},{3,1},{4,6},{5,3},{7,5},{8,10},{10,12},{11,9},{12,14},... | collective-permute-start | bytes 3145736 | tf_op jit(solution)/shard_map/ppermute | solution.py:255
  44.8 36.4 %copy-start.5 = (bf16[256,2048]{1,0:T(8,128)(2,1)}, bf16[256,2048]{1,0:T(8,128)(2,1)S(1)}, u32[]{:S(2)}) copy-start(bf16[256,2048]{1,0:T(8,128)(2,1)S(1)} %collective-permute-done.1.refs_1_) | copy-start | bytes 3145732
  44.8 0.7 collective-permute-start.2
  45.6 24.1 %copy-start.6 = (bf16[256,2048]{1,0:T(8,128)(2,1)}, bf16[256,2048]{1,0:T(8,128)(2,1)S(1)}, u32[]{:S(2)}) copy-start(bf16[256,2048]{1,0:T(8,128)(2,1)S(1)} %collective-permute-done.2.refs_0_.refs_2_) | copy-start | bytes 3145732
  45.6 35.7 %collective-permute-start.3 = (bf16[256,2048]{1,0:T(8,128)(2,1)S(1)}, bf16[256,2048]{1,0:T(8,128)(2,1)S(1)}, u32[]{:S(2)}, u32[]{:S(2)}) collective-permute-start(bf16[256,2048]{1,0:T(8,128)(2,1)S(1)} %collective-permute-done.2.refs_0_.refs_2_), channel_id=1, source_target_pairs={{3,1},{4,6},{11,9},{12,14},{19,17},{20,22},{27,25},{28,30}} | collective-permute-start | bytes 3145736 | tf_op jit(solution)/shard_map/ppermute | solution.py:255
  46.9 35.6 %collective-permute-start.4 = (bf16[256,2048]{1,0:T(8,128)(2,1)S(1)}, bf16[256,2048]{1,0:T(8,128)(2,1)}, u32[]{:S(2)}, u32[]{:S(2)}) collective-permute-start(bf16[256,2048]{1,0:T(8,128)(2,1)S(1)} %collective-permute-done.1.refs_1_), channel_id=1, source_target_pairs={{1,0},{2,3},{3,2},{4,5},{5,4},{6,7},{9,8},{10,11},{11,10},{12,13},... | collective-permute-start | bytes 3145736 | tf_op jit(solution)/shard_map/ppermute | solution.py:255
  48.2 35.1 %collective-permute-start.5 = (bf16[256,2048]{1,0:T(8,128)(2,1)S(1)}, bf16[256,2048]{1,0:T(8,128)(2,1)}, u32[]{:S(2)}, u32[]{:S(2)}) collective-permute-start(bf16[256,2048]{1,0:T(8,128)(2,1)S(1)} %collective-permute-done.2.refs_0_.refs_2_), channel_id=1, source_target_pairs={{1,0},{3,2},{4,5},{6,7},{9,8},{11,10},{12,13},{14,15},{17,16},{19,... | collective-permute-start | bytes 3145736 | tf_op jit(solution)/shard_map/ppermute | solution.py:255
  81.2 16.7 %copy-start.7 = (bf16[256,2048]{1,0:T(8,128)(2,1)}, bf16[256,2048]{1,0:T(8,128)(2,1)S(1)}, u32[]{:S(2)}) copy-start(bf16[256,2048]{1,0:T(8,128)(2,1)S(1)} %collective-permute-done.3.refs_3_) | copy-start | bytes 3145732
  81.2 15.7 %collective-permute-start.6 = (bf16[256,2048]{1,0:T(8,128)(2,1)S(1)}, bf16[256,2048]{1,0:T(8,128)(2,1)S(1)}, u32[]{:S(2)}, u32[]{:S(2)}) collective-permute-start(bf16[256,2048]{1,0:T(8,128)(2,1)S(1)} %collective-permute-done.3.refs_3_), channel_id=1, source_target_pairs={{1,0},{6,7},{9,8},{14,15},{17,16},{22,23},{25,24},{30,31}} | collective-permute-start | bytes 3145736 | tf_op jit(solution)/shard_map/ppermute | solution.py:255
  97.0 1.0 copy-start.8
  124.1 20.7 %collective-permute-start.11 = (bf16[2,4,128,384]{3,2,1,0:T(8,128)(2,1)}, bf16[2,4,128,384]{3,2,1,0:T(8,128)(2,1)S(1)}, u32[]{:S(2)}, u32[]{:S(2)}) collective-permute-start(bf16[2,4,128,384]{3,2,1,0:T(8,128)(2,1)} %get-tuple-element.38), channel_id=1, source_target_pairs={{0,8},{8,0},{16,24},{24,16},{1,9},{9,1},{17,25},{25,17},{2,10},{10... | collective-permute-start | bytes 2359304 | tf_op jit(solution)/shard_map/ppermute | solution.py:350
  125.8 19.0 %copy-start.3 = (bf16[2,4,128,384]{3,2,1,0:T(8,128)(2,1)S(1)}, bf16[2,4,128,384]{3,2,1,0:T(8,128)(2,1)}, u32[]{:S(2)}) copy-start(bf16[2,4,128,384]{3,2,1,0:T(8,128)(2,1)} %get-tuple-element.37) | copy-start | bytes 2359300
  125.8 20.9 %collective-permute-start.13 = (bf16[2,4,128,384]{3,2,1,0:T(8,128)(2,1)}, bf16[2,4,128,384]{3,2,1,0:T(8,128)(2,1)S(1)}, u32[]{:S(2)}, u32[]{:S(2)}) collective-permute-start(bf16[2,4,128,384]{3,2,1,0:T(8,128)(2,1)} %get-tuple-element.40), channel_id=1, source_target_pairs={{0,16},{8,24},{16,0},{24,8},{1,17},{9,25},{17,1},{25,9},{2,18},{10... | collective-permute-start | bytes 2359304 | tf_op jit(solution)/shard_map/ppermute | solution.py:350
  133.8 13.0 %copy-start.2 = (bf16[2,4,128,384]{3,2,1,0:T(8,128)(2,1)S(1)}, bf16[2,4,128,384]{3,2,1,0:T(8,128)(2,1)}, u32[]{:S(2)}) copy-start(bf16[2,4,128,384]{3,2,1,0:T(8,128)(2,1)} %get-tuple-element.39) | copy-start | bytes 2359300
  133.8 27.8 %collective-permute-start.7 = (bf16[2,4,128,384]{3,2,1,0:T(8,128)(2,1)}, bf16[2,4,128,384]{3,2,1,0:T(8,128)(2,1)S(1)}, u32[]{:S(2)}, u32[]{:S(2)}) collective-permute-start(bf16[2,4,128,384]{3,2,1,0:T(8,128)(2,1)} %get-tuple-element.34), channel_id=1, source_target_pairs={{0,8},{8,0},{16,24},{24,16},{1,9},{9,1},{17,25},{25,17},{2,10},{10... | collective-permute-start | bytes 2359304 | tf_op jit(solution)/shard_map/ppermute | solution.py:350
  134.5 29.1 %collective-permute-start.9 = (bf16[2,4,128,384]{3,2,1,0:T(8,128)(2,1)}, bf16[2,4,128,384]{3,2,1,0:T(8,128)(2,1)S(1)}, u32[]{:S(2)}, u32[]{:S(2)}) collective-permute-start(bf16[2,4,128,384]{3,2,1,0:T(8,128)(2,1)} %get-tuple-element.36), channel_id=1, source_target_pairs={{0,16},{8,24},{16,0},{24,8},{1,17},{9,25},{17,1},{25,9},{2,18},{10... | collective-permute-start | bytes 2359304 | tf_op jit(solution)/shard_map/ppermute | solution.py:350
  144.8 16.9 %copy-start.1 = (bf16[2,4,128,384]{3,2,1,0:T(8,128)(2,1)S(1)}, bf16[2,4,128,384]{3,2,1,0:T(8,128)(2,1)}, u32[]{:S(2)}) copy-start(bf16[2,4,128,384]{3,2,1,0:T(8,128)(2,1)} %get-tuple-element.33) | copy-start | bytes 2359300
  145.0 26.7 %collective-permute-start.12 = (bf16[1,4,128,384]{3,2,1,0:T(8,128)(2,1)S(1)}, bf16[1,4,128,384]{3,2,1,0:T(8,128)(2,1)S(1)}, u32[]{:S(2)}, u32[]{:S(2)}) collective-permute-start(bf16[1,4,128,384]{3,2,1,0:T(8,128)(2,1)S(1)} %slice.47), channel_id=1, source_target_pairs={{0,16},{8,24},{16,0},{24,8},{1,17},{9,25},{17,1},{25,9},{2,18},{10... | collective-permute-start | bytes 1179656 | tf_op jit(solution)/shard_map/ppermute | solution.py:350
  146.8 16.8 %copy-start = (bf16[2,4,128,384]{3,2,1,0:T(8,128)(2,1)S(1)}, bf16[2,4,128,384]{3,2,1,0:T(8,128)(2,1)}, u32[]{:S(2)}) copy-start(bf16[2,4,128,384]{3,2,1,0:T(8,128)(2,1)} %get-tuple-element.35) | copy-start | bytes 2359300
  147.0 24.8 %collective-permute-start.14 = (bf16[1,4,128,384]{3,2,1,0:T(8,128)(2,1)S(1)}, bf16[1,4,128,384]{3,2,1,0:T(8,128)(2,1)S(1)}, u32[]{:S(2)}, u32[]{:S(2)}) collective-permute-start(bf16[1,4,128,384]{3,2,1,0:T(8,128)(2,1)S(1)} %slice.49), channel_id=1, source_target_pairs={{0,8},{8,0},{16,24},{24,16},{1,9},{9,1},{17,25},{25,17},{2,10},{10... | collective-permute-start | bytes 1179656 | tf_op jit(solution)/shard_map/ppermute | solution.py:350
  161.9 17.2 %collective-permute-start.8 = (bf16[1,4,128,384]{3,2,1,0:T(8,128)(2,1)S(1)}, bf16[1,4,128,384]{3,2,1,0:T(8,128)(2,1)S(1)}, u32[]{:S(2)}, u32[]{:S(2)}) collective-permute-start(bf16[1,4,128,384]{3,2,1,0:T(8,128)(2,1)S(1)} %slice.43), channel_id=1, source_target_pairs={{0,16},{8,24},{16,0},{24,8},{1,17},{9,25},{17,1},{25,9},{2,18},{10... | collective-permute-start | bytes 1179656 | tf_op jit(solution)/shard_map/ppermute | solution.py:350
  163.9 15.3 %collective-permute-start.10 = (bf16[1,4,128,384]{3,2,1,0:T(8,128)(2,1)S(1)}, bf16[1,4,128,384]{3,2,1,0:T(8,128)(2,1)S(1)}, u32[]{:S(2)}, u32[]{:S(2)}) collective-permute-start(bf16[1,4,128,384]{3,2,1,0:T(8,128)(2,1)S(1)} %slice.45), channel_id=1, source_target_pairs={{0,8},{8,0},{16,24},{24,16},{1,9},{9,1},{17,25},{25,17},{2,10},{10... | collective-permute-start | bytes 1179656 | tf_op jit(solution)/shard_map/ppermute | solution.py:350
Sparse Core Ops, SparseCore 0:
  9.6 59.9 all-gather.1
  117.8 55.9 reduce-scatter.1

commit v8 on v7

--- a/solution.py
+++ b/solution.py
@@ -9,14 +9,12 @@
 
 LANES = 128
 PACK = 16
-SLICES = 2
 GROUP = 2
 VMEM_LIMIT = 60 * 1024 * 1024
 bf16, f32 = jnp.bfloat16, jnp.float32
 ANY = pl.BlockSpec(memory_space=pl.ANY)
 SMEM = pl.BlockSpec(memory_space=pltpu.SMEM)
 FIRST = (((0,), (0,)), ((), ()))
-LAST = (((1,), (1,)), ((), ()))
 
 
 def dot(a, b, dims=(((1,), (0,)), ((), ()))):
@@ -36,30 +34,44 @@
     out[0] = w[0].T
 
 
+def block_copies(place, ref, dst, sem, flip):
+    half = ref.shape[0] // 2
+    copies = []
+    for part in range(2):
+        to = (part ^ flip) * half
+        if not isinstance(flip, int):
+            to = pl.multiple_of(to, half)
+        copies.append(
+            pltpu.make_async_copy(ref.at[pl.ds(part * half, half), :], dst.at[pl.ds(to, half), :], sem.at[part])
+        )
+    return copies
+
+
+def by_side(place, is_left, mine, other, act):
+    for left in (True, False):
+        for core in (True, False):
+            ref = (mine if left == core else other)(left)
+            if ref is not None:
+
+                @pl.when((is_left == left) & ((place[2] == 0) == core))
+                def _():
+                    act(ref, 0 if left else 1)
+
+
 def start_blocks(place, chips, own, mine, other, dst, sem):
-    half = own.shape[0] // 2
-    left_core = place[2] == 0
-
-    def start(ref, slot, flip):
-        for part in range(2):
-            to = (part ^ flip) * half
-            if not isinstance(flip, int):
-                to = pl.multiple_of(to, half)
-            pltpu.make_async_copy(
-                ref.at[pl.ds(part * half, half), :], dst.at[slot, pl.ds(to, half), :], sem.at[slot, part]
-            ).start()
-
-    start(own, 0, place[2])
+    for copy in block_copies(place, own, dst.at[0], sem.at[0], place[2]):
+        copy.start()
     for slot in range(1, chips):
-        left = place[3] >= slot
-        for is_left in (True, False):
-            for is_core in (True, False):
-                step = slot if is_left else chips - slot
-                ref = (mine if is_left == is_core else other)[step - 1]
-
-                @pl.when((left == is_left) & (left_core == is_core))
-                def _():
-                    start(ref, slot, 0 if is_left else 1)
+
+        def pick(blocks, left):
+            step = slot if left else chips - slot
+            return blocks[step - 1] if step <= len(blocks) else None
+
+        def start(ref, flip):
+            for copy in block_copies(place, ref, dst.at[slot], sem.at[slot], flip):
+                copy.start()
+
+        by_side(place, place[3] >= slot, functools.partial(pick, mine), functools.partial(pick, other), start)
 
 
 def up_kernel(groups, width, top, cap, after, place, rows, w_up, *refs):
@@ -106,22 +118,83 @@
         slope_g[0] = (gate * (sig + act * (1.0 - sig))).astype(bf16)
 
 
-def gather_rows(place, i, cap, pick, blocks, moved, held, sem):
-    experts, groups = held.shape[0], moved.shape[0]
-    own, mine, other = blocks[0], blocks[1:groups], blocks[groups:]
+def early_kernel(groups, cap, place, pick, *refs):
+    steps = groups - 2
+    own, mine, other, refs = refs[0], refs[1 : 1 + steps], refs[1 + steps : 1 + 2 * steps], refs[1 + 2 * steps :]
+    w_down, back, kept, held, moved, block_sem, sem = refs
+    experts = held.shape[0]
+    i = pl.program_id(0)
 
     @pl.when(i == 0)
     def _():
-        start_blocks(place, groups, own, mine, other, moved, sem)
-
-    half = own.shape[0] // 2
-    for part in range(2):
-        at = pl.ds(part * half, half)
-        pltpu.make_async_copy(own.at[at, :], moved.at[i, at, :], sem.at[i, part]).wait()
-    first = pl.multiple_of(lax.rem(place[3] - i + groups, groups) * cap, PACK)
-    got = dot(pick[0], moved[i]).astype(bf16)
-    for b in range(experts):
-        held[b, pl.ds(first, cap), :] = got[b * cap : (b + 1) * cap]
+        start_blocks(place, groups, own, mine, other, moved, block_sem)
+
+    here = (i == 0) | (jnp.where(place[3] >= i, i, groups - i) <= steps)
+    first = pl.multiple_of(lax.rem(place[3] - i + 2 * groups, groups) * cap, PACK)
+
+    @pl.when((i < groups) & here)
+    def _():
+        half = own.shape[0] // 2
+        for part in range(2):
+            at = pl.ds(part * half, half)
+            pltpu.make_async_copy(own.at[at, :], moved.at[i, at, :], block_sem.at[i, part]).wait()
+        got = dot(pick[0], moved[i]).astype(bf16)
+        for b in range(experts):
+            held[b, pl.ds(first, cap), :] = got[b * cap : (b + 1) * cap]
+
+    @pl.when((i < groups) & jnp.logical_not(here))
+    def _():
+        for b in range(experts):
+            held[b, pl.ds(first, cap), :] = jnp.zeros((cap, held.shape[2]), bf16)
+
+    @pl.when(i >= groups)
+    def _():
+        b = i - groups
+        pltpu.make_async_copy(held.at[b], kept.at[b], sem.at[b]).start()
+        back[0] = dot(held[b], w_down[0])
+
+    @pl.when(i == groups + experts - 1)
+    def _():
+        for b in range(experts):
+            pltpu.make_async_copy(held.at[b], kept.at[b], sem.at[b]).wait()
+
+
+def last_group(place, groups):
+    chip = place[3]
+    return (chip == 0) | (chip == groups - 1), jnp.where(chip == 0, groups - 1, 0)
+
+
+def fill_kernel(groups, cap, place, pick, mine, other, early, kept, late, rows, table, sem, table_sem, out_sem):
+    del early
+    experts = late.shape[0]
+    has, group = last_group(place, groups)
+
+    @pl.when(has)
+    def _():
+        fetch = pltpu.make_async_copy(pick.at[group], table, table_sem)
+        fetch.start()
+
+        def start(ref, flip):
+            for copy in block_copies(place, ref, rows, sem, flip):
+                copy.start()
+
+        by_side(place, place[3] != 0, lambda left: mine, lambda left: other, start)
+        fetch.wait()
+        for copy in block_copies(place, mine, rows, sem, 0):
+            copy.wait()
+        got = dot(table[...], rows[...]).astype(bf16)
+        for b in range(experts):
+            late[b] = got[b * cap : (b + 1) * cap]
+        at = pl.ds(pl.multiple_of(group * cap, PACK), cap)
+        copies = [pltpu.make_async_copy(late.at[b], kept.at[b, at, :], out_sem.at[b]) for b in range(experts)]
+        for copy in copies:
+            copy.start()
+        for copy in copies:
+            copy.wait()
+
+    @pl.when(jnp.logical_not(has))
+    def _():
+        late[...] = jnp.zeros(late.shape, bf16)
 
 
 def down_copies(orders, b, sent, outs, sem):
@@ -137,26 +210,21 @@
     return copies
 
 
-def down_rows(orders, place, b, s, slices, held, scaled, sent, outs, sem):
+def down_kernel(orders, after, place, rows, scaled, *refs):
+    outs, (sent, sem) = refs[after:-2], refs[-2:]
+    experts = sent.shape[2]
+    b = pl.program_id(0)
     parts = len(orders[0])
-    share = held.shape[1] // parts
-    piece = share // slices
-    cut = piece // len(orders)
-    for q in range(parts):
-        at = pl.multiple_of((place[1] ^ q) * share + s * piece, LANES)
-        full = dot(held[:, pl.ds(at, piece)], scaled, FIRST).astype(bf16)
+    share = rows.shape[2] // parts
+    cut = share // len(orders)
+    for q in reversed(range(parts)):
+        at = pl.multiple_of((place[1] ^ q) * share, LANES)
+        full = dot(rows[0, :, pl.ds(at, share)], scaled[0], FIRST).astype(bf16)
         for g in range(len(orders)):
             sent[g, q, b] = full[g * cut : (g + 1) * cut]
     for copy in down_copies(orders, b, sent, outs, sem):
         copy.start()
 
-
-def down_kernel(orders, s, slices, after, place, rows, scaled, *refs):
-    outs, (sent, sem) = refs[after:-2], refs[-2:]
-    experts = sent.shape[2]
-    b = pl.program_id(0)
-    down_rows(orders, place, b, s, slices, rows.at[0], scaled[0], sent, outs, sem)
-
     @pl.when(b == experts - 1)
     def _():
         for e in range(experts):
@@ -164,37 +232,38 @@
                 copy.wait()
 
 
-def tail_kernel(groups, cap, width, top, place, pick, *refs):
-    blocks, refs = refs[: 2 * groups - 1], refs[2 * groups - 1 :]
-    w_down, w_flip, hid, slope_g, meta, out, kept, held, moved, block_sem, grads, sem = refs
-    experts = held.shape[0]
+def tail_kernel(groups, cap, width, top, after, place, pick, late, early, w_down, w_flip, hid, slope_g, meta, *refs):
+    out, total, grads = refs[after:]
+    experts = grads.shape[1] // cap
     i = pl.program_id(0)
 
-    @pl.when(i < groups)
-    def _():
-        gather_rows(place, i, cap, pick, blocks, moved, held, block_sem)
-
-    @pl.when((i >= groups) & (i < groups + experts))
-    def _():
-        b = i - groups
-        pltpu.make_async_copy(held.at[b], kept.at[b], sem.at[b]).start()
-        back = dot(held[b], w_down[0])
+    @pl.when(i < experts)
+    def _():
+        has, group = last_group(place, groups)
+        total[...] = early[0]
+
+        @pl.when(has)
+        def _():
+            at = pl.ds(pl.multiple_of(group * cap, PACK), cap)
+            total[at, :] = dot(late[0], w_down[0])
+
+        back = total[...]
         gate = jnp.sum(back * hid[0].astype(f32), axis=1, keepdims=True)
         lane = lax.broadcasted_iota(jnp.int32, (back.shape[0], LANES), 1)
-        gate = jnp.where(lane == b, gate, 0.0).astype(bf16)
+        gate = jnp.where(lane == i, gate, 0.0).astype(bf16)
         grad = (back * slope_g[0].astype(f32)).astype(bf16)
         route = dot(grad, w_flip[0]).astype(bf16)
-        at = pl.ds(pl.multiple_of(b * cap, PACK), cap)
+        at = pl.ds(pl.multiple_of(i * cap, PACK), cap)
         for g in range(groups):
             grads[g, at, pl.ds(0, width)] = route[g * cap : (g + 1) * cap]
             grads[g, at, pl.ds(width, LANES)] = gate[g * cap : (g + 1) * cap]
 
-    @pl.when(i >= groups + experts)
-    def _():
-        g = i - groups - experts
-        total = dot(pick[0], grads[g], FIRST)
-        out[:, pl.ds(0, width)] = total[:, :width].astype(bf16)
-        by_expert = total[:, width:]
+    @pl.when(i >= experts)
+    def _():
+        g = i - experts
+        summed = dot(pick[0], grads[g], FIRST)
+        out[:, pl.ds(0, width)] = summed[:, :width].astype(bf16)
+        by_expert = summed[:, width:]
         info = meta[...].astype(f32)
         lane = lax.broadcasted_iota(jnp.int32, info.shape, 1)
         ids = jnp.where(lane < top, info, -1.0)
@@ -204,10 +273,10 @@
             picked = picked + jnp.where(hit, by_expert[:, b : b + 1], 0.0)
         out[:, pl.ds(width, LANES)] = picked.astype(bf16)
 
-    @pl.when(i == 2 * groups + experts - 1)
-    def _():
-        for b in range(experts):
-            pltpu.make_async_copy(held.at[b], kept.at[b], sem.at[b]).wait()
+
+def finish_kernel(width, top, rows, token, gate):
+    token[...] = rows[:, pl.ds(0, width)]
+    gate[...] = rows[:, pl.ds(width, LANES)].astype(f32).T[:top].astype(bf16)
 
 
 def cost(flops, nbytes):
@@ -232,8 +301,6 @@
     bits = dp_count.bit_length() - 1
     turns = 2
     share = width // dp_count
-    slices = SLICES if share % (SLICES * LANES) == 0 else 1
-    piece = share // slices
 
     def shape(*dims, dtype=bf16):
         return jax.ShapeDtypeStruct(dims, dtype)
@@ -299,22 +366,26 @@
     )(w_up)
     dy_own = jnp.concatenate([cotangent, hop(cotangent, [(p, p ^ 1) for p in range(ep_count)])], axis=0)
     moving, dy_mine, dy_other = dy_own, [], []
-    for step in range(1, groups):
-        line = [(p, reach(p, 1)) for p in range(ep_count) if None not in (reach(p, 1), reach(p, 1 - step))]
-        swap = [(p, p ^ 1) for p in range(ep_count) if reach(p, -step) is not None]
-        moving = hop(moving, line)
-        dy_mine.append(moving)
-        dy_other.append(swap)
+    lines = [None] + [
+        [(p, reach(p, 1)) for p in range(ep_count) if None not in (reach(p, 1), reach(p, 1 - step))]
+        for step in range(1, groups)
+    ]
+    swaps = [None] + [
+        [(p, p ^ 1) for p in range(ep_count) if reach(p, -step) is not None] for step in range(1, groups)
+    ]
+    for step in range(1, groups - 1):
+        moving = hop(moving, lines[step])
         if step == 1:
             moving, w_flip = lax.optimization_barrier((moving, w_flip))
-    dy_other = [hop(part, swap) for part, swap in zip(dy_mine[:-1], dy_other[:-1])] + dy_other[-1:]
+        dy_mine.append(moving)
+        dy_other.append(hop(moving, swaps[step]))
 
     act = shape(experts, routes, hidden)
     act_spec = by_expert(routes, hidden)
     pick_spec = pl.BlockSpec((1, experts * cap, members), lambda i, *_: (at_group(i), 0, 0))
     pick_flops = 2 * total * experts * cap * width
     main_flops = 2 * experts * routes * width * hidden
-    up_after = dy_mine[-2:-1]
+    up_after = dy_other[:1]
     pick, meta, hid, scaled, slope_g = call(
         functools.partial(up_kernel, groups, width, top, cap, len(up_after)),
         "up",
@@ -327,8 +398,45 @@
         scratch_shapes=[pltpu.VMEM((experts, routes, width), bf16), pltpu.VMEM((experts, routes, LANES), f32)],
     )(place, x_all, w_up, *up_after)
 
-    last_block, hid = lax.optimization_barrier((dy_mine[-1], hid))
-    dy_other[-1] = hop(last_block, dy_other[-1])
+    moving, hid = lax.optimization_barrier((moving, hid))
+    moving = hop(moving, lines[-1])
+    slot_spec = pl.BlockSpec((1, experts * cap, members), lambda i, place: (at_slot(i, place), 0, 0))
+    back, kept = call(
+        functools.partial(early_kernel, groups, cap),
+        "early",
+        groups + experts,
+        8 * main_flops,
+        4 * row_bytes,
+        prefetch=1,
+        in_specs=[slot_spec] + [ANY] * (2 * groups - 3) + [by_expert(width, hidden)],
+        out_specs=[act_spec, ANY],
+        out_shape=[shape(experts, routes, hidden, dtype=f32), shape(experts, routes, width)],
+        scratch_shapes=[
+            pltpu.VMEM((experts, routes, width), bf16),
+            pltpu.VMEM((groups, members, width), bf16),
+            pltpu.SemaphoreType.DMA((groups, 2)),
+            pltpu.SemaphoreType.DMA((experts,)),
+        ],
+    )(place, pick, dy_own, *dy_mine, *dy_other, w_down)
+    last_mine, kept = lax.optimization_barrier((moving, kept))
+    last_other = hop(last_mine, swaps[-1])
+    kept, late = pl.pallas_call(
+        functools.partial(fill_kernel, groups, cap),
+        in_specs=[SMEM] + [ANY] * 4,
+        out_specs=[ANY, pl.BlockSpec(memory_space=pltpu.VMEM)],
+        out_shape=[shape(experts, routes, width), shape(experts, cap, width)],
+        input_output_aliases={4: 0},
+        scratch_shapes=[
+            pltpu.VMEM((members, width), bf16),
+            pltpu.VMEM((experts * cap, members), bf16),
+            pltpu.SemaphoreType.DMA((2,)),
+            pltpu.SemaphoreType.DMA,
+            pltpu.SemaphoreType.DMA((experts,)),
+        ],
+        compiler_params=pltpu.CompilerParams(vmem_limit_bytes=VMEM_LIMIT),
+        cost_estimate=cost(pick_flops // groups, 2 * total * width),
+        name="fill",
+    )(place, pick, last_mine, last_other, kept)
 
     orders = []
     for g in range(turns):
@@ -337,12 +445,27 @@
             tuple(sum(((p >> (bits - 1 - t)) & 1) << turn[t] for t in range(bits)) for p in range(dp_count))
         )
     orders = tuple(orders)
-    cut_rows = piece // turns
-    down_outs = [shape(dp_count // 2, experts, cut_rows, hidden)] * (2 * turns)
-    down_scratch = [
-        pltpu.VMEM((turns, dp_count, experts, cut_rows, hidden), bf16),
-        pltpu.SemaphoreType.DMA((turns, dp_count, experts)),
-    ]
+    cut_rows = share // turns
+
+    def down(start, count, after):
+        outs = call(
+            functools.partial(down_kernel, orders, len(after)),
+            "down",
+            count,
+            (400 if after else 1) * main_flops,
+            row_bytes,
+            in_specs=[SMEM]
+            + [pl.BlockSpec((1, routes, n), lambda b: (b + start, 0, 0)) for n in (width, hidden)]
+            + [ANY] * len(after),
+            out_specs=[ANY] * (2 * turns),
+            out_shape=[shape(dp_count // 2, count, cut_rows, hidden)] * (2 * turns),
+            scratch_shapes=[
+                pltpu.VMEM((turns, dp_count, count, cut_rows, hidden), bf16),
+                pltpu.SemaphoreType.DMA((turns, dp_count, count)),
+            ],
+        )(place, kept, scaled, *after)
+        return [(outs[2 * g], outs[2 * g + 1]) for g in range(turns)]
+
     def exchange(state, t):
         new = []
         for g, (keep, send) in enumerate(state):
@@ -355,60 +478,65 @@
             new.append((both[:half], both[half:]) if half else both[0])
         return new
 
+    counts = [1, experts - 1] if experts > 1 else [experts]
+    states = [down(0, counts[0], [])]
+    ahead = [pair[0] for pair in states[0]][:1]
+    states[0] = exchange(states[0], 0)
+
     def at_end(i):
-        return jnp.clip(i - groups - experts, 0, groups - 1)
-
-    token_part, kept = call(
-        functools.partial(tail_kernel, groups, cap, width, top),
+        return jnp.clip(i - experts, 0, groups - 1)
+
+    def at_first(rows, n):
+        return pl.BlockSpec((1, rows, n), lambda i, *_: (jnp.minimum(i, experts - 1), 0, 0))
+
+    token_part = call(
+        functools.partial(tail_kernel, groups, cap, width, top, len(ahead)),
         "tail",
-        2 * groups + experts,
-        8 * main_flops,
+        groups + experts,
+        100 * main_flops,
         4 * row_bytes,
         prefetch=1,
         in_specs=[
-            pl.BlockSpec(
-                (1, experts * cap, members),
-                lambda i, place: (jnp.where(i < groups, at_slot(i, place), at_end(i)), 0, 0),
-            ),
+            pl.BlockSpec((1, experts * cap, members), lambda i, *_: (at_end(i), 0, 0)),
+            at_first(cap, width),
+            at_first(routes, hidden),
+            at_first(width, hidden),
+            at_first(hidden, width),
+            at_first(routes, hidden),
+            at_first(routes, hidden),
+            pl.BlockSpec((members, LANES), lambda i, *_: (at_end(i), 0)),
         ]
-        + [ANY] * (2 * groups - 1)
-        + [
-            by_expert(width, hidden),
-            by_expert(hidden, width),
-            act_spec,
-            act_spec,
-            pl.BlockSpec((members, LANES), lambda i, *_: (at_end(i), 0)),
+        + [ANY] * len(ahead),
+        out_specs=pl.BlockSpec((members, full), lambda i, *_: (at_end(i), 0)),
+        out_shape=shape(total, full),
+        scratch_shapes=[
+            pltpu.VMEM((routes, hidden), f32),
+            pltpu.VMEM((groups, experts * cap, full), bf16),
         ],
-        out_specs=[pl.BlockSpec((members, full), lambda i, *_: (at_end(i), 0)), ANY],
-        out_shape=[shape(total, full), shape(experts, routes, width)],
-        scratch_shapes=[
-            pltpu.VMEM((experts, routes, width), bf16),
-            pltpu.VMEM((groups, members, width), bf16),
-            pltpu.SemaphoreType.DMA((groups, 2)),
-            pltpu.VMEM((groups, experts * cap, full), bf16),
-            pltpu.SemaphoreType.DMA((experts,)),
-        ],
-    )(place, pick, dy_own, *dy_mine, *dy_other, w_down, w_flip, hid, slope_g, meta)
+    )(place, pick, late, back, w_down, w_flip, hid, slope_g, meta, *ahead)
     summed = lax.psum_scatter(token_part, "ep", scatter_dimension=0, tiled=True)
 
-    states = []
-    for s in range(slices):
-        outs = call(
-            functools.partial(down_kernel, orders, s, slices, 0),
-            "down",
-            experts,
-            16 * main_flops,
-            8 * row_bytes,
-            in_specs=[SMEM] + [pl.BlockSpec((1, routes, n), lambda b: (b, 0, 0)) for n in (width, hidden)],
-            out_specs=[ANY] * len(down_outs),
-            out_shape=down_outs,
-            scratch_shapes=down_scratch,
-        )(place, kept, scaled)
-        states.append([(outs[2 * g], outs[2 * g + 1]) for g in range(turns)])
+    done = [1]
+    if len(counts) > 1:
+        sums = [pair[0] if isinstance(pair, tuple) else pair for pair in states[0]]
+        states.append(down(counts[0], counts[1], sums))
+        done.append(0)
     for t in range(bits):
-        states = [exchange(state, t) for state in states]
-    down_grad = jnp.concatenate([part for state in states for part in state], axis=1)
-    return (summed[:, :width], summed[:, width : width + top], down_grad)
+        states = [state if t < first else exchange(state, t) for state, first in zip(states, done)]
+    down_grad = jnp.zeros((experts, share, hidden), f32)
+    start = 0
+    for count, state in zip(counts, states):
+        for g, part in enumerate(state):
+            down_grad = lax.dynamic_update_slice(down_grad, part, (start, g * cut_rows, 0))
+        start += count
+    token_grad, gate_grad = pl.pallas_call(
+        functools.partial(finish_kernel, width, top),
+        out_shape=[shape(tok_rows, width), shape(top, tok_rows)],
+        compiler_params=pltpu.CompilerParams(vmem_limit_bytes=VMEM_LIMIT),
+        cost_estimate=cost(0, 4 * tok_rows * width),
+        name="finish",
+    )(summed)
+    return (token_grad, gate_grad.T, down_grad)
 
 
 def solution(mesh):

time: 193 us -> 212 us (1.098)
  Pallas kernels: 53 us -> 65.4 us
  waiting for transfers between devices: 93.1 us -> 99.2 us
    pallas_call x3 -> x6, Pallas kernels: 32.5 us -> 45.1 us  [the longest x1 14.7 us: shards(): call(functools.partial(tail_kernel, groups, cap, width, top, len(ahead)),...]
    ppermute x7, waiting for transfers between devices: 36.4 us -> 42.5 us  [hop(): return lax.ppermute(value, 'ep', pairs)]
    ppermute x8, waiting for transfers between devices: 36.5 us -> 41.4 us  [exchange(): got = lax.ppermute(send, 'dp', [(i, i ^ bit) for i in range(dp_count)])]
    all_gather x1, waiting for transfers between devices: 20.2 us -> 15.3 us  [shards(): x_all = lax.all_gather(x_own, 'ep', axis=0, tiled=True)]
    slice x2 -> x0, local copies, waits for them, and re-layouts: 2.64 us -> none  [shards(): return (summed[:, :width], summed[:, width:width + top], down_grad)]
    convert_element_type x4, other arithmetic: 0.78 us -> 3.22 us  [exchange(): both = both.astype(bf16)]
    unnamed x20 -> x35, local copies, waits for them, and re-layouts: 2.76 us -> 4.34 us
  transfers between devices with their start and end apart: 17 -> 17, of which waited for: 9 -> 8; matrix products, arithmetic and copies ran while one was open for 3% -> 3% of each run, Pallas kernels for 16% -> 25%
where the time goes in v8:
time: 212 us; the launch traced here: 210 us
  waiting for transfers between devices  99.2 us (47%)
  Pallas kernels  65.4 us (31%)
  starting transfers between devices  20.2 us (10%)
  between operations  14.4 us (7%)
  local copies, waits for them, and re-layouts  6.29 us (3%)
  other arithmetic  4.12 us (2%)
    ppermute x7, waiting for transfers between devices, hop(): return lax.ppermute(value, 'ep', pairs)  42.5 us
    ppermute x8, waiting for transfers between devices, exchange(): got = lax.ppermute(send, 'dp', [(i, i ^ bit) for i in range(dp_count)])  41.4 us
    all_gather x1, waiting for transfers between devices, shards(): x_all = lax.all_gather(x_own, 'ep', axis=0, tiled=True)  15.3 us
    pallas_call x1, Pallas kernels, shards(): call(functools.partial(tail_kernel, groups, cap, width, top, len(ahead)),...  14.7 us
    pallas_call x1, Pallas kernels, shards(): call(functools.partial(early_kernel, groups, cap), 'early', groups + expe...  12.7 us
    pallas_call x1, Pallas kernels, shards(): call(functools.partial(up_kernel, groups, width, top, cap, len(up_after))...  11.6 us
    ppermute x7, starting transfers between devices, hop(): return lax.ppermute(value, 'ep', pairs)  10.8 us
    pallas_call x2, Pallas kernels, down(): call(functools.partial(down_kernel, orders, len(after)), 'down', count, (...  10.7 us
  transfers between devices with their start and end apart: 17, of which 8 were waited for; matrix products, arithmetic and copies ran while one was open for 3% of the time, Pallas kernels for 25%

profile of v8, /device:TPU:0, one launch (start us, length us, event | category | flops | bytes accessed | tf_op | source)
XLA Modules:
  0.0 209.5 jit_solution(2678343428493946783)
XLA Ops:
  7.2 2.0 pack.1
  9.3 0.5 collective-permute-start
  9.9 1.7 collective-permute-done
  11.6 4.9 %collective-permute-start.1 = (bf16[256,2048]{1,0:T(8,128)(2,1)S(1)}, bf16[256,2048]{1,0:T(8,128)(2,1)S(1)}, u32[]{:S(2)}, u32[]{:S(2)}) collective-permute-start(bf16[256,2048]{1,0:T(8,128)(2,1)S(1)} %constant_dynamic-update-slice_fusion.refs_0_), channel_id=1, source_target_pairs={{0,2},{2,4},{3,1},{4,6},{5,3},{7,5},{8,10},{10,12},{11,9},{12,14},... | collective-permute-start | bytes 3145736 | tf_op jit(solution)/shard_map/ppermute | solution.py:322
  16.6 6.7 %flip.1.w_flip = bf16[4,384,2048]{2,1,0:T(8,128)(2,1)} custom-call(bf16[4,2048,384]{2,1,0:T(8,128)(2,1)} %w_up.1), custom_call_target="tpu_custom_call" | custom-call | bytes 12582912 | tf_op jit(solution)/shard_map/flip/pallas_call | solution.py:356
  23.3 20.5 %collective-permute-done.1.refs_1_ = bf16[256,2048]{1,0:T(8,128)(2,1)S(1)} collective-permute-done((bf16[256,2048]{1,0:T(8,128)(2,1)S(1)}, bf16[256,2048]{1,0:T(8,128)(2,1)S(1)}, u32[]{:S(2)}, u32[]{:S(2)}) %collective-permute-start.1) | collective-permute-done | bytes 1048608 | tf_op jit(solution)/shard_map/ppermute | solution.py:322
  43.8 0.7 collective-permute-start.3
  44.5 1.3 collective-permute-start.2
  45.8 1.3 collective-permute-start.5
  47.1 0.6 pad_add_fusion.place
  47.7 6.7 %collective-permute-done.2.refs_0_.refs_3_ = bf16[256,2048]{1,0:T(8,128)(2,1)} collective-permute-done((bf16[256,2048]{1,0:T(8,128)(2,1)S(1)}, bf16[256,2048]{1,0:T(8,128)(2,1)}, u32[]{:S(2)}, u32[]{:S(2)}) %collective-permute-start.2) | collective-permute-done | bytes 1048608 | tf_op jit(solution)/shard_map/ppermute | solution.py:322
  54.4 15.3 %all-gather.2.cloned.1.call-done.rows = bf16[1024,2176]{1,0:T(8,128)(2,1)} async-done(((bf16[128,2176]{1,0:T(8,128)(2,1)}), bf16[1024,2176]{1,0:T(8,128)(2,1)}) %all-gather.2.cloned.1.call-update) | async-done | bytes 4456464 | tf_op jit(solution)/shard_map/all_gather | solution.py:315
  69.7 11.6 %up.1 = (bf16[4,320,256]{2,1,0:T(8,128)(2,1)}, bf16[1024,128]{1,0:T(8,128)(2,1)}, bf16[4,320,384]{2,1,0:T(8,128)(2,1)}, bf16[4,320,384]{2,1,0:T(8,128)(2,1)}, bf16[4,320,384]{2,1,0:T(8,128)(2,1)}) custom-call(s32[4]{0:T(128)} %pad_add_fusion.place, bf16[1024,2176]{1,0:T(8,128)(2,1)} %all-gather.2.cloned.1.call-done.rows, bf16[4,2048,384]{2,1,0:T(8,128)(2,1)} %w_up.1, ...), custom_call_target="tpu_custom_call" | custom-call | flops 3355443200 | bytes 10747904 | tf_op jit(solution)/shard_map/up/pallas_call | solution.py:389
  81.3 0.7 collective-permute-start.4
  82.0 12.7 %early.1 = (f32[4,320,384]{2,1,0:T(8,128)}, bf16[4,320,2048]{2,1,0:T(8,128)(2,1)}) custom-call(s32[4]{0:T(128)} %pad_add_fusion.place, bf16[4,320,256]{2,1,0:T(8,128)(2,1)} %get-tuple-element.29.pick, bf16[256,2048]{1,0:T(8,128)(2,1)} %copy-done.11, bf16[256,2048]{1,0:T(8,128)(2,1)} %copy-done.14, bf16[256,2048]{1,0:T(8,128)(2,1)} %copy-done.15, ...), custom_call_target="tpu_custom_call" | custom-call | flops 16106127360 | bytes 25165824 | tf_op jit(solution)/shard_map/early/pallas_call | solution.py:404
  94.8 1.3 collective-permute-start.6
  96.1 13.6 %collective-permute-done.6.other = bf16[256,2048]{1,0:T(8,128)(2,1)S(1)} collective-permute-done((bf16[256,2048]{1,0:T(8,128)(2,1)S(1)}, bf16[256,2048]{1,0:T(8,128)(2,1)S(1)}, u32[]{:S(2)}, u32[]{:S(2)}) %collective-permute-start.6) | collective-permute-done | bytes 1048608 | tf_op jit(solution)/shard_map/ppermute | solution.py:322
  109.6 1.0 copy-done.7
  110.6 4.6 %fill.1 = (bf16[4,320,2048]{2,1,0:T(8,128)(2,1)}, bf16[4,80,2048]{2,1,0:T(8,128)(2,1)}) custom-call(s32[4]{0:T(128)} %pad_add_fusion.place, bf16[4,320,256]{2,1,0:T(8,128)(2,1)} %get-tuple-element.29.pick, bf16[256,2048]{1,0:T(8,128)(2,1)} %copy-done.6, bf16[256,2048]{1,0:T(8,128)(2,1)} %copy-done.7, ...), custom_call_target="tpu_custom_call", output_to_operand_aliasing={{0}: (4, {})} | custom-call | flops 335544320 | bytes 4194304 | tf_op jit(solution)/shard_map/fill/pallas_call | solution.py:423
  115.2 3.7 %down.2 = (bf16[2,1,256,384]{3,2,1,0:T(8,128)(2,1)}, bf16[2,1,256,384]{3,2,1,0:T(8,128)(2,1)}, bf16[2,1,256,384]{3,2,1,0:T(8,128)(2,1)}, bf16[2,1,256,384]{3,2,1,0:T(8,128)(2,1)}) custom-call(s32[4]{0:T(128)} %pad_add_fusion.place, bf16[4,320,2048]{2,1,0:T(8,128)(2,1)} %get-tuple-element.41.rows, bf16[4,320,384]{2,1,0:T(8,128)(2,1)} %get-tuple-element.42.scaled), custom_call_target="tpu_custom_call" | custom-call | flops 2013265920 | bytes 6291456 | tf_op jit(solution)/shard_map/down/pallas_call | solution.py:451
  119.0 1.5 collective-permute-start.7
  120.5 14.7 %tail.1 = bf16[1024,2176]{1,0:T(8,128)(2,1)} custom-call(s32[4]{0:T(128)} %pad_add_fusion.place, bf16[4,320,256]{2,1,0:T(8,128)(2,1)} %get-tuple-element.29.pick, bf16[4,80,2048]{2,1,0:T(8,128)(2,1)} %get-tuple-element.35.late, f32[4,320,384]{2,1,0:T(8,128)} %get-tuple-element.36.early, bf16[4,2048,384]{2,1,0:T(8,128)(2,1)} %w_down.1, ...), custom_call_target="tpu_custom_call" | custom-call | flops 201326592000 | bytes 25165824 | tf_op jit(solution)/shard_map/tail/pallas_call | solution.py:492
  135.3 1.0 copy-done.16
  136.3 1.5 collective-permute-start.9
  137.8 1.1 add_convert_fusion.3
  138.9 0.7 copy-done.1
  139.6 0.8 fusion.1
  140.4 6.7 %collective-permute-done.9 = bf16[2,1,256,384]{3,2,1,0:T(8,128)(2,1)S(1)} collective-permute-done((bf16[2,1,256,384]{3,2,1,0:T(8,128)(2,1)S(1)}, bf16[2,1,256,384]{3,2,1,0:T(8,128)(2,1)S(1)}, u32[]{:S(2)}, u32[]{:S(2)}) %collective-permute-start.9) | collective-permute-done | bytes 393248 | tf_op jit(solution)/shard_map/ppermute | solution.py:473
  147.1 0.1 add_convert_fusion.2
  147.3 0.7 copy-done.3
  148.0 0.8 fusion
  148.8 7.0 %down.3 = (bf16[2,3,256,384]{3,2,1,0:T(8,128)(2,1)}, bf16[2,3,256,384]{3,2,1,0:T(8,128)(2,1)}, bf16[2,3,256,384]{3,2,1,0:T(8,128)(2,1)}, bf16[2,3,256,384]{3,2,1,0:T(8,128)(2,1)}) custom-call(s32[4]{0:T(128)} %pad_add_fusion.place, bf16[4,320,2048]{2,1,0:T(8,128)(2,1)} %get-tuple-element.41.rows, bf16[4,320,384]{2,1,0:T(8,128)(2,1)} %get-tuple-element.42.scaled, ...), custom_call_target="tpu_custom_call" | custom-call | flops 805306368000 | bytes 6291456 | tf_op jit(solution)/shard_map/down/pallas_call | solution.py:451
  155.8 0.6 collective-permute-start.11
  156.4 1.5 collective-permute-start.13
  157.9 0.5 collective-permute-start.8
  158.5 1.5 collective-permute-start.10
  159.9 25.1 %collective-permute-done.11 = bf16[2,3,256,384]{3,2,1,0:T(8,128)(2,1)S(1)} collective-permute-done((bf16[2,3,256,384]{3,2,1,0:T(8,128)(2,1)}, bf16[2,3,256,384]{3,2,1,0:T(8,128)(2,1)S(1)}, u32[]{:S(2)}, u32[]{:S(2)}) %collective-permute-start.11) | collective-permute-done | bytes 1179680 | tf_op jit(solution)/shard_map/ppermute | solution.py:473
  185.0 1.7 add_convert_fusion.1
  186.8 1.6 collective-permute-start.12
  188.4 0.3 add_convert_fusion
  188.8 0.6 collective-permute-start.14
  189.3 0.1 copy-done.2
  189.5 0.2 dynamic_update_slice.12
  189.7 0.8 copy-done.4
  190.5 9.6 %collective-permute-done.12 = bf16[1,3,256,384]{3,2,1,0:T(8,128)(2,1)S(1)} collective-permute-done((bf16[1,3,256,384]{3,2,1,0:T(8,128)(2,1)S(1)}, bf16[1,3,256,384]{3,2,1,0:T(8,128)(2,1)S(1)}, u32[]{:S(2)}, u32[]{:S(2)}) %collective-permute-start.12) | collective-permute-done | bytes 589856 | tf_op jit(solution)/shard_map/ppermute | solution.py:473
  200.1 0.1 bitcast_dynamic-update-slice_fusion.1
  200.2 0.1 bitcast_dynamic-update-slice_fusion
  200.4 2.3 %finish.1 = (bf16[128,2048]{1,0:T(8,128)(2,1)}, bf16[8,128]{1,0:T(8,128)(2,1)}) custom-call(bf16[128,2176]{1,0:T(8,128)(2,1)} %reduce-scatter.2.cloned.1.call-done.rows), custom_call_target="tpu_custom_call" | custom-call | bytes 1048576 | tf_op jit(solution)/shard_map/finish/pallas_call | solution.py:532
  (47 shorter events, 0.5 us)
Async XLA Ops:
  7.2 2.7 %copy-start.8 = (bf16[128,2048]{1,0:T(8,128)(2,1)S(1)}, bf16[128,2048]{1,0:T(8,128)(2,1)}, u32[]{:S(2)}) copy-start(bf16[128,2048]{1,0:T(8,128)(2,1)} %param.7) | copy-start | bytes 1572868
  7.2 62.5 %all-gather.2.cloned.1.call-start = ((), (), s32[]{:S(2)}) async-start(), calls=%async_computation.1 | async-start | bytes 5013504 | tf_op jit(solution)/shard_map/all_gather | solution.py:315
  9.3 191.1 %reduce-scatter.2.cloned.1.call-start = ((), (), s32[]{:S(2)}) async-start(), calls=%async_computation.2 | async-start | bytes 5013504 | tf_op jit(solution)/shard_map/reduce_scatter | solution.py:517
  9.3 2.3 %collective-permute-start = (bf16[128,2048]{1,0:T(8,128)(2,1)}, bf16[128,2048]{1,0:T(8,128)(2,1)S(1)}, u32[]{:S(2)}, u32[]{:S(2)}) collective-permute-start(bf16[128,2048]{1,0:T(8,128)(2,1)} %param.7), channel_id=1, source_target_pairs={{0,1},{1,0},{2,3},{3,2},{4,5},{5,4},{6,7},{7,6},{8,9},{9,8},{10,11... | collective-permute-start | bytes 1572872 | tf_op jit(solution)/shard_map/ppermute | solution.py:322
  11.6 11.7 %copy-start.11 = (bf16[256,2048]{1,0:T(8,128)(2,1)}, bf16[256,2048]{1,0:T(8,128)(2,1)S(1)}, u32[]{:S(2)}) copy-start(bf16[256,2048]{1,0:T(8,128)(2,1)S(1)} %constant_dynamic-update-slice_fusion.refs_0_) | copy-start | bytes 3145732
  11.6 32.1 %collective-permute-start.1 = (bf16[256,2048]{1,0:T(8,128)(2,1)S(1)}, bf16[256,2048]{1,0:T(8,128)(2,1)S(1)}, u32[]{:S(2)}, u32[]{:S(2)}) collective-permute-start(bf16[256,2048]{1,0:T(8,128)(2,1)S(1)} %constant_dynamic-update-slice_fusion.refs_0_), channel_id=1, source_target_pairs={{0,2},{2,4},{3,1},{4,6},{5,3},{7,5},{8,10},{10,12},{11,9},{12,14},... | collective-permute-start | bytes 3145736 | tf_op jit(solution)/shard_map/ppermute | solution.py:322
  43.8 37.5 %copy-start.14 = (bf16[256,2048]{1,0:T(8,128)(2,1)}, bf16[256,2048]{1,0:T(8,128)(2,1)S(1)}, u32[]{:S(2)}) copy-start(bf16[256,2048]{1,0:T(8,128)(2,1)S(1)} %collective-permute-done.1.refs_1_) | copy-start | bytes 3145732
  43.8 2.0 collective-permute-start.3
  44.5 9.9 %collective-permute-start.2 = (bf16[256,2048]{1,0:T(8,128)(2,1)S(1)}, bf16[256,2048]{1,0:T(8,128)(2,1)}, u32[]{:S(2)}, u32[]{:S(2)}) collective-permute-start(bf16[256,2048]{1,0:T(8,128)(2,1)S(1)} %collective-permute-done.1.refs_1_), channel_id=1, source_target_pairs={{1,0},{2,3},{3,2},{4,5},{5,4},{6,7},{9,8},{10,11},{11,10},{12,13},... | collective-permute-start | bytes 3145736 | tf_op jit(solution)/shard_map/ppermute | solution.py:322
  45.8 35.5 %copy-start.15 = (bf16[256,2048]{1,0:T(8,128)(2,1)}, bf16[256,2048]{1,0:T(8,128)(2,1)S(1)}, u32[]{:S(2)}) copy-start(bf16[256,2048]{1,0:T(8,128)(2,1)S(1)} %collective-permute-done.3.refs_2_) | copy-start | bytes 3145732
  45.8 36.2 %collective-permute-start.5 = (bf16[256,2048]{1,0:T(8,128)(2,1)S(1)}, bf16[256,2048]{1,0:T(8,128)(2,1)}, u32[]{:S(2)}, u32[]{:S(2)}) collective-permute-start(bf16[256,2048]{1,0:T(8,128)(2,1)S(1)} %collective-permute-done.3.refs_2_), channel_id=1, source_target_pairs={{1,0},{3,2},{4,5},{6,7},{9,8},{11,10},{12,13},{14,15},{17,16},{19,... | collective-permute-start | bytes 3145736 | tf_op jit(solution)/shard_map/ppermute | solution.py:322
  81.3 13.5 %collective-permute-start.4 = (bf16[256,2048]{1,0:T(8,128)(2,1)S(1)}, bf16[256,2048]{1,0:T(8,128)(2,1)S(1)}, u32[]{:S(2)}, u32[]{:S(2)}) collective-permute-start(bf16[256,2048]{1,0:T(8,128)(2,1)S(1)} %collective-permute-done.3.refs_2_), channel_id=1, source_target_pairs={{3,1},{4,6},{11,9},{12,14},{19,17},{20,22},{27,25},{28,30}} | collective-permute-start | bytes 3145736 | tf_op jit(solution)/shard_map/ppermute | solution.py:322
  94.8 14.9 %copy-start.6 = (bf16[256,2048]{1,0:T(8,128)(2,1)}, bf16[256,2048]{1,0:T(8,128)(2,1)S(1)}, u32[]{:S(2)}) copy-start(bf16[256,2048]{1,0:T(8,128)(2,1)S(1)} %collective-permute-done.4.mine) | copy-start | bytes 3145732
  94.8 14.9 %collective-permute-start.6 = (bf16[256,2048]{1,0:T(8,128)(2,1)S(1)}, bf16[256,2048]{1,0:T(8,128)(2,1)S(1)}, u32[]{:S(2)}, u32[]{:S(2)}) collective-permute-start(bf16[256,2048]{1,0:T(8,128)(2,1)S(1)} %collective-permute-done.4.mine), channel_id=1, source_target_pairs={{1,0},{6,7},{9,8},{14,15},{17,16},{22,23},{25,24},{30,31}} | collective-permute-start | bytes 3145736 | tf_op jit(solution)/shard_map/ppermute | solution.py:322
  109.6 1.0 copy-start.7
  119.0 18.8 %collective-permute-start.7 = (bf16[2,1,256,384]{3,2,1,0:T(8,128)(2,1)}, bf16[2,1,256,384]{3,2,1,0:T(8,128)(2,1)}, u32[]{:S(2)}, u32[]{:S(2)}) collective-permute-start(bf16[2,1,256,384]{3,2,1,0:T(8,128)(2,1)} %get-tuple-element.46), channel_id=1, source_target_pairs={{0,8},{8,0},{16,24},{24,16},{1,9},{9,1},{17,25},{25,17},{2,10},{10... | collective-permute-start | bytes 1179656 | tf_op jit(solution)/shard_map/ppermute | solution.py:473
  135.3 1.0 copy-start.16
  135.3 2.5 %copy-start.10 = (bf16[2,1,256,384]{3,2,1,0:T(8,128)(2,1)S(1)}, bf16[2,1,256,384]{3,2,1,0:T(8,128)(2,1)}, u32[]{:S(2)}) copy-start(bf16[2,1,256,384]{3,2,1,0:T(8,128)(2,1)} %get-tuple-element.43.refs_0_) | copy-start | bytes 1179652
  135.3 11.9 %copy-start.9 = (bf16[2,1,256,384]{3,2,1,0:T(8,128)(2,1)S(1)}, bf16[2,1,256,384]{3,2,1,0:T(8,128)(2,1)}, u32[]{:S(2)}) copy-start(bf16[2,1,256,384]{3,2,1,0:T(8,128)(2,1)} %get-tuple-element.47) | copy-start | bytes 1179652
  136.3 10.9 %collective-permute-start.9 = (bf16[2,1,256,384]{3,2,1,0:T(8,128)(2,1)S(1)}, bf16[2,1,256,384]{3,2,1,0:T(8,128)(2,1)S(1)}, u32[]{:S(2)}, u32[]{:S(2)}) collective-permute-start(bf16[2,1,256,384]{3,2,1,0:T(8,128)(2,1)S(1)} %copy-done.16), channel_id=1, source_target_pairs={{0,16},{8,24},{16,0},{24,8},{1,17},{9,25},{17,1},{25,9},{2,18},{10... | collective-permute-start | bytes 1179656 | tf_op jit(solution)/shard_map/ppermute | solution.py:473
  138.9 0.7 copy-start.1
  147.2 0.8 copy-start.3
  148.8 9.1 %copy-start.12 = (bf16[1,1,256,384]{3,2,1,0:T(8,128)(2,1)S(1)}, bf16[1,1,256,384]{3,2,1,0:T(8,128)(2,1)}, u32[]{:S(2)}) copy-start(bf16[1,1,256,384]{3,2,1,0:T(8,128)(2,1)} %get-tuple-element.56) | copy-start | bytes 589828
  148.8 9.7 %copy-start.13 = (bf16[1,1,256,384]{3,2,1,0:T(8,128)(2,1)S(1)}, bf16[1,1,256,384]{3,2,1,0:T(8,128)(2,1)}, u32[]{:S(2)}) copy-start(bf16[1,1,256,384]{3,2,1,0:T(8,128)(2,1)} %get-tuple-element.54) | copy-start | bytes 589828
  155.8 29.2 %collective-permute-start.11 = (bf16[2,3,256,384]{3,2,1,0:T(8,128)(2,1)}, bf16[2,3,256,384]{3,2,1,0:T(8,128)(2,1)S(1)}, u32[]{:S(2)}, u32[]{:S(2)}) collective-permute-start(bf16[2,3,256,384]{3,2,1,0:T(8,128)(2,1)} %get-tuple-element.50), channel_id=1, source_target_pairs={{0,8},{8,0},{16,24},{24,16},{1,9},{9,1},{17,25},{25,17},{2,10},{10... | collective-permute-start | bytes 3538952 | tf_op jit(solution)/shard_map/ppermute | solution.py:473
  156.4 32.0 %collective-permute-start.13 = (bf16[2,3,256,384]{3,2,1,0:T(8,128)(2,1)}, bf16[2,3,256,384]{3,2,1,0:T(8,128)(2,1)S(1)}, u32[]{:S(2)}, u32[]{:S(2)}) collective-permute-start(bf16[2,3,256,384]{3,2,1,0:T(8,128)(2,1)} %get-tuple-element.52), channel_id=1, source_target_pairs={{0,16},{8,24},{16,0},{24,8},{1,17},{9,25},{17,1},{25,9},{2,18},{10... | collective-permute-start | bytes 3538952 | tf_op jit(solution)/shard_map/ppermute | solution.py:473
  157.9 31.4 %collective-permute-start.8 = (bf16[1,1,256,384]{3,2,1,0:T(8,128)(2,1)S(1)}, bf16[1,1,256,384]{3,2,1,0:T(8,128)(2,1)S(1)}, u32[]{:S(2)}, u32[]{:S(2)}) collective-permute-start(bf16[1,1,256,384]{3,2,1,0:T(8,128)(2,1)S(1)} %copy-done.12), channel_id=1, source_target_pairs={{0,16},{8,24},{16,0},{24,8},{1,17},{9,25},{17,1},{25,9},{2,18},{10... | collective-permute-start | bytes 589832 | tf_op jit(solution)/shard_map/ppermute | solution.py:473
  158.5 31.2 %collective-permute-start.10 = (bf16[1,1,256,384]{3,2,1,0:T(8,128)(2,1)S(1)}, bf16[1,1,256,384]{3,2,1,0:T(8,128)(2,1)S(1)}, u32[]{:S(2)}, u32[]{:S(2)}) collective-permute-start(bf16[1,1,256,384]{3,2,1,0:T(8,128)(2,1)S(1)} %copy-done.13), channel_id=1, source_target_pairs={{0,8},{8,0},{16,24},{24,16},{1,9},{9,1},{17,25},{25,17},{2,10},{10... | collective-permute-start | bytes 589832 | tf_op jit(solution)/shard_map/ppermute | solution.py:473
  185.0 3.4 %copy-start.5 = (bf16[2,3,256,384]{3,2,1,0:T(8,128)(2,1)S(1)}, bf16[2,3,256,384]{3,2,1,0:T(8,128)(2,1)}, u32[]{:S(2)}) copy-start(bf16[2,3,256,384]{3,2,1,0:T(8,128)(2,1)} %get-tuple-element.51) | copy-start | bytes 3538948
  186.8 13.3 %collective-permute-start.12 = (bf16[1,3,256,384]{3,2,1,0:T(8,128)(2,1)S(1)}, bf16[1,3,256,384]{3,2,1,0:T(8,128)(2,1)S(1)}, u32[]{:S(2)}, u32[]{:S(2)}) collective-permute-start(bf16[1,3,256,384]{3,2,1,0:T(8,128)(2,1)S(1)} %slice.37), channel_id=1, source_target_pairs={{0,16},{8,24},{16,0},{24,8},{1,17},{9,25},{17,1},{25,9},{2,18},{10... | collective-permute-start | bytes 1769480 | tf_op jit(solution)/shard_map/ppermute | solution.py:473
  188.4 1.0 copy-start.2
  188.8 11.4 %collective-permute-start.14 = (bf16[1,3,256,384]{3,2,1,0:T(8,128)(2,1)S(1)}, bf16[1,3,256,384]{3,2,1,0:T(8,128)(2,1)S(1)}, u32[]{:S(2)}, u32[]{:S(2)}) collective-permute-start(bf16[1,3,256,384]{3,2,1,0:T(8,128)(2,1)S(1)} %slice.39), channel_id=1, source_target_pairs={{0,8},{8,0},{16,24},{24,16},{1,9},{9,1},{17,25},{25,17},{2,10},{10... | collective-permute-start | bytes 1769480 | tf_op jit(solution)/shard_map/ppermute | solution.py:473
  189.4 1.0 copy-start.4
  200.4 2.3 %copy-start = (f32[4,512,384]{2,1,0:T(8,128)}, f32[4,512,384]{2,1,0:T(8,128)S(1)}, u32[]{:S(2)}) copy-start(f32[4,512,384]{2,1,0:T(8,128)S(1)} %bitcast_dynamic-update-slice_fusion) | copy-start | bytes 9437188
Sparse Core Ops, SparseCore 0:
  10.2 59.4 all-gather.1
  135.4 54.8 reduce-scatter.1

commit v9 on v1

v9 whole, which is shorter than its diff:
```python
import functools

import jax
import jax.numpy as jnp
from jax import lax
from jax.experimental import pallas as pl
from jax.experimental.pallas import tpu as pltpu
from jax.sharding import PartitionSpec as P

LANES = 128
PACK = 16
GROUP = 2
VMEM_LIMIT = 60 * 1024 * 1024
bf16, f32 = jnp.bfloat16, jnp.float32
ANY = pl.BlockSpec(memory_space=pl.ANY)
SMEM = pl.BlockSpec(memory_space=pltpu.SMEM)
FIRST = (((0,), (0,)), ((), ()))


def dot(a, b, dims=(((1,), (0,)), ((), ()))):
    return lax.dot_general(a, b, dims, preferred_element_type=f32)


def pack_kernel(top, tokens, ids, gates, x_out):
    count, width = tokens.shape
    x_out[:, pl.ds(0, width)] = tokens[...]
    info = jnp.concatenate(
        [ids[...].astype(f32), gates[...].astype(f32), jnp.zeros((LANES - 2 * top, count), f32)], axis=0
    )
    x_out[:, pl.ds(width, LANES)] = info.T.astype(bf16)


def flip_kernel(w, out):
    out[0] = w[0].T


def block_copies(place, ref, dst, sem, flip):
    half = ref.shape[0] // 2
    copies = []
    for part in range(2):
        to = (part ^ flip) * half
        if not isinstance(flip, int):
            to = pl.multiple_of(to, half)
        copies.append(
            pltpu.make_async_copy(ref.at[pl.ds(part * half, half), :], dst.at[pl.ds(to, half), :], sem.at[part])
        )
    return copies


def by_side(place, is_left, mine, other, act):
    for left in (True, False):
        for core in (True, False):
            ref = (mine if left == core else other)(left)
            if ref is not None:

                @pl.when((is_left == left) & ((place[2] == 0) == core))
                def _():
                    act(ref, 0 if left else 1)


def start_blocks(place, chips, own, mine, other, dst, sem):
    for copy in block_copies(place, own, dst.at[0], sem.at[0], place[2]):
        copy.start()
    for slot in range(1, chips):

        def pick(blocks, left):
            step = slot if left else chips - slot
            return blocks[step - 1] if step <= len(blocks) else None

        def start(ref, flip):
            for copy in block_copies(place, ref, dst.at[slot], sem.at[slot], flip):
                copy.start()

        by_side(place, place[3] >= slot, functools.partial(pick, mine), functools.partial(pick, other), start)


def copy_all(pairs, sem):
    copies = [pltpu.make_async_copy(src, dst, sem.at[n]) for n, (src, dst) in enumerate(pairs)]
    for copy in copies:
        copy.start()
    return copies


def up_kernel(groups, width, top, cap, after, place, x_all, w_up, *refs):
    refs = refs[after:]
    pick_out, meta, hid_out, scaled_out, slope_out, rows, w_v, held, gates, pick, hid, scaled, slope, sems, out_sem = refs
    experts, members = held.shape[0], rows.shape[1]
    arrive = copy_all([(x_all.at[pl.ds(g * members, members), :], rows.at[g]) for g in range(groups)], sems.at[0])
    weights = copy_all([(w_up.at[b], w_v.at[b]) for b in range(experts)], sems.at[1])
    before = lax.broadcasted_iota(jnp.int32, (members, members), 0) < lax.broadcasted_iota(
        jnp.int32, (members, members), 1
    )
    before = before.astype(bf16)
    spot = lax.broadcasted_iota(jnp.int32, (cap, members), 0).astype(f32)
    for g in range(groups):
        arrive[g].wait()
        info = rows[g, :, pl.ds(width, LANES)]
        meta[pl.ds(g * members, members), :] = info
        across = info.astype(f32).T
        ids, parts = across[:top], across[top : 2 * top]
        chosen = [ids == (place[0] * experts + b).astype(f32) for b in range(experts)]
        member = [jnp.sum(jnp.where(hit, 1.0, 0.0), axis=0, keepdims=True) for hit in chosen]
        table = jnp.concatenate(member + [jnp.zeros((PACK - experts, members), f32)], axis=0)
        prior = dot(table.astype(bf16), before)
        for b in range(experts):
            rank = jnp.where(member[b] > 0.0, prior[b : b + 1], -1.0)
            one = jnp.where(spot == rank, 1.0, 0.0)
            gate = jnp.sum(jnp.where(chosen[b], parts, 0.0), axis=0, keepdims=True)
            pick[g, pl.ds(b * cap, cap), :] = one.astype(bf16)
            gates[b, pl.ds(g * cap, cap), :] = jnp.broadcast_to(
                jnp.sum(one * gate, axis=1, keepdims=True), (cap, LANES)
            )
        got = dot(pick[g], rows[g, :, pl.ds(0, width)]).astype(bf16)
        for b in range(experts):
            held[b, pl.ds(g * cap, cap), :] = got[b * cap : (b + 1) * cap]
    outs = copy_all([(pick, pick_out)], out_sem.at[3])
    for b in range(experts):
        weights[b].wait()
        pre = dot(held[b], w_v[b])
        gate = gates[b][:, :1]
        sig = 0.5 + 0.5 * jnp.tanh(0.5 * pre)
        act = pre * sig
        hid[b] = act.astype(bf16)
        scaled[b] = (gate * act).astype(bf16)
        slope[b] = (gate * (sig + act * (1.0 - sig))).astype(bf16)
        for n, (src, dst) in enumerate(((hid, hid_out), (scaled, scaled_out), (slope, slope_out))):
            copy = pltpu.make_async_copy(src.at[b], dst.at[b], out_sem.at[n, b])
            copy.start()
            outs.append(copy)
    for copy in outs:
        copy.wait()


def down_kernel(orders, start, place, kept, scaled_in, *refs):
    outs, (rows, scaled, sent, in_sem, sem) = refs[:-5], refs[-5:]
    experts = sent.shape[2]
    arrive = copy_all([(kept.at[start + b], rows.at[b]) for b in range(experts)], in_sem.at[0])
    others = copy_all([(scaled_in.at[start + b], scaled.at[b]) for b in range(experts)], in_sem.at[1])
    parts = len(orders[0])
    half = parts // 2
    share = rows.shape[2] // parts
    cut = share // len(orders)
    copies = []
    for b in range(experts):
        arrive[b].wait()
        others[b].wait()
        for q in range(parts):
            at = pl.multiple_of((place[1] ^ q) * share, LANES)
            full = dot(rows[b, :, pl.ds(at, share)], scaled[b], FIRST).astype(bf16)
            for g, order in enumerate(orders):
                sent[g, q, b] = full[g * cut : (g + 1) * cut]
                p = order.index(q)
                copy = pltpu.make_async_copy(
                    sent.at[g, q, b], outs[2 * g + p // half].at[p % half, b], sem.at[g, q, b]
                )
                copy.start()
                copies.append(copy)
    for copy in copies:
        copy.wait()


def tail_kernel(groups, cap, width, top, place, *refs):
    steps = groups - 1
    own, mine, other, refs = refs[0], refs[1 : 1 + steps], refs[1 + steps : 1 + 2 * steps], refs[1 + 2 * steps :]
    pick_in, w_down, w_flip, hid_in, slope_in, meta, out_all, kept = refs[:8]
    pick, moved, held, grads, out, down_v, flip_v, hid, slope, block_sem, sems, keep_sem, out_sem = refs[8:]
    experts, members = held.shape[0], moved.shape[1]
    half = members // 2
    first_pick = copy_all([(pick_in, pick)], sems.at[0])
    start_blocks(place, groups, own, mine, other, moved, block_sem)
    loads = [
        copy_all([(src.at[b], dst.at[b]) for b in range(experts)], sems.at[n])
        for n, (src, dst) in enumerate(((w_down, down_v), (hid_in, hid), (slope_in, slope), (w_flip, flip_v)), 1)
    ]
    first_pick[0].wait()
    for slot in range(groups):
        for part in range(2):
            at = pl.ds(part * half, half)
            pltpu.make_async_copy(own.at[at, :], moved.at[slot, at, :], block_sem.at[slot, part]).wait()
        group = lax.rem(place[3] - slot + groups, groups)
        first = pl.multiple_of(group * cap, PACK)
        got = dot(pick[group], moved[slot]).astype(bf16)
        for b in range(experts):
            held[b, pl.ds(first, cap), :] = got[b * cap : (b + 1) * cap]
    keep = copy_all([(held.at[b], kept.at[b]) for b in range(experts)], keep_sem)
    lane = lax.broadcasted_iota(jnp.int32, (groups * cap, LANES), 1)
    for b in range(experts):
        for load in loads[:3]:
            load[b].wait()
        back = dot(held[b], down_v[b])
        gate = jnp.sum(back * hid[b].astype(f32), axis=1, keepdims=True)
        gate = jnp.where(lane == b, gate, 0.0).astype(bf16)
        grad = (back * slope[b].astype(f32)).astype(bf16)
        loads[3][b].wait()
        route = dot(grad, flip_v[b]).astype(bf16)
        for g in range(groups):
            grads[g, pl.ds(b * cap, cap), pl.ds(0, width)] = route[g * cap : (g + 1) * cap]
            grads[g, pl.ds(b * cap, cap), pl.ds(width, LANES)] = gate[g * cap : (g + 1) * cap]
    lane = lax.broadcasted_iota(jnp.int32, (members, LANES), 1)
    for g in range(groups):
        total = dot(pick[g], grads[g], FIRST)
        out[g, :, pl.ds(0, width)] = total[:, :width].astype(bf16)
        by_expert = total[:, width:]
        ids = jnp.where(lane < top, meta[pl.ds(g * members, members), :].astype(f32), -1.0)
        picked = jnp.zeros(ids.shape, f32)
        for b in range(experts):
            hit = ids == (place[0] * experts + b).astype(f32)
            picked = picked + jnp.where(hit, by_expert[:, b : b + 1], 0.0)
        out[g, :, pl.ds(width, LANES)] = picked.astype(bf16)
        copy = pltpu.make_async_copy(out.at[g], out_all.at[pl.ds(g * members, members), :], out_sem.at[g])
        copy.start()
        keep.append(copy)
    for copy in keep:
        copy.wait()


def finish_kernel(width, top, rows, token, gate):
    token[...] = rows[:, pl.ds(0, width)]
    gate[...] = rows[:, pl.ds(width, LANES)].astype(f32).T[:top].astype(bf16)


def cost(flops, nbytes):
    return pl.CostEstimate(flops=int(flops), bytes_accessed=int(nbytes), transcendentals=0)


def shards(tokens, cotangent, expert_ids, gate_weights, w_up, w_down):
    tok_rows, width = tokens.shape
    top = expert_ids.shape[1]
    ep_count, dp_count = lax.axis_size("ep"), lax.axis_size("dp")
    experts, _, hidden = w_up.shape
    base_load = tok_rows * top // (experts * ep_count)
    capacity = base_load + max(1, base_load // 16)
    total = ep_count * tok_rows
    groups = ep_count // GROUP
    members = GROUP * tok_rows
    cap = -(-GROUP * capacity // PACK) * PACK
    routes = groups * cap
    full = width + LANES
    here = lax.axis_index("ep")
    place = jnp.stack([here, lax.axis_index("dp"), here % GROUP, here // GROUP]).astype(jnp.int32)
    bits = dp_count.bit_length() - 1
    turns = 2
    share = width // dp_count

    def shape(*dims, dtype=bf16):
        return jax.ShapeDtypeStruct(dims, dtype)

    x_own = pl.pallas_call(
        functools.partial(pack_kernel, top),
        out_shape=shape(tok_rows, full),
        compiler_params=pltpu.CompilerParams(vmem_limit_bytes=VMEM_LIMIT),
        cost_estimate=cost(0, 4 * tok_rows * width),
        name="pack",
    )(tokens, expert_ids.T, gate_weights.T)
    x_all = lax.all_gather(x_own, "ep", axis=0, tiled=True)

    def reach(p, step):
        q = p + GROUP * step if p % GROUP == 0 else p - GROUP * step
        return q if 0 <= q < ep_count else None

    def hop(value, pairs):
        return lax.ppermute(value, "ep", pairs)

    def at_group(i):
        return jnp.minimum(i, groups - 1)

    def at_expert(i):
        return jnp.clip(i - groups, 0, experts - 1)

    def at_slot(i, place):
        return lax.rem(place[3] - at_group(i) + groups, groups)

    def by_group(n):
        return pl.BlockSpec((members, n), lambda i, *_: (at_group(i), 0))

    def by_expert(rows, n):
        return pl.BlockSpec((1, rows, n), lambda i, *_: (at_expert(i), 0, 0))

    def call(kernel, name, grid, flops, nbytes, in_specs, out_specs, out_shape, scratch_shapes, prefetch=0):
        return pl.pallas_call(
            kernel,
            grid_spec=pltpu.PrefetchScalarGridSpec(
                num_scalar_prefetch=prefetch,
                grid=(grid,),
                in_specs=in_specs,
                out_specs=out_specs,
                scratch_shapes=scratch_shapes,
            ),
            out_shape=out_shape,
            compiler_params=pltpu.CompilerParams(vmem_limit_bytes=VMEM_LIMIT),
            cost_estimate=cost(flops, nbytes),
            name=name,
        )

    row_bytes = 2 * experts * hidden * width
    w_flip = call(
        flip_kernel,
        "flip",
        experts,
        0,
        2 * row_bytes,
        in_specs=[pl.BlockSpec((1, width, hidden), lambda b: (b, 0, 0))],
        out_specs=pl.BlockSpec((1, hidden, width), lambda b: (b, 0, 0)),
        out_shape=shape(experts, hidden, width),
        scratch_shapes=[],
    )(w_up)
    dy_own = jnp.concatenate([cotangent, hop(cotangent, [(p, p ^ 1) for p in range(ep_count)])], axis=0)
    lines = [None] + [
        [(p, reach(p, 1)) for p in range(ep_count) if None not in (reach(p, 1), reach(p, 1 - step))]
        for step in range(1, groups)
    ]
    swaps = [None] + [
        [(p, p ^ 1) for p in range(ep_count) if reach(p, -step) is not None] for step in range(1, groups)
    ]
    moving, dy_mine, dy_other = dy_own, [], []
    for step in range(1, groups - 1):
        moving = hop(moving, lines[step])
        if step == 1:
            moving, w_flip = lax.optimization_barrier((moving, w_flip))
        dy_mine.append(moving)

    act = shape(experts, routes, hidden)
    act_spec = by_expert(routes, hidden)
    pick_spec = pl.BlockSpec((1, experts * cap, members), lambda i, *_: (at_group(i), 0, 0))
    pick_flops = 2 * total * experts * cap * width
    main_flops = 2 * experts * routes * width * hidden
    act3 = pltpu.VMEM((experts, routes, hidden), bf16)
    pick_v = pltpu.VMEM((groups, experts * cap, members), bf16)
    most = max(experts, groups)

    def one(kernel, name, flops, nbytes, in_specs, out_specs, out_shape, scratch_shapes):
        return pl.pallas_call(
            kernel,
            in_specs=in_specs,
            out_specs=out_specs,
            out_shape=out_shape,
            scratch_shapes=scratch_shapes,
            compiler_params=pltpu.CompilerParams(vmem_limit_bytes=VMEM_LIMIT),
            cost_estimate=cost(flops, nbytes),
            name=name,
        )

    pick, meta, hid, scaled, slope_g = one(
        functools.partial(up_kernel, groups, width, top, cap, 0),
        "up",
        pick_flops + main_flops,
        2 * total * full + row_bytes,
        [SMEM, ANY, ANY],
        [ANY, pl.BlockSpec(memory_space=pltpu.VMEM), ANY, ANY, ANY],
        [shape(groups, experts * cap, members), shape(total, LANES), act, act, act],
        [
            pltpu.VMEM((groups, members, full), bf16),
            pltpu.VMEM((experts, width, hidden), bf16),
            pltpu.VMEM((experts, routes, width), bf16),
            pltpu.VMEM((experts, routes, LANES), f32),
            pick_v,
            act3,
            act3,
            act3,
            pltpu.SemaphoreType.DMA((2, most)),
            pltpu.SemaphoreType.DMA((4, experts)),
        ],
    )(place, x_all, w_up)
    *dy_mine, hid = lax.optimization_barrier((*dy_mine, hid))
    dy_mine.append(hop(dy_mine[-1], lines[-1]))
    dy_other = [hop(part, swap) for part, swap in zip(dy_mine, swaps[1:])]

    orders = []
    for g in range(turns):
        turn = [(g + t) % bits for t in range(bits)]
        orders.append(
            tuple(sum(((p >> (bits - 1 - t)) & 1) << turn[t] for t in range(bits)) for p in range(dp_count))
        )
    orders = tuple(orders)
    cut_rows = share // turns

    def down(start, count):
        outs = one(
            functools.partial(down_kernel, orders, start),
            "down",
            16 * main_flops,
            8 * row_bytes,
            [SMEM, ANY, ANY],
            [ANY] * (2 * turns),
            [shape(dp_count // 2, count, cut_rows, hidden)] * (2 * turns),
            [
                pltpu.VMEM((count, routes, width), bf16),
                pltpu.VMEM((count, routes, hidden), bf16),
                pltpu.VMEM((turns, dp_count, count, cut_rows, hidden), bf16),
                pltpu.SemaphoreType.DMA((2, count)),
                pltpu.SemaphoreType.DMA((turns, dp_count, count)),
            ],
        )(place, kept, scaled)
        return [(outs[2 * g], outs[2 * g + 1]) for g in range(turns)]

    def exchange(state, t):
        new = []
        for g, (keep, send) in enumerate(state):
            bit = 1 << ((g + t) % bits)
            got = lax.ppermute(send, "dp", [(i, i ^ bit) for i in range(dp_count)])
            both = keep.astype(f32) + got.astype(f32)
            if t < bits - 1:
                both = both.astype(bf16)
            half = both.shape[0] // 2
            new.append((both[:half], both[half:]) if half else both[0])
        return new

    token_part, kept = one(
        functools.partial(tail_kernel, groups, cap, width, top),
        "tail",
        8 * main_flops,
        4 * row_bytes,
        [SMEM] + [ANY] * (2 * groups - 1) + [ANY] * 5 + [pl.BlockSpec(memory_space=pltpu.VMEM)],
        [ANY, ANY],
        [shape(total, full), shape(experts, routes, width)],
        [
            pick_v,
            pltpu.VMEM((groups, members, width), bf16),
            pltpu.VMEM((experts, routes, width), bf16),
            pltpu.VMEM((groups, experts * cap, full), bf16),
            pltpu.VMEM((groups, members, full), bf16),
            pltpu.VMEM((experts, width, hidden), bf16),
            pltpu.VMEM((experts, hidden, width), bf16),
            act3,
            act3,
            pltpu.SemaphoreType.DMA((groups, 2)),
            pltpu.SemaphoreType.DMA((5, experts)),
            pltpu.SemaphoreType.DMA((experts,)),
            pltpu.SemaphoreType.DMA((groups,)),
        ],
    )(place, dy_own, *dy_mine, *dy_other, pick, w_down, w_flip, hid, slope_g, meta)
    summed = lax.psum_scatter(token_part, "ep", scatter_dimension=0, tiled=True)
    token_grad, gate_grad = pl.pallas_call(
        functools.partial(finish_kernel, width, top),
        out_shape=[shape(tok_rows, width), shape(top, tok_rows)],
        compiler_params=pltpu.CompilerParams(vmem_limit_bytes=VMEM_LIMIT),
        cost_estimate=cost(0, 4 * tok_rows * width),
        name="finish",
    )(summed)

    counts = [experts // 2, experts - experts // 2] if experts > 1 else [experts]
    states = [down(start, count) for start, count in zip((0, counts[0]), counts)]
    for t in range(bits):
        states = [exchange(state, t) for state in states]
    token_grad, states = lax.optimization_barrier((token_grad, states))
    down_grad = jnp.concatenate([jnp.concatenate(state, axis=1) for state in states], axis=0)
    return (token_grad, gate_grad.T, down_grad)


def solution(mesh):
    return jax.shard_map(
        shards,
        mesh=mesh,
        in_specs=(
            P(("dp", "ep"), None),
            P(("dp", "ep"), None),
            P(("dp", "ep"), None),
            P(("dp", "ep"), None),
            P("ep", None, None),
            P("ep", None, None),
        ),
        out_specs=(P(("dp", "ep"), None), P(("dp", "ep"), None), P("ep", "dp", None)),
        check_vma=False,
    )
```

time: 288 us -> 191 us (0.66)
  waiting for transfers between devices: 188 us -> 98 us
  Pallas kernels: 0 us -> 50.5 us
  matrix products: 49.3 us -> 0 us
  blocking collectives: 28.9 us -> 0 us
  starting transfers between devices: 0.38 us -> 21.5 us
    reduce_scatter x2 -> x1, waiting for transfers between devices: 120 us -> 0.02 us  [shards(): summed = lax.psum_scatter(token_part, 'ep', scatter_dimension=0, tiled=True)]
    ppermute x0 -> x15, waiting for transfers between devices: none -> 74.5 us  [the longest x8 38.1 us: exchange(): got = lax.ppermute(send, 'dp', [(i, i ^ bit) for i in range(dp_count)])]
    pallas_call x0 -> x7, Pallas kernels: none -> 50.5 us  [the longest x1 17.8 us: shards(): one(functools.partial(tail_kernel, groups, cap, width, top), 'tail', 8 *...]
    dot_general x7 -> x0, matrix products: 49.3 us -> none  [the longest x1 12 us: shards(): jnp.einsum('brt,brd->td', pick, route_grad, preferred_element_type=f32)]
    all_gather x2 -> x1, waiting for transfers between devices: 59.3 us -> 23.5 us  [shards(): x_all = lax.all_gather(x_own, 'ep', axis=0, tiled=True)]
    all_gather x2 -> x0, blocking collectives: 28.9 us -> none  [the longest x1 15.8 us: shards(): ids_all = lax.all_gather(expert_ids, 'ep', axis=0, tiled=True)]
    ppermute x0 -> x15, starting transfers between devices: none -> 21.4 us  [the longest x7 10.9 us: hop(): return lax.ppermute(value, 'ep', pairs)]
    unnamed x6 -> x2, waiting for transfers between devices: 9.12 us -> 0.03 us
  transfers between devices with their start and end apart: 5 -> 17, of which waited for: 5 -> 9; matrix products, arithmetic and copies ran while one was open for 13% -> 2% of each run, Pallas kernels for 0% -> 15%
where the time goes in v9:
time: 191 us; the launch traced here: 190 us
  waiting for transfers between devices  98 us (51%)
  Pallas kernels  50.5 us (26%)
  starting transfers between devices  21.5 us (11%)
  between operations  14.3 us (7%)
  other arithmetic  3.6 us (2%)
  local copies, waits for them, and re-layouts  2.31 us (1%)
    ppermute x8, waiting for transfers between devices, exchange(): got = lax.ppermute(send, 'dp', [(i, i ^ bit) for i in range(dp_count)])  38.1 us
    ppermute x7, waiting for transfers between devices, hop(): return lax.ppermute(value, 'ep', pairs)  36.3 us
    all_gather x1, waiting for transfers between devices, shards(): x_all = lax.all_gather(x_own, 'ep', axis=0, tiled=True)  23.5 us
    pallas_call x1, Pallas kernels, shards(): one(functools.partial(tail_kernel, groups, cap, width, top), 'tail', 8 *...  17.8 us
    pallas_call x2, Pallas kernels, down(): one(functools.partial(down_kernel, orders, start), 'down', 16 * main_flop...  11.5 us
    ppermute x7, starting transfers between devices, hop(): return lax.ppermute(value, 'ep', pairs)  10.9 us
    ppermute x8, starting transfers between devices, exchange(): got = lax.ppermute(send, 'dp', [(i, i ^ bit) for i in range(dp_count)])  10.5 us
    pallas_call x1, Pallas kernels, shards(): one(functools.partial(up_kernel, groups, width, top, cap, 0), 'up', pick_...  10.4 us
  transfers between devices with their start and end apart: 17, of which 9 were waited for; matrix products, arithmetic and copies ran while one was open for 2% of the time, Pallas kernels for 15%

profile of v9, /device:TPU:0, one launch (start us, length us, event | category | flops | bytes accessed | tf_op | source)
XLA Modules:
  0.0 190.2 jit_solution(813297588774278492)
XLA Ops:
  7.2 0.0 all-gather.2.cloned.1.call-start
  7.2 2.0 %pack.1 = bf16[128,2176]{1,0:T(8,128)(2,1)} custom-call(bf16[128,2048]{1,0:T(8,128)(2,1)} %tokens.1, s32[8,128]{1,0:T(8,128)} %bitcast.15, bf16[8,128]{1,0:T(8,128)(2,1)} %bitcast.16), custom_call_target="tpu_custom_call" | custom-call | bytes 1048576 | tf_op jit(solution)/shard_map/pack/pallas_call | solution.py:248
  9.2 0.0 all-gather.2.cloned.1.call-update
  9.2 0.0 reduce-scatter.2.cloned.1.call-start
  9.2 0.5 collective-permute-start
  9.8 1.1 constant_dynamic-update-slice_fusion.1
  10.8 0.7 collective-permute-done
  11.6 4.9 %collective-permute-start.1 = (bf16[256,2048]{1,0:T(8,128)(2,1)S(1)}, bf16[256,2048]{1,0:T(8,128)(2,1)S(1)}, u32[]{:S(2)}, u32[]{:S(2)}) collective-permute-start(bf16[256,2048]{1,0:T(8,128)(2,1)S(1)} %constant_dynamic-update-slice_fusion.refs_0_), channel_id=1, source_target_pairs={{0,2},{2,4},{3,1},{4,6},{5,3},{7,5},{8,10},{10,12},{11,9},{12,14},... | collective-permute-start | bytes 3145736 | tf_op jit(solution)/shard_map/ppermute | solution.py:262
  16.5 7.0 %flip.1.refs_9_ = bf16[4,384,2048]{2,1,0:T(8,128)(2,1)} custom-call(bf16[4,2048,384]{2,1,0:T(8,128)(2,1)} %w_up.1), custom_call_target="tpu_custom_call" | custom-call | bytes 12582912 | tf_op jit(solution)/shard_map/flip/pallas_call | solution.py:296
  23.5 21.3 %collective-permute-done.1.refs_1_ = bf16[256,2048]{1,0:T(8,128)(2,1)S(1)} collective-permute-done((bf16[256,2048]{1,0:T(8,128)(2,1)S(1)}, bf16[256,2048]{1,0:T(8,128)(2,1)S(1)}, u32[]{:S(2)}, u32[]{:S(2)}) %collective-permute-start.1) | collective-permute-done | bytes 1048608 | tf_op jit(solution)/shard_map/ppermute | solution.py:262
  44.8 0.7 collective-permute-start.2
  45.5 0.6 pad_add_fusion.place
  46.2 23.5 %all-gather.2.cloned.1.call-done.x_all = bf16[1024,2176]{1,0:T(8,128)(2,1)} async-done(((bf16[128,2176]{1,0:T(8,128)(2,1)}), bf16[1024,2176]{1,0:T(8,128)(2,1)}) %all-gather.2.cloned.1.call-update) | async-done | bytes 4456464 | tf_op jit(solution)/shard_map/all_gather | solution.py:255
  69.7 10.4 %up.1 = (bf16[4,320,256]{2,1,0:T(8,128)(2,1)}, bf16[1024,128]{1,0:T(8,128)(2,1)}, bf16[4,320,384]{2,1,0:T(8,128)(2,1)}, bf16[4,320,384]{2,1,0:T(8,128)(2,1)}, bf16[4,320,384]{2,1,0:T(8,128)(2,1)}) custom-call(s32[4]{0:T(128)} %pad_add_fusion.place, bf16[1024,2176]{1,0:T(8,128)(2,1)} %all-gather.2.cloned.1.call-done.x_all, bf16[4,2048,384]{2,1,0:T(8,128)(2,1)} %w_up.1), custom_call_target="tpu_custom_call" | custom-call | flops 3355443200 | bytes 10747904 | tf_op jit(solution)/shard_map/up/pallas_call | solution.py:343
  80.1 0.7 collective-permute-start.3
  80.8 1.3 collective-permute-start.5
  82.1 1.3 collective-permute-start.4
  83.5 1.5 collective-permute-start.6
  84.9 1.9 %collective-permute-done.4.refs_4_ = bf16[256,2048]{1,0:T(8,128)(2,1)S(1)} collective-permute-done((bf16[256,2048]{1,0:T(8,128)(2,1)S(1)}, bf16[256,2048]{1,0:T(8,128)(2,1)S(1)}, u32[]{:S(2)}, u32[]{:S(2)}) %collective-permute-start.4) | collective-permute-done | bytes 1048608 | tf_op jit(solution)/shard_map/ppermute | solution.py:262
  86.9 12.4 %collective-permute-done.6.refs_6_ = bf16[256,2048]{1,0:T(8,128)(2,1)S(1)} collective-permute-done((bf16[256,2048]{1,0:T(8,128)(2,1)S(1)}, bf16[256,2048]{1,0:T(8,128)(2,1)S(1)}, u32[]{:S(2)}, u32[]{:S(2)}) %collective-permute-start.6) | collective-permute-done | bytes 1048608 | tf_op jit(solution)/shard_map/ppermute | solution.py:262
  99.3 1.0 copy-done.10
  100.3 17.8 %tail.1 = (bf16[1024,2176]{1,0:T(8,128)(2,1)}, bf16[4,320,2048]{2,1,0:T(8,128)(2,1)}) custom-call(s32[4]{0:T(128)} %pad_add_fusion.place, bf16[256,2048]{1,0:T(8,128)(2,1)} %copy-done.4, bf16[256,2048]{1,0:T(8,128)(2,1)} %copy-done.5, bf16[256,2048]{1,0:T(8,128)(2,1)} %copy-done.6, bf16[256,2048]{1,0:T(8,128)(2,1)} %copy-done.7, ...), custom_call_target="tpu_custom_call" | custom-call | flops 16106127360 | bytes 25165824 | tf_op jit(solution)/shard_map/tail/pallas_call | solution.py:408
  118.1 0.0 reduce-scatter.2.cloned.1.call-update
  118.1 5.6 %down.3 = (bf16[2,2,256,384]{3,2,1,0:T(8,128)(2,1)}, bf16[2,2,256,384]{3,2,1,0:T(8,128)(2,1)}, bf16[2,2,256,384]{3,2,1,0:T(8,128)(2,1)}, bf16[2,2,256,384]{3,2,1,0:T(8,128)(2,1)}) custom-call(s32[4]{0:T(128)} %pad_add_fusion.place, bf16[4,320,2048]{2,1,0:T(8,128)(2,1)} %get-tuple-element.41.kept, bf16[4,320,384]{2,1,0:T(8,128)(2,1)} %get-tuple-element.42.scaled_in), custom_call_target="tpu_custom_call" | custom-call | flops 32212254720 | bytes 50331648 | tf_op jit(solution)/shard_map/down/pallas_call | solution.py:378
  123.8 1.6 collective-permute-start.11
  125.3 1.5 collective-permute-start.13
  126.8 5.9 %down.2 = (bf16[2,2,256,384]{3,2,1,0:T(8,128)(2,1)}, bf16[2,2,256,384]{3,2,1,0:T(8,128)(2,1)}, bf16[2,2,256,384]{3,2,1,0:T(8,128)(2,1)}, bf16[2,2,256,384]{3,2,1,0:T(8,128)(2,1)}) custom-call(s32[4]{0:T(128)} %pad_add_fusion.place, bf16[4,320,2048]{2,1,0:T(8,128)(2,1)} %get-tuple-element.41.kept, bf16[4,320,384]{2,1,0:T(8,128)(2,1)} %get-tuple-element.42.scaled_in), custom_call_target="tpu_custom_call" | custom-call | flops 32212254720 | bytes 50331648 | tf_op jit(solution)/shard_map/down/pallas_call | solution.py:378
  132.7 0.6 collective-permute-start.7
  133.3 0.5 collective-permute-start.9
  133.8 10.5 %collective-permute-done.11 = bf16[2,2,256,384]{3,2,1,0:T(8,128)(2,1)S(1)} collective-permute-done((bf16[2,2,256,384]{3,2,1,0:T(8,128)(2,1)}, bf16[2,2,256,384]{3,2,1,0:T(8,128)(2,1)S(1)}, u32[]{:S(2)}, u32[]{:S(2)}) %collective-permute-start.11) | collective-permute-done | bytes 786464 | tf_op jit(solution)/shard_map/ppermute | solution.py:400
  144.4 0.2 add_convert_fusion.1
  144.6 1.6 collective-permute-start.12
  146.2 0.2 add_convert_fusion
  146.5 1.6 collective-permute-start.14
  148.0 13.2 %collective-permute-done.7 = bf16[2,2,256,384]{3,2,1,0:T(8,128)(2,1)S(1)} collective-permute-done((bf16[2,2,256,384]{3,2,1,0:T(8,128)(2,1)}, bf16[2,2,256,384]{3,2,1,0:T(8,128)(2,1)S(1)}, u32[]{:S(2)}, u32[]{:S(2)}) %collective-permute-start.7) | collective-permute-done | bytes 786464 | tf_op jit(solution)/shard_map/ppermute | solution.py:400
  161.2 0.2 add_convert_fusion.3
  161.5 1.6 collective-permute-start.8
  163.1 0.2 add_convert_fusion.2
  163.3 1.6 collective-permute-start.10
  164.9 6.3 %collective-permute-done.12 = bf16[1,2,256,384]{3,2,1,0:T(8,128)(2,1)S(1)} collective-permute-done((bf16[1,2,256,384]{3,2,1,0:T(8,128)(2,1)S(1)}, bf16[1,2,256,384]{3,2,1,0:T(8,128)(2,1)S(1)}, u32[]{:S(2)}, u32[]{:S(2)}) %collective-permute-start.12) | collective-permute-done | bytes 393248 | tf_op jit(solution)/shard_map/ppermute | solution.py:400
  171.2 0.1 add_bitcast_fusion.1
  171.3 0.1 add_bitcast_fusion
  171.4 8.0 %collective-permute-done.8 = bf16[1,2,256,384]{3,2,1,0:T(8,128)(2,1)S(1)} collective-permute-done((bf16[1,2,256,384]{3,2,1,0:T(8,128)(2,1)S(1)}, bf16[1,2,256,384]{3,2,1,0:T(8,128)(2,1)S(1)}, u32[]{:S(2)}, u32[]{:S(2)}) %collective-permute-start.8) | collective-permute-done | bytes 393248 | tf_op jit(solution)/shard_map/ppermute | solution.py:400
  179.4 0.1 add_bitcast_fusion.3
  179.5 0.1 add_bitcast_fusion.2
  179.6 0.0 reduce-scatter.2.cloned.1.call-done.rows
  179.6 1.9 finish.1
  181.5 1.9 maximum_maximum_fusion
  (33 shorter events, 0.3 us)
Async XLA Ops:
  7.2 62.5 %all-gather.2.cloned.1.call-start = ((), (), s32[]{:S(2)}) async-start(), calls=%async_computation.1 | async-start | bytes 5013504 | tf_op jit(solution)/shard_map/all_gather | solution.py:255
  9.2 170.4 %reduce-scatter.2.cloned.1.call-start = ((), (), s32[]{:S(2)}) async-start(), calls=%async_computation.2 | async-start | bytes 5013504 | tf_op jit(solution)/shard_map/reduce_scatter | solution.py:432
  9.2 2.3 %collective-permute-start = (bf16[128,2048]{1,0:T(8,128)(2,1)}, bf16[128,2048]{1,0:T(8,128)(2,1)S(1)}, u32[]{:S(2)}, u32[]{:S(2)}) collective-permute-start(bf16[128,2048]{1,0:T(8,128)(2,1)} %param.7), channel_id=1, source_target_pairs={{0,1},{1,0},{2,3},{3,2},{4,5},{5,4},{6,7},{7,6},{8,9},{9,8},{10,11... | collective-permute-start | bytes 1572872 | tf_op jit(solution)/shard_map/ppermute | solution.py:262
  11.6 11.9 %copy-start.4 = (bf16[256,2048]{1,0:T(8,128)(2,1)}, bf16[256,2048]{1,0:T(8,128)(2,1)S(1)}, u32[]{:S(2)}) copy-start(bf16[256,2048]{1,0:T(8,128)(2,1)S(1)} %constant_dynamic-update-slice_fusion.refs_0_) | copy-start | bytes 3145732
  11.6 33.2 %collective-permute-start.1 = (bf16[256,2048]{1,0:T(8,128)(2,1)S(1)}, bf16[256,2048]{1,0:T(8,128)(2,1)S(1)}, u32[]{:S(2)}, u32[]{:S(2)}) collective-permute-start(bf16[256,2048]{1,0:T(8,128)(2,1)S(1)} %constant_dynamic-update-slice_fusion.refs_0_), channel_id=1, source_target_pairs={{0,2},{2,4},{3,1},{4,6},{5,3},{7,5},{8,10},{10,12},{11,9},{12,14},... | collective-permute-start | bytes 3145736 | tf_op jit(solution)/shard_map/ppermute | solution.py:262
  44.8 37.3 %copy-start.5 = (bf16[256,2048]{1,0:T(8,128)(2,1)}, bf16[256,2048]{1,0:T(8,128)(2,1)S(1)}, u32[]{:S(2)}) copy-start(bf16[256,2048]{1,0:T(8,128)(2,1)S(1)} %collective-permute-done.1.refs_1_) | copy-start | bytes 3145732
  44.8 35.3 %collective-permute-start.2 = (bf16[256,2048]{1,0:T(8,128)(2,1)S(1)}, bf16[256,2048]{1,0:T(8,128)(2,1)S(1)}, u32[]{:S(2)}, u32[]{:S(2)}) collective-permute-start(bf16[256,2048]{1,0:T(8,128)(2,1)S(1)} %collective-permute-done.1.refs_1_), channel_id=1, source_target_pairs={{2,4},{3,1},{4,6},{5,3},{10,12},{11,9},{12,14},{13,11},{18,20},{19... | collective-permute-start | bytes 3145736 | tf_op jit(solution)/shard_map/ppermute | solution.py:262
  80.1 20.2 %copy-start.6 = (bf16[256,2048]{1,0:T(8,128)(2,1)}, bf16[256,2048]{1,0:T(8,128)(2,1)S(1)}, u32[]{:S(2)}) copy-start(bf16[256,2048]{1,0:T(8,128)(2,1)S(1)} %collective-permute-done.2.refs_2_) | copy-start | bytes 3145732
  80.1 3.3 %collective-permute-start.3 = (bf16[256,2048]{1,0:T(8,128)(2,1)S(1)}, bf16[256,2048]{1,0:T(8,128)(2,1)S(1)}, u32[]{:S(2)}, u32[]{:S(2)}) collective-permute-start(bf16[256,2048]{1,0:T(8,128)(2,1)S(1)} %collective-permute-done.2.refs_2_), channel_id=1, source_target_pairs={{3,1},{4,6},{11,9},{12,14},{19,17},{20,22},{27,25},{28,30}} | collective-permute-start | bytes 3145736 | tf_op jit(solution)/shard_map/ppermute | solution.py:262
  80.8 6.1 %collective-permute-start.5 = (bf16[256,2048]{1,0:T(8,128)(2,1)S(1)}, bf16[256,2048]{1,0:T(8,128)(2,1)S(1)}, u32[]{:S(2)}, u32[]{:S(2)}) collective-permute-start(bf16[256,2048]{1,0:T(8,128)(2,1)S(1)} %collective-permute-done.2.refs_2_), channel_id=1, source_target_pairs={{1,0},{3,2},{4,5},{6,7},{9,8},{11,10},{12,13},{14,15},{17,16},{19,... | collective-permute-start | bytes 3145736 | tf_op jit(solution)/shard_map/ppermute | solution.py:262
  82.1 4.7 %collective-permute-start.4 = (bf16[256,2048]{1,0:T(8,128)(2,1)S(1)}, bf16[256,2048]{1,0:T(8,128)(2,1)S(1)}, u32[]{:S(2)}, u32[]{:S(2)}) collective-permute-start(bf16[256,2048]{1,0:T(8,128)(2,1)S(1)} %collective-permute-done.1.refs_1_), channel_id=1, source_target_pairs={{1,0},{2,3},{3,2},{4,5},{5,4},{6,7},{9,8},{10,11},{11,10},{12,13},... | collective-permute-start | bytes 3145736 | tf_op jit(solution)/shard_map/ppermute | solution.py:262
  83.4 16.9 %copy-start.7 = (bf16[256,2048]{1,0:T(8,128)(2,1)}, bf16[256,2048]{1,0:T(8,128)(2,1)S(1)}, u32[]{:S(2)}) copy-start(bf16[256,2048]{1,0:T(8,128)(2,1)S(1)} %collective-permute-done.3.refs_3_) | copy-start | bytes 3145732
  83.5 15.8 %collective-permute-start.6 = (bf16[256,2048]{1,0:T(8,128)(2,1)S(1)}, bf16[256,2048]{1,0:T(8,128)(2,1)S(1)}, u32[]{:S(2)}, u32[]{:S(2)}) collective-permute-start(bf16[256,2048]{1,0:T(8,128)(2,1)S(1)} %collective-permute-done.3.refs_3_), channel_id=1, source_target_pairs={{1,0},{6,7},{9,8},{14,15},{17,16},{22,23},{25,24},{30,31}} | collective-permute-start | bytes 3145736 | tf_op jit(solution)/shard_map/ppermute | solution.py:262
  86.9 12.4 %copy-start.9 = (bf16[256,2048]{1,0:T(8,128)(2,1)}, bf16[256,2048]{1,0:T(8,128)(2,1)S(1)}, u32[]{:S(2)}) copy-start(bf16[256,2048]{1,0:T(8,128)(2,1)S(1)} %collective-permute-done.4.refs_4_) | copy-start | bytes 3145732
  86.9 12.4 %copy-start.8 = (bf16[256,2048]{1,0:T(8,128)(2,1)}, bf16[256,2048]{1,0:T(8,128)(2,1)S(1)}, u32[]{:S(2)}) copy-start(bf16[256,2048]{1,0:T(8,128)(2,1)S(1)} %collective-permute-done.5.refs_5_) | copy-start | bytes 3145732
  99.3 1.0 copy-start.10
  123.8 20.6 %collective-permute-start.11 = (bf16[2,2,256,384]{3,2,1,0:T(8,128)(2,1)}, bf16[2,2,256,384]{3,2,1,0:T(8,128)(2,1)S(1)}, u32[]{:S(2)}, u32[]{:S(2)}) collective-permute-start(bf16[2,2,256,384]{3,2,1,0:T(8,128)(2,1)} %get-tuple-element.48), channel_id=1, source_target_pairs={{0,8},{8,0},{16,24},{24,16},{1,9},{9,1},{17,25},{25,17},{2,10},{10... | collective-permute-start | bytes 2359304 | tf_op jit(solution)/shard_map/ppermute | solution.py:400
  125.3 19.1 %copy-start.3 = (bf16[2,2,256,384]{3,2,1,0:T(8,128)(2,1)S(1)}, bf16[2,2,256,384]{3,2,1,0:T(8,128)(2,1)}, u32[]{:S(2)}) copy-start(bf16[2,2,256,384]{3,2,1,0:T(8,128)(2,1)} %get-tuple-element.47) | copy-start | bytes 2359300
  125.3 20.9 %collective-permute-start.13 = (bf16[2,2,256,384]{3,2,1,0:T(8,128)(2,1)}, bf16[2,2,256,384]{3,2,1,0:T(8,128)(2,1)S(1)}, u32[]{:S(2)}, u32[]{:S(2)}) collective-permute-start(bf16[2,2,256,384]{3,2,1,0:T(8,128)(2,1)} %get-tuple-element.50), channel_id=1, source_target_pairs={{0,16},{8,24},{16,0},{24,8},{1,17},{9,25},{17,1},{25,9},{2,18},{10... | collective-permute-start | bytes 2359304 | tf_op jit(solution)/shard_map/ppermute | solution.py:400
  132.7 13.5 %copy-start.2 = (bf16[2,2,256,384]{3,2,1,0:T(8,128)(2,1)S(1)}, bf16[2,2,256,384]{3,2,1,0:T(8,128)(2,1)}, u32[]{:S(2)}) copy-start(bf16[2,2,256,384]{3,2,1,0:T(8,128)(2,1)} %get-tuple-element.49) | copy-start | bytes 2359300
  132.7 28.5 %collective-permute-start.7 = (bf16[2,2,256,384]{3,2,1,0:T(8,128)(2,1)}, bf16[2,2,256,384]{3,2,1,0:T(8,128)(2,1)S(1)}, u32[]{:S(2)}, u32[]{:S(2)}) collective-permute-start(bf16[2,2,256,384]{3,2,1,0:T(8,128)(2,1)} %get-tuple-element.44), channel_id=1, source_target_pairs={{0,8},{8,0},{16,24},{24,16},{1,9},{9,1},{17,25},{25,17},{2,10},{10... | collective-permute-start | bytes 2359304 | tf_op jit(solution)/shard_map/ppermute | solution.py:400
  133.3 29.7 %collective-permute-start.9 = (bf16[2,2,256,384]{3,2,1,0:T(8,128)(2,1)}, bf16[2,2,256,384]{3,2,1,0:T(8,128)(2,1)S(1)}, u32[]{:S(2)}, u32[]{:S(2)}) collective-permute-start(bf16[2,2,256,384]{3,2,1,0:T(8,128)(2,1)} %get-tuple-element.46), channel_id=1, source_target_pairs={{0,16},{8,24},{16,0},{24,8},{1,17},{9,25},{17,1},{25,9},{2,18},{10... | collective-permute-start | bytes 2359304 | tf_op jit(solution)/shard_map/ppermute | solution.py:400
  144.4 16.9 %copy-start.1 = (bf16[2,2,256,384]{3,2,1,0:T(8,128)(2,1)S(1)}, bf16[2,2,256,384]{3,2,1,0:T(8,128)(2,1)}, u32[]{:S(2)}) copy-start(bf16[2,2,256,384]{3,2,1,0:T(8,128)(2,1)} %get-tuple-element.43) | copy-start | bytes 2359300
  144.6 26.6 %collective-permute-start.12 = (bf16[1,2,256,384]{3,2,1,0:T(8,128)(2,1)S(1)}, bf16[1,2,256,384]{3,2,1,0:T(8,128)(2,1)S(1)}, u32[]{:S(2)}, u32[]{:S(2)}) collective-permute-start(bf16[1,2,256,384]{3,2,1,0:T(8,128)(2,1)S(1)} %slice.37), channel_id=1, source_target_pairs={{0,16},{8,24},{16,0},{24,8},{1,17},{9,25},{17,1},{25,9},{2,18},{10... | collective-permute-start | bytes 1179656 | tf_op jit(solution)/shard_map/ppermute | solution.py:400
  146.2 16.9 %copy-start = (bf16[2,2,256,384]{3,2,1,0:T(8,128)(2,1)S(1)}, bf16[2,2,256,384]{3,2,1,0:T(8,128)(2,1)}, u32[]{:S(2)}) copy-start(bf16[2,2,256,384]{3,2,1,0:T(8,128)(2,1)} %get-tuple-element.45) | copy-start | bytes 2359300
  146.5 24.8 %collective-permute-start.14 = (bf16[1,2,256,384]{3,2,1,0:T(8,128)(2,1)S(1)}, bf16[1,2,256,384]{3,2,1,0:T(8,128)(2,1)S(1)}, u32[]{:S(2)}, u32[]{:S(2)}) collective-permute-start(bf16[1,2,256,384]{3,2,1,0:T(8,128)(2,1)S(1)} %slice.39), channel_id=1, source_target_pairs={{0,8},{8,0},{16,24},{24,16},{1,9},{9,1},{17,25},{25,17},{2,10},{10... | collective-permute-start | bytes 1179656 | tf_op jit(solution)/shard_map/ppermute | solution.py:400
  161.5 18.0 %collective-permute-start.8 = (bf16[1,2,256,384]{3,2,1,0:T(8,128)(2,1)S(1)}, bf16[1,2,256,384]{3,2,1,0:T(8,128)(2,1)S(1)}, u32[]{:S(2)}, u32[]{:S(2)}) collective-permute-start(bf16[1,2,256,384]{3,2,1,0:T(8,128)(2,1)S(1)} %slice.33), channel_id=1, source_target_pairs={{0,16},{8,24},{16,0},{24,8},{1,17},{9,25},{17,1},{25,9},{2,18},{10... | collective-permute-start | bytes 1179656 | tf_op jit(solution)/shard_map/ppermute | solution.py:400
  163.3 16.2 %collective-permute-start.10 = (bf16[1,2,256,384]{3,2,1,0:T(8,128)(2,1)S(1)}, bf16[1,2,256,384]{3,2,1,0:T(8,128)(2,1)S(1)}, u32[]{:S(2)}, u32[]{:S(2)}) collective-permute-start(bf16[1,2,256,384]{3,2,1,0:T(8,128)(2,1)S(1)} %slice.35), channel_id=1, source_target_pairs={{0,8},{8,0},{16,24},{24,16},{1,9},{9,1},{17,25},{25,17},{2,10},{10... | collective-permute-start | bytes 1179656 | tf_op jit(solution)/shard_map/ppermute | solution.py:400
Sparse Core Ops, SparseCore 0:
  9.6 59.9 all-gather.1
  118.3 51.7 reduce-scatter.1

commit v10 on v9

--- a/solution.py
+++ b/solution.py
@@ -159,8 +159,28 @@
         copy.wait()
 
 
-def tail_kernel(groups, cap, width, top, place, *refs):
-    steps = groups - 1
+def last_group(place, groups):
+    return (place[3] == 0) | (place[3] == groups - 1), jnp.where(place[3] == 0, groups - 1, 0)
+
+
+def gate_columns(place, top, experts, by_expert, info):
+    lane = lax.broadcasted_iota(jnp.int32, info.shape, 1)
+    ids = jnp.where(lane < top, info, -1.0)
+    picked = jnp.zeros(info.shape, f32)
+    for b in range(experts):
+        hit = ids == (place[0] * experts + b).astype(f32)
+        picked = picked + jnp.where(hit, by_expert[:, b : b + 1], 0.0)
+    return picked
+
+
+def gate_terms(back, hid, b):
+    lane = lax.broadcasted_iota(jnp.int32, (back.shape[0], LANES), 1)
+    gate = jnp.sum(back * hid.astype(f32), axis=1, keepdims=True)
+    return jnp.where(lane == b, gate, 0.0).astype(bf16)
+
+
+def early_kernel(groups, cap, width, top, place, *refs):
+    steps = groups - 2
     own, mine, other, refs = refs[0], refs[1 : 1 + steps], refs[1 + steps : 1 + 2 * steps], refs[1 + 2 * steps :]
     pick_in, w_down, w_flip, hid_in, slope_in, meta, out_all, kept = refs[:8]
     pick, moved, held, grads, out, down_v, flip_v, hid, slope, block_sem, sems, keep_sem, out_sem = refs[8:]
@@ -174,44 +194,91 @@
     ]
     first_pick[0].wait()
     for slot in range(groups):
-        for part in range(2):
-            at = pl.ds(part * half, half)
-            pltpu.make_async_copy(own.at[at, :], moved.at[slot, at, :], block_sem.at[slot, part]).wait()
         group = lax.rem(place[3] - slot + groups, groups)
         first = pl.multiple_of(group * cap, PACK)
-        got = dot(pick[group], moved[slot]).astype(bf16)
-        for b in range(experts):
-            held[b, pl.ds(first, cap), :] = got[b * cap : (b + 1) * cap]
+        here = True if slot == 0 else jnp.where(place[3] >= slot, slot, groups - slot) <= steps
+
+        @pl.when(here)
+        def _():
+            for part in range(2):
+                at = pl.ds(part * half, half)
+                pltpu.make_async_copy(own.at[at, :], moved.at[slot, at, :], block_sem.at[slot, part]).wait()
+            got = dot(pick[group], moved[slot]).astype(bf16)
+            for b in range(experts):
+                held[b, pl.ds(first, cap), :] = got[b * cap : (b + 1) * cap]
+
+        @pl.when(jnp.logical_not(here))
+        def _():
+            for b in range(experts):
+                held[b, pl.ds(first, cap), :] = jnp.zeros((cap, width), bf16)
+
     keep = copy_all([(held.at[b], kept.at[b]) for b in range(experts)], keep_sem)
-    lane = lax.broadcasted_iota(jnp.int32, (groups * cap, LANES), 1)
     for b in range(experts):
         for load in loads[:3]:
             load[b].wait()
         back = dot(held[b], down_v[b])
-        gate = jnp.sum(back * hid[b].astype(f32), axis=1, keepdims=True)
-        gate = jnp.where(lane == b, gate, 0.0).astype(bf16)
+        gate = gate_terms(back, hid[b], b)
         grad = (back * slope[b].astype(f32)).astype(bf16)
         loads[3][b].wait()
         route = dot(grad, flip_v[b]).astype(bf16)
         for g in range(groups):
             grads[g, pl.ds(b * cap, cap), pl.ds(0, width)] = route[g * cap : (g + 1) * cap]
             grads[g, pl.ds(b * cap, cap), pl.ds(width, LANES)] = gate[g * cap : (g + 1) * cap]
-    lane = lax.broadcasted_iota(jnp.int32, (members, LANES), 1)
     for g in range(groups):
         total = dot(pick[g], grads[g], FIRST)
         out[g, :, pl.ds(0, width)] = total[:, :width].astype(bf16)
-        by_expert = total[:, width:]
-        ids = jnp.where(lane < top, meta[pl.ds(g * members, members), :].astype(f32), -1.0)
-        picked = jnp.zeros(ids.shape, f32)
-        for b in range(experts):
-            hit = ids == (place[0] * experts + b).astype(f32)
-            picked = picked + jnp.where(hit, by_expert[:, b : b + 1], 0.0)
-        out[g, :, pl.ds(width, LANES)] = picked.astype(bf16)
+        info = meta[pl.ds(g * members, members), :].astype(f32)
+        out[g, :, pl.ds(width, LANES)] = gate_columns(place, top, experts, total[:, width:], info).astype(bf16)
         copy = pltpu.make_async_copy(out.at[g], out_all.at[pl.ds(g * members, members), :], out_sem.at[g])
         copy.start()
         keep.append(copy)
     for copy in keep:
         copy.wait()
+
+
+def late_kernel(groups, cap, width, top, place, pick_in, mine, other, w_down, w_flip, hid_in, slope_in, *refs):
+    meta, _, _, out_all, kept, pick, moved, held, grads, out, down_v, flip_v, hid, slope, info, block_sem, sems = refs
+    experts, members = held.shape[0], moved.shape[0]
+    has, group = last_group(place, groups)
+    at = pl.ds(pl.multiple_of(group * cap, PACK), cap)
+    tokens = pl.ds(pl.multiple_of(group * members, members), members)
+
+    @pl.when(has)
+    def _():
+        def start(ref, flip):
+            for copy in block_copies(place, ref, moved, block_sem, flip):
+                copy.start()
+
+        by_side(place, place[3] != 0, lambda left: mine, lambda left: other, start)
+        small = copy_all([(pick_in.at[group], pick), (meta.at[tokens, :], info)], sems.at[0])
+        loads = [
+            copy_all([(src.at[b], dst.at[b]) for b in range(experts)], sems.at[n])
+            for n, (src, dst) in enumerate(((w_down, down_v), (w_flip, flip_v)), 1)
+        ]
+        loads += [
+            copy_all([(src.at[b, at, :], dst.at[b]) for b in range(experts)], sems.at[n])
+            for n, (src, dst) in enumerate(((hid_in, hid), (slope_in, slope)), 3)
+        ]
+        for copy in small + block_copies(place, mine, moved, block_sem, 0):
+            copy.wait()
+        got = dot(pick[...], moved[...]).astype(bf16)
+        for b in range(experts):
+            held[b] = got[b * cap : (b + 1) * cap]
+        ends = copy_all([(held.at[b], kept.at[b, at, :]) for b in range(experts)], sems.at[5])
+        for b in range(experts):
+            for load in loads:
+                load[b].wait()
+            back = dot(held[b], down_v[b])
+            grad = (back * slope[b].astype(f32)).astype(bf16)
+            grads[pl.ds(b * cap, cap), pl.ds(0, width)] = dot(grad, flip_v[b]).astype(bf16)
+            grads[pl.ds(b * cap, cap), pl.ds(width, LANES)] = gate_terms(back, hid[b], b)
+        total = dot(pick[...], grads[...], FIRST)
+        out[:, pl.ds(0, width)] = total[:, :width].astype(bf16)
+        columns = gate_columns(place, top, experts, total[:, width:], info[...].astype(f32))
+        out[:, pl.ds(width, LANES)] = columns.astype(bf16)
+        ends += copy_all([(out, out_all.at[tokens, :])], sems.at[6])
+        for copy in ends:
+            copy.wait()
 
 
 def finish_kernel(width, top, rows, token, gate):
@@ -362,7 +429,7 @@
         ],
     )(place, x_all, w_up)
     *dy_mine, hid = lax.optimization_barrier((*dy_mine, hid))
-    dy_mine.append(hop(dy_mine[-1], lines[-1]))
+    moving = hop(dy_mine[-1], lines[-1])
     dy_other = [hop(part, swap) for part, swap in zip(dy_mine, swaps[1:])]
 
     orders = []
@@ -405,22 +472,23 @@
             new.append((both[:half], both[half:]) if half else both[0])
         return new
 
+    weights_v = [pltpu.VMEM((experts, width, hidden), bf16), pltpu.VMEM((experts, hidden, width), bf16)]
+    parts_shape = [shape(total, full), shape(experts, routes, width)]
     token_part, kept = one(
-        functools.partial(tail_kernel, groups, cap, width, top),
-        "tail",
+        functools.partial(early_kernel, groups, cap, width, top),
+        "early",
         8 * main_flops,
         4 * row_bytes,
-        [SMEM] + [ANY] * (2 * groups - 1) + [ANY] * 5 + [pl.BlockSpec(memory_space=pltpu.VMEM)],
+        [SMEM] + [ANY] * (2 * groups - 3) + [ANY] * 5 + [pl.BlockSpec(memory_space=pltpu.VMEM)],
         [ANY, ANY],
-        [shape(total, full), shape(experts, routes, width)],
+        parts_shape,
         [
             pick_v,
             pltpu.VMEM((groups, members, width), bf16),
             pltpu.VMEM((experts, routes, width), bf16),
             pltpu.VMEM((groups, experts * cap, full), bf16),
             pltpu.VMEM((groups, members, full), bf16),
-            pltpu.VMEM((experts, width, hidden), bf16),
-            pltpu.VMEM((experts, hidden, width), bf16),
+            *weights_v,
             act3,
             act3,
             pltpu.SemaphoreType.DMA((groups, 2)),
@@ -429,6 +497,31 @@
             pltpu.SemaphoreType.DMA((groups,)),
         ],
     )(place, dy_own, *dy_mine, *dy_other, pick, w_down, w_flip, hid, slope_g, meta)
+    moving, kept = lax.optimization_barrier((moving, kept))
+    act_v = pltpu.VMEM((experts, cap, hidden), bf16)
+    token_part, kept = pl.pallas_call(
+        functools.partial(late_kernel, groups, cap, width, top),
+        in_specs=[SMEM] + [ANY] * 10,
+        out_specs=[ANY, ANY],
+        out_shape=parts_shape,
+        input_output_aliases={9: 0, 10: 1},
+        scratch_shapes=[
+            pltpu.VMEM((experts * cap, members), bf16),
+            pltpu.VMEM((members, width), bf16),
+            pltpu.VMEM((experts, cap, width), bf16),
+            pltpu.VMEM((experts * cap, full), bf16),
+            pltpu.VMEM((members, full), bf16),
+            *weights_v,
+            act_v,
+            act_v,
+            pltpu.VMEM((members, LANES), bf16),
+            pltpu.SemaphoreType.DMA((2,)),
+            pltpu.SemaphoreType.DMA((7, most)),
+        ],
+        compiler_params=pltpu.CompilerParams(vmem_limit_bytes=VMEM_LIMIT),
+        cost_estimate=cost(main_flops, 2 * row_bytes),
+        name="late",
+    )(place, pick, moving, hop(moving, swaps[-1]), w_down, w_flip, hid, slope_g, meta, token_part, kept)
     summed = lax.psum_scatter(token_part, "ep", scatter_dimension=0, tiled=True)
     token_grad, gate_grad = pl.pallas_call(
         functools.partial(finish_kernel, width, top),
@@ -441,8 +534,13 @@
     counts = [experts // 2, experts - experts // 2] if experts > 1 else [experts]
     states = [down(start, count) for start, count in zip((0, counts[0]), counts)]
     for t in range(bits):
+        if t == bits - 1:
+            keeps = [[pair[0] for pair in state] for state in states]
+            token_grad, keeps[-1] = lax.optimization_barrier((token_grad, keeps[-1]))
+            states = [
+                [(keep, pair[1]) for keep, pair in zip(kept_back, state)] for kept_back, state in zip(keeps, states)
+            ]
         states = [exchange(state, t) for state in states]
-    token_grad, states = lax.optimization_barrier((token_grad, states))
     down_grad = jnp.concatenate([jnp.concatenate(state, axis=1) for state in states], axis=0)
     return (token_grad, gate_grad.T, down_grad)
 

time: 191 us -> 193 us (1.010)
  Pallas kernels: 50.5 us -> 61.9 us
  waiting for transfers between devices: 98 us -> 87.1 us
    pallas_call x1 -> x2, Pallas kernels: 17.8 us -> 29.4 us  [the longest x1 17.7 us: shards(): one(functools.partial(early_kernel, groups, cap, width, top), 'early', 8...]
    ppermute x7, waiting for transfers between devices: 36.3 us -> 27.9 us  [hop(): return lax.ppermute(value, 'ep', pairs)]
    ppermute x8, waiting for transfers between devices: 38.1 us -> 35.6 us  [exchange(): got = lax.ppermute(send, 'dp', [(i, i ^ bit) for i in range(dp_count)])]
  transfers between devices with their start and end apart: 17 -> 17, of which waited for: 9 -> 10; matrix products, arithmetic and copies ran while one was open for 2% -> 2% of each run, Pallas kernels for 15% -> 25%
where the time goes in v10:
time: 193 us
  waiting for transfers between devices  87.1 us (45%)
  Pallas kernels  61.9 us (32%)
  starting transfers between devices  21.3 us (11%)
  between operations  14.3 us (7%)
  other arithmetic  4.65 us (2%)
  local copies, waits for them, and re-layouts  3.35 us (2%)
    ppermute x8, waiting for transfers between devices, exchange(): got = lax.ppermute(send, 'dp', [(i, i ^ bit) for i in range(dp_count)])  35.6 us
    ppermute x7, waiting for transfers between devices, hop(): return lax.ppermute(value, 'ep', pairs)  27.9 us
    all_gather x1, waiting for transfers between devices, shards(): x_all = lax.all_gather(x_own, 'ep', axis=0, tiled=True)  23.5 us
    pallas_call x1, Pallas kernels, shards(): one(functools.partial(early_kernel, groups, cap, width, top), 'early', 8...  17.7 us
    pallas_call x1, Pallas kernels, shards(): pl.pallas_call(functools.partial(late_kernel, groups, cap, width, top), i...  11.7 us
    pallas_call x2, Pallas kernels, down(): one(functools.partial(down_kernel, orders, start), 'down', 16 * main_flop...  11.2 us
    ppermute x7, starting transfers between devices, hop(): return lax.ppermute(value, 'ep', pairs)  10.8 us
    ppermute x8, starting transfers between devices, exchange(): got = lax.ppermute(send, 'dp', [(i, i ^ bit) for i in range(dp_count)])  10.5 us
  transfers between devices with their start and end apart: 17, of which 10 were waited for; matrix products, arithmetic and copies ran while one was open for 2% of the time, Pallas kernels for 25%

profile of v10, /device:TPU:0, one launch (start us, length us, event | category | flops | bytes accessed | tf_op | source)
XLA Modules:
  0.0 192.6 jit_solution(12323908284088844016)
XLA Ops:
  7.2 2.0 %pack.1 = bf16[128,2176]{1,0:T(8,128)(2,1)} custom-call(bf16[128,2048]{1,0:T(8,128)(2,1)} %tokens.1, s32[8,128]{1,0:T(8,128)} %bitcast.15, bf16[8,128]{1,0:T(8,128)(2,1)} %bitcast.16), custom_call_target="tpu_custom_call" | custom-call | bytes 1048576 | tf_op jit(solution)/shard_map/pack/pallas_call | solution.py:315
  9.3 0.5 collective-permute-start
  9.8 1.1 constant_dynamic-update-slice_fusion.1
  10.9 0.7 collective-permute-done
  11.6 4.9 %collective-permute-start.1 = (bf16[256,2048]{1,0:T(8,128)(2,1)S(1)}, bf16[256,2048]{1,0:T(8,128)(2,1)S(1)}, u32[]{:S(2)}, u32[]{:S(2)}) collective-permute-start(bf16[256,2048]{1,0:T(8,128)(2,1)S(1)} %constant_dynamic-update-slice_fusion.refs_0_), channel_id=1, source_target_pairs={{0,2},{2,4},{3,1},{4,6},{5,3},{7,5},{8,10},{10,12},{11,9},{12,14},... | collective-permute-start | bytes 3145736 | tf_op jit(solution)/shard_map/ppermute | solution.py:329
  16.5 7.0 %flip.1.refs_7_.w_flip = bf16[4,384,2048]{2,1,0:T(8,128)(2,1)} custom-call(bf16[4,2048,384]{2,1,0:T(8,128)(2,1)} %w.1), custom_call_target="tpu_custom_call" | custom-call | bytes 12582912 | tf_op jit(solution)/shard_map/flip/pallas_call | solution.py:363
  23.5 21.3 %collective-permute-done.1.refs_1_ = bf16[256,2048]{1,0:T(8,128)(2,1)S(1)} collective-permute-done((bf16[256,2048]{1,0:T(8,128)(2,1)S(1)}, bf16[256,2048]{1,0:T(8,128)(2,1)S(1)}, u32[]{:S(2)}, u32[]{:S(2)}) %collective-permute-start.1) | collective-permute-done | bytes 1048608 | tf_op jit(solution)/shard_map/ppermute | solution.py:329
  44.8 0.7 collective-permute-start.2
  45.5 0.6 pad_add_fusion.place
  46.1 23.5 %all-gather.2.cloned.1.call-done.x_all = bf16[1024,2176]{1,0:T(8,128)(2,1)} async-done(((bf16[128,2176]{1,0:T(8,128)(2,1)}), bf16[1024,2176]{1,0:T(8,128)(2,1)}) %all-gather.2.cloned.1.call-update) | async-done | bytes 4456464 | tf_op jit(solution)/shard_map/all_gather | solution.py:322
  69.7 10.4 %up.1 = (bf16[4,320,256]{2,1,0:T(8,128)(2,1)}, bf16[1024,128]{1,0:T(8,128)(2,1)}, bf16[4,320,384]{2,1,0:T(8,128)(2,1)}, bf16[4,320,384]{2,1,0:T(8,128)(2,1)}, bf16[4,320,384]{2,1,0:T(8,128)(2,1)}) custom-call(s32[4]{0:T(128)} %pad_add_fusion.place, bf16[1024,2176]{1,0:T(8,128)(2,1)} %all-gather.2.cloned.1.call-done.x_all, bf16[4,2048,384]{2,1,0:T(8,128)(2,1)} %w.1), custom_call_target="tpu_custom_call" | custom-call | flops 3355443200 | bytes 10747904 | tf_op jit(solution)/shard_map/up/pallas_call | solution.py:410
  80.1 1.3 collective-permute-start.4
  81.4 1.3 collective-permute-start.5
  82.7 0.7 collective-permute-start.3
  83.4 1.2 collective-permute-done.4.refs_3_
  84.7 1.5 collective-permute-done.5.refs_4_
  86.2 1.0 copy-done.10
  87.1 17.7 %early.1 = (bf16[1024,2176]{1,0:T(8,128)(2,1)}, bf16[4,320,2048]{2,1,0:T(8,128)(2,1)}) custom-call(s32[4]{0:T(128)} %pad_add_fusion.place, bf16[256,2048]{1,0:T(8,128)(2,1)} %copy-done.6, bf16[256,2048]{1,0:T(8,128)(2,1)} %copy-done.7, bf16[256,2048]{1,0:T(8,128)(2,1)} %copy-done.8, bf16[256,2048]{1,0:T(8,128)(2,1)} %copy-done.9, ...), custom_call_target="tpu_custom_call" | custom-call | flops 16106127360 | bytes 25165824 | tf_op jit(solution)/shard_map/early/pallas_call | solution.py:477
  104.8 1.3 collective-permute-start.6
  106.1 3.3 %collective-permute-done.6.other = bf16[256,2048]{1,0:T(8,128)(2,1)S(1)} collective-permute-done((bf16[256,2048]{1,0:T(8,128)(2,1)S(1)}, bf16[256,2048]{1,0:T(8,128)(2,1)S(1)}, u32[]{:S(2)}, u32[]{:S(2)}) %collective-permute-start.6) | collective-permute-done | bytes 1048608 | tf_op jit(solution)/shard_map/ppermute | solution.py:329
  109.4 1.0 copy-done.1
  110.4 11.7 %late.1 = (bf16[1024,2176]{1,0:T(8,128)(2,1)}, bf16[4,320,2048]{2,1,0:T(8,128)(2,1)}) custom-call(s32[4]{0:T(128)} %pad_add_fusion.place, bf16[4,320,256]{2,1,0:T(8,128)(2,1)} %get-tuple-element.32.refs_5_.pick_in, bf16[256,2048]{1,0:T(8,128)(2,1)} %copy-done, bf16[256,2048]{1,0:T(8,128)(2,1)} %copy-done.1, ...), custom_call_target="tpu_custom_call", output_to_operand_aliasing={{0}: (9, {}), {1}: (10, {})} | custom-call | flops 2013265920 | bytes 12582912 | tf_op jit(solution)/shard_map/late/pallas_call | solution.py:502
  122.1 5.6 %down.3 = (bf16[2,2,256,384]{3,2,1,0:T(8,128)(2,1)}, bf16[2,2,256,384]{3,2,1,0:T(8,128)(2,1)}, bf16[2,2,256,384]{3,2,1,0:T(8,128)(2,1)}, bf16[2,2,256,384]{3,2,1,0:T(8,128)(2,1)}) custom-call(s32[4]{0:T(128)} %pad_add_fusion.place, bf16[4,320,2048]{2,1,0:T(8,128)(2,1)} %get-tuple-element.47.kept, bf16[4,320,384]{2,1,0:T(8,128)(2,1)} %get-tuple-element.48.scaled_in), custom_call_target="tpu_custom_call" | custom-call | flops 32212254720 | bytes 50331648 | tf_op jit(solution)/shard_map/down/pallas_call | solution.py:445
  127.8 1.6 collective-permute-start.9
  129.3 1.5 collective-permute-start.11
  130.8 5.6 %down.2 = (bf16[2,2,256,384]{3,2,1,0:T(8,128)(2,1)}, bf16[2,2,256,384]{3,2,1,0:T(8,128)(2,1)}, bf16[2,2,256,384]{3,2,1,0:T(8,128)(2,1)}, bf16[2,2,256,384]{3,2,1,0:T(8,128)(2,1)}) custom-call(s32[4]{0:T(128)} %pad_add_fusion.place, bf16[4,320,2048]{2,1,0:T(8,128)(2,1)} %get-tuple-element.47.kept, bf16[4,320,384]{2,1,0:T(8,128)(2,1)} %get-tuple-element.48.scaled_in), custom_call_target="tpu_custom_call" | custom-call | flops 32212254720 | bytes 50331648 | tf_op jit(solution)/shard_map/down/pallas_call | solution.py:445
  136.5 0.6 collective-permute-start.7
  137.0 0.5 collective-permute-start.8
  137.6 10.9 %collective-permute-done.9 = bf16[2,2,256,384]{3,2,1,0:T(8,128)(2,1)S(1)} collective-permute-done((bf16[2,2,256,384]{3,2,1,0:T(8,128)(2,1)}, bf16[2,2,256,384]{3,2,1,0:T(8,128)(2,1)S(1)}, u32[]{:S(2)}, u32[]{:S(2)}) %collective-permute-start.9) | collective-permute-done | bytes 786464 | tf_op jit(solution)/shard_map/ppermute | solution.py:467
  148.4 0.2 add_convert_fusion.1
  148.7 1.6 collective-permute-start.10
  150.3 0.2 add_convert_fusion
  150.5 1.6 collective-permute-start.12
  152.1 13.2 %collective-permute-done.7 = bf16[2,2,256,384]{3,2,1,0:T(8,128)(2,1)S(1)} collective-permute-done((bf16[2,2,256,384]{3,2,1,0:T(8,128)(2,1)}, bf16[2,2,256,384]{3,2,1,0:T(8,128)(2,1)S(1)}, u32[]{:S(2)}, u32[]{:S(2)}) %collective-permute-start.7) | collective-permute-done | bytes 786464 | tf_op jit(solution)/shard_map/ppermute | solution.py:467
  165.3 0.2 add_convert_fusion.3
  165.5 0.1 fusion
  165.6 1.6 collective-permute-start.13
  167.1 0.2 add_convert_fusion.2
  167.3 0.1 fusion.1
  167.4 1.6 collective-permute-start.14
  169.0 6.2 %collective-permute-done.10 = bf16[1,2,256,384]{3,2,1,0:T(8,128)(2,1)S(1)} collective-permute-done((bf16[1,2,256,384]{3,2,1,0:T(8,128)(2,1)S(1)}, bf16[1,2,256,384]{3,2,1,0:T(8,128)(2,1)S(1)}, u32[]{:S(2)}, u32[]{:S(2)}) %collective-permute-start.10) | collective-permute-done | bytes 393248 | tf_op jit(solution)/shard_map/ppermute | solution.py:467
  175.2 0.1 add_bitcast_fusion.3
  175.3 0.1 add_bitcast_fusion.2
  175.4 1.9 finish.1
  177.3 5.3 %collective-permute-done.13 = bf16[1,2,256,384]{3,2,1,0:T(8,128)(2,1)S(1)} collective-permute-done((bf16[1,2,256,384]{3,2,1,0:T(8,128)(2,1)S(1)}, bf16[1,2,256,384]{3,2,1,0:T(8,128)(2,1)S(1)}, u32[]{:S(2)}, u32[]{:S(2)}) %collective-permute-start.13) | collective-permute-done | bytes 393248 | tf_op jit(solution)/shard_map/ppermute | solution.py:467
  182.6 0.1 add_bitcast_fusion.1
  182.7 1.1 add_bitcast_fusion
  183.8 2.0 %maximum_maximum_fusion = f32[4,512,384]{2,1,0:T(8,128)} fusion(f32[2,256,384]{2,1,0:T(8,128)S(1)} %add_bitcast_fusion, f32[2,256,384]{2,1,0:T(8,128)S(1)} %add_bitcast_fusion.1, f32[2,256,384]{2,1,0:T(8,128)S(1)} %add_bitcast_fusion.2, f32[2,256,384]{2,1,0:T(8,128)S(1)} %add_bitcast_fusion.3), kind=kLoop, calls=%fused_computation | loop fusion | flops 2359296 | bytes 6291456 | tf_op jit(solution)/shard_map/concatenate | solution.py:544
  (34 shorter events, 0.3 us)
Async XLA Ops:
  7.2 62.5 %all-gather.2.cloned.1.call-start = ((), (), s32[]{:S(2)}) async-start(), calls=%async_computation.1 | async-start | bytes 5013504 | tf_op jit(solution)/shard_map/all_gather | solution.py:322
  9.2 166.2 %reduce-scatter.2.cloned.1.call-start = ((), (), s32[]{:S(2)}) async-start(), calls=%async_computation.2 | async-start | bytes 5013504 | tf_op jit(solution)/shard_map/reduce_scatter | solution.py:525
  9.3 2.3 %collective-permute-start = (bf16[128,2048]{1,0:T(8,128)(2,1)}, bf16[128,2048]{1,0:T(8,128)(2,1)S(1)}, u32[]{:S(2)}, u32[]{:S(2)}) collective-permute-start(bf16[128,2048]{1,0:T(8,128)(2,1)} %param.7), channel_id=1, source_target_pairs={{0,1},{1,0},{2,3},{3,2},{4,5},{5,4},{6,7},{7,6},{8,9},{9,8},{10,11... | collective-permute-start | bytes 1572872 | tf_op jit(solution)/shard_map/ppermute | solution.py:329
  11.6 11.9 %copy-start.6 = (bf16[256,2048]{1,0:T(8,128)(2,1)}, bf16[256,2048]{1,0:T(8,128)(2,1)S(1)}, u32[]{:S(2)}) copy-start(bf16[256,2048]{1,0:T(8,128)(2,1)S(1)} %constant_dynamic-update-slice_fusion.refs_0_) | copy-start | bytes 3145732
  11.6 33.2 %collective-permute-start.1 = (bf16[256,2048]{1,0:T(8,128)(2,1)S(1)}, bf16[256,2048]{1,0:T(8,128)(2,1)S(1)}, u32[]{:S(2)}, u32[]{:S(2)}) collective-permute-start(bf16[256,2048]{1,0:T(8,128)(2,1)S(1)} %constant_dynamic-update-slice_fusion.refs_0_), channel_id=1, source_target_pairs={{0,2},{2,4},{3,1},{4,6},{5,3},{7,5},{8,10},{10,12},{11,9},{12,14},... | collective-permute-start | bytes 3145736 | tf_op jit(solution)/shard_map/ppermute | solution.py:329
  44.8 35.3 %copy-start.7 = (bf16[256,2048]{1,0:T(8,128)(2,1)}, bf16[256,2048]{1,0:T(8,128)(2,1)S(1)}, u32[]{:S(2)}) copy-start(bf16[256,2048]{1,0:T(8,128)(2,1)S(1)} %collective-permute-done.1.refs_1_) | copy-start | bytes 3145732
  44.8 35.3 %collective-permute-start.2 = (bf16[256,2048]{1,0:T(8,128)(2,1)S(1)}, bf16[256,2048]{1,0:T(8,128)(2,1)S(1)}, u32[]{:S(2)}, u32[]{:S(2)}) collective-permute-start(bf16[256,2048]{1,0:T(8,128)(2,1)S(1)} %collective-permute-done.1.refs_1_), channel_id=1, source_target_pairs={{2,4},{3,1},{4,6},{5,3},{10,12},{11,9},{12,14},{13,11},{18,20},{19... | collective-permute-start | bytes 3145736 | tf_op jit(solution)/shard_map/ppermute | solution.py:329
  80.1 7.0 %copy-start.8 = (bf16[256,2048]{1,0:T(8,128)(2,1)}, bf16[256,2048]{1,0:T(8,128)(2,1)S(1)}, u32[]{:S(2)}) copy-start(bf16[256,2048]{1,0:T(8,128)(2,1)S(1)} %collective-permute-done.2.refs_2_) | copy-start | bytes 3145732
  80.1 4.6 %collective-permute-start.4 = (bf16[256,2048]{1,0:T(8,128)(2,1)S(1)}, bf16[256,2048]{1,0:T(8,128)(2,1)S(1)}, u32[]{:S(2)}, u32[]{:S(2)}) collective-permute-start(bf16[256,2048]{1,0:T(8,128)(2,1)S(1)} %collective-permute-done.1.refs_1_), channel_id=1, source_target_pairs={{1,0},{2,3},{3,2},{4,5},{5,4},{6,7},{9,8},{10,11},{11,10},{12,13},... | collective-permute-start | bytes 3145736 | tf_op jit(solution)/shard_map/ppermute | solution.py:329
  81.4 4.8 %collective-permute-start.5 = (bf16[256,2048]{1,0:T(8,128)(2,1)S(1)}, bf16[256,2048]{1,0:T(8,128)(2,1)S(1)}, u32[]{:S(2)}, u32[]{:S(2)}) collective-permute-start(bf16[256,2048]{1,0:T(8,128)(2,1)S(1)} %collective-permute-done.2.refs_2_), channel_id=1, source_target_pairs={{1,0},{3,2},{4,5},{6,7},{9,8},{11,10},{12,13},{14,15},{17,16},{19,... | collective-permute-start | bytes 3145736 | tf_op jit(solution)/shard_map/ppermute | solution.py:329
  82.7 22.1 %collective-permute-start.3 = (bf16[256,2048]{1,0:T(8,128)(2,1)S(1)}, bf16[256,2048]{1,0:T(8,128)(2,1)S(1)}, u32[]{:S(2)}, u32[]{:S(2)}) collective-permute-start(bf16[256,2048]{1,0:T(8,128)(2,1)S(1)} %collective-permute-done.2.refs_2_), channel_id=1, source_target_pairs={{3,1},{4,6},{11,9},{12,14},{19,17},{20,22},{27,25},{28,30}} | collective-permute-start | bytes 3145736 | tf_op jit(solution)/shard_map/ppermute | solution.py:329
  84.7 1.5 copy-start.9
  86.2 1.0 copy-start.10
  104.8 4.6 %copy-start = (bf16[256,2048]{1,0:T(8,128)(2,1)}, bf16[256,2048]{1,0:T(8,128)(2,1)S(1)}, u32[]{:S(2)}) copy-start(bf16[256,2048]{1,0:T(8,128)(2,1)S(1)} %collective-permute-done.3.mine) | copy-start | bytes 3145732
  104.8 4.6 %collective-permute-start.6 = (bf16[256,2048]{1,0:T(8,128)(2,1)S(1)}, bf16[256,2048]{1,0:T(8,128)(2,1)S(1)}, u32[]{:S(2)}, u32[]{:S(2)}) collective-permute-start(bf16[256,2048]{1,0:T(8,128)(2,1)S(1)} %collective-permute-done.3.mine), channel_id=1, source_target_pairs={{1,0},{6,7},{9,8},{14,15},{17,16},{22,23},{25,24},{30,31}} | collective-permute-start | bytes 3145736 | tf_op jit(solution)/shard_map/ppermute | solution.py:329
  109.4 1.0 copy-start.1
  127.8 20.7 %collective-permute-start.9 = (bf16[2,2,256,384]{3,2,1,0:T(8,128)(2,1)}, bf16[2,2,256,384]{3,2,1,0:T(8,128)(2,1)S(1)}, u32[]{:S(2)}, u32[]{:S(2)}) collective-permute-start(bf16[2,2,256,384]{3,2,1,0:T(8,128)(2,1)} %get-tuple-element.56), channel_id=1, source_target_pairs={{0,8},{8,0},{16,24},{24,16},{1,9},{9,1},{17,25},{25,17},{2,10},{10... | collective-permute-start | bytes 2359304 | tf_op jit(solution)/shard_map/ppermute | solution.py:467
  129.3 19.1 %copy-start.5 = (bf16[2,2,256,384]{3,2,1,0:T(8,128)(2,1)S(1)}, bf16[2,2,256,384]{3,2,1,0:T(8,128)(2,1)}, u32[]{:S(2)}) copy-start(bf16[2,2,256,384]{3,2,1,0:T(8,128)(2,1)} %get-tuple-element.55) | copy-start | bytes 2359300
  129.3 20.9 %collective-permute-start.11 = (bf16[2,2,256,384]{3,2,1,0:T(8,128)(2,1)}, bf16[2,2,256,384]{3,2,1,0:T(8,128)(2,1)S(1)}, u32[]{:S(2)}, u32[]{:S(2)}) collective-permute-start(bf16[2,2,256,384]{3,2,1,0:T(8,128)(2,1)} %get-tuple-element.58), channel_id=1, source_target_pairs={{0,16},{8,24},{16,0},{24,8},{1,17},{9,25},{17,1},{25,9},{2,18},{10... | collective-permute-start | bytes 2359304 | tf_op jit(solution)/shard_map/ppermute | solution.py:467
  136.4 13.8 %copy-start.4 = (bf16[2,2,256,384]{3,2,1,0:T(8,128)(2,1)S(1)}, bf16[2,2,256,384]{3,2,1,0:T(8,128)(2,1)}, u32[]{:S(2)}) copy-start(bf16[2,2,256,384]{3,2,1,0:T(8,128)(2,1)} %get-tuple-element.57) | copy-start | bytes 2359300
  136.5 28.8 %collective-permute-start.7 = (bf16[2,2,256,384]{3,2,1,0:T(8,128)(2,1)}, bf16[2,2,256,384]{3,2,1,0:T(8,128)(2,1)S(1)}, u32[]{:S(2)}, u32[]{:S(2)}) collective-permute-start(bf16[2,2,256,384]{3,2,1,0:T(8,128)(2,1)} %get-tuple-element.50), channel_id=1, source_target_pairs={{0,8},{8,0},{16,24},{24,16},{1,9},{9,1},{17,25},{25,17},{2,10},{10... | collective-permute-start | bytes 2359304 | tf_op jit(solution)/shard_map/ppermute | solution.py:467
  137.0 30.1 %collective-permute-start.8 = (bf16[2,2,256,384]{3,2,1,0:T(8,128)(2,1)}, bf16[2,2,256,384]{3,2,1,0:T(8,128)(2,1)S(1)}, u32[]{:S(2)}, u32[]{:S(2)}) collective-permute-start(bf16[2,2,256,384]{3,2,1,0:T(8,128)(2,1)} %get-tuple-element.52), channel_id=1, source_target_pairs={{0,16},{8,24},{16,0},{24,8},{1,17},{9,25},{17,1},{25,9},{2,18},{10... | collective-permute-start | bytes 2359304 | tf_op jit(solution)/shard_map/ppermute | solution.py:467
  148.4 16.9 %copy-start.3 = (bf16[2,2,256,384]{3,2,1,0:T(8,128)(2,1)S(1)}, bf16[2,2,256,384]{3,2,1,0:T(8,128)(2,1)}, u32[]{:S(2)}) copy-start(bf16[2,2,256,384]{3,2,1,0:T(8,128)(2,1)} %get-tuple-element.49) | copy-start | bytes 2359300
  148.7 26.6 %collective-permute-start.10 = (bf16[1,2,256,384]{3,2,1,0:T(8,128)(2,1)S(1)}, bf16[1,2,256,384]{3,2,1,0:T(8,128)(2,1)S(1)}, u32[]{:S(2)}, u32[]{:S(2)}) collective-permute-start(bf16[1,2,256,384]{3,2,1,0:T(8,128)(2,1)S(1)} %slice.35), channel_id=1, source_target_pairs={{0,16},{8,24},{16,0},{24,8},{1,17},{9,25},{17,1},{25,9},{2,18},{10... | collective-permute-start | bytes 1179656 | tf_op jit(solution)/shard_map/ppermute | solution.py:467
  150.2 16.9 %copy-start.2 = (bf16[2,2,256,384]{3,2,1,0:T(8,128)(2,1)S(1)}, bf16[2,2,256,384]{3,2,1,0:T(8,128)(2,1)}, u32[]{:S(2)}) copy-start(bf16[2,2,256,384]{3,2,1,0:T(8,128)(2,1)} %get-tuple-element.51) | copy-start | bytes 2359300
  150.5 24.8 %collective-permute-start.12 = (bf16[1,2,256,384]{3,2,1,0:T(8,128)(2,1)S(1)}, bf16[1,2,256,384]{3,2,1,0:T(8,128)(2,1)S(1)}, u32[]{:S(2)}, u32[]{:S(2)}) collective-permute-start(bf16[1,2,256,384]{3,2,1,0:T(8,128)(2,1)S(1)} %slice.37), channel_id=1, source_target_pairs={{0,8},{8,0},{16,24},{24,16},{1,9},{9,1},{17,25},{25,17},{2,10},{10... | collective-permute-start | bytes 1179656 | tf_op jit(solution)/shard_map/ppermute | solution.py:467
  165.6 17.0 %collective-permute-start.13 = (bf16[1,2,256,384]{3,2,1,0:T(8,128)(2,1)S(1)}, bf16[1,2,256,384]{3,2,1,0:T(8,128)(2,1)S(1)}, u32[]{:S(2)}, u32[]{:S(2)}) collective-permute-start(bf16[1,2,256,384]{3,2,1,0:T(8,128)(2,1)S(1)} %get-tuple-element.61), channel_id=1, source_target_pairs={{0,16},{8,24},{16,0},{24,8},{1,17},{9,25},{17,1},{25,9},{2,18},{10... | collective-permute-start | bytes 1179656 | tf_op jit(solution)/shard_map/ppermute | solution.py:467
  167.4 15.2 %collective-permute-start.14 = (bf16[1,2,256,384]{3,2,1,0:T(8,128)(2,1)S(1)}, bf16[1,2,256,384]{3,2,1,0:T(8,128)(2,1)}, u32[]{:S(2)}, u32[]{:S(2)}) collective-permute-start(bf16[1,2,256,384]{3,2,1,0:T(8,128)(2,1)S(1)} %get-tuple-element.63), channel_id=1, source_target_pairs={{0,8},{8,0},{16,24},{24,16},{1,9},{9,1},{17,25},{25,17},{2,10},{10... | collective-permute-start | bytes 1179656 | tf_op jit(solution)/shard_map/ppermute | solution.py:467
Sparse Core Ops, SparseCore 0:
  9.6 59.9 all-gather.1
  122.3 50.6 reduce-scatter.1

commit v11 on v9

--- a/solution.py
+++ b/solution.py
@@ -1,4 +1,5 @@
 import functools
+import math
 
 import jax
 import jax.numpy as jnp
@@ -10,10 +11,11 @@
 LANES = 128
 PACK = 16
 GROUP = 2
-VMEM_LIMIT = 60 * 1024 * 1024
+SLACK = 6 * 1024 * 1024
 bf16, f32 = jnp.bfloat16, jnp.float32
 ANY = pl.BlockSpec(memory_space=pl.ANY)
 SMEM = pl.BlockSpec(memory_space=pltpu.SMEM)
+VMEM = pl.BlockSpec(memory_space=pltpu.VMEM)
 FIRST = (((0,), (0,)), ((), ()))
 
 
@@ -83,10 +85,9 @@
 
 def up_kernel(groups, width, top, cap, after, place, x_all, w_up, *refs):
     refs = refs[after:]
-    pick_out, meta, hid_out, scaled_out, slope_out, rows, w_v, held, gates, pick, hid, scaled, slope, sems, out_sem = refs
+    pick_out, meta, hid_out, scaled_out, slope_out, rows, held, gates, pick, hid, scaled, slope, sems, out_sem = refs
     experts, members = held.shape[0], rows.shape[1]
     arrive = copy_all([(x_all.at[pl.ds(g * members, members), :], rows.at[g]) for g in range(groups)], sems.at[0])
-    weights = copy_all([(w_up.at[b], w_v.at[b]) for b in range(experts)], sems.at[1])
     before = lax.broadcasted_iota(jnp.int32, (members, members), 0) < lax.broadcasted_iota(
         jnp.int32, (members, members), 1
     )
@@ -115,8 +116,7 @@
             held[b, pl.ds(g * cap, cap), :] = got[b * cap : (b + 1) * cap]
     outs = copy_all([(pick, pick_out)], out_sem.at[3])
     for b in range(experts):
-        weights[b].wait()
-        pre = dot(held[b], w_v[b])
+        pre = dot(held[b], w_up[b])
         gate = gates[b][:, :1]
         sig = 0.5 + 0.5 * jnp.tanh(0.5 * pre)
         act = pre * sig
@@ -162,17 +162,11 @@
 def tail_kernel(groups, cap, width, top, place, *refs):
     steps = groups - 1
     own, mine, other, refs = refs[0], refs[1 : 1 + steps], refs[1 + steps : 1 + 2 * steps], refs[1 + 2 * steps :]
-    pick_in, w_down, w_flip, hid_in, slope_in, meta, out_all, kept = refs[:8]
-    pick, moved, held, grads, out, down_v, flip_v, hid, slope, block_sem, sems, keep_sem, out_sem = refs[8:]
+    pick, w_down, w_flip, hid, slope, meta, out_all, kept = refs[:8]
+    moved, held, grads, out, block_sem, keep_sem, out_sem = refs[8:]
     experts, members = held.shape[0], moved.shape[1]
     half = members // 2
-    first_pick = copy_all([(pick_in, pick)], sems.at[0])
     start_blocks(place, groups, own, mine, other, moved, block_sem)
-    loads = [
-        copy_all([(src.at[b], dst.at[b]) for b in range(experts)], sems.at[n])
-        for n, (src, dst) in enumerate(((w_down, down_v), (hid_in, hid), (slope_in, slope), (w_flip, flip_v)), 1)
-    ]
-    first_pick[0].wait()
     for slot in range(groups):
         for part in range(2):
             at = pl.ds(part * half, half)
@@ -185,14 +179,11 @@
     keep = copy_all([(held.at[b], kept.at[b]) for b in range(experts)], keep_sem)
     lane = lax.broadcasted_iota(jnp.int32, (groups * cap, LANES), 1)
     for b in range(experts):
-        for load in loads[:3]:
-            load[b].wait()
-        back = dot(held[b], down_v[b])
+        back = dot(held[b], w_down[b])
         gate = jnp.sum(back * hid[b].astype(f32), axis=1, keepdims=True)
         gate = jnp.where(lane == b, gate, 0.0).astype(bf16)
         grad = (back * slope[b].astype(f32)).astype(bf16)
-        loads[3][b].wait()
-        route = dot(grad, flip_v[b]).astype(bf16)
+        route = dot(grad, w_flip[b]).astype(bf16)
         for g in range(groups):
             grads[g, pl.ds(b * cap, cap), pl.ds(0, width)] = route[g * cap : (g + 1) * cap]
             grads[g, pl.ds(b * cap, cap), pl.ds(width, LANES)] = gate[g * cap : (g + 1) * cap]
@@ -248,7 +239,7 @@
     x_own = pl.pallas_call(
         functools.partial(pack_kernel, top),
         out_shape=shape(tok_rows, full),
-        compiler_params=pltpu.CompilerParams(vmem_limit_bytes=VMEM_LIMIT),
+        compiler_params=pltpu.CompilerParams(vmem_limit_bytes=SLACK * 4),
         cost_estimate=cost(0, 4 * tok_rows * width),
         name="pack",
     )(tokens, expert_ids.T, gate_weights.T)
@@ -275,6 +266,24 @@
 
     def by_expert(rows, n):
         return pl.BlockSpec((1, rows, n), lambda i, *_: (at_expert(i), 0, 0))
+
+    def one(kernel, name, flops, nbytes, in_specs, out_specs, out_shape, scratch_shapes):
+        def run(*args):
+            held = [x.inner_aval if hasattr(x, "inner_aval") else x for x in scratch_shapes]
+            held += [x for x, spec in zip((*args, *out_shape), (*in_specs, *out_specs)) if spec is VMEM]
+            room = sum(math.prod(x.shape) * jnp.dtype(x.dtype).itemsize for x in held if hasattr(x, "dtype") and jnp.issubdtype(x.dtype, jnp.floating))
+            return pl.pallas_call(
+                kernel,
+                in_specs=in_specs,
+                out_specs=out_specs,
+                out_shape=out_shape,
+                scratch_shapes=scratch_shapes,
+                compiler_params=pltpu.CompilerParams(vmem_limit_bytes=room + SLACK),
+                cost_estimate=cost(flops, nbytes),
+                name=name,
+            )(*args)
+
+        return run
 
     def call(kernel, name, grid, flops, nbytes, in_specs, out_specs, out_shape, scratch_shapes, prefetch=0):
         return pl.pallas_call(
@@ -287,7 +296,7 @@
                 scratch_shapes=scratch_shapes,
             ),
             out_shape=out_shape,
-            compiler_params=pltpu.CompilerParams(vmem_limit_bytes=VMEM_LIMIT),
+            compiler_params=pltpu.CompilerParams(vmem_limit_bytes=SLACK * 4),
             cost_estimate=cost(flops, nbytes),
             name=name,
         )
@@ -328,29 +337,16 @@
     pick_v = pltpu.VMEM((groups, experts * cap, members), bf16)
     most = max(experts, groups)
 
-    def one(kernel, name, flops, nbytes, in_specs, out_specs, out_shape, scratch_shapes):
-        return pl.pallas_call(
-            kernel,
-            in_specs=in_specs,
-            out_specs=out_specs,
-            out_shape=out_shape,
-            scratch_shapes=scratch_shapes,
-            compiler_params=pltpu.CompilerParams(vmem_limit_bytes=VMEM_LIMIT),
-            cost_estimate=cost(flops, nbytes),
-            name=name,
-        )
-
     pick, meta, hid, scaled, slope_g = one(
         functools.partial(up_kernel, groups, width, top, cap, 0),
         "up",
         pick_flops + main_flops,
         2 * total * full + row_bytes,
-        [SMEM, ANY, ANY],
-        [ANY, pl.BlockSpec(memory_space=pltpu.VMEM), ANY, ANY, ANY],
+        [SMEM, ANY, VMEM],
+        [ANY, VMEM, ANY, ANY, ANY],
         [shape(groups, experts * cap, members), shape(total, LANES), act, act, act],
         [
             pltpu.VMEM((groups, members, full), bf16),
-            pltpu.VMEM((experts, width, hidden), bf16),
             pltpu.VMEM((experts, routes, width), bf16),
             pltpu.VMEM((experts, routes, LANES), f32),
             pick_v,
@@ -410,21 +406,15 @@
         "tail",
         8 * main_flops,
         4 * row_bytes,
-        [SMEM] + [ANY] * (2 * groups - 1) + [ANY] * 5 + [pl.BlockSpec(memory_space=pltpu.VMEM)],
+        [SMEM] + [ANY] * (2 * groups - 1) + [VMEM] * 6,
         [ANY, ANY],
         [shape(total, full), shape(experts, routes, width)],
         [
-            pick_v,
             pltpu.VMEM((groups, members, width), bf16),
             pltpu.VMEM((experts, routes, width), bf16),
             pltpu.VMEM((groups, experts * cap, full), bf16),
             pltpu.VMEM((groups, members, full), bf16),
-            pltpu.VMEM((experts, width, hidden), bf16),
-            pltpu.VMEM((experts, hidden, width), bf16),
-            act3,
-            act3,
             pltpu.SemaphoreType.DMA((groups, 2)),
-            pltpu.SemaphoreType.DMA((5, experts)),
             pltpu.SemaphoreType.DMA((experts,)),
             pltpu.SemaphoreType.DMA((groups,)),
         ],
@@ -433,7 +423,7 @@
     token_grad, gate_grad = pl.pallas_call(
         functools.partial(finish_kernel, width, top),
         out_shape=[shape(tok_rows, width), shape(top, tok_rows)],
-        compiler_params=pltpu.CompilerParams(vmem_limit_bytes=VMEM_LIMIT),
+        compiler_params=pltpu.CompilerParams(vmem_limit_bytes=SLACK * 4),
         cost_estimate=cost(0, 4 * tok_rows * width),
         name="finish",
     )(summed)

time: 191 us -> 206 us (1.079)
  local copies, waits for them, and re-layouts: 2.31 us -> 22 us
  waiting for transfers between devices: 98 us -> 92.6 us
  Pallas kernels: 50.5 us -> 52.6 us
    unnamed x23 -> x25, local copies, waits for them, and re-layouts: 2.11 us -> 21.8 us
    pallas_call x4, Pallas kernels: 39.7 us -> 48.9 us  [run(): pl.pallas_call(kernel, in_specs=in_specs, out_specs=out_specs, out_shape=...]
    pallas_call x1, Pallas kernels: 6.99 us -> 1.94 us  [shards(): call(flip_kernel, 'flip', experts, 0, 2 * row_bytes, in_specs=[pl.BlockSp...]
    ppermute x8, waiting for transfers between devices: 38.1 us -> 33.3 us  [exchange(): got = lax.ppermute(send, 'dp', [(i, i ^ bit) for i in range(dp_count)])]
  transfers between devices with their start and end apart: 17 -> 17, of which waited for: 9 -> 9; matrix products, arithmetic and copies ran while one was open for 2% -> 1% of each run, Pallas kernels for 15% -> 16%
where the time goes in v11:
time: 206 us
  waiting for transfers between devices  92.6 us (45%)
  Pallas kernels  52.6 us (26%)
  local copies, waits for them, and re-layouts  22 us (11%)
  starting transfers between devices  21.3 us (10%)
  between operations  14.3 us (7%)
  other arithmetic  3.09 us (2%)
    pallas_call x4, Pallas kernels, run(): pl.pallas_call(kernel, in_specs=in_specs, out_specs=out_specs, out_shape=...  48.9 us
    ppermute x7, waiting for transfers between devices, hop(): return lax.ppermute(value, 'ep', pairs)  36.6 us
    ppermute x8, waiting for transfers between devices, exchange(): got = lax.ppermute(send, 'dp', [(i, i ^ bit) for i in range(dp_count)])  33.3 us
    all_gather x1, waiting for transfers between devices, shards(): x_all = lax.all_gather(x_own, 'ep', axis=0, tiled=True)  22.7 us
    unnamed x25, local copies, waits for them, and re-layouts  21.8 us
    ppermute x7, starting transfers between devices, hop(): return lax.ppermute(value, 'ep', pairs)  10.7 us
    ppermute x8, starting transfers between devices, exchange(): got = lax.ppermute(send, 'dp', [(i, i ^ bit) for i in range(dp_count)])  10.5 us
  transfers between devices with their start and end apart: 17, of which 9 were waited for; matrix products, arithmetic and copies ran while one was open for 1% of the time, Pallas kernels for 16%

profile of v11, /device:TPU:0, one launch (start us, length us, event | category | flops | bytes accessed | tf_op | source)
XLA Modules:
  0.0 205.9 jit_solution(9814762248183556454)
XLA Ops:
  7.2 1.0 copy-done.5
  8.3 0.7 copy-done.6
  8.9 0.7 copy-done.7
  9.6 0.9 pack.1
  10.6 0.5 collective-permute-start
  11.1 1.1 constant_dynamic-update-slice_fusion.1
  12.2 0.7 collective-permute-done
  12.9 4.9 %collective-permute-start.1 = (bf16[256,2048]{1,0:T(8,128)(2,1)S(1)}, bf16[256,2048]{1,0:T(8,128)(2,1)S(1)}, u32[]{:S(2)}, u32[]{:S(2)}) collective-permute-start(bf16[256,2048]{1,0:T(8,128)(2,1)S(1)} %constant_dynamic-update-slice_fusion.refs_0_), channel_id=1, source_target_pairs={{0,2},{2,4},{3,1},{4,6},{5,3},{7,5},{8,10},{10,12},{11,9},{12,14},... | collective-permute-start | bytes 3145736 | tf_op jit(solution)/shard_map/ppermute | solution.py:253
  17.8 3.0 %copy-done = bf16[4,2048,384]{2,1,0:T(8,128)(2,1)S(1)} copy-done((bf16[4,2048,384]{2,1,0:T(8,128)(2,1)S(1)}, bf16[4,2048,384]{2,1,0:T(8,128)(2,1)}, u32[]{:S(2)}) %copy-start) | copy-done | bytes 6291480
  20.8 1.9 flip.1.refs_9_
  22.8 2.6 %copy-done.2 = bf16[4,384,2048]{2,1,0:T(8,128)(2,1)} copy-done((bf16[4,384,2048]{2,1,0:T(8,128)(2,1)}, bf16[4,384,2048]{2,1,0:T(8,128)(2,1)S(1)}, u32[]{:S(2)}) %copy-start.2) | copy-done | bytes 6291480
  25.4 21.3 %collective-permute-done.1.refs_1_ = bf16[256,2048]{1,0:T(8,128)(2,1)S(1)} collective-permute-done((bf16[256,2048]{1,0:T(8,128)(2,1)S(1)}, bf16[256,2048]{1,0:T(8,128)(2,1)S(1)}, u32[]{:S(2)}, u32[]{:S(2)}) %collective-permute-start.1) | collective-permute-done | bytes 1048608 | tf_op jit(solution)/shard_map/ppermute | solution.py:253
  46.7 0.7 collective-permute-start.2
  47.5 22.7 %all-gather.2.cloned.1.call-done.x_all = bf16[1024,2176]{1,0:T(8,128)(2,1)} async-done(((bf16[128,2176]{1,0:T(8,128)(2,1)}), bf16[1024,2176]{1,0:T(8,128)(2,1)}) %all-gather.2.cloned.1.call-update) | async-done | bytes 4456464 | tf_op jit(solution)/shard_map/all_gather | solution.py:246
  70.2 2.8 %copy-done.1 = bf16[4,2048,384]{2,1,0:T(8,128)(2,1)S(1)} copy-done((bf16[4,2048,384]{2,1,0:T(8,128)(2,1)S(1)}, bf16[4,2048,384]{2,1,0:T(8,128)(2,1)}, u32[]{:S(2)}) %copy-start.1) | copy-done | bytes 6291480
  73.0 2.3 %copy-done.8 = bf16[1024,2176]{1,0:T(8,128)(2,1)S(1)} copy-done((bf16[1024,2176]{1,0:T(8,128)(2,1)S(1)}, bf16[1024,2176]{1,0:T(8,128)(2,1)}, u32[]{:S(2)}) %copy-start.8) | copy-done | bytes 4456472
  75.3 12.0 %up.1 = (bf16[4,320,256]{2,1,0:T(8,128)(2,1)S(1)}, bf16[1024,128]{1,0:T(8,128)(2,1)S(1)}, bf16[4,320,384]{2,1,0:T(8,128)(2,1)S(1)}, bf16[4,320,384]{2,1,0:T(8,128)(2,1)S(1)}, bf16[4,320,384]{2,1,0:T(8,128)(2,1)S(1)}) custom-call(s32[4]{0:T(128)S(1)} %pad_add_fusion.place, bf16[1024,2176]{1,0:T(8,128)(2,1)S(1)} %copy-done.8, bf16[4,2048,384]{2,1,0:T(8,128)(2,1)S(1)} %copy-done.1), custom_call_target="tpu_custom_call" | custom-call | flops 3355443200 | bytes 10747904 | tf_op jit(solution)/shard_map/up/pallas_call | solution.py:275
  87.3 0.9 copy-done.9
  88.3 0.7 collective-permute-start.3
  89.0 1.3 collective-permute-start.5
  90.3 1.3 collective-permute-start.4
  91.6 1.3 collective-permute-start.6
  92.9 2.1 %collective-permute-done.4.refs_4_ = bf16[256,2048]{1,0:T(8,128)(2,1)S(1)} collective-permute-done((bf16[256,2048]{1,0:T(8,128)(2,1)S(1)}, bf16[256,2048]{1,0:T(8,128)(2,1)S(1)}, u32[]{:S(2)}, u32[]{:S(2)}) %collective-permute-start.4) | collective-permute-done | bytes 1048608 | tf_op jit(solution)/shard_map/ppermute | solution.py:253
  95.1 12.4 %collective-permute-done.6.refs_6_ = bf16[256,2048]{1,0:T(8,128)(2,1)S(1)} collective-permute-done((bf16[256,2048]{1,0:T(8,128)(2,1)S(1)}, bf16[256,2048]{1,0:T(8,128)(2,1)S(1)}, u32[]{:S(2)}, u32[]{:S(2)}) %collective-permute-start.6) | collective-permute-done | bytes 1048608 | tf_op jit(solution)/shard_map/ppermute | solution.py:253
  107.5 17.7 %tail.1 = (bf16[1024,2176]{1,0:T(8,128)(2,1)S(1)}, bf16[4,320,2048]{2,1,0:T(8,128)(2,1)}) custom-call(s32[4]{0:T(128)S(1)} %pad_add_fusion.place, bf16[256,2048]{1,0:T(8,128)(2,1)S(1)} %constant_dynamic-update-slice_fusion.refs_0_, bf16[256,2048]{1,0:T(8,128)(2,1)S(1)} %collective-permute-done.1.refs_1_, ...), custom_call_target="tpu_custom_call" | custom-call | flops 16106127360 | bytes 25165824 | tf_op jit(solution)/shard_map/tail/pallas_call | solution.py:275
  125.2 2.0 copy-done.3
  127.3 1.2 copy-done.10
  128.5 2.5 %copy-done.11 = bf16[4,320,2048]{2,1,0:T(8,128)(2,1)S(1)} copy-done((bf16[4,320,2048]{2,1,0:T(8,128)(2,1)S(1)}, bf16[4,320,2048]{2,1,0:T(8,128)(2,1)}, u32[]{:S(2)}) %copy-start.11) | copy-done | bytes 5242904
  130.9 9.6 %down.3 = (bf16[2,2,256,384]{3,2,1,0:T(8,128)(2,1)S(1)}, bf16[2,2,256,384]{3,2,1,0:T(8,128)(2,1)S(1)}, bf16[2,2,256,384]{3,2,1,0:T(8,128)(2,1)S(1)}, bf16[2,2,256,384]{3,2,1,0:T(8,128)(2,1)S(1)}) custom-call(s32[4]{0:T(128)S(1)} %pad_add_fusion.place, bf16[4,320,2048]{2,1,0:T(8,128)(2,1)S(1)} %copy-done.11, bf16[4,320,384]{2,1,0:T(8,128)(2,1)S(1)} %copy-done.10), custom_call_target="tpu_custom_call" | custom-call | flops 32212254720 | bytes 50331648 | tf_op jit(solution)/shard_map/down/pallas_call | solution.py:275
  140.5 1.6 collective-permute-start.11
  142.1 1.5 collective-permute-start.13
  143.6 9.6 %down.2 = (bf16[2,2,256,384]{3,2,1,0:T(8,128)(2,1)S(1)}, bf16[2,2,256,384]{3,2,1,0:T(8,128)(2,1)S(1)}, bf16[2,2,256,384]{3,2,1,0:T(8,128)(2,1)S(1)}, bf16[2,2,256,384]{3,2,1,0:T(8,128)(2,1)S(1)}) custom-call(s32[4]{0:T(128)S(1)} %pad_add_fusion.place, bf16[4,320,2048]{2,1,0:T(8,128)(2,1)S(1)} %copy-done.11, bf16[4,320,384]{2,1,0:T(8,128)(2,1)S(1)} %copy-done.10), custom_call_target="tpu_custom_call" | custom-call | flops 32212254720 | bytes 50331648 | tf_op jit(solution)/shard_map/down/pallas_call | solution.py:275
  153.2 0.6 collective-permute-start.7
  153.8 0.5 collective-permute-start.9
  154.3 6.7 %collective-permute-done.11 = bf16[2,2,256,384]{3,2,1,0:T(8,128)(2,1)S(1)} collective-permute-done((bf16[2,2,256,384]{3,2,1,0:T(8,128)(2,1)S(1)}, bf16[2,2,256,384]{3,2,1,0:T(8,128)(2,1)S(1)}, u32[]{:S(2)}, u32[]{:S(2)}) %collective-permute-start.11) | collective-permute-done | bytes 786464 | tf_op jit(solution)/shard_map/ppermute | solution.py:396
  161.0 0.2 add_convert_fusion.1
  161.2 1.6 collective-permute-start.12
  162.8 0.2 add_convert_fusion
  163.1 1.6 collective-permute-start.14
  164.6 13.2 %collective-permute-done.7 = bf16[2,2,256,384]{3,2,1,0:T(8,128)(2,1)S(1)} collective-permute-done((bf16[2,2,256,384]{3,2,1,0:T(8,128)(2,1)S(1)}, bf16[2,2,256,384]{3,2,1,0:T(8,128)(2,1)S(1)}, u32[]{:S(2)}, u32[]{:S(2)}) %collective-permute-start.7) | collective-permute-done | bytes 786464 | tf_op jit(solution)/shard_map/ppermute | solution.py:396
  178.1 1.6 collective-permute-start.8
  179.7 0.2 add_convert_fusion.2
  179.9 1.6 collective-permute-start.10
  181.5 6.3 %collective-permute-done.12 = bf16[1,2,256,384]{3,2,1,0:T(8,128)(2,1)S(1)} collective-permute-done((bf16[1,2,256,384]{3,2,1,0:T(8,128)(2,1)S(1)}, bf16[1,2,256,384]{3,2,1,0:T(8,128)(2,1)S(1)}, u32[]{:S(2)}, u32[]{:S(2)}) %collective-permute-start.12) | collective-permute-done | bytes 393248 | tf_op jit(solution)/shard_map/ppermute | solution.py:396
  188.0 7.1 %collective-permute-done.8 = bf16[1,2,256,384]{3,2,1,0:T(8,128)(2,1)S(1)} collective-permute-done((bf16[1,2,256,384]{3,2,1,0:T(8,128)(2,1)S(1)}, bf16[1,2,256,384]{3,2,1,0:T(8,128)(2,1)S(1)}, u32[]{:S(2)}, u32[]{:S(2)}) %collective-permute-start.8) | collective-permute-done | bytes 393248 | tf_op jit(solution)/shard_map/ppermute | solution.py:396
  195.3 1.0 copy-done.4
  196.4 0.8 finish.1
  197.2 1.9 maximum_maximum_fusion
  (35 shorter events, 1.0 us)
Async XLA Ops:
  7.2 63.1 %all-gather.2.cloned.1.call-start = ((), (), s32[]{:S(2)}) async-start(), calls=%async_computation.1 | async-start | bytes 5013504 | tf_op jit(solution)/shard_map/all_gather | solution.py:246
  7.2 1.0 copy-start.5
  8.3 0.7 copy-start.6
  8.9 0.7 copy-start.7
  10.6 184.8 %reduce-scatter.2.cloned.1.call-start = ((), (), s32[]{:S(2)}) async-start(), calls=%async_computation.2 | async-start | bytes 5013504 | tf_op jit(solution)/shard_map/reduce_scatter | solution.py:422
  10.6 2.3 %collective-permute-start = (bf16[128,2048]{1,0:T(8,128)(2,1)}, bf16[128,2048]{1,0:T(8,128)(2,1)S(1)}, u32[]{:S(2)}, u32[]{:S(2)}) collective-permute-start(bf16[128,2048]{1,0:T(8,128)(2,1)} %param.7), channel_id=1, source_target_pairs={{0,1},{1,0},{2,3},{3,2},{4,5},{5,4},{6,7},{7,6},{8,9},{9,8},{10,11... | collective-permute-start | bytes 1572872 | tf_op jit(solution)/shard_map/ppermute | solution.py:253
  12.9 33.8 %collective-permute-start.1 = (bf16[256,2048]{1,0:T(8,128)(2,1)S(1)}, bf16[256,2048]{1,0:T(8,128)(2,1)S(1)}, u32[]{:S(2)}, u32[]{:S(2)}) collective-permute-start(bf16[256,2048]{1,0:T(8,128)(2,1)S(1)} %constant_dynamic-update-slice_fusion.refs_0_), channel_id=1, source_target_pairs={{0,2},{2,4},{3,1},{4,6},{5,3},{7,5},{8,10},{10,12},{11,9},{12,14},... | collective-permute-start | bytes 3145736 | tf_op jit(solution)/shard_map/ppermute | solution.py:253
  17.8 3.0 %copy-start = (bf16[4,2048,384]{2,1,0:T(8,128)(2,1)S(1)}, bf16[4,2048,384]{2,1,0:T(8,128)(2,1)}, u32[]{:S(2)}) copy-start(bf16[4,2048,384]{2,1,0:T(8,128)(2,1)} %w_up.1) | copy-start | bytes 18874372
  22.8 2.6 %copy-start.2 = (bf16[4,384,2048]{2,1,0:T(8,128)(2,1)}, bf16[4,384,2048]{2,1,0:T(8,128)(2,1)S(1)}, u32[]{:S(2)}) copy-start(bf16[4,384,2048]{2,1,0:T(8,128)(2,1)S(1)} %flip.1.refs_9_) | copy-start | bytes 18874372
  46.7 41.5 %collective-permute-start.2 = (bf16[256,2048]{1,0:T(8,128)(2,1)S(1)}, bf16[256,2048]{1,0:T(8,128)(2,1)S(1)}, u32[]{:S(2)}, u32[]{:S(2)}) collective-permute-start(bf16[256,2048]{1,0:T(8,128)(2,1)S(1)} %collective-permute-done.1.refs_1_), channel_id=1, source_target_pairs={{2,4},{3,1},{4,6},{5,3},{10,12},{11,9},{12,14},{13,11},{18,20},{19... | collective-permute-start | bytes 3145736 | tf_op jit(solution)/shard_map/ppermute | solution.py:253
  70.2 2.8 %copy-start.1 = (bf16[4,2048,384]{2,1,0:T(8,128)(2,1)S(1)}, bf16[4,2048,384]{2,1,0:T(8,128)(2,1)}, u32[]{:S(2)}) copy-start(bf16[4,2048,384]{2,1,0:T(8,128)(2,1)} %w_up.1) | copy-start | bytes 18874372
  73.0 2.3 %copy-start.8 = (bf16[1024,2176]{1,0:T(8,128)(2,1)S(1)}, bf16[1024,2176]{1,0:T(8,128)(2,1)}, u32[]{:S(2)}) copy-start(bf16[1024,2176]{1,0:T(8,128)(2,1)} %all-gather.2.cloned.1.call-done.x_all) | copy-start | bytes 13369348
  87.3 0.9 copy-start.9
  88.3 3.3 %collective-permute-start.3 = (bf16[256,2048]{1,0:T(8,128)(2,1)S(1)}, bf16[256,2048]{1,0:T(8,128)(2,1)S(1)}, u32[]{:S(2)}, u32[]{:S(2)}) collective-permute-start(bf16[256,2048]{1,0:T(8,128)(2,1)S(1)} %collective-permute-done.2.refs_2_), channel_id=1, source_target_pairs={{3,1},{4,6},{11,9},{12,14},{19,17},{20,22},{27,25},{28,30}} | collective-permute-start | bytes 3145736 | tf_op jit(solution)/shard_map/ppermute | solution.py:253
  89.0 6.1 %collective-permute-start.5 = (bf16[256,2048]{1,0:T(8,128)(2,1)S(1)}, bf16[256,2048]{1,0:T(8,128)(2,1)S(1)}, u32[]{:S(2)}, u32[]{:S(2)}) collective-permute-start(bf16[256,2048]{1,0:T(8,128)(2,1)S(1)} %collective-permute-done.2.refs_2_), channel_id=1, source_target_pairs={{1,0},{3,2},{4,5},{6,7},{9,8},{11,10},{12,13},{14,15},{17,16},{19,... | collective-permute-start | bytes 3145736 | tf_op jit(solution)/shard_map/ppermute | solution.py:253
  90.3 4.8 %collective-permute-start.4 = (bf16[256,2048]{1,0:T(8,128)(2,1)S(1)}, bf16[256,2048]{1,0:T(8,128)(2,1)S(1)}, u32[]{:S(2)}, u32[]{:S(2)}) collective-permute-start(bf16[256,2048]{1,0:T(8,128)(2,1)S(1)} %collective-permute-done.1.refs_1_), channel_id=1, source_target_pairs={{1,0},{2,3},{3,2},{4,5},{5,4},{6,7},{9,8},{10,11},{11,10},{12,13},... | collective-permute-start | bytes 3145736 | tf_op jit(solution)/shard_map/ppermute | solution.py:253
  91.6 15.9 %collective-permute-start.6 = (bf16[256,2048]{1,0:T(8,128)(2,1)S(1)}, bf16[256,2048]{1,0:T(8,128)(2,1)S(1)}, u32[]{:S(2)}, u32[]{:S(2)}) collective-permute-start(bf16[256,2048]{1,0:T(8,128)(2,1)S(1)} %collective-permute-done.3.refs_3_), channel_id=1, source_target_pairs={{1,0},{6,7},{9,8},{14,15},{17,16},{22,23},{25,24},{30,31}} | collective-permute-start | bytes 3145736 | tf_op jit(solution)/shard_map/ppermute | solution.py:253
  125.2 2.0 copy-start.3
  127.3 1.2 copy-start.10
  128.5 2.5 %copy-start.11 = (bf16[4,320,2048]{2,1,0:T(8,128)(2,1)S(1)}, bf16[4,320,2048]{2,1,0:T(8,128)(2,1)}, u32[]{:S(2)}) copy-start(bf16[4,320,2048]{2,1,0:T(8,128)(2,1)} %get-tuple-element.41.kept) | copy-start | bytes 15728644
  140.5 20.4 %collective-permute-start.11 = (bf16[2,2,256,384]{3,2,1,0:T(8,128)(2,1)S(1)}, bf16[2,2,256,384]{3,2,1,0:T(8,128)(2,1)S(1)}, u32[]{:S(2)}, u32[]{:S(2)}) collective-permute-start(bf16[2,2,256,384]{3,2,1,0:T(8,128)(2,1)S(1)} %get-tuple-element.48), channel_id=1, source_target_pairs={{0,8},{8,0},{16,24},{24,16},{1,9},{9,1},{17,25},{25,17},{2,10},{10... | collective-permute-start | bytes 2359304 | tf_op jit(solution)/shard_map/ppermute | solution.py:396
  142.1 20.7 %collective-permute-start.13 = (bf16[2,2,256,384]{3,2,1,0:T(8,128)(2,1)S(1)}, bf16[2,2,256,384]{3,2,1,0:T(8,128)(2,1)S(1)}, u32[]{:S(2)}, u32[]{:S(2)}) collective-permute-start(bf16[2,2,256,384]{3,2,1,0:T(8,128)(2,1)S(1)} %get-tuple-element.50), channel_id=1, source_target_pairs={{0,16},{8,24},{16,0},{24,8},{1,17},{9,25},{17,1},{25,9},{2,18},{10... | collective-permute-start | bytes 2359304 | tf_op jit(solution)/shard_map/ppermute | solution.py:396
  153.2 24.7 %collective-permute-start.7 = (bf16[2,2,256,384]{3,2,1,0:T(8,128)(2,1)S(1)}, bf16[2,2,256,384]{3,2,1,0:T(8,128)(2,1)S(1)}, u32[]{:S(2)}, u32[]{:S(2)}) collective-permute-start(bf16[2,2,256,384]{3,2,1,0:T(8,128)(2,1)S(1)} %get-tuple-element.44), channel_id=1, source_target_pairs={{0,8},{8,0},{16,24},{24,16},{1,9},{9,1},{17,25},{25,17},{2,10},{10... | collective-permute-start | bytes 2359304 | tf_op jit(solution)/shard_map/ppermute | solution.py:396
  153.8 25.9 %collective-permute-start.9 = (bf16[2,2,256,384]{3,2,1,0:T(8,128)(2,1)S(1)}, bf16[2,2,256,384]{3,2,1,0:T(8,128)(2,1)S(1)}, u32[]{:S(2)}, u32[]{:S(2)}) collective-permute-start(bf16[2,2,256,384]{3,2,1,0:T(8,128)(2,1)S(1)} %get-tuple-element.46), channel_id=1, source_target_pairs={{0,16},{8,24},{16,0},{24,8},{1,17},{9,25},{17,1},{25,9},{2,18},{10... | collective-permute-start | bytes 2359304 | tf_op jit(solution)/shard_map/ppermute | solution.py:396
  161.2 26.5 %collective-permute-start.12 = (bf16[1,2,256,384]{3,2,1,0:T(8,128)(2,1)S(1)}, bf16[1,2,256,384]{3,2,1,0:T(8,128)(2,1)S(1)}, u32[]{:S(2)}, u32[]{:S(2)}) collective-permute-start(bf16[1,2,256,384]{3,2,1,0:T(8,128)(2,1)S(1)} %slice.37), channel_id=1, source_target_pairs={{0,16},{8,24},{16,0},{24,8},{1,17},{9,25},{17,1},{25,9},{2,18},{10... | collective-permute-start | bytes 1179656 | tf_op jit(solution)/shard_map/ppermute | solution.py:396
  163.1 24.8 %collective-permute-start.14 = (bf16[1,2,256,384]{3,2,1,0:T(8,128)(2,1)S(1)}, bf16[1,2,256,384]{3,2,1,0:T(8,128)(2,1)S(1)}, u32[]{:S(2)}, u32[]{:S(2)}) collective-permute-start(bf16[1,2,256,384]{3,2,1,0:T(8,128)(2,1)S(1)} %slice.39), channel_id=1, source_target_pairs={{0,8},{8,0},{16,24},{24,16},{1,9},{9,1},{17,25},{25,17},{2,10},{10... | collective-permute-start | bytes 1179656 | tf_op jit(solution)/shard_map/ppermute | solution.py:396
  178.1 17.0 %collective-permute-start.8 = (bf16[1,2,256,384]{3,2,1,0:T(8,128)(2,1)S(1)}, bf16[1,2,256,384]{3,2,1,0:T(8,128)(2,1)S(1)}, u32[]{:S(2)}, u32[]{:S(2)}) collective-permute-start(bf16[1,2,256,384]{3,2,1,0:T(8,128)(2,1)S(1)} %slice.33), channel_id=1, source_target_pairs={{0,16},{8,24},{16,0},{24,8},{1,17},{9,25},{17,1},{25,9},{2,18},{10... | collective-permute-start | bytes 1179656 | tf_op jit(solution)/shard_map/ppermute | solution.py:396
  179.9 15.3 %collective-permute-start.10 = (bf16[1,2,256,384]{3,2,1,0:T(8,128)(2,1)S(1)}, bf16[1,2,256,384]{3,2,1,0:T(8,128)(2,1)S(1)}, u32[]{:S(2)}, u32[]{:S(2)}) collective-permute-start(bf16[1,2,256,384]{3,2,1,0:T(8,128)(2,1)S(1)} %slice.35), channel_id=1, source_target_pairs={{0,8},{8,0},{16,24},{24,16},{1,9},{9,1},{17,25},{25,17},{2,10},{10... | collective-permute-start | bytes 1179656 | tf_op jit(solution)/shard_map/ppermute | solution.py:396
  195.3 1.1 copy-start.4
Sparse Core Ops, SparseCore 0:
  10.7 59.5 all-gather.1
  127.4 53.0 reduce-scatter.1

commit v12 on v9

--- a/solution.py
+++ b/solution.py
@@ -9,11 +9,13 @@
 
 LANES = 128
 PACK = 16
+SLICES = 2
 GROUP = 2
 VMEM_LIMIT = 60 * 1024 * 1024
 bf16, f32 = jnp.bfloat16, jnp.float32
 ANY = pl.BlockSpec(memory_space=pl.ANY)
 SMEM = pl.BlockSpec(memory_space=pltpu.SMEM)
+VMEM = pl.BlockSpec(memory_space=pltpu.VMEM)
 FIRST = (((0,), (0,)), ((), ()))
 
 
@@ -21,13 +23,17 @@
     return lax.dot_general(a, b, dims, preferred_element_type=f32)
 
 
-def pack_kernel(top, tokens, ids, gates, x_out):
+def pack_kernel(top, parts, tokens, cotangent, ids, gates, x_out, *dy_out):
     count, width = tokens.shape
     x_out[:, pl.ds(0, width)] = tokens[...]
     info = jnp.concatenate(
         [ids[...].astype(f32), gates[...].astype(f32), jnp.zeros((LANES - 2 * top, count), f32)], axis=0
     )
     x_out[:, pl.ds(width, LANES)] = info.T.astype(bf16)
+    piece = width // parts // len(dy_out)
+    for s, out in enumerate(dy_out):
+        for i in range(parts):
+            out[:, pl.ds(i * piece, piece)] = cotangent[:, pl.ds((i * len(dy_out) + s) * piece, piece)]
 
 
 def flip_kernel(w, out):
@@ -131,67 +137,114 @@
         copy.wait()
 
 
-def down_kernel(orders, start, place, kept, scaled_in, *refs):
-    outs, (rows, scaled, sent, in_sem, sem) = refs[:-5], refs[-5:]
-    experts = sent.shape[2]
-    arrive = copy_all([(kept.at[start + b], rows.at[b]) for b in range(experts)], in_sem.at[0])
-    others = copy_all([(scaled_in.at[start + b], scaled.at[b]) for b in range(experts)], in_sem.at[1])
+def slice_copies(weights, dst, pieces, sem):
+    return [
+        copy_all([(weights.at[b, pl.ds(at, size), :], dst.at[b, pl.ds(to, size), :]) for at, size, to in pieces], sem.at[b])
+        for b in range(weights.shape[0])
+    ]
+
+
+def pick_blocks(place, cap, blocks, pick, moved, held, sem):
+    groups, members = moved.shape[0], moved.shape[1]
+    half = members // 2
+    own = blocks[0]
+    for slot in range(groups):
+        for part in range(2):
+            at = pl.ds(part * half, half)
+            pltpu.make_async_copy(own.at[at, :], moved.at[slot, at, :], sem.at[slot, part]).wait()
+        group = lax.rem(place[3] - slot + groups, groups)
+        first = pl.multiple_of(group * cap, PACK)
+        got = dot(pick[group], moved[slot]).astype(bf16)
+        for b in range(held.shape[0]):
+            held[b, pl.ds(first, cap), :] = got[b * cap : (b + 1) * cap]
+
+
+def down_rows(orders, place, b, rows, scaled, made, outs, sem):
+    made[b] = dot(rows, scaled, FIRST).astype(bf16)
     parts = len(orders[0])
     half = parts // 2
-    share = rows.shape[2] // parts
-    cut = share // len(orders)
+    piece = made.shape[1] // parts
+    cut = piece // len(orders)
+    copies = []
+    for g, order in enumerate(orders):
+        for p, q in enumerate(order):
+            at = pl.multiple_of((place[1] ^ q) * piece + g * cut, PACK)
+            out = outs[2 * g + p // half].at[p % half, b]
+            copies.append(pltpu.make_async_copy(made.at[b, pl.ds(at, cut), :], out, sem.at[g, q, b]))
+            copies[-1].start()
+    return copies
+
+
+def mid_kernel(groups, cap, orders, pieces, place, *refs):
+    count = 2 * groups - 1
+    blocks, refs = refs[:count], refs[count:]
+    pick_in, w_down, scaled_in, back_out = refs[:4]
+    outs, refs = refs[4 : 4 + 2 * len(orders)], refs[4 + 2 * len(orders) :]
+    pick, moved, held, down_v, scaled, back, made, block_sem, w_sem, sems, sem = refs
+    experts = held.shape[0]
+    first_pick = copy_all([(pick_in, pick)], sems.at[0])
+    start_blocks(place, groups, blocks[0], blocks[1:groups], blocks[groups:], moved, block_sem)
+    weights = slice_copies(w_down, down_v, pieces, w_sem)
+    others = copy_all([(scaled_in.at[b], scaled.at[b]) for b in range(experts)], sems.at[1])
+    first_pick[0].wait()
+    pick_blocks(place, cap, blocks, pick, moved, held, block_sem)
+    copies = []
+    for b in range(experts):
+        others[b].wait()
+        copies += down_rows(orders, place, b, held[b], scaled[b], made, outs, sem)
+    for b in range(experts):
+        for copy in weights[b]:
+            copy.wait()
+        back[b] = dot(held[b], down_v[b])
+        copies.append(pltpu.make_async_copy(back.at[b], back_out.at[b], sems.at[2, b]))
+        copies[-1].start()
+    for copy in copies:
+        copy.wait()
+
+
+def down_kernel(orders, after, place, kept, scaled_in, *refs):
+    outs, (rows, scaled, made, in_sem, sem) = refs[after:-5], refs[-5:]
+    experts = made.shape[0]
+    arrive = copy_all([(kept.at[b], rows.at[b]) for b in range(experts)], in_sem.at[0])
+    others = copy_all([(scaled_in.at[b], scaled.at[b]) for b in range(experts)], in_sem.at[1])
     copies = []
     for b in range(experts):
         arrive[b].wait()
         others[b].wait()
-        for q in range(parts):
-            at = pl.multiple_of((place[1] ^ q) * share, LANES)
-            full = dot(rows[b, :, pl.ds(at, share)], scaled[b], FIRST).astype(bf16)
-            for g, order in enumerate(orders):
-                sent[g, q, b] = full[g * cut : (g + 1) * cut]
-                p = order.index(q)
-                copy = pltpu.make_async_copy(
-                    sent.at[g, q, b], outs[2 * g + p // half].at[p % half, b], sem.at[g, q, b]
-                )
-                copy.start()
-                copies.append(copy)
+        copies += down_rows(orders, place, b, rows[b], scaled[b], made, outs, sem)
     for copy in copies:
         copy.wait()
 
 
-def tail_kernel(groups, cap, width, top, place, *refs):
-    steps = groups - 1
-    own, mine, other, refs = refs[0], refs[1 : 1 + steps], refs[1 + steps : 1 + 2 * steps], refs[1 + 2 * steps :]
-    pick_in, w_down, w_flip, hid_in, slope_in, meta, out_all, kept = refs[:8]
-    pick, moved, held, grads, out, down_v, flip_v, hid, slope, block_sem, sems, keep_sem, out_sem = refs[8:]
+def tail_kernel(groups, cap, width, top, pieces, has_before, place, *refs):
+    count = 2 * groups - 1
+    blocks, refs = refs[:count], refs[count:]
+    pick_in, w_down, w_flip, hid_in, slope_in, meta = refs[:6]
+    before_in = refs[6] if has_before else None
+    out_all, kept = refs[6 + has_before : 8 + has_before]
+    refs = refs[8 + has_before :]
+    pick, moved, held, grads, out, down_v, flip_v, hid, slope, before, block_sem, w_sem, sems, keep_sem, out_sem = refs
     experts, members = held.shape[0], moved.shape[1]
-    half = members // 2
     first_pick = copy_all([(pick_in, pick)], sems.at[0])
-    start_blocks(place, groups, own, mine, other, moved, block_sem)
+    start_blocks(place, groups, blocks[0], blocks[1:groups], blocks[groups:], moved, block_sem)
+    weights = slice_copies(w_down, down_v, pieces, w_sem)
+    sources = [(hid_in, hid), (slope_in, slope), (w_flip, flip_v)] + ([(before_in, before)] if has_before else [])
     loads = [
-        copy_all([(src.at[b], dst.at[b]) for b in range(experts)], sems.at[n])
-        for n, (src, dst) in enumerate(((w_down, down_v), (hid_in, hid), (slope_in, slope), (w_flip, flip_v)), 1)
+        copy_all([(src.at[b], dst.at[b]) for b in range(experts)], sems.at[n]) for n, (src, dst) in enumerate(sources, 1)
     ]
     first_pick[0].wait()
-    for slot in range(groups):
-        for part in range(2):
-            at = pl.ds(part * half, half)
-            pltpu.make_async_copy(own.at[at, :], moved.at[slot, at, :], block_sem.at[slot, part]).wait()
-        group = lax.rem(place[3] - slot + groups, groups)
-        first = pl.multiple_of(group * cap, PACK)
-        got = dot(pick[group], moved[slot]).astype(bf16)
-        for b in range(experts):
-            held[b, pl.ds(first, cap), :] = got[b * cap : (b + 1) * cap]
+    pick_blocks(place, cap, blocks, pick, moved, held, block_sem)
     keep = copy_all([(held.at[b], kept.at[b]) for b in range(experts)], keep_sem)
     lane = lax.broadcasted_iota(jnp.int32, (groups * cap, LANES), 1)
     for b in range(experts):
-        for load in loads[:3]:
-            load[b].wait()
+        for copy in weights[b] + [load[b] for load in loads]:
+            copy.wait()
         back = dot(held[b], down_v[b])
+        if has_before:
+            back = back + before[b]
         gate = jnp.sum(back * hid[b].astype(f32), axis=1, keepdims=True)
         gate = jnp.where(lane == b, gate, 0.0).astype(bf16)
         grad = (back * slope[b].astype(f32)).astype(bf16)
-        loads[3][b].wait()
         route = dot(grad, flip_v[b]).astype(bf16)
         for g in range(groups):
             grads[g, pl.ds(b * cap, cap), pl.ds(0, width)] = route[g * cap : (g + 1) * cap]
@@ -214,6 +267,15 @@
         copy.wait()
 
 
+def add_kernel(*refs):
+    count = len(refs) // 4
+    for n in range(count):
+        total = (refs[2 * n][...].astype(f32) + refs[2 * n + 1][...].astype(f32)).astype(bf16)
+        half = total.shape[0] // 2
+        refs[2 * count + 2 * n][...] = total[:half]
+        refs[2 * count + 2 * n + 1][...] = total[half:]
+
+
 def finish_kernel(width, top, rows, token, gate):
     token[...] = rows[:, pl.ds(0, width)]
     gate[...] = rows[:, pl.ds(width, LANES)].astype(f32).T[:top].astype(bf16)
@@ -241,17 +303,20 @@
     bits = dp_count.bit_length() - 1
     turns = 2
     share = width // dp_count
+    slices = SLICES if share % (SLICES * LANES) == 0 else 1
+    piece = share // slices
+    cols = dp_count * piece
 
     def shape(*dims, dtype=bf16):
         return jax.ShapeDtypeStruct(dims, dtype)
 
-    x_own = pl.pallas_call(
-        functools.partial(pack_kernel, top),
-        out_shape=shape(tok_rows, full),
+    x_own, *dy_own = pl.pallas_call(
+        functools.partial(pack_kernel, top, dp_count),
+        out_shape=[shape(tok_rows, full)] + [shape(tok_rows, cols)] * slices,
         compiler_params=pltpu.CompilerParams(vmem_limit_bytes=VMEM_LIMIT),
-        cost_estimate=cost(0, 4 * tok_rows * width),
+        cost_estimate=cost(0, 8 * tok_rows * width),
         name="pack",
-    )(tokens, expert_ids.T, gate_weights.T)
+    )(tokens, cotangent, expert_ids.T, gate_weights.T)
     x_all = lax.all_gather(x_own, "ep", axis=0, tiled=True)
 
     def reach(p, step):
@@ -304,7 +369,7 @@
         out_shape=shape(experts, hidden, width),
         scratch_shapes=[],
     )(w_up)
-    dy_own = jnp.concatenate([cotangent, hop(cotangent, [(p, p ^ 1) for p in range(ep_count)])], axis=0)
+    dy_own = [jnp.concatenate([part, hop(part, [(p, p ^ 1) for p in range(ep_count)])], axis=0) for part in dy_own]
     lines = [None] + [
         [(p, reach(p, 1)) for p in range(ep_count) if None not in (reach(p, 1), reach(p, 1 - step))]
         for step in range(1, groups)
@@ -314,9 +379,9 @@
     ]
     moving, dy_mine, dy_other = dy_own, [], []
     for step in range(1, groups - 1):
-        moving = hop(moving, lines[step])
+        moving = [hop(part, lines[step]) for part in moving]
         if step == 1:
-            moving, w_flip = lax.optimization_barrier((moving, w_flip))
+            moving[0], w_flip = lax.optimization_barrier((moving[0], w_flip))
         dy_mine.append(moving)
 
     act = shape(experts, routes, hidden)
@@ -361,9 +426,10 @@
             pltpu.SemaphoreType.DMA((4, experts)),
         ],
     )(place, x_all, w_up)
-    *dy_mine, hid = lax.optimization_barrier((*dy_mine, hid))
-    dy_mine.append(hop(dy_mine[-1], lines[-1]))
-    dy_other = [hop(part, swap) for part, swap in zip(dy_mine, swaps[1:])]
+    dy_mine, hid = lax.optimization_barrier((dy_mine, hid))
+    dy_mine.append([hop(part, lines[-1]) for part in dy_mine[-1]])
+    dy_other = [[hop(part, swap) for part in row] for row, swap in zip(dy_mine, swaps[1:])]
+    blocks = [[dy_own[s]] + [row[s] for row in dy_mine] + [row[s] for row in dy_other] for s in range(slices)]
 
     orders = []
     for g in range(turns):
@@ -372,63 +438,86 @@
             tuple(sum(((p >> (bits - 1 - t)) & 1) << turn[t] for t in range(bits)) for p in range(dp_count))
         )
     orders = tuple(orders)
-    cut_rows = share // turns
-
-    def down(start, count):
-        outs = one(
-            functools.partial(down_kernel, orders, start),
-            "down",
-            16 * main_flops,
-            8 * row_bytes,
-            [SMEM, ANY, ANY],
-            [ANY] * (2 * turns),
-            [shape(dp_count // 2, count, cut_rows, hidden)] * (2 * turns),
-            [
-                pltpu.VMEM((count, routes, width), bf16),
-                pltpu.VMEM((count, routes, hidden), bf16),
-                pltpu.VMEM((turns, dp_count, count, cut_rows, hidden), bf16),
-                pltpu.SemaphoreType.DMA((2, count)),
-                pltpu.SemaphoreType.DMA((turns, dp_count, count)),
-            ],
-        )(place, kept, scaled)
+    cut_rows = piece // turns
+
+    down_outs = [shape(dp_count // 2, experts, cut_rows, hidden)] * (2 * turns)
+    made = pltpu.VMEM((experts, cols, hidden), bf16)
+    made_sem = pltpu.SemaphoreType.DMA((turns, dp_count, experts))
+    held = pltpu.VMEM((experts, routes, cols), bf16)
+    moved = pltpu.VMEM((groups, members, cols), bf16)
+    down_v = pltpu.VMEM((experts, cols, hidden), bf16)
+    back_v = pltpu.VMEM((experts, routes, hidden), f32)
+    block_sem = pltpu.SemaphoreType.DMA((groups, 2))
+    w_sem = pltpu.SemaphoreType.DMA((experts, dp_count))
+
+    def pieces(s):
+        return tuple((i * share + s * piece, piece, i * piece) for i in range(dp_count))
+
+    def pairs(outs):
         return [(outs[2 * g], outs[2 * g + 1]) for g in range(turns)]
 
     def exchange(state, t):
-        new = []
-        for g, (keep, send) in enumerate(state):
-            bit = 1 << ((g + t) % bits)
-            got = lax.ppermute(send, "dp", [(i, i ^ bit) for i in range(dp_count)])
-            both = keep.astype(f32) + got.astype(f32)
-            if t < bits - 1:
-                both = both.astype(bf16)
-            half = both.shape[0] // 2
-            new.append((both[:half], both[half:]) if half else both[0])
-        return new
-
+        got = [
+            lax.ppermute(send, "dp", [(i, i ^ (1 << ((g + t) % bits))) for i in range(dp_count)])
+            for g, (_, send) in enumerate(state)
+        ]
+        if t == bits - 1:
+            return [keep.astype(f32)[0] + more.astype(f32)[0] for (keep, _), more in zip(state, got)]
+        operands = [x for (keep, _), more in zip(state, got) for x in (keep, more)]
+        half = shape(operands[0].shape[0] // 2, *operands[0].shape[1:])
+        return pairs(
+            one(
+                add_kernel,
+                "add",
+                0,
+                sum(4 * x.size for x in operands),
+                [VMEM] * len(operands),
+                [VMEM] * len(operands),
+                [half] * len(operands),
+                [],
+            )(*operands)
+        )
+
+    states, before = [], []
+    for s in range(slices - 1):
+        back, *outs = one(
+            functools.partial(mid_kernel, groups, cap, orders, pieces(s)),
+            "mid",
+            main_flops,
+            row_bytes,
+            [SMEM] + [ANY] * (2 * groups + 2),
+            [ANY] * (1 + 2 * turns),
+            [shape(experts, routes, hidden, dtype=f32)] + down_outs,
+            [pick_v, moved, held, down_v, act3, back_v, made, block_sem, w_sem, pltpu.SemaphoreType.DMA((3, most)), made_sem],
+        )(place, *blocks[s], pick, w_down, scaled)
+        before = [back]
+        states.append(exchange(pairs(outs), 0) if bits > 1 else pairs(outs))
     token_part, kept = one(
-        functools.partial(tail_kernel, groups, cap, width, top),
+        functools.partial(tail_kernel, groups, cap, width, top, pieces(slices - 1), len(before)),
         "tail",
-        8 * main_flops,
+        100 * main_flops,
         4 * row_bytes,
-        [SMEM] + [ANY] * (2 * groups - 1) + [ANY] * 5 + [pl.BlockSpec(memory_space=pltpu.VMEM)],
+        [SMEM] + [ANY] * (2 * groups - 1) + [ANY] * 5 + [VMEM] + [ANY] * len(before),
         [ANY, ANY],
-        [shape(total, full), shape(experts, routes, width)],
+        [shape(total, full), shape(experts, routes, cols)],
         [
             pick_v,
-            pltpu.VMEM((groups, members, width), bf16),
-            pltpu.VMEM((experts, routes, width), bf16),
+            moved,
+            held,
             pltpu.VMEM((groups, experts * cap, full), bf16),
             pltpu.VMEM((groups, members, full), bf16),
-            pltpu.VMEM((experts, width, hidden), bf16),
+            down_v,
             pltpu.VMEM((experts, hidden, width), bf16),
             act3,
             act3,
-            pltpu.SemaphoreType.DMA((groups, 2)),
+            back_v,
+            block_sem,
+            w_sem,
             pltpu.SemaphoreType.DMA((5, experts)),
             pltpu.SemaphoreType.DMA((experts,)),
             pltpu.SemaphoreType.DMA((groups,)),
         ],
-    )(place, dy_own, *dy_mine, *dy_other, pick, w_down, w_flip, hid, slope_g, meta)
+    )(place, *blocks[-1], pick, w_down, w_flip, hid, slope_g, meta, *before)
     summed = lax.psum_scatter(token_part, "ep", scatter_dimension=0, tiled=True)
     token_grad, gate_grad = pl.pallas_call(
         functools.partial(finish_kernel, width, top),
@@ -438,12 +527,27 @@
         name="finish",
     )(summed)
 
-    counts = [experts // 2, experts - experts // 2] if experts > 1 else [experts]
-    states = [down(start, count) for start, count in zip((0, counts[0]), counts)]
-    for t in range(bits):
+    after = [pair[0] for state in states for pair in state] if bits > 1 else []
+    outs = one(
+        functools.partial(down_kernel, orders, len(after)),
+        "down",
+        400 * main_flops,
+        row_bytes,
+        [SMEM] + [ANY] * (2 + len(after)),
+        [ANY] * (2 * turns),
+        down_outs,
+        [held, act3, made, pltpu.SemaphoreType.DMA((2, experts)), made_sem],
+    )(place, kept, scaled, *after)
+    if bits > 1:
+        states.append(exchange(pairs(outs), 0))
+        keeps = [pair[0] for pair in states[-1]]
+        token_grad, keeps = lax.optimization_barrier((token_grad, keeps))
+        states[-1] = [(keep, pair[1]) for keep, pair in zip(keeps, states[-1])]
+    else:
+        states.append(pairs(outs))
+    for t in range(1 if bits > 1 else 0, bits):
         states = [exchange(state, t) for state in states]
-    token_grad, states = lax.optimization_barrier((token_grad, states))
-    down_grad = jnp.concatenate([jnp.concatenate(state, axis=1) for state in states], axis=0)
+    down_grad = jnp.concatenate([part for state in states for part in state], axis=1)
     return (token_grad, gate_grad.T, down_grad)
 
 

time: 191 us -> 195 us (1.021)
  waiting for transfers between devices: 98 us -> 79.9 us
  Pallas kernels: 50.5 us -> 60.9 us
  starting transfers between devices: 21.5 us -> 30.5 us
  local copies, waits for them, and re-layouts: 2.31 us -> 4.51 us
    ppermute x8, waiting for transfers between devices: 38.1 us -> 16.8 us  [exchange(): lax.ppermute(send, 'dp', [(i, i ^ 1 << (g + t) % bits) for i in range(dp_...]
    reduce_scatter x1, waiting for transfers between devices: 0.02 us -> 19.7 us  [shards(): summed = lax.psum_scatter(token_part, 'ep', scatter_dimension=0, tiled=True)]
    ppermute x7 -> x14, waiting for transfers between devices: 36.3 us -> 19.7 us  [hop(): return lax.ppermute(value, 'ep', pairs)]
    pallas_call x4 -> x6, Pallas kernels: 31.2 us -> 41.6 us  [the longest x1 15.7 us: shards(): one(functools.partial(tail_kernel, groups, cap, width, top, pieces(slices...]
    ppermute x7 -> x14, starting transfers between devices: 10.9 us -> 21.3 us  [hop(): return lax.ppermute(value, 'ep', pairs)]
    unnamed x23 -> x38, local copies, waits for them, and re-layouts: 2.11 us -> 4.47 us
  transfers between devices with their start and end apart: 17 -> 24, of which waited for: 9 -> 8; matrix products, arithmetic and copies ran while one was open for 2% -> 2% of each run, Pallas kernels for 15% -> 30%
where the time goes in v12:
time: 195 us; the launch traced here: 194 us
  waiting for transfers between devices  79.9 us (41%)
  Pallas kernels  60.9 us (31%)
  starting transfers between devices  30.5 us (16%)
  between operations  14.4 us (7%)
  local copies, waits for them, and re-layouts  4.51 us (2%)
  other arithmetic  3.83 us (2%)
    all_gather x1, waiting for transfers between devices, shards(): x_all = lax.all_gather(x_own, 'ep', axis=0, tiled=True)  23.7 us
    ppermute x14, starting transfers between devices, hop(): return lax.ppermute(value, 'ep', pairs)  21.3 us
    ppermute x14, waiting for transfers between devices, hop(): return lax.ppermute(value, 'ep', pairs)  19.7 us
    reduce_scatter x1, waiting for transfers between devices, shards(): summed = lax.psum_scatter(token_part, 'ep', scatter_dimension=0, tiled=True)  19.7 us
    ppermute x8, waiting for transfers between devices, exchange(): lax.ppermute(send, 'dp', [(i, i ^ 1 << (g + t) % bits) for i in range(dp_...  16.8 us
    pallas_call x1, Pallas kernels, shards(): one(functools.partial(tail_kernel, groups, cap, width, top, pieces(slices...  15.7 us
    pallas_call x1, Pallas kernels, shards(): one(functools.partial(mid_kernel, groups, cap, orders, pieces(s)), 'mid',...  10.7 us
    pallas_call x1, Pallas kernels, shards(): one(functools.partial(up_kernel, groups, width, top, cap, 0), 'up', pick_...  10.4 us
  transfers between devices with their start and end apart: 24, of which 8 were waited for; matrix products, arithmetic and copies ran while one was open for 2% of the time, Pallas kernels for 30%

profile of v12, /device:TPU:0, one launch (start us, length us, event | category | flops | bytes accessed | tf_op | source)
XLA Modules:
  0.0 194.0 jit_solution(9712236714181587792)
XLA Ops:
  7.2 2.2 %pack.1 = (bf16[128,2176]{1,0:T(8,128)(2,1)}, bf16[128,1024]{1,0:T(8,128)(2,1)}, bf16[128,1024]{1,0:T(8,128)(2,1)}) custom-call(bf16[128,2048]{1,0:T(8,128)(2,1)} %tokens.1, bf16[128,2048]{1,0:T(8,128)(2,1)} %cotangent.1, s32[8,128]{1,0:T(8,128)} %bitcast.15, bf16[8,128]{1,0:T(8,128)(2,1)} %bitcast.16), custom_call_target="tpu_custom_call" | custom-call | bytes 2097152 | tf_op jit(solution)/shard_map/pack/pallas_call | solution.py:313
  9.5 0.5 collective-permute-start.1
  10.1 1.0 constant_dynamic-update-slice_fusion.3
  11.1 1.0 constant_dynamic-update-slice_fusion.1
  12.1 4.9 %collective-permute-start.2 = (bf16[256,1024]{1,0:T(8,128)(2,1)S(1)}, bf16[256,1024]{1,0:T(8,128)(2,1)S(1)}, u32[]{:S(2)}, u32[]{:S(2)}) collective-permute-start(bf16[256,1024]{1,0:T(8,128)(2,1)S(1)} %constant_dynamic-update-slice_fusion.2.refs_0_), channel_id=1, source_target_pairs={{0,2},{2,4},{3,1},{4,6},{5,3},{7,5},{8,10},{10,12},{11,9},{12,14},... | collective-permute-start | bytes 1572872 | tf_op jit(solution)/shard_map/ppermute | solution.py:327
  17.1 3.5 %collective-permute-start.3 = (bf16[256,1024]{1,0:T(8,128)(2,1)S(1)}, bf16[256,1024]{1,0:T(8,128)(2,1)S(1)}, u32[]{:S(2)}, u32[]{:S(2)}) collective-permute-start(bf16[256,1024]{1,0:T(8,128)(2,1)S(1)} %constant_dynamic-update-slice_fusion.refs_0_), channel_id=1, source_target_pairs={{0,2},{2,4},{3,1},{4,6},{5,3},{7,5},{8,10},{10,12},{11,9},{12,14},... | collective-permute-start | bytes 1572872 | tf_op jit(solution)/shard_map/ppermute | solution.py:327
  20.6 6.9 %flip.1.refs_9_ = bf16[4,384,2048]{2,1,0:T(8,128)(2,1)} custom-call(bf16[4,2048,384]{2,1,0:T(8,128)(2,1)} %w_up.1), custom_call_target="tpu_custom_call" | custom-call | bytes 12582912 | tf_op jit(solution)/shard_map/flip/pallas_call | solution.py:361
  27.5 1.0 collective-permute-done.2.refs_1_
  28.5 0.7 collective-permute-start.4
  29.1 16.2 %collective-permute-done.3.refs_1_ = bf16[256,1024]{1,0:T(8,128)(2,1)S(1)} collective-permute-done((bf16[256,1024]{1,0:T(8,128)(2,1)S(1)}, bf16[256,1024]{1,0:T(8,128)(2,1)S(1)}, u32[]{:S(2)}, u32[]{:S(2)}) %collective-permute-start.3) | collective-permute-done | bytes 524320 | tf_op jit(solution)/shard_map/ppermute | solution.py:327
  45.3 1.4 collective-permute-start.5
  46.8 0.6 pad_add_fusion.place
  47.4 23.7 %all-gather.2.cloned.1.call-done.x_all = bf16[1024,2176]{1,0:T(8,128)(2,1)} async-done(((bf16[128,2176]{1,0:T(8,128)(2,1)}), bf16[1024,2176]{1,0:T(8,128)(2,1)}) %all-gather.2.cloned.1.call-update) | async-done | bytes 4456464 | tf_op jit(solution)/shard_map/all_gather | solution.py:320
  71.1 10.4 %up.1 = (bf16[4,320,256]{2,1,0:T(8,128)(2,1)}, bf16[1024,128]{1,0:T(8,128)(2,1)}, bf16[4,320,384]{2,1,0:T(8,128)(2,1)}, bf16[4,320,384]{2,1,0:T(8,128)(2,1)}, bf16[4,320,384]{2,1,0:T(8,128)(2,1)}) custom-call(s32[4]{0:T(128)} %pad_add_fusion.place, bf16[1024,2176]{1,0:T(8,128)(2,1)} %all-gather.2.cloned.1.call-done.x_all, bf16[4,2048,384]{2,1,0:T(8,128)(2,1)} %w_up.1), custom_call_target="tpu_custom_call" | custom-call | flops 3355443200 | bytes 10747904 | tf_op jit(solution)/shard_map/up/pallas_call | solution.py:408
  81.5 0.7 collective-permute-start.10
  82.2 1.3 collective-permute-start.11
  83.5 1.5 collective-permute-start.6
  85.0 1.3 collective-permute-start.12
  86.3 1.3 collective-permute-start.13
  87.6 1.3 collective-permute-start.8
  89.0 1.3 collective-permute-start.7
  90.3 1.5 collective-permute-start.9
  91.8 2.6 %collective-permute-done.13.refs_6_ = bf16[256,1024]{1,0:T(8,128)(2,1)S(1)} collective-permute-done((bf16[256,1024]{1,0:T(8,128)(2,1)S(1)}, bf16[256,1024]{1,0:T(8,128)(2,1)S(1)}, u32[]{:S(2)}, u32[]{:S(2)}) %collective-permute-start.13) | collective-permute-done | bytes 524320 | tf_op jit(solution)/shard_map/ppermute | solution.py:327
  94.4 0.8 copy-done.8
  95.2 10.7 %mid.1 = (f32[4,320,384]{2,1,0:T(8,128)}, bf16[2,4,128,384]{3,2,1,0:T(8,128)(2,1)}, bf16[2,4,128,384]{3,2,1,0:T(8,128)(2,1)}, bf16[2,4,128,384]{3,2,1,0:T(8,128)(2,1)}, bf16[2,4,128,384]{3,2,1,0:T(8,128)(2,1)}) custom-call(s32[4]{0:T(128)} %pad_add_fusion.place, bf16[256,1024]{1,0:T(8,128)(2,1)} %copy-done, bf16[256,1024]{1,0:T(8,128)(2,1)} %copy-done.3, ...), custom_call_target="tpu_custom_call" | custom-call | flops 2013265920 | bytes 6291456 | tf_op jit(solution)/shard_map/mid/pallas_call | solution.py:483
  105.9 1.5 collective-permute-start.14
  107.5 1.5 collective-permute-start.15
  109.0 0.8 copy-done.15
  109.7 15.7 %tail.1 = (bf16[1024,2176]{1,0:T(8,128)(2,1)}, bf16[4,320,1024]{2,1,0:T(8,128)(2,1)}) custom-call(s32[4]{0:T(128)} %pad_add_fusion.place, bf16[256,1024]{1,0:T(8,128)(2,1)} %copy-done.13, bf16[256,1024]{1,0:T(8,128)(2,1)} %copy-done.14, bf16[256,1024]{1,0:T(8,128)(2,1)} %collective-permute-done.5.refs_2_, bf16[256,1024]{1,0:T(8,128)(2,1)} %collective-permute-done.6.refs_3_, ...), custom_call_target="tpu_custom_call" | custom-call | flops 201326592000 | bytes 25165824 | tf_op jit(solution)/shard_map/tail/pallas_call | solution.py:495
  125.5 3.1 %add.53 = (bf16[1,4,128,384]{3,2,1,0:T(8,128)(2,1)}, bf16[1,4,128,384]{3,2,1,0:T(8,128)(2,1)}, bf16[1,4,128,384]{3,2,1,0:T(8,128)(2,1)}, bf16[1,4,128,384]{3,2,1,0:T(8,128)(2,1)}) custom-call(bf16[2,4,128,384]{3,2,1,0:T(8,128)(2,1)} %get-tuple-element.61.refs_0_, bf16[2,4,128,384]{3,2,1,0:T(8,128)(2,1)} %collective-permute-done.14.refs_1_, ...), custom_call_target="tpu_custom_call" | custom-call | bytes 6291456 | tf_op jit(solution)/shard_map/add/pallas_call | solution.py:469
  128.6 6.8 %down.1 = (bf16[2,4,128,384]{3,2,1,0:T(8,128)(2,1)}, bf16[2,4,128,384]{3,2,1,0:T(8,128)(2,1)}, bf16[2,4,128,384]{3,2,1,0:T(8,128)(2,1)}, bf16[2,4,128,384]{3,2,1,0:T(8,128)(2,1)}) custom-call(s32[4]{0:T(128)} %pad_add_fusion.place, bf16[4,320,1024]{2,1,0:T(8,128)(2,1)} %get-tuple-element.60.kept, bf16[4,320,384]{2,1,0:T(8,128)(2,1)} %get-tuple-element.56.refs_9_.scaled_in, ...), custom_call_target="tpu_custom_call" | custom-call | flops 805306368000 | bytes 6291456 | tf_op jit(solution)/shard_map/down/pallas_call | solution.py:531
  135.4 0.6 collective-permute-start.16
  136.0 0.6 collective-permute-start.17
  136.6 1.5 collective-permute-start.18
  138.1 1.5 collective-permute-start.19
  139.5 12.0 %collective-permute-done.16.refs_1_ = bf16[2,4,128,384]{3,2,1,0:T(8,128)(2,1)S(1)} collective-permute-done((bf16[2,4,128,384]{3,2,1,0:T(8,128)(2,1)}, bf16[2,4,128,384]{3,2,1,0:T(8,128)(2,1)S(1)}, u32[]{:S(2)}, u32[]{:S(2)}) %collective-permute-start.16) | collective-permute-done | bytes 786464 | tf_op jit(solution)/shard_map/ppermute | solution.py:461
  151.5 1.0 collective-permute-done.17.refs_3_
  152.6 0.9 copy-done.2
  153.4 3.1 %add.54 = (bf16[1,4,128,384]{3,2,1,0:T(8,128)(2,1)}, bf16[1,4,128,384]{3,2,1,0:T(8,128)(2,1)}, bf16[1,4,128,384]{3,2,1,0:T(8,128)(2,1)}, bf16[1,4,128,384]{3,2,1,0:T(8,128)(2,1)}) custom-call(bf16[2,4,128,384]{3,2,1,0:T(8,128)(2,1)} %get-tuple-element.67.refs_0_, bf16[2,4,128,384]{3,2,1,0:T(8,128)(2,1)} %copy-done.1, ...), custom_call_target="tpu_custom_call" | custom-call | bytes 6291456 | tf_op jit(solution)/shard_map/add/pallas_call | solution.py:469
  156.6 0.7 collective-permute-start.20
  157.2 3.7 %collective-permute-done.18 = bf16[1,4,128,384]{3,2,1,0:T(8,128)(2,1)S(1)} collective-permute-done((bf16[1,4,128,384]{3,2,1,0:T(8,128)(2,1)S(1)}, bf16[1,4,128,384]{3,2,1,0:T(8,128)(2,1)S(1)}, u32[]{:S(2)}, u32[]{:S(2)}) %collective-permute-start.18) | collective-permute-done | bytes 393248 | tf_op jit(solution)/shard_map/ppermute | solution.py:461
  161.1 1.4 collective-permute-start.21
  162.4 0.1 add_bitcast_fusion.2
  162.5 19.7 %reduce-scatter.2.cloned.1.call-done.rows = bf16[128,2176]{1,0:T(8,128)(2,1)} async-done(((bf16[1024,2176]{1,0:T(8,128)(2,1)}), bf16[128,2176]{1,0:T(8,128)(2,1)}) %reduce-scatter.2.cloned.1.call-update) | async-done | bytes 557072 | tf_op jit(solution)/shard_map/reduce_scatter | solution.py:521
  182.2 1.9 finish.1
  184.1 1.1 add_bitcast_fusion.1
  185.2 0.1 add_bitcast_fusion
  185.3 1.9 pad_maximum_fusion
  (57 shorter events, 0.4 us)
Async XLA Ops:
  7.2 63.9 %all-gather.2.cloned.1.call-start = ((), (), s32[]{:S(2)}) async-start(), calls=%async_computation.1 | async-start | bytes 5013504 | tf_op jit(solution)/shard_map/all_gather | solution.py:320
  9.4 172.8 %reduce-scatter.2.cloned.1.call-start = ((), (), s32[]{:S(2)}) async-start(), calls=%async_computation.2 | async-start | bytes 5013504 | tf_op jit(solution)/shard_map/reduce_scatter | solution.py:521
  9.5 2.5 %collective-permute-start.1 = (bf16[128,1024]{1,0:T(8,128)(2,1)}, bf16[128,1024]{1,0:T(8,128)(2,1)S(1)}, u32[]{:S(2)}, u32[]{:S(2)}) collective-permute-start(bf16[128,1024]{1,0:T(8,128)(2,1)} %get-tuple-element.43), channel_id=1, source_target_pairs={{0,1},{1,0},{2,3},{3,2},{4,5},{5,4},{6,7},{7,6},{8,9},{9,8},{10,11... | collective-permute-start | bytes 786440 | tf_op jit(solution)/shard_map/ppermute | solution.py:327
  10.0 7.0 %collective-permute-start = (bf16[128,1024]{1,0:T(8,128)(2,1)}, bf16[128,1024]{1,0:T(8,128)(2,1)S(1)}, u32[]{:S(2)}, u32[]{:S(2)}) collective-permute-start(bf16[128,1024]{1,0:T(8,128)(2,1)} %get-tuple-element.42), channel_id=1, source_target_pairs={{0,1},{1,0},{2,3},{3,2},{4,5},{5,4},{6,7},{7,6},{8,9},{9,8},{10,11... | collective-permute-start | bytes 786440 | tf_op jit(solution)/shard_map/ppermute | solution.py:327
  12.1 15.4 %copy-start = (bf16[256,1024]{1,0:T(8,128)(2,1)}, bf16[256,1024]{1,0:T(8,128)(2,1)S(1)}, u32[]{:S(2)}) copy-start(bf16[256,1024]{1,0:T(8,128)(2,1)S(1)} %constant_dynamic-update-slice_fusion.2.refs_0_) | copy-start | bytes 1572868
  12.1 16.4 %collective-permute-start.2 = (bf16[256,1024]{1,0:T(8,128)(2,1)S(1)}, bf16[256,1024]{1,0:T(8,128)(2,1)S(1)}, u32[]{:S(2)}, u32[]{:S(2)}) collective-permute-start(bf16[256,1024]{1,0:T(8,128)(2,1)S(1)} %constant_dynamic-update-slice_fusion.2.refs_0_), channel_id=1, source_target_pairs={{0,2},{2,4},{3,1},{4,6},{5,3},{7,5},{8,10},{10,12},{11,9},{12,14},... | collective-permute-start | bytes 1572872 | tf_op jit(solution)/shard_map/ppermute | solution.py:327
  17.1 10.4 %copy-start.13 = (bf16[256,1024]{1,0:T(8,128)(2,1)}, bf16[256,1024]{1,0:T(8,128)(2,1)S(1)}, u32[]{:S(2)}) copy-start(bf16[256,1024]{1,0:T(8,128)(2,1)S(1)} %constant_dynamic-update-slice_fusion.refs_0_) | copy-start | bytes 1572868
  17.1 28.2 %collective-permute-start.3 = (bf16[256,1024]{1,0:T(8,128)(2,1)S(1)}, bf16[256,1024]{1,0:T(8,128)(2,1)S(1)}, u32[]{:S(2)}, u32[]{:S(2)}) collective-permute-start(bf16[256,1024]{1,0:T(8,128)(2,1)S(1)} %constant_dynamic-update-slice_fusion.refs_0_), channel_id=1, source_target_pairs={{0,2},{2,4},{3,1},{4,6},{5,3},{7,5},{8,10},{10,12},{11,9},{12,14},... | collective-permute-start | bytes 1572872 | tf_op jit(solution)/shard_map/ppermute | solution.py:327
  28.5 53.8 %copy-start.3 = (bf16[256,1024]{1,0:T(8,128)(2,1)}, bf16[256,1024]{1,0:T(8,128)(2,1)S(1)}, u32[]{:S(2)}) copy-start(bf16[256,1024]{1,0:T(8,128)(2,1)S(1)} %collective-permute-done.2.refs_1_) | copy-start | bytes 1572868
  28.5 53.0 %collective-permute-start.4 = (bf16[256,1024]{1,0:T(8,128)(2,1)S(1)}, bf16[256,1024]{1,0:T(8,128)(2,1)S(1)}, u32[]{:S(2)}, u32[]{:S(2)}) collective-permute-start(bf16[256,1024]{1,0:T(8,128)(2,1)S(1)} %collective-permute-done.2.refs_1_), channel_id=1, source_target_pairs={{2,4},{3,1},{4,6},{5,3},{10,12},{11,9},{12,14},{13,11},{18,20},{19... | collective-permute-start | bytes 1572872 | tf_op jit(solution)/shard_map/ppermute | solution.py:327
  45.3 43.6 %copy-start.14 = (bf16[256,1024]{1,0:T(8,128)(2,1)}, bf16[256,1024]{1,0:T(8,128)(2,1)S(1)}, u32[]{:S(2)}) copy-start(bf16[256,1024]{1,0:T(8,128)(2,1)S(1)} %collective-permute-done.3.refs_1_) | copy-start | bytes 1572868
  45.3 36.2 %collective-permute-start.5 = (bf16[256,1024]{1,0:T(8,128)(2,1)S(1)}, bf16[256,1024]{1,0:T(8,128)(2,1)}, u32[]{:S(2)}, u32[]{:S(2)}) collective-permute-start(bf16[256,1024]{1,0:T(8,128)(2,1)S(1)} %collective-permute-done.3.refs_1_), channel_id=1, source_target_pairs={{2,4},{3,1},{4,6},{5,3},{10,12},{11,9},{12,14},{13,11},{18,20},{19... | collective-permute-start | bytes 1572872 | tf_op jit(solution)/shard_map/ppermute | solution.py:327
  81.5 12.9 %copy-start.4 = (bf16[256,1024]{1,0:T(8,128)(2,1)}, bf16[256,1024]{1,0:T(8,128)(2,1)S(1)}, u32[]{:S(2)}) copy-start(bf16[256,1024]{1,0:T(8,128)(2,1)S(1)} %collective-permute-done.4.refs_2_) | copy-start | bytes 1572868
  81.5 4.8 %collective-permute-start.10 = (bf16[256,1024]{1,0:T(8,128)(2,1)S(1)}, bf16[256,1024]{1,0:T(8,128)(2,1)S(1)}, u32[]{:S(2)}, u32[]{:S(2)}) collective-permute-start(bf16[256,1024]{1,0:T(8,128)(2,1)S(1)} %collective-permute-done.4.refs_2_), channel_id=1, source_target_pairs={{3,1},{4,6},{11,9},{12,14},{19,17},{20,22},{27,25},{28,30}} | collective-permute-start | bytes 1572872 | tf_op jit(solution)/shard_map/ppermute | solution.py:327
  82.2 6.7 %collective-permute-start.11 = (bf16[256,1024]{1,0:T(8,128)(2,1)S(1)}, bf16[256,1024]{1,0:T(8,128)(2,1)S(1)}, u32[]{:S(2)}, u32[]{:S(2)}) collective-permute-start(bf16[256,1024]{1,0:T(8,128)(2,1)S(1)} %collective-permute-done.2.refs_1_), channel_id=1, source_target_pairs={{1,0},{2,3},{3,2},{4,5},{5,4},{6,7},{9,8},{10,11},{11,10},{12,13},... | collective-permute-start | bytes 1572872 | tf_op jit(solution)/shard_map/ppermute | solution.py:327
  83.5 6.7 %collective-permute-start.6 = (bf16[256,1024]{1,0:T(8,128)(2,1)}, bf16[256,1024]{1,0:T(8,128)(2,1)}, u32[]{:S(2)}, u32[]{:S(2)}) collective-permute-start(bf16[256,1024]{1,0:T(8,128)(2,1)} %collective-permute-done.5.refs_2_), channel_id=1, source_target_pairs={{3,1},{4,6},{11,9},{12,14},{19,17},{20,22},{27,25},{28,30}} | collective-permute-start | bytes 1572872 | tf_op jit(solution)/shard_map/ppermute | solution.py:327
  85.0 6.7 %collective-permute-start.12 = (bf16[256,1024]{1,0:T(8,128)(2,1)S(1)}, bf16[256,1024]{1,0:T(8,128)(2,1)S(1)}, u32[]{:S(2)}, u32[]{:S(2)}) collective-permute-start(bf16[256,1024]{1,0:T(8,128)(2,1)S(1)} %collective-permute-done.4.refs_2_), channel_id=1, source_target_pairs={{1,0},{3,2},{4,5},{6,7},{9,8},{11,10},{12,13},{14,15},{17,16},{19,... | collective-permute-start | bytes 1572872 | tf_op jit(solution)/shard_map/ppermute | solution.py:327
  86.3 8.0 %copy-start.5 = (bf16[256,1024]{1,0:T(8,128)(2,1)}, bf16[256,1024]{1,0:T(8,128)(2,1)S(1)}, u32[]{:S(2)}) copy-start(bf16[256,1024]{1,0:T(8,128)(2,1)S(1)} %collective-permute-done.10.refs_3_) | copy-start | bytes 1572868
  86.3 8.0 %collective-permute-start.13 = (bf16[256,1024]{1,0:T(8,128)(2,1)S(1)}, bf16[256,1024]{1,0:T(8,128)(2,1)S(1)}, u32[]{:S(2)}, u32[]{:S(2)}) collective-permute-start(bf16[256,1024]{1,0:T(8,128)(2,1)S(1)} %collective-permute-done.10.refs_3_), channel_id=1, source_target_pairs={{1,0},{6,7},{9,8},{14,15},{17,16},{22,23},{25,24},{30,31}} | collective-permute-start | bytes 1572872 | tf_op jit(solution)/shard_map/ppermute | solution.py:327
  87.6 21.3 %collective-permute-start.8 = (bf16[256,1024]{1,0:T(8,128)(2,1)}, bf16[256,1024]{1,0:T(8,128)(2,1)}, u32[]{:S(2)}, u32[]{:S(2)}) collective-permute-start(bf16[256,1024]{1,0:T(8,128)(2,1)} %collective-permute-done.5.refs_2_), channel_id=1, source_target_pairs={{1,0},{3,2},{4,5},{6,7},{9,8},{11,10},{12,13},{14,15},{17,16},{19,... | collective-permute-start | bytes 1572872 | tf_op jit(solution)/shard_map/ppermute | solution.py:327
  89.0 5.4 %copy-start.6 = (bf16[256,1024]{1,0:T(8,128)(2,1)}, bf16[256,1024]{1,0:T(8,128)(2,1)S(1)}, u32[]{:S(2)}) copy-start(bf16[256,1024]{1,0:T(8,128)(2,1)S(1)} %collective-permute-done.11.refs_4_) | copy-start | bytes 1572868
  89.0 20.0 %collective-permute-start.7 = (bf16[256,1024]{1,0:T(8,128)(2,1)S(1)}, bf16[256,1024]{1,0:T(8,128)(2,1)S(1)}, u32[]{:S(2)}, u32[]{:S(2)}) collective-permute-start(bf16[256,1024]{1,0:T(8,128)(2,1)S(1)} %collective-permute-done.3.refs_1_), channel_id=1, source_target_pairs={{1,0},{2,3},{3,2},{4,5},{5,4},{6,7},{9,8},{10,11},{11,10},{12,13},... | collective-permute-start | bytes 1572872 | tf_op jit(solution)/shard_map/ppermute | solution.py:327
  90.3 18.7 %collective-permute-start.9 = (bf16[256,1024]{1,0:T(8,128)(2,1)}, bf16[256,1024]{1,0:T(8,128)(2,1)}, u32[]{:S(2)}, u32[]{:S(2)}) collective-permute-start(bf16[256,1024]{1,0:T(8,128)(2,1)} %collective-permute-done.6.refs_3_), channel_id=1, source_target_pairs={{1,0},{6,7},{9,8},{14,15},{17,16},{22,23},{25,24},{30,31}} | collective-permute-start | bytes 1572872 | tf_op jit(solution)/shard_map/ppermute | solution.py:327
  91.8 2.6 %copy-start.7 = (bf16[256,1024]{1,0:T(8,128)(2,1)}, bf16[256,1024]{1,0:T(8,128)(2,1)S(1)}, u32[]{:S(2)}) copy-start(bf16[256,1024]{1,0:T(8,128)(2,1)S(1)} %collective-permute-done.12.refs_5_) | copy-start | bytes 1572868
  94.4 0.8 copy-start.8
  105.9 19.6 %collective-permute-start.14 = (bf16[2,4,128,384]{3,2,1,0:T(8,128)(2,1)}, bf16[2,4,128,384]{3,2,1,0:T(8,128)(2,1)}, u32[]{:S(2)}, u32[]{:S(2)}) collective-permute-start(bf16[2,4,128,384]{3,2,1,0:T(8,128)(2,1)} %get-tuple-element.62), channel_id=1, source_target_pairs={{0,8},{8,0},{16,24},{24,16},{1,9},{9,1},{17,25},{25,17},{2,10},{10... | collective-permute-start | bytes 2359304 | tf_op jit(solution)/shard_map/ppermute | solution.py:461
  107.5 18.1 %collective-permute-start.15 = (bf16[2,4,128,384]{3,2,1,0:T(8,128)(2,1)}, bf16[2,4,128,384]{3,2,1,0:T(8,128)(2,1)}, u32[]{:S(2)}, u32[]{:S(2)}) collective-permute-start(bf16[2,4,128,384]{3,2,1,0:T(8,128)(2,1)} %get-tuple-element.64), channel_id=1, source_target_pairs={{0,16},{8,24},{16,0},{24,8},{1,17},{9,25},{17,1},{25,9},{2,18},{10... | collective-permute-start | bytes 2359304 | tf_op jit(solution)/shard_map/ppermute | solution.py:461
  108.9 0.8 copy-start.15
  128.6 8.0 %copy-start.17 = (bf16[1,4,128,384]{3,2,1,0:T(8,128)(2,1)S(1)}, bf16[1,4,128,384]{3,2,1,0:T(8,128)(2,1)}, u32[]{:S(2)}) copy-start(bf16[1,4,128,384]{3,2,1,0:T(8,128)(2,1)} %get-tuple-element.75) | copy-start | bytes 1179652
  128.6 9.4 %copy-start.16 = (bf16[1,4,128,384]{3,2,1,0:T(8,128)(2,1)S(1)}, bf16[1,4,128,384]{3,2,1,0:T(8,128)(2,1)}, u32[]{:S(2)}) copy-start(bf16[1,4,128,384]{3,2,1,0:T(8,128)(2,1)} %get-tuple-element.76) | copy-start | bytes 1179652
  135.4 25.6 %copy-start.10 = (bf16[1,4,128,384]{3,2,1,0:T(8,128)(2,1)S(1)}, bf16[1,4,128,384]{3,2,1,0:T(8,128)(2,1)}, u32[]{:S(2)}) copy-start(bf16[1,4,128,384]{3,2,1,0:T(8,128)(2,1)} %get-tuple-element.65.refs_0_) | copy-start | bytes 1179652
  135.4 27.0 %copy-start.9 = (bf16[1,4,128,384]{3,2,1,0:T(8,128)(2,1)S(1)}, bf16[1,4,128,384]{3,2,1,0:T(8,128)(2,1)}, u32[]{:S(2)}) copy-start(bf16[1,4,128,384]{3,2,1,0:T(8,128)(2,1)} %get-tuple-element.66.refs_1_) | copy-start | bytes 1179652
  135.4 16.1 %collective-permute-start.16 = (bf16[2,4,128,384]{3,2,1,0:T(8,128)(2,1)}, bf16[2,4,128,384]{3,2,1,0:T(8,128)(2,1)S(1)}, u32[]{:S(2)}, u32[]{:S(2)}) collective-permute-start(bf16[2,4,128,384]{3,2,1,0:T(8,128)(2,1)} %get-tuple-element.68), channel_id=1, source_target_pairs={{0,8},{8,0},{16,24},{24,16},{1,9},{9,1},{17,25},{25,17},{2,10},{10... | collective-permute-start | bytes 2359304 | tf_op jit(solution)/shard_map/ppermute | solution.py:461
  136.0 16.5 %collective-permute-start.17 = (bf16[2,4,128,384]{3,2,1,0:T(8,128)(2,1)}, bf16[2,4,128,384]{3,2,1,0:T(8,128)(2,1)S(1)}, u32[]{:S(2)}, u32[]{:S(2)}) collective-permute-start(bf16[2,4,128,384]{3,2,1,0:T(8,128)(2,1)} %get-tuple-element.70), channel_id=1, source_target_pairs={{0,16},{8,24},{16,0},{24,8},{1,17},{9,25},{17,1},{25,9},{2,18},{10... | collective-permute-start | bytes 2359304 | tf_op jit(solution)/shard_map/ppermute | solution.py:461
  136.6 24.4 %collective-permute-start.18 = (bf16[1,4,128,384]{3,2,1,0:T(8,128)(2,1)S(1)}, bf16[1,4,128,384]{3,2,1,0:T(8,128)(2,1)S(1)}, u32[]{:S(2)}, u32[]{:S(2)}) collective-permute-start(bf16[1,4,128,384]{3,2,1,0:T(8,128)(2,1)S(1)} %copy-done.17), channel_id=1, source_target_pairs={{0,16},{8,24},{16,0},{24,8},{1,17},{9,25},{17,1},{25,9},{2,18},{10... | collective-permute-start | bytes 1179656 | tf_op jit(solution)/shard_map/ppermute | solution.py:461
  138.1 24.4 %collective-permute-start.19 = (bf16[1,4,128,384]{3,2,1,0:T(8,128)(2,1)S(1)}, bf16[1,4,128,384]{3,2,1,0:T(8,128)(2,1)S(1)}, u32[]{:S(2)}, u32[]{:S(2)}) collective-permute-start(bf16[1,4,128,384]{3,2,1,0:T(8,128)(2,1)S(1)} %copy-done.16), channel_id=1, source_target_pairs={{0,8},{8,0},{16,24},{24,16},{1,9},{9,1},{17,25},{25,17},{2,10},{10... | collective-permute-start | bytes 1179656 | tf_op jit(solution)/shard_map/ppermute | solution.py:461
  151.5 1.0 copy-start.1
  152.6 0.9 copy-start.2
  156.6 27.5 %copy-start.12 = (bf16[1,4,128,384]{3,2,1,0:T(8,128)(2,1)S(1)}, bf16[1,4,128,384]{3,2,1,0:T(8,128)(2,1)}, u32[]{:S(2)}) copy-start(bf16[1,4,128,384]{3,2,1,0:T(8,128)(2,1)} %get-tuple-element.77) | copy-start | bytes 1179652
  156.6 28.6 %copy-start.11 = (bf16[1,4,128,384]{3,2,1,0:T(8,128)(2,1)S(1)}, bf16[1,4,128,384]{3,2,1,0:T(8,128)(2,1)}, u32[]{:S(2)}) copy-start(bf16[1,4,128,384]{3,2,1,0:T(8,128)(2,1)} %get-tuple-element.79) | copy-start | bytes 1179652
  156.6 27.5 %collective-permute-start.20 = (bf16[1,4,128,384]{3,2,1,0:T(8,128)(2,1)}, bf16[1,4,128,384]{3,2,1,0:T(8,128)(2,1)}, u32[]{:S(2)}, u32[]{:S(2)}) collective-permute-start(bf16[1,4,128,384]{3,2,1,0:T(8,128)(2,1)} %get-tuple-element.78), channel_id=1, source_target_pairs={{0,16},{8,24},{16,0},{24,8},{1,17},{9,25},{17,1},{25,9},{2,18},{10... | collective-permute-start | bytes 1179656 | tf_op jit(solution)/shard_map/ppermute | solution.py:461
  161.1 24.1 %collective-permute-start.21 = (bf16[1,4,128,384]{3,2,1,0:T(8,128)(2,1)}, bf16[1,4,128,384]{3,2,1,0:T(8,128)(2,1)S(1)}, u32[]{:S(2)}, u32[]{:S(2)}) collective-permute-start(bf16[1,4,128,384]{3,2,1,0:T(8,128)(2,1)} %get-tuple-element.80), channel_id=1, source_target_pairs={{0,8},{8,0},{16,24},{24,16},{1,9},{9,1},{17,25},{25,17},{2,10},{10... | collective-permute-start | bytes 1179656 | tf_op jit(solution)/shard_map/ppermute | solution.py:461
Sparse Core Ops, SparseCore 0:
  10.2 60.8 all-gather.1
  125.6 56.5 reduce-scatter.1

commit v13 on v9

--- a/solution.py
+++ b/solution.py
@@ -14,6 +14,7 @@
 bf16, f32 = jnp.bfloat16, jnp.float32
 ANY = pl.BlockSpec(memory_space=pl.ANY)
 SMEM = pl.BlockSpec(memory_space=pltpu.SMEM)
+VMEM = pl.BlockSpec(memory_space=pltpu.VMEM)
 FIRST = (((0,), (0,)), ((), ()))
 
 
@@ -214,6 +215,24 @@
         copy.wait()
 
 
+def put_kernel(start, *refs):
+    *pairs, out, total, sem = refs
+    count = total.shape[1]
+    cut = total.shape[2]
+    copies = []
+    for g in range(total.shape[0]):
+        keep, got = pairs[2 * g], pairs[2 * g + 1]
+        total[g] = keep[0].astype(f32) + got[0].astype(f32)
+        copies.append(
+            pltpu.make_async_copy(
+                total.at[g], out.at[pl.ds(start, count), pl.ds(g * cut, cut), :], sem.at[g]
+            )
+        )
+        copies[-1].start()
+    for copy in copies:
+        copy.wait()
+
+
 def finish_kernel(width, top, rows, token, gate):
     token[...] = rows[:, pl.ds(0, width)]
     gate[...] = rows[:, pl.ds(width, LANES)].astype(f32).T[:top].astype(bf16)
@@ -312,12 +331,13 @@
     swaps = [None] + [
         [(p, p ^ 1) for p in range(ep_count) if reach(p, -step) is not None] for step in range(1, groups)
     ]
-    moving, dy_mine, dy_other = dy_own, [], []
-    for step in range(1, groups - 1):
-        moving = hop(moving, lines[step])
-        if step == 1:
-            moving, w_flip = lax.optimization_barrier((moving, w_flip))
-        dy_mine.append(moving)
+    far = [(p, reach(p, 2)) for p in range(ep_count) if reach(p, 2) is not None]
+    dy_mine = [hop(dy_own, lines[1])]
+    far_own, w_flip = lax.optimization_barrier((dy_own, w_flip))
+    if groups > 2:
+        dy_mine.append(hop(far_own, far))
+    for step in range(3, groups - 1):
+        dy_mine.append(hop(dy_mine[-1], lines[step]))
 
     act = shape(experts, routes, hidden)
     act_spec = by_expert(routes, hidden)
@@ -362,7 +382,8 @@
         ],
     )(place, x_all, w_up)
     *dy_mine, hid = lax.optimization_barrier((*dy_mine, hid))
-    dy_mine.append(hop(dy_mine[-1], lines[-1]))
+    if groups > 3:
+        dy_mine.append(hop(dy_mine[-1], lines[-1]))
     dy_other = [hop(part, swap) for part, swap in zip(dy_mine, swaps[1:])]
 
     orders = []
@@ -440,10 +461,42 @@
 
     counts = [experts // 2, experts - experts // 2] if experts > 1 else [experts]
     states = [down(start, count) for start, count in zip((0, counts[0]), counts)]
-    for t in range(bits):
+    for t in range(bits - 1):
         states = [exchange(state, t) for state in states]
-    token_grad, states = lax.optimization_barrier((token_grad, states))
-    down_grad = jnp.concatenate([jnp.concatenate(state, axis=1) for state in states], axis=0)
+    last = bits - 1
+    states = [
+        [
+            (keep, lax.ppermute(send, "dp", [(i, i ^ (1 << ((g + last) % bits))) for i in range(dp_count)]))
+            for g, (keep, send) in enumerate(state)
+        ]
+        for state in states
+    ]
+    keeps = [keep for keep, _ in states[-1]]
+    token_grad, keeps = lax.optimization_barrier((token_grad, keeps))
+    states[-1] = [(keep, got) for keep, (_, got) in zip(keeps, states[-1])]
+    down_grad, start = None, 0
+    for count, state in zip(counts, states):
+        operands = [x for pair in state for x in pair]
+        dest = [] if down_grad is None else [down_grad]
+
+        def put(*refs, start=start, skip=len(dest), used=len(operands)):
+            put_kernel(start, *refs[:used], *refs[used + skip :])
+
+        down_grad = pl.pallas_call(
+            put,
+            in_specs=[VMEM] * len(operands) + [ANY] * len(dest),
+            out_specs=ANY,
+            out_shape=shape(experts, share, hidden, dtype=f32),
+            input_output_aliases={len(operands): 0} if dest else {},
+            scratch_shapes=[
+                pltpu.VMEM((turns, count, cut_rows, hidden), f32),
+                pltpu.SemaphoreType.DMA((turns,)),
+            ],
+            compiler_params=pltpu.CompilerParams(vmem_limit_bytes=VMEM_LIMIT // 2),
+            cost_estimate=cost(0, 4 * experts * share * hidden),
+            name="put",
+        )(*operands, *dest)
+        start += count
     return (token_grad, gate_grad.T, down_grad)
 
 

time: 191 us -> 201 us (1.052)
  waiting for transfers between devices: 98 us -> 105 us
  starting transfers between devices: 21.5 us -> 25.9 us
  other arithmetic: 3.6 us -> 1.33 us
  Pallas kernels: 50.5 us -> 52.6 us
    all_gather x1, waiting for transfers between devices: 23.5 us -> 46.7 us  [shards(): x_all = lax.all_gather(x_own, 'ep', axis=0, tiled=True)]
    ppermute x8 -> x4, waiting for transfers between devices: 38.1 us -> 23.7 us  [exchange(): got = lax.ppermute(send, 'dp', [(i, i ^ bit) for i in range(dp_count)])]
    ppermute x7, waiting for transfers between devices: 36.3 us -> 23.1 us  [hop(): return lax.ppermute(value, 'ep', pairs)]
    ppermute x0 -> x4, waiting for transfers between devices: none -> 11.3 us  [shards(): lax.ppermute(send, 'dp', [(i, i ^ 1 << (g + last) % bits) for i in range(...]
    ppermute x0 -> x4, starting transfers between devices: none -> 6.3 us  [shards(): lax.ppermute(send, 'dp', [(i, i ^ 1 << (g + last) % bits) for i in range(...]
    ppermute x8 -> x4, starting transfers between devices: 10.5 us -> 4.19 us  [exchange(): got = lax.ppermute(send, 'dp', [(i, i ^ bit) for i in range(dp_count)])]
    ppermute x7, starting transfers between devices: 10.9 us -> 15.3 us  [hop(): return lax.ppermute(value, 'ep', pairs)]
    pallas_call x0 -> x2, Pallas kernels: none -> 2.47 us  [shards(): pl.pallas_call(put, in_specs=[VMEM] * len(operands) + [ANY] * len(dest),...]
  transfers between devices with their start and end apart: 17 -> 17, of which waited for: 9 -> 7; matrix products, arithmetic and copies ran while one was open for 2% -> 1% of each run, Pallas kernels for 15% -> 16%
where the time goes in v13:
time: 201 us; the launch traced here: 200 us
  waiting for transfers between devices  105 us (52%)
  Pallas kernels  52.6 us (26%)
  starting transfers between devices  25.9 us (13%)
  between operations  14.3 us (7%)
    all_gather x1, waiting for transfers between devices, shards(): x_all = lax.all_gather(x_own, 'ep', axis=0, tiled=True)  46.7 us
    ppermute x4, waiting for transfers between devices, exchange(): got = lax.ppermute(send, 'dp', [(i, i ^ bit) for i in range(dp_count)])  23.7 us
    ppermute x7, waiting for transfers between devices, hop(): return lax.ppermute(value, 'ep', pairs)  23.1 us
    pallas_call x1, Pallas kernels, shards(): one(functools.partial(tail_kernel, groups, cap, width, top), 'tail', 8 *...  17.8 us
    ppermute x7, starting transfers between devices, hop(): return lax.ppermute(value, 'ep', pairs)  15.3 us
    pallas_call x2, Pallas kernels, down(): one(functools.partial(down_kernel, orders, start), 'down', 16 * main_flop...  11.4 us
    ppermute x4, waiting for transfers between devices, shards(): lax.ppermute(send, 'dp', [(i, i ^ 1 << (g + last) % bits) for i in range(...  11.3 us
    pallas_call x1, Pallas kernels, shards(): one(functools.partial(up_kernel, groups, width, top, cap, 0), 'up', pick_...  10.4 us
  transfers between devices with their start and end apart: 17, of which 7 were waited for; matrix products, arithmetic and copies ran while one was open for 1% of the time, Pallas kernels for 16%

profile of v13, /device:TPU:0, one launch (start us, length us, event | category | flops | bytes accessed | tf_op | source)
XLA Modules:
  0.0 200.4 jit_solution(12858359125636405161)
XLA Ops:
  7.2 0.0 all-gather.2.cloned.1.call-start
  7.2 2.0 %pack.1 = bf16[128,2176]{1,0:T(8,128)(2,1)} custom-call(bf16[128,2048]{1,0:T(8,128)(2,1)} %tokens.1, s32[8,128]{1,0:T(8,128)} %bitcast.7, bf16[8,128]{1,0:T(8,128)(2,1)} %bitcast.8), custom_call_target="tpu_custom_call" | custom-call | bytes 1048576 | tf_op jit(solution)/shard_map/pack/pallas_call | solution.py:267
  9.2 0.0 all-gather.2.cloned.1.call-update
  9.3 0.0 reduce-scatter.2.cloned.1.call-start
  9.3 0.5 collective-permute-start
  9.8 6.6 %flip.1.refs_9_ = bf16[4,384,2048]{2,1,0:T(8,128)(2,1)} custom-call(bf16[4,2048,384]{2,1,0:T(8,128)(2,1)} %w_up.1), custom_call_target="tpu_custom_call" | custom-call | bytes 12582912 | tf_op jit(solution)/shard_map/flip/pallas_call | solution.py:315
  16.6 0.0 copy-start.5
  16.6 4.6 %collective-permute-start.1 = (bf16[256,2048]{1,0:T(8,128)(2,1)S(1)}, bf16[256,2048]{1,0:T(8,128)(2,1)S(1)}, u32[]{:S(2)}, u32[]{:S(2)}) collective-permute-start(bf16[256,2048]{1,0:T(8,128)(2,1)S(1)} %constant_dynamic-update-slice_fusion.refs_0_), channel_id=1, source_target_pairs={{0,2},{2,4},{3,1},{4,6},{5,3},{7,5},{8,10},{10,12},{11,9},{12,14},... | collective-permute-start | bytes 3145736 | tf_op jit(solution)/shard_map/ppermute | solution.py:281
  21.1 5.4 %collective-permute-start.2 = (bf16[256,2048]{1,0:T(8,128)(2,1)S(1)}, bf16[256,2048]{1,0:T(8,128)(2,1)}, u32[]{:S(2)}, u32[]{:S(2)}) collective-permute-start(bf16[256,2048]{1,0:T(8,128)(2,1)S(1)} %constant_dynamic-update-slice_fusion.refs_0_), channel_id=1, source_target_pairs={{0,4},{2,6},{5,1},{7,3},{8,12},{10,14},{13,9},{15,11},{16,20},{18,... | collective-permute-start | bytes 3145736 | tf_op jit(solution)/shard_map/ppermute | solution.py:281
  26.6 0.6 pad_add_fusion.place
  27.1 46.7 %all-gather.2.cloned.1.call-done.x_all = bf16[1024,2176]{1,0:T(8,128)(2,1)} async-done(((bf16[128,2176]{1,0:T(8,128)(2,1)}), bf16[1024,2176]{1,0:T(8,128)(2,1)}) %all-gather.2.cloned.1.call-update) | async-done | bytes 4456464 | tf_op jit(solution)/shard_map/all_gather | solution.py:274
  73.8 10.4 %up.1 = (bf16[4,320,256]{2,1,0:T(8,128)(2,1)}, bf16[1024,128]{1,0:T(8,128)(2,1)}, bf16[4,320,384]{2,1,0:T(8,128)(2,1)}, bf16[4,320,384]{2,1,0:T(8,128)(2,1)}, bf16[4,320,384]{2,1,0:T(8,128)(2,1)}) custom-call(s32[4]{0:T(128)} %pad_add_fusion.place, bf16[1024,2176]{1,0:T(8,128)(2,1)} %all-gather.2.cloned.1.call-done.x_all, bf16[4,2048,384]{2,1,0:T(8,128)(2,1)} %w_up.1), custom_call_target="tpu_custom_call" | custom-call | flops 3355443200 | bytes 10747904 | tf_op jit(solution)/shard_map/up/pallas_call | solution.py:363
  84.3 0.0 collective-permute-done.1.refs_1_
  84.3 0.7 collective-permute-start.3
  85.0 1.3 collective-permute-start.5
  86.3 1.3 collective-permute-start.4
  87.6 1.5 collective-permute-start.6
  89.1 10.1 %collective-permute-done.4.refs_4_ = bf16[256,2048]{1,0:T(8,128)(2,1)S(1)} collective-permute-done((bf16[256,2048]{1,0:T(8,128)(2,1)S(1)}, bf16[256,2048]{1,0:T(8,128)(2,1)S(1)}, u32[]{:S(2)}, u32[]{:S(2)}) %collective-permute-start.4) | collective-permute-done | bytes 1048608 | tf_op jit(solution)/shard_map/ppermute | solution.py:281
  99.2 12.9 %collective-permute-done.6.refs_6_ = bf16[256,2048]{1,0:T(8,128)(2,1)S(1)} collective-permute-done((bf16[256,2048]{1,0:T(8,128)(2,1)S(1)}, bf16[256,2048]{1,0:T(8,128)(2,1)S(1)}, u32[]{:S(2)}, u32[]{:S(2)}) %collective-permute-start.6) | collective-permute-done | bytes 1048608 | tf_op jit(solution)/shard_map/ppermute | solution.py:281
  112.2 1.0 copy-done.10
  113.2 17.8 %tail.1 = (bf16[1024,2176]{1,0:T(8,128)(2,1)}, bf16[4,320,2048]{2,1,0:T(8,128)(2,1)}) custom-call(s32[4]{0:T(128)} %pad_add_fusion.place, bf16[256,2048]{1,0:T(8,128)(2,1)} %copy-done.5, bf16[256,2048]{1,0:T(8,128)(2,1)} %copy-done.6, bf16[256,2048]{1,0:T(8,128)(2,1)} %collective-permute-done.2.refs_2_, bf16[256,2048]{1,0:T(8,128)(2,1)} %copy-done.7, ...), custom_call_target="tpu_custom_call" | custom-call | flops 16106127360 | bytes 25165824 | tf_op jit(solution)/shard_map/tail/pallas_call | solution.py:429
  131.0 0.0 reduce-scatter.2.cloned.1.call-update
  131.0 5.6 %down.3 = (bf16[2,2,256,384]{3,2,1,0:T(8,128)(2,1)}, bf16[2,2,256,384]{3,2,1,0:T(8,128)(2,1)}, bf16[2,2,256,384]{3,2,1,0:T(8,128)(2,1)}, bf16[2,2,256,384]{3,2,1,0:T(8,128)(2,1)}) custom-call(s32[4]{0:T(128)} %pad_add_fusion.place, bf16[4,320,2048]{2,1,0:T(8,128)(2,1)} %get-tuple-element.39.kept, bf16[4,320,384]{2,1,0:T(8,128)(2,1)} %get-tuple-element.40.scaled_in), custom_call_target="tpu_custom_call" | custom-call | flops 32212254720 | bytes 50331648 | tf_op jit(solution)/shard_map/down/pallas_call | solution.py:399
  136.6 1.6 collective-permute-start.11
  138.2 1.5 collective-permute-start.13
  139.7 5.8 %down.2 = (bf16[2,2,256,384]{3,2,1,0:T(8,128)(2,1)}, bf16[2,2,256,384]{3,2,1,0:T(8,128)(2,1)}, bf16[2,2,256,384]{3,2,1,0:T(8,128)(2,1)}, bf16[2,2,256,384]{3,2,1,0:T(8,128)(2,1)}) custom-call(s32[4]{0:T(128)} %pad_add_fusion.place, bf16[4,320,2048]{2,1,0:T(8,128)(2,1)} %get-tuple-element.39.kept, bf16[4,320,384]{2,1,0:T(8,128)(2,1)} %get-tuple-element.40.scaled_in), custom_call_target="tpu_custom_call" | custom-call | flops 32212254720 | bytes 50331648 | tf_op jit(solution)/shard_map/down/pallas_call | solution.py:399
  145.6 0.6 collective-permute-start.7
  146.2 0.5 collective-permute-start.8
  146.7 10.6 %collective-permute-done.11 = bf16[2,2,256,384]{3,2,1,0:T(8,128)(2,1)S(1)} collective-permute-done((bf16[2,2,256,384]{3,2,1,0:T(8,128)(2,1)}, bf16[2,2,256,384]{3,2,1,0:T(8,128)(2,1)S(1)}, u32[]{:S(2)}, u32[]{:S(2)}) %collective-permute-start.11) | collective-permute-done | bytes 786464 | tf_op jit(solution)/shard_map/ppermute | solution.py:421
  157.3 0.2 add_convert_fusion.1
  157.4 0.1 fusion.1
  157.5 1.6 collective-permute-start.12
  159.1 0.2 add_convert_fusion
  159.3 0.1 fusion
  159.4 1.6 collective-permute-start.14
  161.0 13.1 %collective-permute-done.7 = bf16[2,2,256,384]{3,2,1,0:T(8,128)(2,1)S(1)} collective-permute-done((bf16[2,2,256,384]{3,2,1,0:T(8,128)(2,1)}, bf16[2,2,256,384]{3,2,1,0:T(8,128)(2,1)S(1)}, u32[]{:S(2)}, u32[]{:S(2)}) %collective-permute-start.7) | collective-permute-done | bytes 786464 | tf_op jit(solution)/shard_map/ppermute | solution.py:421
  174.1 0.2 add_convert_fusion.3
  174.3 0.1 fusion.3
  174.4 1.6 collective-permute-start.9
  176.0 0.2 add_convert_fusion.2
  176.2 0.1 fusion.2
  176.3 1.6 collective-permute-start.10
  177.8 6.3 %collective-permute-done.12.refs_1_ = bf16[1,2,256,384]{3,2,1,0:T(8,128)(2,1)S(1)} collective-permute-done((bf16[1,2,256,384]{3,2,1,0:T(8,128)(2,1)S(1)}, bf16[1,2,256,384]{3,2,1,0:T(8,128)(2,1)S(1)}, u32[]{:S(2)}, u32[]{:S(2)}) %collective-permute-start.12) | collective-permute-done | bytes 393248 | tf_op jit(solution)/shard_map/ppermute | solution.py:469
  184.1 1.2 put.2.refs_4_
  185.3 0.0 reduce-scatter.2.cloned.1.call-done.rows
  185.4 1.9 finish.1
  187.2 5.1 %collective-permute-done.9.refs_1_ = bf16[1,2,256,384]{3,2,1,0:T(8,128)(2,1)S(1)} collective-permute-done((bf16[1,2,256,384]{3,2,1,0:T(8,128)(2,1)S(1)}, bf16[1,2,256,384]{3,2,1,0:T(8,128)(2,1)S(1)}, u32[]{:S(2)}, u32[]{:S(2)}) %collective-permute-start.9) | collective-permute-done | bytes 393248 | tf_op jit(solution)/shard_map/ppermute | solution.py:469
  192.3 1.2 put.3
  (30 shorter events, 0.1 us)
Async XLA Ops:
  7.2 2.1 %copy-start.4 = (bf16[128,2048]{1,0:T(8,128)(2,1)S(1)}, bf16[128,2048]{1,0:T(8,128)(2,1)}, u32[]{:S(2)}) copy-start(bf16[128,2048]{1,0:T(8,128)(2,1)} %param.7) | copy-start | bytes 1572868
  7.2 66.7 %all-gather.2.cloned.1.call-start = ((), (), s32[]{:S(2)}) async-start(), calls=%async_computation.1 | async-start | bytes 5013504 | tf_op jit(solution)/shard_map/all_gather | solution.py:274
  9.3 176.1 %reduce-scatter.2.cloned.1.call-start = ((), (), s32[]{:S(2)}) async-start(), calls=%async_computation.2 | async-start | bytes 5013504 | tf_op jit(solution)/shard_map/reduce_scatter | solution.py:453
  9.3 7.2 %collective-permute-start = (bf16[128,2048]{1,0:T(8,128)(2,1)S(1)}, bf16[128,2048]{1,0:T(8,128)(2,1)S(1)}, u32[]{:S(2)}, u32[]{:S(2)}) collective-permute-start(bf16[128,2048]{1,0:T(8,128)(2,1)S(1)} %copy-done.4), channel_id=1, source_target_pairs={{0,1},{1,0},{2,3},{3,2},{4,5},{5,4},{6,7},{7,6},{8,9},{9,8},{10,11... | collective-permute-start | bytes 1572872 | tf_op jit(solution)/shard_map/ppermute | solution.py:281
  16.6 67.7 %copy-start.5 = (bf16[256,2048]{1,0:T(8,128)(2,1)}, bf16[256,2048]{1,0:T(8,128)(2,1)S(1)}, u32[]{:S(2)}) copy-start(bf16[256,2048]{1,0:T(8,128)(2,1)S(1)} %constant_dynamic-update-slice_fusion.refs_0_) | copy-start | bytes 3145732
  16.6 67.7 %collective-permute-start.1 = (bf16[256,2048]{1,0:T(8,128)(2,1)S(1)}, bf16[256,2048]{1,0:T(8,128)(2,1)S(1)}, u32[]{:S(2)}, u32[]{:S(2)}) collective-permute-start(bf16[256,2048]{1,0:T(8,128)(2,1)S(1)} %constant_dynamic-update-slice_fusion.refs_0_), channel_id=1, source_target_pairs={{0,2},{2,4},{3,1},{4,6},{5,3},{7,5},{8,10},{10,12},{11,9},{12,14},... | collective-permute-start | bytes 3145736 | tf_op jit(solution)/shard_map/ppermute | solution.py:281
  21.1 63.1 %collective-permute-start.2 = (bf16[256,2048]{1,0:T(8,128)(2,1)S(1)}, bf16[256,2048]{1,0:T(8,128)(2,1)}, u32[]{:S(2)}, u32[]{:S(2)}) collective-permute-start(bf16[256,2048]{1,0:T(8,128)(2,1)S(1)} %constant_dynamic-update-slice_fusion.refs_0_), channel_id=1, source_target_pairs={{0,4},{2,6},{5,1},{7,3},{8,12},{10,14},{13,9},{15,11},{16,20},{18,... | collective-permute-start | bytes 3145736 | tf_op jit(solution)/shard_map/ppermute | solution.py:281
  84.3 28.9 %copy-start.6 = (bf16[256,2048]{1,0:T(8,128)(2,1)}, bf16[256,2048]{1,0:T(8,128)(2,1)S(1)}, u32[]{:S(2)}) copy-start(bf16[256,2048]{1,0:T(8,128)(2,1)S(1)} %collective-permute-done.1.refs_1_) | copy-start | bytes 3145732
  84.3 3.3 %collective-permute-start.3 = (bf16[256,2048]{1,0:T(8,128)(2,1)}, bf16[256,2048]{1,0:T(8,128)(2,1)S(1)}, u32[]{:S(2)}, u32[]{:S(2)}) collective-permute-start(bf16[256,2048]{1,0:T(8,128)(2,1)} %collective-permute-done.2.refs_2_), channel_id=1, source_target_pairs={{3,1},{4,6},{11,9},{12,14},{19,17},{20,22},{27,25},{28,30}} | collective-permute-start | bytes 3145736 | tf_op jit(solution)/shard_map/ppermute | solution.py:281
  85.0 14.2 %collective-permute-start.5 = (bf16[256,2048]{1,0:T(8,128)(2,1)}, bf16[256,2048]{1,0:T(8,128)(2,1)S(1)}, u32[]{:S(2)}, u32[]{:S(2)}) collective-permute-start(bf16[256,2048]{1,0:T(8,128)(2,1)} %collective-permute-done.2.refs_2_), channel_id=1, source_target_pairs={{1,0},{3,2},{4,5},{6,7},{9,8},{11,10},{12,13},{14,15},{17,16},{19,... | collective-permute-start | bytes 3145736 | tf_op jit(solution)/shard_map/ppermute | solution.py:281
  86.3 12.9 %collective-permute-start.4 = (bf16[256,2048]{1,0:T(8,128)(2,1)S(1)}, bf16[256,2048]{1,0:T(8,128)(2,1)S(1)}, u32[]{:S(2)}, u32[]{:S(2)}) collective-permute-start(bf16[256,2048]{1,0:T(8,128)(2,1)S(1)} %collective-permute-done.1.refs_1_), channel_id=1, source_target_pairs={{1,0},{2,3},{3,2},{4,5},{5,4},{6,7},{9,8},{10,11},{11,10},{12,13},... | collective-permute-start | bytes 3145736 | tf_op jit(solution)/shard_map/ppermute | solution.py:281
  87.6 25.5 %copy-start.7 = (bf16[256,2048]{1,0:T(8,128)(2,1)}, bf16[256,2048]{1,0:T(8,128)(2,1)S(1)}, u32[]{:S(2)}) copy-start(bf16[256,2048]{1,0:T(8,128)(2,1)S(1)} %collective-permute-done.3.refs_3_) | copy-start | bytes 3145732
  87.6 24.5 %collective-permute-start.6 = (bf16[256,2048]{1,0:T(8,128)(2,1)S(1)}, bf16[256,2048]{1,0:T(8,128)(2,1)S(1)}, u32[]{:S(2)}, u32[]{:S(2)}) collective-permute-start(bf16[256,2048]{1,0:T(8,128)(2,1)S(1)} %collective-permute-done.3.refs_3_), channel_id=1, source_target_pairs={{1,0},{6,7},{9,8},{14,15},{17,16},{22,23},{25,24},{30,31}} | collective-permute-start | bytes 3145736 | tf_op jit(solution)/shard_map/ppermute | solution.py:281
  99.2 12.9 %copy-start.9 = (bf16[256,2048]{1,0:T(8,128)(2,1)}, bf16[256,2048]{1,0:T(8,128)(2,1)S(1)}, u32[]{:S(2)}) copy-start(bf16[256,2048]{1,0:T(8,128)(2,1)S(1)} %collective-permute-done.4.refs_4_) | copy-start | bytes 3145732
  99.2 13.9 %copy-start.8 = (bf16[256,2048]{1,0:T(8,128)(2,1)}, bf16[256,2048]{1,0:T(8,128)(2,1)S(1)}, u32[]{:S(2)}) copy-start(bf16[256,2048]{1,0:T(8,128)(2,1)S(1)} %collective-permute-done.5.refs_5_) | copy-start | bytes 3145732
  112.2 1.0 copy-start.10
  136.6 20.6 %collective-permute-start.11 = (bf16[2,2,256,384]{3,2,1,0:T(8,128)(2,1)}, bf16[2,2,256,384]{3,2,1,0:T(8,128)(2,1)S(1)}, u32[]{:S(2)}, u32[]{:S(2)}) collective-permute-start(bf16[2,2,256,384]{3,2,1,0:T(8,128)(2,1)} %get-tuple-element.50), channel_id=1, source_target_pairs={{0,8},{8,0},{16,24},{24,16},{1,9},{9,1},{17,25},{25,17},{2,10},{10... | collective-permute-start | bytes 2359304 | tf_op jit(solution)/shard_map/ppermute | solution.py:421
  138.2 19.1 %copy-start.3 = (bf16[2,2,256,384]{3,2,1,0:T(8,128)(2,1)S(1)}, bf16[2,2,256,384]{3,2,1,0:T(8,128)(2,1)}, u32[]{:S(2)}) copy-start(bf16[2,2,256,384]{3,2,1,0:T(8,128)(2,1)} %get-tuple-element.49) | copy-start | bytes 2359300
  138.2 20.9 %collective-permute-start.13 = (bf16[2,2,256,384]{3,2,1,0:T(8,128)(2,1)}, bf16[2,2,256,384]{3,2,1,0:T(8,128)(2,1)S(1)}, u32[]{:S(2)}, u32[]{:S(2)}) collective-permute-start(bf16[2,2,256,384]{3,2,1,0:T(8,128)(2,1)} %get-tuple-element.52), channel_id=1, source_target_pairs={{0,16},{8,24},{16,0},{24,8},{1,17},{9,25},{17,1},{25,9},{2,18},{10... | collective-permute-start | bytes 2359304 | tf_op jit(solution)/shard_map/ppermute | solution.py:421
  145.6 28.5 %collective-permute-start.7 = (bf16[2,2,256,384]{3,2,1,0:T(8,128)(2,1)}, bf16[2,2,256,384]{3,2,1,0:T(8,128)(2,1)S(1)}, u32[]{:S(2)}, u32[]{:S(2)}) collective-permute-start(bf16[2,2,256,384]{3,2,1,0:T(8,128)(2,1)} %get-tuple-element.42), channel_id=1, source_target_pairs={{0,8},{8,0},{16,24},{24,16},{1,9},{9,1},{17,25},{25,17},{2,10},{10... | collective-permute-start | bytes 2359304 | tf_op jit(solution)/shard_map/ppermute | solution.py:421
  146.2 29.8 %collective-permute-start.8 = (bf16[2,2,256,384]{3,2,1,0:T(8,128)(2,1)}, bf16[2,2,256,384]{3,2,1,0:T(8,128)(2,1)S(1)}, u32[]{:S(2)}, u32[]{:S(2)}) collective-permute-start(bf16[2,2,256,384]{3,2,1,0:T(8,128)(2,1)} %get-tuple-element.44), channel_id=1, source_target_pairs={{0,16},{8,24},{16,0},{24,8},{1,17},{9,25},{17,1},{25,9},{2,18},{10... | collective-permute-start | bytes 2359304 | tf_op jit(solution)/shard_map/ppermute | solution.py:421
  157.3 1.9 copy-start.2
  157.5 26.6 %collective-permute-start.12 = (bf16[1,2,256,384]{3,2,1,0:T(8,128)(2,1)S(1)}, bf16[1,2,256,384]{3,2,1,0:T(8,128)(2,1)S(1)}, u32[]{:S(2)}, u32[]{:S(2)}) collective-permute-start(bf16[1,2,256,384]{3,2,1,0:T(8,128)(2,1)S(1)} %get-tuple-element.55), channel_id=1, source_target_pairs={{0,16},{8,24},{16,0},{24,8},{1,17},{9,25},{17,1},{25,9},{2,18},{10... | collective-permute-start | bytes 1179656 | tf_op jit(solution)/shard_map/ppermute | solution.py:469
  159.1 15.0 %copy-start.1 = (bf16[2,2,256,384]{3,2,1,0:T(8,128)(2,1)S(1)}, bf16[2,2,256,384]{3,2,1,0:T(8,128)(2,1)}, u32[]{:S(2)}) copy-start(bf16[2,2,256,384]{3,2,1,0:T(8,128)(2,1)} %get-tuple-element.41) | copy-start | bytes 2359300
  159.4 24.7 %collective-permute-start.14 = (bf16[1,2,256,384]{3,2,1,0:T(8,128)(2,1)S(1)}, bf16[1,2,256,384]{3,2,1,0:T(8,128)(2,1)S(1)}, u32[]{:S(2)}, u32[]{:S(2)}) collective-permute-start(bf16[1,2,256,384]{3,2,1,0:T(8,128)(2,1)S(1)} %get-tuple-element.53), channel_id=1, source_target_pairs={{0,8},{8,0},{16,24},{24,16},{1,9},{9,1},{17,25},{25,17},{2,10},{10... | collective-permute-start | bytes 1179656 | tf_op jit(solution)/shard_map/ppermute | solution.py:469
  174.1 1.9 copy-start
  174.4 17.9 %collective-permute-start.9 = (bf16[1,2,256,384]{3,2,1,0:T(8,128)(2,1)S(1)}, bf16[1,2,256,384]{3,2,1,0:T(8,128)(2,1)S(1)}, u32[]{:S(2)}, u32[]{:S(2)}) collective-permute-start(bf16[1,2,256,384]{3,2,1,0:T(8,128)(2,1)S(1)} %get-tuple-element.59), channel_id=1, source_target_pairs={{0,16},{8,24},{16,0},{24,8},{1,17},{9,25},{17,1},{25,9},{2,18},{10... | collective-permute-start | bytes 1179656 | tf_op jit(solution)/shard_map/ppermute | solution.py:469
  176.3 16.0 %collective-permute-start.10 = (bf16[1,2,256,384]{3,2,1,0:T(8,128)(2,1)S(1)}, bf16[1,2,256,384]{3,2,1,0:T(8,128)(2,1)S(1)}, u32[]{:S(2)}, u32[]{:S(2)}) collective-permute-start(bf16[1,2,256,384]{3,2,1,0:T(8,128)(2,1)S(1)} %get-tuple-element.57), channel_id=1, source_target_pairs={{0,8},{8,0},{16,24},{24,16},{1,9},{9,1},{17,25},{25,17},{2,10},{10... | collective-permute-start | bytes 1179656 | tf_op jit(solution)/shard_map/ppermute | solution.py:469
Sparse Core Ops, SparseCore 0:
  9.6 64.1 all-gather.1
  131.1 52.6 reduce-scatter.1

commit v14 on v13

--- a/solution.py
+++ b/solution.py
@@ -35,44 +35,25 @@
     out[0] = w[0].T
 
 
-def block_copies(place, ref, dst, sem, flip):
-    half = ref.shape[0] // 2
-    copies = []
-    for part in range(2):
-        to = (part ^ flip) * half
-        if not isinstance(flip, int):
-            to = pl.multiple_of(to, half)
-        copies.append(
-            pltpu.make_async_copy(ref.at[pl.ds(part * half, half), :], dst.at[pl.ds(to, half), :], sem.at[part])
-        )
-    return copies
-
-
-def by_side(place, is_left, mine, other, act):
-    for left in (True, False):
-        for core in (True, False):
-            ref = (mine if left == core else other)(left)
-            if ref is not None:
-
-                @pl.when((is_left == left) & ((place[2] == 0) == core))
+def start_blocks(place, chips, own, mine, other, dst, sem):
+    half = dst.shape[1] // 2
+
+    def start(pair, slot, flip):
+        for part in range(2):
+            to = (part ^ flip) * half
+            if not isinstance(flip, int):
+                to = pl.multiple_of(to, half)
+            pltpu.make_async_copy(pair[part], dst.at[slot, pl.ds(to, half), :], sem.at[slot, part]).start()
+
+    start(own, 0, place[2])
+    for slot in range(1, chips):
+        for left in (True, False):
+            for core in (True, False):
+                pair = (mine if left == core else other)[(slot if left else chips - slot) - 1]
+
+                @pl.when(((place[3] >= slot) == left) & ((place[2] == 0) == core))
                 def _():
-                    act(ref, 0 if left else 1)
-
-
-def start_blocks(place, chips, own, mine, other, dst, sem):
-    for copy in block_copies(place, own, dst.at[0], sem.at[0], place[2]):
-        copy.start()
-    for slot in range(1, chips):
-
-        def pick(blocks, left):
-            step = slot if left else chips - slot
-            return blocks[step - 1] if step <= len(blocks) else None
-
-        def start(ref, flip):
-            for copy in block_copies(place, ref, dst.at[slot], sem.at[slot], flip):
-                copy.start()
-
-        by_side(place, place[3] >= slot, functools.partial(pick, mine), functools.partial(pick, other), start)
+                    start(pair, slot, 0 if left else 1)
 
 
 def copy_all(pairs, sem):
@@ -161,8 +142,9 @@
 
 
 def tail_kernel(groups, cap, width, top, place, *refs):
-    steps = groups - 1
-    own, mine, other, refs = refs[0], refs[1 : 1 + steps], refs[1 + steps : 1 + 2 * steps], refs[1 + 2 * steps :]
+    count = 2 * groups - 1
+    halves = [(refs[2 * n], refs[2 * n + 1]) for n in range(count)]
+    own, mine, other, refs = halves[0], halves[1:groups], halves[groups:], refs[2 * count :]
     pick_in, w_down, w_flip, hid_in, slope_in, meta, out_all, kept = refs[:8]
     pick, moved, held, grads, out, down_v, flip_v, hid, slope, block_sem, sems, keep_sem, out_sem = refs[8:]
     experts, members = held.shape[0], moved.shape[1]
@@ -177,7 +159,7 @@
     for slot in range(groups):
         for part in range(2):
             at = pl.ds(part * half, half)
-            pltpu.make_async_copy(own.at[at, :], moved.at[slot, at, :], block_sem.at[slot, part]).wait()
+            pltpu.make_async_copy(own[0], moved.at[slot, at, :], block_sem.at[slot, part]).wait()
         group = lax.rem(place[3] - slot + groups, groups)
         first = pl.multiple_of(group * cap, PACK)
         got = dot(pick[group], moved[slot]).astype(bf16)
@@ -323,6 +305,49 @@
         out_shape=shape(experts, hidden, width),
         scratch_shapes=[],
     )(w_up)
+    def at_group(i):
+        return jnp.minimum(i, groups - 1)
+
+    def at_expert(i):
+        return jnp.clip(i - groups, 0, experts - 1)
+
+    def at_slot(i, place):
+        return lax.rem(place[3] - at_group(i) + groups, groups)
+
+    def by_group(n):
+        return pl.BlockSpec((members, n), lambda i, *_: (at_group(i), 0))
+
+    def by_expert(rows, n):
+        return pl.BlockSpec((1, rows, n), lambda i, *_: (at_expert(i), 0, 0))
+
+    def call(kernel, name, grid, flops, nbytes, in_specs, out_specs, out_shape, scratch_shapes, prefetch=0):
+        return pl.pallas_call(
+            kernel,
+            grid_spec=pltpu.PrefetchScalarGridSpec(
+                num_scalar_prefetch=prefetch,
+                grid=(grid,),
+                in_specs=in_specs,
+                out_specs=out_specs,
+                scratch_shapes=scratch_shapes,
+            ),
+            out_shape=out_shape,
+            compiler_params=pltpu.CompilerParams(vmem_limit_bytes=VMEM_LIMIT),
+            cost_estimate=cost(flops, nbytes),
+            name=name,
+        )
+
+    row_bytes = 2 * experts * hidden * width
+    w_flip = call(
+        flip_kernel,
+        "flip",
+        experts,
+        0,
+        2 * row_bytes,
+        in_specs=[pl.BlockSpec((1, width, hidden), lambda b: (b, 0, 0))],
+        out_specs=pl.BlockSpec((1, hidden, width), lambda b: (b, 0, 0)),
+        out_shape=shape(experts, hidden, width),
+        scratch_shapes=[],
+    )(w_up)
     dy_own = jnp.concatenate([cotangent, hop(cotangent, [(p, p ^ 1) for p in range(ep_count)])], axis=0)
     lines = [None] + [
         [(p, reach(p, 1)) for p in range(ep_count) if None not in (reach(p, 1), reach(p, 1 - step))]
@@ -331,13 +356,13 @@
     swaps = [None] + [
         [(p, p ^ 1) for p in range(ep_count) if reach(p, -step) is not None] for step in range(1, groups)
     ]
-    far = [(p, reach(p, 2)) for p in range(ep_count) if reach(p, 2) is not None]
-    dy_mine = [hop(dy_own, lines[1])]
-    far_own, w_flip = lax.optimization_barrier((dy_own, w_flip))
-    if groups > 2:
-        dy_mine.append(hop(far_own, far))
-    for step in range(3, groups - 1):
-        dy_mine.append(hop(dy_mine[-1], lines[step]))
+    dy_own = [cotangent, hop(cotangent, [(p, p ^ 1) for p in range(ep_count)])]
+    dy_mine = [[hop(part, lines[1]) for part in dy_own]]
+    dy_mine[0][0], w_flip = lax.optimization_barrier((dy_mine[0][0], w_flip))
+    for step in range(2, groups - 1):
+        dy_mine.append([hop(part, lines[step]) for part in dy_mine[-1]])
+    last_own = hop(dy_mine[-1][0], lines[-1])
+    dy_other = [[hop(part, swaps[1]) for part in dy_mine[0]]]
 
     act = shape(experts, routes, hidden)
     act_spec = by_expert(routes, hidden)
@@ -360,12 +385,13 @@
             name=name,
         )
 
+    up_after = dy_other[0] + dy_mine[-1][:1]
     pick, meta, hid, scaled, slope_g = one(
-        functools.partial(up_kernel, groups, width, top, cap, 0),
+        functools.partial(up_kernel, groups, width, top, cap, len(up_after)),
         "up",
         pick_flops + main_flops,
         2 * total * full + row_bytes,
-        [SMEM, ANY, ANY],
+        [SMEM, ANY, ANY] + [ANY] * len(up_after),
         [ANY, pl.BlockSpec(memory_space=pltpu.VMEM), ANY, ANY, ANY],
         [shape(groups, experts * cap, members), shape(total, LANES), act, act, act],
         [
@@ -380,11 +406,11 @@
             pltpu.SemaphoreType.DMA((2, most)),
             pltpu.SemaphoreType.DMA((4, experts)),
         ],
-    )(place, x_all, w_up)
-    *dy_mine, hid = lax.optimization_barrier((*dy_mine, hid))
-    if groups > 3:
-        dy_mine.append(hop(dy_mine[-1], lines[-1]))
-    dy_other = [hop(part, swap) for part, swap in zip(dy_mine, swaps[1:])]
+    )(place, x_all, w_up, *up_after)
+    dy_mine, hid = lax.optimization_barrier((dy_mine, hid))
+    dy_mine.append([last_own, hop(dy_mine[-1][1], lines[-1])])
+    dy_other += [[hop(part, swap) for part in row] for row, swap in zip(dy_mine[1:], swaps[2:])]
+    blocks = [part for row in [dy_own] + dy_mine + dy_other for part in row]
 
     orders = []
     for g in range(turns):
@@ -431,7 +457,7 @@
         "tail",
         8 * main_flops,
         4 * row_bytes,
-        [SMEM] + [ANY] * (2 * groups - 1) + [ANY] * 5 + [pl.BlockSpec(memory_space=pltpu.VMEM)],
+        [SMEM] + [ANY] * (4 * groups - 2) + [ANY] * 5 + [pl.BlockSpec(memory_space=pltpu.VMEM)],
         [ANY, ANY],
         [shape(total, full), shape(experts, routes, width)],
         [
@@ -449,7 +475,7 @@
             pltpu.SemaphoreType.DMA((experts,)),
             pltpu.SemaphoreType.DMA((groups,)),
         ],
-    )(place, dy_own, *dy_mine, *dy_other, pick, w_down, w_flip, hid, slope_g, meta)
+    )(place, *blocks, pick, w_down, w_flip, hid, slope_g, meta)
     summed = lax.psum_scatter(token_part, "ep", scatter_dimension=0, tiled=True)
     token_grad, gate_grad = pl.pallas_call(
         functools.partial(finish_kernel, width, top),

time: 201 us -> 183 us (0.910)
  waiting for transfers between devices: 105 us -> 82.2 us
  starting transfers between devices: 25.9 us -> 30.3 us
    all_gather x1, waiting for transfers between devices: 46.7 us -> 28.5 us  [shards(): x_all = lax.all_gather(x_own, 'ep', axis=0, tiled=True)]
    ppermute x7 -> x13, starting transfers between devices: 15.3 us -> 20 us  [hop(): return lax.ppermute(value, 'ep', pairs)]
    ppermute x7 -> x13, waiting for transfers between devices: 23.1 us -> 18.6 us  [hop(): return lax.ppermute(value, 'ep', pairs)]
  transfers between devices with their start and end apart: 17 -> 23, of which waited for: 7 -> 10; matrix products, arithmetic and copies ran while one was open for 1% -> 1% of each run, Pallas kernels for 16% -> 17%
where the time goes in v14:
time: 183 us; the launch traced here: 182 us
  waiting for transfers between devices  82.2 us (45%)
  Pallas kernels  52.3 us (29%)
  starting transfers between devices  30.3 us (17%)
  between operations  14.4 us (8%)
    all_gather x1, waiting for transfers between devices, shards(): x_all = lax.all_gather(x_own, 'ep', axis=0, tiled=True)  28.5 us
    ppermute x4, waiting for transfers between devices, exchange(): got = lax.ppermute(send, 'dp', [(i, i ^ bit) for i in range(dp_count)])  23.4 us
    ppermute x13, starting transfers between devices, hop(): return lax.ppermute(value, 'ep', pairs)  20 us
    ppermute x13, waiting for transfers between devices, hop(): return lax.ppermute(value, 'ep', pairs)  18.6 us
    pallas_call x1, Pallas kernels, shards(): one(functools.partial(tail_kernel, groups, cap, width, top), 'tail', 8 *...  17.3 us
    pallas_call x2, Pallas kernels, down(): one(functools.partial(down_kernel, orders, start), 'down', 16 * main_flop...  11.5 us
    pallas_call x1, Pallas kernels, shards(): one(functools.partial(up_kernel, groups, width, top, cap, len(up_after)),...  10.4 us
    ppermute x4, waiting for transfers between devices, shards(): lax.ppermute(send, 'dp', [(i, i ^ 1 << (g + last) % bits) for i in range(...  9.96 us
  transfers between devices with their start and end apart: 23, of which 10 were waited for; matrix products, arithmetic and copies ran while one was open for 1% of the time, Pallas kernels for 17%

profile of v14, /device:TPU:0, one launch (start us, length us, event | category | flops | bytes accessed | tf_op | source)
XLA Modules:
  0.0 181.9 jit_solution(11983072185166163647)
XLA Ops:
  7.2 2.0 %pack.1 = bf16[128,2176]{1,0:T(8,128)(2,1)} custom-call(bf16[128,2048]{1,0:T(8,128)(2,1)} %tokens.1, s32[8,128]{1,0:T(8,128)} %bitcast.7, bf16[8,128]{1,0:T(8,128)(2,1)} %bitcast.8), custom_call_target="tpu_custom_call" | custom-call | bytes 1048576 | tf_op jit(solution)/shard_map/pack/pallas_call | solution.py:249
  9.3 0.5 collective-permute-start
  9.8 4.5 %collective-permute-start.1 = (bf16[128,2048]{1,0:T(8,128)(2,1)S(1)}, bf16[128,2048]{1,0:T(8,128)(2,1)S(1)}, u32[]{:S(2)}, u32[]{:S(2)}) collective-permute-start(bf16[128,2048]{1,0:T(8,128)(2,1)S(1)} %copy-done.4), channel_id=1, source_target_pairs={{0,2},{2,4},{3,1},{4,6},{5,3},{7,5},{8,10},{10,12},{11,9},{12,14},... | collective-permute-start | bytes 1572872 | tf_op jit(solution)/shard_map/ppermute | solution.py:263
  14.4 3.5 %collective-permute-start.2 = (bf16[128,2048]{1,0:T(8,128)(2,1)S(1)}, bf16[128,2048]{1,0:T(8,128)(2,1)S(1)}, u32[]{:S(2)}, u32[]{:S(2)}) collective-permute-start(bf16[128,2048]{1,0:T(8,128)(2,1)S(1)} %collective-permute-done.refs_1_), channel_id=1, source_target_pairs={{0,2},{2,4},{3,1},{4,6},{5,3},{7,5},{8,10},{10,12},{11,9},{12,14},... | collective-permute-start | bytes 1572872 | tf_op jit(solution)/shard_map/ppermute | solution.py:263
  17.9 6.7 %flip.1.refs_16_ = bf16[4,384,2048]{2,1,0:T(8,128)(2,1)} custom-call(bf16[4,2048,384]{2,1,0:T(8,128)(2,1)} %w_up.1), custom_call_target="tpu_custom_call" | custom-call | bytes 12582912 | tf_op jit(solution)/shard_map/flip/pallas_call | solution.py:340
  24.6 0.7 collective-permute-start.3
  25.3 1.3 collective-permute-start.5
  26.6 10.7 %collective-permute-done.2.refs_3_ = bf16[128,2048]{1,0:T(8,128)(2,1)S(1)} collective-permute-done((bf16[128,2048]{1,0:T(8,128)(2,1)S(1)}, bf16[128,2048]{1,0:T(8,128)(2,1)S(1)}, u32[]{:S(2)}, u32[]{:S(2)}) %collective-permute-start.2) | collective-permute-done | bytes 524320 | tf_op jit(solution)/shard_map/ppermute | solution.py:263
  37.3 1.3 collective-permute-start.6
  38.6 0.7 collective-permute-start.4
  39.3 0.7 pad_add_fusion.place
  40.0 1.4 collective-permute-start.7
  41.5 1.1 collective-permute-done.6.refs_1_.refs_9_
  42.6 28.5 %all-gather.2.cloned.1.call-done.x_all = bf16[1024,2176]{1,0:T(8,128)(2,1)} async-done(((bf16[128,2176]{1,0:T(8,128)(2,1)}), bf16[1024,2176]{1,0:T(8,128)(2,1)}) %all-gather.2.cloned.1.call-update) | async-done | bytes 4456464 | tf_op jit(solution)/shard_map/all_gather | solution.py:256
  71.1 10.4 %up.1 = (bf16[4,320,256]{2,1,0:T(8,128)(2,1)}, bf16[1024,128]{1,0:T(8,128)(2,1)}, bf16[4,320,384]{2,1,0:T(8,128)(2,1)}, bf16[4,320,384]{2,1,0:T(8,128)(2,1)}, bf16[4,320,384]{2,1,0:T(8,128)(2,1)}) custom-call(s32[4]{0:T(128)} %pad_add_fusion.place, bf16[1024,2176]{1,0:T(8,128)(2,1)} %all-gather.2.cloned.1.call-done.x_all, bf16[4,2048,384]{2,1,0:T(8,128)(2,1)} %w_up.1, ...), custom_call_target="tpu_custom_call" | custom-call | flops 3355443200 | bytes 10747904 | tf_op jit(solution)/shard_map/up/pallas_call | solution.py:389
  81.5 0.7 collective-permute-start.8
  82.2 1.3 collective-permute-start.11
  83.5 1.3 collective-permute-start.10
  84.8 1.3 collective-permute-start.9
  86.1 1.5 collective-permute-start.12
  87.6 1.3 collective-permute-done.9.refs_10_
  88.9 5.4 %collective-permute-done.12.refs_13_ = bf16[128,2048]{1,0:T(8,128)(2,1)S(1)} collective-permute-done((bf16[128,2048]{1,0:T(8,128)(2,1)S(1)}, bf16[128,2048]{1,0:T(8,128)(2,1)S(1)}, u32[]{:S(2)}, u32[]{:S(2)}) %collective-permute-start.12) | collective-permute-done | bytes 524320 | tf_op jit(solution)/shard_map/ppermute | solution.py:263
  94.4 0.8 copy-done.16
  95.2 17.3 %tail.1 = (bf16[1024,2176]{1,0:T(8,128)(2,1)}, bf16[4,320,2048]{2,1,0:T(8,128)(2,1)}) custom-call(s32[4]{0:T(128)} %pad_add_fusion.place, bf16[128,2048]{1,0:T(8,128)(2,1)} %refs_0_.1, bf16[128,2048]{1,0:T(8,128)(2,1)} %copy-done.5, bf16[128,2048]{1,0:T(8,128)(2,1)} %copy-done.6, bf16[128,2048]{1,0:T(8,128)(2,1)} %copy-done.7, bf16[128,2048]{1,0:T(8,128)(2,1)} %copy-done.8, ...), custom_call_target="tpu_custom_call" | custom-call | flops 16106127360 | bytes 25165824 | tf_op jit(solution)/shard_map/tail/pallas_call | solution.py:455
  112.6 5.6 %down.3 = (bf16[2,2,256,384]{3,2,1,0:T(8,128)(2,1)}, bf16[2,2,256,384]{3,2,1,0:T(8,128)(2,1)}, bf16[2,2,256,384]{3,2,1,0:T(8,128)(2,1)}, bf16[2,2,256,384]{3,2,1,0:T(8,128)(2,1)}) custom-call(s32[4]{0:T(128)} %pad_add_fusion.place, bf16[4,320,2048]{2,1,0:T(8,128)(2,1)} %get-tuple-element.43.kept, bf16[4,320,384]{2,1,0:T(8,128)(2,1)} %get-tuple-element.44.scaled_in), custom_call_target="tpu_custom_call" | custom-call | flops 32212254720 | bytes 50331648 | tf_op jit(solution)/shard_map/down/pallas_call | solution.py:425
  118.2 1.5 collective-permute-start.17
  119.7 1.5 collective-permute-start.19
  121.2 5.9 %down.2 = (bf16[2,2,256,384]{3,2,1,0:T(8,128)(2,1)}, bf16[2,2,256,384]{3,2,1,0:T(8,128)(2,1)}, bf16[2,2,256,384]{3,2,1,0:T(8,128)(2,1)}, bf16[2,2,256,384]{3,2,1,0:T(8,128)(2,1)}) custom-call(s32[4]{0:T(128)} %pad_add_fusion.place, bf16[4,320,2048]{2,1,0:T(8,128)(2,1)} %get-tuple-element.43.kept, bf16[4,320,384]{2,1,0:T(8,128)(2,1)} %get-tuple-element.44.scaled_in), custom_call_target="tpu_custom_call" | custom-call | flops 32212254720 | bytes 50331648 | tf_op jit(solution)/shard_map/down/pallas_call | solution.py:425
  127.1 0.9 collective-permute-start.13
  128.1 0.2 collective-permute-start.14
  128.3 10.2 %collective-permute-done.17 = bf16[2,2,256,384]{3,2,1,0:T(8,128)(2,1)S(1)} collective-permute-done((bf16[2,2,256,384]{3,2,1,0:T(8,128)(2,1)}, bf16[2,2,256,384]{3,2,1,0:T(8,128)(2,1)S(1)}, u32[]{:S(2)}, u32[]{:S(2)}) %collective-permute-start.17) | collective-permute-done | bytes 786464 | tf_op jit(solution)/shard_map/ppermute | solution.py:447
  138.5 0.2 add_convert_fusion.1
  138.7 0.1 fusion.1
  138.7 1.5 collective-permute-start.18
  140.3 0.2 add_convert_fusion
  140.6 1.5 collective-permute-start.20
  142.1 13.2 %collective-permute-done.13 = bf16[2,2,256,384]{3,2,1,0:T(8,128)(2,1)S(1)} collective-permute-done((bf16[2,2,256,384]{3,2,1,0:T(8,128)(2,1)}, bf16[2,2,256,384]{3,2,1,0:T(8,128)(2,1)S(1)}, u32[]{:S(2)}, u32[]{:S(2)}) %collective-permute-start.13) | collective-permute-done | bytes 786464 | tf_op jit(solution)/shard_map/ppermute | solution.py:447
  155.3 0.2 add_convert_fusion.3
  155.5 0.1 fusion.3
  155.6 1.5 collective-permute-start.15
  157.1 0.2 add_convert_fusion.2
  157.4 1.5 collective-permute-start.16
  159.0 6.4 %collective-permute-done.18.refs_1_ = bf16[1,2,256,384]{3,2,1,0:T(8,128)(2,1)S(1)} collective-permute-done((bf16[1,2,256,384]{3,2,1,0:T(8,128)(2,1)S(1)}, bf16[1,2,256,384]{3,2,1,0:T(8,128)(2,1)S(1)}, u32[]{:S(2)}, u32[]{:S(2)}) %collective-permute-start.18) | collective-permute-done | bytes 393248 | tf_op jit(solution)/shard_map/ppermute | solution.py:495
  165.4 1.2 put.2.refs_4_
  166.7 1.8 reduce-scatter.2.cloned.1.call-done.rows
  168.4 1.9 %finish.1 = (bf16[128,2048]{1,0:T(8,128)(2,1)}, bf16[8,128]{1,0:T(8,128)(2,1)}) custom-call(bf16[128,2176]{1,0:T(8,128)(2,1)} %reduce-scatter.2.cloned.1.call-done.rows), custom_call_target="tpu_custom_call" | custom-call | bytes 1048576 | tf_op jit(solution)/shard_map/finish/pallas_call | solution.py:480
  170.3 3.5 %collective-permute-done.15.refs_1_ = bf16[1,2,256,384]{3,2,1,0:T(8,128)(2,1)S(1)} collective-permute-done((bf16[1,2,256,384]{3,2,1,0:T(8,128)(2,1)S(1)}, bf16[1,2,256,384]{3,2,1,0:T(8,128)(2,1)S(1)}, u32[]{:S(2)}, u32[]{:S(2)}) %collective-permute-start.15) | collective-permute-done | bytes 393248 | tf_op jit(solution)/shard_map/ppermute | solution.py:495
  173.8 1.2 put.3
  (52 shorter events, 0.4 us)
Async XLA Ops:
  7.2 2.1 %copy-start.4 = (bf16[128,2048]{1,0:T(8,128)(2,1)S(1)}, bf16[128,2048]{1,0:T(8,128)(2,1)}, u32[]{:S(2)}) copy-start(bf16[128,2048]{1,0:T(8,128)(2,1)} %refs_0_.1) | copy-start | bytes 1572868
  7.2 63.9 %all-gather.2.cloned.1.call-start = ((), (), s32[]{:S(2)}) async-start(), calls=%async_computation.1 | async-start | bytes 5013504 | tf_op jit(solution)/shard_map/all_gather | solution.py:256
  9.3 159.2 %reduce-scatter.2.cloned.1.call-start = ((), (), s32[]{:S(2)}) async-start(), calls=%async_computation.2 | async-start | bytes 5013504 | tf_op jit(solution)/shard_map/reduce_scatter | solution.py:479
  9.3 5.0 %collective-permute-start = (bf16[128,2048]{1,0:T(8,128)(2,1)S(1)}, bf16[128,2048]{1,0:T(8,128)(2,1)S(1)}, u32[]{:S(2)}, u32[]{:S(2)}) collective-permute-start(bf16[128,2048]{1,0:T(8,128)(2,1)S(1)} %copy-done.4), channel_id=1, source_target_pairs={{0,1},{1,0},{2,3},{3,2},{4,5},{5,4},{6,7},{7,6},{8,9},{9,8},{10,11... | collective-permute-start | bytes 1572872 | tf_op jit(solution)/shard_map/ppermute | solution.py:263
  9.8 14.7 %collective-permute-start.1 = (bf16[128,2048]{1,0:T(8,128)(2,1)S(1)}, bf16[128,2048]{1,0:T(8,128)(2,1)S(1)}, u32[]{:S(2)}, u32[]{:S(2)}) collective-permute-start(bf16[128,2048]{1,0:T(8,128)(2,1)S(1)} %copy-done.4), channel_id=1, source_target_pairs={{0,2},{2,4},{3,1},{4,6},{5,3},{7,5},{8,10},{10,12},{11,9},{12,14},... | collective-permute-start | bytes 1572872 | tf_op jit(solution)/shard_map/ppermute | solution.py:263
  14.4 10.2 %copy-start.5 = (bf16[128,2048]{1,0:T(8,128)(2,1)}, bf16[128,2048]{1,0:T(8,128)(2,1)S(1)}, u32[]{:S(2)}) copy-start(bf16[128,2048]{1,0:T(8,128)(2,1)S(1)} %collective-permute-done.refs_1_) | copy-start | bytes 1572868
  14.4 22.9 %collective-permute-start.2 = (bf16[128,2048]{1,0:T(8,128)(2,1)S(1)}, bf16[128,2048]{1,0:T(8,128)(2,1)S(1)}, u32[]{:S(2)}, u32[]{:S(2)}) collective-permute-start(bf16[128,2048]{1,0:T(8,128)(2,1)S(1)} %collective-permute-done.refs_1_), channel_id=1, source_target_pairs={{0,2},{2,4},{3,1},{4,6},{5,3},{7,5},{8,10},{10,12},{11,9},{12,14},... | collective-permute-start | bytes 1572872 | tf_op jit(solution)/shard_map/ppermute | solution.py:263
  24.6 56.9 %copy-start.6 = (bf16[128,2048]{1,0:T(8,128)(2,1)}, bf16[128,2048]{1,0:T(8,128)(2,1)S(1)}, u32[]{:S(2)}) copy-start(bf16[128,2048]{1,0:T(8,128)(2,1)S(1)} %collective-permute-done.1.refs_2_) | copy-start | bytes 1572868
  24.6 15.4 %collective-permute-start.3 = (bf16[128,2048]{1,0:T(8,128)(2,1)S(1)}, bf16[128,2048]{1,0:T(8,128)(2,1)S(1)}, u32[]{:S(2)}, u32[]{:S(2)}) collective-permute-start(bf16[128,2048]{1,0:T(8,128)(2,1)S(1)} %collective-permute-done.1.refs_2_), channel_id=1, source_target_pairs={{2,4},{3,1},{4,6},{5,3},{10,12},{11,9},{12,14},{13,11},{18,20},{19... | collective-permute-start | bytes 1572872 | tf_op jit(solution)/shard_map/ppermute | solution.py:263
  25.3 16.2 %collective-permute-start.5 = (bf16[128,2048]{1,0:T(8,128)(2,1)S(1)}, bf16[128,2048]{1,0:T(8,128)(2,1)S(1)}, u32[]{:S(2)}, u32[]{:S(2)}) collective-permute-start(bf16[128,2048]{1,0:T(8,128)(2,1)S(1)} %collective-permute-done.1.refs_2_), channel_id=1, source_target_pairs={{1,0},{2,3},{3,2},{4,5},{5,4},{6,7},{9,8},{10,11},{11,10},{12,13},... | collective-permute-start | bytes 1572872 | tf_op jit(solution)/shard_map/ppermute | solution.py:263
  37.3 44.2 %copy-start.7 = (bf16[128,2048]{1,0:T(8,128)(2,1)}, bf16[128,2048]{1,0:T(8,128)(2,1)S(1)}, u32[]{:S(2)}) copy-start(bf16[128,2048]{1,0:T(8,128)(2,1)S(1)} %collective-permute-done.2.refs_3_) | copy-start | bytes 1572868
  37.3 5.3 %collective-permute-start.6 = (bf16[128,2048]{1,0:T(8,128)(2,1)S(1)}, bf16[128,2048]{1,0:T(8,128)(2,1)S(1)}, u32[]{:S(2)}, u32[]{:S(2)}) collective-permute-start(bf16[128,2048]{1,0:T(8,128)(2,1)S(1)} %collective-permute-done.2.refs_3_), channel_id=1, source_target_pairs={{1,0},{2,3},{3,2},{4,5},{5,4},{6,7},{9,8},{10,11},{11,10},{12,13},... | collective-permute-start | bytes 1572872 | tf_op jit(solution)/shard_map/ppermute | solution.py:263
  38.6 42.9 %collective-permute-start.4 = (bf16[128,2048]{1,0:T(8,128)(2,1)S(1)}, bf16[128,2048]{1,0:T(8,128)(2,1)S(1)}, u32[]{:S(2)}, u32[]{:S(2)}) collective-permute-start(bf16[128,2048]{1,0:T(8,128)(2,1)S(1)} %collective-permute-done.2.refs_3_), channel_id=1, source_target_pairs={{2,4},{3,1},{4,6},{5,3},{10,12},{11,9},{12,14},{13,11},{18,20},{19... | collective-permute-start | bytes 1572872 | tf_op jit(solution)/shard_map/ppermute | solution.py:263
  40.0 31.1 %copy-start.8 = (bf16[128,2048]{1,0:T(8,128)(2,1)}, bf16[128,2048]{1,0:T(8,128)(2,1)S(1)}, u32[]{:S(2)}) copy-start(bf16[128,2048]{1,0:T(8,128)(2,1)S(1)} %collective-permute-done.3.refs_2_.refs_4_) | copy-start | bytes 1572868
  40.0 42.2 %collective-permute-start.7 = (bf16[128,2048]{1,0:T(8,128)(2,1)S(1)}, bf16[128,2048]{1,0:T(8,128)(2,1)}, u32[]{:S(2)}, u32[]{:S(2)}) collective-permute-start(bf16[128,2048]{1,0:T(8,128)(2,1)S(1)} %collective-permute-done.3.refs_2_.refs_4_), channel_id=1, source_target_pairs={{3,1},{4,6},{11,9},{12,14},{19,17},{20,22},{27,25},{28,30}} | collective-permute-start | bytes 1572872 | tf_op jit(solution)/shard_map/ppermute | solution.py:263
  41.5 29.6 %copy-start.9 = (bf16[128,2048]{1,0:T(8,128)(2,1)}, bf16[128,2048]{1,0:T(8,128)(2,1)S(1)}, u32[]{:S(2)}) copy-start(bf16[128,2048]{1,0:T(8,128)(2,1)S(1)} %collective-permute-done.5.refs_0_.refs_8_) | copy-start | bytes 1572868
  42.6 28.5 %copy-start.10 = (bf16[128,2048]{1,0:T(8,128)(2,1)}, bf16[128,2048]{1,0:T(8,128)(2,1)S(1)}, u32[]{:S(2)}) copy-start(bf16[128,2048]{1,0:T(8,128)(2,1)S(1)} %collective-permute-done.6.refs_1_.refs_9_) | copy-start | bytes 1572868
  81.5 12.9 %copy-start.11 = (bf16[128,2048]{1,0:T(8,128)(2,1)}, bf16[128,2048]{1,0:T(8,128)(2,1)S(1)}, u32[]{:S(2)}) copy-start(bf16[128,2048]{1,0:T(8,128)(2,1)S(1)} %collective-permute-done.4.refs_5_) | copy-start | bytes 1572868
  81.5 4.6 %collective-permute-start.8 = (bf16[128,2048]{1,0:T(8,128)(2,1)S(1)}, bf16[128,2048]{1,0:T(8,128)(2,1)S(1)}, u32[]{:S(2)}, u32[]{:S(2)}) collective-permute-start(bf16[128,2048]{1,0:T(8,128)(2,1)S(1)} %collective-permute-done.4.refs_5_), channel_id=1, source_target_pairs={{3,1},{4,6},{11,9},{12,14},{19,17},{20,22},{27,25},{28,30}} | collective-permute-start | bytes 1572872 | tf_op jit(solution)/shard_map/ppermute | solution.py:263
  82.2 5.4 %collective-permute-start.11 = (bf16[128,2048]{1,0:T(8,128)(2,1)}, bf16[128,2048]{1,0:T(8,128)(2,1)S(1)}, u32[]{:S(2)}, u32[]{:S(2)}) collective-permute-start(bf16[128,2048]{1,0:T(8,128)(2,1)} %collective-permute-done.7.refs_6_), channel_id=1, source_target_pairs={{1,0},{6,7},{9,8},{14,15},{17,16},{22,23},{25,24},{30,31}} | collective-permute-start | bytes 1572872 | tf_op jit(solution)/shard_map/ppermute | solution.py:263
  83.5 5.4 %collective-permute-start.10 = (bf16[128,2048]{1,0:T(8,128)(2,1)S(1)}, bf16[128,2048]{1,0:T(8,128)(2,1)S(1)}, u32[]{:S(2)}, u32[]{:S(2)}) collective-permute-start(bf16[128,2048]{1,0:T(8,128)(2,1)S(1)} %collective-permute-done.4.refs_5_), channel_id=1, source_target_pairs={{1,0},{3,2},{4,5},{6,7},{9,8},{11,10},{12,13},{14,15},{17,16},{19,... | collective-permute-start | bytes 1572872 | tf_op jit(solution)/shard_map/ppermute | solution.py:263
  84.8 4.1 %collective-permute-start.9 = (bf16[128,2048]{1,0:T(8,128)(2,1)}, bf16[128,2048]{1,0:T(8,128)(2,1)S(1)}, u32[]{:S(2)}, u32[]{:S(2)}) collective-permute-start(bf16[128,2048]{1,0:T(8,128)(2,1)} %copy-done.8), channel_id=1, source_target_pairs={{1,0},{3,2},{4,5},{6,7},{9,8},{11,10},{12,13},{14,15},{17,16},{19,... | collective-permute-start | bytes 1572872 | tf_op jit(solution)/shard_map/ppermute | solution.py:263
  86.1 8.2 %copy-start.12 = (bf16[128,2048]{1,0:T(8,128)(2,1)}, bf16[128,2048]{1,0:T(8,128)(2,1)S(1)}, u32[]{:S(2)}) copy-start(bf16[128,2048]{1,0:T(8,128)(2,1)S(1)} %collective-permute-done.8.refs_7_) | copy-start | bytes 1572868
  86.1 8.2 %collective-permute-start.12 = (bf16[128,2048]{1,0:T(8,128)(2,1)S(1)}, bf16[128,2048]{1,0:T(8,128)(2,1)S(1)}, u32[]{:S(2)}, u32[]{:S(2)}) collective-permute-start(bf16[128,2048]{1,0:T(8,128)(2,1)S(1)} %collective-permute-done.8.refs_7_), channel_id=1, source_target_pairs={{1,0},{6,7},{9,8},{14,15},{17,16},{22,23},{25,24},{30,31}} | collective-permute-start | bytes 1572872 | tf_op jit(solution)/shard_map/ppermute | solution.py:263
  87.6 6.7 %copy-start.13 = (bf16[128,2048]{1,0:T(8,128)(2,1)}, bf16[128,2048]{1,0:T(8,128)(2,1)S(1)}, u32[]{:S(2)}) copy-start(bf16[128,2048]{1,0:T(8,128)(2,1)S(1)} %collective-permute-done.11.refs_12_) | copy-start | bytes 1572868
  88.9 5.5 %copy-start.15 = (bf16[128,2048]{1,0:T(8,128)(2,1)}, bf16[128,2048]{1,0:T(8,128)(2,1)S(1)}, u32[]{:S(2)}) copy-start(bf16[128,2048]{1,0:T(8,128)(2,1)S(1)} %collective-permute-done.9.refs_10_) | copy-start | bytes 1572868
  88.9 5.5 %copy-start.14 = (bf16[128,2048]{1,0:T(8,128)(2,1)}, bf16[128,2048]{1,0:T(8,128)(2,1)S(1)}, u32[]{:S(2)}) copy-start(bf16[128,2048]{1,0:T(8,128)(2,1)S(1)} %collective-permute-done.10.refs_11_) | copy-start | bytes 1572868
  94.3 0.9 copy-start.16
  118.2 20.3 %collective-permute-start.17 = (bf16[2,2,256,384]{3,2,1,0:T(8,128)(2,1)}, bf16[2,2,256,384]{3,2,1,0:T(8,128)(2,1)S(1)}, u32[]{:S(2)}, u32[]{:S(2)}) collective-permute-start(bf16[2,2,256,384]{3,2,1,0:T(8,128)(2,1)} %get-tuple-element.54), channel_id=1, source_target_pairs={{0,8},{8,0},{16,24},{24,16},{1,9},{9,1},{17,25},{25,17},{2,10},{10... | collective-permute-start | bytes 2359304 | tf_op jit(solution)/shard_map/ppermute | solution.py:447
  119.7 18.7 %copy-start.3 = (bf16[2,2,256,384]{3,2,1,0:T(8,128)(2,1)S(1)}, bf16[2,2,256,384]{3,2,1,0:T(8,128)(2,1)}, u32[]{:S(2)}) copy-start(bf16[2,2,256,384]{3,2,1,0:T(8,128)(2,1)} %get-tuple-element.53) | copy-start | bytes 2359300
  119.7 20.5 %collective-permute-start.19 = (bf16[2,2,256,384]{3,2,1,0:T(8,128)(2,1)}, bf16[2,2,256,384]{3,2,1,0:T(8,128)(2,1)S(1)}, u32[]{:S(2)}, u32[]{:S(2)}) collective-permute-start(bf16[2,2,256,384]{3,2,1,0:T(8,128)(2,1)} %get-tuple-element.56), channel_id=1, source_target_pairs={{0,16},{8,24},{16,0},{24,8},{1,17},{9,25},{17,1},{25,9},{2,18},{10... | collective-permute-start | bytes 2359304 | tf_op jit(solution)/shard_map/ppermute | solution.py:447
  127.1 28.2 %collective-permute-start.13 = (bf16[2,2,256,384]{3,2,1,0:T(8,128)(2,1)}, bf16[2,2,256,384]{3,2,1,0:T(8,128)(2,1)S(1)}, u32[]{:S(2)}, u32[]{:S(2)}) collective-permute-start(bf16[2,2,256,384]{3,2,1,0:T(8,128)(2,1)} %get-tuple-element.46), channel_id=1, source_target_pairs={{0,8},{8,0},{16,24},{24,16},{1,9},{9,1},{17,25},{25,17},{2,10},{10... | collective-permute-start | bytes 2359304 | tf_op jit(solution)/shard_map/ppermute | solution.py:447
  128.1 29.1 %collective-permute-start.14 = (bf16[2,2,256,384]{3,2,1,0:T(8,128)(2,1)}, bf16[2,2,256,384]{3,2,1,0:T(8,128)(2,1)S(1)}, u32[]{:S(2)}, u32[]{:S(2)}) collective-permute-start(bf16[2,2,256,384]{3,2,1,0:T(8,128)(2,1)} %get-tuple-element.48), channel_id=1, source_target_pairs={{0,16},{8,24},{16,0},{24,8},{1,17},{9,25},{17,1},{25,9},{2,18},{10... | collective-permute-start | bytes 2359304 | tf_op jit(solution)/shard_map/ppermute | solution.py:447
  138.5 1.8 %copy-start.2 = (bf16[2,2,256,384]{3,2,1,0:T(8,128)(2,1)S(1)}, bf16[2,2,256,384]{3,2,1,0:T(8,128)(2,1)}, u32[]{:S(2)}) copy-start(bf16[2,2,256,384]{3,2,1,0:T(8,128)(2,1)} %get-tuple-element.55) | copy-start | bytes 2359300
  138.7 26.7 %collective-permute-start.18 = (bf16[1,2,256,384]{3,2,1,0:T(8,128)(2,1)S(1)}, bf16[1,2,256,384]{3,2,1,0:T(8,128)(2,1)S(1)}, u32[]{:S(2)}, u32[]{:S(2)}) collective-permute-start(bf16[1,2,256,384]{3,2,1,0:T(8,128)(2,1)S(1)} %get-tuple-element.59), channel_id=1, source_target_pairs={{0,16},{8,24},{16,0},{24,8},{1,17},{9,25},{17,1},{25,9},{2,18},{10... | collective-permute-start | bytes 1179656 | tf_op jit(solution)/shard_map/ppermute | solution.py:495
  140.3 15.0 %copy-start.1 = (bf16[2,2,256,384]{3,2,1,0:T(8,128)(2,1)S(1)}, bf16[2,2,256,384]{3,2,1,0:T(8,128)(2,1)}, u32[]{:S(2)}) copy-start(bf16[2,2,256,384]{3,2,1,0:T(8,128)(2,1)} %get-tuple-element.45) | copy-start | bytes 2359300
  140.6 24.8 %collective-permute-start.20 = (bf16[1,2,256,384]{3,2,1,0:T(8,128)(2,1)S(1)}, bf16[1,2,256,384]{3,2,1,0:T(8,128)(2,1)S(1)}, u32[]{:S(2)}, u32[]{:S(2)}) collective-permute-start(bf16[1,2,256,384]{3,2,1,0:T(8,128)(2,1)S(1)} %get-tuple-element.57), channel_id=1, source_target_pairs={{0,8},{8,0},{16,24},{24,16},{1,9},{9,1},{17,25},{25,17},{2,10},{10... | collective-permute-start | bytes 1179656 | tf_op jit(solution)/shard_map/ppermute | solution.py:495
  155.3 1.8 %copy-start = (bf16[2,2,256,384]{3,2,1,0:T(8,128)(2,1)S(1)}, bf16[2,2,256,384]{3,2,1,0:T(8,128)(2,1)}, u32[]{:S(2)}) copy-start(bf16[2,2,256,384]{3,2,1,0:T(8,128)(2,1)} %get-tuple-element.47) | copy-start | bytes 2359300
  155.6 18.2 %collective-permute-start.15 = (bf16[1,2,256,384]{3,2,1,0:T(8,128)(2,1)S(1)}, bf16[1,2,256,384]{3,2,1,0:T(8,128)(2,1)S(1)}, u32[]{:S(2)}, u32[]{:S(2)}) collective-permute-start(bf16[1,2,256,384]{3,2,1,0:T(8,128)(2,1)S(1)} %get-tuple-element.63), channel_id=1, source_target_pairs={{0,16},{8,24},{16,0},{24,8},{1,17},{9,25},{17,1},{25,9},{2,18},{10... | collective-permute-start | bytes 1179656 | tf_op jit(solution)/shard_map/ppermute | solution.py:495
  157.4 16.4 %collective-permute-start.16 = (bf16[1,2,256,384]{3,2,1,0:T(8,128)(2,1)S(1)}, bf16[1,2,256,384]{3,2,1,0:T(8,128)(2,1)S(1)}, u32[]{:S(2)}, u32[]{:S(2)}) collective-permute-start(bf16[1,2,256,384]{3,2,1,0:T(8,128)(2,1)S(1)} %get-tuple-element.61), channel_id=1, source_target_pairs={{0,8},{8,0},{16,24},{24,16},{1,9},{9,1},{17,25},{25,17},{2,10},{10... | collective-permute-start | bytes 1179656 | tf_op jit(solution)/shard_map/ppermute | solution.py:495
Sparse Core Ops, SparseCore 0:
  10.2 60.8 all-gather.1
  112.7 55.7 reduce-scatter.1

commit v15 on v14

--- a/solution.py
+++ b/solution.py
@@ -113,8 +113,8 @@
         copy.wait()
 
 
-def down_kernel(orders, start, place, kept, scaled_in, *refs):
-    outs, (rows, scaled, sent, in_sem, sem) = refs[:-5], refs[-5:]
+def down_kernel(orders, start, after, place, kept, scaled_in, *refs):
+    outs, (rows, scaled, sent, in_sem, sem) = refs[after:-5], refs[-5:]
     experts = sent.shape[2]
     arrive = copy_all([(kept.at[start + b], rows.at[b]) for b in range(experts)], in_sem.at[0])
     others = copy_all([(scaled_in.at[start + b], scaled.at[b]) for b in range(experts)], in_sem.at[1])
@@ -361,8 +361,9 @@
     dy_mine[0][0], w_flip = lax.optimization_barrier((dy_mine[0][0], w_flip))
     for step in range(2, groups - 1):
         dy_mine.append([hop(part, lines[step]) for part in dy_mine[-1]])
-    last_own = hop(dy_mine[-1][0], lines[-1])
+    dy_mine.append([hop(part, lines[-1]) for part in dy_mine[-1]])
     dy_other = [[hop(part, swaps[1]) for part in dy_mine[0]]]
+    early_swap = hop(dy_mine[1][0], swaps[2])
 
     act = shape(experts, routes, hidden)
     act_spec = by_expert(routes, hidden)
@@ -385,7 +386,7 @@
             name=name,
         )
 
-    up_after = dy_other[0] + dy_mine[-1][:1]
+    up_after = dy_other[0] + [early_swap] + dy_mine[-2][1:]
     pick, meta, hid, scaled, slope_g = one(
         functools.partial(up_kernel, groups, width, top, cap, len(up_after)),
         "up",
@@ -407,9 +408,14 @@
             pltpu.SemaphoreType.DMA((4, experts)),
         ],
     )(place, x_all, w_up, *up_after)
-    dy_mine, hid = lax.optimization_barrier((dy_mine, hid))
-    dy_mine.append([last_own, hop(dy_mine[-1][1], lines[-1])])
-    dy_other += [[hop(part, swap) for part in row] for row, swap in zip(dy_mine[1:], swaps[2:])]
+    for row, swap in zip(dy_mine[1:], swaps[2:]):
+        dy_other.append([])
+        for n, part in enumerate(row):
+            if len(dy_other) == 2 and n == 0:
+                dy_other[-1].append(early_swap)
+                continue
+            part, hid = lax.optimization_barrier((part, hid))
+            dy_other[-1].append(hop(part, swap))
     blocks = [part for row in [dy_own] + dy_mine + dy_other for part in row]
 
     orders = []
@@ -421,13 +427,13 @@
     orders = tuple(orders)
     cut_rows = share // turns
 
-    def down(start, count):
+    def down(start, count, after):
         outs = one(
-            functools.partial(down_kernel, orders, start),
+            functools.partial(down_kernel, orders, start, len(after)),
             "down",
             16 * main_flops,
             8 * row_bytes,
-            [SMEM, ANY, ANY],
+            [SMEM, ANY, ANY] + [ANY] * len(after),
             [ANY] * (2 * turns),
             [shape(dp_count // 2, count, cut_rows, hidden)] * (2 * turns),
             [
@@ -437,7 +443,7 @@
                 pltpu.SemaphoreType.DMA((2, count)),
                 pltpu.SemaphoreType.DMA((turns, dp_count, count)),
             ],
-        )(place, kept, scaled)
+        )(place, kept, scaled, *after)
         return [(outs[2 * g], outs[2 * g + 1]) for g in range(turns)]
 
     def exchange(state, t):
@@ -485,8 +491,10 @@
         name="finish",
     )(summed)
 
-    counts = [experts // 2, experts - experts // 2] if experts > 1 else [experts]
-    states = [down(start, count) for start, count in zip((0, counts[0]), counts)]
+    counts = [1, experts - 1] if experts > 1 else [experts]
+    states = [down(0, counts[0], [])]
+    if len(counts) > 1:
+        states.append(down(counts[0], counts[1], [states[0][0][0]]))
     for t in range(bits - 1):
         states = [exchange(state, t) for state in states]
     last = bits - 1

time: 183 us -> 196 us (1.071)
  waiting for transfers between devices: 82.2 us -> 95 us
    all_gather x1, waiting for transfers between devices: 28.5 us -> 2.18 us  [shards(): x_all = lax.all_gather(x_own, 'ep', axis=0, tiled=True)]
    ppermute x13, waiting for transfers between devices: 18.6 us -> 42.5 us  [hop(): return lax.ppermute(value, 'ep', pairs)]
    ppermute x4, waiting for transfers between devices: 23.4 us -> 32.9 us  [exchange(): got = lax.ppermute(send, 'dp', [(i, i ^ bit) for i in range(dp_count)])]
    ppermute x4, waiting for transfers between devices: 9.96 us -> 17.3 us  [shards(): lax.ppermute(send, 'dp', [(i, i ^ 1 << (g + last) % bits) for i in range(...]
  transfers between devices with their start and end apart: 23 -> 23, of which waited for: 10 -> 10; matrix products, arithmetic and copies ran while one was open for 1% -> 1% of each run, Pallas kernels for 17% -> 16%
where the time goes in v15:
time: 196 us; the launch traced here: 195 us
  waiting for transfers between devices  95 us (48%)
  Pallas kernels  52.4 us (27%)
  starting transfers between devices  29.6 us (15%)
  between operations  14.4 us (7%)
    ppermute x13, waiting for transfers between devices, hop(): return lax.ppermute(value, 'ep', pairs)  42.5 us
    ppermute x4, waiting for transfers between devices, exchange(): got = lax.ppermute(send, 'dp', [(i, i ^ bit) for i in range(dp_count)])  32.9 us
    ppermute x13, starting transfers between devices, hop(): return lax.ppermute(value, 'ep', pairs)  20.8 us
    ppermute x4, waiting for transfers between devices, shards(): lax.ppermute(send, 'dp', [(i, i ^ 1 << (g + last) % bits) for i in range(...  17.3 us
    pallas_call x1, Pallas kernels, shards(): one(functools.partial(tail_kernel, groups, cap, width, top), 'tail', 8 *...  17.3 us
    pallas_call x2, Pallas kernels, down(): one(functools.partial(down_kernel, orders, start, len(after)), 'down', 16...  11.6 us
    pallas_call x1, Pallas kernels, shards(): one(functools.partial(up_kernel, groups, width, top, cap, len(up_after)),...  10.4 us
    pallas_call x1, Pallas kernels, shards(): call(flip_kernel, 'flip', experts, 0, 2 * row_bytes, in_specs=[pl.BlockSp...  6.76 us
  transfers between devices with their start and end apart: 23, of which 10 were waited for; matrix products, arithmetic and copies ran while one was open for 1% of the time, Pallas kernels for 16%

profile of v15, /device:TPU:0, one launch (start us, length us, event | category | flops | bytes accessed | tf_op | source)
XLA Modules:
  0.0 194.7 jit_solution(16580559991536789432)
XLA Ops:
  7.2 2.0 %pack.1 = bf16[128,2176]{1,0:T(8,128)(2,1)} custom-call(bf16[128,2048]{1,0:T(8,128)(2,1)} %tokens.1, s32[8,128]{1,0:T(8,128)} %bitcast.7, bf16[8,128]{1,0:T(8,128)(2,1)} %bitcast.8), custom_call_target="tpu_custom_call" | custom-call | bytes 1048576 | tf_op jit(solution)/shard_map/pack/pallas_call | solution.py:249
  9.3 0.5 collective-permute-start
  9.8 5.3 %collective-permute-start.1 = (bf16[128,2048]{1,0:T(8,128)(2,1)S(1)}, bf16[128,2048]{1,0:T(8,128)(2,1)}, u32[]{:S(2)}, u32[]{:S(2)}) collective-permute-start(bf16[128,2048]{1,0:T(8,128)(2,1)S(1)} %copy-done.8), channel_id=1, source_target_pairs={{0,2},{2,4},{3,1},{4,6},{5,3},{7,5},{8,10},{10,12},{11,9},{12,14},... | collective-permute-start | bytes 1572872 | tf_op jit(solution)/shard_map/ppermute | solution.py:263
  15.2 3.5 %collective-permute-start.2 = (bf16[128,2048]{1,0:T(8,128)(2,1)S(1)}, bf16[128,2048]{1,0:T(8,128)(2,1)}, u32[]{:S(2)}, u32[]{:S(2)}) collective-permute-start(bf16[128,2048]{1,0:T(8,128)(2,1)S(1)} %collective-permute-done.refs_1_), channel_id=1, source_target_pairs={{0,2},{2,4},{3,1},{4,6},{5,3},{7,5},{8,10},{10,12},{11,9},{12,14},... | collective-permute-start | bytes 1572872 | tf_op jit(solution)/shard_map/ppermute | solution.py:263
  18.6 6.8 %flip.1.refs_16_ = bf16[4,384,2048]{2,1,0:T(8,128)(2,1)} custom-call(bf16[4,2048,384]{2,1,0:T(8,128)(2,1)} %w_up.1), custom_call_target="tpu_custom_call" | custom-call | bytes 12582912 | tf_op jit(solution)/shard_map/flip/pallas_call | solution.py:340
  25.4 0.7 collective-permute-start.3
  26.1 11.2 %collective-permute-done.2.refs_3_ = bf16[128,2048]{1,0:T(8,128)(2,1)} collective-permute-done((bf16[128,2048]{1,0:T(8,128)(2,1)S(1)}, bf16[128,2048]{1,0:T(8,128)(2,1)}, u32[]{:S(2)}, u32[]{:S(2)}) %collective-permute-start.2) | collective-permute-done | bytes 524320 | tf_op jit(solution)/shard_map/ppermute | solution.py:263
  37.3 0.7 collective-permute-start.4
  38.0 1.3 collective-permute-start.7
  39.3 1.3 collective-permute-start.8
  40.6 1.3 collective-permute-start.9
  41.9 0.7 collective-permute-start.5
  42.7 1.5 collective-permute-start.6
  44.1 0.6 pad_add_fusion.place
  44.7 0.8 collective-permute-done.8.refs_1_.refs_9_
  45.5 23.4 %collective-permute-done.9.refs_2_.refs_10_ = bf16[128,2048]{1,0:T(8,128)(2,1)S(1)} collective-permute-done((bf16[128,2048]{1,0:T(8,128)(2,1)S(1)}, bf16[128,2048]{1,0:T(8,128)(2,1)S(1)}, u32[]{:S(2)}, u32[]{:S(2)}) %collective-permute-start.9) | collective-permute-done | bytes 524320 | tf_op jit(solution)/shard_map/ppermute | solution.py:263
  68.9 2.2 %all-gather.2.cloned.1.call-done.x_all = bf16[1024,2176]{1,0:T(8,128)(2,1)} async-done(((bf16[128,2176]{1,0:T(8,128)(2,1)}), bf16[1024,2176]{1,0:T(8,128)(2,1)}) %all-gather.2.cloned.1.call-update) | async-done | bytes 4456464 | tf_op jit(solution)/shard_map/all_gather | solution.py:256
  71.1 10.4 %up.1 = (bf16[4,320,256]{2,1,0:T(8,128)(2,1)}, bf16[1024,128]{1,0:T(8,128)(2,1)}, bf16[4,320,384]{2,1,0:T(8,128)(2,1)}, bf16[4,320,384]{2,1,0:T(8,128)(2,1)}, bf16[4,320,384]{2,1,0:T(8,128)(2,1)}) custom-call(s32[4]{0:T(128)} %pad_add_fusion.place, bf16[1024,2176]{1,0:T(8,128)(2,1)} %all-gather.2.cloned.1.call-done.x_all, bf16[4,2048,384]{2,1,0:T(8,128)(2,1)} %w_up.1, ...), custom_call_target="tpu_custom_call" | custom-call | flops 3355443200 | bytes 10747904 | tf_op jit(solution)/shard_map/up/pallas_call | solution.py:390
  81.5 1.3 collective-permute-start.10
  82.8 1.3 collective-permute-start.12
  84.1 1.5 collective-permute-start.11
  85.6 4.6 %collective-permute-done.10.refs_11_ = bf16[128,2048]{1,0:T(8,128)(2,1)S(1)} collective-permute-done((bf16[128,2048]{1,0:T(8,128)(2,1)}, bf16[128,2048]{1,0:T(8,128)(2,1)S(1)}, u32[]{:S(2)}, u32[]{:S(2)}) %collective-permute-start.10) | collective-permute-done | bytes 524320 | tf_op jit(solution)/shard_map/ppermute | solution.py:263
  90.2 1.4 collective-permute-done.12.refs_13_
  91.5 1.1 collective-permute-done.11.refs_12_
  92.6 0.8 copy-done.14
  93.4 17.3 %tail.1 = (bf16[1024,2176]{1,0:T(8,128)(2,1)}, bf16[4,320,2048]{2,1,0:T(8,128)(2,1)}) custom-call(s32[4]{0:T(128)} %pad_add_fusion.place, bf16[128,2048]{1,0:T(8,128)(2,1)} %refs_0_.1, bf16[128,2048]{1,0:T(8,128)(2,1)} %copy-done.9, bf16[128,2048]{1,0:T(8,128)(2,1)} %collective-permute-done.1.refs_2_, bf16[128,2048]{1,0:T(8,128)(2,1)} %collective-permute-done.2.refs_3_, ...), custom_call_target="tpu_custom_call" | custom-call | flops 16106127360 | bytes 25165824 | tf_op jit(solution)/shard_map/tail/pallas_call | solution.py:461
  110.8 4.0 %down.2 = (bf16[2,1,256,384]{3,2,1,0:T(8,128)(2,1)}, bf16[2,1,256,384]{3,2,1,0:T(8,128)(2,1)}, bf16[2,1,256,384]{3,2,1,0:T(8,128)(2,1)}, bf16[2,1,256,384]{3,2,1,0:T(8,128)(2,1)}) custom-call(s32[4]{0:T(128)} %pad_add_fusion.place, bf16[4,320,2048]{2,1,0:T(8,128)(2,1)} %get-tuple-element.45.kept, bf16[4,320,384]{2,1,0:T(8,128)(2,1)} %get-tuple-element.46.scaled_in), custom_call_target="tpu_custom_call" | custom-call | flops 32212254720 | bytes 50331648 | tf_op jit(solution)/shard_map/down/pallas_call | solution.py:431
  114.8 7.6 %down.3 = (bf16[2,3,256,384]{3,2,1,0:T(8,128)(2,1)}, bf16[2,3,256,384]{3,2,1,0:T(8,128)(2,1)}, bf16[2,3,256,384]{3,2,1,0:T(8,128)(2,1)}, bf16[2,3,256,384]{3,2,1,0:T(8,128)(2,1)}) custom-call(s32[4]{0:T(128)} %pad_add_fusion.place, bf16[4,320,2048]{2,1,0:T(8,128)(2,1)} %get-tuple-element.45.kept, bf16[4,320,384]{2,1,0:T(8,128)(2,1)} %get-tuple-element.46.scaled_in, ...), custom_call_target="tpu_custom_call" | custom-call | flops 32212254720 | bytes 50331648 | tf_op jit(solution)/shard_map/down/pallas_call | solution.py:431
  122.4 1.8 collective-permute-start.13
  124.2 0.3 collective-permute-start.17
  124.5 1.7 collective-permute-start.14
  126.2 0.3 collective-permute-start.19
  126.6 32.9 %collective-permute-done.17 = bf16[2,1,256,384]{3,2,1,0:T(8,128)(2,1)S(1)} collective-permute-done((bf16[2,1,256,384]{3,2,1,0:T(8,128)(2,1)S(1)}, bf16[2,1,256,384]{3,2,1,0:T(8,128)(2,1)S(1)}, u32[]{:S(2)}, u32[]{:S(2)}) %collective-permute-start.17) | collective-permute-done | bytes 393248 | tf_op jit(solution)/shard_map/ppermute | solution.py:453
  159.6 1.7 collective-permute-start.18
  161.4 0.3 add_convert_fusion.1
  161.7 0.1 fusion.1
  161.8 0.4 collective-permute-start.15
  162.2 0.7 copy-done
  163.0 0.3 add_convert_fusion
  163.3 0.1 fusion
  163.5 1.6 collective-permute-start.16
  165.0 0.1 add_convert_fusion.2
  165.2 0.9 collective-permute-start.20
  166.1 1.4 collective-permute-done.18.refs_1_
  167.5 15.9 %collective-permute-done.20.refs_3_ = bf16[1,1,256,384]{3,2,1,0:T(8,128)(2,1)S(1)} collective-permute-done((bf16[1,1,256,384]{3,2,1,0:T(8,128)(2,1)S(1)}, bf16[1,1,256,384]{3,2,1,0:T(8,128)(2,1)S(1)}, u32[]{:S(2)}, u32[]{:S(2)}) %collective-permute-start.20) | collective-permute-done | bytes 196640 | tf_op jit(solution)/shard_map/ppermute | solution.py:503
  183.4 0.9 put.2.refs_4_
  184.4 1.9 finish.1
  186.3 1.5 put.3
  (50 shorter events, 0.4 us)
Async XLA Ops:
  7.2 2.1 %copy-start.8 = (bf16[128,2048]{1,0:T(8,128)(2,1)S(1)}, bf16[128,2048]{1,0:T(8,128)(2,1)}, u32[]{:S(2)}) copy-start(bf16[128,2048]{1,0:T(8,128)(2,1)} %refs_0_.1) | copy-start | bytes 1572868
  7.2 63.9 %all-gather.2.cloned.1.call-start = ((), (), s32[]{:S(2)}) async-start(), calls=%async_computation.1 | async-start | bytes 5013504 | tf_op jit(solution)/shard_map/all_gather | solution.py:256
  9.3 175.1 %reduce-scatter.2.cloned.1.call-start = ((), (), s32[]{:S(2)}) async-start(), calls=%async_computation.2 | async-start | bytes 5013504 | tf_op jit(solution)/shard_map/reduce_scatter | solution.py:485
  9.3 5.8 %collective-permute-start = (bf16[128,2048]{1,0:T(8,128)(2,1)S(1)}, bf16[128,2048]{1,0:T(8,128)(2,1)S(1)}, u32[]{:S(2)}, u32[]{:S(2)}) collective-permute-start(bf16[128,2048]{1,0:T(8,128)(2,1)S(1)} %copy-done.8), channel_id=1, source_target_pairs={{0,1},{1,0},{2,3},{3,2},{4,5},{5,4},{6,7},{7,6},{8,9},{9,8},{10,11... | collective-permute-start | bytes 1572872 | tf_op jit(solution)/shard_map/ppermute | solution.py:263
  9.8 15.6 %collective-permute-start.1 = (bf16[128,2048]{1,0:T(8,128)(2,1)S(1)}, bf16[128,2048]{1,0:T(8,128)(2,1)}, u32[]{:S(2)}, u32[]{:S(2)}) collective-permute-start(bf16[128,2048]{1,0:T(8,128)(2,1)S(1)} %copy-done.8), channel_id=1, source_target_pairs={{0,2},{2,4},{3,1},{4,6},{5,3},{7,5},{8,10},{10,12},{11,9},{12,14},... | collective-permute-start | bytes 1572872 | tf_op jit(solution)/shard_map/ppermute | solution.py:263
  15.2 10.2 %copy-start.9 = (bf16[128,2048]{1,0:T(8,128)(2,1)}, bf16[128,2048]{1,0:T(8,128)(2,1)S(1)}, u32[]{:S(2)}) copy-start(bf16[128,2048]{1,0:T(8,128)(2,1)S(1)} %collective-permute-done.refs_1_) | copy-start | bytes 1572868
  15.2 22.2 %collective-permute-start.2 = (bf16[128,2048]{1,0:T(8,128)(2,1)S(1)}, bf16[128,2048]{1,0:T(8,128)(2,1)}, u32[]{:S(2)}, u32[]{:S(2)}) collective-permute-start(bf16[128,2048]{1,0:T(8,128)(2,1)S(1)} %collective-permute-done.refs_1_), channel_id=1, source_target_pairs={{0,2},{2,4},{3,1},{4,6},{5,3},{7,5},{8,10},{10,12},{11,9},{12,14},... | collective-permute-start | bytes 1572872 | tf_op jit(solution)/shard_map/ppermute | solution.py:263
  25.4 15.2 %collective-permute-start.3 = (bf16[128,2048]{1,0:T(8,128)(2,1)}, bf16[128,2048]{1,0:T(8,128)(2,1)S(1)}, u32[]{:S(2)}, u32[]{:S(2)}) collective-permute-start(bf16[128,2048]{1,0:T(8,128)(2,1)} %collective-permute-done.1.refs_2_), channel_id=1, source_target_pairs={{2,4},{3,1},{4,6},{5,3},{10,12},{11,9},{12,14},{13,11},{18,20},{19... | collective-permute-start | bytes 1572872 | tf_op jit(solution)/shard_map/ppermute | solution.py:263
  37.3 5.3 %collective-permute-start.4 = (bf16[128,2048]{1,0:T(8,128)(2,1)}, bf16[128,2048]{1,0:T(8,128)(2,1)S(1)}, u32[]{:S(2)}, u32[]{:S(2)}) collective-permute-start(bf16[128,2048]{1,0:T(8,128)(2,1)} %collective-permute-done.2.refs_3_), channel_id=1, source_target_pairs={{2,4},{3,1},{4,6},{5,3},{10,12},{11,9},{12,14},{13,11},{18,20},{19... | collective-permute-start | bytes 1572872 | tf_op jit(solution)/shard_map/ppermute | solution.py:263
  38.0 6.7 %collective-permute-start.7 = (bf16[128,2048]{1,0:T(8,128)(2,1)}, bf16[128,2048]{1,0:T(8,128)(2,1)S(1)}, u32[]{:S(2)}, u32[]{:S(2)}) collective-permute-start(bf16[128,2048]{1,0:T(8,128)(2,1)} %collective-permute-done.1.refs_2_), channel_id=1, source_target_pairs={{1,0},{2,3},{3,2},{4,5},{5,4},{6,7},{9,8},{10,11},{11,10},{12,13},... | collective-permute-start | bytes 1572872 | tf_op jit(solution)/shard_map/ppermute | solution.py:263
  39.3 6.2 %collective-permute-start.8 = (bf16[128,2048]{1,0:T(8,128)(2,1)}, bf16[128,2048]{1,0:T(8,128)(2,1)S(1)}, u32[]{:S(2)}, u32[]{:S(2)}) collective-permute-start(bf16[128,2048]{1,0:T(8,128)(2,1)} %collective-permute-done.2.refs_3_), channel_id=1, source_target_pairs={{1,0},{2,3},{3,2},{4,5},{5,4},{6,7},{9,8},{10,11},{11,10},{12,13},... | collective-permute-start | bytes 1572872 | tf_op jit(solution)/shard_map/ppermute | solution.py:263
  40.6 40.8 %copy-start.10 = (bf16[128,2048]{1,0:T(8,128)(2,1)}, bf16[128,2048]{1,0:T(8,128)(2,1)S(1)}, u32[]{:S(2)}) copy-start(bf16[128,2048]{1,0:T(8,128)(2,1)S(1)} %collective-permute-done.3.refs_4_) | copy-start | bytes 1572868
  40.6 28.3 %collective-permute-start.9 = (bf16[128,2048]{1,0:T(8,128)(2,1)S(1)}, bf16[128,2048]{1,0:T(8,128)(2,1)S(1)}, u32[]{:S(2)}, u32[]{:S(2)}) collective-permute-start(bf16[128,2048]{1,0:T(8,128)(2,1)S(1)} %collective-permute-done.3.refs_4_), channel_id=1, source_target_pairs={{1,0},{3,2},{4,5},{6,7},{9,8},{11,10},{12,13},{14,15},{17,16},{19,... | collective-permute-start | bytes 1572872 | tf_op jit(solution)/shard_map/ppermute | solution.py:263
  41.9 40.8 %collective-permute-start.5 = (bf16[128,2048]{1,0:T(8,128)(2,1)S(1)}, bf16[128,2048]{1,0:T(8,128)(2,1)S(1)}, u32[]{:S(2)}, u32[]{:S(2)}) collective-permute-start(bf16[128,2048]{1,0:T(8,128)(2,1)S(1)} %collective-permute-done.3.refs_4_), channel_id=1, source_target_pairs={{3,1},{4,6},{11,9},{12,14},{19,17},{20,22},{27,25},{28,30}} | collective-permute-start | bytes 1572872 | tf_op jit(solution)/shard_map/ppermute | solution.py:263
  42.6 28.4 %copy-start.2 = (bf16[128,2048]{1,0:T(8,128)(2,1)}, bf16[128,2048]{1,0:T(8,128)(2,1)S(1)}, u32[]{:S(2)}) copy-start(bf16[128,2048]{1,0:T(8,128)(2,1)S(1)} %collective-permute-done.4.refs_3_.refs_5_) | copy-start | bytes 1572868
  42.7 40.1 %collective-permute-start.6 = (bf16[128,2048]{1,0:T(8,128)(2,1)S(1)}, bf16[128,2048]{1,0:T(8,128)(2,1)}, u32[]{:S(2)}, u32[]{:S(2)}) collective-permute-start(bf16[128,2048]{1,0:T(8,128)(2,1)S(1)} %collective-permute-done.4.refs_3_.refs_5_), channel_id=1, source_target_pairs={{3,1},{4,6},{11,9},{12,14},{19,17},{20,22},{27,25},{28,30}} | collective-permute-start | bytes 1572872 | tf_op jit(solution)/shard_map/ppermute | solution.py:263
  44.7 26.4 %copy-start.3 = (bf16[128,2048]{1,0:T(8,128)(2,1)}, bf16[128,2048]{1,0:T(8,128)(2,1)S(1)}, u32[]{:S(2)}) copy-start(bf16[128,2048]{1,0:T(8,128)(2,1)S(1)} %collective-permute-done.7.refs_0_.refs_8_) | copy-start | bytes 1572868
  45.5 25.6 %copy-start.4 = (bf16[128,2048]{1,0:T(8,128)(2,1)}, bf16[128,2048]{1,0:T(8,128)(2,1)S(1)}, u32[]{:S(2)}) copy-start(bf16[128,2048]{1,0:T(8,128)(2,1)S(1)} %collective-permute-done.8.refs_1_.refs_9_) | copy-start | bytes 1572868
  68.9 2.2 %copy-start.5 = (bf16[128,2048]{1,0:T(8,128)(2,1)}, bf16[128,2048]{1,0:T(8,128)(2,1)S(1)}, u32[]{:S(2)}) copy-start(bf16[128,2048]{1,0:T(8,128)(2,1)S(1)} %collective-permute-done.9.refs_2_.refs_10_) | copy-start | bytes 1572868
  81.5 8.7 %collective-permute-start.10 = (bf16[128,2048]{1,0:T(8,128)(2,1)}, bf16[128,2048]{1,0:T(8,128)(2,1)S(1)}, u32[]{:S(2)}, u32[]{:S(2)}) collective-permute-start(bf16[128,2048]{1,0:T(8,128)(2,1)} %copy-done.2), channel_id=1, source_target_pairs={{1,0},{3,2},{4,5},{6,7},{9,8},{11,10},{12,13},{14,15},{17,16},{19,... | collective-permute-start | bytes 1572872 | tf_op jit(solution)/shard_map/ppermute | solution.py:263
  82.8 9.9 %copy-start.11 = (bf16[128,2048]{1,0:T(8,128)(2,1)}, bf16[128,2048]{1,0:T(8,128)(2,1)S(1)}, u32[]{:S(2)}) copy-start(bf16[128,2048]{1,0:T(8,128)(2,1)S(1)} %collective-permute-done.5.refs_6_) | copy-start | bytes 1572868
  82.8 8.7 %collective-permute-start.12 = (bf16[128,2048]{1,0:T(8,128)(2,1)}, bf16[128,2048]{1,0:T(8,128)(2,1)S(1)}, u32[]{:S(2)}, u32[]{:S(2)}) collective-permute-start(bf16[128,2048]{1,0:T(8,128)(2,1)} %collective-permute-done.6.refs_7_), channel_id=1, source_target_pairs={{1,0},{6,7},{9,8},{14,15},{17,16},{22,23},{25,24},{30,31}} | collective-permute-start | bytes 1572872 | tf_op jit(solution)/shard_map/ppermute | solution.py:263
  84.1 8.5 %collective-permute-start.11 = (bf16[128,2048]{1,0:T(8,128)(2,1)S(1)}, bf16[128,2048]{1,0:T(8,128)(2,1)S(1)}, u32[]{:S(2)}, u32[]{:S(2)}) collective-permute-start(bf16[128,2048]{1,0:T(8,128)(2,1)S(1)} %collective-permute-done.5.refs_6_), channel_id=1, source_target_pairs={{1,0},{6,7},{9,8},{14,15},{17,16},{22,23},{25,24},{30,31}} | collective-permute-start | bytes 1572872 | tf_op jit(solution)/shard_map/ppermute | solution.py:263
  90.2 2.5 %copy-start.12 = (bf16[128,2048]{1,0:T(8,128)(2,1)}, bf16[128,2048]{1,0:T(8,128)(2,1)S(1)}, u32[]{:S(2)}) copy-start(bf16[128,2048]{1,0:T(8,128)(2,1)S(1)} %collective-permute-done.10.refs_11_) | copy-start | bytes 1572868
  91.5 1.1 copy-start.13
  92.6 0.8 copy-start.14
  114.8 9.4 %copy-start.15 = (bf16[2,1,256,384]{3,2,1,0:T(8,128)(2,1)S(1)}, bf16[2,1,256,384]{3,2,1,0:T(8,128)(2,1)}, u32[]{:S(2)}) copy-start(bf16[2,1,256,384]{3,2,1,0:T(8,128)(2,1)} %get-tuple-element.56) | copy-start | bytes 1179652
  114.8 44.7 %copy-start.7 = (bf16[2,1,256,384]{3,2,1,0:T(8,128)(2,1)S(1)}, bf16[2,1,256,384]{3,2,1,0:T(8,128)(2,1)}, u32[]{:S(2)}) copy-start(bf16[2,1,256,384]{3,2,1,0:T(8,128)(2,1)} %get-tuple-element.47.refs_0_) | copy-start | bytes 1179652
  122.4 39.0 %copy-start.1 = (bf16[2,3,256,384]{3,2,1,0:T(8,128)(2,1)S(1)}, bf16[2,3,256,384]{3,2,1,0:T(8,128)(2,1)}, u32[]{:S(2)}) copy-start(bf16[2,3,256,384]{3,2,1,0:T(8,128)(2,1)} %get-tuple-element.48) | copy-start | bytes 3538948
  122.4 38.9 %collective-permute-start.13 = (bf16[2,3,256,384]{3,2,1,0:T(8,128)(2,1)}, bf16[2,3,256,384]{3,2,1,0:T(8,128)(2,1)S(1)}, u32[]{:S(2)}, u32[]{:S(2)}) collective-permute-start(bf16[2,3,256,384]{3,2,1,0:T(8,128)(2,1)} %get-tuple-element.49), channel_id=1, source_target_pairs={{0,8},{8,0},{16,24},{24,16},{1,9},{9,1},{17,25},{25,17},{2,10},{10... | collective-permute-start | bytes 3538952 | tf_op jit(solution)/shard_map/ppermute | solution.py:453
  124.2 35.3 %collective-permute-start.17 = (bf16[2,1,256,384]{3,2,1,0:T(8,128)(2,1)S(1)}, bf16[2,1,256,384]{3,2,1,0:T(8,128)(2,1)S(1)}, u32[]{:S(2)}, u32[]{:S(2)}) collective-permute-start(bf16[2,1,256,384]{3,2,1,0:T(8,128)(2,1)S(1)} %copy-done.15), channel_id=1, source_target_pairs={{0,8},{8,0},{16,24},{24,16},{1,9},{9,1},{17,25},{25,17},{2,10},{10... | collective-permute-start | bytes 1179656 | tf_op jit(solution)/shard_map/ppermute | solution.py:453
  124.5 37.7 %collective-permute-start.14 = (bf16[2,3,256,384]{3,2,1,0:T(8,128)(2,1)}, bf16[2,3,256,384]{3,2,1,0:T(8,128)(2,1)S(1)}, u32[]{:S(2)}, u32[]{:S(2)}) collective-permute-start(bf16[2,3,256,384]{3,2,1,0:T(8,128)(2,1)} %get-tuple-element.51), channel_id=1, source_target_pairs={{0,16},{8,24},{16,0},{24,8},{1,17},{9,25},{17,1},{25,9},{2,18},{10... | collective-permute-start | bytes 3538952 | tf_op jit(solution)/shard_map/ppermute | solution.py:453
  126.2 38.8 %collective-permute-start.19 = (bf16[2,1,256,384]{3,2,1,0:T(8,128)(2,1)}, bf16[2,1,256,384]{3,2,1,0:T(8,128)(2,1)S(1)}, u32[]{:S(2)}, u32[]{:S(2)}) collective-permute-start(bf16[2,1,256,384]{3,2,1,0:T(8,128)(2,1)} %get-tuple-element.58), channel_id=1, source_target_pairs={{0,16},{8,24},{16,0},{24,8},{1,17},{9,25},{17,1},{25,9},{2,18},{10... | collective-permute-start | bytes 1179656 | tf_op jit(solution)/shard_map/ppermute | solution.py:453
  159.6 7.8 %collective-permute-start.18 = (bf16[1,1,256,384]{3,2,1,0:T(8,128)(2,1)S(1)}, bf16[1,1,256,384]{3,2,1,0:T(8,128)(2,1)S(1)}, u32[]{:S(2)}, u32[]{:S(2)}) collective-permute-start(bf16[1,1,256,384]{3,2,1,0:T(8,128)(2,1)S(1)} %get-tuple-element.65), channel_id=1, source_target_pairs={{0,16},{8,24},{16,0},{24,8},{1,17},{9,25},{17,1},{25,9},{2,18},{10... | collective-permute-start | bytes 589832 | tf_op jit(solution)/shard_map/ppermute | solution.py:503
  161.7 1.3 copy-start
  161.8 24.4 %collective-permute-start.15 = (bf16[1,3,256,384]{3,2,1,0:T(8,128)(2,1)S(1)}, bf16[1,3,256,384]{3,2,1,0:T(8,128)(2,1)S(1)}, u32[]{:S(2)}, u32[]{:S(2)}) collective-permute-start(bf16[1,3,256,384]{3,2,1,0:T(8,128)(2,1)S(1)} %get-tuple-element.61), channel_id=1, source_target_pairs={{0,16},{8,24},{16,0},{24,8},{1,17},{9,25},{17,1},{25,9},{2,18},{10... | collective-permute-start | bytes 1769480 | tf_op jit(solution)/shard_map/ppermute | solution.py:503
  163.3 1.7 copy-start.6
  163.5 22.8 %collective-permute-start.16 = (bf16[1,3,256,384]{3,2,1,0:T(8,128)(2,1)S(1)}, bf16[1,3,256,384]{3,2,1,0:T(8,128)(2,1)S(1)}, u32[]{:S(2)}, u32[]{:S(2)}) collective-permute-start(bf16[1,3,256,384]{3,2,1,0:T(8,128)(2,1)S(1)} %get-tuple-element.59), channel_id=1, source_target_pairs={{0,8},{8,0},{16,24},{24,16},{1,9},{9,1},{17,25},{25,17},{2,10},{10... | collective-permute-start | bytes 1769480 | tf_op jit(solution)/shard_map/ppermute | solution.py:503
  165.2 18.2 %collective-permute-start.20 = (bf16[1,1,256,384]{3,2,1,0:T(8,128)(2,1)S(1)}, bf16[1,1,256,384]{3,2,1,0:T(8,128)(2,1)S(1)}, u32[]{:S(2)}, u32[]{:S(2)}) collective-permute-start(bf16[1,1,256,384]{3,2,1,0:T(8,128)(2,1)S(1)} %get-tuple-element.63), channel_id=1, source_target_pairs={{0,8},{8,0},{16,24},{24,16},{1,9},{9,1},{17,25},{25,17},{2,10},{10... | collective-permute-start | bytes 589832 | tf_op jit(solution)/shard_map/ppermute | solution.py:503
Sparse Core Ops, SparseCore 0:
  10.2 60.8 all-gather.1
  110.9 55.9 reduce-scatter.1

commit v16 on v14

--- a/solution.py
+++ b/solution.py
@@ -361,8 +361,9 @@
     dy_mine[0][0], w_flip = lax.optimization_barrier((dy_mine[0][0], w_flip))
     for step in range(2, groups - 1):
         dy_mine.append([hop(part, lines[step]) for part in dy_mine[-1]])
-    last_own = hop(dy_mine[-1][0], lines[-1])
+    dy_mine.append([hop(part, lines[-1]) for part in dy_mine[-1]])
     dy_other = [[hop(part, swaps[1]) for part in dy_mine[0]]]
+    early_swap = hop(dy_mine[1][0], swaps[2])
 
     act = shape(experts, routes, hidden)
     act_spec = by_expert(routes, hidden)
@@ -385,7 +386,7 @@
             name=name,
         )
 
-    up_after = dy_other[0] + dy_mine[-1][:1]
+    up_after = dy_other[0] + [early_swap] + dy_mine[-2][1:]
     pick, meta, hid, scaled, slope_g = one(
         functools.partial(up_kernel, groups, width, top, cap, len(up_after)),
         "up",
@@ -407,9 +408,14 @@
             pltpu.SemaphoreType.DMA((4, experts)),
         ],
     )(place, x_all, w_up, *up_after)
-    dy_mine, hid = lax.optimization_barrier((dy_mine, hid))
-    dy_mine.append([last_own, hop(dy_mine[-1][1], lines[-1])])
-    dy_other += [[hop(part, swap) for part in row] for row, swap in zip(dy_mine[1:], swaps[2:])]
+    for row, swap in zip(dy_mine[1:], swaps[2:]):
+        dy_other.append([])
+        for n, part in enumerate(row):
+            if len(dy_other) == 2 and n == 0:
+                dy_other[-1].append(early_swap)
+                continue
+            part, hid = lax.optimization_barrier((part, hid))
+            dy_other[-1].append(hop(part, swap))
     blocks = [part for row in [dy_own] + dy_mine + dy_other for part in row]
 
     orders = []

time: 183 us -> 182 us (level)
  waiting for transfers between devices: 82.2 us -> 79.4 us
    all_gather x1, waiting for transfers between devices: 28.5 us -> 2.18 us  [shards(): x_all = lax.all_gather(x_own, 'ep', axis=0, tiled=True)]
    ppermute x13, waiting for transfers between devices: 18.6 us -> 42.4 us  [hop(): return lax.ppermute(value, 'ep', pairs)]
  transfers between devices with their start and end apart: 23 -> 23, of which waited for: 10 -> 12; matrix products, arithmetic and copies ran while one was open for 1% -> 1% of each run, Pallas kernels for 17% -> 18%
where the time goes in v16:
time: 182 us; the launch traced here: 180 us
  waiting for transfers between devices  79.4 us (44%)
  Pallas kernels  52.4 us (29%)
  starting transfers between devices  31.7 us (17%)
  between operations  14.3 us (8%)
    ppermute x13, waiting for transfers between devices, hop(): return lax.ppermute(value, 'ep', pairs)  42.4 us
    ppermute x4, waiting for transfers between devices, exchange(): got = lax.ppermute(send, 'dp', [(i, i ^ bit) for i in range(dp_count)])  23 us
    ppermute x13, starting transfers between devices, hop(): return lax.ppermute(value, 'ep', pairs)  20.8 us
    pallas_call x1, Pallas kernels, shards(): one(functools.partial(tail_kernel, groups, cap, width, top), 'tail', 8 *...  17.3 us
    pallas_call x2, Pallas kernels, down(): one(functools.partial(down_kernel, orders, start), 'down', 16 * main_flop...  11.6 us
    pallas_call x1, Pallas kernels, shards(): one(functools.partial(up_kernel, groups, width, top, cap, len(up_after)),...  10.4 us
    ppermute x4, waiting for transfers between devices, shards(): lax.ppermute(send, 'dp', [(i, i ^ 1 << (g + last) % bits) for i in range(...  9.84 us
    pallas_call x1, Pallas kernels, shards(): call(flip_kernel, 'flip', experts, 0, 2 * row_bytes, in_specs=[pl.BlockSp...  6.76 us
  transfers between devices with their start and end apart: 23, of which 12 were waited for; matrix products, arithmetic and copies ran while one was open for 1% of the time, Pallas kernels for 18%

profile of v16, /device:TPU:0, one launch (start us, length us, event | category | flops | bytes accessed | tf_op | source)
XLA Modules:
  0.0 180.3 jit_solution(17992974944891090810)
XLA Ops:
  7.2 2.0 %pack.1 = bf16[128,2176]{1,0:T(8,128)(2,1)} custom-call(bf16[128,2048]{1,0:T(8,128)(2,1)} %tokens.1, s32[8,128]{1,0:T(8,128)} %bitcast.7, bf16[8,128]{1,0:T(8,128)(2,1)} %bitcast.8), custom_call_target="tpu_custom_call" | custom-call | bytes 1048576 | tf_op jit(solution)/shard_map/pack/pallas_call | solution.py:249
  9.3 0.5 collective-permute-start
  9.8 5.3 %collective-permute-start.1 = (bf16[128,2048]{1,0:T(8,128)(2,1)S(1)}, bf16[128,2048]{1,0:T(8,128)(2,1)}, u32[]{:S(2)}, u32[]{:S(2)}) collective-permute-start(bf16[128,2048]{1,0:T(8,128)(2,1)S(1)} %copy-done.8), channel_id=1, source_target_pairs={{0,2},{2,4},{3,1},{4,6},{5,3},{7,5},{8,10},{10,12},{11,9},{12,14},... | collective-permute-start | bytes 1572872 | tf_op jit(solution)/shard_map/ppermute | solution.py:263
  15.2 3.5 %collective-permute-start.2 = (bf16[128,2048]{1,0:T(8,128)(2,1)S(1)}, bf16[128,2048]{1,0:T(8,128)(2,1)}, u32[]{:S(2)}, u32[]{:S(2)}) collective-permute-start(bf16[128,2048]{1,0:T(8,128)(2,1)S(1)} %collective-permute-done.refs_1_), channel_id=1, source_target_pairs={{0,2},{2,4},{3,1},{4,6},{5,3},{7,5},{8,10},{10,12},{11,9},{12,14},... | collective-permute-start | bytes 1572872 | tf_op jit(solution)/shard_map/ppermute | solution.py:263
  18.6 6.8 %flip.1.refs_16_ = bf16[4,384,2048]{2,1,0:T(8,128)(2,1)} custom-call(bf16[4,2048,384]{2,1,0:T(8,128)(2,1)} %w_up.1), custom_call_target="tpu_custom_call" | custom-call | bytes 12582912 | tf_op jit(solution)/shard_map/flip/pallas_call | solution.py:340
  25.4 0.7 collective-permute-start.3
  26.1 11.2 %collective-permute-done.2.refs_3_ = bf16[128,2048]{1,0:T(8,128)(2,1)} collective-permute-done((bf16[128,2048]{1,0:T(8,128)(2,1)S(1)}, bf16[128,2048]{1,0:T(8,128)(2,1)}, u32[]{:S(2)}, u32[]{:S(2)}) %collective-permute-start.2) | collective-permute-done | bytes 524320 | tf_op jit(solution)/shard_map/ppermute | solution.py:263
  37.3 0.7 collective-permute-start.4
  38.0 1.3 collective-permute-start.7
  39.3 1.3 collective-permute-start.8
  40.6 1.3 collective-permute-start.9
  41.9 0.7 collective-permute-start.5
  42.7 1.5 collective-permute-start.6
  44.1 0.6 pad_add_fusion.place
  44.7 0.8 collective-permute-done.8.refs_1_.refs_9_
  45.5 23.4 %collective-permute-done.9.refs_2_.refs_10_ = bf16[128,2048]{1,0:T(8,128)(2,1)S(1)} collective-permute-done((bf16[128,2048]{1,0:T(8,128)(2,1)S(1)}, bf16[128,2048]{1,0:T(8,128)(2,1)S(1)}, u32[]{:S(2)}, u32[]{:S(2)}) %collective-permute-start.9) | collective-permute-done | bytes 524320 | tf_op jit(solution)/shard_map/ppermute | solution.py:263
  68.9 2.2 %all-gather.2.cloned.1.call-done.x_all = bf16[1024,2176]{1,0:T(8,128)(2,1)} async-done(((bf16[128,2176]{1,0:T(8,128)(2,1)}), bf16[1024,2176]{1,0:T(8,128)(2,1)}) %all-gather.2.cloned.1.call-update) | async-done | bytes 4456464 | tf_op jit(solution)/shard_map/all_gather | solution.py:256
  71.1 10.4 %up.1 = (bf16[4,320,256]{2,1,0:T(8,128)(2,1)}, bf16[1024,128]{1,0:T(8,128)(2,1)}, bf16[4,320,384]{2,1,0:T(8,128)(2,1)}, bf16[4,320,384]{2,1,0:T(8,128)(2,1)}, bf16[4,320,384]{2,1,0:T(8,128)(2,1)}) custom-call(s32[4]{0:T(128)} %pad_add_fusion.place, bf16[1024,2176]{1,0:T(8,128)(2,1)} %all-gather.2.cloned.1.call-done.x_all, bf16[4,2048,384]{2,1,0:T(8,128)(2,1)} %w_up.1, ...), custom_call_target="tpu_custom_call" | custom-call | flops 3355443200 | bytes 10747904 | tf_op jit(solution)/shard_map/up/pallas_call | solution.py:390
  81.5 1.3 collective-permute-start.10
  82.8 1.3 collective-permute-start.12
  84.1 1.5 collective-permute-start.11
  85.6 4.6 %collective-permute-done.10.refs_11_ = bf16[128,2048]{1,0:T(8,128)(2,1)S(1)} collective-permute-done((bf16[128,2048]{1,0:T(8,128)(2,1)}, bf16[128,2048]{1,0:T(8,128)(2,1)S(1)}, u32[]{:S(2)}, u32[]{:S(2)}) %collective-permute-start.10) | collective-permute-done | bytes 524320 | tf_op jit(solution)/shard_map/ppermute | solution.py:263
  90.2 1.4 collective-permute-done.12.refs_13_
  91.5 1.1 collective-permute-done.11.refs_12_
  92.6 0.8 copy-done.14
  93.5 17.3 %tail.1 = (bf16[1024,2176]{1,0:T(8,128)(2,1)}, bf16[4,320,2048]{2,1,0:T(8,128)(2,1)}) custom-call(s32[4]{0:T(128)} %pad_add_fusion.place, bf16[128,2048]{1,0:T(8,128)(2,1)} %refs_0_.1, bf16[128,2048]{1,0:T(8,128)(2,1)} %copy-done.9, bf16[128,2048]{1,0:T(8,128)(2,1)} %collective-permute-done.1.refs_2_, bf16[128,2048]{1,0:T(8,128)(2,1)} %collective-permute-done.2.refs_3_, ...), custom_call_target="tpu_custom_call" | custom-call | flops 16106127360 | bytes 25165824 | tf_op jit(solution)/shard_map/tail/pallas_call | solution.py:461
  110.8 5.6 %down.3 = (bf16[2,2,256,384]{3,2,1,0:T(8,128)(2,1)}, bf16[2,2,256,384]{3,2,1,0:T(8,128)(2,1)}, bf16[2,2,256,384]{3,2,1,0:T(8,128)(2,1)}, bf16[2,2,256,384]{3,2,1,0:T(8,128)(2,1)}) custom-call(s32[4]{0:T(128)} %pad_add_fusion.place, bf16[4,320,2048]{2,1,0:T(8,128)(2,1)} %get-tuple-element.45.kept, bf16[4,320,384]{2,1,0:T(8,128)(2,1)} %get-tuple-element.46.scaled_in), custom_call_target="tpu_custom_call" | custom-call | flops 32212254720 | bytes 50331648 | tf_op jit(solution)/shard_map/down/pallas_call | solution.py:431
  116.5 1.7 collective-permute-start.17
  118.2 1.5 collective-permute-start.19
  119.7 5.9 %down.2 = (bf16[2,2,256,384]{3,2,1,0:T(8,128)(2,1)}, bf16[2,2,256,384]{3,2,1,0:T(8,128)(2,1)}, bf16[2,2,256,384]{3,2,1,0:T(8,128)(2,1)}, bf16[2,2,256,384]{3,2,1,0:T(8,128)(2,1)}) custom-call(s32[4]{0:T(128)} %pad_add_fusion.place, bf16[4,320,2048]{2,1,0:T(8,128)(2,1)} %get-tuple-element.45.kept, bf16[4,320,384]{2,1,0:T(8,128)(2,1)} %get-tuple-element.46.scaled_in), custom_call_target="tpu_custom_call" | custom-call | flops 32212254720 | bytes 50331648 | tf_op jit(solution)/shard_map/down/pallas_call | solution.py:431
  125.6 0.9 collective-permute-start.13
  126.6 10.1 %collective-permute-done.17 = bf16[2,2,256,384]{3,2,1,0:T(8,128)(2,1)S(1)} collective-permute-done((bf16[2,2,256,384]{3,2,1,0:T(8,128)(2,1)}, bf16[2,2,256,384]{3,2,1,0:T(8,128)(2,1)S(1)}, u32[]{:S(2)}, u32[]{:S(2)}) %collective-permute-start.17) | collective-permute-done | bytes 786464 | tf_op jit(solution)/shard_map/ppermute | solution.py:453
  136.7 0.2 add_convert_fusion.1
  137.0 1.7 collective-permute-start.18
  138.7 0.2 add_convert_fusion
  139.0 1.6 collective-permute-start.20
  140.6 13.0 %collective-permute-done.13 = bf16[2,2,256,384]{3,2,1,0:T(8,128)(2,1)S(1)} collective-permute-done((bf16[2,2,256,384]{3,2,1,0:T(8,128)(2,1)}, bf16[2,2,256,384]{3,2,1,0:T(8,128)(2,1)S(1)}, u32[]{:S(2)}, u32[]{:S(2)}) %collective-permute-start.13) | collective-permute-done | bytes 786464 | tf_op jit(solution)/shard_map/ppermute | solution.py:453
  153.5 0.2 add_convert_fusion.3
  153.7 0.1 fusion.3
  153.8 1.7 collective-permute-start.15
  155.5 0.2 add_convert_fusion.2
  155.8 1.6 collective-permute-start.16
  157.4 6.4 %collective-permute-done.18.refs_1_ = bf16[1,2,256,384]{3,2,1,0:T(8,128)(2,1)S(1)} collective-permute-done((bf16[1,2,256,384]{3,2,1,0:T(8,128)(2,1)S(1)}, bf16[1,2,256,384]{3,2,1,0:T(8,128)(2,1)S(1)}, u32[]{:S(2)}, u32[]{:S(2)}) %collective-permute-start.18) | collective-permute-done | bytes 393248 | tf_op jit(solution)/shard_map/ppermute | solution.py:501
  163.8 1.2 put.2.refs_4_
  165.1 1.9 %reduce-scatter.2.cloned.1.call-done.rows = bf16[128,2176]{1,0:T(8,128)(2,1)} async-done(((bf16[1024,2176]{1,0:T(8,128)(2,1)}), bf16[128,2176]{1,0:T(8,128)(2,1)}) %reduce-scatter.2.cloned.1.call-update) | async-done | bytes 557072 | tf_op jit(solution)/shard_map/reduce_scatter | solution.py:485
  166.9 1.9 %finish.1 = (bf16[128,2048]{1,0:T(8,128)(2,1)}, bf16[8,128]{1,0:T(8,128)(2,1)}) custom-call(bf16[128,2176]{1,0:T(8,128)(2,1)} %reduce-scatter.2.cloned.1.call-done.rows), custom_call_target="tpu_custom_call" | custom-call | bytes 1048576 | tf_op jit(solution)/shard_map/finish/pallas_call | solution.py:486
  168.8 3.4 %collective-permute-done.15.refs_1_ = bf16[1,2,256,384]{3,2,1,0:T(8,128)(2,1)S(1)} collective-permute-done((bf16[1,2,256,384]{3,2,1,0:T(8,128)(2,1)S(1)}, bf16[1,2,256,384]{3,2,1,0:T(8,128)(2,1)S(1)}, u32[]{:S(2)}, u32[]{:S(2)}) %collective-permute-start.15) | collective-permute-done | bytes 393248 | tf_op jit(solution)/shard_map/ppermute | solution.py:501
  172.2 1.2 put.3
  (48 shorter events, 0.5 us)
Async XLA Ops:
  7.2 2.1 %copy-start.8 = (bf16[128,2048]{1,0:T(8,128)(2,1)S(1)}, bf16[128,2048]{1,0:T(8,128)(2,1)}, u32[]{:S(2)}) copy-start(bf16[128,2048]{1,0:T(8,128)(2,1)} %refs_0_.1) | copy-start | bytes 1572868
  7.2 63.9 %all-gather.2.cloned.1.call-start = ((), (), s32[]{:S(2)}) async-start(), calls=%async_computation.1 | async-start | bytes 5013504 | tf_op jit(solution)/shard_map/all_gather | solution.py:256
  9.3 157.7 %reduce-scatter.2.cloned.1.call-start = ((), (), s32[]{:S(2)}) async-start(), calls=%async_computation.2 | async-start | bytes 5013504 | tf_op jit(solution)/shard_map/reduce_scatter | solution.py:485
  9.3 5.8 %collective-permute-start = (bf16[128,2048]{1,0:T(8,128)(2,1)S(1)}, bf16[128,2048]{1,0:T(8,128)(2,1)S(1)}, u32[]{:S(2)}, u32[]{:S(2)}) collective-permute-start(bf16[128,2048]{1,0:T(8,128)(2,1)S(1)} %copy-done.8), channel_id=1, source_target_pairs={{0,1},{1,0},{2,3},{3,2},{4,5},{5,4},{6,7},{7,6},{8,9},{9,8},{10,11... | collective-permute-start | bytes 1572872 | tf_op jit(solution)/shard_map/ppermute | solution.py:263
  9.8 15.6 %collective-permute-start.1 = (bf16[128,2048]{1,0:T(8,128)(2,1)S(1)}, bf16[128,2048]{1,0:T(8,128)(2,1)}, u32[]{:S(2)}, u32[]{:S(2)}) collective-permute-start(bf16[128,2048]{1,0:T(8,128)(2,1)S(1)} %copy-done.8), channel_id=1, source_target_pairs={{0,2},{2,4},{3,1},{4,6},{5,3},{7,5},{8,10},{10,12},{11,9},{12,14},... | collective-permute-start | bytes 1572872 | tf_op jit(solution)/shard_map/ppermute | solution.py:263
  15.1 10.3 %copy-start.9 = (bf16[128,2048]{1,0:T(8,128)(2,1)}, bf16[128,2048]{1,0:T(8,128)(2,1)S(1)}, u32[]{:S(2)}) copy-start(bf16[128,2048]{1,0:T(8,128)(2,1)S(1)} %collective-permute-done.refs_1_) | copy-start | bytes 1572868
  15.2 22.2 %collective-permute-start.2 = (bf16[128,2048]{1,0:T(8,128)(2,1)S(1)}, bf16[128,2048]{1,0:T(8,128)(2,1)}, u32[]{:S(2)}, u32[]{:S(2)}) collective-permute-start(bf16[128,2048]{1,0:T(8,128)(2,1)S(1)} %collective-permute-done.refs_1_), channel_id=1, source_target_pairs={{0,2},{2,4},{3,1},{4,6},{5,3},{7,5},{8,10},{10,12},{11,9},{12,14},... | collective-permute-start | bytes 1572872 | tf_op jit(solution)/shard_map/ppermute | solution.py:263
  25.4 15.2 %collective-permute-start.3 = (bf16[128,2048]{1,0:T(8,128)(2,1)}, bf16[128,2048]{1,0:T(8,128)(2,1)S(1)}, u32[]{:S(2)}, u32[]{:S(2)}) collective-permute-start(bf16[128,2048]{1,0:T(8,128)(2,1)} %collective-permute-done.1.refs_2_), channel_id=1, source_target_pairs={{2,4},{3,1},{4,6},{5,3},{10,12},{11,9},{12,14},{13,11},{18,20},{19... | collective-permute-start | bytes 1572872 | tf_op jit(solution)/shard_map/ppermute | solution.py:263
  37.3 5.3 %collective-permute-start.4 = (bf16[128,2048]{1,0:T(8,128)(2,1)}, bf16[128,2048]{1,0:T(8,128)(2,1)S(1)}, u32[]{:S(2)}, u32[]{:S(2)}) collective-permute-start(bf16[128,2048]{1,0:T(8,128)(2,1)} %collective-permute-done.2.refs_3_), channel_id=1, source_target_pairs={{2,4},{3,1},{4,6},{5,3},{10,12},{11,9},{12,14},{13,11},{18,20},{19... | collective-permute-start | bytes 1572872 | tf_op jit(solution)/shard_map/ppermute | solution.py:263
  38.0 6.7 %collective-permute-start.7 = (bf16[128,2048]{1,0:T(8,128)(2,1)}, bf16[128,2048]{1,0:T(8,128)(2,1)S(1)}, u32[]{:S(2)}, u32[]{:S(2)}) collective-permute-start(bf16[128,2048]{1,0:T(8,128)(2,1)} %collective-permute-done.1.refs_2_), channel_id=1, source_target_pairs={{1,0},{2,3},{3,2},{4,5},{5,4},{6,7},{9,8},{10,11},{11,10},{12,13},... | collective-permute-start | bytes 1572872 | tf_op jit(solution)/shard_map/ppermute | solution.py:263
  39.3 6.2 %collective-permute-start.8 = (bf16[128,2048]{1,0:T(8,128)(2,1)}, bf16[128,2048]{1,0:T(8,128)(2,1)S(1)}, u32[]{:S(2)}, u32[]{:S(2)}) collective-permute-start(bf16[128,2048]{1,0:T(8,128)(2,1)} %collective-permute-done.2.refs_3_), channel_id=1, source_target_pairs={{1,0},{2,3},{3,2},{4,5},{5,4},{6,7},{9,8},{10,11},{11,10},{12,13},... | collective-permute-start | bytes 1572872 | tf_op jit(solution)/shard_map/ppermute | solution.py:263
  40.6 40.8 %copy-start.10 = (bf16[128,2048]{1,0:T(8,128)(2,1)}, bf16[128,2048]{1,0:T(8,128)(2,1)S(1)}, u32[]{:S(2)}) copy-start(bf16[128,2048]{1,0:T(8,128)(2,1)S(1)} %collective-permute-done.3.refs_4_) | copy-start | bytes 1572868
  40.6 28.3 %collective-permute-start.9 = (bf16[128,2048]{1,0:T(8,128)(2,1)S(1)}, bf16[128,2048]{1,0:T(8,128)(2,1)S(1)}, u32[]{:S(2)}, u32[]{:S(2)}) collective-permute-start(bf16[128,2048]{1,0:T(8,128)(2,1)S(1)} %collective-permute-done.3.refs_4_), channel_id=1, source_target_pairs={{1,0},{3,2},{4,5},{6,7},{9,8},{11,10},{12,13},{14,15},{17,16},{19,... | collective-permute-start | bytes 1572872 | tf_op jit(solution)/shard_map/ppermute | solution.py:263
  41.9 40.8 %collective-permute-start.5 = (bf16[128,2048]{1,0:T(8,128)(2,1)S(1)}, bf16[128,2048]{1,0:T(8,128)(2,1)S(1)}, u32[]{:S(2)}, u32[]{:S(2)}) collective-permute-start(bf16[128,2048]{1,0:T(8,128)(2,1)S(1)} %collective-permute-done.3.refs_4_), channel_id=1, source_target_pairs={{3,1},{4,6},{11,9},{12,14},{19,17},{20,22},{27,25},{28,30}} | collective-permute-start | bytes 1572872 | tf_op jit(solution)/shard_map/ppermute | solution.py:263
  42.6 28.4 %copy-start.4 = (bf16[128,2048]{1,0:T(8,128)(2,1)}, bf16[128,2048]{1,0:T(8,128)(2,1)S(1)}, u32[]{:S(2)}) copy-start(bf16[128,2048]{1,0:T(8,128)(2,1)S(1)} %collective-permute-done.4.refs_3_.refs_5_) | copy-start | bytes 1572868
  42.7 40.1 %collective-permute-start.6 = (bf16[128,2048]{1,0:T(8,128)(2,1)S(1)}, bf16[128,2048]{1,0:T(8,128)(2,1)}, u32[]{:S(2)}, u32[]{:S(2)}) collective-permute-start(bf16[128,2048]{1,0:T(8,128)(2,1)S(1)} %collective-permute-done.4.refs_3_.refs_5_), channel_id=1, source_target_pairs={{3,1},{4,6},{11,9},{12,14},{19,17},{20,22},{27,25},{28,30}} | collective-permute-start | bytes 1572872 | tf_op jit(solution)/shard_map/ppermute | solution.py:263
  44.7 26.3 %copy-start.5 = (bf16[128,2048]{1,0:T(8,128)(2,1)}, bf16[128,2048]{1,0:T(8,128)(2,1)S(1)}, u32[]{:S(2)}) copy-start(bf16[128,2048]{1,0:T(8,128)(2,1)S(1)} %collective-permute-done.7.refs_0_.refs_8_) | copy-start | bytes 1572868
  45.5 25.6 %copy-start.6 = (bf16[128,2048]{1,0:T(8,128)(2,1)}, bf16[128,2048]{1,0:T(8,128)(2,1)S(1)}, u32[]{:S(2)}) copy-start(bf16[128,2048]{1,0:T(8,128)(2,1)S(1)} %collective-permute-done.8.refs_1_.refs_9_) | copy-start | bytes 1572868
  68.9 2.2 %copy-start.7 = (bf16[128,2048]{1,0:T(8,128)(2,1)}, bf16[128,2048]{1,0:T(8,128)(2,1)S(1)}, u32[]{:S(2)}) copy-start(bf16[128,2048]{1,0:T(8,128)(2,1)S(1)} %collective-permute-done.9.refs_2_.refs_10_) | copy-start | bytes 1572868
  81.5 8.7 %collective-permute-start.10 = (bf16[128,2048]{1,0:T(8,128)(2,1)}, bf16[128,2048]{1,0:T(8,128)(2,1)S(1)}, u32[]{:S(2)}, u32[]{:S(2)}) collective-permute-start(bf16[128,2048]{1,0:T(8,128)(2,1)} %copy-done.4), channel_id=1, source_target_pairs={{1,0},{3,2},{4,5},{6,7},{9,8},{11,10},{12,13},{14,15},{17,16},{19,... | collective-permute-start | bytes 1572872 | tf_op jit(solution)/shard_map/ppermute | solution.py:263
  82.8 9.9 %copy-start.11 = (bf16[128,2048]{1,0:T(8,128)(2,1)}, bf16[128,2048]{1,0:T(8,128)(2,1)S(1)}, u32[]{:S(2)}) copy-start(bf16[128,2048]{1,0:T(8,128)(2,1)S(1)} %collective-permute-done.5.refs_6_) | copy-start | bytes 1572868
  82.8 8.7 %collective-permute-start.12 = (bf16[128,2048]{1,0:T(8,128)(2,1)}, bf16[128,2048]{1,0:T(8,128)(2,1)S(1)}, u32[]{:S(2)}, u32[]{:S(2)}) collective-permute-start(bf16[128,2048]{1,0:T(8,128)(2,1)} %collective-permute-done.6.refs_7_), channel_id=1, source_target_pairs={{1,0},{6,7},{9,8},{14,15},{17,16},{22,23},{25,24},{30,31}} | collective-permute-start | bytes 1572872 | tf_op jit(solution)/shard_map/ppermute | solution.py:263
  84.1 8.5 %collective-permute-start.11 = (bf16[128,2048]{1,0:T(8,128)(2,1)S(1)}, bf16[128,2048]{1,0:T(8,128)(2,1)S(1)}, u32[]{:S(2)}, u32[]{:S(2)}) collective-permute-start(bf16[128,2048]{1,0:T(8,128)(2,1)S(1)} %collective-permute-done.5.refs_6_), channel_id=1, source_target_pairs={{1,0},{6,7},{9,8},{14,15},{17,16},{22,23},{25,24},{30,31}} | collective-permute-start | bytes 1572872 | tf_op jit(solution)/shard_map/ppermute | solution.py:263
  90.1 2.5 %copy-start.12 = (bf16[128,2048]{1,0:T(8,128)(2,1)}, bf16[128,2048]{1,0:T(8,128)(2,1)S(1)}, u32[]{:S(2)}) copy-start(bf16[128,2048]{1,0:T(8,128)(2,1)S(1)} %collective-permute-done.10.refs_11_) | copy-start | bytes 1572868
  91.5 1.1 copy-start.13
  92.6 0.8 copy-start.14
  116.5 20.2 %collective-permute-start.17 = (bf16[2,2,256,384]{3,2,1,0:T(8,128)(2,1)}, bf16[2,2,256,384]{3,2,1,0:T(8,128)(2,1)S(1)}, u32[]{:S(2)}, u32[]{:S(2)}) collective-permute-start(bf16[2,2,256,384]{3,2,1,0:T(8,128)(2,1)} %get-tuple-element.56), channel_id=1, source_target_pairs={{0,8},{8,0},{16,24},{24,16},{1,9},{9,1},{17,25},{25,17},{2,10},{10... | collective-permute-start | bytes 2359304 | tf_op jit(solution)/shard_map/ppermute | solution.py:453
  118.2 18.5 %copy-start.3 = (bf16[2,2,256,384]{3,2,1,0:T(8,128)(2,1)S(1)}, bf16[2,2,256,384]{3,2,1,0:T(8,128)(2,1)}, u32[]{:S(2)}) copy-start(bf16[2,2,256,384]{3,2,1,0:T(8,128)(2,1)} %get-tuple-element.55) | copy-start | bytes 2359300
  118.2 20.5 %collective-permute-start.19 = (bf16[2,2,256,384]{3,2,1,0:T(8,128)(2,1)}, bf16[2,2,256,384]{3,2,1,0:T(8,128)(2,1)S(1)}, u32[]{:S(2)}, u32[]{:S(2)}) collective-permute-start(bf16[2,2,256,384]{3,2,1,0:T(8,128)(2,1)} %get-tuple-element.58), channel_id=1, source_target_pairs={{0,16},{8,24},{16,0},{24,8},{1,17},{9,25},{17,1},{25,9},{2,18},{10... | collective-permute-start | bytes 2359304 | tf_op jit(solution)/shard_map/ppermute | solution.py:453
  125.6 27.9 %collective-permute-start.13 = (bf16[2,2,256,384]{3,2,1,0:T(8,128)(2,1)}, bf16[2,2,256,384]{3,2,1,0:T(8,128)(2,1)S(1)}, u32[]{:S(2)}, u32[]{:S(2)}) collective-permute-start(bf16[2,2,256,384]{3,2,1,0:T(8,128)(2,1)} %get-tuple-element.48), channel_id=1, source_target_pairs={{0,8},{8,0},{16,24},{24,16},{1,9},{9,1},{17,25},{25,17},{2,10},{10... | collective-permute-start | bytes 2359304 | tf_op jit(solution)/shard_map/ppermute | solution.py:453
  126.5 29.0 %collective-permute-start.14 = (bf16[2,2,256,384]{3,2,1,0:T(8,128)(2,1)}, bf16[2,2,256,384]{3,2,1,0:T(8,128)(2,1)S(1)}, u32[]{:S(2)}, u32[]{:S(2)}) collective-permute-start(bf16[2,2,256,384]{3,2,1,0:T(8,128)(2,1)} %get-tuple-element.50), channel_id=1, source_target_pairs={{0,16},{8,24},{16,0},{24,8},{1,17},{9,25},{17,1},{25,9},{2,18},{10... | collective-permute-start | bytes 2359304 | tf_op jit(solution)/shard_map/ppermute | solution.py:453
  136.7 2.0 %copy-start.2 = (bf16[2,2,256,384]{3,2,1,0:T(8,128)(2,1)S(1)}, bf16[2,2,256,384]{3,2,1,0:T(8,128)(2,1)}, u32[]{:S(2)}) copy-start(bf16[2,2,256,384]{3,2,1,0:T(8,128)(2,1)} %get-tuple-element.57) | copy-start | bytes 2359300
  137.0 26.9 %collective-permute-start.18 = (bf16[1,2,256,384]{3,2,1,0:T(8,128)(2,1)S(1)}, bf16[1,2,256,384]{3,2,1,0:T(8,128)(2,1)S(1)}, u32[]{:S(2)}, u32[]{:S(2)}) collective-permute-start(bf16[1,2,256,384]{3,2,1,0:T(8,128)(2,1)S(1)} %get-tuple-element.61), channel_id=1, source_target_pairs={{0,16},{8,24},{16,0},{24,8},{1,17},{9,25},{17,1},{25,9},{2,18},{10... | collective-permute-start | bytes 1179656 | tf_op jit(solution)/shard_map/ppermute | solution.py:501
  138.7 14.8 %copy-start.1 = (bf16[2,2,256,384]{3,2,1,0:T(8,128)(2,1)S(1)}, bf16[2,2,256,384]{3,2,1,0:T(8,128)(2,1)}, u32[]{:S(2)}) copy-start(bf16[2,2,256,384]{3,2,1,0:T(8,128)(2,1)} %get-tuple-element.47) | copy-start | bytes 2359300
  139.0 24.8 %collective-permute-start.20 = (bf16[1,2,256,384]{3,2,1,0:T(8,128)(2,1)S(1)}, bf16[1,2,256,384]{3,2,1,0:T(8,128)(2,1)S(1)}, u32[]{:S(2)}, u32[]{:S(2)}) collective-permute-start(bf16[1,2,256,384]{3,2,1,0:T(8,128)(2,1)S(1)} %get-tuple-element.59), channel_id=1, source_target_pairs={{0,8},{8,0},{16,24},{24,16},{1,9},{9,1},{17,25},{25,17},{2,10},{10... | collective-permute-start | bytes 1179656 | tf_op jit(solution)/shard_map/ppermute | solution.py:501
  153.5 2.0 %copy-start = (bf16[2,2,256,384]{3,2,1,0:T(8,128)(2,1)S(1)}, bf16[2,2,256,384]{3,2,1,0:T(8,128)(2,1)}, u32[]{:S(2)}) copy-start(bf16[2,2,256,384]{3,2,1,0:T(8,128)(2,1)} %get-tuple-element.49) | copy-start | bytes 2359300
  153.8 18.4 %collective-permute-start.15 = (bf16[1,2,256,384]{3,2,1,0:T(8,128)(2,1)S(1)}, bf16[1,2,256,384]{3,2,1,0:T(8,128)(2,1)S(1)}, u32[]{:S(2)}, u32[]{:S(2)}) collective-permute-start(bf16[1,2,256,384]{3,2,1,0:T(8,128)(2,1)S(1)} %get-tuple-element.65), channel_id=1, source_target_pairs={{0,16},{8,24},{16,0},{24,8},{1,17},{9,25},{17,1},{25,9},{2,18},{10... | collective-permute-start | bytes 1179656 | tf_op jit(solution)/shard_map/ppermute | solution.py:501
  155.8 16.4 %collective-permute-start.16 = (bf16[1,2,256,384]{3,2,1,0:T(8,128)(2,1)S(1)}, bf16[1,2,256,384]{3,2,1,0:T(8,128)(2,1)S(1)}, u32[]{:S(2)}, u32[]{:S(2)}) collective-permute-start(bf16[1,2,256,384]{3,2,1,0:T(8,128)(2,1)S(1)} %get-tuple-element.63), channel_id=1, source_target_pairs={{0,8},{8,0},{16,24},{24,16},{1,9},{9,1},{17,25},{25,17},{2,10},{10... | collective-permute-start | bytes 1179656 | tf_op jit(solution)/shard_map/ppermute | solution.py:501
Sparse Core Ops, SparseCore 0:
  10.2 60.8 all-gather.1
  111.0 55.9 reduce-scatter.1

commit v17 on v16

--- a/solution.py
+++ b/solution.py
@@ -31,7 +31,8 @@
     x_out[:, pl.ds(width, LANES)] = info.T.astype(bf16)
 
 
-def flip_kernel(w, out):
+def flip_kernel(place, w, out):
+    del place
     out[0] = w[0].T
 
 
@@ -56,8 +57,16 @@
                     start(pair, slot, 0 if left else 1)
 
 
+def copies_of(pairs, sem):
+    return [pltpu.make_async_copy(src, dst, sem.at[n]) for n, (src, dst) in enumerate(pairs)]
+
+
+def staged(steps, later):
+    return [later[len(later) * n // steps : len(later) * (n + 1) // steps] for n in range(steps)]
+
+
 def copy_all(pairs, sem):
-    copies = [pltpu.make_async_copy(src, dst, sem.at[n]) for n, (src, dst) in enumerate(pairs)]
+    copies = copies_of(pairs, sem)
     for copy in copies:
         copy.start()
     return copies
@@ -68,7 +77,8 @@
     pick_out, meta, hid_out, scaled_out, slope_out, rows, w_v, held, gates, pick, hid, scaled, slope, sems, out_sem = refs
     experts, members = held.shape[0], rows.shape[1]
     arrive = copy_all([(x_all.at[pl.ds(g * members, members), :], rows.at[g]) for g in range(groups)], sems.at[0])
-    weights = copy_all([(w_up.at[b], w_v.at[b]) for b in range(experts)], sems.at[1])
+    weights = copies_of([(w_up.at[b], w_v.at[b]) for b in range(experts)], sems.at[1])
+    stages = staged(groups, weights)
     before = lax.broadcasted_iota(jnp.int32, (members, members), 0) < lax.broadcasted_iota(
         jnp.int32, (members, members), 1
     )
@@ -76,6 +86,8 @@
     spot = lax.broadcasted_iota(jnp.int32, (cap, members), 0).astype(f32)
     for g in range(groups):
         arrive[g].wait()
+        for copy in stages[g]:
+            copy.start()
         info = rows[g, :, pl.ds(width, LANES)]
         meta[pl.ds(g * members, members), :] = info
         across = info.astype(f32).T
@@ -152,14 +164,17 @@
     first_pick = copy_all([(pick_in, pick)], sems.at[0])
     start_blocks(place, groups, own, mine, other, moved, block_sem)
     loads = [
-        copy_all([(src.at[b], dst.at[b]) for b in range(experts)], sems.at[n])
+        copies_of([(src.at[b], dst.at[b]) for b in range(experts)], sems.at[n])
         for n, (src, dst) in enumerate(((w_down, down_v), (hid_in, hid), (slope_in, slope), (w_flip, flip_v)), 1)
     ]
+    stages = staged(groups, [load[b] for b in range(experts) for load in loads])
     first_pick[0].wait()
     for slot in range(groups):
         for part in range(2):
             at = pl.ds(part * half, half)
             pltpu.make_async_copy(own[0], moved.at[slot, at, :], block_sem.at[slot, part]).wait()
+        for copy in stages[slot]:
+            copy.start()
         group = lax.rem(place[3] - slot + groups, groups)
         first = pl.multiple_of(group * cap, PACK)
         got = dot(pick[group], moved[slot]).astype(bf16)
@@ -262,21 +277,6 @@
     def hop(value, pairs):
         return lax.ppermute(value, "ep", pairs)
 
-    def at_group(i):
-        return jnp.minimum(i, groups - 1)
-
-    def at_expert(i):
-        return jnp.clip(i - groups, 0, experts - 1)
-
-    def at_slot(i, place):
-        return lax.rem(place[3] - at_group(i) + groups, groups)
-
-    def by_group(n):
-        return pl.BlockSpec((members, n), lambda i, *_: (at_group(i), 0))
-
-    def by_expert(rows, n):
-        return pl.BlockSpec((1, rows, n), lambda i, *_: (at_expert(i), 0, 0))
-
     def call(kernel, name, grid, flops, nbytes, in_specs, out_specs, out_shape, scratch_shapes, prefetch=0):
         return pl.pallas_call(
             kernel,
@@ -300,55 +300,12 @@
         experts,
         0,
         2 * row_bytes,
-        in_specs=[pl.BlockSpec((1, width, hidden), lambda b: (b, 0, 0))],
+        in_specs=[SMEM, pl.BlockSpec((1, width, hidden), lambda b: (b, 0, 0))],
         out_specs=pl.BlockSpec((1, hidden, width), lambda b: (b, 0, 0)),
         out_shape=shape(experts, hidden, width),
         scratch_shapes=[],
-    )(w_up)
-    def at_group(i):
-        return jnp.minimum(i, groups - 1)
-
-    def at_expert(i):
-        return jnp.clip(i - groups, 0, experts - 1)
-
-    def at_slot(i, place):
-        return lax.rem(place[3] - at_group(i) + groups, groups)
-
-    def by_group(n):
-        return pl.BlockSpec((members, n), lambda i, *_: (at_group(i), 0))
-
-    def by_expert(rows, n):
-        return pl.BlockSpec((1, rows, n), lambda i, *_: (at_expert(i), 0, 0))
-
-    def call(kernel, name, grid, flops, nbytes, in_specs, out_specs, out_shape, scratch_shapes, prefetch=0):
-        return pl.pallas_call(
-            kernel,
-            grid_spec=pltpu.PrefetchScalarGridSpec(
-                num_scalar_prefetch=prefetch,
-                grid=(grid,),
-                in_specs=in_specs,
-                out_specs=out_specs,
-                scratch_shapes=scratch_shapes,
-            ),
-            out_shape=out_shape,
-            compiler_params=pltpu.CompilerParams(vmem_limit_bytes=VMEM_LIMIT),
-            cost_estimate=cost(flops, nbytes),
-            name=name,
-        )
-
-    row_bytes = 2 * experts * hidden * width
-    w_flip = call(
-        flip_kernel,
-        "flip",
-        experts,
-        0,
-        2 * row_bytes,
-        in_specs=[pl.BlockSpec((1, width, hidden), lambda b: (b, 0, 0))],
-        out_specs=pl.BlockSpec((1, hidden, width), lambda b: (b, 0, 0)),
-        out_shape=shape(experts, hidden, width),
-        scratch_shapes=[],
-    )(w_up)
-    dy_own = jnp.concatenate([cotangent, hop(cotangent, [(p, p ^ 1) for p in range(ep_count)])], axis=0)
+    )(place, w_up)
+
     lines = [None] + [
         [(p, reach(p, 1)) for p in range(ep_count) if None not in (reach(p, 1), reach(p, 1 - step))]
         for step in range(1, groups)
@@ -363,11 +320,8 @@
         dy_mine.append([hop(part, lines[step]) for part in dy_mine[-1]])
     dy_mine.append([hop(part, lines[-1]) for part in dy_mine[-1]])
     dy_other = [[hop(part, swaps[1]) for part in dy_mine[0]]]
-    early_swap = hop(dy_mine[1][0], swaps[2])
 
     act = shape(experts, routes, hidden)
-    act_spec = by_expert(routes, hidden)
-    pick_spec = pl.BlockSpec((1, experts * cap, members), lambda i, *_: (at_group(i), 0, 0))
     pick_flops = 2 * total * experts * cap * width
     main_flops = 2 * experts * routes * width * hidden
     act3 = pltpu.VMEM((experts, routes, hidden), bf16)
@@ -386,7 +340,7 @@
             name=name,
         )
 
-    up_after = dy_other[0] + [early_swap] + dy_mine[-2][1:]
+    up_after = dy_other[0] + dy_mine[-2][1:]
     pick, meta, hid, scaled, slope_g = one(
         functools.partial(up_kernel, groups, width, top, cap, len(up_after)),
         "up",
@@ -410,10 +364,7 @@
     )(place, x_all, w_up, *up_after)
     for row, swap in zip(dy_mine[1:], swaps[2:]):
         dy_other.append([])
-        for n, part in enumerate(row):
-            if len(dy_other) == 2 and n == 0:
-                dy_other[-1].append(early_swap)
-                continue
+        for part in row:
             part, hid = lax.optimization_barrier((part, hid))
             dy_other[-1].append(hop(part, swap))
     blocks = [part for row in [dy_own] + dy_mine + dy_other for part in row]

time: 182 us -> 180 us (0.989)
    all_gather x1, waiting for transfers between devices: 2.18 us -> 25.8 us  [shards(): x_all = lax.all_gather(x_own, 'ep', axis=0, tiled=True)]
    ppermute x13, waiting for transfers between devices: 42.4 us -> 19.6 us  [hop(): return lax.ppermute(value, 'ep', pairs)]
  transfers between devices with their start and end apart: 23 -> 23, of which waited for: 12 -> 13; matrix products, arithmetic and copies ran while one was open for 1% -> 1% of each run, Pallas kernels for 18% -> 18%
where the time goes in v17:
time: 180 us; the launch traced here: 179 us
  waiting for transfers between devices  79.1 us (44%)
  Pallas kernels  51.2 us (28%)
  starting transfers between devices  31.9 us (18%)
  between operations  14.4 us (8%)
    all_gather x1, waiting for transfers between devices, shards(): x_all = lax.all_gather(x_own, 'ep', axis=0, tiled=True)  25.8 us
    ppermute x4, waiting for transfers between devices, exchange(): got = lax.ppermute(send, 'dp', [(i, i ^ bit) for i in range(dp_count)])  23.3 us
    ppermute x13, starting transfers between devices, hop(): return lax.ppermute(value, 'ep', pairs)  20.8 us
    ppermute x13, waiting for transfers between devices, hop(): return lax.ppermute(value, 'ep', pairs)  19.6 us
    pallas_call x1, Pallas kernels, shards(): one(functools.partial(tail_kernel, groups, cap, width, top), 'tail', 8 *...  16.2 us
    pallas_call x2, Pallas kernels, down(): one(functools.partial(down_kernel, orders, start), 'down', 16 * main_flop...  11.5 us
    pallas_call x1, Pallas kernels, shards(): one(functools.partial(up_kernel, groups, width, top, cap, len(up_after)),...  10.4 us
    ppermute x4, waiting for transfers between devices, shards(): lax.ppermute(send, 'dp', [(i, i ^ 1 << (g + last) % bits) for i in range(...  9.74 us
  transfers between devices with their start and end apart: 23, of which 13 were waited for; matrix products, arithmetic and copies ran while one was open for 1% of the time, Pallas kernels for 18%

profile of v17, /device:TPU:0, one launch (start us, length us, event | category | flops | bytes accessed | tf_op | source)
XLA Modules:
  0.0 179.1 jit_solution(11153820548646997509)
XLA Ops:
  7.2 2.0 %pack.1 = bf16[128,2176]{1,0:T(8,128)(2,1)} custom-call(bf16[128,2048]{1,0:T(8,128)(2,1)} %tokens.1, s32[8,128]{1,0:T(8,128)} %bitcast.7, bf16[8,128]{1,0:T(8,128)(2,1)} %bitcast.8), custom_call_target="tpu_custom_call" | custom-call | bytes 1048576 | tf_op jit(solution)/shard_map/pack/pallas_call | solution.py:264
  9.3 0.5 collective-permute-start
  9.8 4.5 %collective-permute-start.1 = (bf16[128,2048]{1,0:T(8,128)(2,1)S(1)}, bf16[128,2048]{1,0:T(8,128)(2,1)S(1)}, u32[]{:S(2)}, u32[]{:S(2)}) collective-permute-start(bf16[128,2048]{1,0:T(8,128)(2,1)S(1)} %copy-done.4), channel_id=1, source_target_pairs={{0,2},{2,4},{3,1},{4,6},{5,3},{7,5},{8,10},{10,12},{11,9},{12,14},... | collective-permute-start | bytes 1572872 | tf_op jit(solution)/shard_map/ppermute | solution.py:278
  14.4 3.5 %collective-permute-start.2 = (bf16[128,2048]{1,0:T(8,128)(2,1)S(1)}, bf16[128,2048]{1,0:T(8,128)(2,1)S(1)}, u32[]{:S(2)}, u32[]{:S(2)}) collective-permute-start(bf16[128,2048]{1,0:T(8,128)(2,1)S(1)} %collective-permute-done.refs_1_), channel_id=1, source_target_pairs={{0,2},{2,4},{3,1},{4,6},{5,3},{7,5},{8,10},{10,12},{11,9},{12,14},... | collective-permute-start | bytes 1572872 | tf_op jit(solution)/shard_map/ppermute | solution.py:278
  17.9 0.6 pad_add_fusion.place
  18.5 6.8 %flip.1.refs_16_ = bf16[4,384,2048]{2,1,0:T(8,128)(2,1)} custom-call(s32[4]{0:T(128)} %pad_add_fusion.place, bf16[4,2048,384]{2,1,0:T(8,128)(2,1)} %w_up.1), custom_call_target="tpu_custom_call" | custom-call | bytes 12582912 | tf_op jit(solution)/shard_map/flip/pallas_call | solution.py:297
  25.3 0.7 collective-permute-start.3
  26.0 11.3 %collective-permute-done.2.refs_3_ = bf16[128,2048]{1,0:T(8,128)(2,1)S(1)} collective-permute-done((bf16[128,2048]{1,0:T(8,128)(2,1)S(1)}, bf16[128,2048]{1,0:T(8,128)(2,1)S(1)}, u32[]{:S(2)}, u32[]{:S(2)}) %collective-permute-start.2) | collective-permute-done | bytes 524320 | tf_op jit(solution)/shard_map/ppermute | solution.py:278
  37.3 0.7 collective-permute-start.4
  38.0 1.3 collective-permute-start.7
  39.3 1.3 collective-permute-start.8
  40.6 1.5 collective-permute-start.5
  42.1 1.5 collective-permute-start.6
  43.6 0.3 collective-permute-done.7.refs_0_.refs_8_
  43.9 1.4 collective-permute-done.8.refs_1_.refs_9_
  45.3 25.8 %all-gather.2.cloned.1.call-done.x_all = bf16[1024,2176]{1,0:T(8,128)(2,1)} async-done(((bf16[128,2176]{1,0:T(8,128)(2,1)}), bf16[1024,2176]{1,0:T(8,128)(2,1)}) %all-gather.2.cloned.1.call-update) | async-done | bytes 4456464 | tf_op jit(solution)/shard_map/all_gather | solution.py:271
  71.1 10.4 %up.1 = (bf16[4,320,256]{2,1,0:T(8,128)(2,1)}, bf16[1024,128]{1,0:T(8,128)(2,1)}, bf16[4,320,384]{2,1,0:T(8,128)(2,1)}, bf16[4,320,384]{2,1,0:T(8,128)(2,1)}, bf16[4,320,384]{2,1,0:T(8,128)(2,1)}) custom-call(s32[4]{0:T(128)} %pad_add_fusion.place, bf16[1024,2176]{1,0:T(8,128)(2,1)} %all-gather.2.cloned.1.call-done.x_all, bf16[4,2048,384]{2,1,0:T(8,128)(2,1)} %w_up.1, ...), custom_call_target="tpu_custom_call" | custom-call | flops 3355443200 | bytes 10747904 | tf_op jit(solution)/shard_map/up/pallas_call | solution.py:344
  81.5 1.3 collective-permute-start.10
  82.8 1.3 collective-permute-start.9
  84.1 1.3 collective-permute-start.12
  85.4 1.5 collective-permute-start.11
  86.9 2.5 %collective-permute-done.10.refs_11_ = bf16[128,2048]{1,0:T(8,128)(2,1)S(1)} collective-permute-done((bf16[128,2048]{1,0:T(8,128)(2,1)}, bf16[128,2048]{1,0:T(8,128)(2,1)S(1)}, u32[]{:S(2)}, u32[]{:S(2)}) %collective-permute-start.10) | collective-permute-done | bytes 524320 | tf_op jit(solution)/shard_map/ppermute | solution.py:278
  89.4 1.1 collective-permute-done.9.refs_10_
  90.5 1.6 collective-permute-done.12.refs_13_
  92.0 1.3 collective-permute-done.11.refs_12_
  93.4 0.8 copy-done.15
  94.2 16.2 %tail.1 = (bf16[1024,2176]{1,0:T(8,128)(2,1)}, bf16[4,320,2048]{2,1,0:T(8,128)(2,1)}) custom-call(s32[4]{0:T(128)} %pad_add_fusion.place, bf16[128,2048]{1,0:T(8,128)(2,1)} %refs_0_.1, bf16[128,2048]{1,0:T(8,128)(2,1)} %copy-done.5, bf16[128,2048]{1,0:T(8,128)(2,1)} %copy-done.6, bf16[128,2048]{1,0:T(8,128)(2,1)} %copy-done.7, bf16[128,2048]{1,0:T(8,128)(2,1)} %copy-done.8, ...), custom_call_target="tpu_custom_call" | custom-call | flops 16106127360 | bytes 25165824 | tf_op jit(solution)/shard_map/tail/pallas_call | solution.py:412
  110.4 5.6 %down.3 = (bf16[2,2,256,384]{3,2,1,0:T(8,128)(2,1)}, bf16[2,2,256,384]{3,2,1,0:T(8,128)(2,1)}, bf16[2,2,256,384]{3,2,1,0:T(8,128)(2,1)}, bf16[2,2,256,384]{3,2,1,0:T(8,128)(2,1)}) custom-call(s32[4]{0:T(128)} %pad_add_fusion.place, bf16[4,320,2048]{2,1,0:T(8,128)(2,1)} %get-tuple-element.49.kept, bf16[4,320,384]{2,1,0:T(8,128)(2,1)} %get-tuple-element.50.scaled_in), custom_call_target="tpu_custom_call" | custom-call | flops 32212254720 | bytes 50331648 | tf_op jit(solution)/shard_map/down/pallas_call | solution.py:382
  116.0 1.7 collective-permute-start.17
  117.8 1.5 collective-permute-start.19
  119.3 5.9 %down.2 = (bf16[2,2,256,384]{3,2,1,0:T(8,128)(2,1)}, bf16[2,2,256,384]{3,2,1,0:T(8,128)(2,1)}, bf16[2,2,256,384]{3,2,1,0:T(8,128)(2,1)}, bf16[2,2,256,384]{3,2,1,0:T(8,128)(2,1)}) custom-call(s32[4]{0:T(128)} %pad_add_fusion.place, bf16[4,320,2048]{2,1,0:T(8,128)(2,1)} %get-tuple-element.49.kept, bf16[4,320,384]{2,1,0:T(8,128)(2,1)} %get-tuple-element.50.scaled_in), custom_call_target="tpu_custom_call" | custom-call | flops 32212254720 | bytes 50331648 | tf_op jit(solution)/shard_map/down/pallas_call | solution.py:382
  125.2 0.8 collective-permute-start.13
  125.9 0.4 collective-permute-start.14
  126.4 10.4 %collective-permute-done.17 = bf16[2,2,256,384]{3,2,1,0:T(8,128)(2,1)S(1)} collective-permute-done((bf16[2,2,256,384]{3,2,1,0:T(8,128)(2,1)}, bf16[2,2,256,384]{3,2,1,0:T(8,128)(2,1)S(1)}, u32[]{:S(2)}, u32[]{:S(2)}) %collective-permute-start.17) | collective-permute-done | bytes 786464 | tf_op jit(solution)/shard_map/ppermute | solution.py:404
  136.7 0.2 add_convert_fusion.1
  137.0 1.7 collective-permute-start.18
  139.0 1.6 collective-permute-start.20
  140.6 13.0 %collective-permute-done.13 = bf16[2,2,256,384]{3,2,1,0:T(8,128)(2,1)S(1)} collective-permute-done((bf16[2,2,256,384]{3,2,1,0:T(8,128)(2,1)}, bf16[2,2,256,384]{3,2,1,0:T(8,128)(2,1)S(1)}, u32[]{:S(2)}, u32[]{:S(2)}) %collective-permute-start.13) | collective-permute-done | bytes 786464 | tf_op jit(solution)/shard_map/ppermute | solution.py:404
  153.6 0.2 add_convert_fusion.3
  153.9 1.7 collective-permute-start.15
  155.6 0.2 add_convert_fusion.2
  155.9 1.6 collective-permute-start.16
  157.5 6.2 %collective-permute-done.18.refs_1_ = bf16[1,2,256,384]{3,2,1,0:T(8,128)(2,1)S(1)} collective-permute-done((bf16[1,2,256,384]{3,2,1,0:T(8,128)(2,1)S(1)}, bf16[1,2,256,384]{3,2,1,0:T(8,128)(2,1)S(1)}, u32[]{:S(2)}, u32[]{:S(2)}) %collective-permute-start.18) | collective-permute-done | bytes 393248 | tf_op jit(solution)/shard_map/ppermute | solution.py:452
  163.7 1.2 put.2.refs_4_
  164.9 0.7 reduce-scatter.2.cloned.1.call-done.rows
  165.6 1.9 %finish.1 = (bf16[128,2048]{1,0:T(8,128)(2,1)}, bf16[8,128]{1,0:T(8,128)(2,1)}) custom-call(bf16[128,2176]{1,0:T(8,128)(2,1)} %reduce-scatter.2.cloned.1.call-done.rows), custom_call_target="tpu_custom_call" | custom-call | bytes 1048576 | tf_op jit(solution)/shard_map/finish/pallas_call | solution.py:437
  167.5 3.5 %collective-permute-done.15.refs_1_ = bf16[1,2,256,384]{3,2,1,0:T(8,128)(2,1)S(1)} collective-permute-done((bf16[1,2,256,384]{3,2,1,0:T(8,128)(2,1)S(1)}, bf16[1,2,256,384]{3,2,1,0:T(8,128)(2,1)S(1)}, u32[]{:S(2)}, u32[]{:S(2)}) %collective-permute-start.15) | collective-permute-done | bytes 393248 | tf_op jit(solution)/shard_map/ppermute | solution.py:452
  171.0 1.2 put.3
  (50 shorter events, 0.7 us)
Async XLA Ops:
  7.2 2.1 %copy-start.4 = (bf16[128,2048]{1,0:T(8,128)(2,1)S(1)}, bf16[128,2048]{1,0:T(8,128)(2,1)}, u32[]{:S(2)}) copy-start(bf16[128,2048]{1,0:T(8,128)(2,1)} %refs_0_.1) | copy-start | bytes 1572868
  7.2 63.9 %all-gather.2.cloned.1.call-start = ((), (), s32[]{:S(2)}) async-start(), calls=%async_computation.1 | async-start | bytes 5013504 | tf_op jit(solution)/shard_map/all_gather | solution.py:271
  9.3 156.3 %reduce-scatter.2.cloned.1.call-start = ((), (), s32[]{:S(2)}) async-start(), calls=%async_computation.2 | async-start | bytes 5013504 | tf_op jit(solution)/shard_map/reduce_scatter | solution.py:436
  9.3 5.0 %collective-permute-start = (bf16[128,2048]{1,0:T(8,128)(2,1)S(1)}, bf16[128,2048]{1,0:T(8,128)(2,1)S(1)}, u32[]{:S(2)}, u32[]{:S(2)}) collective-permute-start(bf16[128,2048]{1,0:T(8,128)(2,1)S(1)} %copy-done.4), channel_id=1, source_target_pairs={{0,1},{1,0},{2,3},{3,2},{4,5},{5,4},{6,7},{7,6},{8,9},{9,8},{10,11... | collective-permute-start | bytes 1572872 | tf_op jit(solution)/shard_map/ppermute | solution.py:278
  9.8 15.4 %collective-permute-start.1 = (bf16[128,2048]{1,0:T(8,128)(2,1)S(1)}, bf16[128,2048]{1,0:T(8,128)(2,1)S(1)}, u32[]{:S(2)}, u32[]{:S(2)}) collective-permute-start(bf16[128,2048]{1,0:T(8,128)(2,1)S(1)} %copy-done.4), channel_id=1, source_target_pairs={{0,2},{2,4},{3,1},{4,6},{5,3},{7,5},{8,10},{10,12},{11,9},{12,14},... | collective-permute-start | bytes 1572872 | tf_op jit(solution)/shard_map/ppermute | solution.py:278
  14.4 10.9 %copy-start.5 = (bf16[128,2048]{1,0:T(8,128)(2,1)}, bf16[128,2048]{1,0:T(8,128)(2,1)S(1)}, u32[]{:S(2)}) copy-start(bf16[128,2048]{1,0:T(8,128)(2,1)S(1)} %collective-permute-done.refs_1_) | copy-start | bytes 1572868
  14.4 22.9 %collective-permute-start.2 = (bf16[128,2048]{1,0:T(8,128)(2,1)S(1)}, bf16[128,2048]{1,0:T(8,128)(2,1)S(1)}, u32[]{:S(2)}, u32[]{:S(2)}) collective-permute-start(bf16[128,2048]{1,0:T(8,128)(2,1)S(1)} %collective-permute-done.refs_1_), channel_id=1, source_target_pairs={{0,2},{2,4},{3,1},{4,6},{5,3},{7,5},{8,10},{10,12},{11,9},{12,14},... | collective-permute-start | bytes 1572872 | tf_op jit(solution)/shard_map/ppermute | solution.py:278
  25.3 56.2 %copy-start.6 = (bf16[128,2048]{1,0:T(8,128)(2,1)}, bf16[128,2048]{1,0:T(8,128)(2,1)S(1)}, u32[]{:S(2)}) copy-start(bf16[128,2048]{1,0:T(8,128)(2,1)S(1)} %collective-permute-done.1.refs_2_) | copy-start | bytes 1572868
  25.3 15.3 %collective-permute-start.3 = (bf16[128,2048]{1,0:T(8,128)(2,1)S(1)}, bf16[128,2048]{1,0:T(8,128)(2,1)S(1)}, u32[]{:S(2)}, u32[]{:S(2)}) collective-permute-start(bf16[128,2048]{1,0:T(8,128)(2,1)S(1)} %collective-permute-done.1.refs_2_), channel_id=1, source_target_pairs={{2,4},{3,1},{4,6},{5,3},{10,12},{11,9},{12,14},{13,11},{18,20},{19... | collective-permute-start | bytes 1572872 | tf_op jit(solution)/shard_map/ppermute | solution.py:278
  37.3 44.2 %copy-start.7 = (bf16[128,2048]{1,0:T(8,128)(2,1)}, bf16[128,2048]{1,0:T(8,128)(2,1)S(1)}, u32[]{:S(2)}) copy-start(bf16[128,2048]{1,0:T(8,128)(2,1)S(1)} %collective-permute-done.2.refs_3_) | copy-start | bytes 1572868
  37.3 4.8 %collective-permute-start.4 = (bf16[128,2048]{1,0:T(8,128)(2,1)S(1)}, bf16[128,2048]{1,0:T(8,128)(2,1)S(1)}, u32[]{:S(2)}, u32[]{:S(2)}) collective-permute-start(bf16[128,2048]{1,0:T(8,128)(2,1)S(1)} %collective-permute-done.2.refs_3_), channel_id=1, source_target_pairs={{2,4},{3,1},{4,6},{5,3},{10,12},{11,9},{12,14},{13,11},{18,20},{19... | collective-permute-start | bytes 1572872 | tf_op jit(solution)/shard_map/ppermute | solution.py:278
  38.0 5.9 %collective-permute-start.7 = (bf16[128,2048]{1,0:T(8,128)(2,1)S(1)}, bf16[128,2048]{1,0:T(8,128)(2,1)S(1)}, u32[]{:S(2)}, u32[]{:S(2)}) collective-permute-start(bf16[128,2048]{1,0:T(8,128)(2,1)S(1)} %collective-permute-done.1.refs_2_), channel_id=1, source_target_pairs={{1,0},{2,3},{3,2},{4,5},{5,4},{6,7},{9,8},{10,11},{11,10},{12,13},... | collective-permute-start | bytes 1572872 | tf_op jit(solution)/shard_map/ppermute | solution.py:278
  39.3 6.0 %collective-permute-start.8 = (bf16[128,2048]{1,0:T(8,128)(2,1)S(1)}, bf16[128,2048]{1,0:T(8,128)(2,1)S(1)}, u32[]{:S(2)}, u32[]{:S(2)}) collective-permute-start(bf16[128,2048]{1,0:T(8,128)(2,1)S(1)} %collective-permute-done.2.refs_3_), channel_id=1, source_target_pairs={{1,0},{2,3},{3,2},{4,5},{5,4},{6,7},{9,8},{10,11},{11,10},{12,13},... | collective-permute-start | bytes 1572872 | tf_op jit(solution)/shard_map/ppermute | solution.py:278
  40.6 42.2 %copy-start.8 = (bf16[128,2048]{1,0:T(8,128)(2,1)}, bf16[128,2048]{1,0:T(8,128)(2,1)S(1)}, u32[]{:S(2)}) copy-start(bf16[128,2048]{1,0:T(8,128)(2,1)S(1)} %collective-permute-done.3.refs_4_) | copy-start | bytes 1572868
  40.6 43.5 %collective-permute-start.5 = (bf16[128,2048]{1,0:T(8,128)(2,1)S(1)}, bf16[128,2048]{1,0:T(8,128)(2,1)}, u32[]{:S(2)}, u32[]{:S(2)}) collective-permute-start(bf16[128,2048]{1,0:T(8,128)(2,1)S(1)} %collective-permute-done.3.refs_4_), channel_id=1, source_target_pairs={{3,1},{4,6},{11,9},{12,14},{19,17},{20,22},{27,25},{28,30}} | collective-permute-start | bytes 1572872 | tf_op jit(solution)/shard_map/ppermute | solution.py:278
  42.1 29.0 %copy-start.9 = (bf16[128,2048]{1,0:T(8,128)(2,1)}, bf16[128,2048]{1,0:T(8,128)(2,1)S(1)}, u32[]{:S(2)}) copy-start(bf16[128,2048]{1,0:T(8,128)(2,1)S(1)} %collective-permute-done.4.refs_2_.refs_5_) | copy-start | bytes 1572868
  42.1 42.0 %collective-permute-start.6 = (bf16[128,2048]{1,0:T(8,128)(2,1)S(1)}, bf16[128,2048]{1,0:T(8,128)(2,1)}, u32[]{:S(2)}, u32[]{:S(2)}) collective-permute-start(bf16[128,2048]{1,0:T(8,128)(2,1)S(1)} %collective-permute-done.4.refs_2_.refs_5_), channel_id=1, source_target_pairs={{3,1},{4,6},{11,9},{12,14},{19,17},{20,22},{27,25},{28,30}} | collective-permute-start | bytes 1572872 | tf_op jit(solution)/shard_map/ppermute | solution.py:278
  43.9 27.2 %copy-start.10 = (bf16[128,2048]{1,0:T(8,128)(2,1)}, bf16[128,2048]{1,0:T(8,128)(2,1)S(1)}, u32[]{:S(2)}) copy-start(bf16[128,2048]{1,0:T(8,128)(2,1)S(1)} %collective-permute-done.7.refs_0_.refs_8_) | copy-start | bytes 1572868
  45.3 25.8 %copy-start.11 = (bf16[128,2048]{1,0:T(8,128)(2,1)}, bf16[128,2048]{1,0:T(8,128)(2,1)S(1)}, u32[]{:S(2)}) copy-start(bf16[128,2048]{1,0:T(8,128)(2,1)S(1)} %collective-permute-done.8.refs_1_.refs_9_) | copy-start | bytes 1572868
  81.5 7.9 %collective-permute-start.10 = (bf16[128,2048]{1,0:T(8,128)(2,1)}, bf16[128,2048]{1,0:T(8,128)(2,1)S(1)}, u32[]{:S(2)}, u32[]{:S(2)}) collective-permute-start(bf16[128,2048]{1,0:T(8,128)(2,1)} %copy-done.9), channel_id=1, source_target_pairs={{1,0},{3,2},{4,5},{6,7},{9,8},{11,10},{12,13},{14,15},{17,16},{19,... | collective-permute-start | bytes 1572872 | tf_op jit(solution)/shard_map/ppermute | solution.py:278
  82.8 7.7 %collective-permute-start.9 = (bf16[128,2048]{1,0:T(8,128)(2,1)S(1)}, bf16[128,2048]{1,0:T(8,128)(2,1)S(1)}, u32[]{:S(2)}, u32[]{:S(2)}) collective-permute-start(bf16[128,2048]{1,0:T(8,128)(2,1)S(1)} %collective-permute-done.3.refs_4_), channel_id=1, source_target_pairs={{1,0},{3,2},{4,5},{6,7},{9,8},{11,10},{12,13},{14,15},{17,16},{19,... | collective-permute-start | bytes 1572872 | tf_op jit(solution)/shard_map/ppermute | solution.py:278
  84.1 7.9 %collective-permute-start.12 = (bf16[128,2048]{1,0:T(8,128)(2,1)}, bf16[128,2048]{1,0:T(8,128)(2,1)S(1)}, u32[]{:S(2)}, u32[]{:S(2)}) collective-permute-start(bf16[128,2048]{1,0:T(8,128)(2,1)} %collective-permute-done.6.refs_7_), channel_id=1, source_target_pairs={{1,0},{6,7},{9,8},{14,15},{17,16},{22,23},{25,24},{30,31}} | collective-permute-start | bytes 1572872 | tf_op jit(solution)/shard_map/ppermute | solution.py:278
  85.4 8.0 %collective-permute-start.11 = (bf16[128,2048]{1,0:T(8,128)(2,1)}, bf16[128,2048]{1,0:T(8,128)(2,1)S(1)}, u32[]{:S(2)}, u32[]{:S(2)}) collective-permute-start(bf16[128,2048]{1,0:T(8,128)(2,1)} %collective-permute-done.5.refs_6_), channel_id=1, source_target_pairs={{1,0},{6,7},{9,8},{14,15},{17,16},{22,23},{25,24},{30,31}} | collective-permute-start | bytes 1572872 | tf_op jit(solution)/shard_map/ppermute | solution.py:278
  89.3 4.0 %copy-start.12 = (bf16[128,2048]{1,0:T(8,128)(2,1)}, bf16[128,2048]{1,0:T(8,128)(2,1)S(1)}, u32[]{:S(2)}) copy-start(bf16[128,2048]{1,0:T(8,128)(2,1)S(1)} %collective-permute-done.10.refs_11_) | copy-start | bytes 1572868
  90.5 2.9 %copy-start.13 = (bf16[128,2048]{1,0:T(8,128)(2,1)}, bf16[128,2048]{1,0:T(8,128)(2,1)S(1)}, u32[]{:S(2)}) copy-start(bf16[128,2048]{1,0:T(8,128)(2,1)S(1)} %collective-permute-done.9.refs_10_) | copy-start | bytes 1572868
  92.0 1.3 copy-start.14
  93.4 0.8 copy-start.15
  116.0 20.7 %collective-permute-start.17 = (bf16[2,2,256,384]{3,2,1,0:T(8,128)(2,1)}, bf16[2,2,256,384]{3,2,1,0:T(8,128)(2,1)S(1)}, u32[]{:S(2)}, u32[]{:S(2)}) collective-permute-start(bf16[2,2,256,384]{3,2,1,0:T(8,128)(2,1)} %get-tuple-element.60), channel_id=1, source_target_pairs={{0,8},{8,0},{16,24},{24,16},{1,9},{9,1},{17,25},{25,17},{2,10},{10... | collective-permute-start | bytes 2359304 | tf_op jit(solution)/shard_map/ppermute | solution.py:404
  117.8 18.9 %copy-start.3 = (bf16[2,2,256,384]{3,2,1,0:T(8,128)(2,1)S(1)}, bf16[2,2,256,384]{3,2,1,0:T(8,128)(2,1)}, u32[]{:S(2)}) copy-start(bf16[2,2,256,384]{3,2,1,0:T(8,128)(2,1)} %get-tuple-element.59) | copy-start | bytes 2359300
  117.8 21.0 %collective-permute-start.19 = (bf16[2,2,256,384]{3,2,1,0:T(8,128)(2,1)}, bf16[2,2,256,384]{3,2,1,0:T(8,128)(2,1)S(1)}, u32[]{:S(2)}, u32[]{:S(2)}) collective-permute-start(bf16[2,2,256,384]{3,2,1,0:T(8,128)(2,1)} %get-tuple-element.62), channel_id=1, source_target_pairs={{0,16},{8,24},{16,0},{24,8},{1,17},{9,25},{17,1},{25,9},{2,18},{10... | collective-permute-start | bytes 2359304 | tf_op jit(solution)/shard_map/ppermute | solution.py:404
  125.2 28.4 %collective-permute-start.13 = (bf16[2,2,256,384]{3,2,1,0:T(8,128)(2,1)}, bf16[2,2,256,384]{3,2,1,0:T(8,128)(2,1)S(1)}, u32[]{:S(2)}, u32[]{:S(2)}) collective-permute-start(bf16[2,2,256,384]{3,2,1,0:T(8,128)(2,1)} %get-tuple-element.52), channel_id=1, source_target_pairs={{0,8},{8,0},{16,24},{24,16},{1,9},{9,1},{17,25},{25,17},{2,10},{10... | collective-permute-start | bytes 2359304 | tf_op jit(solution)/shard_map/ppermute | solution.py:404
  125.9 29.7 %collective-permute-start.14 = (bf16[2,2,256,384]{3,2,1,0:T(8,128)(2,1)}, bf16[2,2,256,384]{3,2,1,0:T(8,128)(2,1)S(1)}, u32[]{:S(2)}, u32[]{:S(2)}) collective-permute-start(bf16[2,2,256,384]{3,2,1,0:T(8,128)(2,1)} %get-tuple-element.54), channel_id=1, source_target_pairs={{0,16},{8,24},{16,0},{24,8},{1,17},{9,25},{17,1},{25,9},{2,18},{10... | collective-permute-start | bytes 2359304 | tf_op jit(solution)/shard_map/ppermute | solution.py:404
  136.7 2.0 %copy-start.2 = (bf16[2,2,256,384]{3,2,1,0:T(8,128)(2,1)S(1)}, bf16[2,2,256,384]{3,2,1,0:T(8,128)(2,1)}, u32[]{:S(2)}) copy-start(bf16[2,2,256,384]{3,2,1,0:T(8,128)(2,1)} %get-tuple-element.61) | copy-start | bytes 2359300
  137.0 26.7 %collective-permute-start.18 = (bf16[1,2,256,384]{3,2,1,0:T(8,128)(2,1)S(1)}, bf16[1,2,256,384]{3,2,1,0:T(8,128)(2,1)S(1)}, u32[]{:S(2)}, u32[]{:S(2)}) collective-permute-start(bf16[1,2,256,384]{3,2,1,0:T(8,128)(2,1)S(1)} %get-tuple-element.65), channel_id=1, source_target_pairs={{0,16},{8,24},{16,0},{24,8},{1,17},{9,25},{17,1},{25,9},{2,18},{10... | collective-permute-start | bytes 1179656 | tf_op jit(solution)/shard_map/ppermute | solution.py:452
  138.7 14.8 %copy-start.1 = (bf16[2,2,256,384]{3,2,1,0:T(8,128)(2,1)S(1)}, bf16[2,2,256,384]{3,2,1,0:T(8,128)(2,1)}, u32[]{:S(2)}) copy-start(bf16[2,2,256,384]{3,2,1,0:T(8,128)(2,1)} %get-tuple-element.51) | copy-start | bytes 2359300
  139.0 24.7 %collective-permute-start.20 = (bf16[1,2,256,384]{3,2,1,0:T(8,128)(2,1)S(1)}, bf16[1,2,256,384]{3,2,1,0:T(8,128)(2,1)S(1)}, u32[]{:S(2)}, u32[]{:S(2)}) collective-permute-start(bf16[1,2,256,384]{3,2,1,0:T(8,128)(2,1)S(1)} %get-tuple-element.63), channel_id=1, source_target_pairs={{0,8},{8,0},{16,24},{24,16},{1,9},{9,1},{17,25},{25,17},{2,10},{10... | collective-permute-start | bytes 1179656 | tf_op jit(solution)/shard_map/ppermute | solution.py:452
  153.6 2.0 %copy-start = (bf16[2,2,256,384]{3,2,1,0:T(8,128)(2,1)S(1)}, bf16[2,2,256,384]{3,2,1,0:T(8,128)(2,1)}, u32[]{:S(2)}) copy-start(bf16[2,2,256,384]{3,2,1,0:T(8,128)(2,1)} %get-tuple-element.53) | copy-start | bytes 2359300
  153.9 17.1 %collective-permute-start.15 = (bf16[1,2,256,384]{3,2,1,0:T(8,128)(2,1)S(1)}, bf16[1,2,256,384]{3,2,1,0:T(8,128)(2,1)S(1)}, u32[]{:S(2)}, u32[]{:S(2)}) collective-permute-start(bf16[1,2,256,384]{3,2,1,0:T(8,128)(2,1)S(1)} %get-tuple-element.69), channel_id=1, source_target_pairs={{0,16},{8,24},{16,0},{24,8},{1,17},{9,25},{17,1},{25,9},{2,18},{10... | collective-permute-start | bytes 1179656 | tf_op jit(solution)/shard_map/ppermute | solution.py:452
  155.9 15.1 %collective-permute-start.16 = (bf16[1,2,256,384]{3,2,1,0:T(8,128)(2,1)S(1)}, bf16[1,2,256,384]{3,2,1,0:T(8,128)(2,1)S(1)}, u32[]{:S(2)}, u32[]{:S(2)}) collective-permute-start(bf16[1,2,256,384]{3,2,1,0:T(8,128)(2,1)S(1)} %get-tuple-element.67), channel_id=1, source_target_pairs={{0,8},{8,0},{16,24},{24,16},{1,9},{9,1},{17,25},{25,17},{2,10},{10... | collective-permute-start | bytes 1179656 | tf_op jit(solution)/shard_map/ppermute | solution.py:452
Sparse Core Ops, SparseCore 0:
  10.2 60.8 all-gather.1
  110.5 55.0 reduce-scatter.1

commit v18 on v17

--- a/solution.py
+++ b/solution.py
@@ -72,8 +72,7 @@
     return copies
 
 
-def up_kernel(groups, width, top, cap, after, place, x_all, w_up, *refs):
-    refs = refs[after:]
+def up_kernel(groups, width, top, cap, place, x_all, w_up, *refs):
     pick_out, meta, hid_out, scaled_out, slope_out, rows, w_v, held, gates, pick, hid, scaled, slope, sems, out_sem = refs
     experts, members = held.shape[0], rows.shape[1]
     arrive = copy_all([(x_all.at[pl.ds(g * members, members), :], rows.at[g]) for g in range(groups)], sems.at[0])
@@ -318,8 +317,12 @@
     dy_mine[0][0], w_flip = lax.optimization_barrier((dy_mine[0][0], w_flip))
     for step in range(2, groups - 1):
         dy_mine.append([hop(part, lines[step]) for part in dy_mine[-1]])
-    dy_mine.append([hop(part, lines[-1]) for part in dy_mine[-1]])
     dy_other = [[hop(part, swaps[1]) for part in dy_mine[0]]]
+    dy_mine[1][0], dy_other[0] = lax.optimization_barrier((dy_mine[1][0], dy_other[0]))
+    early_swap = hop(dy_mine[1][0], swaps[2])
+    own_last, other_last = dy_mine[-1]
+    other_last, early_swap = lax.optimization_barrier((other_last, early_swap))
+    dy_mine.append([hop(own_last, lines[-1]), hop(other_last, lines[-1])])
 
     act = shape(experts, routes, hidden)
     pick_flops = 2 * total * experts * cap * width
@@ -340,13 +343,13 @@
             name=name,
         )
 
-    up_after = dy_other[0] + dy_mine[-2][1:]
+    x_all, other_last = lax.optimization_barrier((x_all, other_last))
     pick, meta, hid, scaled, slope_g = one(
-        functools.partial(up_kernel, groups, width, top, cap, len(up_after)),
+        functools.partial(up_kernel, groups, width, top, cap),
         "up",
         pick_flops + main_flops,
         2 * total * full + row_bytes,
-        [SMEM, ANY, ANY] + [ANY] * len(up_after),
+        [SMEM, ANY, ANY],
         [ANY, pl.BlockSpec(memory_space=pltpu.VMEM), ANY, ANY, ANY],
         [shape(groups, experts * cap, members), shape(total, LANES), act, act, act],
         [
@@ -361,10 +364,13 @@
             pltpu.SemaphoreType.DMA((2, most)),
             pltpu.SemaphoreType.DMA((4, experts)),
         ],
-    )(place, x_all, w_up, *up_after)
+    )(place, x_all, w_up)
     for row, swap in zip(dy_mine[1:], swaps[2:]):
         dy_other.append([])
-        for part in row:
+        for n, part in enumerate(row):
+            if len(dy_other) == 2 and n == 0:
+                dy_other[-1].append(early_swap)
+                continue
             part, hid = lax.optimization_barrier((part, hid))
             dy_other[-1].append(hop(part, swap))
     blocks = [part for row in [dy_own] + dy_mine + dy_other for part in row]

time: 180 us -> 178 us (0.989)
  waiting for transfers between devices: 79.1 us -> 76.8 us
    all_gather x1, waiting for transfers between devices: 25.8 us -> 0.01 us  [shards(): x_all = lax.all_gather(x_own, 'ep', axis=0, tiled=True)]
    ppermute x13, waiting for transfers between devices: 19.6 us -> 43 us  [hop(): return lax.ppermute(value, 'ep', pairs)]
  transfers between devices with their start and end apart: 23 -> 23, of which waited for: 13 -> 11; matrix products, arithmetic and copies ran while one was open for 1% -> 1% of each run, Pallas kernels for 18% -> 18%
where the time goes in v18:
time: 178 us
  waiting for transfers between devices  76.8 us (43%)
  Pallas kernels  51.2 us (29%)
  starting transfers between devices  31.9 us (18%)
  between operations  14.4 us (8%)
  local copies, waits for them, and re-layouts  2 us (1%)
    ppermute x13, waiting for transfers between devices, hop(): return lax.ppermute(value, 'ep', pairs)  43 us
    ppermute x4, waiting for transfers between devices, exchange(): got = lax.ppermute(send, 'dp', [(i, i ^ bit) for i in range(dp_count)])  23.4 us
    ppermute x13, starting transfers between devices, hop(): return lax.ppermute(value, 'ep', pairs)  20.8 us
    pallas_call x1, Pallas kernels, shards(): one(functools.partial(tail_kernel, groups, cap, width, top), 'tail', 8 *...  16.2 us
    pallas_call x2, Pallas kernels, down(): one(functools.partial(down_kernel, orders, start), 'down', 16 * main_flop...  11.5 us
    pallas_call x1, Pallas kernels, shards(): one(functools.partial(up_kernel, groups, width, top, cap), 'up', pick_flo...  10.4 us
    ppermute x4, waiting for transfers between devices, shards(): lax.ppermute(send, 'dp', [(i, i ^ 1 << (g + last) % bits) for i in range(...  9.71 us
    pallas_call x1, Pallas kernels, shards(): call(flip_kernel, 'flip', experts, 0, 2 * row_bytes, in_specs=[SMEM, pl.B...  6.78 us
  transfers between devices with their start and end apart: 23, of which 11 were waited for; matrix products, arithmetic and copies ran while one was open for 1% of the time, Pallas kernels for 18%

profile of v18, /device:TPU:0, one launch (start us, length us, event | category | flops | bytes accessed | tf_op | source)
XLA Modules:
  0.0 177.6 jit_solution(4921660138717281103)
XLA Ops:
  7.2 2.0 %pack.1 = bf16[128,2176]{1,0:T(8,128)(2,1)} custom-call(bf16[128,2048]{1,0:T(8,128)(2,1)} %tokens.1, s32[8,128]{1,0:T(8,128)} %bitcast.7, bf16[8,128]{1,0:T(8,128)(2,1)} %bitcast.8), custom_call_target="tpu_custom_call" | custom-call | bytes 1048576 | tf_op jit(solution)/shard_map/pack/pallas_call | solution.py:263
  9.3 0.5 collective-permute-start
  9.8 4.5 %collective-permute-start.1 = (bf16[128,2048]{1,0:T(8,128)(2,1)S(1)}, bf16[128,2048]{1,0:T(8,128)(2,1)S(1)}, u32[]{:S(2)}, u32[]{:S(2)}) collective-permute-start(bf16[128,2048]{1,0:T(8,128)(2,1)S(1)} %copy-done.4), channel_id=1, source_target_pairs={{0,2},{2,4},{3,1},{4,6},{5,3},{7,5},{8,10},{10,12},{11,9},{12,14},... | collective-permute-start | bytes 1572872 | tf_op jit(solution)/shard_map/ppermute | solution.py:277
  14.4 3.5 %collective-permute-start.2 = (bf16[128,2048]{1,0:T(8,128)(2,1)S(1)}, bf16[128,2048]{1,0:T(8,128)(2,1)S(1)}, u32[]{:S(2)}, u32[]{:S(2)}) collective-permute-start(bf16[128,2048]{1,0:T(8,128)(2,1)S(1)} %collective-permute-done.refs_1_), channel_id=1, source_target_pairs={{0,2},{2,4},{3,1},{4,6},{5,3},{7,5},{8,10},{10,12},{11,9},{12,14},... | collective-permute-start | bytes 1572872 | tf_op jit(solution)/shard_map/ppermute | solution.py:277
  17.9 0.6 pad_add_fusion.place
  18.5 6.8 %flip.1.refs_16_ = bf16[4,384,2048]{2,1,0:T(8,128)(2,1)} custom-call(s32[4]{0:T(128)} %pad_add_fusion.place, bf16[4,2048,384]{2,1,0:T(8,128)(2,1)} %w_up.1), custom_call_target="tpu_custom_call" | custom-call | bytes 12582912 | tf_op jit(solution)/shard_map/flip/pallas_call | solution.py:296
  25.3 1.3 collective-permute-start.4
  26.6 0.7 collective-permute-start.3
  27.3 10.0 %collective-permute-done.2.refs_3_ = bf16[128,2048]{1,0:T(8,128)(2,1)S(1)} collective-permute-done((bf16[128,2048]{1,0:T(8,128)(2,1)S(1)}, bf16[128,2048]{1,0:T(8,128)(2,1)S(1)}, u32[]{:S(2)}, u32[]{:S(2)}) %collective-permute-start.2) | collective-permute-done | bytes 524320 | tf_op jit(solution)/shard_map/ppermute | solution.py:277
  37.3 1.3 collective-permute-start.5
  38.6 0.7 collective-permute-start.6
  39.4 3.2 %collective-permute-done.5.refs_9_ = bf16[128,2048]{1,0:T(8,128)(2,1)S(1)} collective-permute-done((bf16[128,2048]{1,0:T(8,128)(2,1)S(1)}, bf16[128,2048]{1,0:T(8,128)(2,1)S(1)}, u32[]{:S(2)}, u32[]{:S(2)}) %collective-permute-start.5) | collective-permute-done | bytes 524320 | tf_op jit(solution)/shard_map/ppermute | solution.py:277
  42.6 1.3 collective-permute-start.8
  43.9 1.5 collective-permute-start.7
  45.4 23.5 %collective-permute-done.8.refs_10_ = bf16[128,2048]{1,0:T(8,128)(2,1)S(1)} collective-permute-done((bf16[128,2048]{1,0:T(8,128)(2,1)S(1)}, bf16[128,2048]{1,0:T(8,128)(2,1)S(1)}, u32[]{:S(2)}, u32[]{:S(2)}) %collective-permute-start.8) | collective-permute-done | bytes 524320 | tf_op jit(solution)/shard_map/ppermute | solution.py:277
  68.9 0.8 copy-done.12
  69.7 1.5 collective-permute-start.9
  71.2 10.4 %up.1 = (bf16[4,320,256]{2,1,0:T(8,128)(2,1)}, bf16[1024,128]{1,0:T(8,128)(2,1)}, bf16[4,320,384]{2,1,0:T(8,128)(2,1)}, bf16[4,320,384]{2,1,0:T(8,128)(2,1)}, bf16[4,320,384]{2,1,0:T(8,128)(2,1)}) custom-call(s32[4]{0:T(128)} %pad_add_fusion.place, bf16[1024,2176]{1,0:T(8,128)(2,1)} %all-gather.2.cloned.1.call-done.x_all, bf16[4,2048,384]{2,1,0:T(8,128)(2,1)} %w_up.1), custom_call_target="tpu_custom_call" | custom-call | flops 3355443200 | bytes 10747904 | tf_op jit(solution)/shard_map/up/pallas_call | solution.py:347
  81.6 1.3 collective-permute-start.10
  82.9 1.3 collective-permute-start.12
  84.2 1.5 collective-permute-start.11
  85.7 3.3 %collective-permute-done.10.refs_11_ = bf16[128,2048]{1,0:T(8,128)(2,1)S(1)} collective-permute-done((bf16[128,2048]{1,0:T(8,128)(2,1)S(1)}, bf16[128,2048]{1,0:T(8,128)(2,1)S(1)}, u32[]{:S(2)}, u32[]{:S(2)}) %collective-permute-start.10) | collective-permute-done | bytes 524320 | tf_op jit(solution)/shard_map/ppermute | solution.py:277
  89.0 1.6 collective-permute-done.12.refs_13_
  90.6 1.3 collective-permute-done.11.refs_12_
  91.9 0.8 copy-done.15
  92.7 16.2 %tail.1 = (bf16[1024,2176]{1,0:T(8,128)(2,1)}, bf16[4,320,2048]{2,1,0:T(8,128)(2,1)}) custom-call(s32[4]{0:T(128)} %pad_add_fusion.place, bf16[128,2048]{1,0:T(8,128)(2,1)} %refs_0_.1, bf16[128,2048]{1,0:T(8,128)(2,1)} %copy-done.5, bf16[128,2048]{1,0:T(8,128)(2,1)} %copy-done.6, bf16[128,2048]{1,0:T(8,128)(2,1)} %copy-done.7, bf16[128,2048]{1,0:T(8,128)(2,1)} %copy-done.9, ...), custom_call_target="tpu_custom_call" | custom-call | flops 16106127360 | bytes 25165824 | tf_op jit(solution)/shard_map/tail/pallas_call | solution.py:418
  109.0 5.6 %down.3 = (bf16[2,2,256,384]{3,2,1,0:T(8,128)(2,1)}, bf16[2,2,256,384]{3,2,1,0:T(8,128)(2,1)}, bf16[2,2,256,384]{3,2,1,0:T(8,128)(2,1)}, bf16[2,2,256,384]{3,2,1,0:T(8,128)(2,1)}) custom-call(s32[4]{0:T(128)} %pad_add_fusion.place, bf16[4,320,2048]{2,1,0:T(8,128)(2,1)} %get-tuple-element.57.kept, bf16[4,320,384]{2,1,0:T(8,128)(2,1)} %get-tuple-element.58.scaled_in), custom_call_target="tpu_custom_call" | custom-call | flops 32212254720 | bytes 50331648 | tf_op jit(solution)/shard_map/down/pallas_call | solution.py:388
  114.6 1.7 collective-permute-start.17
  116.3 1.5 collective-permute-start.19
  117.9 5.9 %down.2 = (bf16[2,2,256,384]{3,2,1,0:T(8,128)(2,1)}, bf16[2,2,256,384]{3,2,1,0:T(8,128)(2,1)}, bf16[2,2,256,384]{3,2,1,0:T(8,128)(2,1)}, bf16[2,2,256,384]{3,2,1,0:T(8,128)(2,1)}) custom-call(s32[4]{0:T(128)} %pad_add_fusion.place, bf16[4,320,2048]{2,1,0:T(8,128)(2,1)} %get-tuple-element.57.kept, bf16[4,320,384]{2,1,0:T(8,128)(2,1)} %get-tuple-element.58.scaled_in), custom_call_target="tpu_custom_call" | custom-call | flops 32212254720 | bytes 50331648 | tf_op jit(solution)/shard_map/down/pallas_call | solution.py:388
  123.7 0.8 collective-permute-start.13
  124.5 0.4 collective-permute-start.14
  124.9 10.4 %collective-permute-done.17 = bf16[2,2,256,384]{3,2,1,0:T(8,128)(2,1)S(1)} collective-permute-done((bf16[2,2,256,384]{3,2,1,0:T(8,128)(2,1)}, bf16[2,2,256,384]{3,2,1,0:T(8,128)(2,1)S(1)}, u32[]{:S(2)}, u32[]{:S(2)}) %collective-permute-start.17) | collective-permute-done | bytes 786464 | tf_op jit(solution)/shard_map/ppermute | solution.py:410
  135.3 0.2 add_convert_fusion.1
  135.6 1.7 collective-permute-start.18
  137.3 0.2 add_convert_fusion
  137.6 1.6 collective-permute-start.20
  139.2 13.0 %collective-permute-done.13 = bf16[2,2,256,384]{3,2,1,0:T(8,128)(2,1)S(1)} collective-permute-done((bf16[2,2,256,384]{3,2,1,0:T(8,128)(2,1)}, bf16[2,2,256,384]{3,2,1,0:T(8,128)(2,1)S(1)}, u32[]{:S(2)}, u32[]{:S(2)}) %collective-permute-start.13) | collective-permute-done | bytes 786464 | tf_op jit(solution)/shard_map/ppermute | solution.py:410
  152.1 0.2 add_convert_fusion.3
  152.4 1.7 collective-permute-start.15
  154.2 0.2 add_convert_fusion.2
  154.4 1.6 collective-permute-start.16
  156.0 6.2 %collective-permute-done.18.refs_1_ = bf16[1,2,256,384]{3,2,1,0:T(8,128)(2,1)S(1)} collective-permute-done((bf16[1,2,256,384]{3,2,1,0:T(8,128)(2,1)S(1)}, bf16[1,2,256,384]{3,2,1,0:T(8,128)(2,1)S(1)}, u32[]{:S(2)}, u32[]{:S(2)}) %collective-permute-start.18) | collective-permute-done | bytes 393248 | tf_op jit(solution)/shard_map/ppermute | solution.py:458
  162.2 1.2 put.2.refs_4_
  163.5 0.7 reduce-scatter.2.cloned.1.call-done.rows
  164.2 1.9 %finish.1 = (bf16[128,2048]{1,0:T(8,128)(2,1)}, bf16[8,128]{1,0:T(8,128)(2,1)}) custom-call(bf16[128,2176]{1,0:T(8,128)(2,1)} %reduce-scatter.2.cloned.1.call-done.rows), custom_call_target="tpu_custom_call" | custom-call | bytes 1048576 | tf_op jit(solution)/shard_map/finish/pallas_call | solution.py:443
  166.1 3.5 %collective-permute-done.15.refs_1_ = bf16[1,2,256,384]{3,2,1,0:T(8,128)(2,1)S(1)} collective-permute-done((bf16[1,2,256,384]{3,2,1,0:T(8,128)(2,1)S(1)}, bf16[1,2,256,384]{3,2,1,0:T(8,128)(2,1)S(1)}, u32[]{:S(2)}, u32[]{:S(2)}) %collective-permute-start.15) | collective-permute-done | bytes 393248 | tf_op jit(solution)/shard_map/ppermute | solution.py:458
  169.5 1.2 put.3
  (50 shorter events, 0.5 us)
Async XLA Ops:
  7.2 2.1 %copy-start.4 = (bf16[128,2048]{1,0:T(8,128)(2,1)S(1)}, bf16[128,2048]{1,0:T(8,128)(2,1)}, u32[]{:S(2)}) copy-start(bf16[128,2048]{1,0:T(8,128)(2,1)} %refs_0_.1) | copy-start | bytes 1572868
  7.2 64.0 %all-gather.2.cloned.1.call-start = ((), (), s32[]{:S(2)}) async-start(), calls=%async_computation.1 | async-start | bytes 5013504 | tf_op jit(solution)/shard_map/all_gather | solution.py:270
  9.3 154.9 %reduce-scatter.2.cloned.1.call-start = ((), (), s32[]{:S(2)}) async-start(), calls=%async_computation.2 | async-start | bytes 5013504 | tf_op jit(solution)/shard_map/reduce_scatter | solution.py:442
  9.3 5.0 %collective-permute-start = (bf16[128,2048]{1,0:T(8,128)(2,1)S(1)}, bf16[128,2048]{1,0:T(8,128)(2,1)S(1)}, u32[]{:S(2)}, u32[]{:S(2)}) collective-permute-start(bf16[128,2048]{1,0:T(8,128)(2,1)S(1)} %copy-done.4), channel_id=1, source_target_pairs={{0,1},{1,0},{2,3},{3,2},{4,5},{5,4},{6,7},{7,6},{8,9},{9,8},{10,11... | collective-permute-start | bytes 1572872 | tf_op jit(solution)/shard_map/ppermute | solution.py:277
  9.8 15.4 %collective-permute-start.1 = (bf16[128,2048]{1,0:T(8,128)(2,1)S(1)}, bf16[128,2048]{1,0:T(8,128)(2,1)S(1)}, u32[]{:S(2)}, u32[]{:S(2)}) collective-permute-start(bf16[128,2048]{1,0:T(8,128)(2,1)S(1)} %copy-done.4), channel_id=1, source_target_pairs={{0,2},{2,4},{3,1},{4,6},{5,3},{7,5},{8,10},{10,12},{11,9},{12,14},... | collective-permute-start | bytes 1572872 | tf_op jit(solution)/shard_map/ppermute | solution.py:277
  14.4 10.9 %copy-start.5 = (bf16[128,2048]{1,0:T(8,128)(2,1)}, bf16[128,2048]{1,0:T(8,128)(2,1)S(1)}, u32[]{:S(2)}) copy-start(bf16[128,2048]{1,0:T(8,128)(2,1)S(1)} %collective-permute-done.refs_1_) | copy-start | bytes 1572868
  14.4 22.9 %collective-permute-start.2 = (bf16[128,2048]{1,0:T(8,128)(2,1)S(1)}, bf16[128,2048]{1,0:T(8,128)(2,1)S(1)}, u32[]{:S(2)}, u32[]{:S(2)}) collective-permute-start(bf16[128,2048]{1,0:T(8,128)(2,1)S(1)} %collective-permute-done.refs_1_), channel_id=1, source_target_pairs={{0,2},{2,4},{3,1},{4,6},{5,3},{7,5},{8,10},{10,12},{11,9},{12,14},... | collective-permute-start | bytes 1572872 | tf_op jit(solution)/shard_map/ppermute | solution.py:277
  25.3 56.3 %copy-start.6 = (bf16[128,2048]{1,0:T(8,128)(2,1)}, bf16[128,2048]{1,0:T(8,128)(2,1)S(1)}, u32[]{:S(2)}) copy-start(bf16[128,2048]{1,0:T(8,128)(2,1)S(1)} %collective-permute-done.1.refs_2_) | copy-start | bytes 1572868
  25.3 14.0 %collective-permute-start.4 = (bf16[128,2048]{1,0:T(8,128)(2,1)S(1)}, bf16[128,2048]{1,0:T(8,128)(2,1)S(1)}, u32[]{:S(2)}, u32[]{:S(2)}) collective-permute-start(bf16[128,2048]{1,0:T(8,128)(2,1)S(1)} %collective-permute-done.1.refs_2_), channel_id=1, source_target_pairs={{1,0},{2,3},{3,2},{4,5},{5,4},{6,7},{9,8},{10,11},{11,10},{12,13},... | collective-permute-start | bytes 1572872 | tf_op jit(solution)/shard_map/ppermute | solution.py:277
  26.6 12.8 %collective-permute-start.3 = (bf16[128,2048]{1,0:T(8,128)(2,1)S(1)}, bf16[128,2048]{1,0:T(8,128)(2,1)S(1)}, u32[]{:S(2)}, u32[]{:S(2)}) collective-permute-start(bf16[128,2048]{1,0:T(8,128)(2,1)S(1)} %collective-permute-done.1.refs_2_), channel_id=1, source_target_pairs={{2,4},{3,1},{4,6},{5,3},{10,12},{11,9},{12,14},{13,11},{18,20},{19... | collective-permute-start | bytes 1572872 | tf_op jit(solution)/shard_map/ppermute | solution.py:277
  37.3 44.2 %copy-start.7 = (bf16[128,2048]{1,0:T(8,128)(2,1)}, bf16[128,2048]{1,0:T(8,128)(2,1)S(1)}, u32[]{:S(2)}) copy-start(bf16[128,2048]{1,0:T(8,128)(2,1)S(1)} %collective-permute-done.2.refs_3_) | copy-start | bytes 1572868
  37.3 5.3 %collective-permute-start.5 = (bf16[128,2048]{1,0:T(8,128)(2,1)S(1)}, bf16[128,2048]{1,0:T(8,128)(2,1)S(1)}, u32[]{:S(2)}, u32[]{:S(2)}) collective-permute-start(bf16[128,2048]{1,0:T(8,128)(2,1)S(1)} %collective-permute-done.2.refs_3_), channel_id=1, source_target_pairs={{1,0},{2,3},{3,2},{4,5},{5,4},{6,7},{9,8},{10,11},{11,10},{12,13},... | collective-permute-start | bytes 1572872 | tf_op jit(solution)/shard_map/ppermute | solution.py:277
  38.6 6.8 %collective-permute-start.6 = (bf16[128,2048]{1,0:T(8,128)(2,1)S(1)}, bf16[128,2048]{1,0:T(8,128)(2,1)S(1)}, u32[]{:S(2)}, u32[]{:S(2)}) collective-permute-start(bf16[128,2048]{1,0:T(8,128)(2,1)S(1)} %collective-permute-done.2.refs_3_), channel_id=1, source_target_pairs={{2,4},{3,1},{4,6},{5,3},{10,12},{11,9},{12,14},{13,11},{18,20},{19... | collective-permute-start | bytes 1572872 | tf_op jit(solution)/shard_map/ppermute | solution.py:277
  39.3 42.2 %copy-start.8 = (bf16[128,2048]{1,0:T(8,128)(2,1)}, bf16[128,2048]{1,0:T(8,128)(2,1)S(1)}, u32[]{:S(2)}) copy-start(bf16[128,2048]{1,0:T(8,128)(2,1)S(1)} %collective-permute-done.4.refs_8_) | copy-start | bytes 1572868
  39.3 42.2 %copy-start.9 = (bf16[128,2048]{1,0:T(8,128)(2,1)}, bf16[128,2048]{1,0:T(8,128)(2,1)S(1)}, u32[]{:S(2)}) copy-start(bf16[128,2048]{1,0:T(8,128)(2,1)S(1)} %collective-permute-done.3.refs_4_) | copy-start | bytes 1572868
  42.6 39.0 %copy-start.10 = (bf16[128,2048]{1,0:T(8,128)(2,1)}, bf16[128,2048]{1,0:T(8,128)(2,1)S(1)}, u32[]{:S(2)}) copy-start(bf16[128,2048]{1,0:T(8,128)(2,1)S(1)} %collective-permute-done.5.refs_9_) | copy-start | bytes 1572868
  42.6 26.3 %collective-permute-start.8 = (bf16[128,2048]{1,0:T(8,128)(2,1)S(1)}, bf16[128,2048]{1,0:T(8,128)(2,1)S(1)}, u32[]{:S(2)}, u32[]{:S(2)}) collective-permute-start(bf16[128,2048]{1,0:T(8,128)(2,1)S(1)} %collective-permute-done.3.refs_4_), channel_id=1, source_target_pairs={{1,0},{3,2},{4,5},{6,7},{9,8},{11,10},{12,13},{14,15},{17,16},{19,... | collective-permute-start | bytes 1572872 | tf_op jit(solution)/shard_map/ppermute | solution.py:277
  43.9 39.0 %collective-permute-start.7 = (bf16[128,2048]{1,0:T(8,128)(2,1)S(1)}, bf16[128,2048]{1,0:T(8,128)(2,1)}, u32[]{:S(2)}, u32[]{:S(2)}) collective-permute-start(bf16[128,2048]{1,0:T(8,128)(2,1)S(1)} %collective-permute-done.3.refs_4_), channel_id=1, source_target_pairs={{3,1},{4,6},{11,9},{12,14},{19,17},{20,22},{27,25},{28,30}} | collective-permute-start | bytes 1572872 | tf_op jit(solution)/shard_map/ppermute | solution.py:277
  45.4 36.2 %copy-start.11 = (bf16[128,2048]{1,0:T(8,128)(2,1)}, bf16[128,2048]{1,0:T(8,128)(2,1)S(1)}, u32[]{:S(2)}) copy-start(bf16[128,2048]{1,0:T(8,128)(2,1)S(1)} %collective-permute-done.6.refs_5_) | copy-start | bytes 1572868
  68.9 0.8 copy-start.12
  69.7 13.2 %collective-permute-start.9 = (bf16[128,2048]{1,0:T(8,128)(2,1)S(1)}, bf16[128,2048]{1,0:T(8,128)(2,1)}, u32[]{:S(2)}, u32[]{:S(2)}) collective-permute-start(bf16[128,2048]{1,0:T(8,128)(2,1)S(1)} %collective-permute-done.6.refs_5_), channel_id=1, source_target_pairs={{3,1},{4,6},{11,9},{12,14},{19,17},{20,22},{27,25},{28,30}} | collective-permute-start | bytes 1572872 | tf_op jit(solution)/shard_map/ppermute | solution.py:277
  81.6 7.4 %collective-permute-start.10 = (bf16[128,2048]{1,0:T(8,128)(2,1)S(1)}, bf16[128,2048]{1,0:T(8,128)(2,1)S(1)}, u32[]{:S(2)}, u32[]{:S(2)}) collective-permute-start(bf16[128,2048]{1,0:T(8,128)(2,1)S(1)} %collective-permute-done.6.refs_5_), channel_id=1, source_target_pairs={{1,0},{3,2},{4,5},{6,7},{9,8},{11,10},{12,13},{14,15},{17,16},{19,... | collective-permute-start | bytes 1572872 | tf_op jit(solution)/shard_map/ppermute | solution.py:277
  82.9 7.7 %collective-permute-start.12 = (bf16[128,2048]{1,0:T(8,128)(2,1)}, bf16[128,2048]{1,0:T(8,128)(2,1)S(1)}, u32[]{:S(2)}, u32[]{:S(2)}) collective-permute-start(bf16[128,2048]{1,0:T(8,128)(2,1)} %collective-permute-done.9.refs_7_), channel_id=1, source_target_pairs={{1,0},{6,7},{9,8},{14,15},{17,16},{22,23},{25,24},{30,31}} | collective-permute-start | bytes 1572872 | tf_op jit(solution)/shard_map/ppermute | solution.py:277
  84.2 7.7 %collective-permute-start.11 = (bf16[128,2048]{1,0:T(8,128)(2,1)}, bf16[128,2048]{1,0:T(8,128)(2,1)S(1)}, u32[]{:S(2)}, u32[]{:S(2)}) collective-permute-start(bf16[128,2048]{1,0:T(8,128)(2,1)} %collective-permute-done.7.refs_6_), channel_id=1, source_target_pairs={{1,0},{6,7},{9,8},{14,15},{17,16},{22,23},{25,24},{30,31}} | collective-permute-start | bytes 1572872 | tf_op jit(solution)/shard_map/ppermute | solution.py:277
  89.0 2.9 %copy-start.13 = (bf16[128,2048]{1,0:T(8,128)(2,1)}, bf16[128,2048]{1,0:T(8,128)(2,1)S(1)}, u32[]{:S(2)}) copy-start(bf16[128,2048]{1,0:T(8,128)(2,1)S(1)} %collective-permute-done.10.refs_11_) | copy-start | bytes 1572868
  90.6 1.3 copy-start.14
  91.9 0.8 copy-start.15
  114.6 20.7 %collective-permute-start.17 = (bf16[2,2,256,384]{3,2,1,0:T(8,128)(2,1)}, bf16[2,2,256,384]{3,2,1,0:T(8,128)(2,1)S(1)}, u32[]{:S(2)}, u32[]{:S(2)}) collective-permute-start(bf16[2,2,256,384]{3,2,1,0:T(8,128)(2,1)} %get-tuple-element.68), channel_id=1, source_target_pairs={{0,8},{8,0},{16,24},{24,16},{1,9},{9,1},{17,25},{25,17},{2,10},{10... | collective-permute-start | bytes 2359304 | tf_op jit(solution)/shard_map/ppermute | solution.py:410
  116.3 18.9 %copy-start.3 = (bf16[2,2,256,384]{3,2,1,0:T(8,128)(2,1)S(1)}, bf16[2,2,256,384]{3,2,1,0:T(8,128)(2,1)}, u32[]{:S(2)}) copy-start(bf16[2,2,256,384]{3,2,1,0:T(8,128)(2,1)} %get-tuple-element.67) | copy-start | bytes 2359300
  116.3 21.0 %collective-permute-start.19 = (bf16[2,2,256,384]{3,2,1,0:T(8,128)(2,1)}, bf16[2,2,256,384]{3,2,1,0:T(8,128)(2,1)S(1)}, u32[]{:S(2)}, u32[]{:S(2)}) collective-permute-start(bf16[2,2,256,384]{3,2,1,0:T(8,128)(2,1)} %get-tuple-element.70), channel_id=1, source_target_pairs={{0,16},{8,24},{16,0},{24,8},{1,17},{9,25},{17,1},{25,9},{2,18},{10... | collective-permute-start | bytes 2359304 | tf_op jit(solution)/shard_map/ppermute | solution.py:410
  123.7 28.4 %collective-permute-start.13 = (bf16[2,2,256,384]{3,2,1,0:T(8,128)(2,1)}, bf16[2,2,256,384]{3,2,1,0:T(8,128)(2,1)S(1)}, u32[]{:S(2)}, u32[]{:S(2)}) collective-permute-start(bf16[2,2,256,384]{3,2,1,0:T(8,128)(2,1)} %get-tuple-element.60), channel_id=1, source_target_pairs={{0,8},{8,0},{16,24},{24,16},{1,9},{9,1},{17,25},{25,17},{2,10},{10... | collective-permute-start | bytes 2359304 | tf_op jit(solution)/shard_map/ppermute | solution.py:410
  124.5 29.7 %collective-permute-start.14 = (bf16[2,2,256,384]{3,2,1,0:T(8,128)(2,1)}, bf16[2,2,256,384]{3,2,1,0:T(8,128)(2,1)S(1)}, u32[]{:S(2)}, u32[]{:S(2)}) collective-permute-start(bf16[2,2,256,384]{3,2,1,0:T(8,128)(2,1)} %get-tuple-element.62), channel_id=1, source_target_pairs={{0,16},{8,24},{16,0},{24,8},{1,17},{9,25},{17,1},{25,9},{2,18},{10... | collective-permute-start | bytes 2359304 | tf_op jit(solution)/shard_map/ppermute | solution.py:410
  135.3 2.0 %copy-start.2 = (bf16[2,2,256,384]{3,2,1,0:T(8,128)(2,1)S(1)}, bf16[2,2,256,384]{3,2,1,0:T(8,128)(2,1)}, u32[]{:S(2)}) copy-start(bf16[2,2,256,384]{3,2,1,0:T(8,128)(2,1)} %get-tuple-element.69) | copy-start | bytes 2359300
  135.6 26.7 %collective-permute-start.18 = (bf16[1,2,256,384]{3,2,1,0:T(8,128)(2,1)S(1)}, bf16[1,2,256,384]{3,2,1,0:T(8,128)(2,1)S(1)}, u32[]{:S(2)}, u32[]{:S(2)}) collective-permute-start(bf16[1,2,256,384]{3,2,1,0:T(8,128)(2,1)S(1)} %get-tuple-element.73), channel_id=1, source_target_pairs={{0,16},{8,24},{16,0},{24,8},{1,17},{9,25},{17,1},{25,9},{2,18},{10... | collective-permute-start | bytes 1179656 | tf_op jit(solution)/shard_map/ppermute | solution.py:458
  137.3 14.8 %copy-start.1 = (bf16[2,2,256,384]{3,2,1,0:T(8,128)(2,1)S(1)}, bf16[2,2,256,384]{3,2,1,0:T(8,128)(2,1)}, u32[]{:S(2)}) copy-start(bf16[2,2,256,384]{3,2,1,0:T(8,128)(2,1)} %get-tuple-element.59) | copy-start | bytes 2359300
  137.6 24.7 %collective-permute-start.20 = (bf16[1,2,256,384]{3,2,1,0:T(8,128)(2,1)S(1)}, bf16[1,2,256,384]{3,2,1,0:T(8,128)(2,1)S(1)}, u32[]{:S(2)}, u32[]{:S(2)}) collective-permute-start(bf16[1,2,256,384]{3,2,1,0:T(8,128)(2,1)S(1)} %get-tuple-element.71), channel_id=1, source_target_pairs={{0,8},{8,0},{16,24},{24,16},{1,9},{9,1},{17,25},{25,17},{2,10},{10... | collective-permute-start | bytes 1179656 | tf_op jit(solution)/shard_map/ppermute | solution.py:458
  152.1 2.0 %copy-start = (bf16[2,2,256,384]{3,2,1,0:T(8,128)(2,1)S(1)}, bf16[2,2,256,384]{3,2,1,0:T(8,128)(2,1)}, u32[]{:S(2)}) copy-start(bf16[2,2,256,384]{3,2,1,0:T(8,128)(2,1)} %get-tuple-element.61) | copy-start | bytes 2359300
  152.4 17.1 %collective-permute-start.15 = (bf16[1,2,256,384]{3,2,1,0:T(8,128)(2,1)S(1)}, bf16[1,2,256,384]{3,2,1,0:T(8,128)(2,1)S(1)}, u32[]{:S(2)}, u32[]{:S(2)}) collective-permute-start(bf16[1,2,256,384]{3,2,1,0:T(8,128)(2,1)S(1)} %get-tuple-element.77), channel_id=1, source_target_pairs={{0,16},{8,24},{16,0},{24,8},{1,17},{9,25},{17,1},{25,9},{2,18},{10... | collective-permute-start | bytes 1179656 | tf_op jit(solution)/shard_map/ppermute | solution.py:458
  154.4 15.1 %collective-permute-start.16 = (bf16[1,2,256,384]{3,2,1,0:T(8,128)(2,1)S(1)}, bf16[1,2,256,384]{3,2,1,0:T(8,128)(2,1)S(1)}, u32[]{:S(2)}, u32[]{:S(2)}) collective-permute-start(bf16[1,2,256,384]{3,2,1,0:T(8,128)(2,1)S(1)} %get-tuple-element.75), channel_id=1, source_target_pairs={{0,8},{8,0},{16,24},{24,16},{1,9},{9,1},{17,25},{25,17},{2,10},{10... | collective-permute-start | bytes 1179656 | tf_op jit(solution)/shard_map/ppermute | solution.py:458
Sparse Core Ops, SparseCore 0:
  10.2 60.8 all-gather.1
  109.1 55.0 reduce-scatter.1

commit v19 on v18

--- a/solution.py
+++ b/solution.py
@@ -22,13 +22,18 @@
     return lax.dot_general(a, b, dims, preferred_element_type=f32)
 
 
-def pack_kernel(top, tokens, ids, gates, x_out):
+def pack_kernel(top, tokens, ids, gates, x_out, extra, sem):
     count, width = tokens.shape
-    x_out[:, pl.ds(0, width)] = tokens[...]
+    rows = pltpu.make_async_copy(tokens, x_out.at[:, pl.ds(0, width)], sem.at[0])
+    rows.start()
     info = jnp.concatenate(
         [ids[...].astype(f32), gates[...].astype(f32), jnp.zeros((LANES - 2 * top, count), f32)], axis=0
     )
-    x_out[:, pl.ds(width, LANES)] = info.T.astype(bf16)
+    extra[...] = info.T.astype(bf16)
+    columns = pltpu.make_async_copy(extra, x_out.at[:, pl.ds(width, LANES)], sem.at[1])
+    columns.start()
+    rows.wait()
+    columns.wait()
 
 
 def flip_kernel(place, w, out):
@@ -179,7 +184,6 @@
         got = dot(pick[group], moved[slot]).astype(bf16)
         for b in range(experts):
             held[b, pl.ds(first, cap), :] = got[b * cap : (b + 1) * cap]
-    keep = copy_all([(held.at[b], kept.at[b]) for b in range(experts)], keep_sem)
     lane = lax.broadcasted_iota(jnp.int32, (groups * cap, LANES), 1)
     for b in range(experts):
         for load in loads[:3]:
@@ -193,6 +197,7 @@
         for g in range(groups):
             grads[g, pl.ds(b * cap, cap), pl.ds(0, width)] = route[g * cap : (g + 1) * cap]
             grads[g, pl.ds(b * cap, cap), pl.ds(width, LANES)] = gate[g * cap : (g + 1) * cap]
+    keep = copy_all([(held.at[b], kept.at[b]) for b in range(experts)], keep_sem)
     lane = lax.broadcasted_iota(jnp.int32, (members, LANES), 1)
     for g in range(groups):
         total = dot(pick[g], grads[g], FIRST)
@@ -262,7 +267,10 @@
 
     x_own = pl.pallas_call(
         functools.partial(pack_kernel, top),
+        in_specs=[ANY, VMEM, VMEM],
+        out_specs=ANY,
         out_shape=shape(tok_rows, full),
+        scratch_shapes=[pltpu.VMEM((tok_rows, LANES), bf16), pltpu.SemaphoreType.DMA((2,))],
         compiler_params=pltpu.CompilerParams(vmem_limit_bytes=VMEM_LIMIT),
         cost_estimate=cost(0, 4 * tok_rows * width),
         name="pack",

time: 178 us -> 195 us (1.096)
  Pallas kernels: 51.2 us -> 68.2 us
    pallas_call x1, Pallas kernels: 2.01 us -> 17.7 us  [shards(): pl.pallas_call(functools.partial(pack_kernel, top), in_specs=[ANY, VMEM,...]
  transfers between devices with their start and end apart: 23 -> 23, of which waited for: 11 -> 11; matrix products, arithmetic and copies ran while one was open for 1% -> 1% of each run, Pallas kernels for 18% -> 16%
where the time goes in v19:
time: 195 us
  waiting for transfers between devices  76.6 us (39%)
  Pallas kernels  68.2 us (35%)
  starting transfers between devices  32 us (16%)
  between operations  14.4 us (7%)
  local copies, waits for them, and re-layouts  2 us (1%)
    ppermute x13, waiting for transfers between devices, hop(): return lax.ppermute(value, 'ep', pairs)  43.1 us
    ppermute x4, waiting for transfers between devices, exchange(): got = lax.ppermute(send, 'dp', [(i, i ^ bit) for i in range(dp_count)])  23.2 us
    ppermute x13, starting transfers between devices, hop(): return lax.ppermute(value, 'ep', pairs)  20.8 us
    pallas_call x1, Pallas kernels, shards(): pl.pallas_call(functools.partial(pack_kernel, top), in_specs=[ANY, VMEM,...  17.7 us
    pallas_call x1, Pallas kernels, shards(): one(functools.partial(tail_kernel, groups, cap, width, top), 'tail', 8 *...  17.5 us
    pallas_call x2, Pallas kernels, down(): one(functools.partial(down_kernel, orders, start), 'down', 16 * main_flop...  11.5 us
    pallas_call x1, Pallas kernels, shards(): one(functools.partial(up_kernel, groups, width, top, cap), 'up', pick_flo...  10.4 us
    ppermute x4, waiting for transfers between devices, shards(): lax.ppermute(send, 'dp', [(i, i ^ 1 << (g + last) % bits) for i in range(...  9.87 us
  transfers between devices with their start and end apart: 23, of which 11 were waited for; matrix products, arithmetic and copies ran while one was open for 1% of the time, Pallas kernels for 16%

profile of v19, /device:TPU:0, one launch (start us, length us, event | category | flops | bytes accessed | tf_op | source)
XLA Modules:
  0.0 194.5 jit_solution(9431681492081887412)
XLA Ops:
  7.2 17.7 %pack.1 = bf16[128,2176]{1,0:T(8,128)(2,1)} custom-call(bf16[128,2048]{1,0:T(8,128)(2,1)} %tokens.1, s32[8,128]{1,0:T(8,128)} %bitcast.7, bf16[8,128]{1,0:T(8,128)(2,1)} %bitcast.8), custom_call_target="tpu_custom_call" | custom-call | bytes 1048576 | tf_op jit(solution)/shard_map/pack/pallas_call | solution.py:268
  25.1 0.5 collective-permute-start
  25.6 4.5 %collective-permute-start.1 = (bf16[128,2048]{1,0:T(8,128)(2,1)S(1)}, bf16[128,2048]{1,0:T(8,128)(2,1)S(1)}, u32[]{:S(2)}, u32[]{:S(2)}) collective-permute-start(bf16[128,2048]{1,0:T(8,128)(2,1)S(1)} %copy-done.4), channel_id=1, source_target_pairs={{0,2},{2,4},{3,1},{4,6},{5,3},{7,5},{8,10},{10,12},{11,9},{12,14},... | collective-permute-start | bytes 1572872 | tf_op jit(solution)/shard_map/ppermute | solution.py:285
  30.1 3.5 %collective-permute-start.2 = (bf16[128,2048]{1,0:T(8,128)(2,1)S(1)}, bf16[128,2048]{1,0:T(8,128)(2,1)S(1)}, u32[]{:S(2)}, u32[]{:S(2)}) collective-permute-start(bf16[128,2048]{1,0:T(8,128)(2,1)S(1)} %collective-permute-done.refs_1_), channel_id=1, source_target_pairs={{0,2},{2,4},{3,1},{4,6},{5,3},{7,5},{8,10},{10,12},{11,9},{12,14},... | collective-permute-start | bytes 1572872 | tf_op jit(solution)/shard_map/ppermute | solution.py:285
  33.6 0.6 pad_add_fusion.place
  34.2 6.8 %flip.1.refs_16_ = bf16[4,384,2048]{2,1,0:T(8,128)(2,1)} custom-call(s32[4]{0:T(128)} %pad_add_fusion.place, bf16[4,2048,384]{2,1,0:T(8,128)(2,1)} %w_up.1), custom_call_target="tpu_custom_call" | custom-call | bytes 12582912 | tf_op jit(solution)/shard_map/flip/pallas_call | solution.py:304
  41.0 1.3 collective-permute-start.4
  42.3 0.7 collective-permute-start.3
  43.0 11.7 %collective-permute-done.2.refs_3_ = bf16[128,2048]{1,0:T(8,128)(2,1)S(1)} collective-permute-done((bf16[128,2048]{1,0:T(8,128)(2,1)S(1)}, bf16[128,2048]{1,0:T(8,128)(2,1)S(1)}, u32[]{:S(2)}, u32[]{:S(2)}) %collective-permute-start.2) | collective-permute-done | bytes 524320 | tf_op jit(solution)/shard_map/ppermute | solution.py:285
  54.8 1.3 collective-permute-start.5
  56.0 0.7 collective-permute-start.6
  56.8 5.5 %collective-permute-done.5.refs_9_ = bf16[128,2048]{1,0:T(8,128)(2,1)S(1)} collective-permute-done((bf16[128,2048]{1,0:T(8,128)(2,1)S(1)}, bf16[128,2048]{1,0:T(8,128)(2,1)S(1)}, u32[]{:S(2)}, u32[]{:S(2)}) %collective-permute-start.5) | collective-permute-done | bytes 524320 | tf_op jit(solution)/shard_map/ppermute | solution.py:285
  62.3 1.3 collective-permute-start.8
  63.6 1.5 collective-permute-start.7
  65.1 21.3 %collective-permute-done.8.refs_10_ = bf16[128,2048]{1,0:T(8,128)(2,1)S(1)} collective-permute-done((bf16[128,2048]{1,0:T(8,128)(2,1)S(1)}, bf16[128,2048]{1,0:T(8,128)(2,1)S(1)}, u32[]{:S(2)}, u32[]{:S(2)}) %collective-permute-start.8) | collective-permute-done | bytes 524320 | tf_op jit(solution)/shard_map/ppermute | solution.py:285
  86.4 0.8 copy-done.12
  87.2 1.5 collective-permute-start.9
  88.6 10.4 %up.1 = (bf16[4,320,256]{2,1,0:T(8,128)(2,1)}, bf16[1024,128]{1,0:T(8,128)(2,1)}, bf16[4,320,384]{2,1,0:T(8,128)(2,1)}, bf16[4,320,384]{2,1,0:T(8,128)(2,1)}, bf16[4,320,384]{2,1,0:T(8,128)(2,1)}) custom-call(s32[4]{0:T(128)} %pad_add_fusion.place, bf16[1024,2176]{1,0:T(8,128)(2,1)} %all-gather.2.cloned.1.call-done.x_all, bf16[4,2048,384]{2,1,0:T(8,128)(2,1)} %w_up.1), custom_call_target="tpu_custom_call" | custom-call | flops 3355443200 | bytes 10747904 | tf_op jit(solution)/shard_map/up/pallas_call | solution.py:355
  99.1 1.3 collective-permute-start.10
  100.4 1.3 collective-permute-start.12
  101.7 1.5 collective-permute-start.11
  103.2 1.6 collective-permute-done.10.refs_11_
  104.8 1.6 collective-permute-done.12.refs_13_
  106.3 1.3 collective-permute-done.11.refs_12_
  107.7 0.8 copy-done.15
  108.5 17.5 %tail.1 = (bf16[1024,2176]{1,0:T(8,128)(2,1)}, bf16[4,320,2048]{2,1,0:T(8,128)(2,1)}) custom-call(s32[4]{0:T(128)} %pad_add_fusion.place, bf16[128,2048]{1,0:T(8,128)(2,1)} %refs_0_.1, bf16[128,2048]{1,0:T(8,128)(2,1)} %copy-done.5, bf16[128,2048]{1,0:T(8,128)(2,1)} %copy-done.6, bf16[128,2048]{1,0:T(8,128)(2,1)} %copy-done.7, bf16[128,2048]{1,0:T(8,128)(2,1)} %copy-done.9, ...), custom_call_target="tpu_custom_call" | custom-call | flops 16106127360 | bytes 25165824 | tf_op jit(solution)/shard_map/tail/pallas_call | solution.py:426
  126.0 5.6 %down.3 = (bf16[2,2,256,384]{3,2,1,0:T(8,128)(2,1)}, bf16[2,2,256,384]{3,2,1,0:T(8,128)(2,1)}, bf16[2,2,256,384]{3,2,1,0:T(8,128)(2,1)}, bf16[2,2,256,384]{3,2,1,0:T(8,128)(2,1)}) custom-call(s32[4]{0:T(128)} %pad_add_fusion.place, bf16[4,320,2048]{2,1,0:T(8,128)(2,1)} %get-tuple-element.57.kept, bf16[4,320,384]{2,1,0:T(8,128)(2,1)} %get-tuple-element.58.scaled_in), custom_call_target="tpu_custom_call" | custom-call | flops 32212254720 | bytes 50331648 | tf_op jit(solution)/shard_map/down/pallas_call | solution.py:396
  131.7 1.7 collective-permute-start.17
  133.4 1.5 collective-permute-start.19
  134.9 5.9 %down.2 = (bf16[2,2,256,384]{3,2,1,0:T(8,128)(2,1)}, bf16[2,2,256,384]{3,2,1,0:T(8,128)(2,1)}, bf16[2,2,256,384]{3,2,1,0:T(8,128)(2,1)}, bf16[2,2,256,384]{3,2,1,0:T(8,128)(2,1)}) custom-call(s32[4]{0:T(128)} %pad_add_fusion.place, bf16[4,320,2048]{2,1,0:T(8,128)(2,1)} %get-tuple-element.57.kept, bf16[4,320,384]{2,1,0:T(8,128)(2,1)} %get-tuple-element.58.scaled_in), custom_call_target="tpu_custom_call" | custom-call | flops 32212254720 | bytes 50331648 | tf_op jit(solution)/shard_map/down/pallas_call | solution.py:396
  140.8 0.7 collective-permute-start.13
  141.5 0.6 collective-permute-start.14
  142.1 10.3 %collective-permute-done.17 = bf16[2,2,256,384]{3,2,1,0:T(8,128)(2,1)S(1)} collective-permute-done((bf16[2,2,256,384]{3,2,1,0:T(8,128)(2,1)}, bf16[2,2,256,384]{3,2,1,0:T(8,128)(2,1)S(1)}, u32[]{:S(2)}, u32[]{:S(2)}) %collective-permute-start.17) | collective-permute-done | bytes 786464 | tf_op jit(solution)/shard_map/ppermute | solution.py:418
  152.4 0.2 add_convert_fusion.1
  152.6 1.7 collective-permute-start.18
  154.4 0.2 add_convert_fusion
  154.7 1.6 collective-permute-start.20
  156.2 13.0 %collective-permute-done.13 = bf16[2,2,256,384]{3,2,1,0:T(8,128)(2,1)S(1)} collective-permute-done((bf16[2,2,256,384]{3,2,1,0:T(8,128)(2,1)}, bf16[2,2,256,384]{3,2,1,0:T(8,128)(2,1)S(1)}, u32[]{:S(2)}, u32[]{:S(2)}) %collective-permute-start.13) | collective-permute-done | bytes 786464 | tf_op jit(solution)/shard_map/ppermute | solution.py:418
  169.2 0.2 add_convert_fusion.3
  169.5 1.7 collective-permute-start.15
  171.2 0.2 add_convert_fusion.2
  171.5 1.6 collective-permute-start.16
  173.1 6.2 %collective-permute-done.18.refs_1_ = bf16[1,2,256,384]{3,2,1,0:T(8,128)(2,1)S(1)} collective-permute-done((bf16[1,2,256,384]{3,2,1,0:T(8,128)(2,1)S(1)}, bf16[1,2,256,384]{3,2,1,0:T(8,128)(2,1)S(1)}, u32[]{:S(2)}, u32[]{:S(2)}) %collective-permute-start.18) | collective-permute-done | bytes 393248 | tf_op jit(solution)/shard_map/ppermute | solution.py:466
  179.3 1.2 put.2.refs_4_
  180.6 0.4 reduce-scatter.2.cloned.1.call-done.rows
  180.9 1.9 finish.1
  182.8 3.6 %collective-permute-done.15.refs_1_ = bf16[1,2,256,384]{3,2,1,0:T(8,128)(2,1)S(1)} collective-permute-done((bf16[1,2,256,384]{3,2,1,0:T(8,128)(2,1)S(1)}, bf16[1,2,256,384]{3,2,1,0:T(8,128)(2,1)S(1)}, u32[]{:S(2)}, u32[]{:S(2)}) %collective-permute-start.15) | collective-permute-done | bytes 393248 | tf_op jit(solution)/shard_map/ppermute | solution.py:466
  186.5 1.2 put.3
  (50 shorter events, 0.5 us)
Async XLA Ops:
  7.2 17.9 %copy-start.4 = (bf16[128,2048]{1,0:T(8,128)(2,1)S(1)}, bf16[128,2048]{1,0:T(8,128)(2,1)}, u32[]{:S(2)}) copy-start(bf16[128,2048]{1,0:T(8,128)(2,1)} %refs_0_.1) | copy-start | bytes 1572868
  7.2 81.5 %all-gather.2.cloned.1.call-start = ((), (), s32[]{:S(2)}) async-start(), calls=%async_computation.1 | async-start | bytes 5013504 | tf_op jit(solution)/shard_map/all_gather | solution.py:278
  25.0 155.9 %reduce-scatter.2.cloned.1.call-start = ((), (), s32[]{:S(2)}) async-start(), calls=%async_computation.2 | async-start | bytes 5013504 | tf_op jit(solution)/shard_map/reduce_scatter | solution.py:450
  25.1 5.0 %collective-permute-start = (bf16[128,2048]{1,0:T(8,128)(2,1)S(1)}, bf16[128,2048]{1,0:T(8,128)(2,1)S(1)}, u32[]{:S(2)}, u32[]{:S(2)}) collective-permute-start(bf16[128,2048]{1,0:T(8,128)(2,1)S(1)} %copy-done.4), channel_id=1, source_target_pairs={{0,1},{1,0},{2,3},{3,2},{4,5},{5,4},{6,7},{7,6},{8,9},{9,8},{10,11... | collective-permute-start | bytes 1572872 | tf_op jit(solution)/shard_map/ppermute | solution.py:285
  25.6 15.4 %collective-permute-start.1 = (bf16[128,2048]{1,0:T(8,128)(2,1)S(1)}, bf16[128,2048]{1,0:T(8,128)(2,1)S(1)}, u32[]{:S(2)}, u32[]{:S(2)}) collective-permute-start(bf16[128,2048]{1,0:T(8,128)(2,1)S(1)} %copy-done.4), channel_id=1, source_target_pairs={{0,2},{2,4},{3,1},{4,6},{5,3},{7,5},{8,10},{10,12},{11,9},{12,14},... | collective-permute-start | bytes 1572872 | tf_op jit(solution)/shard_map/ppermute | solution.py:285
  30.1 10.9 %copy-start.5 = (bf16[128,2048]{1,0:T(8,128)(2,1)}, bf16[128,2048]{1,0:T(8,128)(2,1)S(1)}, u32[]{:S(2)}) copy-start(bf16[128,2048]{1,0:T(8,128)(2,1)S(1)} %collective-permute-done.refs_1_) | copy-start | bytes 1572868
  30.1 24.6 %collective-permute-start.2 = (bf16[128,2048]{1,0:T(8,128)(2,1)S(1)}, bf16[128,2048]{1,0:T(8,128)(2,1)S(1)}, u32[]{:S(2)}, u32[]{:S(2)}) collective-permute-start(bf16[128,2048]{1,0:T(8,128)(2,1)S(1)} %collective-permute-done.refs_1_), channel_id=1, source_target_pairs={{0,2},{2,4},{3,1},{4,6},{5,3},{7,5},{8,10},{10,12},{11,9},{12,14},... | collective-permute-start | bytes 1572872 | tf_op jit(solution)/shard_map/ppermute | solution.py:285
  41.0 58.0 %copy-start.6 = (bf16[128,2048]{1,0:T(8,128)(2,1)}, bf16[128,2048]{1,0:T(8,128)(2,1)S(1)}, u32[]{:S(2)}) copy-start(bf16[128,2048]{1,0:T(8,128)(2,1)S(1)} %collective-permute-done.1.refs_2_) | copy-start | bytes 1572868
  41.0 15.7 %collective-permute-start.4 = (bf16[128,2048]{1,0:T(8,128)(2,1)S(1)}, bf16[128,2048]{1,0:T(8,128)(2,1)S(1)}, u32[]{:S(2)}, u32[]{:S(2)}) collective-permute-start(bf16[128,2048]{1,0:T(8,128)(2,1)S(1)} %collective-permute-done.1.refs_2_), channel_id=1, source_target_pairs={{1,0},{2,3},{3,2},{4,5},{5,4},{6,7},{9,8},{10,11},{11,10},{12,13},... | collective-permute-start | bytes 1572872 | tf_op jit(solution)/shard_map/ppermute | solution.py:285
  42.3 14.5 %collective-permute-start.3 = (bf16[128,2048]{1,0:T(8,128)(2,1)S(1)}, bf16[128,2048]{1,0:T(8,128)(2,1)S(1)}, u32[]{:S(2)}, u32[]{:S(2)}) collective-permute-start(bf16[128,2048]{1,0:T(8,128)(2,1)S(1)} %collective-permute-done.1.refs_2_), channel_id=1, source_target_pairs={{2,4},{3,1},{4,6},{5,3},{10,12},{11,9},{12,14},{13,11},{18,20},{19... | collective-permute-start | bytes 1572872 | tf_op jit(solution)/shard_map/ppermute | solution.py:285
  54.8 44.3 %copy-start.7 = (bf16[128,2048]{1,0:T(8,128)(2,1)}, bf16[128,2048]{1,0:T(8,128)(2,1)S(1)}, u32[]{:S(2)}) copy-start(bf16[128,2048]{1,0:T(8,128)(2,1)S(1)} %collective-permute-done.2.refs_3_) | copy-start | bytes 1572868
  54.8 7.5 %collective-permute-start.5 = (bf16[128,2048]{1,0:T(8,128)(2,1)S(1)}, bf16[128,2048]{1,0:T(8,128)(2,1)S(1)}, u32[]{:S(2)}, u32[]{:S(2)}) collective-permute-start(bf16[128,2048]{1,0:T(8,128)(2,1)S(1)} %collective-permute-done.2.refs_3_), channel_id=1, source_target_pairs={{1,0},{2,3},{3,2},{4,5},{5,4},{6,7},{9,8},{10,11},{11,10},{12,13},... | collective-permute-start | bytes 1572872 | tf_op jit(solution)/shard_map/ppermute | solution.py:285
  56.0 9.0 %collective-permute-start.6 = (bf16[128,2048]{1,0:T(8,128)(2,1)S(1)}, bf16[128,2048]{1,0:T(8,128)(2,1)S(1)}, u32[]{:S(2)}, u32[]{:S(2)}) collective-permute-start(bf16[128,2048]{1,0:T(8,128)(2,1)S(1)} %collective-permute-done.2.refs_3_), channel_id=1, source_target_pairs={{2,4},{3,1},{4,6},{5,3},{10,12},{11,9},{12,14},{13,11},{18,20},{19... | collective-permute-start | bytes 1572872 | tf_op jit(solution)/shard_map/ppermute | solution.py:285
  56.8 42.3 %copy-start.8 = (bf16[128,2048]{1,0:T(8,128)(2,1)}, bf16[128,2048]{1,0:T(8,128)(2,1)S(1)}, u32[]{:S(2)}) copy-start(bf16[128,2048]{1,0:T(8,128)(2,1)S(1)} %collective-permute-done.4.refs_8_) | copy-start | bytes 1572868
  56.8 42.3 %copy-start.9 = (bf16[128,2048]{1,0:T(8,128)(2,1)}, bf16[128,2048]{1,0:T(8,128)(2,1)S(1)}, u32[]{:S(2)}) copy-start(bf16[128,2048]{1,0:T(8,128)(2,1)S(1)} %collective-permute-done.3.refs_4_) | copy-start | bytes 1572868
  62.3 36.8 %copy-start.10 = (bf16[128,2048]{1,0:T(8,128)(2,1)}, bf16[128,2048]{1,0:T(8,128)(2,1)S(1)}, u32[]{:S(2)}) copy-start(bf16[128,2048]{1,0:T(8,128)(2,1)S(1)} %collective-permute-done.5.refs_9_) | copy-start | bytes 1572868
  62.3 24.1 %collective-permute-start.8 = (bf16[128,2048]{1,0:T(8,128)(2,1)S(1)}, bf16[128,2048]{1,0:T(8,128)(2,1)S(1)}, u32[]{:S(2)}, u32[]{:S(2)}) collective-permute-start(bf16[128,2048]{1,0:T(8,128)(2,1)S(1)} %collective-permute-done.3.refs_4_), channel_id=1, source_target_pairs={{1,0},{3,2},{4,5},{6,7},{9,8},{11,10},{12,13},{14,15},{17,16},{19,... | collective-permute-start | bytes 1572872 | tf_op jit(solution)/shard_map/ppermute | solution.py:285
  63.6 36.8 %collective-permute-start.7 = (bf16[128,2048]{1,0:T(8,128)(2,1)S(1)}, bf16[128,2048]{1,0:T(8,128)(2,1)}, u32[]{:S(2)}, u32[]{:S(2)}) collective-permute-start(bf16[128,2048]{1,0:T(8,128)(2,1)S(1)} %collective-permute-done.3.refs_4_), channel_id=1, source_target_pairs={{3,1},{4,6},{11,9},{12,14},{19,17},{20,22},{27,25},{28,30}} | collective-permute-start | bytes 1572872 | tf_op jit(solution)/shard_map/ppermute | solution.py:285
  65.1 34.0 %copy-start.11 = (bf16[128,2048]{1,0:T(8,128)(2,1)}, bf16[128,2048]{1,0:T(8,128)(2,1)S(1)}, u32[]{:S(2)}) copy-start(bf16[128,2048]{1,0:T(8,128)(2,1)S(1)} %collective-permute-done.6.refs_5_) | copy-start | bytes 1572868
  86.4 0.8 copy-start.12
  87.2 13.2 %collective-permute-start.9 = (bf16[128,2048]{1,0:T(8,128)(2,1)S(1)}, bf16[128,2048]{1,0:T(8,128)(2,1)}, u32[]{:S(2)}, u32[]{:S(2)}) collective-permute-start(bf16[128,2048]{1,0:T(8,128)(2,1)S(1)} %collective-permute-done.6.refs_5_), channel_id=1, source_target_pairs={{3,1},{4,6},{11,9},{12,14},{19,17},{20,22},{27,25},{28,30}} | collective-permute-start | bytes 1572872 | tf_op jit(solution)/shard_map/ppermute | solution.py:285
  99.1 5.7 %collective-permute-start.10 = (bf16[128,2048]{1,0:T(8,128)(2,1)S(1)}, bf16[128,2048]{1,0:T(8,128)(2,1)S(1)}, u32[]{:S(2)}, u32[]{:S(2)}) collective-permute-start(bf16[128,2048]{1,0:T(8,128)(2,1)S(1)} %collective-permute-done.6.refs_5_), channel_id=1, source_target_pairs={{1,0},{3,2},{4,5},{6,7},{9,8},{11,10},{12,13},{14,15},{17,16},{19,... | collective-permute-start | bytes 1572872 | tf_op jit(solution)/shard_map/ppermute | solution.py:285
  100.4 6.0 %collective-permute-start.12 = (bf16[128,2048]{1,0:T(8,128)(2,1)}, bf16[128,2048]{1,0:T(8,128)(2,1)S(1)}, u32[]{:S(2)}, u32[]{:S(2)}) collective-permute-start(bf16[128,2048]{1,0:T(8,128)(2,1)} %collective-permute-done.9.refs_7_), channel_id=1, source_target_pairs={{1,0},{6,7},{9,8},{14,15},{17,16},{22,23},{25,24},{30,31}} | collective-permute-start | bytes 1572872 | tf_op jit(solution)/shard_map/ppermute | solution.py:285
  101.7 6.0 %collective-permute-start.11 = (bf16[128,2048]{1,0:T(8,128)(2,1)}, bf16[128,2048]{1,0:T(8,128)(2,1)S(1)}, u32[]{:S(2)}, u32[]{:S(2)}) collective-permute-start(bf16[128,2048]{1,0:T(8,128)(2,1)} %collective-permute-done.7.refs_6_), channel_id=1, source_target_pairs={{1,0},{6,7},{9,8},{14,15},{17,16},{22,23},{25,24},{30,31}} | collective-permute-start | bytes 1572872 | tf_op jit(solution)/shard_map/ppermute | solution.py:285
  104.8 2.9 %copy-start.13 = (bf16[128,2048]{1,0:T(8,128)(2,1)}, bf16[128,2048]{1,0:T(8,128)(2,1)S(1)}, u32[]{:S(2)}) copy-start(bf16[128,2048]{1,0:T(8,128)(2,1)S(1)} %collective-permute-done.10.refs_11_) | copy-start | bytes 1572868
  106.3 1.3 copy-start.14
  107.7 0.8 copy-start.15
  131.7 20.7 %collective-permute-start.17 = (bf16[2,2,256,384]{3,2,1,0:T(8,128)(2,1)}, bf16[2,2,256,384]{3,2,1,0:T(8,128)(2,1)S(1)}, u32[]{:S(2)}, u32[]{:S(2)}) collective-permute-start(bf16[2,2,256,384]{3,2,1,0:T(8,128)(2,1)} %get-tuple-element.68), channel_id=1, source_target_pairs={{0,8},{8,0},{16,24},{24,16},{1,9},{9,1},{17,25},{25,17},{2,10},{10... | collective-permute-start | bytes 2359304 | tf_op jit(solution)/shard_map/ppermute | solution.py:418
  133.4 19.0 %copy-start.3 = (bf16[2,2,256,384]{3,2,1,0:T(8,128)(2,1)S(1)}, bf16[2,2,256,384]{3,2,1,0:T(8,128)(2,1)}, u32[]{:S(2)}) copy-start(bf16[2,2,256,384]{3,2,1,0:T(8,128)(2,1)} %get-tuple-element.67) | copy-start | bytes 2359300
  133.4 21.0 %collective-permute-start.19 = (bf16[2,2,256,384]{3,2,1,0:T(8,128)(2,1)}, bf16[2,2,256,384]{3,2,1,0:T(8,128)(2,1)S(1)}, u32[]{:S(2)}, u32[]{:S(2)}) collective-permute-start(bf16[2,2,256,384]{3,2,1,0:T(8,128)(2,1)} %get-tuple-element.70), channel_id=1, source_target_pairs={{0,16},{8,24},{16,0},{24,8},{1,17},{9,25},{17,1},{25,9},{2,18},{10... | collective-permute-start | bytes 2359304 | tf_op jit(solution)/shard_map/ppermute | solution.py:418
  140.8 28.4 %collective-permute-start.13 = (bf16[2,2,256,384]{3,2,1,0:T(8,128)(2,1)}, bf16[2,2,256,384]{3,2,1,0:T(8,128)(2,1)S(1)}, u32[]{:S(2)}, u32[]{:S(2)}) collective-permute-start(bf16[2,2,256,384]{3,2,1,0:T(8,128)(2,1)} %get-tuple-element.60), channel_id=1, source_target_pairs={{0,8},{8,0},{16,24},{24,16},{1,9},{9,1},{17,25},{25,17},{2,10},{10... | collective-permute-start | bytes 2359304 | tf_op jit(solution)/shard_map/ppermute | solution.py:418
  141.5 29.8 %collective-permute-start.14 = (bf16[2,2,256,384]{3,2,1,0:T(8,128)(2,1)}, bf16[2,2,256,384]{3,2,1,0:T(8,128)(2,1)S(1)}, u32[]{:S(2)}, u32[]{:S(2)}) collective-permute-start(bf16[2,2,256,384]{3,2,1,0:T(8,128)(2,1)} %get-tuple-element.62), channel_id=1, source_target_pairs={{0,16},{8,24},{16,0},{24,8},{1,17},{9,25},{17,1},{25,9},{2,18},{10... | collective-permute-start | bytes 2359304 | tf_op jit(solution)/shard_map/ppermute | solution.py:418
  152.4 2.0 %copy-start.2 = (bf16[2,2,256,384]{3,2,1,0:T(8,128)(2,1)S(1)}, bf16[2,2,256,384]{3,2,1,0:T(8,128)(2,1)}, u32[]{:S(2)}) copy-start(bf16[2,2,256,384]{3,2,1,0:T(8,128)(2,1)} %get-tuple-element.69) | copy-start | bytes 2359300
  152.6 26.7 %collective-permute-start.18 = (bf16[1,2,256,384]{3,2,1,0:T(8,128)(2,1)S(1)}, bf16[1,2,256,384]{3,2,1,0:T(8,128)(2,1)S(1)}, u32[]{:S(2)}, u32[]{:S(2)}) collective-permute-start(bf16[1,2,256,384]{3,2,1,0:T(8,128)(2,1)S(1)} %get-tuple-element.73), channel_id=1, source_target_pairs={{0,16},{8,24},{16,0},{24,8},{1,17},{9,25},{17,1},{25,9},{2,18},{10... | collective-permute-start | bytes 1179656 | tf_op jit(solution)/shard_map/ppermute | solution.py:466
  154.4 14.8 %copy-start.1 = (bf16[2,2,256,384]{3,2,1,0:T(8,128)(2,1)S(1)}, bf16[2,2,256,384]{3,2,1,0:T(8,128)(2,1)}, u32[]{:S(2)}) copy-start(bf16[2,2,256,384]{3,2,1,0:T(8,128)(2,1)} %get-tuple-element.59) | copy-start | bytes 2359300
  154.7 24.7 %collective-permute-start.20 = (bf16[1,2,256,384]{3,2,1,0:T(8,128)(2,1)S(1)}, bf16[1,2,256,384]{3,2,1,0:T(8,128)(2,1)S(1)}, u32[]{:S(2)}, u32[]{:S(2)}) collective-permute-start(bf16[1,2,256,384]{3,2,1,0:T(8,128)(2,1)S(1)} %get-tuple-element.71), channel_id=1, source_target_pairs={{0,8},{8,0},{16,24},{24,16},{1,9},{9,1},{17,25},{25,17},{2,10},{10... | collective-permute-start | bytes 1179656 | tf_op jit(solution)/shard_map/ppermute | solution.py:466
  169.2 2.0 %copy-start = (bf16[2,2,256,384]{3,2,1,0:T(8,128)(2,1)S(1)}, bf16[2,2,256,384]{3,2,1,0:T(8,128)(2,1)}, u32[]{:S(2)}) copy-start(bf16[2,2,256,384]{3,2,1,0:T(8,128)(2,1)} %get-tuple-element.61) | copy-start | bytes 2359300
  169.5 17.0 %collective-permute-start.15 = (bf16[1,2,256,384]{3,2,1,0:T(8,128)(2,1)S(1)}, bf16[1,2,256,384]{3,2,1,0:T(8,128)(2,1)S(1)}, u32[]{:S(2)}, u32[]{:S(2)}) collective-permute-start(bf16[1,2,256,384]{3,2,1,0:T(8,128)(2,1)S(1)} %get-tuple-element.77), channel_id=1, source_target_pairs={{0,16},{8,24},{16,0},{24,8},{1,17},{9,25},{17,1},{25,9},{2,18},{10... | collective-permute-start | bytes 1179656 | tf_op jit(solution)/shard_map/ppermute | solution.py:466
  171.5 14.9 %collective-permute-start.16 = (bf16[1,2,256,384]{3,2,1,0:T(8,128)(2,1)S(1)}, bf16[1,2,256,384]{3,2,1,0:T(8,128)(2,1)S(1)}, u32[]{:S(2)}, u32[]{:S(2)}) collective-permute-start(bf16[1,2,256,384]{3,2,1,0:T(8,128)(2,1)S(1)} %get-tuple-element.75), channel_id=1, source_target_pairs={{0,8},{8,0},{16,24},{24,16},{1,9},{9,1},{17,25},{25,17},{2,10},{10... | collective-permute-start | bytes 1179656 | tf_op jit(solution)/shard_map/ppermute | solution.py:466
Sparse Core Ops, SparseCore 0:
  25.1 60.8 all-gather.1
  126.2 54.7 reduce-scatter.1

commit v20 on v18

--- a/solution.py
+++ b/solution.py
@@ -448,7 +448,7 @@
         name="finish",
     )(summed)
 
-    counts = [experts // 2, experts - experts // 2] if experts > 1 else [experts]
+    counts = [experts - 1, 1] if experts > 1 else [experts]
     states = [down(start, count) for start, count in zip((0, counts[0]), counts)]
     for t in range(bits - 1):
         states = [exchange(state, t) for state in states]

time: 178 us -> 188 us (1.056)
  waiting for transfers between devices: 76.8 us -> 85.6 us
    ppermute x4, waiting for transfers between devices: 23.4 us -> 28.7 us  [exchange(): got = lax.ppermute(send, 'dp', [(i, i ^ bit) for i in range(dp_count)])]
    ppermute x4, waiting for transfers between devices: 9.71 us -> 13.8 us  [shards(): lax.ppermute(send, 'dp', [(i, i ^ 1 << (g + last) % bits) for i in range(...]
  transfers between devices with their start and end apart: 23 -> 23, of which waited for: 11 -> 9; matrix products, arithmetic and copies ran while one was open for 1% -> 1% of each run, Pallas kernels for 18% -> 17%
where the time goes in v20:
time: 188 us; the launch traced here: 187 us
  waiting for transfers between devices  85.6 us (46%)
  Pallas kernels  51.1 us (27%)
  starting transfers between devices  30.5 us (16%)
  between operations  14.4 us (8%)
  local copies, waits for them, and re-layouts  2.74 us (1%)
  other arithmetic  2.42 us (1%)
    ppermute x13, waiting for transfers between devices, hop(): return lax.ppermute(value, 'ep', pairs)  43 us
    ppermute x4, waiting for transfers between devices, exchange(): got = lax.ppermute(send, 'dp', [(i, i ^ bit) for i in range(dp_count)])  28.7 us
    ppermute x13, starting transfers between devices, hop(): return lax.ppermute(value, 'ep', pairs)  20.8 us
    pallas_call x1, Pallas kernels, shards(): one(functools.partial(tail_kernel, groups, cap, width, top), 'tail', 8 *...  16.2 us
    ppermute x4, waiting for transfers between devices, shards(): lax.ppermute(send, 'dp', [(i, i ^ 1 << (g + last) % bits) for i in range(...  13.8 us
    pallas_call x2, Pallas kernels, down(): one(functools.partial(down_kernel, orders, start), 'down', 16 * main_flop...  11.4 us
    pallas_call x1, Pallas kernels, shards(): one(functools.partial(up_kernel, groups, width, top, cap), 'up', pick_flo...  10.4 us
    pallas_call x1, Pallas kernels, shards(): call(flip_kernel, 'flip', experts, 0, 2 * row_bytes, in_specs=[SMEM, pl.B...  6.78 us
  transfers between devices with their start and end apart: 23, of which 9 were waited for; matrix products, arithmetic and copies ran while one was open for 1% of the time, Pallas kernels for 17%

profile of v20, /device:TPU:0, one launch (start us, length us, event | category | flops | bytes accessed | tf_op | source)
XLA Modules:
  0.0 186.9 jit_solution(17793248147136748831)
XLA Ops:
  7.2 2.0 %pack.1 = bf16[128,2176]{1,0:T(8,128)(2,1)} custom-call(bf16[128,2048]{1,0:T(8,128)(2,1)} %tokens.1, s32[8,128]{1,0:T(8,128)} %bitcast.7, bf16[8,128]{1,0:T(8,128)(2,1)} %bitcast.8), custom_call_target="tpu_custom_call" | custom-call | bytes 1048576 | tf_op jit(solution)/shard_map/pack/pallas_call | solution.py:263
  9.3 0.5 collective-permute-start
  9.8 4.5 %collective-permute-start.1 = (bf16[128,2048]{1,0:T(8,128)(2,1)S(1)}, bf16[128,2048]{1,0:T(8,128)(2,1)S(1)}, u32[]{:S(2)}, u32[]{:S(2)}) collective-permute-start(bf16[128,2048]{1,0:T(8,128)(2,1)S(1)} %copy-done.4), channel_id=1, source_target_pairs={{0,2},{2,4},{3,1},{4,6},{5,3},{7,5},{8,10},{10,12},{11,9},{12,14},... | collective-permute-start | bytes 1572872 | tf_op jit(solution)/shard_map/ppermute | solution.py:277
  14.4 3.5 %collective-permute-start.2 = (bf16[128,2048]{1,0:T(8,128)(2,1)S(1)}, bf16[128,2048]{1,0:T(8,128)(2,1)S(1)}, u32[]{:S(2)}, u32[]{:S(2)}) collective-permute-start(bf16[128,2048]{1,0:T(8,128)(2,1)S(1)} %collective-permute-done.refs_1_), channel_id=1, source_target_pairs={{0,2},{2,4},{3,1},{4,6},{5,3},{7,5},{8,10},{10,12},{11,9},{12,14},... | collective-permute-start | bytes 1572872 | tf_op jit(solution)/shard_map/ppermute | solution.py:277
  17.9 0.6 pad_add_fusion.place
  18.5 6.8 %flip.1.refs_16_ = bf16[4,384,2048]{2,1,0:T(8,128)(2,1)} custom-call(s32[4]{0:T(128)} %pad_add_fusion.place, bf16[4,2048,384]{2,1,0:T(8,128)(2,1)} %w_up.1), custom_call_target="tpu_custom_call" | custom-call | bytes 12582912 | tf_op jit(solution)/shard_map/flip/pallas_call | solution.py:296
  25.3 1.3 collective-permute-start.4
  26.6 0.7 collective-permute-start.3
  27.3 10.0 %collective-permute-done.2.refs_3_ = bf16[128,2048]{1,0:T(8,128)(2,1)S(1)} collective-permute-done((bf16[128,2048]{1,0:T(8,128)(2,1)S(1)}, bf16[128,2048]{1,0:T(8,128)(2,1)S(1)}, u32[]{:S(2)}, u32[]{:S(2)}) %collective-permute-start.2) | collective-permute-done | bytes 524320 | tf_op jit(solution)/shard_map/ppermute | solution.py:277
  37.3 1.3 collective-permute-start.5
  38.6 0.7 collective-permute-start.6
  39.4 3.2 %collective-permute-done.5.refs_9_ = bf16[128,2048]{1,0:T(8,128)(2,1)S(1)} collective-permute-done((bf16[128,2048]{1,0:T(8,128)(2,1)S(1)}, bf16[128,2048]{1,0:T(8,128)(2,1)S(1)}, u32[]{:S(2)}, u32[]{:S(2)}) %collective-permute-start.5) | collective-permute-done | bytes 524320 | tf_op jit(solution)/shard_map/ppermute | solution.py:277
  42.6 1.3 collective-permute-start.8
  43.9 1.5 collective-permute-start.7
  45.4 23.5 %collective-permute-done.8.refs_10_ = bf16[128,2048]{1,0:T(8,128)(2,1)S(1)} collective-permute-done((bf16[128,2048]{1,0:T(8,128)(2,1)S(1)}, bf16[128,2048]{1,0:T(8,128)(2,1)S(1)}, u32[]{:S(2)}, u32[]{:S(2)}) %collective-permute-start.8) | collective-permute-done | bytes 524320 | tf_op jit(solution)/shard_map/ppermute | solution.py:277
  68.9 0.8 copy-done.12
  69.7 1.5 collective-permute-start.9
  71.2 10.4 %up.1 = (bf16[4,320,256]{2,1,0:T(8,128)(2,1)}, bf16[1024,128]{1,0:T(8,128)(2,1)}, bf16[4,320,384]{2,1,0:T(8,128)(2,1)}, bf16[4,320,384]{2,1,0:T(8,128)(2,1)}, bf16[4,320,384]{2,1,0:T(8,128)(2,1)}) custom-call(s32[4]{0:T(128)} %pad_add_fusion.place, bf16[1024,2176]{1,0:T(8,128)(2,1)} %all-gather.2.cloned.1.call-done.x_all, bf16[4,2048,384]{2,1,0:T(8,128)(2,1)} %w_up.1), custom_call_target="tpu_custom_call" | custom-call | flops 3355443200 | bytes 10747904 | tf_op jit(solution)/shard_map/up/pallas_call | solution.py:347
  81.6 1.3 collective-permute-start.10
  82.9 1.3 collective-permute-start.12
  84.2 1.5 collective-permute-start.11
  85.7 3.3 %collective-permute-done.10.refs_11_ = bf16[128,2048]{1,0:T(8,128)(2,1)S(1)} collective-permute-done((bf16[128,2048]{1,0:T(8,128)(2,1)S(1)}, bf16[128,2048]{1,0:T(8,128)(2,1)S(1)}, u32[]{:S(2)}, u32[]{:S(2)}) %collective-permute-start.10) | collective-permute-done | bytes 524320 | tf_op jit(solution)/shard_map/ppermute | solution.py:277
  89.0 1.6 collective-permute-done.12.refs_13_
  90.6 1.3 collective-permute-done.11.refs_12_
  91.9 0.8 copy-done.15
  92.7 16.2 %tail.1 = (bf16[1024,2176]{1,0:T(8,128)(2,1)}, bf16[4,320,2048]{2,1,0:T(8,128)(2,1)}) custom-call(s32[4]{0:T(128)} %pad_add_fusion.place, bf16[128,2048]{1,0:T(8,128)(2,1)} %refs_0_.1, bf16[128,2048]{1,0:T(8,128)(2,1)} %copy-done.5, bf16[128,2048]{1,0:T(8,128)(2,1)} %copy-done.6, bf16[128,2048]{1,0:T(8,128)(2,1)} %copy-done.7, bf16[128,2048]{1,0:T(8,128)(2,1)} %copy-done.9, ...), custom_call_target="tpu_custom_call" | custom-call | flops 16106127360 | bytes 25165824 | tf_op jit(solution)/shard_map/tail/pallas_call | solution.py:418
  109.0 7.5 %down.3 = (bf16[2,3,256,384]{3,2,1,0:T(8,128)(2,1)}, bf16[2,3,256,384]{3,2,1,0:T(8,128)(2,1)}, bf16[2,3,256,384]{3,2,1,0:T(8,128)(2,1)}, bf16[2,3,256,384]{3,2,1,0:T(8,128)(2,1)}) custom-call(s32[4]{0:T(128)} %pad_add_fusion.place, bf16[4,320,2048]{2,1,0:T(8,128)(2,1)} %get-tuple-element.57.kept, bf16[4,320,384]{2,1,0:T(8,128)(2,1)} %get-tuple-element.58.scaled_in), custom_call_target="tpu_custom_call" | custom-call | flops 32212254720 | bytes 50331648 | tf_op jit(solution)/shard_map/down/pallas_call | solution.py:388
  116.5 1.7 collective-permute-start.17
  118.2 4.0 %down.2 = (bf16[2,1,256,384]{3,2,1,0:T(8,128)(2,1)}, bf16[2,1,256,384]{3,2,1,0:T(8,128)(2,1)}, bf16[2,1,256,384]{3,2,1,0:T(8,128)(2,1)}, bf16[2,1,256,384]{3,2,1,0:T(8,128)(2,1)}) custom-call(s32[4]{0:T(128)} %pad_add_fusion.place, bf16[4,320,2048]{2,1,0:T(8,128)(2,1)} %get-tuple-element.57.kept, bf16[4,320,384]{2,1,0:T(8,128)(2,1)} %get-tuple-element.58.scaled_in), custom_call_target="tpu_custom_call" | custom-call | flops 32212254720 | bytes 50331648 | tf_op jit(solution)/shard_map/down/pallas_call | solution.py:388
  122.2 0.5 collective-permute-start.13
  122.7 1.6 collective-permute-start.19
  124.3 0.4 collective-permute-start.14
  124.7 28.5 %collective-permute-done.13 = bf16[2,1,256,384]{3,2,1,0:T(8,128)(2,1)S(1)} collective-permute-done((bf16[2,1,256,384]{3,2,1,0:T(8,128)(2,1)}, bf16[2,1,256,384]{3,2,1,0:T(8,128)(2,1)S(1)}, u32[]{:S(2)}, u32[]{:S(2)}) %collective-permute-start.13) | collective-permute-done | bytes 393248 | tf_op jit(solution)/shard_map/ppermute | solution.py:410
  153.2 1.1 add_convert_fusion.3
  154.3 1.7 collective-permute-start.15
  156.1 0.3 add_convert_fusion.1
  156.4 0.1 fusion.1
  156.5 0.4 collective-permute-start.18
  157.0 0.7 copy-done
  157.7 0.3 add_convert_fusion
  158.0 0.1 fusion
  158.2 1.6 collective-permute-start.20
  159.7 0.3 collective-permute-done.14
  160.2 1.7 collective-permute-start.16
  161.8 13.8 %collective-permute-done.18.refs_1_ = bf16[1,3,256,384]{3,2,1,0:T(8,128)(2,1)S(1)} collective-permute-done((bf16[1,3,256,384]{3,2,1,0:T(8,128)(2,1)S(1)}, bf16[1,3,256,384]{3,2,1,0:T(8,128)(2,1)S(1)}, u32[]{:S(2)}, u32[]{:S(2)}) %collective-permute-start.18) | collective-permute-done | bytes 589856 | tf_op jit(solution)/shard_map/ppermute | solution.py:458
  175.6 1.5 put.2.refs_4_
  177.2 1.9 %finish.1 = (bf16[128,2048]{1,0:T(8,128)(2,1)}, bf16[8,128]{1,0:T(8,128)(2,1)}) custom-call(bf16[128,2176]{1,0:T(8,128)(2,1)} %reduce-scatter.2.cloned.1.call-done.rows), custom_call_target="tpu_custom_call" | custom-call | bytes 1048576 | tf_op jit(solution)/shard_map/finish/pallas_call | solution.py:443
  179.1 0.9 put.3
  (50 shorter events, 0.4 us)
Async XLA Ops:
  7.2 2.1 %copy-start.4 = (bf16[128,2048]{1,0:T(8,128)(2,1)S(1)}, bf16[128,2048]{1,0:T(8,128)(2,1)}, u32[]{:S(2)}) copy-start(bf16[128,2048]{1,0:T(8,128)(2,1)} %refs_0_.1) | copy-start | bytes 1572868
  7.2 64.0 %all-gather.2.cloned.1.call-start = ((), (), s32[]{:S(2)}) async-start(), calls=%async_computation.1 | async-start | bytes 5013504 | tf_op jit(solution)/shard_map/all_gather | solution.py:270
  9.3 167.9 %reduce-scatter.2.cloned.1.call-start = ((), (), s32[]{:S(2)}) async-start(), calls=%async_computation.2 | async-start | bytes 5013504 | tf_op jit(solution)/shard_map/reduce_scatter | solution.py:442
  9.3 5.0 %collective-permute-start = (bf16[128,2048]{1,0:T(8,128)(2,1)S(1)}, bf16[128,2048]{1,0:T(8,128)(2,1)S(1)}, u32[]{:S(2)}, u32[]{:S(2)}) collective-permute-start(bf16[128,2048]{1,0:T(8,128)(2,1)S(1)} %copy-done.4), channel_id=1, source_target_pairs={{0,1},{1,0},{2,3},{3,2},{4,5},{5,4},{6,7},{7,6},{8,9},{9,8},{10,11... | collective-permute-start | bytes 1572872 | tf_op jit(solution)/shard_map/ppermute | solution.py:277
  9.8 15.4 %collective-permute-start.1 = (bf16[128,2048]{1,0:T(8,128)(2,1)S(1)}, bf16[128,2048]{1,0:T(8,128)(2,1)S(1)}, u32[]{:S(2)}, u32[]{:S(2)}) collective-permute-start(bf16[128,2048]{1,0:T(8,128)(2,1)S(1)} %copy-done.4), channel_id=1, source_target_pairs={{0,2},{2,4},{3,1},{4,6},{5,3},{7,5},{8,10},{10,12},{11,9},{12,14},... | collective-permute-start | bytes 1572872 | tf_op jit(solution)/shard_map/ppermute | solution.py:277
  14.4 10.9 %copy-start.5 = (bf16[128,2048]{1,0:T(8,128)(2,1)}, bf16[128,2048]{1,0:T(8,128)(2,1)S(1)}, u32[]{:S(2)}) copy-start(bf16[128,2048]{1,0:T(8,128)(2,1)S(1)} %collective-permute-done.refs_1_) | copy-start | bytes 1572868
  14.4 22.9 %collective-permute-start.2 = (bf16[128,2048]{1,0:T(8,128)(2,1)S(1)}, bf16[128,2048]{1,0:T(8,128)(2,1)S(1)}, u32[]{:S(2)}, u32[]{:S(2)}) collective-permute-start(bf16[128,2048]{1,0:T(8,128)(2,1)S(1)} %collective-permute-done.refs_1_), channel_id=1, source_target_pairs={{0,2},{2,4},{3,1},{4,6},{5,3},{7,5},{8,10},{10,12},{11,9},{12,14},... | collective-permute-start | bytes 1572872 | tf_op jit(solution)/shard_map/ppermute | solution.py:277
  25.3 56.3 %copy-start.6 = (bf16[128,2048]{1,0:T(8,128)(2,1)}, bf16[128,2048]{1,0:T(8,128)(2,1)S(1)}, u32[]{:S(2)}) copy-start(bf16[128,2048]{1,0:T(8,128)(2,1)S(1)} %collective-permute-done.1.refs_2_) | copy-start | bytes 1572868
  25.3 14.0 %collective-permute-start.4 = (bf16[128,2048]{1,0:T(8,128)(2,1)S(1)}, bf16[128,2048]{1,0:T(8,128)(2,1)S(1)}, u32[]{:S(2)}, u32[]{:S(2)}) collective-permute-start(bf16[128,2048]{1,0:T(8,128)(2,1)S(1)} %collective-permute-done.1.refs_2_), channel_id=1, source_target_pairs={{1,0},{2,3},{3,2},{4,5},{5,4},{6,7},{9,8},{10,11},{11,10},{12,13},... | collective-permute-start | bytes 1572872 | tf_op jit(solution)/shard_map/ppermute | solution.py:277
  26.6 12.8 %collective-permute-start.3 = (bf16[128,2048]{1,0:T(8,128)(2,1)S(1)}, bf16[128,2048]{1,0:T(8,128)(2,1)S(1)}, u32[]{:S(2)}, u32[]{:S(2)}) collective-permute-start(bf16[128,2048]{1,0:T(8,128)(2,1)S(1)} %collective-permute-done.1.refs_2_), channel_id=1, source_target_pairs={{2,4},{3,1},{4,6},{5,3},{10,12},{11,9},{12,14},{13,11},{18,20},{19... | collective-permute-start | bytes 1572872 | tf_op jit(solution)/shard_map/ppermute | solution.py:277
  37.3 44.2 %copy-start.7 = (bf16[128,2048]{1,0:T(8,128)(2,1)}, bf16[128,2048]{1,0:T(8,128)(2,1)S(1)}, u32[]{:S(2)}) copy-start(bf16[128,2048]{1,0:T(8,128)(2,1)S(1)} %collective-permute-done.2.refs_3_) | copy-start | bytes 1572868
  37.3 5.3 %collective-permute-start.5 = (bf16[128,2048]{1,0:T(8,128)(2,1)S(1)}, bf16[128,2048]{1,0:T(8,128)(2,1)S(1)}, u32[]{:S(2)}, u32[]{:S(2)}) collective-permute-start(bf16[128,2048]{1,0:T(8,128)(2,1)S(1)} %collective-permute-done.2.refs_3_), channel_id=1, source_target_pairs={{1,0},{2,3},{3,2},{4,5},{5,4},{6,7},{9,8},{10,11},{11,10},{12,13},... | collective-permute-start | bytes 1572872 | tf_op jit(solution)/shard_map/ppermute | solution.py:277
  38.6 6.8 %collective-permute-start.6 = (bf16[128,2048]{1,0:T(8,128)(2,1)S(1)}, bf16[128,2048]{1,0:T(8,128)(2,1)S(1)}, u32[]{:S(2)}, u32[]{:S(2)}) collective-permute-start(bf16[128,2048]{1,0:T(8,128)(2,1)S(1)} %collective-permute-done.2.refs_3_), channel_id=1, source_target_pairs={{2,4},{3,1},{4,6},{5,3},{10,12},{11,9},{12,14},{13,11},{18,20},{19... | collective-permute-start | bytes 1572872 | tf_op jit(solution)/shard_map/ppermute | solution.py:277
  39.3 42.2 %copy-start.8 = (bf16[128,2048]{1,0:T(8,128)(2,1)}, bf16[128,2048]{1,0:T(8,128)(2,1)S(1)}, u32[]{:S(2)}) copy-start(bf16[128,2048]{1,0:T(8,128)(2,1)S(1)} %collective-permute-done.4.refs_8_) | copy-start | bytes 1572868
  39.3 42.2 %copy-start.9 = (bf16[128,2048]{1,0:T(8,128)(2,1)}, bf16[128,2048]{1,0:T(8,128)(2,1)S(1)}, u32[]{:S(2)}) copy-start(bf16[128,2048]{1,0:T(8,128)(2,1)S(1)} %collective-permute-done.3.refs_4_) | copy-start | bytes 1572868
  42.6 39.0 %copy-start.10 = (bf16[128,2048]{1,0:T(8,128)(2,1)}, bf16[128,2048]{1,0:T(8,128)(2,1)S(1)}, u32[]{:S(2)}) copy-start(bf16[128,2048]{1,0:T(8,128)(2,1)S(1)} %collective-permute-done.5.refs_9_) | copy-start | bytes 1572868
  42.6 26.3 %collective-permute-start.8 = (bf16[128,2048]{1,0:T(8,128)(2,1)S(1)}, bf16[128,2048]{1,0:T(8,128)(2,1)S(1)}, u32[]{:S(2)}, u32[]{:S(2)}) collective-permute-start(bf16[128,2048]{1,0:T(8,128)(2,1)S(1)} %collective-permute-done.3.refs_4_), channel_id=1, source_target_pairs={{1,0},{3,2},{4,5},{6,7},{9,8},{11,10},{12,13},{14,15},{17,16},{19,... | collective-permute-start | bytes 1572872 | tf_op jit(solution)/shard_map/ppermute | solution.py:277
  43.9 39.0 %collective-permute-start.7 = (bf16[128,2048]{1,0:T(8,128)(2,1)S(1)}, bf16[128,2048]{1,0:T(8,128)(2,1)}, u32[]{:S(2)}, u32[]{:S(2)}) collective-permute-start(bf16[128,2048]{1,0:T(8,128)(2,1)S(1)} %collective-permute-done.3.refs_4_), channel_id=1, source_target_pairs={{3,1},{4,6},{11,9},{12,14},{19,17},{20,22},{27,25},{28,30}} | collective-permute-start | bytes 1572872 | tf_op jit(solution)/shard_map/ppermute | solution.py:277
  45.4 36.2 %copy-start.11 = (bf16[128,2048]{1,0:T(8,128)(2,1)}, bf16[128,2048]{1,0:T(8,128)(2,1)S(1)}, u32[]{:S(2)}) copy-start(bf16[128,2048]{1,0:T(8,128)(2,1)S(1)} %collective-permute-done.6.refs_5_) | copy-start | bytes 1572868
  68.9 0.8 copy-start.12
  69.7 13.2 %collective-permute-start.9 = (bf16[128,2048]{1,0:T(8,128)(2,1)S(1)}, bf16[128,2048]{1,0:T(8,128)(2,1)}, u32[]{:S(2)}, u32[]{:S(2)}) collective-permute-start(bf16[128,2048]{1,0:T(8,128)(2,1)S(1)} %collective-permute-done.6.refs_5_), channel_id=1, source_target_pairs={{3,1},{4,6},{11,9},{12,14},{19,17},{20,22},{27,25},{28,30}} | collective-permute-start | bytes 1572872 | tf_op jit(solution)/shard_map/ppermute | solution.py:277
  81.6 7.4 %collective-permute-start.10 = (bf16[128,2048]{1,0:T(8,128)(2,1)S(1)}, bf16[128,2048]{1,0:T(8,128)(2,1)S(1)}, u32[]{:S(2)}, u32[]{:S(2)}) collective-permute-start(bf16[128,2048]{1,0:T(8,128)(2,1)S(1)} %collective-permute-done.6.refs_5_), channel_id=1, source_target_pairs={{1,0},{3,2},{4,5},{6,7},{9,8},{11,10},{12,13},{14,15},{17,16},{19,... | collective-permute-start | bytes 1572872 | tf_op jit(solution)/shard_map/ppermute | solution.py:277
  82.9 7.7 %collective-permute-start.12 = (bf16[128,2048]{1,0:T(8,128)(2,1)}, bf16[128,2048]{1,0:T(8,128)(2,1)S(1)}, u32[]{:S(2)}, u32[]{:S(2)}) collective-permute-start(bf16[128,2048]{1,0:T(8,128)(2,1)} %collective-permute-done.9.refs_7_), channel_id=1, source_target_pairs={{1,0},{6,7},{9,8},{14,15},{17,16},{22,23},{25,24},{30,31}} | collective-permute-start | bytes 1572872 | tf_op jit(solution)/shard_map/ppermute | solution.py:277
  84.2 7.7 %collective-permute-start.11 = (bf16[128,2048]{1,0:T(8,128)(2,1)}, bf16[128,2048]{1,0:T(8,128)(2,1)S(1)}, u32[]{:S(2)}, u32[]{:S(2)}) collective-permute-start(bf16[128,2048]{1,0:T(8,128)(2,1)} %collective-permute-done.7.refs_6_), channel_id=1, source_target_pairs={{1,0},{6,7},{9,8},{14,15},{17,16},{22,23},{25,24},{30,31}} | collective-permute-start | bytes 1572872 | tf_op jit(solution)/shard_map/ppermute | solution.py:277
  89.0 2.9 %copy-start.13 = (bf16[128,2048]{1,0:T(8,128)(2,1)}, bf16[128,2048]{1,0:T(8,128)(2,1)S(1)}, u32[]{:S(2)}) copy-start(bf16[128,2048]{1,0:T(8,128)(2,1)S(1)} %collective-permute-done.10.refs_11_) | copy-start | bytes 1572868
  90.6 1.3 copy-start.14
  91.9 0.8 copy-start.15
  116.5 6.2 %copy-start.3 = (bf16[2,3,256,384]{3,2,1,0:T(8,128)(2,1)S(1)}, bf16[2,3,256,384]{3,2,1,0:T(8,128)(2,1)}, u32[]{:S(2)}) copy-start(bf16[2,3,256,384]{3,2,1,0:T(8,128)(2,1)} %get-tuple-element.70) | copy-start | bytes 3538948
  116.5 39.6 %collective-permute-start.17 = (bf16[2,3,256,384]{3,2,1,0:T(8,128)(2,1)}, bf16[2,3,256,384]{3,2,1,0:T(8,128)(2,1)S(1)}, u32[]{:S(2)}, u32[]{:S(2)}) collective-permute-start(bf16[2,3,256,384]{3,2,1,0:T(8,128)(2,1)} %get-tuple-element.68), channel_id=1, source_target_pairs={{0,8},{8,0},{16,24},{24,16},{1,9},{9,1},{17,25},{25,17},{2,10},{10... | collective-permute-start | bytes 3538952 | tf_op jit(solution)/shard_map/ppermute | solution.py:410
  122.2 33.9 %copy-start.1 = (bf16[2,3,256,384]{3,2,1,0:T(8,128)(2,1)S(1)}, bf16[2,3,256,384]{3,2,1,0:T(8,128)(2,1)}, u32[]{:S(2)}) copy-start(bf16[2,3,256,384]{3,2,1,0:T(8,128)(2,1)} %get-tuple-element.67) | copy-start | bytes 3538948
  122.2 31.0 %collective-permute-start.13 = (bf16[2,1,256,384]{3,2,1,0:T(8,128)(2,1)}, bf16[2,1,256,384]{3,2,1,0:T(8,128)(2,1)S(1)}, u32[]{:S(2)}, u32[]{:S(2)}) collective-permute-start(bf16[2,1,256,384]{3,2,1,0:T(8,128)(2,1)} %get-tuple-element.60), channel_id=1, source_target_pairs={{0,8},{8,0},{16,24},{24,16},{1,9},{9,1},{17,25},{25,17},{2,10},{10... | collective-permute-start | bytes 1179656 | tf_op jit(solution)/shard_map/ppermute | solution.py:410
  122.7 34.3 %collective-permute-start.19 = (bf16[2,3,256,384]{3,2,1,0:T(8,128)(2,1)S(1)}, bf16[2,3,256,384]{3,2,1,0:T(8,128)(2,1)S(1)}, u32[]{:S(2)}, u32[]{:S(2)}) collective-permute-start(bf16[2,3,256,384]{3,2,1,0:T(8,128)(2,1)S(1)} %copy-done.3), channel_id=1, source_target_pairs={{0,16},{8,24},{16,0},{24,8},{1,17},{9,25},{17,1},{25,9},{2,18},{10... | collective-permute-start | bytes 3538952 | tf_op jit(solution)/shard_map/ppermute | solution.py:410
  124.3 35.7 %collective-permute-start.14 = (bf16[2,1,256,384]{3,2,1,0:T(8,128)(2,1)}, bf16[2,1,256,384]{3,2,1,0:T(8,128)(2,1)S(1)}, u32[]{:S(2)}, u32[]{:S(2)}) collective-permute-start(bf16[2,1,256,384]{3,2,1,0:T(8,128)(2,1)} %get-tuple-element.62), channel_id=1, source_target_pairs={{0,16},{8,24},{16,0},{24,8},{1,17},{9,25},{17,1},{25,9},{2,18},{10... | collective-permute-start | bytes 1179656 | tf_op jit(solution)/shard_map/ppermute | solution.py:410
  154.3 24.7 %collective-permute-start.15 = (bf16[1,1,256,384]{3,2,1,0:T(8,128)(2,1)S(1)}, bf16[1,1,256,384]{3,2,1,0:T(8,128)(2,1)S(1)}, u32[]{:S(2)}, u32[]{:S(2)}) collective-permute-start(bf16[1,1,256,384]{3,2,1,0:T(8,128)(2,1)S(1)} %get-tuple-element.77), channel_id=1, source_target_pairs={{0,16},{8,24},{16,0},{24,8},{1,17},{9,25},{17,1},{25,9},{2,18},{10... | collective-permute-start | bytes 589832 | tf_op jit(solution)/shard_map/ppermute | solution.py:458
  156.4 1.3 copy-start
  156.5 19.1 %collective-permute-start.18 = (bf16[1,3,256,384]{3,2,1,0:T(8,128)(2,1)S(1)}, bf16[1,3,256,384]{3,2,1,0:T(8,128)(2,1)S(1)}, u32[]{:S(2)}, u32[]{:S(2)}) collective-permute-start(bf16[1,3,256,384]{3,2,1,0:T(8,128)(2,1)S(1)} %get-tuple-element.73), channel_id=1, source_target_pairs={{0,16},{8,24},{16,0},{24,8},{1,17},{9,25},{17,1},{25,9},{2,18},{10... | collective-permute-start | bytes 1769480 | tf_op jit(solution)/shard_map/ppermute | solution.py:458
  158.0 2.0 %copy-start.2 = (bf16[2,1,256,384]{3,2,1,0:T(8,128)(2,1)S(1)}, bf16[2,1,256,384]{3,2,1,0:T(8,128)(2,1)}, u32[]{:S(2)}) copy-start(bf16[2,1,256,384]{3,2,1,0:T(8,128)(2,1)} %get-tuple-element.61) | copy-start | bytes 1179652
  158.2 17.5 %collective-permute-start.20 = (bf16[1,3,256,384]{3,2,1,0:T(8,128)(2,1)S(1)}, bf16[1,3,256,384]{3,2,1,0:T(8,128)(2,1)S(1)}, u32[]{:S(2)}, u32[]{:S(2)}) collective-permute-start(bf16[1,3,256,384]{3,2,1,0:T(8,128)(2,1)S(1)} %get-tuple-element.71), channel_id=1, source_target_pairs={{0,8},{8,0},{16,24},{24,16},{1,9},{9,1},{17,25},{25,17},{2,10},{10... | collective-permute-start | bytes 1769480 | tf_op jit(solution)/shard_map/ppermute | solution.py:458
  160.2 18.9 %collective-permute-start.16 = (bf16[1,1,256,384]{3,2,1,0:T(8,128)(2,1)S(1)}, bf16[1,1,256,384]{3,2,1,0:T(8,128)(2,1)S(1)}, u32[]{:S(2)}, u32[]{:S(2)}) collective-permute-start(bf16[1,1,256,384]{3,2,1,0:T(8,128)(2,1)S(1)} %get-tuple-element.75), channel_id=1, source_target_pairs={{0,8},{8,0},{16,24},{24,16},{1,9},{9,1},{17,25},{25,17},{2,10},{10... | collective-permute-start | bytes 589832 | tf_op jit(solution)/shard_map/ppermute | solution.py:458
Sparse Core Ops, SparseCore 0:
  10.2 60.8 all-gather.1
  109.1 55.0 reduce-scatter.1
